TPU v7x, 256 devices: a whole 4x4x8 slice. The times are simulated.
256 devices in a mesh: dp: 16 (over z_lo, y), expert: 16 (over x, z_hi, core).
Axes of the slice: x: 4, y: 4, z: 8 (z_hi: 2, z_lo: 4; z = z_hi * 4 + z_lo), core: 2. Of those that a mesh axis runs over, the one named last changes fastest.
Arguments:
- tokens: bfloat16 [128, 256, 1280], P('dp'), may hold values from -288 to 288
- out_grad: bfloat16 [128, 256, 1280], P('dp'), may hold values from -6 to 6
- slot_params: bfloat16 [1280, 128], P(None, 'expert'), may hold values from -0.75 to 0.75
- w_in: bfloat16 [1280, 81920], P('dp', 'expert'), may hold values from -0.15625 to 0.15625
- w_out: bfloat16 [81920, 1280], P('expert', 'dp'), may hold values from -0.078125 to 0.078125
Outputs:
- token_grad: bfloat16 [128, 256, 1280], P('dp', 'expert')
- slot_grad: float32 [1280, 128], P(None, 'expert')
All inputs are finite; a program needn't handle non-finite values.
Results may differ from a plain program's by a relative error of at most 0.02.
Values may be sent and summed in bfloat16 or wider, within the bound.
No kernel may reach another device: no remote copies, remote signals or barrier semaphores. Data moves between devices by JAX's collectives and lax.ppermute only.
A program may use at most 128 MiB of HBM per device.

v0:
```python
import math
import jax
import jax.numpy as jnp
from jax import lax
from jax.experimental import pallas as pl
from jax.experimental.pallas import tpu as pltpu
from jax.sharding import PartitionSpec as P

F32 = jnp.float32
BF16 = jnp.bfloat16
ROOT = math.sqrt(2.0 / math.pi)


def swap(value, axis, k):
    count = lax.axis_size(axis)
    return lax.ppermute(value, axis, [(i, i ^ k) for i in range(count)])


def nt(a, b):
    return lax.dot_general(a, b, (((1,), (1,)), ((), ())), preferred_element_type=F32)


def ffn_kernel(rows_in, rows_go, *refs):
    blocks = refs[:20]
    out_own, out_far, grad_own, grad_far = refs[20:24]
    w1, w2, hid, pgr, slope, sems = refs[24:]
    me = lax.axis_index("dp")
    depth = w1.shape[0] // 16

    def place(index):
        return pl.ds(pl.multiple_of((me ^ index) * depth, 16), depth)

    copies = ([], [])
    for which, dst in ((0, w1), (1, w2)):
        for a in range(4):
            own, left, right, far1, far2 = blocks[5 * a : 5 * a + 5]
            for b, src in ((0, own.at[which]), (1, left.at[which]), (3, right.at[which]), (2, (far1, far2)[which])):
                copy = pltpu.make_async_copy(src, dst.at[place(4 * a + b)], sems.at[which * 16 + 4 * a + b])
                copy.start()
                copies[which].append(copy)
    for copy in copies[0]:
        copy.wait()

    width = w1.shape[1]
    tile = 256

    @pl.loop(0, width // tile)
    def _(t):
        cols = pl.ds(pl.multiple_of(t * tile, tile), tile)
        pre = jnp.dot(rows_in[...], w1[:, cols], preferred_element_type=F32)
        sq = pre * pre
        th = jnp.tanh(ROOT * (pre + 0.044715 * (sq * pre)))
        cdf = 0.5 * (1.0 + th)
        hid[:, cols] = (pre * cdf).astype(BF16)
        slope[:, cols] = cdf + 0.5 * pre * (1.0 - th * th) * (ROOT * (1.0 + 3 * 0.044715 * sq))

    for copy in copies[1]:
        copy.wait()

    @pl.loop(0, width // tile)
    def _(t):
        cols = pl.ds(pl.multiple_of(t * tile, tile), tile)
        hg = jnp.dot(rows_go[...], w2[:, cols], preferred_element_type=F32)
        pgr[:, cols] = (hg * slope[:, cols]).astype(BF16)

    own_rows = out_own.shape[0]

    @pl.loop(0, w1.shape[0] // tile)
    def _(t):
        cols = pl.ds(pl.multiple_of(t * tile, tile), tile)
        grad = nt(pgr[...], w1[cols, :])
        grad_own[:, cols] = grad[:own_rows]
        grad_far[:, cols] = grad[own_rows:].astype(BF16)
        out = nt(hid[...], w2[cols, :])
        out_own[:, cols] = out[:own_rows]
        out_far[:, cols] = out[own_rows:].astype(BF16)


def ffn(rows_in, rows_go, blocks, own_rows):
    rows, width = rows_in.shape
    quarter = blocks[0].shape[2]
    any_spec = pl.BlockSpec(memory_space=pl.ANY)
    vmem = pl.BlockSpec(memory_space=pltpu.VMEM)
    return pl.pallas_call(
        ffn_kernel,
        out_shape=[
            jax.ShapeDtypeStruct((own_rows, width), F32),
            jax.ShapeDtypeStruct((rows - own_rows, width), BF16),
        ]
        * 2,
        in_specs=[vmem, vmem] + [any_spec] * 20,
        out_specs=[vmem] * 4,
        scratch_shapes=[
            pltpu.VMEM((width, quarter), BF16),
            pltpu.VMEM((width, quarter), BF16),
            pltpu.VMEM((rows, quarter), BF16),
            pltpu.VMEM((rows, quarter), BF16),
            pltpu.VMEM((rows, quarter), F32),
            pltpu.SemaphoreType.DMA((32,)),
        ],
        compiler_params=pltpu.CompilerParams(vmem_limit_bytes=32 * 2**20),
        cost_estimate=pl.CostEstimate(
            flops=8 * rows * width * quarter, bytes_accessed=4 * width * quarter, transcendentals=rows * quarter
        ),
        name="ffn",
    )(rows_in, rows_go, *blocks)


def pick_rows(rows, count):
    start = lax.axis_index("expert") * rows
    col = lax.broadcasted_iota(jnp.int32, (rows, count), 1)
    row = lax.broadcasted_iota(jnp.int32, (rows, count), 0)
    return (col == row + start).astype(BF16)


def slots_kernel(table, tokens, out_grad, rows, dispatch_own, combine_own, spread):
    step = pl.program_id(0)
    own = 8
    slots = table.shape[0]
    count = tokens.shape[1]
    pick = pick_rows(16, count)
    ins, gos, disp, comb, spr = [], [], [], [], []
    for i in range(2):
        logits = nt(table[...], tokens[i])
        up = jnp.exp(logits - jnp.max(logits, axis=1, keepdims=True))
        dispatch = up / jnp.sum(up, axis=1, keepdims=True)
        down = jnp.exp(logits - jnp.max(logits, axis=0, keepdims=True))
        combine = down[:own] / jnp.sum(down, axis=0, keepdims=True)
        dispatch_b = dispatch.astype(BF16)
        ins.append(jnp.dot(dispatch_b[:16], tokens[i], preferred_element_type=F32)[:own])
        both = jnp.concatenate([combine, combine], axis=0).astype(BF16)
        gos.append(jnp.dot(both, out_grad[i], preferred_element_type=F32)[:own])
        disp.append(dispatch[:own])
        comb.append(combine)
        mine = nt(pick, dispatch_b).astype(BF16)
        image = 2 * step + i
        q = lax.broadcasted_iota(jnp.int32, (slots, 8 * slots), 0)
        col = lax.broadcasted_iota(jnp.int32, (slots, 8 * slots), 1)
        wide = (col == (q // 8) * 64 + q % 8 + image * 8).astype(BF16)
        spr.append(jnp.dot(mine, wide, preferred_element_type=F32))
    rows[0] = jnp.concatenate(ins, axis=0).astype(BF16)
    rows[1] = jnp.concatenate(gos, axis=0).astype(BF16)
    dispatch_own[...] = jnp.concatenate(disp, axis=0)
    combine_own[...] = jnp.concatenate(comb, axis=0)
    spread[...] = jnp.concatenate(spr, axis=0).astype(BF16)


def slots_call(table, tokens, out_grad):
    images, count, width = tokens.shape
    slots = table.shape[0]
    return pl.pallas_call(
        slots_kernel,
        grid=(images // 2,),
        out_shape=[
            jax.ShapeDtypeStruct((2, images * 8, width), BF16),
            jax.ShapeDtypeStruct((images * 8, count), F32),
            jax.ShapeDtypeStruct((images * 8, count), F32),
            jax.ShapeDtypeStruct((images * 16, slots * 8), BF16),
        ],
        in_specs=[
            pl.BlockSpec((slots, width), lambda i: (0, 0)),
            pl.BlockSpec((2, count, width), lambda i: (i, 0, 0)),
            pl.BlockSpec((2, count, width), lambda i: (i, 0, 0)),
        ],
        out_specs=[
            pl.BlockSpec((2, 16, width), lambda i: (0, i, 0)),
            pl.BlockSpec((16, count), lambda i: (i, 0)),
            pl.BlockSpec((16, count), lambda i: (i, 0)),
            pl.BlockSpec((32, slots * 8), lambda i: (i, 0)),
        ],
        compiler_params=pltpu.CompilerParams(vmem_limit_bytes=24 * 2**20),
        name="slots",
    )(table, tokens, out_grad)


def against_kernel(over_tokens, rows, big, weight, *outs):
    value = rows[...]
    high = value.astype(BF16)
    low = (value - high.astype(F32)).astype(BF16)
    both = jnp.concatenate([high, low], axis=0)
    prods = []
    for i in range(2):
        prod = nt(both, big[i])
        prods.append(prod[8 * i : 8 * i + 8] + prod[16 + 8 * i : 24 + 8 * i])
    prod = jnp.concatenate(prods, axis=0)
    w = weight[...]
    part = w * prod
    if over_tokens:
        outs[0][...] = w * (prod - jnp.sum(part, axis=1, keepdims=True))
    else:
        outs[0][...] = part
        step = pl.program_id(0)
        for i in range(2):
            outs[1][pl.ds(2 * step + i, 1), :] = jnp.sum(part[8 * i : 8 * i + 8], axis=0, keepdims=True)


def against(rows, big, weight, over_tokens):
    images, count, width = big.shape
    total = images * 8
    out_shape = [jax.ShapeDtypeStruct((total, count), F32)]
    out_specs = [pl.BlockSpec((16, count), lambda i: (i, 0))]
    if not over_tokens:
        out_shape.append(jax.ShapeDtypeStruct((images, count), F32))
        out_specs.append(pl.BlockSpec((images, count), lambda i: (0, 0)))
    return pl.pallas_call(
        lambda *refs: against_kernel(over_tokens, *refs),
        grid=(images // 2,),
        out_shape=out_shape,
        in_specs=[
            pl.BlockSpec((16, width), lambda i: (i, 0)),
            pl.BlockSpec((2, count, width), lambda i: (i, 0, 0)),
            pl.BlockSpec((16, count), lambda i: (i, 0)),
        ],
        out_specs=out_specs,
        compiler_params=pltpu.CompilerParams(vmem_limit_bytes=16 * 2**20),
        name="dispatch_grad" if over_tokens else "combine_grad",
    )(rows, big, weight)


def lines_kernel(grads, out):
    total, count = grads.shape
    x = nt(pick_rows(16, count), grads[...])
    x = jnp.concatenate([x] * 8, axis=0)
    row = lax.broadcasted_iota(jnp.int32, x.shape, 0)
    col = lax.broadcasted_iota(jnp.int32, x.shape, 1)
    x = jnp.where((col // 8) % 8 == row // 16, x, 0.0).astype(BF16)
    c = lax.broadcasted_iota(jnp.int32, (total, total // 8), 0)
    q = lax.broadcasted_iota(jnp.int32, (total, total // 8), 1)
    fold = ((c // 64 == q // 8) & (c % 8 == q % 8)).astype(BF16)
    out[...] = jnp.dot(x, fold, preferred_element_type=F32).astype(BF16)


def lines(grads):
    total = grads.shape[0]
    vmem = pl.BlockSpec(memory_space=pltpu.VMEM)
    return pl.pallas_call(
        lines_kernel,
        out_shape=jax.ShapeDtypeStruct((total // 8, total // 8), BF16),
        in_specs=[vmem],
        out_specs=vmem,
        compiler_params=pltpu.CompilerParams(vmem_limit_bytes=16 * 2**20),
        name="lines",
    )(grads)


def tokens_kernel(spread, rows, table, pair, one, three, two_a, two_b, pair_s, one_s, three_s, two_as, two_bs, out, held, sems):
    pieces = [
        (pair, pair_s),
        (one, one_s),
        ((two_a, two_b), (two_as, two_bs)),
        (three, three_s),
    ]
    copies = []
    size = two_a.shape[0]
    for x, sides in enumerate(pieces):
        for c, side in enumerate(sides):
            for h in range(2):
                src = side[h] if isinstance(side, tuple) else side.at[h]
                r = 4 * x + 2 * h + c
                copy = pltpu.make_async_copy(src, held.at[pl.ds(r * size, size)], sems.at[r])
                copy.start()
                copies.append(copy)
    base = jnp.dot(rows[...], table[...], preferred_element_type=F32)
    for copy in copies:
        copy.wait()
    total = base + jnp.dot(spread[...], held[...], preferred_element_type=F32)
    out[...] = total.astype(BF16)


def tokens_call(spread, rows, table, pieces):
    width = table.shape[1]
    vmem = pl.BlockSpec(memory_space=pltpu.VMEM)
    any_spec = pl.BlockSpec(memory_space=pl.ANY)
    return pl.pallas_call(
        tokens_kernel,
        out_shape=jax.ShapeDtypeStruct((spread.shape[0], width), BF16),
        in_specs=[vmem] * 3 + [any_spec] * 10,
        out_specs=vmem,
        scratch_shapes=[pltpu.VMEM((spread.shape[1], width), BF16), pltpu.SemaphoreType.DMA((16,))],
        compiler_params=pltpu.CompilerParams(vmem_limit_bytes=24 * 2**20),
        name="token_grad",
    )(spread, rows, table, *pieces)


def after(value, *earlier):
    return lax.optimization_barrier((value,) + earlier)[0]


def units_of(w_in, w_out):
    z = lax.axis_index("dp") // 4
    quarter = w_in.shape[1] // 4

    def unit(zz):
        start = zz * quarter
        return jnp.stack(
            [
                lax.dynamic_slice_in_dim(w_in, start, quarter, 1),
                lax.dynamic_slice_in_dim(w_out, start, quarter, 1),
            ]
        )

    return [unit(z ^ a) for a in range(4)]


def ring_y(unit):
    return swap(unit, "dp", 1), swap(unit, "dp", 3)


def far_y(left, right):
    return swap(right[0], "dp", 1), swap(left[1], "dp", 3)


def reduce_z(own, far):
    count = own.shape[0]
    total = own
    for a in (1, 2, 3):
        total = total + swap(far[(a - 1) * count : a * count], "dp", 4 * a).astype(F32)
    return total


def gather_x(v):
    return jnp.concatenate([v, swap(v, "expert", 4), swap(v, "expert", 8), swap(v, "expert", 12)], axis=0)


def sum_expert(v):
    v = (v + swap(v, "expert", 1)) + (swap(v, "expert", 2) + swap(v, "expert", 3))
    return (v + swap(v, "expert", 4)) + (swap(v, "expert", 8) + swap(v, "expert", 12))


def gather_expert(rows, far):
    pair = jnp.stack([rows, far])
    one = swap(pair, "expert", 4)
    three = swap(pair, "expert", 12)
    two_a = swap(three[0], "expert", 4)
    two_b = swap(one[1], "expert", 12)
    near = [pair, one, three, two_a, two_b]
    return near + [swap(v, "expert", 1) for v in near]


def per_device(tokens, out_grad, slot_params, w_in, w_out):
    images, count, width = tokens.shape
    own = slot_params.shape[1]
    params = slot_params.T

    units = units_of(w_in, w_out.T)
    l0, r0 = ring_y(units[0])
    u1 = swap(units[1], "dp", 4)
    u2 = swap(units[2], "dp", 8)
    table = jnp.concatenate([params, swap(params, "expert", 1)], axis=0)
    l0, r0, u1, u2, table = lax.optimization_barrier((l0, r0, u1, u2, table))
    u3 = swap(after(units[3], u1), "dp", 12)
    l1, r1 = ring_y(u1)
    p0, q0 = far_y(l0, r0)
    table = jnp.concatenate([table, swap(table, "expert", 2)], axis=0)
    table = gather_x(table)
    l1, r1, table = lax.optimization_barrier((l1, r1, table))
    l2, r2 = ring_y(after(u2, l1, r1))
    l1, r1, u3, p0, q0 = lax.optimization_barrier((l1, r1, u3, p0, q0))
    p1, q1 = far_y(l1, r1)

    rows, dispatch, combine, spread = slots_call(table, tokens, out_grad)
    rows = after(rows.reshape(2 * images * own, width), u3)
    z1, z2 = swap(rows, "dp", 4), swap(rows, "dp", 8)
    z3 = swap(z2, "dp", 4)
    l3, r3 = ring_y(after(u3, l2, r2, p1, q1))
    p2, q2 = far_y(l2, r2)
    l3, r3, p2, q2 = lax.optimization_barrier((l3, r3, p2, q2))
    p3, q3 = far_y(l3, r3)
    blocks = [units[0], l0, r0, p0, q0, u1, l1, r1, p1, q1, u2, l2, r2, p2, q2, u3, l3, r3, p3, q3]
    half = images * own
    rows_in = jnp.concatenate([v[:half] for v in (rows, z1, z2, z3)], axis=0)
    rows_go = jnp.concatenate([v[half:] for v in (rows, z1, z2, z3)], axis=0)

    out_own, out_far, grad_own, grad_far = ffn(rows_in, rows_go, blocks, half)
    slot_in_grad = reduce_z(grad_own, grad_far)
    slot_out = reduce_z(out_own, out_far)
    near = slot_in_grad.astype(BF16)
    far = swap(near, "expert", 2)
    pieces = gather_expert(near, far)

    part, mix = against(after(slot_out, far), out_grad, combine, False)
    mix = sum_expert(mix)
    (through,) = against(slot_in_grad, tokens, dispatch, True)
    part = after(part, pieces[1], pieces[2])
    logit_grad = through + (part - combine * jnp.repeat(mix, own, axis=0))
    logit_grad_b = logit_grad.astype(BF16)
    slot_term = jnp.einsum(
        "bsm,bmd->sd", logit_grad_b.reshape(images, own, count), tokens, preferred_element_type=F32
    )

    all_grads = jnp.concatenate([logit_grad_b, swap(logit_grad_b, "expert", 1)], axis=0)
    all_grads = jnp.concatenate([all_grads, swap(all_grads, "expert", 2)], axis=0)
    all_grads = gather_x(all_grads)

    term = slot_term.astype(BF16)
    for step in ((4, 8, 12), (1, 2, 3)):
        acc = term.astype(F32)
        for k in step:
            acc = acc + swap(term, "dp", k).astype(F32)
        term = acc.astype(BF16)
    slot_grad = acc.T

    token_grad = tokens_call(spread, lines(all_grads), table, pieces)
    return (token_grad.reshape(images, -1, width), slot_grad)


def solution(mesh):
    return jax.shard_map(
        per_device,
        mesh=mesh,
        in_specs=(
            P("dp", None, None),
            P("dp", None, None),
            P(None, "expert"),
            P("dp", "expert"),
            P("expert", "dp"),
        ),
        out_specs=(P("dp", "expert", None), P(None, "expert")),
        check_vma=False,
    )
```

profile of v0, /device:TPU:1, one launch (start us, length us, event | category | flops | bytes accessed | tf_op | source)
XLA Modules:
  0.0 234.7 jit_solution(4601551752181546410)
XLA Ops:
  0.7 1.4 dynamic-slice_bitcast_fusion.1
  2.3 3.7 %collective-permute-start.1 = (bf16[2,80,1280]{2,1,0:T(8,128)(2,1)S(1)}, bf16[2,80,1280]{2,1,0:T(8,128)(2,1)S(1)}, u32[]{:S(2)}, u32[]{:S(2)}) collective-permute-start(bf16[2,80,1280]{2,1,0:T(8,128)(2,1)S(1)} %pad_maximum_fusion.2.refs_0_), channel_id=1, source_target_pairs={{0,48},{16,32},{32,16},{48,0},{64,112},{80,96},{96,80},{112,64},{1... | collective-permute-start | bytes 1228808 | tf_op jit(solution)/shard_map/ppermute | solution.py:16
  5.9 1.1 collective-permute-start.4
  7.0 3.1 %collective-permute-start.3 = (bf16[2,80,1280]{2,1,0:T(8,128)(2,1)S(1)}, bf16[2,80,1280]{2,1,0:T(8,128)(2,1)S(1)}, u32[]{:S(2)}, u32[]{:S(2)}) collective-permute-start(bf16[2,80,1280]{2,1,0:T(8,128)(2,1)S(1)} %pad_maximum_fusion.4), channel_id=1, source_target_pairs={{0,128},{16,144},{32,160},{48,176},{64,192},{80,208},{96,224},{112... | collective-permute-start | bytes 1228808 | tf_op jit(solution)/shard_map/ppermute | solution.py:16
  10.2 1.7 collective-permute-start.2
  12.0 16.8 %collective-permute-done.3.refs_10_ = bf16[2,80,1280]{2,1,0:T(8,128)(2,1)S(1)} collective-permute-done((bf16[2,80,1280]{2,1,0:T(8,128)(2,1)S(1)}, bf16[2,80,1280]{2,1,0:T(8,128)(2,1)S(1)}, u32[]{:S(2)}, u32[]{:S(2)}) %collective-permute-start.3) | collective-permute-done | bytes 409632 | tf_op jit(solution)/shard_map/ppermute | solution.py:16
  28.8 0.8 collective-permute-start.6
  29.6 1.3 collective-permute-start.5
  30.9 5.8 %collective-permute-start.7 = (bf16[16,1280]{1,0:T(8,128)(2,1)S(1)}, bf16[16,1280]{1,0:T(8,128)(2,1)S(1)}, u32[]{:S(2)}, u32[]{:S(2)}) collective-permute-start(bf16[16,1280]{1,0:T(8,128)(2,1)S(1)} %pad_maximum_fusion.9), channel_id=1, source_target_pairs={{0,2},{1,3},{2,0},{3,1},{4,6},{5,7},{6,4},{7,5},{8,10},{9,11},{10,... | collective-permute-start | bytes 122888 | tf_op jit(solution)/shard_map/ppermute | solution.py:16
  36.7 1.4 collective-permute-done.7
  38.1 1.2 collective-permute-start.8
  39.3 2.0 collective-permute-start.13
  41.3 2.7 %collective-permute-start.11 = (bf16[2,80,1280]{2,1,0:T(8,128)(2,1)S(1)}, bf16[2,80,1280]{2,1,0:T(8,128)(2,1)S(1)}, u32[]{:S(2)}, u32[]{:S(2)}) collective-permute-start(bf16[2,80,1280]{2,1,0:T(8,128)(2,1)S(1)} %pad_maximum_fusion.5), channel_id=1, source_target_pairs={{0,192},{16,208},{32,224},{48,240},{64,128},{80,144},{96,160},{112... | collective-permute-start | bytes 1228808 | tf_op jit(solution)/shard_map/ppermute | solution.py:16
  44.1 2.5 %collective-permute-start.9 = (bf16[32,1280]{1,0:T(8,128)(2,1)S(1)}, bf16[32,1280]{1,0:T(8,128)(2,1)S(1)}, u32[]{:S(2)}, u32[]{:S(2)}) collective-permute-start(bf16[32,1280]{1,0:T(8,128)(2,1)S(1)} %get-tuple-element.94), channel_id=1, source_target_pairs={{0,8},{1,9},{2,10},{3,11},{4,12},{5,13},{6,14},{7,15},{8,0},{9,1},... | collective-permute-start | bytes 245768 | tf_op jit(solution)/shard_map/ppermute | solution.py:16
  46.5 2.3 collective-permute-done.9
  48.9 1.8 collective-permute-start.10
  50.7 3.0 %collective-permute-done.10 = bf16[32,1280]{1,0:T(8,128)(2,1)S(1)} collective-permute-done((bf16[32,1280]{1,0:T(8,128)(2,1)S(1)}, bf16[32,1280]{1,0:T(8,128)(2,1)S(1)}, u32[]{:S(2)}, u32[]{:S(2)}) %collective-permute-start.10) | collective-permute-done | bytes 81952 | tf_op jit(solution)/shard_map/ppermute | solution.py:16
  53.7 0.9 collective-permute-start.20
  54.6 0.9 collective-permute-start.19
  55.4 2.8 %collective-permute-done.12.refs_3_ = bf16[80,1280]{1,0:T(8,128)(2,1)S(1)} collective-permute-done((bf16[80,1280]{1,0:T(8,128)(2,1)S(1)}, bf16[80,1280]{1,0:T(8,128)(2,1)S(1)}, u32[]{:S(2)}, u32[]{:S(2)}) %collective-permute-start.12) | collective-permute-done | bytes 204832 | tf_op jit(solution)/shard_map/ppermute | solution.py:16
  58.3 2.5 %copy-done.1 = bf16[8,256,1280]{2,1,0:T(8,128)(2,1)S(1)} copy-done((bf16[8,256,1280]{2,1,0:T(8,128)(2,1)S(1)}, bf16[8,256,1280]{2,1,0:T(8,128)(2,1)}, u32[]{:S(2)}) %copy-start.1) | copy-done | bytes 5242904
  60.8 7.5 %slots.1 = (bf16[2,64,1280]{2,1,0:T(8,128)(2,1)S(1)}, f32[64,256]{1,0:T(8,128)S(1)}, f32[64,256]{1,0:T(8,128)S(1)}, bf16[128,1024]{1,0:T(8,128)(2,1)S(1)}) custom-call(bf16[128,1280]{1,0:T(8,128)(2,1)S(1)} %constant_dynamic-update-slice_fusion.2.table, bf16[8,256,1280]{2,1,0:T(8,128)(2,1)S(1)} %copy-done, bf16[8,256,1280]{2,1,0:T(8,128)(2,1)S(1)} %copy-done.1), custom_call_target="tpu_custom_call" | custom-call | tf_op jit(solution)/shard_map/slots/pallas_call | solution.py:151
  68.3 1.3 collective-permute-start.15
  69.7 0.9 collective-permute-start.14
  70.7 8.7 %collective-permute-done.15 = bf16[128,1280]{1,0:T(8,128)(2,1)S(1)} collective-permute-done((bf16[128,1280]{1,0:T(8,128)(2,1)S(1)}, bf16[128,1280]{1,0:T(8,128)(2,1)S(1)}, u32[]{:S(2)}, u32[]{:S(2)}) %collective-permute-start.15) | collective-permute-done | bytes 327712 | tf_op jit(solution)/shard_map/ppermute | solution.py:16
  80.3 5.3 %collective-permute-done.18.refs_9_ = bf16[80,1280]{1,0:T(8,128)(2,1)S(1)} collective-permute-done((bf16[80,1280]{1,0:T(8,128)(2,1)S(1)}, bf16[80,1280]{1,0:T(8,128)(2,1)S(1)}, u32[]{:S(2)}, u32[]{:S(2)}) %collective-permute-start.18) | collective-permute-done | bytes 204832 | tf_op jit(solution)/shard_map/ppermute | solution.py:16
  85.8 1.5 collective-permute-start.23
  87.4 2.6 %collective-permute-start.24 = (bf16[80,1280]{1,0:T(8,128)(2,1)S(1)}, bf16[80,1280]{1,0:T(8,128)(2,1)S(1)}, u32[]{:S(2)}, u32[]{:S(2)}) collective-permute-start(bf16[80,1280]{1,0:T(8,128)(2,1)S(1)} %slice_bitcast_fusion), channel_id=1, source_target_pairs={{0,48},{16,32},{32,16},{48,0},{64,112},{80,96},{96,80},{112,64},{1... | collective-permute-start | bytes 614408 | tf_op jit(solution)/shard_map/ppermute | solution.py:16
  90.0 5.1 %collective-permute-done.23.refs_13_ = bf16[80,1280]{1,0:T(8,128)(2,1)S(1)} collective-permute-done((bf16[80,1280]{1,0:T(8,128)(2,1)S(1)}, bf16[80,1280]{1,0:T(8,128)(2,1)S(1)}, u32[]{:S(2)}, u32[]{:S(2)}) %collective-permute-start.23) | collective-permute-done | bytes 204832 | tf_op jit(solution)/shard_map/ppermute | solution.py:16
  95.1 3.0 %collective-permute-done.24.refs_14_ = bf16[80,1280]{1,0:T(8,128)(2,1)S(1)} collective-permute-done((bf16[80,1280]{1,0:T(8,128)(2,1)S(1)}, bf16[80,1280]{1,0:T(8,128)(2,1)S(1)}, u32[]{:S(2)}, u32[]{:S(2)}) %collective-permute-start.24) | collective-permute-done | bytes 204832 | tf_op jit(solution)/shard_map/ppermute | solution.py:16
  98.5 6.8 %collective-permute-done.25.refs_18_ = bf16[80,1280]{1,0:T(8,128)(2,1)S(1)} collective-permute-done((bf16[80,1280]{1,0:T(8,128)(2,1)S(1)}, bf16[80,1280]{1,0:T(8,128)(2,1)S(1)}, u32[]{:S(2)}, u32[]{:S(2)}) %collective-permute-start.25) | collective-permute-done | bytes 204832 | tf_op jit(solution)/shard_map/ppermute | solution.py:16
  105.3 1.4 collective-permute-done.26.refs_19_
  106.6 16.4 %ffn.1 = (f32[64,1280]{1,0:T(8,128)S(1)}, bf16[192,1280]{1,0:T(8,128)(2,1)S(1)}, f32[64,1280]{1,0:T(8,128)S(1)}, bf16[192,1280]{1,0:T(8,128)(2,1)S(1)}) custom-call(bf16[256,1280]{1,0:T(8,128)(2,1)S(1)} %get-tuple-element.98.rows_in, bf16[256,1280]{1,0:T(8,128)(2,1)S(1)} %get-tuple-element.99.rows_go, bf16[2,80,1280]{2,1,0:T(8,128)(2,1)S(1)} %pad_maximum_fusion.2.refs_0_, ...), custom_call_target="tpu_custom_call" | custom-call | flops 3355443200 | bytes 6553600 | tf_op jit(solution)/shard_map/ffn/pallas_call | solution.py:84
  123.2 2.2 collective-permute-start.29
  125.9 1.1 collective-permute-start.30
  127.0 2.1 collective-permute-start.32
  129.1 0.9 collective-permute-done.29
  130.0 7.5 %collective-permute-done.28 = bf16[64,1280]{1,0:T(8,128)(2,1)S(1)} collective-permute-done((bf16[64,1280]{1,0:T(8,128)(2,1)S(1)}, bf16[64,1280]{1,0:T(8,128)(2,1)S(1)}, u32[]{:S(2)}, u32[]{:S(2)}) %collective-permute-start.28) | collective-permute-done | bytes 163872 | tf_op jit(solution)/shard_map/ppermute | solution.py:16
  137.5 5.4 %collective-permute-start.33 = (bf16[64,1280]{1,0:T(8,128)(2,1)S(1)}, bf16[64,1280]{1,0:T(8,128)(2,1)S(1)}, u32[]{:S(2)}, u32[]{:S(2)}) collective-permute-start(bf16[64,1280]{1,0:T(8,128)(2,1)S(1)} %get-tuple-element.70), channel_id=1, source_target_pairs={{0,2},{1,3},{2,0},{3,1},{4,6},{5,7},{6,4},{7,5},{8,10},{9,11},{10,... | collective-permute-start | bytes 491528 | tf_op jit(solution)/shard_map/ppermute | solution.py:16
  142.9 11.5 %collective-permute-done.31 = bf16[64,1280]{1,0:T(8,128)(2,1)S(1)} collective-permute-done((bf16[64,1280]{1,0:T(8,128)(2,1)S(1)}, bf16[64,1280]{1,0:T(8,128)(2,1)S(1)}, u32[]{:S(2)}, u32[]{:S(2)}) %collective-permute-start.31) | collective-permute-done | bytes 163872 | tf_op jit(solution)/shard_map/ppermute | solution.py:16
  154.5 2.1 combine_grad.1
  156.6 16.3 %collective-permute-start.38 = (f32[8,256]{1,0:T(8,128)S(1)}, f32[8,256]{1,0:T(8,128)S(1)}, u32[]{:S(2)}, u32[]{:S(2)}) collective-permute-start(f32[8,256]{1,0:T(8,128)S(1)} %get-tuple-element.67), channel_id=1, source_target_pairs={{0,3},{1,2},{2,1},{3,0},{4,7},{5,6},{6,5},{7,4},{8,11},{9,10},{10,... | collective-permute-start | bytes 24584 | tf_op jit(solution)/shard_map/ppermute | solution.py:16
  173.9 12.1 %collective-permute-start.34 = (bf16[2,64,1280]{2,1,0:T(8,128)(2,1)S(1)}, bf16[2,64,1280]{2,1,0:T(8,128)(2,1)S(1)}, u32[]{:S(2)}, u32[]{:S(2)}) collective-permute-start(bf16[2,64,1280]{2,1,0:T(8,128)(2,1)S(1)} %pad_maximum_fusion.6.pair), channel_id=1, source_target_pairs={{0,4},{1,5},{2,6},{3,7},{4,0},{5,1},{6,2},{7,3},{8,12},{9,13},{10,... | collective-permute-start | bytes 983048 | tf_op jit(solution)/shard_map/ppermute | solution.py:16
  186.0 1.0 collective-permute-start.41
  187.0 0.9 collective-permute-start.40
  187.9 1.4 collective-permute-start.39
  189.3 2.3 dispatch_grad.1
  191.6 2.9 %collective-permute-done.40 = f32[8,256]{1,0:T(8,128)S(1)} collective-permute-done((f32[8,256]{1,0:T(8,128)S(1)}, f32[8,256]{1,0:T(8,128)S(1)}, u32[]{:S(2)}, u32[]{:S(2)}) %collective-permute-start.40) | collective-permute-done | bytes 8224 | tf_op jit(solution)/shard_map/ppermute | solution.py:16
  194.6 0.8 fusion
  195.4 2.3 collective-permute-start.56
  197.7 1.2 collective-permute-start.54
  198.9 2.3 collective-permute-start.42
  201.8 1.8 collective-permute-start.48
  203.6 2.4 %collective-permute-start.59 = (bf16[8,1280]{1,0:T(8,128)(2,1)S(1)}, bf16[8,1280]{1,0:T(8,128)(2,1)S(1)}, u32[]{:S(2)}, u32[]{:S(2)}) collective-permute-start(bf16[8,1280]{1,0:T(8,128)(2,1)S(1)} %add_convert_fusion), channel_id=1, source_target_pairs={{0,48},{16,32},{32,16},{48,0},{64,112},{80,96},{96,80},{112,64},{1... | collective-permute-start | bytes 61448 | tf_op jit(solution)/shard_map/ppermute | solution.py:16
  206.2 3.4 %collective-permute-start.43 = (bf16[128,256]{1,0:T(8,128)(2,1)S(1)}, bf16[128,256]{1,0:T(8,128)(2,1)S(1)}, u32[]{:S(2)}, u32[]{:S(2)}) collective-permute-start(bf16[128,256]{1,0:T(8,128)(2,1)S(1)} %pad_maximum_fusion.8), channel_id=1, source_target_pairs={{0,2},{1,3},{2,0},{3,1},{4,6},{5,7},{6,4},{7,5},{8,10},{9,11},{10,... | collective-permute-start | bytes 196616 | tf_op jit(solution)/shard_map/ppermute | solution.py:16
  209.6 3.7 %collective-permute-done.43 = bf16[128,256]{1,0:T(8,128)(2,1)S(1)} collective-permute-done((bf16[128,256]{1,0:T(8,128)(2,1)S(1)}, bf16[128,256]{1,0:T(8,128)(2,1)S(1)}, u32[]{:S(2)}, u32[]{:S(2)}) %collective-permute-start.43) | collective-permute-done | bytes 65568 | tf_op jit(solution)/shard_map/ppermute | solution.py:16
  213.3 0.9 collective-permute-start.57
  214.3 1.6 collective-permute-done.57
  216.5 1.0 collective-permute-start.46
  217.5 0.8 collective-permute-start.45
  218.3 5.1 %collective-permute-start.49 = (bf16[2,64,1280]{2,1,0:T(8,128)(2,1)S(1)}, bf16[2,64,1280]{2,1,0:T(8,128)(2,1)S(1)}, u32[]{:S(2)}, u32[]{:S(2)}) collective-permute-start(bf16[2,64,1280]{2,1,0:T(8,128)(2,1)S(1)} %pad_maximum_fusion.6.pair), channel_id=1, source_target_pairs={{0,1},{1,0},{2,3},{3,2},{4,5},{5,4},{6,7},{7,6},{8,9},{9,8},{10,11... | collective-permute-start | bytes 983048 | tf_op jit(solution)/shard_map/ppermute | solution.py:16
  224.0 2.8 %collective-permute-start.52 = (bf16[64,1280]{1,0:T(8,128)(2,1)S(1)}, bf16[64,1280]{1,0:T(8,128)(2,1)S(1)}, u32[]{:S(2)}, u32[]{:S(2)}) collective-permute-start(bf16[64,1280]{1,0:T(8,128)(2,1)S(1)} %collective-permute-done.47.two_a), channel_id=1, source_target_pairs={{0,1},{1,0},{2,3},{3,2},{4,5},{5,4},{6,7},{7,6},{8,9},{9,8},{10,11... | collective-permute-start | bytes 491528 | tf_op jit(solution)/shard_map/ppermute | solution.py:16
  226.8 1.8 collective-permute-start.53
  229.6 4.9 %token_grad.1 = bf16[128,1280]{1,0:T(8,128)(2,1)} custom-call(bf16[128,1024]{1,0:T(8,128)(2,1)S(1)} %get-tuple-element.38.spread, bf16[128,128]{1,0:T(8,128)(2,1)S(1)} %lines.1.rows, bf16[128,1280]{1,0:T(8,128)(2,1)S(1)} %constant_dynamic-update-slice_fusion.2.table, bf16[2,64,1280]{2,1,0:T(8,128)(2,1)S(1)} %pad_maximum_fusion.6.pair, ...), custom_call_target="tpu_custom_call" | custom-call | tf_op jit(solution)/shard_map/token_grad/pallas_call | solution.py:274
  (120 shorter events, 6.8 us)
Async XLA Ops:
  0.7 5.2 %copy-start.3 = (bf16[1280,8]{0,1:T(8,128)(2,1)S(1)}, bf16[1280,8]{0,1:T(8,128)(2,1)}, u32[]{:S(2)}) copy-start(bf16[1280,8]{0,1:T(8,128)(2,1)} %param.7) | copy-start | bytes 61444
  2.1 56.1 %copy-start = (bf16[8,256,1280]{2,1,0:T(8,128)(2,1)S(1)}, bf16[8,256,1280]{2,1,0:T(8,128)(2,1)}, u32[]{:S(2)}) copy-start(bf16[8,256,1280]{2,1,0:T(8,128)(2,1)} %refs_1_.2) | copy-start | bytes 15728644
  2.3 26.5 %collective-permute-start.1 = (bf16[2,80,1280]{2,1,0:T(8,128)(2,1)S(1)}, bf16[2,80,1280]{2,1,0:T(8,128)(2,1)S(1)}, u32[]{:S(2)}, u32[]{:S(2)}) collective-permute-start(bf16[2,80,1280]{2,1,0:T(8,128)(2,1)S(1)} %pad_maximum_fusion.2.refs_0_), channel_id=1, source_target_pairs={{0,48},{16,32},{32,16},{48,0},{64,112},{80,96},{96,80},{112,64},{1... | collective-permute-start | bytes 1228808 | tf_op jit(solution)/shard_map/ppermute | solution.py:16
  5.9 22.9 %collective-permute-start = (bf16[2,80,1280]{2,1,0:T(8,128)(2,1)S(1)}, bf16[2,80,1280]{2,1,0:T(8,128)(2,1)S(1)}, u32[]{:S(2)}, u32[]{:S(2)}) collective-permute-start(bf16[2,80,1280]{2,1,0:T(8,128)(2,1)S(1)} %pad_maximum_fusion.2.refs_0_), channel_id=1, source_target_pairs={{0,16},{16,0},{32,48},{48,32},{64,80},{80,64},{96,112},{112,96},{1... | collective-permute-start | bytes 1228808 | tf_op jit(solution)/shard_map/ppermute | solution.py:16
  5.9 6.0 %collective-permute-start.4 = (bf16[8,1280]{1,0:T(8,128)(2,1)S(1)}, bf16[8,1280]{1,0:T(8,128)(2,1)S(1)}, u32[]{:S(2)}, u32[]{:S(2)}) collective-permute-start(bf16[8,1280]{1,0:T(8,128)(2,1)S(1)} %bitcast.76), channel_id=1, source_target_pairs={{0,1},{1,0},{2,3},{3,2},{4,5},{5,4},{6,7},{7,6},{8,9},{9,8},{10,11... | collective-permute-start | bytes 61448 | tf_op jit(solution)/shard_map/ppermute | solution.py:16
  7.0 21.7 %collective-permute-start.3 = (bf16[2,80,1280]{2,1,0:T(8,128)(2,1)S(1)}, bf16[2,80,1280]{2,1,0:T(8,128)(2,1)S(1)}, u32[]{:S(2)}, u32[]{:S(2)}) collective-permute-start(bf16[2,80,1280]{2,1,0:T(8,128)(2,1)S(1)} %pad_maximum_fusion.4), channel_id=1, source_target_pairs={{0,128},{16,144},{32,160},{48,176},{64,192},{80,208},{96,224},{112... | collective-permute-start | bytes 1228808 | tf_op jit(solution)/shard_map/ppermute | solution.py:16
  10.2 18.6 %collective-permute-start.2 = (bf16[2,80,1280]{2,1,0:T(8,128)(2,1)S(1)}, bf16[2,80,1280]{2,1,0:T(8,128)(2,1)S(1)}, u32[]{:S(2)}, u32[]{:S(2)}) collective-permute-start(bf16[2,80,1280]{2,1,0:T(8,128)(2,1)S(1)} %pad_maximum_fusion.3), channel_id=1, source_target_pairs={{0,64},{16,80},{32,96},{48,112},{64,0},{80,16},{96,32},{112,48},{1... | collective-permute-start | bytes 1228808 | tf_op jit(solution)/shard_map/ppermute | solution.py:16
  28.8 24.9 %collective-permute-start.6 = (bf16[2,80,1280]{2,1,0:T(8,128)(2,1)S(1)}, bf16[2,80,1280]{2,1,0:T(8,128)(2,1)S(1)}, u32[]{:S(2)}, u32[]{:S(2)}) collective-permute-start(bf16[2,80,1280]{2,1,0:T(8,128)(2,1)S(1)} %collective-permute-done.2.refs_5_), channel_id=1, source_target_pairs={{0,48},{16,32},{32,16},{48,0},{64,112},{80,96},{96,80},{112,64},{1... | collective-permute-start | bytes 1228808 | tf_op jit(solution)/shard_map/ppermute | solution.py:16
  29.6 24.1 %collective-permute-start.5 = (bf16[2,80,1280]{2,1,0:T(8,128)(2,1)S(1)}, bf16[2,80,1280]{2,1,0:T(8,128)(2,1)S(1)}, u32[]{:S(2)}, u32[]{:S(2)}) collective-permute-start(bf16[2,80,1280]{2,1,0:T(8,128)(2,1)S(1)} %collective-permute-done.2.refs_5_), channel_id=1, source_target_pairs={{0,16},{16,0},{32,48},{48,32},{64,80},{80,64},{96,112},{112,96},{1... | collective-permute-start | bytes 1228808 | tf_op jit(solution)/shard_map/ppermute | solution.py:16
  30.9 7.2 %collective-permute-start.7 = (bf16[16,1280]{1,0:T(8,128)(2,1)S(1)}, bf16[16,1280]{1,0:T(8,128)(2,1)S(1)}, u32[]{:S(2)}, u32[]{:S(2)}) collective-permute-start(bf16[16,1280]{1,0:T(8,128)(2,1)S(1)} %pad_maximum_fusion.9), channel_id=1, source_target_pairs={{0,2},{1,3},{2,0},{3,1},{4,6},{5,7},{6,4},{7,5},{8,10},{9,11},{10,... | collective-permute-start | bytes 122888 | tf_op jit(solution)/shard_map/ppermute | solution.py:16
  38.1 6.0 %collective-permute-start.8 = (bf16[32,1280]{1,0:T(8,128)(2,1)S(1)}, bf16[32,1280]{1,0:T(8,128)(2,1)S(1)}, u32[]{:S(2)}, u32[]{:S(2)}) collective-permute-start(bf16[32,1280]{1,0:T(8,128)(2,1)S(1)} %get-tuple-element.94), channel_id=1, source_target_pairs={{0,4},{1,5},{2,6},{3,7},{4,0},{5,1},{6,2},{7,3},{8,12},{9,13},{10,... | collective-permute-start | bytes 245768 | tf_op jit(solution)/shard_map/ppermute | solution.py:16
  39.3 16.1 %collective-permute-start.13 = (bf16[80,1280]{1,0:T(8,128)(2,1)S(1)}, bf16[80,1280]{1,0:T(8,128)(2,1)S(1)}, u32[]{:S(2)}, u32[]{:S(2)}) collective-permute-start(bf16[80,1280]{1,0:T(8,128)(2,1)S(1)} %slice_bitcast_fusion.6), channel_id=1, source_target_pairs={{0,48},{16,32},{32,16},{48,0},{64,112},{80,96},{96,80},{112,64},{1... | collective-permute-start | bytes 614408 | tf_op jit(solution)/shard_map/ppermute | solution.py:16
  41.3 16.9 %collective-permute-start.11 = (bf16[2,80,1280]{2,1,0:T(8,128)(2,1)S(1)}, bf16[2,80,1280]{2,1,0:T(8,128)(2,1)S(1)}, u32[]{:S(2)}, u32[]{:S(2)}) collective-permute-start(bf16[2,80,1280]{2,1,0:T(8,128)(2,1)S(1)} %pad_maximum_fusion.5), channel_id=1, source_target_pairs={{0,192},{16,208},{32,224},{48,240},{64,128},{80,144},{96,160},{112... | collective-permute-start | bytes 1228808 | tf_op jit(solution)/shard_map/ppermute | solution.py:16
  44.1 4.8 %collective-permute-start.9 = (bf16[32,1280]{1,0:T(8,128)(2,1)S(1)}, bf16[32,1280]{1,0:T(8,128)(2,1)S(1)}, u32[]{:S(2)}, u32[]{:S(2)}) collective-permute-start(bf16[32,1280]{1,0:T(8,128)(2,1)S(1)} %get-tuple-element.94), channel_id=1, source_target_pairs={{0,8},{1,9},{2,10},{3,11},{4,12},{5,13},{6,14},{7,15},{8,0},{9,1},... | collective-permute-start | bytes 245768 | tf_op jit(solution)/shard_map/ppermute | solution.py:16
  48.9 4.8 %collective-permute-start.10 = (bf16[32,1280]{1,0:T(8,128)(2,1)S(1)}, bf16[32,1280]{1,0:T(8,128)(2,1)S(1)}, u32[]{:S(2)}, u32[]{:S(2)}) collective-permute-start(bf16[32,1280]{1,0:T(8,128)(2,1)S(1)} %get-tuple-element.94), channel_id=1, source_target_pairs={{0,12},{1,13},{2,14},{3,15},{4,8},{5,9},{6,10},{7,11},{8,4},{9,5},... | collective-permute-start | bytes 245768 | tf_op jit(solution)/shard_map/ppermute | solution.py:16
  53.7 4.6 %collective-permute-start.12 = (bf16[80,1280]{1,0:T(8,128)(2,1)S(1)}, bf16[80,1280]{1,0:T(8,128)(2,1)S(1)}, u32[]{:S(2)}, u32[]{:S(2)}) collective-permute-start(bf16[80,1280]{1,0:T(8,128)(2,1)S(1)} %slice_bitcast_fusion.7), channel_id=1, source_target_pairs={{0,16},{16,0},{32,48},{48,32},{64,80},{80,64},{96,112},{112,96},{1... | collective-permute-start | bytes 614408 | tf_op jit(solution)/shard_map/ppermute | solution.py:16
  53.7 31.9 %collective-permute-start.20 = (bf16[2,80,1280]{2,1,0:T(8,128)(2,1)S(1)}, bf16[2,80,1280]{2,1,0:T(8,128)(2,1)S(1)}, u32[]{:S(2)}, u32[]{:S(2)}) collective-permute-start(bf16[2,80,1280]{2,1,0:T(8,128)(2,1)S(1)} %collective-permute-done.3.refs_10_), channel_id=1, source_target_pairs={{0,48},{16,32},{32,16},{48,0},{64,112},{80,96},{96,80},{112,64},{1... | collective-permute-start | bytes 1228808 | tf_op jit(solution)/shard_map/ppermute | solution.py:16
  54.6 31.1 %collective-permute-start.19 = (bf16[2,80,1280]{2,1,0:T(8,128)(2,1)S(1)}, bf16[2,80,1280]{2,1,0:T(8,128)(2,1)S(1)}, u32[]{:S(2)}, u32[]{:S(2)}) collective-permute-start(bf16[2,80,1280]{2,1,0:T(8,128)(2,1)S(1)} %collective-permute-done.3.refs_10_), channel_id=1, source_target_pairs={{0,16},{16,0},{32,48},{48,32},{64,80},{80,64},{96,112},{112,96},{1... | collective-permute-start | bytes 1228808 | tf_op jit(solution)/shard_map/ppermute | solution.py:16
  68.3 11.1 %collective-permute-start.15 = (bf16[128,1280]{1,0:T(8,128)(2,1)S(1)}, bf16[128,1280]{1,0:T(8,128)(2,1)S(1)}, u32[]{:S(2)}, u32[]{:S(2)}) collective-permute-start(bf16[128,1280]{1,0:T(8,128)(2,1)S(1)} %bitcast.71), channel_id=1, source_target_pairs={{0,128},{16,144},{32,160},{48,176},{64,192},{80,208},{96,224},{112... | collective-permute-start | bytes 983048 | tf_op jit(solution)/shard_map/ppermute | solution.py:16
  69.7 10.1 %collective-permute-start.14 = (bf16[128,1280]{1,0:T(8,128)(2,1)S(1)}, bf16[128,1280]{1,0:T(8,128)(2,1)S(1)}, u32[]{:S(2)}, u32[]{:S(2)}) collective-permute-start(bf16[128,1280]{1,0:T(8,128)(2,1)S(1)} %bitcast.72), channel_id=1, source_target_pairs={{0,64},{16,80},{32,96},{48,112},{64,0},{80,16},{96,32},{112,48},{1... | collective-permute-start | bytes 983048 | tf_op jit(solution)/shard_map/ppermute | solution.py:16
  70.6 9.7 %collective-permute-start.17 = (bf16[80,1280]{1,0:T(8,128)(2,1)S(1)}, bf16[80,1280]{1,0:T(8,128)(2,1)S(1)}, u32[]{:S(2)}, u32[]{:S(2)}) collective-permute-start(bf16[80,1280]{1,0:T(8,128)(2,1)S(1)} %slice_bitcast_fusion.5), channel_id=1, source_target_pairs={{0,16},{16,0},{32,48},{48,32},{64,80},{80,64},{96,112},{112,96},{1... | collective-permute-start | bytes 614408 | tf_op jit(solution)/shard_map/ppermute | solution.py:16
  79.4 6.2 %collective-permute-start.18 = (bf16[80,1280]{1,0:T(8,128)(2,1)S(1)}, bf16[80,1280]{1,0:T(8,128)(2,1)S(1)}, u32[]{:S(2)}, u32[]{:S(2)}) collective-permute-start(bf16[80,1280]{1,0:T(8,128)(2,1)S(1)} %slice_bitcast_fusion.4), channel_id=1, source_target_pairs={{0,48},{16,32},{32,16},{48,0},{64,112},{80,96},{96,80},{112,64},{1... | collective-permute-start | bytes 614408 | tf_op jit(solution)/shard_map/ppermute | solution.py:16
  79.8 10.1 %collective-permute-start.16 = (bf16[128,1280]{1,0:T(8,128)(2,1)S(1)}, bf16[128,1280]{1,0:T(8,128)(2,1)S(1)}, u32[]{:S(2)}, u32[]{:S(2)}) collective-permute-start(bf16[128,1280]{1,0:T(8,128)(2,1)S(1)} %collective-permute-done.15), channel_id=1, source_target_pairs={{0,64},{16,80},{32,96},{48,112},{64,0},{80,16},{96,32},{112,48},{1... | collective-permute-start | bytes 983048 | tf_op jit(solution)/shard_map/ppermute | solution.py:16
  85.6 12.4 %collective-permute-start.22 = (bf16[2,80,1280]{2,1,0:T(8,128)(2,1)S(1)}, bf16[2,80,1280]{2,1,0:T(8,128)(2,1)S(1)}, u32[]{:S(2)}, u32[]{:S(2)}) collective-permute-start(bf16[2,80,1280]{2,1,0:T(8,128)(2,1)S(1)} %collective-permute-done.11.refs_15_), channel_id=1, source_target_pairs={{0,48},{16,32},{32,16},{48,0},{64,112},{80,96},{96,80},{112,64},{1... | collective-permute-start | bytes 1228808 | tf_op jit(solution)/shard_map/ppermute | solution.py:16
  85.8 12.3 %collective-permute-start.21 = (bf16[2,80,1280]{2,1,0:T(8,128)(2,1)S(1)}, bf16[2,80,1280]{2,1,0:T(8,128)(2,1)S(1)}, u32[]{:S(2)}, u32[]{:S(2)}) collective-permute-start(bf16[2,80,1280]{2,1,0:T(8,128)(2,1)S(1)} %collective-permute-done.11.refs_15_), channel_id=1, source_target_pairs={{0,16},{16,0},{32,48},{48,32},{64,80},{80,64},{96,112},{112,96},{1... | collective-permute-start | bytes 1228808 | tf_op jit(solution)/shard_map/ppermute | solution.py:16
  85.8 9.3 %collective-permute-start.23 = (bf16[80,1280]{1,0:T(8,128)(2,1)S(1)}, bf16[80,1280]{1,0:T(8,128)(2,1)S(1)}, u32[]{:S(2)}, u32[]{:S(2)}) collective-permute-start(bf16[80,1280]{1,0:T(8,128)(2,1)S(1)} %slice_bitcast_fusion.1), channel_id=1, source_target_pairs={{0,16},{16,0},{32,48},{48,32},{64,80},{80,64},{96,112},{112,96},{1... | collective-permute-start | bytes 614408 | tf_op jit(solution)/shard_map/ppermute | solution.py:16
  87.4 10.7 %collective-permute-start.24 = (bf16[80,1280]{1,0:T(8,128)(2,1)S(1)}, bf16[80,1280]{1,0:T(8,128)(2,1)S(1)}, u32[]{:S(2)}, u32[]{:S(2)}) collective-permute-start(bf16[80,1280]{1,0:T(8,128)(2,1)S(1)} %slice_bitcast_fusion), channel_id=1, source_target_pairs={{0,48},{16,32},{32,16},{48,0},{64,112},{80,96},{96,80},{112,64},{1... | collective-permute-start | bytes 614408 | tf_op jit(solution)/shard_map/ppermute | solution.py:16
  98.1 7.2 %collective-permute-start.25 = (bf16[80,1280]{1,0:T(8,128)(2,1)S(1)}, bf16[80,1280]{1,0:T(8,128)(2,1)S(1)}, u32[]{:S(2)}, u32[]{:S(2)}) collective-permute-start(bf16[80,1280]{1,0:T(8,128)(2,1)S(1)} %slice_bitcast_fusion.3), channel_id=1, source_target_pairs={{0,16},{16,0},{32,48},{48,32},{64,80},{80,64},{96,112},{112,96},{1... | collective-permute-start | bytes 614408 | tf_op jit(solution)/shard_map/ppermute | solution.py:16
  98.2 8.5 %collective-permute-start.26 = (bf16[80,1280]{1,0:T(8,128)(2,1)S(1)}, bf16[80,1280]{1,0:T(8,128)(2,1)S(1)}, u32[]{:S(2)}, u32[]{:S(2)}) collective-permute-start(bf16[80,1280]{1,0:T(8,128)(2,1)S(1)} %slice_bitcast_fusion.2), channel_id=1, source_target_pairs={{0,48},{16,32},{32,16},{48,0},{64,112},{80,96},{96,80},{112,64},{1... | collective-permute-start | bytes 614408 | tf_op jit(solution)/shard_map/ppermute | solution.py:16
  106.6 47.8 %slice-start = ((s8[5242880]{0:T(1024)(128)(4,1)}), s8[4194304]{0:T(1024)(128)(4,1)S(1)}, s32[]{:S(2)}) async-start(s8[5242880]{0:T(1024)(128)(4,1)} %bitcast.68), calls=%async_computation | async-start | bytes 8388608
  106.6 47.8 %slice-start.1 = ((s8[5242880]{0:T(1024)(128)(4,1)}), s8[1048576]{0:T(1024)(128)(4,1)S(1)}, s32[]{:S(2)}) async-start(s8[5242880]{0:T(1024)(128)(4,1)} %bitcast.68), calls=%async_computation.1 | async-start | bytes 2097152
  123.1 6.0 %collective-permute-start.27 = (bf16[64,1280]{1,0:T(8,128)(2,1)S(1)}, bf16[64,1280]{1,0:T(8,128)(2,1)S(1)}, u32[]{:S(2)}, u32[]{:S(2)}) collective-permute-start(bf16[64,1280]{1,0:T(8,128)(2,1)S(1)} %get-tuple-element.83), channel_id=1, source_target_pairs={{0,64},{16,80},{32,96},{48,112},{64,0},{80,16},{96,32},{112,48},{1... | collective-permute-start | bytes 491528 | tf_op jit(solution)/shard_map/ppermute | solution.py:16
  123.2 6.8 %collective-permute-start.29 = (bf16[64,1280]{1,0:T(8,128)(2,1)S(1)}, bf16[64,1280]{1,0:T(8,128)(2,1)S(1)}, u32[]{:S(2)}, u32[]{:S(2)}) collective-permute-start(bf16[64,1280]{1,0:T(8,128)(2,1)S(1)} %get-tuple-element.84), channel_id=1, source_target_pairs={{0,192},{16,208},{32,224},{48,240},{64,128},{80,144},{96,160},{112... | collective-permute-start | bytes 491528 | tf_op jit(solution)/shard_map/ppermute | solution.py:16
  125.4 12.0 %collective-permute-start.28 = (bf16[64,1280]{1,0:T(8,128)(2,1)S(1)}, bf16[64,1280]{1,0:T(8,128)(2,1)S(1)}, u32[]{:S(2)}, u32[]{:S(2)}) collective-permute-start(bf16[64,1280]{1,0:T(8,128)(2,1)S(1)} %get-tuple-element.85), channel_id=1, source_target_pairs={{0,128},{16,144},{32,160},{48,176},{64,192},{80,208},{96,224},{112... | collective-permute-start | bytes 491528 | tf_op jit(solution)/shard_map/ppermute | solution.py:16
  125.9 17.1 %collective-permute-start.30 = (bf16[64,1280]{1,0:T(8,128)(2,1)S(1)}, bf16[64,1280]{1,0:T(8,128)(2,1)S(1)}, u32[]{:S(2)}, u32[]{:S(2)}) collective-permute-start(bf16[64,1280]{1,0:T(8,128)(2,1)S(1)} %get-tuple-element.80), channel_id=1, source_target_pairs={{0,64},{16,80},{32,96},{48,112},{64,0},{80,16},{96,32},{112,48},{1... | collective-permute-start | bytes 491528 | tf_op jit(solution)/shard_map/ppermute | solution.py:16
  127.0 16.0 %collective-permute-start.32 = (bf16[64,1280]{1,0:T(8,128)(2,1)S(1)}, bf16[64,1280]{1,0:T(8,128)(2,1)S(1)}, u32[]{:S(2)}, u32[]{:S(2)}) collective-permute-start(bf16[64,1280]{1,0:T(8,128)(2,1)S(1)} %get-tuple-element.81), channel_id=1, source_target_pairs={{0,192},{16,208},{32,224},{48,240},{64,128},{80,144},{96,160},{112... | collective-permute-start | bytes 491528 | tf_op jit(solution)/shard_map/ppermute | solution.py:16
  129.1 25.3 %collective-permute-start.31 = (bf16[64,1280]{1,0:T(8,128)(2,1)S(1)}, bf16[64,1280]{1,0:T(8,128)(2,1)S(1)}, u32[]{:S(2)}, u32[]{:S(2)}) collective-permute-start(bf16[64,1280]{1,0:T(8,128)(2,1)S(1)} %get-tuple-element.82), channel_id=1, source_target_pairs={{0,128},{16,144},{32,160},{48,176},{64,192},{80,208},{96,224},{112... | collective-permute-start | bytes 491528 | tf_op jit(solution)/shard_map/ppermute | solution.py:16
  137.5 17.0 %collective-permute-start.33 = (bf16[64,1280]{1,0:T(8,128)(2,1)S(1)}, bf16[64,1280]{1,0:T(8,128)(2,1)S(1)}, u32[]{:S(2)}, u32[]{:S(2)}) collective-permute-start(bf16[64,1280]{1,0:T(8,128)(2,1)S(1)} %get-tuple-element.70), channel_id=1, source_target_pairs={{0,2},{1,3},{2,0},{3,1},{4,6},{5,7},{6,4},{7,5},{8,10},{9,11},{10,... | collective-permute-start | bytes 491528 | tf_op jit(solution)/shard_map/ppermute | solution.py:16
  156.6 29.4 %collective-permute-start.38 = (f32[8,256]{1,0:T(8,128)S(1)}, f32[8,256]{1,0:T(8,128)S(1)}, u32[]{:S(2)}, u32[]{:S(2)}) collective-permute-start(f32[8,256]{1,0:T(8,128)S(1)} %get-tuple-element.67), channel_id=1, source_target_pairs={{0,3},{1,2},{2,1},{3,0},{4,7},{5,6},{6,5},{7,4},{8,11},{9,10},{10,... | collective-permute-start | bytes 24584 | tf_op jit(solution)/shard_map/ppermute | solution.py:16
  172.9 13.0 %collective-permute-start.37 = (f32[8,256]{1,0:T(8,128)S(1)}, f32[8,256]{1,0:T(8,128)S(1)}, u32[]{:S(2)}, u32[]{:S(2)}) collective-permute-start(f32[8,256]{1,0:T(8,128)S(1)} %get-tuple-element.67), channel_id=1, source_target_pairs={{0,2},{1,3},{2,0},{3,1},{4,6},{5,7},{6,4},{7,5},{8,10},{9,11},{10,... | collective-permute-start | bytes 24584 | tf_op jit(solution)/shard_map/ppermute | solution.py:16
  172.9 13.0 %collective-permute-start.36 = (f32[8,256]{1,0:T(8,128)S(1)}, f32[8,256]{1,0:T(8,128)S(1)}, u32[]{:S(2)}, u32[]{:S(2)}) collective-permute-start(f32[8,256]{1,0:T(8,128)S(1)} %get-tuple-element.67), channel_id=1, source_target_pairs={{0,1},{1,0},{2,3},{3,2},{4,5},{5,4},{6,7},{7,6},{8,9},{9,8},{10,11... | collective-permute-start | bytes 24584 | tf_op jit(solution)/shard_map/ppermute | solution.py:16
  173.4 21.1 %collective-permute-start.35 = (bf16[2,64,1280]{2,1,0:T(8,128)(2,1)S(1)}, bf16[2,64,1280]{2,1,0:T(8,128)(2,1)S(1)}, u32[]{:S(2)}, u32[]{:S(2)}) collective-permute-start(bf16[2,64,1280]{2,1,0:T(8,128)(2,1)S(1)} %pad_maximum_fusion.6.pair), channel_id=1, source_target_pairs={{0,12},{1,13},{2,14},{3,15},{4,8},{5,9},{6,10},{7,11},{8,4},{9,5},... | collective-permute-start | bytes 983048 | tf_op jit(solution)/shard_map/ppermute | solution.py:16
  173.9 20.7 %collective-permute-start.34 = (bf16[2,64,1280]{2,1,0:T(8,128)(2,1)S(1)}, bf16[2,64,1280]{2,1,0:T(8,128)(2,1)S(1)}, u32[]{:S(2)}, u32[]{:S(2)}) collective-permute-start(bf16[2,64,1280]{2,1,0:T(8,128)(2,1)S(1)} %pad_maximum_fusion.6.pair), channel_id=1, source_target_pairs={{0,4},{1,5},{2,6},{3,7},{4,0},{5,1},{6,2},{7,3},{8,12},{9,13},{10,... | collective-permute-start | bytes 983048 | tf_op jit(solution)/shard_map/ppermute | solution.py:16
  186.0 5.6 %collective-permute-start.41 = (f32[8,256]{1,0:T(8,128)S(1)}, f32[8,256]{1,0:T(8,128)S(1)}, u32[]{:S(2)}, u32[]{:S(2)}) collective-permute-start(f32[8,256]{1,0:T(8,128)S(1)} %add_add_fusion.1), channel_id=1, source_target_pairs={{0,12},{1,13},{2,14},{3,15},{4,8},{5,9},{6,10},{7,11},{8,4},{9,5},... | collective-permute-start | bytes 24584 | tf_op jit(solution)/shard_map/ppermute | solution.py:16
  187.0 7.6 %collective-permute-start.40 = (f32[8,256]{1,0:T(8,128)S(1)}, f32[8,256]{1,0:T(8,128)S(1)}, u32[]{:S(2)}, u32[]{:S(2)}) collective-permute-start(f32[8,256]{1,0:T(8,128)S(1)} %add_add_fusion.1), channel_id=1, source_target_pairs={{0,8},{1,9},{2,10},{3,11},{4,12},{5,13},{6,14},{7,15},{8,0},{9,1},... | collective-permute-start | bytes 24584 | tf_op jit(solution)/shard_map/ppermute | solution.py:16
  187.9 6.6 %collective-permute-start.39 = (f32[8,256]{1,0:T(8,128)S(1)}, f32[8,256]{1,0:T(8,128)S(1)}, u32[]{:S(2)}, u32[]{:S(2)}) collective-permute-start(f32[8,256]{1,0:T(8,128)S(1)} %add_add_fusion.1), channel_id=1, source_target_pairs={{0,4},{1,5},{2,6},{3,7},{4,0},{5,1},{6,2},{7,3},{8,12},{9,13},{10,... | collective-permute-start | bytes 24584 | tf_op jit(solution)/shard_map/ppermute | solution.py:16
  195.4 6.4 %collective-permute-start.56 = (bf16[8,1280]{1,0:T(8,128)(2,1)S(1)}, bf16[8,1280]{1,0:T(8,128)(2,1)S(1)}, u32[]{:S(2)}, u32[]{:S(2)}) collective-permute-start(bf16[8,1280]{1,0:T(8,128)(2,1)S(1)} %fusion), channel_id=1, source_target_pairs={{0,192},{16,208},{32,224},{48,240},{64,128},{80,144},{96,160},{112... | collective-permute-start | bytes 61448 | tf_op jit(solution)/shard_map/ppermute | solution.py:16
  197.7 5.9 %collective-permute-start.55 = (bf16[8,1280]{1,0:T(8,128)(2,1)S(1)}, bf16[8,1280]{1,0:T(8,128)(2,1)S(1)}, u32[]{:S(2)}, u32[]{:S(2)}) collective-permute-start(bf16[8,1280]{1,0:T(8,128)(2,1)S(1)} %fusion), channel_id=1, source_target_pairs={{0,128},{16,144},{32,160},{48,176},{64,192},{80,208},{96,224},{112... | collective-permute-start | bytes 61448 | tf_op jit(solution)/shard_map/ppermute | solution.py:16
  197.7 5.9 %collective-permute-start.54 = (bf16[8,1280]{1,0:T(8,128)(2,1)S(1)}, bf16[8,1280]{1,0:T(8,128)(2,1)S(1)}, u32[]{:S(2)}, u32[]{:S(2)}) collective-permute-start(bf16[8,1280]{1,0:T(8,128)(2,1)S(1)} %fusion), channel_id=1, source_target_pairs={{0,64},{16,80},{32,96},{48,112},{64,0},{80,16},{96,32},{112,48},{1... | collective-permute-start | bytes 61448 | tf_op jit(solution)/shard_map/ppermute | solution.py:16
  198.9 7.2 %collective-permute-start.42 = (bf16[64,256]{1,0:T(8,128)(2,1)S(1)}, bf16[64,256]{1,0:T(8,128)(2,1)S(1)}, u32[]{:S(2)}, u32[]{:S(2)}) collective-permute-start(bf16[64,256]{1,0:T(8,128)(2,1)S(1)} %get-tuple-element.69), channel_id=1, source_target_pairs={{0,1},{1,0},{2,3},{3,2},{4,5},{5,4},{6,7},{7,6},{8,9},{9,8},{10,11... | collective-permute-start | bytes 98312 | tf_op jit(solution)/shard_map/ppermute | solution.py:16
  201.3 17.0 %collective-permute-start.47 = (bf16[64,1280]{1,0:T(8,128)(2,1)S(1)}, bf16[64,1280]{1,0:T(8,128)(2,1)S(1)}, u32[]{:S(2)}, u32[]{:S(2)}) collective-permute-start(bf16[64,1280]{1,0:T(8,128)(2,1)S(1)} %slice_bitcast_fusion.9), channel_id=1, source_target_pairs={{0,4},{1,5},{2,6},{3,7},{4,0},{5,1},{6,2},{7,3},{8,12},{9,13},{10,... | collective-permute-start | bytes 491528 | tf_op jit(solution)/shard_map/ppermute | solution.py:16
  201.8 21.7 %collective-permute-start.48 = (bf16[64,1280]{1,0:T(8,128)(2,1)S(1)}, bf16[64,1280]{1,0:T(8,128)(2,1)S(1)}, u32[]{:S(2)}, u32[]{:S(2)}) collective-permute-start(bf16[64,1280]{1,0:T(8,128)(2,1)S(1)} %slice_bitcast_fusion.8), channel_id=1, source_target_pairs={{0,12},{1,13},{2,14},{3,15},{4,8},{5,9},{6,10},{7,11},{8,4},{9,5},... | collective-permute-start | bytes 491528 | tf_op jit(solution)/shard_map/ppermute | solution.py:16
  203.6 10.6 %collective-permute-start.59 = (bf16[8,1280]{1,0:T(8,128)(2,1)S(1)}, bf16[8,1280]{1,0:T(8,128)(2,1)S(1)}, u32[]{:S(2)}, u32[]{:S(2)}) collective-permute-start(bf16[8,1280]{1,0:T(8,128)(2,1)S(1)} %add_convert_fusion), channel_id=1, source_target_pairs={{0,48},{16,32},{32,16},{48,0},{64,112},{80,96},{96,80},{112,64},{1... | collective-permute-start | bytes 61448 | tf_op jit(solution)/shard_map/ppermute | solution.py:16
  206.1 8.3 %collective-permute-start.58 = (bf16[8,1280]{1,0:T(8,128)(2,1)S(1)}, bf16[8,1280]{1,0:T(8,128)(2,1)S(1)}, u32[]{:S(2)}, u32[]{:S(2)}) collective-permute-start(bf16[8,1280]{1,0:T(8,128)(2,1)S(1)} %add_convert_fusion), channel_id=1, source_target_pairs={{0,32},{16,48},{32,0},{48,16},{64,96},{80,112},{96,64},{112,80},{1... | collective-permute-start | bytes 61448 | tf_op jit(solution)/shard_map/ppermute | solution.py:16
  206.2 7.1 %collective-permute-start.43 = (bf16[128,256]{1,0:T(8,128)(2,1)S(1)}, bf16[128,256]{1,0:T(8,128)(2,1)S(1)}, u32[]{:S(2)}, u32[]{:S(2)}) collective-permute-start(bf16[128,256]{1,0:T(8,128)(2,1)S(1)} %pad_maximum_fusion.8), channel_id=1, source_target_pairs={{0,2},{1,3},{2,0},{3,1},{4,6},{5,7},{6,4},{7,5},{8,10},{9,11},{10,... | collective-permute-start | bytes 196616 | tf_op jit(solution)/shard_map/ppermute | solution.py:16
  213.3 2.6 %collective-permute-start.57 = (bf16[8,1280]{1,0:T(8,128)(2,1)S(1)}, bf16[8,1280]{1,0:T(8,128)(2,1)S(1)}, u32[]{:S(2)}, u32[]{:S(2)}) collective-permute-start(bf16[8,1280]{1,0:T(8,128)(2,1)S(1)} %add_convert_fusion), channel_id=1, source_target_pairs={{0,16},{16,0},{32,48},{48,32},{64,80},{80,64},{96,112},{112,96},{1... | collective-permute-start | bytes 61448 | tf_op jit(solution)/shard_map/ppermute | solution.py:16
  214.2 9.4 %collective-permute-start.44 = (bf16[256,256]{1,0:T(8,128)(2,1)S(1)}, bf16[256,256]{1,0:T(8,128)(2,1)S(1)}, u32[]{:S(2)}, u32[]{:S(2)}) collective-permute-start(bf16[256,256]{1,0:T(8,128)(2,1)S(1)} %pad_maximum_fusion.7), channel_id=1, source_target_pairs={{0,4},{1,5},{2,6},{3,7},{4,0},{5,1},{6,2},{7,3},{8,12},{9,13},{10,... | collective-permute-start | bytes 393224 | tf_op jit(solution)/shard_map/ppermute | solution.py:16
  216.5 7.5 %collective-permute-start.46 = (bf16[256,256]{1,0:T(8,128)(2,1)S(1)}, bf16[256,256]{1,0:T(8,128)(2,1)S(1)}, u32[]{:S(2)}, u32[]{:S(2)}) collective-permute-start(bf16[256,256]{1,0:T(8,128)(2,1)S(1)} %pad_maximum_fusion.7), channel_id=1, source_target_pairs={{0,12},{1,13},{2,14},{3,15},{4,8},{5,9},{6,10},{7,11},{8,4},{9,5},... | collective-permute-start | bytes 393224 | tf_op jit(solution)/shard_map/ppermute | solution.py:16
  217.5 9.3 %collective-permute-start.45 = (bf16[256,256]{1,0:T(8,128)(2,1)S(1)}, bf16[256,256]{1,0:T(8,128)(2,1)S(1)}, u32[]{:S(2)}, u32[]{:S(2)}) collective-permute-start(bf16[256,256]{1,0:T(8,128)(2,1)S(1)} %pad_maximum_fusion.7), channel_id=1, source_target_pairs={{0,8},{1,9},{2,10},{3,11},{4,12},{5,13},{6,14},{7,15},{8,0},{9,1},... | collective-permute-start | bytes 393224 | tf_op jit(solution)/shard_map/ppermute | solution.py:16
  218.3 10.7 %collective-permute-start.49 = (bf16[2,64,1280]{2,1,0:T(8,128)(2,1)S(1)}, bf16[2,64,1280]{2,1,0:T(8,128)(2,1)S(1)}, u32[]{:S(2)}, u32[]{:S(2)}) collective-permute-start(bf16[2,64,1280]{2,1,0:T(8,128)(2,1)S(1)} %pad_maximum_fusion.6.pair), channel_id=1, source_target_pairs={{0,1},{1,0},{2,3},{3,2},{4,5},{5,4},{6,7},{7,6},{8,9},{9,8},{10,11... | collective-permute-start | bytes 983048 | tf_op jit(solution)/shard_map/ppermute | solution.py:16
  223.5 5.6 %collective-permute-start.51 = (bf16[2,64,1280]{2,1,0:T(8,128)(2,1)S(1)}, bf16[2,64,1280]{2,1,0:T(8,128)(2,1)S(1)}, u32[]{:S(2)}, u32[]{:S(2)}) collective-permute-start(bf16[2,64,1280]{2,1,0:T(8,128)(2,1)S(1)} %collective-permute-done.35.three), channel_id=1, source_target_pairs={{0,1},{1,0},{2,3},{3,2},{4,5},{5,4},{6,7},{7,6},{8,9},{9,8},{10,11... | collective-permute-start | bytes 983048 | tf_op jit(solution)/shard_map/ppermute | solution.py:16
  223.6 5.5 %collective-permute-start.50 = (bf16[2,64,1280]{2,1,0:T(8,128)(2,1)S(1)}, bf16[2,64,1280]{2,1,0:T(8,128)(2,1)S(1)}, u32[]{:S(2)}, u32[]{:S(2)}) collective-permute-start(bf16[2,64,1280]{2,1,0:T(8,128)(2,1)S(1)} %collective-permute-done.34.one), channel_id=1, source_target_pairs={{0,1},{1,0},{2,3},{3,2},{4,5},{5,4},{6,7},{7,6},{8,9},{9,8},{10,11... | collective-permute-start | bytes 983048 | tf_op jit(solution)/shard_map/ppermute | solution.py:16
  224.0 5.1 %collective-permute-start.52 = (bf16[64,1280]{1,0:T(8,128)(2,1)S(1)}, bf16[64,1280]{1,0:T(8,128)(2,1)S(1)}, u32[]{:S(2)}, u32[]{:S(2)}) collective-permute-start(bf16[64,1280]{1,0:T(8,128)(2,1)S(1)} %collective-permute-done.47.two_a), channel_id=1, source_target_pairs={{0,1},{1,0},{2,3},{3,2},{4,5},{5,4},{6,7},{7,6},{8,9},{9,8},{10,11... | collective-permute-start | bytes 491528 | tf_op jit(solution)/shard_map/ppermute | solution.py:16
  226.8 2.8 %collective-permute-start.53 = (bf16[64,1280]{1,0:T(8,128)(2,1)S(1)}, bf16[64,1280]{1,0:T(8,128)(2,1)S(1)}, u32[]{:S(2)}, u32[]{:S(2)}) collective-permute-start(bf16[64,1280]{1,0:T(8,128)(2,1)S(1)} %collective-permute-done.48.two_b), channel_id=1, source_target_pairs={{0,1},{1,0},{2,3},{3,2},{4,5},{5,4},{6,7},{7,6},{8,9},{9,8},{10,11... | collective-permute-start | bytes 491528 | tf_op jit(solution)/shard_map/ppermute | solution.py:16
  (2 other events, 4.0 us)
where the time goes:
time: 239 us; the launch traced here: 235 us
  starting transfers between devices  108 us (45%)
  waiting for transfers between devices  85.2 us (36%)
  Pallas kernels  33.6 us (14%)
  local copies, waits for them, and re-layouts  4.39 us (2%)
    ppermute x60, starting transfers between devices, swap(): return lax.ppermute(value, axis, [(i, i ^ k) for i in range(count)])  108 us
    ppermute x60, waiting for transfers between devices, swap(): return lax.ppermute(value, axis, [(i, i ^ k) for i in range(count)])  85.2 us
    pallas_call x1, Pallas kernels, ffn(): pl.pallas_call(ffn_kernel, out_shape=[jax.ShapeDtypeStruct((own_rows, wid...  16.4 us
    pallas_call x1, Pallas kernels, slots_call(): pl.pallas_call(slots_kernel, grid=(images // 2,), out_shape=[jax.ShapeDty...  7.55 us
    pallas_call x1, Pallas kernels, tokens_call(): pl.pallas_call(tokens_kernel, out_shape=jax.ShapeDtypeStruct((spread.shap...  4.85 us
  transfers between devices with their start and end apart: 60, of which 18 were waited for; matrix products, arithmetic and copies ran while one was open for 1% of the time, Pallas kernels for 4%

commit v1 on v0

v1 whole, which is shorter than its diff:
```python
import math
import jax
import jax.numpy as jnp
from jax import lax
from jax.experimental import pallas as pl
from jax.experimental.pallas import tpu as pltpu
from jax.sharding import PartitionSpec as P

F32 = jnp.float32
BF16 = jnp.bfloat16
ROOT = math.sqrt(2.0 / math.pi)


def swap(value, axis, k):
    count = lax.axis_size(axis)
    return lax.ppermute(value, axis, [(i, i ^ k) for i in range(count)])


def nt(a, b):
    return lax.dot_general(a, b, (((1,), (1,)), ((), ())), preferred_element_type=F32)


def ffn_kernel(rows_in, rows_go, *refs):
    own, l0, r0, f0, both, lb, rb, pb, qb, last, l3, r3, f3 = refs[:13]
    out_own, out_far, grad_own, grad_far = refs[13:17]
    w1, w2 = refs[17:]
    me = lax.axis_index("dp")
    depth = w1.shape[0] // 16

    def place(which, dst):
        for a, sources in (
            (0, (own.at[which], l0.at[which], f0.at[which], r0.at[which])),
            (3, (last.at[which], l3.at[which], f3.at[which], r3.at[which])),
            (1, (both.at[which, 0], lb.at[which, 0], (pb, qb)[which].at[0], rb.at[which, 0])),
            (2, (both.at[which, 1], lb.at[which, 1], (pb, qb)[which].at[1], rb.at[which, 1])),
        ):
            for b, src in enumerate(sources):
                start = pl.multiple_of((me ^ (4 * a + b)) * depth, 16)
                dst[pl.ds(start, depth), :] = src[...]

    place(0, w1)
    place(1, w2)
    pre = jnp.dot(rows_in[...], w1[...], preferred_element_type=F32)
    sq = pre * pre
    th = jnp.tanh(ROOT * (pre + 0.044715 * (sq * pre)))
    cdf = 0.5 * (1.0 + th)
    hidden = (pre * cdf).astype(BF16)
    slope = cdf + 0.5 * pre * (1.0 - th * th) * (ROOT * (1.0 + 3 * 0.044715 * sq))
    hidden_grad = jnp.dot(rows_go[...], w2[...], preferred_element_type=F32)
    pre_grad = (hidden_grad * slope).astype(BF16)
    own_rows = out_own.shape[0]
    grad = nt(pre_grad, w1[...])
    grad_own[...] = grad[:own_rows]
    grad_far[...] = grad[own_rows:].astype(BF16)
    out = nt(hidden, w2[...])
    out_own[...] = out[:own_rows]
    out_far[...] = out[own_rows:].astype(BF16)


def ffn(rows_in, rows_go, blocks, own_rows):
    rows, width = rows_in.shape
    quarter = blocks[0].shape[2]
    vmem = pl.BlockSpec(memory_space=pltpu.VMEM)
    return pl.pallas_call(
        ffn_kernel,
        out_shape=[
            jax.ShapeDtypeStruct((own_rows, width), F32),
            jax.ShapeDtypeStruct((rows - own_rows, width), BF16),
        ]
        * 2,
        in_specs=[vmem] * (2 + len(blocks)),
        out_specs=[vmem] * 4,
        scratch_shapes=[pltpu.VMEM((width, quarter), BF16), pltpu.VMEM((width, quarter), BF16)],
        compiler_params=pltpu.CompilerParams(vmem_limit_bytes=40 * 2**20),
        name="ffn",
    )(rows_in, rows_go, *blocks)


def pick_rows(count):
    col = lax.broadcasted_iota(jnp.int32, (32, count), 1)
    row = lax.broadcasted_iota(jnp.int32, (32, count), 0)
    owner = lax.axis_index("expert") ^ (row // 16)
    return (col == owner * 16 + row % 16).astype(BF16)


def slots_kernel(table, tokens, out_grad, rows, dispatch_own, combine_own, spread):
    step = pl.program_id(0)
    own = 8
    near = table.shape[0] // 2
    count = tokens.shape[1]
    pick = pick_rows(count)
    ins, gos, disp, comb, mine, theirs = [], [], [], [], [], []
    for i in range(2):
        logits = nt(table[...], tokens[i])
        up = jnp.exp(logits[:near] - jnp.max(logits[:near], axis=1, keepdims=True))
        dispatch = up / jnp.sum(up, axis=1, keepdims=True)
        down = jnp.exp(logits - jnp.max(logits, axis=0, keepdims=True))
        combine = down[:own] / jnp.sum(down, axis=0, keepdims=True)
        dispatch_b = dispatch.astype(BF16)
        ins.append(jnp.dot(dispatch_b[:16], tokens[i], preferred_element_type=F32)[:own])
        both = jnp.concatenate([combine, combine], axis=0).astype(BF16)
        gos.append(jnp.dot(both, out_grad[i], preferred_element_type=F32)[:own])
        disp.append(dispatch[:own])
        comb.append(combine)
        lines = nt(pick, dispatch_b).astype(BF16)
        image = 2 * step + i
        q = lax.broadcasted_iota(jnp.int32, (near, 8 * near), 0)
        col = lax.broadcasted_iota(jnp.int32, (near, 8 * near), 1)
        wide = (col == (q // 8) * 64 + q % 8 + image * 8).astype(BF16)
        lines = jnp.dot(lines, wide, preferred_element_type=F32)
        mine.append(lines[:16])
        theirs.append(lines[16:])
    rows[0] = jnp.concatenate(ins, axis=0).astype(BF16)
    rows[1] = jnp.concatenate(gos, axis=0).astype(BF16)
    dispatch_own[...] = jnp.concatenate(disp, axis=0)
    combine_own[...] = jnp.concatenate(comb, axis=0)
    spread[0] = jnp.concatenate(mine, axis=0).astype(BF16)
    spread[1] = jnp.concatenate(theirs, axis=0).astype(BF16)


def slots_call(table, tokens, out_grad):
    images, count, width = tokens.shape
    slots = table.shape[0]
    return pl.pallas_call(
        slots_kernel,
        grid=(images // 2,),
        out_shape=[
            jax.ShapeDtypeStruct((2, images * 8, width), BF16),
            jax.ShapeDtypeStruct((images * 8, count), F32),
            jax.ShapeDtypeStruct((images * 8, count), F32),
            jax.ShapeDtypeStruct((2, images * 16, slots * 4), BF16),
        ],
        in_specs=[
            pl.BlockSpec((slots, width), lambda i: (0, 0)),
            pl.BlockSpec((2, count, width), lambda i: (i, 0, 0)),
            pl.BlockSpec((2, count, width), lambda i: (i, 0, 0)),
        ],
        out_specs=[
            pl.BlockSpec((2, 16, width), lambda i: (0, i, 0)),
            pl.BlockSpec((16, count), lambda i: (i, 0)),
            pl.BlockSpec((16, count), lambda i: (i, 0)),
            pl.BlockSpec((2, 32, slots * 4), lambda i: (0, i, 0)),
        ],
        compiler_params=pltpu.CompilerParams(vmem_limit_bytes=24 * 2**20),
        name="slots",
    )(table, tokens, out_grad)


def against_kernel(over_tokens, rows, big, weight, *outs):
    value = rows[...]
    high = value.astype(BF16)
    low = (value - high.astype(F32)).astype(BF16)
    both = jnp.concatenate([high, low], axis=0)
    prods = []
    for i in range(2):
        prod = nt(both, big[i])
        prods.append(prod[8 * i : 8 * i + 8] + prod[16 + 8 * i : 24 + 8 * i])
    prod = jnp.concatenate(prods, axis=0)
    w = weight[...]
    part = w * prod
    if over_tokens:
        outs[0][...] = w * (prod - jnp.sum(part, axis=1, keepdims=True))
    else:
        outs[0][...] = part
        step = pl.program_id(0)
        for i in range(2):
            outs[1][pl.ds(2 * step + i, 1), :] = jnp.sum(part[8 * i : 8 * i + 8], axis=0, keepdims=True)


def against(rows, big, weight, over_tokens):
    images, count, width = big.shape
    total = images * 8
    out_shape = [jax.ShapeDtypeStruct((total, count), F32)]
    out_specs = [pl.BlockSpec((16, count), lambda i: (i, 0))]
    if not over_tokens:
        out_shape.append(jax.ShapeDtypeStruct((images, count), F32))
        out_specs.append(pl.BlockSpec((images, count), lambda i: (0, 0)))
    return pl.pallas_call(
        lambda *refs: against_kernel(over_tokens, *refs),
        grid=(images // 2,),
        out_shape=out_shape,
        in_specs=[
            pl.BlockSpec((16, width), lambda i: (i, 0)),
            pl.BlockSpec((2, count, width), lambda i: (i, 0, 0)),
            pl.BlockSpec((16, count), lambda i: (i, 0)),
        ],
        out_specs=out_specs,
        compiler_params=pltpu.CompilerParams(vmem_limit_bytes=16 * 2**20),
        name="dispatch_grad" if over_tokens else "combine_grad",
    )(rows, big, weight)


def spread_kernel(spread, pair, one, two, three, out):
    side = spread[...].reshape(2 * spread.shape[1], spread.shape[2])
    depth = side.shape[1] // 4
    total = jnp.zeros(out.shape, F32)
    for x, piece in enumerate((pair, one, two, three)):
        block = piece[...].reshape(depth, piece.shape[2])
        total = total + jnp.dot(side[:, x * depth : (x + 1) * depth], block, preferred_element_type=F32)
    out[...] = total


def spread_call(spread, pieces):
    width = pieces[0].shape[2]
    vmem = pl.BlockSpec(memory_space=pltpu.VMEM)
    return pl.pallas_call(
        spread_kernel,
        out_shape=jax.ShapeDtypeStruct((2 * spread.shape[1], width), F32),
        in_specs=[vmem] * 5,
        out_specs=vmem,
        compiler_params=pltpu.CompilerParams(vmem_limit_bytes=24 * 2**20),
        name="through_slots",
    )(spread, *pieces)


def lines_kernel(pair, one, two, three, table, through, mine, theirs):
    count = pair.shape[1]
    grads = jnp.concatenate([pair[...], one[...], two[...], three[...]], axis=0)
    total = grads.shape[0]
    near = total // 8
    c = lax.broadcasted_iota(jnp.int32, (total, near), 0)
    q = lax.broadcasted_iota(jnp.int32, (total, near), 1)
    fold = ((c // 64 == q // 8) & (c % 8 == q % 8)).astype(BF16)
    x = nt(pick_rows(count), grads)
    half = through.shape[0] // 2
    parts = []
    for side in range(2):
        y = jnp.concatenate([x[16 * side : 16 * side + 16]] * 8, axis=0)
        row = lax.broadcasted_iota(jnp.int32, y.shape, 0)
        col = lax.broadcasted_iota(jnp.int32, y.shape, 1)
        y = jnp.where((col // 8) % 8 == row // 16, y, 0.0).astype(BF16)
        parts.append(jnp.dot(y, fold, preferred_element_type=F32).astype(BF16))
    lines = jnp.concatenate(parts, axis=0)
    sums = through[...] + jnp.dot(lines, table[:near], preferred_element_type=F32)
    mine[...] = sums[:half]
    theirs[...] = sums[half:]


def lines_call(pieces, table, through):
    vmem = pl.BlockSpec(memory_space=pltpu.VMEM)
    half = through.shape[0] // 2
    return pl.pallas_call(
        lines_kernel,
        out_shape=[jax.ShapeDtypeStruct((half, through.shape[1]), F32)] * 2,
        in_specs=[vmem] * 6,
        out_specs=[vmem] * 2,
        compiler_params=pltpu.CompilerParams(vmem_limit_bytes=24 * 2**20),
        name="through_logits",
    )(*pieces, table, through)


def after(value, *earlier):
    return lax.optimization_barrier((value,) + earlier)[0]


def units_of(w_in, w_out):
    z = lax.axis_index("dp") // 4
    quarter = w_in.shape[1] // 4

    def unit(zz):
        start = zz * quarter
        return jnp.stack(
            [
                lax.dynamic_slice_in_dim(w_in, start, quarter, 1),
                lax.dynamic_slice_in_dim(w_out, start, quarter, 1),
            ]
        )

    return [unit(z ^ a) for a in range(4)]


def all_y(unit):
    return swap(unit, "dp", 1), swap(unit, "dp", 3), swap(unit, "dp", 2)


def reduce_z(own, far):
    count = own.shape[0]
    total = own
    for a in (1, 2, 3):
        total = total + swap(far[(a - 1) * count : a * count], "dp", 4 * a).astype(F32)
    return total


def all_x(v):
    return [v, swap(v, "expert", 4), swap(v, "expert", 8), swap(v, "expert", 12)]


def sum_expert(v):
    v = (v + swap(v, "expert", 1)) + (swap(v, "expert", 2) + swap(v, "expert", 3))
    return (v + swap(v, "expert", 4)) + (swap(v, "expert", 8) + swap(v, "expert", 12))


def per_device(tokens, out_grad, slot_params, w_in, w_out):
    images, count, width = tokens.shape
    own = slot_params.shape[1]
    half = images * own
    params = slot_params.T

    units = units_of(w_in, w_out.T)
    l0, r0 = swap(units[0], "dp", 1), swap(units[0], "dp", 3)
    u1 = swap(units[1], "dp", 4)
    u2 = swap(units[2], "dp", 8)
    table = jnp.concatenate([params, swap(params, "expert", 2)], axis=0)
    table = jnp.concatenate(all_x(table), axis=0)
    l0, r0, table = lax.optimization_barrier((l0, r0, table))
    p0, q0 = swap(r0[0], "dp", 1), swap(l0[1], "dp", 3)
    table = jnp.concatenate([table, swap(table, "expert", 1)], axis=0)

    u1, u2, p0, q0, table = lax.optimization_barrier((u1, u2, p0, q0, table))
    both = jnp.stack([u1, u2], axis=1)
    lb, rb = swap(both, "dp", 1), swap(both, "dp", 3)
    u3 = swap(after(units[3], u1), "dp", 12)

    rows, dispatch, combine, spread = slots_call(table, tokens, out_grad)
    rows = rows.reshape(2 * half, width)

    lb, rb, rows = lax.optimization_barrier((lb, rb, rows))
    pb, qb = swap(rb[0], "dp", 1), swap(lb[1], "dp", 3)
    z1, z2, z3 = swap(rows, "dp", 4), swap(rows, "dp", 8), swap(rows, "dp", 12)
    u3 = after(u3, lb, rb)
    l3, r3, f3 = all_y(u3)
    rows_in = jnp.concatenate([v[:half] for v in (rows, z1, z2, z3)], axis=0)
    rows_go = jnp.concatenate([v[half:] for v in (rows, z1, z2, z3)], axis=0)

    f0 = jnp.stack([p0, q0])
    blocks = [units[0], l0, r0, f0, both, lb, rb, pb, qb, u3, l3, r3, f3]
    out_own, out_far, grad_own, grad_far = ffn(rows_in, rows_go, blocks, half)
    slot_in_grad = reduce_z(grad_own, grad_far)
    slot_out = reduce_z(out_own, out_far)

    near = slot_in_grad.astype(BF16)
    far = swap(near, "expert", 2)
    pieces = all_x(jnp.stack([near, far]))
    through = spread_call(spread, pieces)

    part, mix = against(after(slot_out, far), out_grad, combine, False)
    mix = sum_expert(mix)
    (back,) = against(slot_in_grad, tokens, dispatch, True)
    part = after(part, *pieces)
    logit_grad = back + (part - combine * jnp.repeat(mix, own, axis=0))
    logit_grad_b = logit_grad.astype(BF16)
    slot_term = jnp.einsum(
        "bsm,bmd->sd", logit_grad_b.reshape(images, own, count), tokens, preferred_element_type=F32
    )
    line = jnp.concatenate([logit_grad_b, swap(logit_grad_b, "expert", 2)], axis=0)
    mine, theirs = lines_call(all_x(line), table, through)

    term = slot_term.astype(BF16)
    for step in ((4, 8, 12), (1, 2, 3)):
        acc = term.astype(F32)
        for k in step:
            acc = acc + swap(term, "dp", k).astype(F32)
        term = acc.astype(BF16)
    slot_grad = acc.T

    token_grad = (mine + swap(theirs, "expert", 1)).astype(BF16)
    return (token_grad.reshape(images, -1, width), slot_grad)


def solution(mesh):
    return jax.shard_map(
        per_device,
        mesh=mesh,
        in_specs=(
            P("dp", None, None),
            P("dp", None, None),
            P(None, "expert"),
            P("dp", "expert"),
            P("expert", "dp"),
        ),
        out_specs=(P("dp", "expert", None), P(None, "expert")),
        check_vma=False,
    )
```

time: 239 us -> 204 us (0.85); the launches traced: 235 us -> 203 us
  starting transfers between devices: 108 us -> 84.3 us
  Pallas kernels: 33.6 us -> 19 us
  waiting for transfers between devices: 85.2 us -> 91.5 us
    ppermute x60 -> x49, starting transfers between devices: 108 us -> 84.3 us  [swap(): return lax.ppermute(value, axis, [(i, i ^ k) for i in range(count)])]
    pallas_call x1, Pallas kernels: 16.4 us -> 3.99 us  [ffn(): pl.pallas_call(ffn_kernel, out_shape=[jax.ShapeDtypeStruct((own_rows, wid...]
    ppermute x60 -> x49, waiting for transfers between devices: 85.2 us -> 91.5 us  [swap(): return lax.ppermute(value, axis, [(i, i ^ k) for i in range(count)])]
    pallas_call x2, Pallas kernels: 5.26 us -> 1.52 us  [the longest x1 0.82 us: spread_call(): pl.pallas_call(spread_kernel, out_shape=jax.ShapeDtypeStruct((2 * spread....]
  transfers between devices with their start and end apart: 60 -> 49, of which waited for: 18 -> 17; matrix products, arithmetic and copies ran while one was open for 1% -> 1% of each run, Pallas kernels for 4% -> 6%
where the time goes in v1:
time: 204 us; the launch traced here: 203 us
  waiting for transfers between devices  91.5 us (45%)
  starting transfers between devices  84.3 us (41%)
  Pallas kernels  19 us (9%)
  local copies, waits for them, and re-layouts  4.28 us (2%)
  other arithmetic  2.04 us (1%)
    ppermute x49, waiting for transfers between devices, swap(): return lax.ppermute(value, axis, [(i, i ^ k) for i in range(count)])  91.5 us
    ppermute x49, starting transfers between devices, swap(): return lax.ppermute(value, axis, [(i, i ^ k) for i in range(count)])  84.3 us
    pallas_call x1, Pallas kernels, slots_call(): pl.pallas_call(slots_kernel, grid=(images // 2,), out_shape=[jax.ShapeDty...  9.18 us
    pallas_call x2, Pallas kernels, against(): pl.pallas_call(lambda *refs: against_kernel(over_tokens, *refs), grid=(im...  4.36 us
  transfers between devices with their start and end apart: 49, of which 17 were waited for; matrix products, arithmetic and copies ran while one was open for 1% of the time, Pallas kernels for 6%

profile of v1, /device:TPU:1, one launch (start us, length us, event | category | flops | bytes accessed | tf_op | source)
XLA Modules:
  0.0 203.0 jit_solution(13233532694303854455)
XLA Ops:
  0.7 1.4 dynamic-slice_bitcast_fusion.1
  2.3 3.7 %collective-permute-start.3 = (bf16[2,80,1280]{2,1,0:T(8,128)(2,1)S(1)}, bf16[2,80,1280]{2,1,0:T(8,128)(2,1)S(1)}, u32[]{:S(2)}, u32[]{:S(2)}) collective-permute-start(bf16[2,80,1280]{2,1,0:T(8,128)(2,1)S(1)} %pad_maximum_fusion.5.refs_0_), channel_id=1, source_target_pairs={{0,48},{16,32},{32,16},{48,0},{64,112},{80,96},{96,80},{112,64},{1... | collective-permute-start | bytes 1228808 | tf_op jit(solution)/shard_map/ppermute | solution.py:16
  5.9 6.9 %collective-permute-start.4 = (bf16[8,1280]{1,0:T(8,128)(2,1)S(1)}, bf16[8,1280]{1,0:T(8,128)(2,1)S(1)}, u32[]{:S(2)}, u32[]{:S(2)}) collective-permute-start(bf16[8,1280]{1,0:T(8,128)(2,1)S(1)} %bitcast.73), channel_id=1, source_target_pairs={{0,2},{1,3},{2,0},{3,1},{4,6},{5,7},{6,4},{7,5},{8,10},{9,11},{10,... | collective-permute-start | bytes 61448 | tf_op jit(solution)/shard_map/ppermute | solution.py:16
  12.9 0.8 collective-permute-start
  13.7 1.3 collective-permute-start.1
  15.0 1.3 collective-permute-start.5
  16.3 1.6 collective-permute-done.5
  18.0 2.7 %collective-permute-start.6 = (bf16[16,1280]{1,0:T(8,128)(2,1)S(1)}, bf16[16,1280]{1,0:T(8,128)(2,1)S(1)}, u32[]{:S(2)}, u32[]{:S(2)}) collective-permute-start(bf16[16,1280]{1,0:T(8,128)(2,1)S(1)} %pad_maximum_fusion.11), channel_id=1, source_target_pairs={{0,8},{1,9},{2,10},{3,11},{4,12},{5,13},{6,14},{7,15},{8,0},{9,1},... | collective-permute-start | bytes 122888 | tf_op jit(solution)/shard_map/ppermute | solution.py:16
  20.7 1.8 collective-permute-done.6
  22.5 2.3 %collective-permute-start.7 = (bf16[16,1280]{1,0:T(8,128)(2,1)S(1)}, bf16[16,1280]{1,0:T(8,128)(2,1)S(1)}, u32[]{:S(2)}, u32[]{:S(2)}) collective-permute-start(bf16[16,1280]{1,0:T(8,128)(2,1)S(1)} %pad_maximum_fusion.11), channel_id=1, source_target_pairs={{0,12},{1,13},{2,14},{3,15},{4,8},{5,9},{6,10},{7,11},{8,4},{9,5},... | collective-permute-start | bytes 122888 | tf_op jit(solution)/shard_map/ppermute | solution.py:16
  24.8 1.9 collective-permute-done.7
  26.7 5.1 %collective-permute-start.10 = (bf16[64,1280]{1,0:T(8,128)(2,1)S(1)}, bf16[64,1280]{1,0:T(8,128)(2,1)S(1)}, u32[]{:S(2)}, u32[]{:S(2)}) collective-permute-start(bf16[64,1280]{1,0:T(8,128)(2,1)S(1)} %constant_dynamic-update-slice_fusion), channel_id=1, source_target_pairs={{0,1},{1,0},{2,3},{3,2},{4,5},{5,4},{6,7},{7,6},{8,9},{9,8},{10,11... | collective-permute-start | bytes 491528 | tf_op jit(solution)/shard_map/ppermute | solution.py:16
  31.9 0.9 collective-permute-start.9
  32.8 0.9 collective-permute-start.8
  33.8 6.1 %collective-permute-done.9 = bf16[80,1280]{1,0:T(8,128)(2,1)S(1)} collective-permute-done((bf16[80,1280]{1,0:T(8,128)(2,1)S(1)}, bf16[80,1280]{1,0:T(8,128)(2,1)S(1)}, u32[]{:S(2)}, u32[]{:S(2)}) %collective-permute-start.9) | collective-permute-done | bytes 204832 | tf_op jit(solution)/shard_map/ppermute | solution.py:16
  40.0 1.2 collective-permute-start.12
  41.7 2.4 %collective-permute-start.18 = (bf16[2,80,1280]{2,1,0:T(8,128)(2,1)S(1)}, bf16[2,80,1280]{2,1,0:T(8,128)(2,1)S(1)}, u32[]{:S(2)}, u32[]{:S(2)}) collective-permute-start(bf16[2,80,1280]{2,1,0:T(8,128)(2,1)S(1)} %pad_maximum_fusion.7), channel_id=1, source_target_pairs={{0,192},{16,208},{32,224},{48,240},{64,128},{80,144},{96,160},{112... | collective-permute-start | bytes 1228808 | tf_op jit(solution)/shard_map/ppermute | solution.py:16
  44.1 2.5 %copy-done.1 = bf16[8,256,1280]{2,1,0:T(8,128)(2,1)S(1)} copy-done((bf16[8,256,1280]{2,1,0:T(8,128)(2,1)S(1)}, bf16[8,256,1280]{2,1,0:T(8,128)(2,1)}, u32[]{:S(2)}) %copy-start.1) | copy-done | bytes 5242904
  46.6 9.2 %slots.1 = (bf16[2,64,1280]{2,1,0:T(8,128)(2,1)S(1)}, f32[64,256]{1,0:T(8,128)S(1)}, f32[64,256]{1,0:T(8,128)S(1)}, bf16[2,128,512]{2,1,0:T(8,128)(2,1)S(1)}) custom-call(bf16[128,1280]{1,0:T(8,128)(2,1)S(1)} %pad_maximum_fusion.8.table, bf16[8,256,1280]{2,1,0:T(8,128)(2,1)S(1)} %copy-done, bf16[8,256,1280]{2,1,0:T(8,128)(2,1)S(1)} %copy-done.1), custom_call_target="tpu_custom_call" | custom-call | tf_op jit(solution)/shard_map/slots/pallas_call | solution.py:124
  55.8 4.4 %collective-permute-done.12.refs_6_ = bf16[2,2,80,1280]{3,2,1,0:T(8,128)(2,1)S(1)} collective-permute-done((bf16[2,2,80,1280]{3,2,1,0:T(8,128)(2,1)S(1)}, bf16[2,2,80,1280]{3,2,1,0:T(8,128)(2,1)S(1)}, u32[]{:S(2)}, u32[]{:S(2)}) %collective-permute-start.12) | collective-permute-done | bytes 819232 | tf_op jit(solution)/shard_map/ppermute | solution.py:16
  60.3 2.3 %collective-permute-start.15 = (bf16[128,1280]{1,0:T(8,128)(2,1)S(1)}, bf16[128,1280]{1,0:T(8,128)(2,1)S(1)}, u32[]{:S(2)}, u32[]{:S(2)}) collective-permute-start(bf16[128,1280]{1,0:T(8,128)(2,1)S(1)} %bitcast.62), channel_id=1, source_target_pairs={{0,192},{16,208},{32,224},{48,240},{64,128},{80,144},{96,160},{112... | collective-permute-start | bytes 983048 | tf_op jit(solution)/shard_map/ppermute | solution.py:16
  62.6 1.2 collective-permute-start.13
  63.9 1.1 collective-permute-start.21
  65.0 1.1 collective-permute-start.20
  66.1 3.6 %collective-permute-done.15 = bf16[128,1280]{1,0:T(8,128)(2,1)S(1)} collective-permute-done((bf16[128,1280]{1,0:T(8,128)(2,1)S(1)}, bf16[128,1280]{1,0:T(8,128)(2,1)S(1)}, u32[]{:S(2)}, u32[]{:S(2)}) %collective-permute-start.15) | collective-permute-done | bytes 327712 | tf_op jit(solution)/shard_map/ppermute | solution.py:16
  69.7 20.2 %collective-permute-done.14 = bf16[128,1280]{1,0:T(8,128)(2,1)S(1)} collective-permute-done((bf16[128,1280]{1,0:T(8,128)(2,1)S(1)}, bf16[128,1280]{1,0:T(8,128)(2,1)S(1)}, u32[]{:S(2)}, u32[]{:S(2)}) %collective-permute-start.14) | collective-permute-done | bytes 327712 | tf_op jit(solution)/shard_map/ppermute | solution.py:16
  90.0 0.5 collective-permute-start.16
  90.5 1.6 collective-permute-start.17
  92.2 6.8 %collective-permute-done.16.refs_7_ = bf16[2,80,1280]{2,1,0:T(8,128)(2,1)S(1)} collective-permute-done((bf16[2,80,1280]{2,1,0:T(8,128)(2,1)S(1)}, bf16[2,80,1280]{2,1,0:T(8,128)(2,1)S(1)}, u32[]{:S(2)}, u32[]{:S(2)}) %collective-permute-start.16) | collective-permute-done | bytes 409632 | tf_op jit(solution)/shard_map/ppermute | solution.py:16
  99.0 2.0 collective-permute-done.17.refs_8_
  101.1 4.0 %ffn.1 = (f32[64,1280]{1,0:T(8,128)S(1)}, bf16[192,1280]{1,0:T(8,128)(2,1)S(1)}, f32[64,1280]{1,0:T(8,128)S(1)}, bf16[192,1280]{1,0:T(8,128)(2,1)S(1)}) custom-call(bf16[256,1280]{1,0:T(8,128)(2,1)S(1)} %get-tuple-element.80.rows_in, bf16[256,1280]{1,0:T(8,128)(2,1)S(1)} %get-tuple-element.81.rows_go, bf16[2,80,1280]{2,1,0:T(8,128)(2,1)S(1)} %pad_maximum_fusion.5.refs_0_, ...), custom_call_target="tpu_custom_call" | custom-call | tf_op jit(solution)/shard_map/ffn/pallas_call | solution.py:64
  105.2 0.9 collective-permute-start.24
  106.1 1.8 collective-permute-start.23
  107.9 1.1 collective-permute-start.25
  109.0 0.8 collective-permute-start.27
  109.8 0.9 collective-permute-start.26
  110.6 0.8 collective-permute-done.24
  111.5 13.7 %collective-permute-done.23 = bf16[64,1280]{1,0:T(8,128)(2,1)S(1)} collective-permute-done((bf16[64,1280]{1,0:T(8,128)(2,1)S(1)}, bf16[64,1280]{1,0:T(8,128)(2,1)S(1)}, u32[]{:S(2)}, u32[]{:S(2)}) %collective-permute-start.23) | collective-permute-done | bytes 163872 | tf_op jit(solution)/shard_map/ppermute | solution.py:16
  125.3 4.5 %collective-permute-start.28 = (bf16[64,1280]{1,0:T(8,128)(2,1)S(1)}, bf16[64,1280]{1,0:T(8,128)(2,1)S(1)}, u32[]{:S(2)}, u32[]{:S(2)}) collective-permute-start(bf16[64,1280]{1,0:T(8,128)(2,1)S(1)} %get-tuple-element.56), channel_id=1, source_target_pairs={{0,2},{1,3},{2,0},{3,1},{4,6},{5,7},{6,4},{7,5},{8,10},{9,11},{10,... | collective-permute-start | bytes 491528 | tf_op jit(solution)/shard_map/ppermute | solution.py:16
  129.7 9.7 %collective-permute-done.26 = bf16[64,1280]{1,0:T(8,128)(2,1)S(1)} collective-permute-done((bf16[64,1280]{1,0:T(8,128)(2,1)S(1)}, bf16[64,1280]{1,0:T(8,128)(2,1)S(1)}, u32[]{:S(2)}, u32[]{:S(2)}) %collective-permute-start.26) | collective-permute-done | bytes 163872 | tf_op jit(solution)/shard_map/ppermute | solution.py:16
  139.5 2.1 %combine_grad.1 = (f32[64,256]{1,0:T(8,128)S(1)}, f32[8,256]{1,0:T(8,128)S(1)}) custom-call(f32[64,1280]{1,0:T(8,128)S(1)} %convert_add_fusion.refs_0_, bf16[8,256,1280]{2,1,0:T(8,128)(2,1)S(1)} %bitcast.61, f32[64,256]{1,0:T(8,128)S(1)} %get-tuple-element.49.refs_2_), custom_call_target="tpu_custom_call" | custom-call | tf_op jit(solution)/shard_map/combine_grad/pallas_call | solution.py:178
  141.6 9.7 %collective-permute-start.34 = (f32[8,256]{1,0:T(8,128)S(1)}, f32[8,256]{1,0:T(8,128)S(1)}, u32[]{:S(2)}, u32[]{:S(2)}) collective-permute-start(f32[8,256]{1,0:T(8,128)S(1)} %get-tuple-element.52), channel_id=1, source_target_pairs={{0,3},{1,2},{2,1},{3,0},{4,7},{5,6},{6,5},{7,4},{8,11},{9,10},{10,... | collective-permute-start | bytes 24584 | tf_op jit(solution)/shard_map/ppermute | solution.py:16
  151.3 2.7 %collective-permute-start.33 = (f32[8,256]{1,0:T(8,128)S(1)}, f32[8,256]{1,0:T(8,128)S(1)}, u32[]{:S(2)}, u32[]{:S(2)}) collective-permute-start(f32[8,256]{1,0:T(8,128)S(1)} %get-tuple-element.52), channel_id=1, source_target_pairs={{0,2},{1,3},{2,0},{3,1},{4,6},{5,7},{6,4},{7,5},{8,10},{9,11},{10,... | collective-permute-start | bytes 24584 | tf_op jit(solution)/shard_map/ppermute | solution.py:16
  154.0 3.8 %collective-permute-start.31 = (bf16[2,64,1280]{2,1,0:T(8,128)(2,1)S(1)}, bf16[2,64,1280]{2,1,0:T(8,128)(2,1)S(1)}, u32[]{:S(2)}, u32[]{:S(2)}) collective-permute-start(bf16[2,64,1280]{2,1,0:T(8,128)(2,1)S(1)} %pad_maximum_fusion.9.pair), channel_id=1, source_target_pairs={{0,12},{1,13},{2,14},{3,15},{4,8},{5,9},{6,10},{7,11},{8,4},{9,5},... | collective-permute-start | bytes 983048 | tf_op jit(solution)/shard_map/ppermute | solution.py:16
  157.8 0.9 collective-permute-start.29
  158.8 2.4 %collective-permute-start.37 = (f32[8,256]{1,0:T(8,128)S(1)}, f32[8,256]{1,0:T(8,128)S(1)}, u32[]{:S(2)}, u32[]{:S(2)}) collective-permute-start(f32[8,256]{1,0:T(8,128)S(1)} %add_add_fusion.1), channel_id=1, source_target_pairs={{0,12},{1,13},{2,14},{3,15},{4,8},{5,9},{6,10},{7,11},{8,4},{9,5},... | collective-permute-start | bytes 24584 | tf_op jit(solution)/shard_map/ppermute | solution.py:16
  161.2 11.5 %collective-permute-done.37 = f32[8,256]{1,0:T(8,128)S(1)} collective-permute-done((f32[8,256]{1,0:T(8,128)S(1)}, f32[8,256]{1,0:T(8,128)S(1)}, u32[]{:S(2)}, u32[]{:S(2)}) %collective-permute-start.37) | collective-permute-done | bytes 8224 | tf_op jit(solution)/shard_map/ppermute | solution.py:16
  172.7 2.3 %dispatch_grad.1 = f32[64,256]{1,0:T(8,128)S(1)} custom-call(f32[64,1280]{1,0:T(8,128)S(1)} %get-tuple-element.57.refs_0_, bf16[8,256,1280]{2,1,0:T(8,128)(2,1)S(1)} %copy-done, f32[64,256]{1,0:T(8,128)S(1)} %get-tuple-element.45.refs_2_), custom_call_target="tpu_custom_call" | custom-call | tf_op jit(solution)/shard_map/dispatch_grad/pallas_call | solution.py:178
  175.5 2.0 %collective-permute-start.38 = (bf16[64,256]{1,0:T(8,128)(2,1)S(1)}, bf16[64,256]{1,0:T(8,128)(2,1)S(1)}, u32[]{:S(2)}, u32[]{:S(2)}) collective-permute-start(bf16[64,256]{1,0:T(8,128)(2,1)S(1)} %fusion.3), channel_id=1, source_target_pairs={{0,2},{1,3},{2,0},{3,1},{4,6},{5,7},{6,4},{7,5},{8,10},{9,11},{10,... | collective-permute-start | bytes 98312 | tf_op jit(solution)/shard_map/ppermute | solution.py:16
  177.6 4.7 %collective-permute-done.38 = bf16[64,256]{1,0:T(8,128)(2,1)S(1)} collective-permute-done((bf16[64,256]{1,0:T(8,128)(2,1)S(1)}, bf16[64,256]{1,0:T(8,128)(2,1)S(1)}, u32[]{:S(2)}, u32[]{:S(2)}) %collective-permute-start.38) | collective-permute-done | bytes 32800 | tf_op jit(solution)/shard_map/ppermute | solution.py:16
  182.3 2.3 %collective-permute-start.41 = (bf16[128,256]{1,0:T(8,128)(2,1)S(1)}, bf16[128,256]{1,0:T(8,128)(2,1)S(1)}, u32[]{:S(2)}, u32[]{:S(2)}) collective-permute-start(bf16[128,256]{1,0:T(8,128)(2,1)S(1)} %pad_maximum_fusion.10.pair), channel_id=1, source_target_pairs={{0,12},{1,13},{2,14},{3,15},{4,8},{5,9},{6,10},{7,11},{8,4},{9,5},... | collective-permute-start | bytes 196616 | tf_op jit(solution)/shard_map/ppermute | solution.py:16
  184.6 1.1 collective-permute-start.40
  185.7 0.8 fusion
  186.5 1.8 collective-permute-start.44
  188.2 1.8 collective-permute-start.43
  190.0 0.8 through_slots.1.through
  190.9 0.7 through_logits.1
  191.6 4.7 %collective-permute-start.42 = (f32[128,1280]{1,0:T(8,128)S(1)}, f32[128,1280]{1,0:T(8,128)S(1)}, u32[]{:S(2)}, u32[]{:S(2)}) collective-permute-start(f32[128,1280]{1,0:T(8,128)S(1)} %get-tuple-element.55), channel_id=1, source_target_pairs={{0,1},{1,0},{2,3},{3,2},{4,5},{5,4},{6,7},{7,6},{8,9},{9,8},{10,11... | collective-permute-start | bytes 1966088 | tf_op jit(solution)/shard_map/ppermute | solution.py:16
  196.3 1.1 collective-permute-start.48
  197.6 2.0 collective-permute-start.46
  199.6 0.6 collective-permute-done.48
  200.2 1.3 collective-permute-done.47
  201.5 0.6 add_bitcast_fusion
  202.2 0.8 add_convert_fusion
  (90 shorter events, 2.4 us)
Async XLA Ops:
  0.6 1.5 copy-start.2
  2.1 3.8 %copy-start.3 = (bf16[1280,8]{0,1:T(8,128)(2,1)S(1)}, bf16[1280,8]{0,1:T(8,128)(2,1)}, u32[]{:S(2)}) copy-start(bf16[1280,8]{0,1:T(8,128)(2,1)} %param.7) | copy-start | bytes 61444
  2.3 24.5 %collective-permute-start.3 = (bf16[2,80,1280]{2,1,0:T(8,128)(2,1)S(1)}, bf16[2,80,1280]{2,1,0:T(8,128)(2,1)S(1)}, u32[]{:S(2)}, u32[]{:S(2)}) collective-permute-start(bf16[2,80,1280]{2,1,0:T(8,128)(2,1)S(1)} %pad_maximum_fusion.5.refs_0_), channel_id=1, source_target_pairs={{0,48},{16,32},{32,16},{48,0},{64,112},{80,96},{96,80},{112,64},{1... | collective-permute-start | bytes 1228808 | tf_op jit(solution)/shard_map/ppermute | solution.py:16
  5.9 20.8 %collective-permute-start.2 = (bf16[2,80,1280]{2,1,0:T(8,128)(2,1)S(1)}, bf16[2,80,1280]{2,1,0:T(8,128)(2,1)S(1)}, u32[]{:S(2)}, u32[]{:S(2)}) collective-permute-start(bf16[2,80,1280]{2,1,0:T(8,128)(2,1)S(1)} %pad_maximum_fusion.5.refs_0_), channel_id=1, source_target_pairs={{0,16},{16,0},{32,48},{48,32},{64,80},{80,64},{96,112},{112,96},{1... | collective-permute-start | bytes 1228808 | tf_op jit(solution)/shard_map/ppermute | solution.py:16
  5.9 9.1 %collective-permute-start.4 = (bf16[8,1280]{1,0:T(8,128)(2,1)S(1)}, bf16[8,1280]{1,0:T(8,128)(2,1)S(1)}, u32[]{:S(2)}, u32[]{:S(2)}) collective-permute-start(bf16[8,1280]{1,0:T(8,128)(2,1)S(1)} %bitcast.73), channel_id=1, source_target_pairs={{0,2},{1,3},{2,0},{3,1},{4,6},{5,7},{6,4},{7,5},{8,10},{9,11},{10,... | collective-permute-start | bytes 61448 | tf_op jit(solution)/shard_map/ppermute | solution.py:16
  12.8 31.3 %copy-start = (bf16[8,256,1280]{2,1,0:T(8,128)(2,1)S(1)}, bf16[8,256,1280]{2,1,0:T(8,128)(2,1)}, u32[]{:S(2)}) copy-start(bf16[8,256,1280]{2,1,0:T(8,128)(2,1)} %refs_1_.2) | copy-start | bytes 15728644
  12.9 20.9 %collective-permute-start = (bf16[2,80,1280]{2,1,0:T(8,128)(2,1)S(1)}, bf16[2,80,1280]{2,1,0:T(8,128)(2,1)S(1)}, u32[]{:S(2)}, u32[]{:S(2)}) collective-permute-start(bf16[2,80,1280]{2,1,0:T(8,128)(2,1)S(1)} %pad_maximum_fusion.3), channel_id=1, source_target_pairs={{0,64},{16,80},{32,96},{48,112},{64,0},{80,16},{96,32},{112,48},{1... | collective-permute-start | bytes 1228808 | tf_op jit(solution)/shard_map/ppermute | solution.py:16
  13.7 20.0 %collective-permute-start.1 = (bf16[2,80,1280]{2,1,0:T(8,128)(2,1)S(1)}, bf16[2,80,1280]{2,1,0:T(8,128)(2,1)S(1)}, u32[]{:S(2)}, u32[]{:S(2)}) collective-permute-start(bf16[2,80,1280]{2,1,0:T(8,128)(2,1)S(1)} %pad_maximum_fusion.4), channel_id=1, source_target_pairs={{0,128},{16,144},{32,160},{48,176},{64,192},{80,208},{96,224},{112... | collective-permute-start | bytes 1228808 | tf_op jit(solution)/shard_map/ppermute | solution.py:16
  15.0 2.9 %collective-permute-start.5 = (bf16[16,1280]{1,0:T(8,128)(2,1)S(1)}, bf16[16,1280]{1,0:T(8,128)(2,1)S(1)}, u32[]{:S(2)}, u32[]{:S(2)}) collective-permute-start(bf16[16,1280]{1,0:T(8,128)(2,1)S(1)} %pad_maximum_fusion.11), channel_id=1, source_target_pairs={{0,4},{1,5},{2,6},{3,7},{4,0},{5,1},{6,2},{7,3},{8,12},{9,13},{10,... | collective-permute-start | bytes 122888 | tf_op jit(solution)/shard_map/ppermute | solution.py:16
  18.0 4.6 %collective-permute-start.6 = (bf16[16,1280]{1,0:T(8,128)(2,1)S(1)}, bf16[16,1280]{1,0:T(8,128)(2,1)S(1)}, u32[]{:S(2)}, u32[]{:S(2)}) collective-permute-start(bf16[16,1280]{1,0:T(8,128)(2,1)S(1)} %pad_maximum_fusion.11), channel_id=1, source_target_pairs={{0,8},{1,9},{2,10},{3,11},{4,12},{5,13},{6,14},{7,15},{8,0},{9,1},... | collective-permute-start | bytes 122888 | tf_op jit(solution)/shard_map/ppermute | solution.py:16
  22.5 4.2 %collective-permute-start.7 = (bf16[16,1280]{1,0:T(8,128)(2,1)S(1)}, bf16[16,1280]{1,0:T(8,128)(2,1)S(1)}, u32[]{:S(2)}, u32[]{:S(2)}) collective-permute-start(bf16[16,1280]{1,0:T(8,128)(2,1)S(1)} %pad_maximum_fusion.11), channel_id=1, source_target_pairs={{0,12},{1,13},{2,14},{3,15},{4,8},{5,9},{6,10},{7,11},{8,4},{9,5},... | collective-permute-start | bytes 122888 | tf_op jit(solution)/shard_map/ppermute | solution.py:16
  26.7 7.0 %collective-permute-start.10 = (bf16[64,1280]{1,0:T(8,128)(2,1)S(1)}, bf16[64,1280]{1,0:T(8,128)(2,1)S(1)}, u32[]{:S(2)}, u32[]{:S(2)}) collective-permute-start(bf16[64,1280]{1,0:T(8,128)(2,1)S(1)} %constant_dynamic-update-slice_fusion), channel_id=1, source_target_pairs={{0,1},{1,0},{2,3},{3,2},{4,5},{5,4},{6,7},{7,6},{8,9},{9,8},{10,11... | collective-permute-start | bytes 491528 | tf_op jit(solution)/shard_map/ppermute | solution.py:16
  31.9 8.0 %collective-permute-start.9 = (bf16[80,1280]{1,0:T(8,128)(2,1)S(1)}, bf16[80,1280]{1,0:T(8,128)(2,1)S(1)}, u32[]{:S(2)}, u32[]{:S(2)}) collective-permute-start(bf16[80,1280]{1,0:T(8,128)(2,1)S(1)} %slice_bitcast_fusion.2), channel_id=1, source_target_pairs={{0,48},{16,32},{32,16},{48,0},{64,112},{80,96},{96,80},{112,64},{1... | collective-permute-start | bytes 614408 | tf_op jit(solution)/shard_map/ppermute | solution.py:16
  32.8 7.1 %collective-permute-start.8 = (bf16[80,1280]{1,0:T(8,128)(2,1)S(1)}, bf16[80,1280]{1,0:T(8,128)(2,1)S(1)}, u32[]{:S(2)}, u32[]{:S(2)}) collective-permute-start(bf16[80,1280]{1,0:T(8,128)(2,1)S(1)} %slice_bitcast_fusion.3), channel_id=1, source_target_pairs={{0,16},{16,0},{32,48},{48,32},{64,80},{80,64},{96,112},{112,96},{1... | collective-permute-start | bytes 614408 | tf_op jit(solution)/shard_map/ppermute | solution.py:16
  40.0 20.3 %collective-permute-start.12 = (bf16[2,2,80,1280]{3,2,1,0:T(8,128)(2,1)S(1)}, bf16[2,2,80,1280]{3,2,1,0:T(8,128)(2,1)S(1)}, u32[]{:S(2)}, u32[]{:S(2)}) collective-permute-start(bf16[2,2,80,1280]{3,2,1,0:T(8,128)(2,1)S(1)} %pad_maximum_fusion.refs_4_), channel_id=1, source_target_pairs={{0,48},{16,32},{32,16},{48,0},{64,112},{80,96},{96,80},{112,64},{1... | collective-permute-start | bytes 2457608 | tf_op jit(solution)/shard_map/ppermute | solution.py:16
  41.2 19.0 %collective-permute-start.11 = (bf16[2,2,80,1280]{3,2,1,0:T(8,128)(2,1)S(1)}, bf16[2,2,80,1280]{3,2,1,0:T(8,128)(2,1)S(1)}, u32[]{:S(2)}, u32[]{:S(2)}) collective-permute-start(bf16[2,2,80,1280]{3,2,1,0:T(8,128)(2,1)S(1)} %pad_maximum_fusion.refs_4_), channel_id=1, source_target_pairs={{0,16},{16,0},{32,48},{48,32},{64,80},{80,64},{96,112},{112,96},{1... | collective-permute-start | bytes 2457608 | tf_op jit(solution)/shard_map/ppermute | solution.py:16
  41.7 22.2 %collective-permute-start.18 = (bf16[2,80,1280]{2,1,0:T(8,128)(2,1)S(1)}, bf16[2,80,1280]{2,1,0:T(8,128)(2,1)S(1)}, u32[]{:S(2)}, u32[]{:S(2)}) collective-permute-start(bf16[2,80,1280]{2,1,0:T(8,128)(2,1)S(1)} %pad_maximum_fusion.7), channel_id=1, source_target_pairs={{0,192},{16,208},{32,224},{48,240},{64,128},{80,144},{96,160},{112... | collective-permute-start | bytes 1228808 | tf_op jit(solution)/shard_map/ppermute | solution.py:16
  44.1 2.5 %copy-start.1 = (bf16[8,256,1280]{2,1,0:T(8,128)(2,1)S(1)}, bf16[8,256,1280]{2,1,0:T(8,128)(2,1)}, u32[]{:S(2)}) copy-start(bf16[8,256,1280]{2,1,0:T(8,128)(2,1)} %refs_1_.3) | copy-start | bytes 15728644
  60.3 9.4 %collective-permute-start.15 = (bf16[128,1280]{1,0:T(8,128)(2,1)S(1)}, bf16[128,1280]{1,0:T(8,128)(2,1)S(1)}, u32[]{:S(2)}, u32[]{:S(2)}) collective-permute-start(bf16[128,1280]{1,0:T(8,128)(2,1)S(1)} %bitcast.62), channel_id=1, source_target_pairs={{0,192},{16,208},{32,224},{48,240},{64,128},{80,144},{96,160},{112... | collective-permute-start | bytes 983048 | tf_op jit(solution)/shard_map/ppermute | solution.py:16
  62.6 27.4 %collective-permute-start.14 = (bf16[128,1280]{1,0:T(8,128)(2,1)S(1)}, bf16[128,1280]{1,0:T(8,128)(2,1)S(1)}, u32[]{:S(2)}, u32[]{:S(2)}) collective-permute-start(bf16[128,1280]{1,0:T(8,128)(2,1)S(1)} %bitcast.63), channel_id=1, source_target_pairs={{0,128},{16,144},{32,160},{48,176},{64,192},{80,208},{96,224},{112... | collective-permute-start | bytes 983048 | tf_op jit(solution)/shard_map/ppermute | solution.py:16
  62.6 27.9 %collective-permute-start.13 = (bf16[128,1280]{1,0:T(8,128)(2,1)S(1)}, bf16[128,1280]{1,0:T(8,128)(2,1)S(1)}, u32[]{:S(2)}, u32[]{:S(2)}) collective-permute-start(bf16[128,1280]{1,0:T(8,128)(2,1)S(1)} %bitcast.64), channel_id=1, source_target_pairs={{0,64},{16,80},{32,96},{48,112},{64,0},{80,16},{96,32},{112,48},{1... | collective-permute-start | bytes 983048 | tf_op jit(solution)/shard_map/ppermute | solution.py:16
  63.9 37.1 %collective-permute-start.21 = (bf16[2,80,1280]{2,1,0:T(8,128)(2,1)S(1)}, bf16[2,80,1280]{2,1,0:T(8,128)(2,1)S(1)}, u32[]{:S(2)}, u32[]{:S(2)}) collective-permute-start(bf16[2,80,1280]{2,1,0:T(8,128)(2,1)S(1)} %collective-permute-done.18.refs_9_), channel_id=1, source_target_pairs={{0,32},{16,48},{32,0},{48,16},{64,96},{80,112},{96,64},{112,80},{1... | collective-permute-start | bytes 1228808 | tf_op jit(solution)/shard_map/ppermute | solution.py:16
  65.0 36.1 %collective-permute-start.20 = (bf16[2,80,1280]{2,1,0:T(8,128)(2,1)S(1)}, bf16[2,80,1280]{2,1,0:T(8,128)(2,1)S(1)}, u32[]{:S(2)}, u32[]{:S(2)}) collective-permute-start(bf16[2,80,1280]{2,1,0:T(8,128)(2,1)S(1)} %collective-permute-done.18.refs_9_), channel_id=1, source_target_pairs={{0,48},{16,32},{32,16},{48,0},{64,112},{80,96},{96,80},{112,64},{1... | collective-permute-start | bytes 1228808 | tf_op jit(solution)/shard_map/ppermute | solution.py:16
  69.7 31.3 %collective-permute-start.19 = (bf16[2,80,1280]{2,1,0:T(8,128)(2,1)S(1)}, bf16[2,80,1280]{2,1,0:T(8,128)(2,1)S(1)}, u32[]{:S(2)}, u32[]{:S(2)}) collective-permute-start(bf16[2,80,1280]{2,1,0:T(8,128)(2,1)S(1)} %collective-permute-done.18.refs_9_), channel_id=1, source_target_pairs={{0,16},{16,0},{32,48},{48,32},{64,80},{80,64},{96,112},{112,96},{1... | collective-permute-start | bytes 1228808 | tf_op jit(solution)/shard_map/ppermute | solution.py:16
  90.0 9.0 %collective-permute-start.16 = (bf16[2,80,1280]{2,1,0:T(8,128)(2,1)S(1)}, bf16[2,80,1280]{2,1,0:T(8,128)(2,1)S(1)}, u32[]{:S(2)}, u32[]{:S(2)}) collective-permute-start(bf16[2,80,1280]{2,1,0:T(8,128)(2,1)S(1)} %slice_bitcast_fusion.1), channel_id=1, source_target_pairs={{0,16},{16,0},{32,48},{48,32},{64,80},{80,64},{96,112},{112,96},{1... | collective-permute-start | bytes 1228808 | tf_op jit(solution)/shard_map/ppermute | solution.py:16
  90.5 10.5 %collective-permute-start.17 = (bf16[2,80,1280]{2,1,0:T(8,128)(2,1)S(1)}, bf16[2,80,1280]{2,1,0:T(8,128)(2,1)S(1)}, u32[]{:S(2)}, u32[]{:S(2)}) collective-permute-start(bf16[2,80,1280]{2,1,0:T(8,128)(2,1)S(1)} %slice_bitcast_fusion), channel_id=1, source_target_pairs={{0,48},{16,32},{32,16},{48,0},{64,112},{80,96},{96,80},{112,64},{1... | collective-permute-start | bytes 1228808 | tf_op jit(solution)/shard_map/ppermute | solution.py:16
  101.0 38.5 %slice-start = ((s8[5242880]{0:T(1024)(128)(4,1)}), s8[4194304]{0:T(1024)(128)(4,1)S(1)}, s32[]{:S(2)}) async-start(s8[5242880]{0:T(1024)(128)(4,1)} %bitcast.60), calls=%async_computation | async-start | bytes 8388608
  101.0 38.5 %slice-start.1 = ((s8[5242880]{0:T(1024)(128)(4,1)}), s8[1048576]{0:T(1024)(128)(4,1)S(1)}, s32[]{:S(2)}) async-start(s8[5242880]{0:T(1024)(128)(4,1)} %bitcast.60), calls=%async_computation.1 | async-start | bytes 2097152
  105.1 4.7 %collective-permute-start.22 = (bf16[64,1280]{1,0:T(8,128)(2,1)S(1)}, bf16[64,1280]{1,0:T(8,128)(2,1)S(1)}, u32[]{:S(2)}, u32[]{:S(2)}) collective-permute-start(bf16[64,1280]{1,0:T(8,128)(2,1)S(1)} %get-tuple-element.69), channel_id=1, source_target_pairs={{0,64},{16,80},{32,96},{48,112},{64,0},{80,16},{96,32},{112,48},{1... | collective-permute-start | bytes 491528 | tf_op jit(solution)/shard_map/ppermute | solution.py:16
  105.2 6.3 %collective-permute-start.24 = (bf16[64,1280]{1,0:T(8,128)(2,1)S(1)}, bf16[64,1280]{1,0:T(8,128)(2,1)S(1)}, u32[]{:S(2)}, u32[]{:S(2)}) collective-permute-start(bf16[64,1280]{1,0:T(8,128)(2,1)S(1)} %get-tuple-element.70), channel_id=1, source_target_pairs={{0,192},{16,208},{32,224},{48,240},{64,128},{80,144},{96,160},{112... | collective-permute-start | bytes 491528 | tf_op jit(solution)/shard_map/ppermute | solution.py:16
  106.1 19.1 %collective-permute-start.23 = (bf16[64,1280]{1,0:T(8,128)(2,1)S(1)}, bf16[64,1280]{1,0:T(8,128)(2,1)S(1)}, u32[]{:S(2)}, u32[]{:S(2)}) collective-permute-start(bf16[64,1280]{1,0:T(8,128)(2,1)S(1)} %get-tuple-element.71), channel_id=1, source_target_pairs={{0,128},{16,144},{32,160},{48,176},{64,192},{80,208},{96,224},{112... | collective-permute-start | bytes 491528 | tf_op jit(solution)/shard_map/ppermute | solution.py:16
  107.9 21.8 %collective-permute-start.25 = (bf16[64,1280]{1,0:T(8,128)(2,1)S(1)}, bf16[64,1280]{1,0:T(8,128)(2,1)S(1)}, u32[]{:S(2)}, u32[]{:S(2)}) collective-permute-start(bf16[64,1280]{1,0:T(8,128)(2,1)S(1)} %get-tuple-element.66), channel_id=1, source_target_pairs={{0,64},{16,80},{32,96},{48,112},{64,0},{80,16},{96,32},{112,48},{1... | collective-permute-start | bytes 491528 | tf_op jit(solution)/shard_map/ppermute | solution.py:16
  109.0 20.8 %collective-permute-start.27 = (bf16[64,1280]{1,0:T(8,128)(2,1)S(1)}, bf16[64,1280]{1,0:T(8,128)(2,1)S(1)}, u32[]{:S(2)}, u32[]{:S(2)}) collective-permute-start(bf16[64,1280]{1,0:T(8,128)(2,1)S(1)} %get-tuple-element.67), channel_id=1, source_target_pairs={{0,192},{16,208},{32,224},{48,240},{64,128},{80,144},{96,160},{112... | collective-permute-start | bytes 491528 | tf_op jit(solution)/shard_map/ppermute | solution.py:16
  109.8 29.7 %collective-permute-start.26 = (bf16[64,1280]{1,0:T(8,128)(2,1)S(1)}, bf16[64,1280]{1,0:T(8,128)(2,1)S(1)}, u32[]{:S(2)}, u32[]{:S(2)}) collective-permute-start(bf16[64,1280]{1,0:T(8,128)(2,1)S(1)} %get-tuple-element.68), channel_id=1, source_target_pairs={{0,128},{16,144},{32,160},{48,176},{64,192},{80,208},{96,224},{112... | collective-permute-start | bytes 491528 | tf_op jit(solution)/shard_map/ppermute | solution.py:16
  125.3 14.2 %collective-permute-start.28 = (bf16[64,1280]{1,0:T(8,128)(2,1)S(1)}, bf16[64,1280]{1,0:T(8,128)(2,1)S(1)}, u32[]{:S(2)}, u32[]{:S(2)}) collective-permute-start(bf16[64,1280]{1,0:T(8,128)(2,1)S(1)} %get-tuple-element.56), channel_id=1, source_target_pairs={{0,2},{1,3},{2,0},{3,1},{4,6},{5,7},{6,4},{7,5},{8,10},{9,11},{10,... | collective-permute-start | bytes 491528 | tf_op jit(solution)/shard_map/ppermute | solution.py:16
  141.6 16.2 %collective-permute-start.34 = (f32[8,256]{1,0:T(8,128)S(1)}, f32[8,256]{1,0:T(8,128)S(1)}, u32[]{:S(2)}, u32[]{:S(2)}) collective-permute-start(f32[8,256]{1,0:T(8,128)S(1)} %get-tuple-element.52), channel_id=1, source_target_pairs={{0,3},{1,2},{2,1},{3,0},{4,7},{5,6},{6,5},{7,4},{8,11},{9,10},{10,... | collective-permute-start | bytes 24584 | tf_op jit(solution)/shard_map/ppermute | solution.py:16
  151.3 7.4 %collective-permute-start.33 = (f32[8,256]{1,0:T(8,128)S(1)}, f32[8,256]{1,0:T(8,128)S(1)}, u32[]{:S(2)}, u32[]{:S(2)}) collective-permute-start(f32[8,256]{1,0:T(8,128)S(1)} %get-tuple-element.52), channel_id=1, source_target_pairs={{0,2},{1,3},{2,0},{3,1},{4,6},{5,7},{6,4},{7,5},{8,10},{9,11},{10,... | collective-permute-start | bytes 24584 | tf_op jit(solution)/shard_map/ppermute | solution.py:16
  154.0 4.8 %collective-permute-start.32 = (f32[8,256]{1,0:T(8,128)S(1)}, f32[8,256]{1,0:T(8,128)S(1)}, u32[]{:S(2)}, u32[]{:S(2)}) collective-permute-start(f32[8,256]{1,0:T(8,128)S(1)} %get-tuple-element.52), channel_id=1, source_target_pairs={{0,1},{1,0},{2,3},{3,2},{4,5},{5,4},{6,7},{7,6},{8,9},{9,8},{10,11... | collective-permute-start | bytes 24584 | tf_op jit(solution)/shard_map/ppermute | solution.py:16
  154.0 21.5 %collective-permute-start.31 = (bf16[2,64,1280]{2,1,0:T(8,128)(2,1)S(1)}, bf16[2,64,1280]{2,1,0:T(8,128)(2,1)S(1)}, u32[]{:S(2)}, u32[]{:S(2)}) collective-permute-start(bf16[2,64,1280]{2,1,0:T(8,128)(2,1)S(1)} %pad_maximum_fusion.9.pair), channel_id=1, source_target_pairs={{0,12},{1,13},{2,14},{3,15},{4,8},{5,9},{6,10},{7,11},{8,4},{9,5},... | collective-permute-start | bytes 983048 | tf_op jit(solution)/shard_map/ppermute | solution.py:16
  157.8 17.6 %collective-permute-start.30 = (bf16[2,64,1280]{2,1,0:T(8,128)(2,1)S(1)}, bf16[2,64,1280]{2,1,0:T(8,128)(2,1)S(1)}, u32[]{:S(2)}, u32[]{:S(2)}) collective-permute-start(bf16[2,64,1280]{2,1,0:T(8,128)(2,1)S(1)} %pad_maximum_fusion.9.pair), channel_id=1, source_target_pairs={{0,8},{1,9},{2,10},{3,11},{4,12},{5,13},{6,14},{7,15},{8,0},{9,1},... | collective-permute-start | bytes 983048 | tf_op jit(solution)/shard_map/ppermute | solution.py:16
  157.8 17.6 %collective-permute-start.29 = (bf16[2,64,1280]{2,1,0:T(8,128)(2,1)S(1)}, bf16[2,64,1280]{2,1,0:T(8,128)(2,1)S(1)}, u32[]{:S(2)}, u32[]{:S(2)}) collective-permute-start(bf16[2,64,1280]{2,1,0:T(8,128)(2,1)S(1)} %pad_maximum_fusion.9.pair), channel_id=1, source_target_pairs={{0,4},{1,5},{2,6},{3,7},{4,0},{5,1},{6,2},{7,3},{8,12},{9,13},{10,... | collective-permute-start | bytes 983048 | tf_op jit(solution)/shard_map/ppermute | solution.py:16
  158.8 13.9 %collective-permute-start.37 = (f32[8,256]{1,0:T(8,128)S(1)}, f32[8,256]{1,0:T(8,128)S(1)}, u32[]{:S(2)}, u32[]{:S(2)}) collective-permute-start(f32[8,256]{1,0:T(8,128)S(1)} %add_add_fusion.1), channel_id=1, source_target_pairs={{0,12},{1,13},{2,14},{3,15},{4,8},{5,9},{6,10},{7,11},{8,4},{9,5},... | collective-permute-start | bytes 24584 | tf_op jit(solution)/shard_map/ppermute | solution.py:16
  161.2 13.7 %collective-permute-start.36 = (f32[8,256]{1,0:T(8,128)S(1)}, f32[8,256]{1,0:T(8,128)S(1)}, u32[]{:S(2)}, u32[]{:S(2)}) collective-permute-start(f32[8,256]{1,0:T(8,128)S(1)} %add_add_fusion.1), channel_id=1, source_target_pairs={{0,8},{1,9},{2,10},{3,11},{4,12},{5,13},{6,14},{7,15},{8,0},{9,1},... | collective-permute-start | bytes 24584 | tf_op jit(solution)/shard_map/ppermute | solution.py:16
  172.7 2.8 %collective-permute-start.35 = (f32[8,256]{1,0:T(8,128)S(1)}, f32[8,256]{1,0:T(8,128)S(1)}, u32[]{:S(2)}, u32[]{:S(2)}) collective-permute-start(f32[8,256]{1,0:T(8,128)S(1)} %add_add_fusion.1), channel_id=1, source_target_pairs={{0,4},{1,5},{2,6},{3,7},{4,0},{5,1},{6,2},{7,3},{8,12},{9,13},{10,... | collective-permute-start | bytes 24584 | tf_op jit(solution)/shard_map/ppermute | solution.py:16
  175.5 6.8 %collective-permute-start.38 = (bf16[64,256]{1,0:T(8,128)(2,1)S(1)}, bf16[64,256]{1,0:T(8,128)(2,1)S(1)}, u32[]{:S(2)}, u32[]{:S(2)}) collective-permute-start(bf16[64,256]{1,0:T(8,128)(2,1)S(1)} %fusion.3), channel_id=1, source_target_pairs={{0,2},{1,3},{2,0},{3,1},{4,6},{5,7},{6,4},{7,5},{8,10},{9,11},{10,... | collective-permute-start | bytes 98312 | tf_op jit(solution)/shard_map/ppermute | solution.py:16
  182.3 6.0 %collective-permute-start.41 = (bf16[128,256]{1,0:T(8,128)(2,1)S(1)}, bf16[128,256]{1,0:T(8,128)(2,1)S(1)}, u32[]{:S(2)}, u32[]{:S(2)}) collective-permute-start(bf16[128,256]{1,0:T(8,128)(2,1)S(1)} %pad_maximum_fusion.10.pair), channel_id=1, source_target_pairs={{0,12},{1,13},{2,14},{3,15},{4,8},{5,9},{6,10},{7,11},{8,4},{9,5},... | collective-permute-start | bytes 196616 | tf_op jit(solution)/shard_map/ppermute | solution.py:16
  184.6 6.3 %collective-permute-start.40 = (bf16[128,256]{1,0:T(8,128)(2,1)S(1)}, bf16[128,256]{1,0:T(8,128)(2,1)S(1)}, u32[]{:S(2)}, u32[]{:S(2)}) collective-permute-start(bf16[128,256]{1,0:T(8,128)(2,1)S(1)} %pad_maximum_fusion.10.pair), channel_id=1, source_target_pairs={{0,8},{1,9},{2,10},{3,11},{4,12},{5,13},{6,14},{7,15},{8,0},{9,1},... | collective-permute-start | bytes 196616 | tf_op jit(solution)/shard_map/ppermute | solution.py:16
  185.7 5.2 %collective-permute-start.39 = (bf16[128,256]{1,0:T(8,128)(2,1)S(1)}, bf16[128,256]{1,0:T(8,128)(2,1)S(1)}, u32[]{:S(2)}, u32[]{:S(2)}) collective-permute-start(bf16[128,256]{1,0:T(8,128)(2,1)S(1)} %pad_maximum_fusion.10.pair), channel_id=1, source_target_pairs={{0,4},{1,5},{2,6},{3,7},{4,0},{5,1},{6,2},{7,3},{8,12},{9,13},{10,... | collective-permute-start | bytes 196616 | tf_op jit(solution)/shard_map/ppermute | solution.py:16
  186.5 9.8 %collective-permute-start.45 = (bf16[8,1280]{1,0:T(8,128)(2,1)S(1)}, bf16[8,1280]{1,0:T(8,128)(2,1)S(1)}, u32[]{:S(2)}, u32[]{:S(2)}) collective-permute-start(bf16[8,1280]{1,0:T(8,128)(2,1)S(1)} %fusion), channel_id=1, source_target_pairs={{0,192},{16,208},{32,224},{48,240},{64,128},{80,144},{96,160},{112... | collective-permute-start | bytes 61448 | tf_op jit(solution)/shard_map/ppermute | solution.py:16
  186.5 9.8 %collective-permute-start.44 = (bf16[8,1280]{1,0:T(8,128)(2,1)S(1)}, bf16[8,1280]{1,0:T(8,128)(2,1)S(1)}, u32[]{:S(2)}, u32[]{:S(2)}) collective-permute-start(bf16[8,1280]{1,0:T(8,128)(2,1)S(1)} %fusion), channel_id=1, source_target_pairs={{0,128},{16,144},{32,160},{48,176},{64,192},{80,208},{96,224},{112... | collective-permute-start | bytes 61448 | tf_op jit(solution)/shard_map/ppermute | solution.py:16
  188.2 8.0 %collective-permute-start.43 = (bf16[8,1280]{1,0:T(8,128)(2,1)S(1)}, bf16[8,1280]{1,0:T(8,128)(2,1)S(1)}, u32[]{:S(2)}, u32[]{:S(2)}) collective-permute-start(bf16[8,1280]{1,0:T(8,128)(2,1)S(1)} %fusion), channel_id=1, source_target_pairs={{0,64},{16,80},{32,96},{48,112},{64,0},{80,16},{96,32},{112,48},{1... | collective-permute-start | bytes 61448 | tf_op jit(solution)/shard_map/ppermute | solution.py:16
  191.6 10.6 %collective-permute-start.42 = (f32[128,1280]{1,0:T(8,128)S(1)}, f32[128,1280]{1,0:T(8,128)S(1)}, u32[]{:S(2)}, u32[]{:S(2)}) collective-permute-start(f32[128,1280]{1,0:T(8,128)S(1)} %get-tuple-element.55), channel_id=1, source_target_pairs={{0,1},{1,0},{2,3},{3,2},{4,5},{5,4},{6,7},{7,6},{8,9},{9,8},{10,11... | collective-permute-start | bytes 1966088 | tf_op jit(solution)/shard_map/ppermute | solution.py:16
  196.3 4.0 %collective-permute-start.48 = (bf16[8,1280]{1,0:T(8,128)(2,1)S(1)}, bf16[8,1280]{1,0:T(8,128)(2,1)S(1)}, u32[]{:S(2)}, u32[]{:S(2)}) collective-permute-start(bf16[8,1280]{1,0:T(8,128)(2,1)S(1)} %add_convert_fusion.1), channel_id=1, source_target_pairs={{0,48},{16,32},{32,16},{48,0},{64,112},{80,96},{96,80},{112,64},{1... | collective-permute-start | bytes 61448 | tf_op jit(solution)/shard_map/ppermute | solution.py:16
  197.4 4.1 %collective-permute-start.47 = (bf16[8,1280]{1,0:T(8,128)(2,1)S(1)}, bf16[8,1280]{1,0:T(8,128)(2,1)S(1)}, u32[]{:S(2)}, u32[]{:S(2)}) collective-permute-start(bf16[8,1280]{1,0:T(8,128)(2,1)S(1)} %add_convert_fusion.1), channel_id=1, source_target_pairs={{0,32},{16,48},{32,0},{48,16},{64,96},{80,112},{96,64},{112,80},{1... | collective-permute-start | bytes 61448 | tf_op jit(solution)/shard_map/ppermute | solution.py:16
  197.6 3.9 %collective-permute-start.46 = (bf16[8,1280]{1,0:T(8,128)(2,1)S(1)}, bf16[8,1280]{1,0:T(8,128)(2,1)S(1)}, u32[]{:S(2)}, u32[]{:S(2)}) collective-permute-start(bf16[8,1280]{1,0:T(8,128)(2,1)S(1)} %add_convert_fusion.1), channel_id=1, source_target_pairs={{0,16},{16,0},{32,48},{48,32},{64,80},{80,64},{96,112},{112,96},{1... | collective-permute-start | bytes 61448 | tf_op jit(solution)/shard_map/ppermute | solution.py:16

commit v2 on v1

--- a/solution.py
+++ b/solution.py
@@ -21,16 +21,16 @@
 
 
 def ffn_kernel(rows_in, rows_go, *refs):
-    own, l0, r0, f0, both, lb, rb, pb, qb, last, l3, r3, f3 = refs[:13]
-    out_own, out_far, grad_own, grad_far = refs[13:17]
-    w1, w2 = refs[17:]
+    own, l0, r0, p0, q0, both, lb, rb, pb, qb, last, l3, r3, p3, q3 = refs[:15]
+    f0, f3 = (p0, q0), (p3, q3)
+    outs, grads, (w1, w2) = refs[15:19], refs[19:23], refs[23:]
     me = lax.axis_index("dp")
     depth = w1.shape[0] // 16
 
     def place(which, dst):
         for a, sources in (
-            (0, (own.at[which], l0.at[which], f0.at[which], r0.at[which])),
-            (3, (last.at[which], l3.at[which], f3.at[which], r3.at[which])),
+            (0, (own.at[which], l0.at[which], f0[which], r0.at[which])),
+            (3, (last.at[which], l3.at[which], f3[which], r3.at[which])),
             (1, (both.at[which, 0], lb.at[which, 0], (pb, qb)[which].at[0], rb.at[which, 0])),
             (2, (both.at[which, 1], lb.at[which, 1], (pb, qb)[which].at[1], rb.at[which, 1])),
         ):
@@ -48,13 +48,10 @@
     slope = cdf + 0.5 * pre * (1.0 - th * th) * (ROOT * (1.0 + 3 * 0.044715 * sq))
     hidden_grad = jnp.dot(rows_go[...], w2[...], preferred_element_type=F32)
     pre_grad = (hidden_grad * slope).astype(BF16)
-    own_rows = out_own.shape[0]
-    grad = nt(pre_grad, w1[...])
-    grad_own[...] = grad[:own_rows]
-    grad_far[...] = grad[own_rows:].astype(BF16)
-    out = nt(hidden, w2[...])
-    out_own[...] = out[:own_rows]
-    out_far[...] = out[own_rows:].astype(BF16)
+    own_rows = outs[0].shape[0]
+    for whole, blocks in ((nt(hidden, w2[...]), outs), (nt(pre_grad, w1[...]), grads)):
+        for a, block in enumerate(blocks):
+            block[...] = whole[a * own_rows : (a + 1) * own_rows].astype(block.dtype)
 
 
 def ffn(rows_in, rows_go, blocks, own_rows):
@@ -63,13 +60,9 @@
     vmem = pl.BlockSpec(memory_space=pltpu.VMEM)
     return pl.pallas_call(
         ffn_kernel,
-        out_shape=[
-            jax.ShapeDtypeStruct((own_rows, width), F32),
-            jax.ShapeDtypeStruct((rows - own_rows, width), BF16),
-        ]
-        * 2,
+        out_shape=[jax.ShapeDtypeStruct((own_rows, width), t) for t in (F32, BF16, BF16, BF16)] * 2,
         in_specs=[vmem] * (2 + len(blocks)),
-        out_specs=[vmem] * 4,
+        out_specs=[vmem] * 8,
         scratch_shapes=[pltpu.VMEM((width, quarter), BF16), pltpu.VMEM((width, quarter), BF16)],
         compiler_params=pltpu.CompilerParams(vmem_limit_bytes=40 * 2**20),
         name="ffn",
@@ -190,39 +183,13 @@
     )(rows, big, weight)
 
 
-def spread_kernel(spread, pair, one, two, three, out):
-    side = spread[...].reshape(2 * spread.shape[1], spread.shape[2])
-    depth = side.shape[1] // 4
-    total = jnp.zeros(out.shape, F32)
-    for x, piece in enumerate((pair, one, two, three)):
-        block = piece[...].reshape(depth, piece.shape[2])
-        total = total + jnp.dot(side[:, x * depth : (x + 1) * depth], block, preferred_element_type=F32)
-    out[...] = total
-
-
-def spread_call(spread, pieces):
-    width = pieces[0].shape[2]
-    vmem = pl.BlockSpec(memory_space=pltpu.VMEM)
-    return pl.pallas_call(
-        spread_kernel,
-        out_shape=jax.ShapeDtypeStruct((2 * spread.shape[1], width), F32),
-        in_specs=[vmem] * 5,
-        out_specs=vmem,
-        compiler_params=pltpu.CompilerParams(vmem_limit_bytes=24 * 2**20),
-        name="through_slots",
-    )(spread, *pieces)
-
-
-def lines_kernel(pair, one, two, three, table, through, mine, theirs):
-    count = pair.shape[1]
-    grads = jnp.concatenate([pair[...], one[...], two[...], three[...]], axis=0)
-    total = grads.shape[0]
+def lines_kernel(grads, table, out):
+    total, count = grads.shape
     near = total // 8
     c = lax.broadcasted_iota(jnp.int32, (total, near), 0)
     q = lax.broadcasted_iota(jnp.int32, (total, near), 1)
     fold = ((c // 64 == q // 8) & (c % 8 == q % 8)).astype(BF16)
-    x = nt(pick_rows(count), grads)
-    half = through.shape[0] // 2
+    x = nt(pick_rows(count), grads[...])
     parts = []
     for side in range(2):
         y = jnp.concatenate([x[16 * side : 16 * side + 16]] * 8, axis=0)
@@ -231,22 +198,44 @@
         y = jnp.where((col // 8) % 8 == row // 16, y, 0.0).astype(BF16)
         parts.append(jnp.dot(y, fold, preferred_element_type=F32).astype(BF16))
     lines = jnp.concatenate(parts, axis=0)
-    sums = through[...] + jnp.dot(lines, table[:near], preferred_element_type=F32)
-    mine[...] = sums[:half]
-    theirs[...] = sums[half:]
-
-
-def lines_call(pieces, table, through):
+    out[...] = jnp.dot(lines, table[:near], preferred_element_type=F32)
+
+
+def lines_call(line, table):
     vmem = pl.BlockSpec(memory_space=pltpu.VMEM)
-    half = through.shape[0] // 2
     return pl.pallas_call(
         lines_kernel,
-        out_shape=[jax.ShapeDtypeStruct((half, through.shape[1]), F32)] * 2,
+        out_shape=jax.ShapeDtypeStruct((256, table.shape[1]), F32),
+        in_specs=[vmem] * 2,
+        out_specs=vmem,
+        compiler_params=pltpu.CompilerParams(vmem_limit_bytes=24 * 2**20),
+        name="through_logits",
+    )(line, table)
+
+
+def spread_kernel(spread, pair, one, two, three, base, mine, theirs):
+    half = mine.shape[0]
+    side = spread[...].reshape(2 * half, spread.shape[2])
+    depth = side.shape[1] // 4
+    total = base[...]
+    for x, piece in enumerate((pair, one, two, three)):
+        block = piece[...].reshape(depth, piece.shape[2])
+        total = total + jnp.dot(side[:, x * depth : (x + 1) * depth], block, preferred_element_type=F32)
+    mine[...] = total[:half]
+    theirs[...] = total[half:]
+
+
+def spread_call(spread, pieces, base):
+    vmem = pl.BlockSpec(memory_space=pltpu.VMEM)
+    half, width = base.shape[0] // 2, base.shape[1]
+    return pl.pallas_call(
+        spread_kernel,
+        out_shape=[jax.ShapeDtypeStruct((half, width), F32)] * 2,
         in_specs=[vmem] * 6,
         out_specs=[vmem] * 2,
         compiler_params=pltpu.CompilerParams(vmem_limit_bytes=24 * 2**20),
-        name="through_logits",
-    )(*pieces, table, through)
+        name="through_slots",
+    )(spread, *pieces, base)
 
 
 def after(value, *earlier):
@@ -269,90 +258,87 @@
     return [unit(z ^ a) for a in range(4)]
 
 
-def all_y(unit):
-    return swap(unit, "dp", 1), swap(unit, "dp", 3), swap(unit, "dp", 2)
-
-
-def reduce_z(own, far):
-    count = own.shape[0]
-    total = own
-    for a in (1, 2, 3):
-        total = total + swap(far[(a - 1) * count : a * count], "dp", 4 * a).astype(F32)
-    return total
+def together(*values):
+    return lax.optimization_barrier(values)
+
+
+def reduce_z(own, *far):
+    one, two, three = together(*[swap(v, "dp", 4 * a) for a, v in enumerate(far, 1)])
+    return (own + one.astype(F32)) + (two.astype(F32) + three.astype(F32))
 
 
 def all_x(v):
-    return [v, swap(v, "expert", 4), swap(v, "expert", 8), swap(v, "expert", 12)]
-
-
-def sum_expert(v):
-    v = (v + swap(v, "expert", 1)) + (swap(v, "expert", 2) + swap(v, "expert", 3))
-    return (v + swap(v, "expert", 4)) + (swap(v, "expert", 8) + swap(v, "expert", 12))
+    return [v, *together(swap(v, "expert", 4), swap(v, "expert", 8), swap(v, "expert", 12))]
+
+
+def doubled(v, axis, *steps):
+    for k in steps:
+        v = jnp.concatenate([v, swap(v, axis, k)], axis=0)
+    return v
+
+
+def summed(v, axis, *steps):
+    for k in steps:
+        v = v + swap(v, axis, k)
+    return v
 
 
 def per_device(tokens, out_grad, slot_params, w_in, w_out):
     images, count, width = tokens.shape
     own = slot_params.shape[1]
     half = images * own
-    params = slot_params.T
 
     units = units_of(w_in, w_out.T)
     l0, r0 = swap(units[0], "dp", 1), swap(units[0], "dp", 3)
     u1 = swap(units[1], "dp", 4)
     u2 = swap(units[2], "dp", 8)
-    table = jnp.concatenate([params, swap(params, "expert", 2)], axis=0)
-    table = jnp.concatenate(all_x(table), axis=0)
-    l0, r0, table = lax.optimization_barrier((l0, r0, table))
+    table = doubled(slot_params.T, "expert", 2, 4)
+    l0, r0, table = together(l0, r0, table)
     p0, q0 = swap(r0[0], "dp", 1), swap(l0[1], "dp", 3)
-    table = jnp.concatenate([table, swap(table, "expert", 1)], axis=0)
-
-    u1, u2, p0, q0, table = lax.optimization_barrier((u1, u2, p0, q0, table))
+    table = doubled(table, "expert", 8, 1)
+
+    u1, u2, p0, q0, table = together(u1, u2, p0, q0, table)
     both = jnp.stack([u1, u2], axis=1)
     lb, rb = swap(both, "dp", 1), swap(both, "dp", 3)
     u3 = swap(after(units[3], u1), "dp", 12)
-
     rows, dispatch, combine, spread = slots_call(table, tokens, out_grad)
     rows = rows.reshape(2 * half, width)
 
-    lb, rb, rows = lax.optimization_barrier((lb, rb, rows))
+    lb, rb, u3, rows = together(lb, rb, u3, rows)
+    z1, z2 = swap(rows, "dp", 4), swap(rows, "dp", 8)
+    l3, r3 = swap(u3, "dp", 1), swap(u3, "dp", 3)
     pb, qb = swap(rb[0], "dp", 1), swap(lb[1], "dp", 3)
-    z1, z2, z3 = swap(rows, "dp", 4), swap(rows, "dp", 8), swap(rows, "dp", 12)
-    u3 = after(u3, lb, rb)
-    l3, r3, f3 = all_y(u3)
+    l3, r3, z2 = together(l3, r3, z2)
+    p3, q3 = swap(r3[0], "dp", 1), swap(l3[1], "dp", 3)
+    z3 = swap(z2, "dp", 4)
+    pb, qb, p3, q3, z3 = together(pb, qb, p3, q3, z3)
     rows_in = jnp.concatenate([v[:half] for v in (rows, z1, z2, z3)], axis=0)
     rows_go = jnp.concatenate([v[half:] for v in (rows, z1, z2, z3)], axis=0)
 
-    f0 = jnp.stack([p0, q0])
-    blocks = [units[0], l0, r0, f0, both, lb, rb, pb, qb, u3, l3, r3, f3]
-    out_own, out_far, grad_own, grad_far = ffn(rows_in, rows_go, blocks, half)
-    slot_in_grad = reduce_z(grad_own, grad_far)
-    slot_out = reduce_z(out_own, out_far)
-
+    blocks = [units[0], l0, r0, p0, q0, both, lb, rb, pb, qb, u3, l3, r3, p3, q3]
+    halves = ffn(rows_in, rows_go, blocks, half)
+    slot_out = reduce_z(*halves[:4])
+    slot_in_grad = reduce_z(*halves[4:])
     near = slot_in_grad.astype(BF16)
     far = swap(near, "expert", 2)
-    pieces = all_x(jnp.stack([near, far]))
-    through = spread_call(spread, pieces)
-
-    part, mix = against(after(slot_out, far), out_grad, combine, False)
-    mix = sum_expert(mix)
+
+    part, mix = against(slot_out, out_grad, combine, False)
+    mix = summed(mix, "expert", 1, 2, 4, 8)
     (back,) = against(slot_in_grad, tokens, dispatch, True)
-    part = after(part, *pieces)
     logit_grad = back + (part - combine * jnp.repeat(mix, own, axis=0))
     logit_grad_b = logit_grad.astype(BF16)
     slot_term = jnp.einsum(
         "bsm,bmd->sd", logit_grad_b.reshape(images, own, count), tokens, preferred_element_type=F32
     )
-    line = jnp.concatenate([logit_grad_b, swap(logit_grad_b, "expert", 2)], axis=0)
-    mine, theirs = lines_call(all_x(line), table, through)
-
-    term = slot_term.astype(BF16)
-    for step in ((4, 8, 12), (1, 2, 3)):
-        acc = term.astype(F32)
-        for k in step:
-            acc = acc + swap(term, "dp", k).astype(F32)
-        term = acc.astype(BF16)
-    slot_grad = acc.T
-
+    line = doubled(logit_grad_b, "expert", 2)
+    line = doubled(after(line, far), "expert", 4, 8)
+    base = lines_call(line, table)
+
+    pieces = all_x(jnp.stack([near, far]))
+    slot_sum = summed(slot_term, "dp", 4, 8, 1)
+    slot_grad = summed(after(slot_sum, *pieces), "dp", 2).T
+
+    mine, theirs = spread_call(spread, pieces, after(base, slot_sum))
     token_grad = (mine + swap(theirs, "expert", 1)).astype(BF16)
     return (token_grad.reshape(images, -1, width), slot_grad)
 

time: 204 us -> 175 us (0.86)
  waiting for transfers between devices: 91.5 us -> 50 us
  starting transfers between devices: 84.3 us -> 98.1 us
    ppermute x49 -> x44, waiting for transfers between devices: 91.5 us -> 50 us  [swap(): return lax.ppermute(value, axis, [(i, i ^ k) for i in range(count)])]
    ppermute x49 -> x44, starting transfers between devices: 84.3 us -> 98.1 us  [swap(): return lax.ppermute(value, axis, [(i, i ^ k) for i in range(count)])]
  transfers between devices with their start and end apart: 49 -> 44, of which waited for: 17 -> 21; matrix products, arithmetic and copies ran while one was open for 1% -> 1% of each run, Pallas kernels for 6% -> 8%
where the time goes in v2:
time: 175 us
  starting transfers between devices  98.1 us (56%)
  waiting for transfers between devices  50 us (29%)
  Pallas kernels  19.1 us (11%)
  local copies, waits for them, and re-layouts  4.23 us (2%)
  other arithmetic  2.06 us (1%)
    ppermute x44, starting transfers between devices, swap(): return lax.ppermute(value, axis, [(i, i ^ k) for i in range(count)])  98.1 us
    ppermute x44, waiting for transfers between devices, swap(): return lax.ppermute(value, axis, [(i, i ^ k) for i in range(count)])  50 us
    pallas_call x1, Pallas kernels, slots_call(): pl.pallas_call(slots_kernel, grid=(images // 2,), out_shape=[jax.ShapeDty...  9.18 us
    pallas_call x2, Pallas kernels, against(): pl.pallas_call(lambda *refs: against_kernel(over_tokens, *refs), grid=(im...  4.36 us
    pallas_call x1, Pallas kernels, ffn(): pl.pallas_call(ffn_kernel, out_shape=[jax.ShapeDtypeStruct((own_rows, wid...  4.03 us
  transfers between devices with their start and end apart: 44, of which 21 were waited for; matrix products, arithmetic and copies ran while one was open for 1% of the time, Pallas kernels for 8%

profile of v2, /device:TPU:1, one launch (start us, length us, event | category | flops | bytes accessed | tf_op | source)
XLA Modules:
  0.0 175.3 jit_solution(16795237199263525050)
XLA Ops:
  0.7 1.4 dynamic-slice_bitcast_fusion.1
  2.3 3.7 %collective-permute-start.3 = (bf16[2,80,1280]{2,1,0:T(8,128)(2,1)S(1)}, bf16[2,80,1280]{2,1,0:T(8,128)(2,1)S(1)}, u32[]{:S(2)}, u32[]{:S(2)}) collective-permute-start(bf16[2,80,1280]{2,1,0:T(8,128)(2,1)S(1)} %pad_maximum_fusion.5.refs_0_), channel_id=1, source_target_pairs={{0,48},{16,32},{32,16},{48,0},{64,112},{80,96},{96,80},{112,64},{1... | collective-permute-start | bytes 1228808 | tf_op jit(solution)/shard_map/ppermute | solution.py:16
  5.9 6.9 %collective-permute-start.4 = (bf16[8,1280]{1,0:T(8,128)(2,1)S(1)}, bf16[8,1280]{1,0:T(8,128)(2,1)S(1)}, u32[]{:S(2)}, u32[]{:S(2)}) collective-permute-start(bf16[8,1280]{1,0:T(8,128)(2,1)S(1)} %bitcast.69), channel_id=1, source_target_pairs={{0,2},{1,3},{2,0},{3,1},{4,6},{5,7},{6,4},{7,5},{8,10},{9,11},{10,... | collective-permute-start | bytes 61448 | tf_op jit(solution)/shard_map/ppermute | solution.py:16
  12.9 0.8 collective-permute-start
  14.0 1.2 collective-permute-start.5
  15.3 1.5 collective-permute-start.1
  17.2 2.8 %collective-permute-start.8 = (bf16[32,1280]{1,0:T(8,128)(2,1)S(1)}, bf16[32,1280]{1,0:T(8,128)(2,1)S(1)}, u32[]{:S(2)}, u32[]{:S(2)}) collective-permute-start(bf16[32,1280]{1,0:T(8,128)(2,1)S(1)} %pad_maximum_fusion.12), channel_id=1, source_target_pairs={{0,8},{1,9},{2,10},{3,11},{4,12},{5,13},{6,14},{7,15},{8,0},{9,1},... | collective-permute-start | bytes 245768 | tf_op jit(solution)/shard_map/ppermute | solution.py:16
  20.0 2.5 %collective-permute-done.8 = bf16[32,1280]{1,0:T(8,128)(2,1)S(1)} collective-permute-done((bf16[32,1280]{1,0:T(8,128)(2,1)S(1)}, bf16[32,1280]{1,0:T(8,128)(2,1)S(1)}, u32[]{:S(2)}, u32[]{:S(2)}) %collective-permute-start.8) | collective-permute-done | bytes 81952 | tf_op jit(solution)/shard_map/ppermute | solution.py:16
  22.5 3.8 %collective-permute-start.9 = (bf16[64,1280]{1,0:T(8,128)(2,1)S(1)}, bf16[64,1280]{1,0:T(8,128)(2,1)S(1)}, u32[]{:S(2)}, u32[]{:S(2)}) collective-permute-start(bf16[64,1280]{1,0:T(8,128)(2,1)S(1)} %pad_maximum_fusion.10), channel_id=1, source_target_pairs={{0,1},{1,0},{2,3},{3,2},{4,5},{5,4},{6,7},{7,6},{8,9},{9,8},{10,11... | collective-permute-start | bytes 491528 | tf_op jit(solution)/shard_map/ppermute | solution.py:16
  26.3 0.9 collective-permute-start.7
  27.2 0.9 collective-permute-start.6
  28.1 2.3 %collective-permute-done = bf16[2,80,1280]{2,1,0:T(8,128)(2,1)S(1)} collective-permute-done((bf16[2,80,1280]{2,1,0:T(8,128)(2,1)S(1)}, bf16[2,80,1280]{2,1,0:T(8,128)(2,1)S(1)}, u32[]{:S(2)}, u32[]{:S(2)}) %collective-permute-start) | collective-permute-done | bytes 409632 | tf_op jit(solution)/shard_map/ppermute | solution.py:16
  30.4 3.8 %collective-permute-done.7.refs_4_ = bf16[80,1280]{1,0:T(8,128)(2,1)S(1)} collective-permute-done((bf16[80,1280]{1,0:T(8,128)(2,1)S(1)}, bf16[80,1280]{1,0:T(8,128)(2,1)S(1)}, u32[]{:S(2)}, u32[]{:S(2)}) %collective-permute-start.7) | collective-permute-done | bytes 204832 | tf_op jit(solution)/shard_map/ppermute | solution.py:16
  34.3 1.2 collective-permute-start.11
  36.0 3.3 %collective-permute-start.12 = (bf16[2,80,1280]{2,1,0:T(8,128)(2,1)S(1)}, bf16[2,80,1280]{2,1,0:T(8,128)(2,1)S(1)}, u32[]{:S(2)}, u32[]{:S(2)}) collective-permute-start(bf16[2,80,1280]{2,1,0:T(8,128)(2,1)S(1)} %pad_maximum_fusion.6), channel_id=1, source_target_pairs={{0,192},{16,208},{32,224},{48,240},{64,128},{80,144},{96,160},{112... | collective-permute-start | bytes 1228808 | tf_op jit(solution)/shard_map/ppermute | solution.py:16
  39.3 2.5 %copy-done.1 = bf16[8,256,1280]{2,1,0:T(8,128)(2,1)S(1)} copy-done((bf16[8,256,1280]{2,1,0:T(8,128)(2,1)S(1)}, bf16[8,256,1280]{2,1,0:T(8,128)(2,1)}, u32[]{:S(2)}) %copy-start.1) | copy-done | bytes 5242904
  41.8 9.2 %slots.1 = (bf16[2,64,1280]{2,1,0:T(8,128)(2,1)S(1)}, f32[64,256]{1,0:T(8,128)S(1)}, f32[64,256]{1,0:T(8,128)S(1)}, bf16[2,128,512]{2,1,0:T(8,128)(2,1)S(1)}) custom-call(bf16[128,1280]{1,0:T(8,128)(2,1)S(1)} %pad_maximum_fusion.7.table, bf16[8,256,1280]{2,1,0:T(8,128)(2,1)S(1)} %copy-done, bf16[8,256,1280]{2,1,0:T(8,128)(2,1)S(1)} %copy-done.1), custom_call_target="tpu_custom_call" | custom-call | tf_op jit(solution)/shard_map/slots/pallas_call | solution.py:117
  51.0 1.7 collective-permute-done.11.refs_7_
  52.9 3.4 %collective-permute-start.16 = (bf16[128,1280]{1,0:T(8,128)(2,1)S(1)}, bf16[128,1280]{1,0:T(8,128)(2,1)S(1)}, u32[]{:S(2)}, u32[]{:S(2)}) collective-permute-start(bf16[128,1280]{1,0:T(8,128)(2,1)S(1)} %bitcast.61), channel_id=1, source_target_pairs={{0,128},{16,144},{32,160},{48,176},{64,192},{80,208},{96,224},{112... | collective-permute-start | bytes 983048 | tf_op jit(solution)/shard_map/ppermute | solution.py:16
  56.2 0.8 collective-permute-start.13
  57.1 1.2 collective-permute-start.15
  58.2 0.9 collective-permute-start.14
  59.1 1.2 collective-permute-start.18
  60.4 7.6 %collective-permute-done.13 = bf16[128,1280]{1,0:T(8,128)(2,1)S(1)} collective-permute-done((bf16[128,1280]{1,0:T(8,128)(2,1)S(1)}, bf16[128,1280]{1,0:T(8,128)(2,1)S(1)}, u32[]{:S(2)}, u32[]{:S(2)}) %collective-permute-start.13) | collective-permute-done | bytes 327712 | tf_op jit(solution)/shard_map/ppermute | solution.py:16
  68.0 0.7 collective-permute-start.17
  68.8 1.9 %collective-permute-start.20 = (bf16[80,1280]{1,0:T(8,128)(2,1)S(1)}, bf16[80,1280]{1,0:T(8,128)(2,1)S(1)}, u32[]{:S(2)}, u32[]{:S(2)}) collective-permute-start(bf16[80,1280]{1,0:T(8,128)(2,1)S(1)} %slice_bitcast_fusion.2), channel_id=1, source_target_pairs={{0,48},{16,32},{32,16},{48,0},{64,112},{80,96},{96,80},{112,64},{1... | collective-permute-start | bytes 614408 | tf_op jit(solution)/shard_map/ppermute | solution.py:16
  71.3 1.9 %collective-permute-start.21 = (bf16[128,1280]{1,0:T(8,128)(2,1)S(1)}, bf16[128,1280]{1,0:T(8,128)(2,1)S(1)}, u32[]{:S(2)}, u32[]{:S(2)}) collective-permute-start(bf16[128,1280]{1,0:T(8,128)(2,1)S(1)} %collective-permute-done.16), channel_id=1, source_target_pairs={{0,64},{16,80},{32,96},{48,112},{64,0},{80,16},{96,32},{112,48},{1... | collective-permute-start | bytes 983048 | tf_op jit(solution)/shard_map/ppermute | solution.py:16
  73.3 1.4 collective-permute-done.18.refs_9_
  74.7 1.1 collective-permute-done.17.refs_8_
  75.8 3.3 %collective-permute-done.20.refs_14_ = bf16[80,1280]{1,0:T(8,128)(2,1)S(1)} collective-permute-done((bf16[80,1280]{1,0:T(8,128)(2,1)S(1)}, bf16[80,1280]{1,0:T(8,128)(2,1)S(1)}, u32[]{:S(2)}, u32[]{:S(2)}) %collective-permute-start.20) | collective-permute-done | bytes 204832 | tf_op jit(solution)/shard_map/ppermute | solution.py:16
  79.1 1.1 collective-permute-done.19.refs_13_
  80.4 4.0 %ffn.1 = (f32[64,1280]{1,0:T(8,128)S(1)}, bf16[64,1280]{1,0:T(8,128)(2,1)S(1)}, bf16[64,1280]{1,0:T(8,128)(2,1)S(1)}, bf16[64,1280]{1,0:T(8,128)(2,1)S(1)}, f32[...) custom-call(bf16[256,1280]{1,0:T(8,128)(2,1)S(1)} %get-tuple-element, ...), custom_call_target="tpu_custom_call" | custom-call | tf_op jit(solution)/shard_map/ffn/pallas_call | solution.py:61
  84.4 2.3 %collective-permute-start.29 = (bf16[64,1280]{1,0:T(8,128)(2,1)S(1)}, bf16[64,1280]{1,0:T(8,128)(2,1)S(1)}, u32[]{:S(2)}, u32[]{:S(2)}) collective-permute-start(bf16[64,1280]{1,0:T(8,128)(2,1)S(1)} %get-tuple-element.86), channel_id=1, source_target_pairs={{0,64},{16,80},{32,96},{48,112},{64,0},{80,16},{96,32},{112,48},{1... | collective-permute-start | bytes 491528 | tf_op jit(solution)/shard_map/ppermute | solution.py:16
  86.7 3.9 %collective-permute-start.30 = (bf16[64,1280]{1,0:T(8,128)(2,1)S(1)}, bf16[64,1280]{1,0:T(8,128)(2,1)S(1)}, u32[]{:S(2)}, u32[]{:S(2)}) collective-permute-start(bf16[64,1280]{1,0:T(8,128)(2,1)S(1)} %get-tuple-element.87), channel_id=1, source_target_pairs={{0,128},{16,144},{32,160},{48,176},{64,192},{80,208},{96,224},{112... | collective-permute-start | bytes 491528 | tf_op jit(solution)/shard_map/ppermute | solution.py:16
  90.6 1.1 collective-permute-start.31
  91.9 2.2 %collective-permute-start.23 = (bf16[64,1280]{1,0:T(8,128)(2,1)S(1)}, bf16[64,1280]{1,0:T(8,128)(2,1)S(1)}, u32[]{:S(2)}, u32[]{:S(2)}) collective-permute-start(bf16[64,1280]{1,0:T(8,128)(2,1)S(1)} %get-tuple-element.76), channel_id=1, source_target_pairs={{0,128},{16,144},{32,160},{48,176},{64,192},{80,208},{96,224},{112... | collective-permute-start | bytes 491528 | tf_op jit(solution)/shard_map/ppermute | solution.py:16
  94.1 1.1 collective-permute-start.24
  95.2 4.4 %collective-permute-done.31 = bf16[64,1280]{1,0:T(8,128)(2,1)S(1)} collective-permute-done((bf16[64,1280]{1,0:T(8,128)(2,1)S(1)}, bf16[64,1280]{1,0:T(8,128)(2,1)S(1)}, u32[]{:S(2)}, u32[]{:S(2)}) %collective-permute-start.31) | collective-permute-done | bytes 163872 | tf_op jit(solution)/shard_map/ppermute | solution.py:16
  99.7 2.1 %combine_grad.1 = (f32[64,256]{1,0:T(8,128)S(1)}, f32[8,256]{1,0:T(8,128)S(1)}) custom-call(f32[64,1280]{1,0:T(8,128)S(1)} %add_add_fusion.refs_0_, bf16[8,256,1280]{2,1,0:T(8,128)(2,1)S(1)} %bitcast.60, f32[64,256]{1,0:T(8,128)S(1)} %get-tuple-element.92.refs_2_), custom_call_target="tpu_custom_call" | custom-call | tf_op jit(solution)/shard_map/combine_grad/pallas_call | solution.py:171
  101.8 7.9 %collective-permute-start.32 = (f32[8,256]{1,0:T(8,128)S(1)}, f32[8,256]{1,0:T(8,128)S(1)}, u32[]{:S(2)}, u32[]{:S(2)}) collective-permute-start(f32[8,256]{1,0:T(8,128)S(1)} %get-tuple-element.94), channel_id=1, source_target_pairs={{0,1},{1,0},{2,3},{3,2},{4,5},{5,4},{6,7},{7,6},{8,9},{9,8},{10,11... | collective-permute-start | bytes 24584 | tf_op jit(solution)/shard_map/ppermute | solution.py:16
  109.7 0.8 collective-permute-done.32
  110.5 4.3 %collective-permute-start.33 = (f32[8,256]{1,0:T(8,128)S(1)}, f32[8,256]{1,0:T(8,128)S(1)}, u32[]{:S(2)}, u32[]{:S(2)}) collective-permute-start(f32[8,256]{1,0:T(8,128)S(1)} %add.75), channel_id=1, source_target_pairs={{0,2},{1,3},{2,0},{3,1},{4,6},{5,7},{6,4},{7,5},{8,10},{9,11},{10,... | collective-permute-start | bytes 24584 | tf_op jit(solution)/shard_map/ppermute | solution.py:16
  114.8 2.2 %collective-permute-done.33 = f32[8,256]{1,0:T(8,128)S(1)} collective-permute-done((f32[8,256]{1,0:T(8,128)S(1)}, f32[8,256]{1,0:T(8,128)S(1)}, u32[]{:S(2)}, u32[]{:S(2)}) %collective-permute-start.33) | collective-permute-done | bytes 8224 | tf_op jit(solution)/shard_map/ppermute | solution.py:16
  117.6 2.0 %collective-permute-done.34 = f32[8,256]{1,0:T(8,128)S(1)} collective-permute-done((f32[8,256]{1,0:T(8,128)S(1)}, f32[8,256]{1,0:T(8,128)S(1)}, u32[]{:S(2)}, u32[]{:S(2)}) %collective-permute-start.34) | collective-permute-done | bytes 8224 | tf_op jit(solution)/shard_map/ppermute | solution.py:16
  119.6 2.0 %collective-permute-start.35 = (f32[8,256]{1,0:T(8,128)S(1)}, f32[8,256]{1,0:T(8,128)S(1)}, u32[]{:S(2)}, u32[]{:S(2)}) collective-permute-start(f32[8,256]{1,0:T(8,128)S(1)} %add.77), channel_id=1, source_target_pairs={{0,8},{1,9},{2,10},{3,11},{4,12},{5,13},{6,14},{7,15},{8,0},{9,1},... | collective-permute-start | bytes 24584 | tf_op jit(solution)/shard_map/ppermute | solution.py:16
  121.7 5.5 %collective-permute-start.25 = (bf16[64,1280]{1,0:T(8,128)(2,1)S(1)}, bf16[64,1280]{1,0:T(8,128)(2,1)S(1)}, u32[]{:S(2)}, u32[]{:S(2)}) collective-permute-start(bf16[64,1280]{1,0:T(8,128)(2,1)S(1)} %get-tuple-element.100), channel_id=1, source_target_pairs={{0,2},{1,3},{2,0},{3,1},{4,6},{5,7},{6,4},{7,5},{8,10},{9,11},{10,... | collective-permute-start | bytes 491528 | tf_op jit(solution)/shard_map/ppermute | solution.py:16
  127.1 2.3 %dispatch_grad.1 = f32[64,256]{1,0:T(8,128)S(1)} custom-call(f32[64,1280]{1,0:T(8,128)S(1)} %get-tuple-element.101.refs_0_, bf16[8,256,1280]{2,1,0:T(8,128)(2,1)S(1)} %copy-done, f32[64,256]{1,0:T(8,128)S(1)} %get-tuple-element.84.refs_2_), custom_call_target="tpu_custom_call" | custom-call | tf_op jit(solution)/shard_map/dispatch_grad/pallas_call | solution.py:171
  129.8 6.7 %collective-permute-done.36 = bf16[64,256]{1,0:T(8,128)(2,1)S(1)} collective-permute-done((bf16[64,256]{1,0:T(8,128)(2,1)S(1)}, bf16[64,256]{1,0:T(8,128)(2,1)S(1)}, u32[]{:S(2)}, u32[]{:S(2)}) %collective-permute-start.36) | collective-permute-done | bytes 32800 | tf_op jit(solution)/shard_map/ppermute | solution.py:16
  136.6 0.7 collective-permute-start.37
  137.6 2.4 %collective-permute-start.27 = (bf16[2,64,1280]{2,1,0:T(8,128)(2,1)S(1)}, bf16[2,64,1280]{2,1,0:T(8,128)(2,1)S(1)}, u32[]{:S(2)}, u32[]{:S(2)}) collective-permute-start(bf16[2,64,1280]{2,1,0:T(8,128)(2,1)S(1)} %pad_maximum_fusion.8.pair), channel_id=1, source_target_pairs={{0,8},{1,9},{2,10},{3,11},{4,12},{5,13},{6,14},{7,15},{8,0},{9,1},... | collective-permute-start | bytes 983048 | tf_op jit(solution)/shard_map/ppermute | solution.py:16
  140.7 1.5 collective-permute-start.38
  142.2 0.8 convolution_bitcast_fusion
  142.9 8.0 %collective-permute-start.39 = (f32[8,1280]{1,0:T(8,128)S(1)}, f32[8,1280]{1,0:T(8,128)S(1)}, u32[]{:S(2)}, u32[]{:S(2)}) collective-permute-start(f32[8,1280]{1,0:T(8,128)S(1)} %convolution_bitcast_fusion), channel_id=1, source_target_pairs={{0,64},{16,80},{32,96},{48,112},{64,0},{80,16},{96,32},{112,48},{1... | collective-permute-start | bytes 122888 | tf_op jit(solution)/shard_map/ppermute | solution.py:16
  150.9 1.7 collective-permute-done.39
  152.6 1.6 collective-permute-start.40
  154.2 2.4 %collective-permute-done.40 = f32[8,1280]{1,0:T(8,128)S(1)} collective-permute-done((f32[8,1280]{1,0:T(8,128)S(1)}, f32[8,1280]{1,0:T(8,128)S(1)}, u32[]{:S(2)}, u32[]{:S(2)}) %collective-permute-start.40) | collective-permute-done | bytes 40992 | tf_op jit(solution)/shard_map/ppermute | solution.py:16
  156.7 0.9 collective-permute-start.41
  157.6 1.9 %collective-permute-done.41 = f32[8,1280]{1,0:T(8,128)S(1)} collective-permute-done((f32[8,1280]{1,0:T(8,128)S(1)}, f32[8,1280]{1,0:T(8,128)S(1)}, u32[]{:S(2)}, u32[]{:S(2)}) %collective-permute-start.41) | collective-permute-done | bytes 40992 | tf_op jit(solution)/shard_map/ppermute | solution.py:16
  159.6 0.7 through_logits.1.base
  160.3 0.8 through_slots.1
  161.1 8.4 %collective-permute-start.42 = (f32[128,1280]{1,0:T(8,128)S(1)}, f32[128,1280]{1,0:T(8,128)S(1)}, u32[]{:S(2)}, u32[]{:S(2)}) collective-permute-start(f32[128,1280]{1,0:T(8,128)S(1)} %get-tuple-element.98), channel_id=1, source_target_pairs={{0,1},{1,0},{2,3},{3,2},{4,5},{5,4},{6,7},{7,6},{8,9},{9,8},{10,11... | collective-permute-start | bytes 1966088 | tf_op jit(solution)/shard_map/ppermute | solution.py:16
  169.6 2.3 %collective-permute-start.43 = (f32[8,1280]{1,0:T(8,128)S(1)}, f32[8,1280]{1,0:T(8,128)S(1)}, u32[]{:S(2)}, u32[]{:S(2)}) collective-permute-start(f32[8,1280]{1,0:T(8,128)S(1)} %add.82), channel_id=1, source_target_pairs={{0,32},{16,48},{32,0},{48,16},{64,96},{80,112},{96,64},{112,80},{1... | collective-permute-start | bytes 122888 | tf_op jit(solution)/shard_map/ppermute | solution.py:16
  171.9 2.1 %collective-permute-done.43 = f32[8,1280]{1,0:T(8,128)S(1)} collective-permute-done((f32[8,1280]{1,0:T(8,128)S(1)}, f32[8,1280]{1,0:T(8,128)S(1)}, u32[]{:S(2)}, u32[]{:S(2)}) %collective-permute-start.43) | collective-permute-done | bytes 40992 | tf_op jit(solution)/shard_map/ppermute | solution.py:16
  174.6 0.8 add_convert_fusion
  (82 shorter events, 5.7 us)
Async XLA Ops:
  0.6 1.5 copy-start.2
  2.1 3.8 %copy-start.3 = (bf16[1280,8]{0,1:T(8,128)(2,1)S(1)}, bf16[1280,8]{0,1:T(8,128)(2,1)}, u32[]{:S(2)}) copy-start(bf16[1280,8]{0,1:T(8,128)(2,1)} %param.7) | copy-start | bytes 61444
  2.3 14.9 %collective-permute-start.3 = (bf16[2,80,1280]{2,1,0:T(8,128)(2,1)S(1)}, bf16[2,80,1280]{2,1,0:T(8,128)(2,1)S(1)}, u32[]{:S(2)}, u32[]{:S(2)}) collective-permute-start(bf16[2,80,1280]{2,1,0:T(8,128)(2,1)S(1)} %pad_maximum_fusion.5.refs_0_), channel_id=1, source_target_pairs={{0,48},{16,32},{32,16},{48,0},{64,112},{80,96},{96,80},{112,64},{1... | collective-permute-start | bytes 1228808 | tf_op jit(solution)/shard_map/ppermute | solution.py:16
  5.9 11.3 %collective-permute-start.2 = (bf16[2,80,1280]{2,1,0:T(8,128)(2,1)S(1)}, bf16[2,80,1280]{2,1,0:T(8,128)(2,1)S(1)}, u32[]{:S(2)}, u32[]{:S(2)}) collective-permute-start(bf16[2,80,1280]{2,1,0:T(8,128)(2,1)S(1)} %pad_maximum_fusion.5.refs_0_), channel_id=1, source_target_pairs={{0,16},{16,0},{32,48},{48,32},{64,80},{80,64},{96,112},{112,96},{1... | collective-permute-start | bytes 1228808 | tf_op jit(solution)/shard_map/ppermute | solution.py:16
  5.9 8.1 %collective-permute-start.4 = (bf16[8,1280]{1,0:T(8,128)(2,1)S(1)}, bf16[8,1280]{1,0:T(8,128)(2,1)S(1)}, u32[]{:S(2)}, u32[]{:S(2)}) collective-permute-start(bf16[8,1280]{1,0:T(8,128)(2,1)S(1)} %bitcast.69), channel_id=1, source_target_pairs={{0,2},{1,3},{2,0},{3,1},{4,6},{5,7},{6,4},{7,5},{8,10},{9,11},{10,... | collective-permute-start | bytes 61448 | tf_op jit(solution)/shard_map/ppermute | solution.py:16
  12.9 17.6 %collective-permute-start = (bf16[2,80,1280]{2,1,0:T(8,128)(2,1)S(1)}, bf16[2,80,1280]{2,1,0:T(8,128)(2,1)S(1)}, u32[]{:S(2)}, u32[]{:S(2)}) collective-permute-start(bf16[2,80,1280]{2,1,0:T(8,128)(2,1)S(1)} %pad_maximum_fusion.3), channel_id=1, source_target_pairs={{0,64},{16,80},{32,96},{48,112},{64,0},{80,16},{96,32},{112,48},{1... | collective-permute-start | bytes 1228808 | tf_op jit(solution)/shard_map/ppermute | solution.py:16
  14.0 3.1 %collective-permute-start.5 = (bf16[16,1280]{1,0:T(8,128)(2,1)S(1)}, bf16[16,1280]{1,0:T(8,128)(2,1)S(1)}, u32[]{:S(2)}, u32[]{:S(2)}) collective-permute-start(bf16[16,1280]{1,0:T(8,128)(2,1)S(1)} %pad_maximum_fusion.14), channel_id=1, source_target_pairs={{0,4},{1,5},{2,6},{3,7},{4,0},{5,1},{6,2},{7,3},{8,12},{9,13},{10,... | collective-permute-start | bytes 122888 | tf_op jit(solution)/shard_map/ppermute | solution.py:16
  15.2 24.1 %copy-start = (bf16[8,256,1280]{2,1,0:T(8,128)(2,1)S(1)}, bf16[8,256,1280]{2,1,0:T(8,128)(2,1)}, u32[]{:S(2)}) copy-start(bf16[8,256,1280]{2,1,0:T(8,128)(2,1)} %refs_1_.2) | copy-start | bytes 15728644
  15.3 15.2 %collective-permute-start.1 = (bf16[2,80,1280]{2,1,0:T(8,128)(2,1)S(1)}, bf16[2,80,1280]{2,1,0:T(8,128)(2,1)S(1)}, u32[]{:S(2)}, u32[]{:S(2)}) collective-permute-start(bf16[2,80,1280]{2,1,0:T(8,128)(2,1)S(1)} %pad_maximum_fusion.4), channel_id=1, source_target_pairs={{0,128},{16,144},{32,160},{48,176},{64,192},{80,208},{96,224},{112... | collective-permute-start | bytes 1228808 | tf_op jit(solution)/shard_map/ppermute | solution.py:16
  17.2 5.3 %collective-permute-start.8 = (bf16[32,1280]{1,0:T(8,128)(2,1)S(1)}, bf16[32,1280]{1,0:T(8,128)(2,1)S(1)}, u32[]{:S(2)}, u32[]{:S(2)}) collective-permute-start(bf16[32,1280]{1,0:T(8,128)(2,1)S(1)} %pad_maximum_fusion.12), channel_id=1, source_target_pairs={{0,8},{1,9},{2,10},{3,11},{4,12},{5,13},{6,14},{7,15},{8,0},{9,1},... | collective-permute-start | bytes 245768 | tf_op jit(solution)/shard_map/ppermute | solution.py:16
  22.5 5.6 %collective-permute-start.9 = (bf16[64,1280]{1,0:T(8,128)(2,1)S(1)}, bf16[64,1280]{1,0:T(8,128)(2,1)S(1)}, u32[]{:S(2)}, u32[]{:S(2)}) collective-permute-start(bf16[64,1280]{1,0:T(8,128)(2,1)S(1)} %pad_maximum_fusion.10), channel_id=1, source_target_pairs={{0,1},{1,0},{2,3},{3,2},{4,5},{5,4},{6,7},{7,6},{8,9},{9,8},{10,11... | collective-permute-start | bytes 491528 | tf_op jit(solution)/shard_map/ppermute | solution.py:16
  26.3 8.0 %collective-permute-start.7 = (bf16[80,1280]{1,0:T(8,128)(2,1)S(1)}, bf16[80,1280]{1,0:T(8,128)(2,1)S(1)}, u32[]{:S(2)}, u32[]{:S(2)}) collective-permute-start(bf16[80,1280]{1,0:T(8,128)(2,1)S(1)} %slice_bitcast_fusion.4), channel_id=1, source_target_pairs={{0,48},{16,32},{32,16},{48,0},{64,112},{80,96},{96,80},{112,64},{1... | collective-permute-start | bytes 614408 | tf_op jit(solution)/shard_map/ppermute | solution.py:16
  27.2 7.1 %collective-permute-start.6 = (bf16[80,1280]{1,0:T(8,128)(2,1)S(1)}, bf16[80,1280]{1,0:T(8,128)(2,1)S(1)}, u32[]{:S(2)}, u32[]{:S(2)}) collective-permute-start(bf16[80,1280]{1,0:T(8,128)(2,1)S(1)} %slice_bitcast_fusion.5), channel_id=1, source_target_pairs={{0,16},{16,0},{32,48},{48,32},{64,80},{80,64},{96,112},{112,96},{1... | collective-permute-start | bytes 614408 | tf_op jit(solution)/shard_map/ppermute | solution.py:16
  34.3 18.3 %collective-permute-start.11 = (bf16[2,2,80,1280]{3,2,1,0:T(8,128)(2,1)S(1)}, bf16[2,2,80,1280]{3,2,1,0:T(8,128)(2,1)S(1)}, u32[]{:S(2)}, u32[]{:S(2)}) collective-permute-start(bf16[2,2,80,1280]{3,2,1,0:T(8,128)(2,1)S(1)} %pad_maximum_fusion.refs_5_), channel_id=1, source_target_pairs={{0,48},{16,32},{32,16},{48,0},{64,112},{80,96},{96,80},{112,64},{1... | collective-permute-start | bytes 2457608 | tf_op jit(solution)/shard_map/ppermute | solution.py:16
  35.6 17.3 %collective-permute-start.10 = (bf16[2,2,80,1280]{3,2,1,0:T(8,128)(2,1)S(1)}, bf16[2,2,80,1280]{3,2,1,0:T(8,128)(2,1)S(1)}, u32[]{:S(2)}, u32[]{:S(2)}) collective-permute-start(bf16[2,2,80,1280]{3,2,1,0:T(8,128)(2,1)S(1)} %pad_maximum_fusion.refs_5_), channel_id=1, source_target_pairs={{0,16},{16,0},{32,48},{48,32},{64,80},{80,64},{96,112},{112,96},{1... | collective-permute-start | bytes 2457608 | tf_op jit(solution)/shard_map/ppermute | solution.py:16
  36.0 15.0 %collective-permute-start.12 = (bf16[2,80,1280]{2,1,0:T(8,128)(2,1)S(1)}, bf16[2,80,1280]{2,1,0:T(8,128)(2,1)S(1)}, u32[]{:S(2)}, u32[]{:S(2)}) collective-permute-start(bf16[2,80,1280]{2,1,0:T(8,128)(2,1)S(1)} %pad_maximum_fusion.6), channel_id=1, source_target_pairs={{0,192},{16,208},{32,224},{48,240},{64,128},{80,144},{96,160},{112... | collective-permute-start | bytes 1228808 | tf_op jit(solution)/shard_map/ppermute | solution.py:16
  39.3 2.5 %copy-start.1 = (bf16[8,256,1280]{2,1,0:T(8,128)(2,1)S(1)}, bf16[8,256,1280]{2,1,0:T(8,128)(2,1)}, u32[]{:S(2)}) copy-start(bf16[8,256,1280]{2,1,0:T(8,128)(2,1)} %refs_1_.3) | copy-start | bytes 15728644
  52.9 15.9 %collective-permute-start.16 = (bf16[128,1280]{1,0:T(8,128)(2,1)S(1)}, bf16[128,1280]{1,0:T(8,128)(2,1)S(1)}, u32[]{:S(2)}, u32[]{:S(2)}) collective-permute-start(bf16[128,1280]{1,0:T(8,128)(2,1)S(1)} %bitcast.61), channel_id=1, source_target_pairs={{0,128},{16,144},{32,160},{48,176},{64,192},{80,208},{96,224},{112... | collective-permute-start | bytes 983048 | tf_op jit(solution)/shard_map/ppermute | solution.py:16
  56.2 11.8 %collective-permute-start.13 = (bf16[128,1280]{1,0:T(8,128)(2,1)S(1)}, bf16[128,1280]{1,0:T(8,128)(2,1)S(1)}, u32[]{:S(2)}, u32[]{:S(2)}) collective-permute-start(bf16[128,1280]{1,0:T(8,128)(2,1)S(1)} %bitcast.62), channel_id=1, source_target_pairs={{0,64},{16,80},{32,96},{48,112},{64,0},{80,16},{96,32},{112,48},{1... | collective-permute-start | bytes 983048 | tf_op jit(solution)/shard_map/ppermute | solution.py:16
  57.1 11.7 %collective-permute-start.15 = (bf16[2,80,1280]{2,1,0:T(8,128)(2,1)S(1)}, bf16[2,80,1280]{2,1,0:T(8,128)(2,1)S(1)}, u32[]{:S(2)}, u32[]{:S(2)}) collective-permute-start(bf16[2,80,1280]{2,1,0:T(8,128)(2,1)S(1)} %collective-permute-done.12.refs_10_), channel_id=1, source_target_pairs={{0,48},{16,32},{32,16},{48,0},{64,112},{80,96},{96,80},{112,64},{1... | collective-permute-start | bytes 1228808 | tf_op jit(solution)/shard_map/ppermute | solution.py:16
  58.2 10.6 %collective-permute-start.14 = (bf16[2,80,1280]{2,1,0:T(8,128)(2,1)S(1)}, bf16[2,80,1280]{2,1,0:T(8,128)(2,1)S(1)}, u32[]{:S(2)}, u32[]{:S(2)}) collective-permute-start(bf16[2,80,1280]{2,1,0:T(8,128)(2,1)S(1)} %collective-permute-done.12.refs_10_), channel_id=1, source_target_pairs={{0,16},{16,0},{32,48},{48,32},{64,80},{80,64},{96,112},{112,96},{1... | collective-permute-start | bytes 1228808 | tf_op jit(solution)/shard_map/ppermute | solution.py:16
  59.1 15.5 %collective-permute-start.18 = (bf16[2,80,1280]{2,1,0:T(8,128)(2,1)S(1)}, bf16[2,80,1280]{2,1,0:T(8,128)(2,1)S(1)}, u32[]{:S(2)}, u32[]{:S(2)}) collective-permute-start(bf16[2,80,1280]{2,1,0:T(8,128)(2,1)S(1)} %slice_bitcast_fusion), channel_id=1, source_target_pairs={{0,48},{16,32},{32,16},{48,0},{64,112},{80,96},{96,80},{112,64},{1... | collective-permute-start | bytes 1228808 | tf_op jit(solution)/shard_map/ppermute | solution.py:16
  68.0 7.8 %collective-permute-start.17 = (bf16[2,80,1280]{2,1,0:T(8,128)(2,1)S(1)}, bf16[2,80,1280]{2,1,0:T(8,128)(2,1)S(1)}, u32[]{:S(2)}, u32[]{:S(2)}) collective-permute-start(bf16[2,80,1280]{2,1,0:T(8,128)(2,1)S(1)} %slice_bitcast_fusion.1), channel_id=1, source_target_pairs={{0,16},{16,0},{32,48},{48,32},{64,80},{80,64},{96,112},{112,96},{1... | collective-permute-start | bytes 1228808 | tf_op jit(solution)/shard_map/ppermute | solution.py:16
  68.8 10.2 %collective-permute-start.20 = (bf16[80,1280]{1,0:T(8,128)(2,1)S(1)}, bf16[80,1280]{1,0:T(8,128)(2,1)S(1)}, u32[]{:S(2)}, u32[]{:S(2)}) collective-permute-start(bf16[80,1280]{1,0:T(8,128)(2,1)S(1)} %slice_bitcast_fusion.2), channel_id=1, source_target_pairs={{0,48},{16,32},{32,16},{48,0},{64,112},{80,96},{96,80},{112,64},{1... | collective-permute-start | bytes 614408 | tf_op jit(solution)/shard_map/ppermute | solution.py:16
  70.7 9.5 %collective-permute-start.19 = (bf16[80,1280]{1,0:T(8,128)(2,1)S(1)}, bf16[80,1280]{1,0:T(8,128)(2,1)S(1)}, u32[]{:S(2)}, u32[]{:S(2)}) collective-permute-start(bf16[80,1280]{1,0:T(8,128)(2,1)S(1)} %slice_bitcast_fusion.3), channel_id=1, source_target_pairs={{0,16},{16,0},{32,48},{48,32},{64,80},{80,64},{96,112},{112,96},{1... | collective-permute-start | bytes 614408 | tf_op jit(solution)/shard_map/ppermute | solution.py:16
  71.3 8.9 %collective-permute-start.21 = (bf16[128,1280]{1,0:T(8,128)(2,1)S(1)}, bf16[128,1280]{1,0:T(8,128)(2,1)S(1)}, u32[]{:S(2)}, u32[]{:S(2)}) collective-permute-start(bf16[128,1280]{1,0:T(8,128)(2,1)S(1)} %collective-permute-done.16), channel_id=1, source_target_pairs={{0,64},{16,80},{32,96},{48,112},{64,0},{80,16},{96,32},{112,48},{1... | collective-permute-start | bytes 983048 | tf_op jit(solution)/shard_map/ppermute | solution.py:16
  80.2 19.5 %slice-start = ((s8[5242880]{0:T(1024)(128)(4,1)}), s8[4194304]{0:T(1024)(128)(4,1)S(1)}, s32[]{:S(2)}) async-start(s8[5242880]{0:T(1024)(128)(4,1)} %bitcast.59), calls=%async_computation | async-start | bytes 8388608
  80.3 19.4 %slice-start.1 = ((s8[5242880]{0:T(1024)(128)(4,1)}), s8[1048576]{0:T(1024)(128)(4,1)S(1)}, s32[]{:S(2)}) async-start(s8[5242880]{0:T(1024)(128)(4,1)} %bitcast.59), calls=%async_computation.1 | async-start | bytes 2097152
  84.4 9.7 %collective-permute-start.29 = (bf16[64,1280]{1,0:T(8,128)(2,1)S(1)}, bf16[64,1280]{1,0:T(8,128)(2,1)S(1)}, u32[]{:S(2)}, u32[]{:S(2)}) collective-permute-start(bf16[64,1280]{1,0:T(8,128)(2,1)S(1)} %get-tuple-element.86), channel_id=1, source_target_pairs={{0,64},{16,80},{32,96},{48,112},{64,0},{80,16},{96,32},{112,48},{1... | collective-permute-start | bytes 491528 | tf_op jit(solution)/shard_map/ppermute | solution.py:16
  86.7 8.5 %collective-permute-start.30 = (bf16[64,1280]{1,0:T(8,128)(2,1)S(1)}, bf16[64,1280]{1,0:T(8,128)(2,1)S(1)}, u32[]{:S(2)}, u32[]{:S(2)}) collective-permute-start(bf16[64,1280]{1,0:T(8,128)(2,1)S(1)} %get-tuple-element.87), channel_id=1, source_target_pairs={{0,128},{16,144},{32,160},{48,176},{64,192},{80,208},{96,224},{112... | collective-permute-start | bytes 491528 | tf_op jit(solution)/shard_map/ppermute | solution.py:16
  90.6 9.1 %collective-permute-start.31 = (bf16[64,1280]{1,0:T(8,128)(2,1)S(1)}, bf16[64,1280]{1,0:T(8,128)(2,1)S(1)}, u32[]{:S(2)}, u32[]{:S(2)}) collective-permute-start(bf16[64,1280]{1,0:T(8,128)(2,1)S(1)} %get-tuple-element.88), channel_id=1, source_target_pairs={{0,192},{16,208},{32,224},{48,240},{64,128},{80,144},{96,160},{112... | collective-permute-start | bytes 491528 | tf_op jit(solution)/shard_map/ppermute | solution.py:16
  91.7 25.9 %collective-permute-start.22 = (bf16[64,1280]{1,0:T(8,128)(2,1)S(1)}, bf16[64,1280]{1,0:T(8,128)(2,1)S(1)}, u32[]{:S(2)}, u32[]{:S(2)}) collective-permute-start(bf16[64,1280]{1,0:T(8,128)(2,1)S(1)} %get-tuple-element.75), channel_id=1, source_target_pairs={{0,64},{16,80},{32,96},{48,112},{64,0},{80,16},{96,32},{112,48},{1... | collective-permute-start | bytes 491528 | tf_op jit(solution)/shard_map/ppermute | solution.py:16
  91.9 25.6 %collective-permute-start.23 = (bf16[64,1280]{1,0:T(8,128)(2,1)S(1)}, bf16[64,1280]{1,0:T(8,128)(2,1)S(1)}, u32[]{:S(2)}, u32[]{:S(2)}) collective-permute-start(bf16[64,1280]{1,0:T(8,128)(2,1)S(1)} %get-tuple-element.76), channel_id=1, source_target_pairs={{0,128},{16,144},{32,160},{48,176},{64,192},{80,208},{96,224},{112... | collective-permute-start | bytes 491528 | tf_op jit(solution)/shard_map/ppermute | solution.py:16
  94.1 23.4 %collective-permute-start.24 = (bf16[64,1280]{1,0:T(8,128)(2,1)S(1)}, bf16[64,1280]{1,0:T(8,128)(2,1)S(1)}, u32[]{:S(2)}, u32[]{:S(2)}) collective-permute-start(bf16[64,1280]{1,0:T(8,128)(2,1)S(1)} %get-tuple-element.77), channel_id=1, source_target_pairs={{0,192},{16,208},{32,224},{48,240},{64,128},{80,144},{96,160},{112... | collective-permute-start | bytes 491528 | tf_op jit(solution)/shard_map/ppermute | solution.py:16
  101.8 8.7 %collective-permute-start.32 = (f32[8,256]{1,0:T(8,128)S(1)}, f32[8,256]{1,0:T(8,128)S(1)}, u32[]{:S(2)}, u32[]{:S(2)}) collective-permute-start(f32[8,256]{1,0:T(8,128)S(1)} %get-tuple-element.94), channel_id=1, source_target_pairs={{0,1},{1,0},{2,3},{3,2},{4,5},{5,4},{6,7},{7,6},{8,9},{9,8},{10,11... | collective-permute-start | bytes 24584 | tf_op jit(solution)/shard_map/ppermute | solution.py:16
  110.5 6.5 %collective-permute-start.33 = (f32[8,256]{1,0:T(8,128)S(1)}, f32[8,256]{1,0:T(8,128)S(1)}, u32[]{:S(2)}, u32[]{:S(2)}) collective-permute-start(f32[8,256]{1,0:T(8,128)S(1)} %add.75), channel_id=1, source_target_pairs={{0,2},{1,3},{2,0},{3,1},{4,6},{5,7},{6,4},{7,5},{8,10},{9,11},{10,... | collective-permute-start | bytes 24584 | tf_op jit(solution)/shard_map/ppermute | solution.py:16
  117.0 2.5 %collective-permute-start.34 = (f32[8,256]{1,0:T(8,128)S(1)}, f32[8,256]{1,0:T(8,128)S(1)}, u32[]{:S(2)}, u32[]{:S(2)}) collective-permute-start(f32[8,256]{1,0:T(8,128)S(1)} %add.76), channel_id=1, source_target_pairs={{0,4},{1,5},{2,6},{3,7},{4,0},{5,1},{6,2},{7,3},{8,12},{9,13},{10,... | collective-permute-start | bytes 24584 | tf_op jit(solution)/shard_map/ppermute | solution.py:16
  119.6 9.9 %collective-permute-start.35 = (f32[8,256]{1,0:T(8,128)S(1)}, f32[8,256]{1,0:T(8,128)S(1)}, u32[]{:S(2)}, u32[]{:S(2)}) collective-permute-start(f32[8,256]{1,0:T(8,128)S(1)} %add.77), channel_id=1, source_target_pairs={{0,8},{1,9},{2,10},{3,11},{4,12},{5,13},{6,14},{7,15},{8,0},{9,1},... | collective-permute-start | bytes 24584 | tf_op jit(solution)/shard_map/ppermute | solution.py:16
  121.7 14.9 %collective-permute-start.25 = (bf16[64,1280]{1,0:T(8,128)(2,1)S(1)}, bf16[64,1280]{1,0:T(8,128)(2,1)S(1)}, u32[]{:S(2)}, u32[]{:S(2)}) collective-permute-start(bf16[64,1280]{1,0:T(8,128)(2,1)S(1)} %get-tuple-element.100), channel_id=1, source_target_pairs={{0,2},{1,3},{2,0},{3,1},{4,6},{5,7},{6,4},{7,5},{8,10},{9,11},{10,... | collective-permute-start | bytes 491528 | tf_op jit(solution)/shard_map/ppermute | solution.py:16
  129.5 7.1 %collective-permute-start.36 = (bf16[64,256]{1,0:T(8,128)(2,1)S(1)}, bf16[64,256]{1,0:T(8,128)(2,1)S(1)}, u32[]{:S(2)}, u32[]{:S(2)}) collective-permute-start(bf16[64,256]{1,0:T(8,128)(2,1)S(1)} %fusion.2), channel_id=1, source_target_pairs={{0,2},{1,3},{2,0},{3,1},{4,6},{5,7},{6,4},{7,5},{8,10},{9,11},{10,... | collective-permute-start | bytes 98312 | tf_op jit(solution)/shard_map/ppermute | solution.py:16
  136.6 4.1 %collective-permute-start.37 = (bf16[128,256]{1,0:T(8,128)(2,1)S(1)}, bf16[128,256]{1,0:T(8,128)(2,1)S(1)}, u32[]{:S(2)}, u32[]{:S(2)}) collective-permute-start(bf16[128,256]{1,0:T(8,128)(2,1)S(1)} %pad_maximum_fusion.13), channel_id=1, source_target_pairs={{0,4},{1,5},{2,6},{3,7},{4,0},{5,1},{6,2},{7,3},{8,12},{9,13},{10,... | collective-permute-start | bytes 196616 | tf_op jit(solution)/shard_map/ppermute | solution.py:16
  137.3 22.9 %collective-permute-start.28 = (bf16[2,64,1280]{2,1,0:T(8,128)(2,1)S(1)}, bf16[2,64,1280]{2,1,0:T(8,128)(2,1)S(1)}, u32[]{:S(2)}, u32[]{:S(2)}) collective-permute-start(bf16[2,64,1280]{2,1,0:T(8,128)(2,1)S(1)} %pad_maximum_fusion.8.pair), channel_id=1, source_target_pairs={{0,12},{1,13},{2,14},{3,15},{4,8},{5,9},{6,10},{7,11},{8,4},{9,5},... | collective-permute-start | bytes 983048 | tf_op jit(solution)/shard_map/ppermute | solution.py:16
  137.6 22.6 %collective-permute-start.27 = (bf16[2,64,1280]{2,1,0:T(8,128)(2,1)S(1)}, bf16[2,64,1280]{2,1,0:T(8,128)(2,1)S(1)}, u32[]{:S(2)}, u32[]{:S(2)}) collective-permute-start(bf16[2,64,1280]{2,1,0:T(8,128)(2,1)S(1)} %pad_maximum_fusion.8.pair), channel_id=1, source_target_pairs={{0,8},{1,9},{2,10},{3,11},{4,12},{5,13},{6,14},{7,15},{8,0},{9,1},... | collective-permute-start | bytes 983048 | tf_op jit(solution)/shard_map/ppermute | solution.py:16
  140.0 20.3 %collective-permute-start.26 = (bf16[2,64,1280]{2,1,0:T(8,128)(2,1)S(1)}, bf16[2,64,1280]{2,1,0:T(8,128)(2,1)S(1)}, u32[]{:S(2)}, u32[]{:S(2)}) collective-permute-start(bf16[2,64,1280]{2,1,0:T(8,128)(2,1)S(1)} %pad_maximum_fusion.8.pair), channel_id=1, source_target_pairs={{0,4},{1,5},{2,6},{3,7},{4,0},{5,1},{6,2},{7,3},{8,12},{9,13},{10,... | collective-permute-start | bytes 983048 | tf_op jit(solution)/shard_map/ppermute | solution.py:16
  140.7 18.8 %collective-permute-start.38 = (bf16[256,256]{1,0:T(8,128)(2,1)S(1)}, bf16[256,256]{1,0:T(8,128)(2,1)S(1)}, u32[]{:S(2)}, u32[]{:S(2)}) collective-permute-start(bf16[256,256]{1,0:T(8,128)(2,1)S(1)} %pad_maximum_fusion.11), channel_id=1, source_target_pairs={{0,8},{1,9},{2,10},{3,11},{4,12},{5,13},{6,14},{7,15},{8,0},{9,1},... | collective-permute-start | bytes 393224 | tf_op jit(solution)/shard_map/ppermute | solution.py:16
  142.9 9.7 %collective-permute-start.39 = (f32[8,1280]{1,0:T(8,128)S(1)}, f32[8,1280]{1,0:T(8,128)S(1)}, u32[]{:S(2)}, u32[]{:S(2)}) collective-permute-start(f32[8,1280]{1,0:T(8,128)S(1)} %convolution_bitcast_fusion), channel_id=1, source_target_pairs={{0,64},{16,80},{32,96},{48,112},{64,0},{80,16},{96,32},{112,48},{1... | collective-permute-start | bytes 122888 | tf_op jit(solution)/shard_map/ppermute | solution.py:16
  152.6 4.0 %collective-permute-start.40 = (f32[8,1280]{1,0:T(8,128)S(1)}, f32[8,1280]{1,0:T(8,128)S(1)}, u32[]{:S(2)}, u32[]{:S(2)}) collective-permute-start(f32[8,1280]{1,0:T(8,128)S(1)} %add.80), channel_id=1, source_target_pairs={{0,128},{16,144},{32,160},{48,176},{64,192},{80,208},{96,224},{112... | collective-permute-start | bytes 122888 | tf_op jit(solution)/shard_map/ppermute | solution.py:16
  156.7 2.9 %collective-permute-start.41 = (f32[8,1280]{1,0:T(8,128)S(1)}, f32[8,1280]{1,0:T(8,128)S(1)}, u32[]{:S(2)}, u32[]{:S(2)}) collective-permute-start(f32[8,1280]{1,0:T(8,128)S(1)} %add.81), channel_id=1, source_target_pairs={{0,16},{16,0},{32,48},{48,32},{64,80},{80,64},{96,112},{112,96},{1... | collective-permute-start | bytes 122888 | tf_op jit(solution)/shard_map/ppermute | solution.py:16
  161.1 13.4 %collective-permute-start.42 = (f32[128,1280]{1,0:T(8,128)S(1)}, f32[128,1280]{1,0:T(8,128)S(1)}, u32[]{:S(2)}, u32[]{:S(2)}) collective-permute-start(f32[128,1280]{1,0:T(8,128)S(1)} %get-tuple-element.98), channel_id=1, source_target_pairs={{0,1},{1,0},{2,3},{3,2},{4,5},{5,4},{6,7},{7,6},{8,9},{9,8},{10,11... | collective-permute-start | bytes 1966088 | tf_op jit(solution)/shard_map/ppermute | solution.py:16
  169.6 4.4 %collective-permute-start.43 = (f32[8,1280]{1,0:T(8,128)S(1)}, f32[8,1280]{1,0:T(8,128)S(1)}, u32[]{:S(2)}, u32[]{:S(2)}) collective-permute-start(f32[8,1280]{1,0:T(8,128)S(1)} %add.82), channel_id=1, source_target_pairs={{0,32},{16,48},{32,0},{48,16},{64,96},{80,112},{96,64},{112,80},{1... | collective-permute-start | bytes 122888 | tf_op jit(solution)/shard_map/ppermute | solution.py:16

commit v3 on v2

--- a/solution.py
+++ b/solution.py
@@ -295,23 +295,25 @@
     table = doubled(slot_params.T, "expert", 2, 4)
     l0, r0, table = together(l0, r0, table)
     p0, q0 = swap(r0[0], "dp", 1), swap(l0[1], "dp", 3)
-    table = doubled(table, "expert", 8, 1)
+    table = doubled(table, "expert", 8)
 
     u1, u2, p0, q0, table = together(u1, u2, p0, q0, table)
     both = jnp.stack([u1, u2], axis=1)
     lb, rb = swap(both, "dp", 1), swap(both, "dp", 3)
     u3 = swap(after(units[3], u1), "dp", 12)
+    table = doubled(table, "expert", 1)
     rows, dispatch, combine, spread = slots_call(table, tokens, out_grad)
     rows = rows.reshape(2 * half, width)
 
     lb, rb, u3, rows = together(lb, rb, u3, rows)
-    z1, z2 = swap(rows, "dp", 4), swap(rows, "dp", 8)
+    z2 = swap(rows, "dp", 8)
     l3, r3 = swap(u3, "dp", 1), swap(u3, "dp", 3)
     pb, qb = swap(rb[0], "dp", 1), swap(lb[1], "dp", 3)
-    l3, r3, z2 = together(l3, r3, z2)
+    l3, r3 = together(l3, r3)
     p3, q3 = swap(r3[0], "dp", 1), swap(l3[1], "dp", 3)
+    z1 = swap(after(rows, l3), "dp", 4)
     z3 = swap(z2, "dp", 4)
-    pb, qb, p3, q3, z3 = together(pb, qb, p3, q3, z3)
+    pb, qb, p3, q3, z1, z3 = together(pb, qb, p3, q3, z1, z3)
     rows_in = jnp.concatenate([v[:half] for v in (rows, z1, z2, z3)], axis=0)
     rows_go = jnp.concatenate([v[half:] for v in (rows, z1, z2, z3)], axis=0)
 
@@ -323,22 +325,28 @@
     far = swap(near, "expert", 2)
 
     part, mix = against(slot_out, out_grad, combine, False)
-    mix = summed(mix, "expert", 1, 2, 4, 8)
+    mix = summed(mix, "expert", 1, 2, 4)
+    mix = summed(after(mix, near), "expert", 8)
     (back,) = against(slot_in_grad, tokens, dispatch, True)
     logit_grad = back + (part - combine * jnp.repeat(mix, own, axis=0))
     logit_grad_b = logit_grad.astype(BF16)
-    slot_term = jnp.einsum(
+    term = jnp.einsum(
         "bsm,bmd->sd", logit_grad_b.reshape(images, own, count), tokens, preferred_element_type=F32
     )
+
     line = doubled(logit_grad_b, "expert", 2)
-    line = doubled(after(line, far), "expert", 4, 8)
+    term = summed(term, "dp", 4)
+    line, term, far = together(line, term, far)
+    pieces = all_x(jnp.stack([near, far]))
+    line = doubled(line, "expert", 4)
+    term = summed(term, "dp", 8)
+    line, term = together(line, term)
+    line = doubled(line, "expert", 8)
+    term = summed(term, "dp", 1)
     base = lines_call(line, table)
-
-    pieces = all_x(jnp.stack([near, far]))
-    slot_sum = summed(slot_term, "dp", 4, 8, 1)
-    slot_grad = summed(after(slot_sum, *pieces), "dp", 2).T
-
-    mine, theirs = spread_call(spread, pieces, after(base, slot_sum))
+    slot_grad = summed(after(term, *pieces), "dp", 2).T
+
+    mine, theirs = spread_call(spread, pieces, after(base, term))
     token_grad = (mine + swap(theirs, "expert", 1)).astype(BF16)
     return (token_grad.reshape(images, -1, width), slot_grad)
 

time: 175 us -> 181 us (1.034)
  waiting for transfers between devices: 50 us -> 56.9 us
    ppermute x44, waiting for transfers between devices: 50 us -> 56.9 us  [swap(): return lax.ppermute(value, axis, [(i, i ^ k) for i in range(count)])]
  transfers between devices with their start and end apart: 44 -> 44, of which waited for: 21 -> 17; matrix products, arithmetic and copies ran while one was open for 1% -> 1% of each run, Pallas kernels for 8% -> 8%
where the time goes in v3:
time: 181 us; the launch traced here: 180 us
  starting transfers between devices  96.3 us (53%)
  waiting for transfers between devices  56.9 us (31%)
  Pallas kernels  19.1 us (11%)
  local copies, waits for them, and re-layouts  4.25 us (2%)
  other arithmetic  2.04 us (1%)
    ppermute x44, starting transfers between devices, swap(): return lax.ppermute(value, axis, [(i, i ^ k) for i in range(count)])  96.3 us
    ppermute x44, waiting for transfers between devices, swap(): return lax.ppermute(value, axis, [(i, i ^ k) for i in range(count)])  56.9 us
    pallas_call x1, Pallas kernels, slots_call(): pl.pallas_call(slots_kernel, grid=(images // 2,), out_shape=[jax.ShapeDty...  9.17 us
    pallas_call x2, Pallas kernels, against(): pl.pallas_call(lambda *refs: against_kernel(over_tokens, *refs), grid=(im...  4.36 us
    pallas_call x1, Pallas kernels, ffn(): pl.pallas_call(ffn_kernel, out_shape=[jax.ShapeDtypeStruct((own_rows, wid...  4.04 us
  transfers between devices with their start and end apart: 44, of which 17 were waited for; matrix products, arithmetic and copies ran while one was open for 1% of the time, Pallas kernels for 8%

profile of v3, /device:TPU:1, one launch (start us, length us, event | category | flops | bytes accessed | tf_op | source)
XLA Modules:
  0.0 180.5 jit_solution(6677122247983007560)
XLA Ops:
  0.7 1.4 dynamic-slice_bitcast_fusion.1
  2.3 3.7 %collective-permute-start.3 = (bf16[2,80,1280]{2,1,0:T(8,128)(2,1)S(1)}, bf16[2,80,1280]{2,1,0:T(8,128)(2,1)S(1)}, u32[]{:S(2)}, u32[]{:S(2)}) collective-permute-start(bf16[2,80,1280]{2,1,0:T(8,128)(2,1)S(1)} %pad_maximum_fusion.5.refs_0_), channel_id=1, source_target_pairs={{0,48},{16,32},{32,16},{48,0},{64,112},{80,96},{96,80},{112,64},{1... | collective-permute-start | bytes 1228808 | tf_op jit(solution)/shard_map/ppermute | solution.py:16
  5.9 6.9 %collective-permute-start.4 = (bf16[8,1280]{1,0:T(8,128)(2,1)S(1)}, bf16[8,1280]{1,0:T(8,128)(2,1)S(1)}, u32[]{:S(2)}, u32[]{:S(2)}) collective-permute-start(bf16[8,1280]{1,0:T(8,128)(2,1)S(1)} %bitcast.69), channel_id=1, source_target_pairs={{0,2},{1,3},{2,0},{3,1},{4,6},{5,7},{6,4},{7,5},{8,10},{9,11},{10,... | collective-permute-start | bytes 61448 | tf_op jit(solution)/shard_map/ppermute | solution.py:16
  12.9 0.8 collective-permute-start
  14.0 1.2 collective-permute-start.5
  15.3 1.5 collective-permute-start.1
  16.8 0.4 collective-permute-done.5
  17.2 2.8 %collective-permute-start.8 = (bf16[32,1280]{1,0:T(8,128)(2,1)S(1)}, bf16[32,1280]{1,0:T(8,128)(2,1)S(1)}, u32[]{:S(2)}, u32[]{:S(2)}) collective-permute-start(bf16[32,1280]{1,0:T(8,128)(2,1)S(1)} %pad_maximum_fusion.11), channel_id=1, source_target_pairs={{0,8},{1,9},{2,10},{3,11},{4,12},{5,13},{6,14},{7,15},{8,0},{9,1},... | collective-permute-start | bytes 245768 | tf_op jit(solution)/shard_map/ppermute | solution.py:16
  20.0 0.7 collective-permute-start.7
  20.8 0.6 collective-permute-start.6
  21.4 1.1 collective-permute-done.8
  22.5 7.9 %collective-permute-done = bf16[2,80,1280]{2,1,0:T(8,128)(2,1)S(1)} collective-permute-done((bf16[2,80,1280]{2,1,0:T(8,128)(2,1)S(1)}, bf16[2,80,1280]{2,1,0:T(8,128)(2,1)S(1)}, u32[]{:S(2)}, u32[]{:S(2)}) %collective-permute-start) | collective-permute-done | bytes 409632 | tf_op jit(solution)/shard_map/ppermute | solution.py:16
  30.5 0.8 collective-permute-start.11
  31.3 0.9 collective-permute-start.10
  32.3 6.8 %collective-permute-start.9 = (bf16[64,1280]{1,0:T(8,128)(2,1)S(1)}, bf16[64,1280]{1,0:T(8,128)(2,1)S(1)}, u32[]{:S(2)}, u32[]{:S(2)}) collective-permute-start(bf16[64,1280]{1,0:T(8,128)(2,1)S(1)} %pad_maximum_fusion.9), channel_id=1, source_target_pairs={{0,1},{1,0},{2,3},{3,2},{4,5},{5,4},{6,7},{7,6},{8,9},{9,8},{10,11... | collective-permute-start | bytes 491528 | tf_op jit(solution)/shard_map/ppermute | solution.py:16
  39.1 2.9 %collective-permute-start.12 = (bf16[2,80,1280]{2,1,0:T(8,128)(2,1)S(1)}, bf16[2,80,1280]{2,1,0:T(8,128)(2,1)S(1)}, u32[]{:S(2)}, u32[]{:S(2)}) collective-permute-start(bf16[2,80,1280]{2,1,0:T(8,128)(2,1)S(1)} %pad_maximum_fusion.6), channel_id=1, source_target_pairs={{0,192},{16,208},{32,224},{48,240},{64,128},{80,144},{96,160},{112... | collective-permute-start | bytes 1228808 | tf_op jit(solution)/shard_map/ppermute | solution.py:16
  42.1 2.5 %copy-done.1 = bf16[8,256,1280]{2,1,0:T(8,128)(2,1)S(1)} copy-done((bf16[8,256,1280]{2,1,0:T(8,128)(2,1)S(1)}, bf16[8,256,1280]{2,1,0:T(8,128)(2,1)}, u32[]{:S(2)}) %copy-start.1) | copy-done | bytes 5242904
  44.6 9.2 %slots.1 = (bf16[2,64,1280]{2,1,0:T(8,128)(2,1)S(1)}, f32[64,256]{1,0:T(8,128)S(1)}, f32[64,256]{1,0:T(8,128)S(1)}, bf16[2,128,512]{2,1,0:T(8,128)(2,1)S(1)}) custom-call(bf16[128,1280]{1,0:T(8,128)(2,1)S(1)} %constant_dynamic-update-slice_fusion.table, bf16[8,256,1280]{2,1,0:T(8,128)(2,1)S(1)} %copy-done, bf16[8,256,1280]{2,1,0:T(8,128)(2,1)S(1)} %copy-done.1), custom_call_target="tpu_custom_call" | custom-call | tf_op jit(solution)/shard_map/slots/pallas_call | solution.py:117
  53.8 2.3 %collective-permute-start.16 = (bf16[2,80,1280]{2,1,0:T(8,128)(2,1)S(1)}, bf16[2,80,1280]{2,1,0:T(8,128)(2,1)S(1)}, u32[]{:S(2)}, u32[]{:S(2)}) collective-permute-start(bf16[2,80,1280]{2,1,0:T(8,128)(2,1)S(1)} %collective-permute-done.12.refs_10_), channel_id=1, source_target_pairs={{0,48},{16,32},{32,16},{48,0},{64,112},{80,96},{96,80},{112,64},{1... | collective-permute-start | bytes 1228808 | tf_op jit(solution)/shard_map/ppermute | solution.py:16
  56.1 5.0 %collective-permute-start.20 = (bf16[128,1280]{1,0:T(8,128)(2,1)S(1)}, bf16[128,1280]{1,0:T(8,128)(2,1)S(1)}, u32[]{:S(2)}, u32[]{:S(2)}) collective-permute-start(bf16[128,1280]{1,0:T(8,128)(2,1)S(1)} %bitcast.61), channel_id=1, source_target_pairs={{0,128},{16,144},{32,160},{48,176},{64,192},{80,208},{96,224},{112... | collective-permute-start | bytes 983048 | tf_op jit(solution)/shard_map/ppermute | solution.py:16
  61.2 0.8 collective-permute-start.14
  62.0 0.9 collective-permute-start.13
  62.9 12.1 %collective-permute-done.20 = bf16[128,1280]{1,0:T(8,128)(2,1)S(1)} collective-permute-done((bf16[128,1280]{1,0:T(8,128)(2,1)S(1)}, bf16[128,1280]{1,0:T(8,128)(2,1)S(1)}, u32[]{:S(2)}, u32[]{:S(2)}) %collective-permute-start.20) | collective-permute-done | bytes 327712 | tf_op jit(solution)/shard_map/ppermute | solution.py:16
  75.0 0.9 collective-permute-start.18
  75.9 0.8 collective-permute-start.17
  76.7 2.4 %collective-permute-start.19 = (bf16[128,1280]{1,0:T(8,128)(2,1)S(1)}, bf16[128,1280]{1,0:T(8,128)(2,1)S(1)}, u32[]{:S(2)}, u32[]{:S(2)}) collective-permute-start(bf16[128,1280]{1,0:T(8,128)(2,1)S(1)} %bitcast.63), channel_id=1, source_target_pairs={{0,64},{16,80},{32,96},{48,112},{64,0},{80,16},{96,32},{112,48},{1... | collective-permute-start | bytes 983048 | tf_op jit(solution)/shard_map/ppermute | solution.py:16
  79.1 1.8 collective-permute-done.18.refs_14_
  80.9 1.4 collective-permute-done.21
  82.3 7.0 %collective-permute-done.19 = bf16[128,1280]{1,0:T(8,128)(2,1)S(1)} collective-permute-done((bf16[128,1280]{1,0:T(8,128)(2,1)S(1)}, bf16[128,1280]{1,0:T(8,128)(2,1)S(1)}, u32[]{:S(2)}, u32[]{:S(2)}) %collective-permute-start.19) | collective-permute-done | bytes 327712 | tf_op jit(solution)/shard_map/ppermute | solution.py:16
  89.5 4.0 %ffn.1 = (f32[64,1280]{1,0:T(8,128)S(1)}, bf16[64,1280]{1,0:T(8,128)(2,1)S(1)}, bf16[64,1280]{1,0:T(8,128)(2,1)S(1)}, bf16[64,1280]{1,0:T(8,128)(2,1)S(1)}, f32[...) custom-call(bf16[256,1280]{1,0:T(8,128)(2,1)S(1)} %pad_maximum_fusio, ...), custom_call_target="tpu_custom_call" | custom-call | tf_op jit(solution)/shard_map/ffn/pallas_call | solution.py:61
  93.5 0.4 collective-permute-start.25
  93.9 2.7 %collective-permute-start.26 = (bf16[64,1280]{1,0:T(8,128)(2,1)S(1)}, bf16[64,1280]{1,0:T(8,128)(2,1)S(1)}, u32[]{:S(2)}, u32[]{:S(2)}) collective-permute-start(bf16[64,1280]{1,0:T(8,128)(2,1)S(1)} %get-tuple-element.91), channel_id=1, source_target_pairs={{0,128},{16,144},{32,160},{48,176},{64,192},{80,208},{96,224},{112... | collective-permute-start | bytes 491528 | tf_op jit(solution)/shard_map/ppermute | solution.py:16
  96.6 0.6 collective-permute-start.27
  97.2 2.9 %collective-permute-start.23 = (bf16[64,1280]{1,0:T(8,128)(2,1)S(1)}, bf16[64,1280]{1,0:T(8,128)(2,1)S(1)}, u32[]{:S(2)}, u32[]{:S(2)}) collective-permute-start(bf16[64,1280]{1,0:T(8,128)(2,1)S(1)} %get-tuple-element.83), channel_id=1, source_target_pairs={{0,128},{16,144},{32,160},{48,176},{64,192},{80,208},{96,224},{112... | collective-permute-start | bytes 491528 | tf_op jit(solution)/shard_map/ppermute | solution.py:16
  100.1 1.5 collective-permute-start.24
  101.6 3.7 %collective-permute-done.27 = bf16[64,1280]{1,0:T(8,128)(2,1)S(1)} collective-permute-done((bf16[64,1280]{1,0:T(8,128)(2,1)S(1)}, bf16[64,1280]{1,0:T(8,128)(2,1)S(1)}, u32[]{:S(2)}, u32[]{:S(2)}) %collective-permute-start.27) | collective-permute-done | bytes 163872 | tf_op jit(solution)/shard_map/ppermute | solution.py:16
  105.4 2.1 %combine_grad.1 = (f32[64,256]{1,0:T(8,128)S(1)}, f32[8,256]{1,0:T(8,128)S(1)}) custom-call(f32[64,1280]{1,0:T(8,128)S(1)} %add_add_fusion.refs_0_, bf16[8,256,1280]{2,1,0:T(8,128)(2,1)S(1)} %bitcast.60, f32[64,256]{1,0:T(8,128)S(1)} %get-tuple-element.96.refs_2_), custom_call_target="tpu_custom_call" | custom-call | tf_op jit(solution)/shard_map/combine_grad/pallas_call | solution.py:171
  107.5 6.7 %collective-permute-start.28 = (f32[8,256]{1,0:T(8,128)S(1)}, f32[8,256]{1,0:T(8,128)S(1)}, u32[]{:S(2)}, u32[]{:S(2)}) collective-permute-start(f32[8,256]{1,0:T(8,128)S(1)} %get-tuple-element.98), channel_id=1, source_target_pairs={{0,1},{1,0},{2,3},{3,2},{4,5},{5,4},{6,7},{7,6},{8,9},{9,8},{10,11... | collective-permute-start | bytes 24584 | tf_op jit(solution)/shard_map/ppermute | solution.py:16
  114.2 0.8 collective-permute-done.28
  115.0 4.4 %collective-permute-start.29 = (f32[8,256]{1,0:T(8,128)S(1)}, f32[8,256]{1,0:T(8,128)S(1)}, u32[]{:S(2)}, u32[]{:S(2)}) collective-permute-start(f32[8,256]{1,0:T(8,128)S(1)} %add.75), channel_id=1, source_target_pairs={{0,2},{1,3},{2,0},{3,1},{4,6},{5,7},{6,4},{7,5},{8,10},{9,11},{10,... | collective-permute-start | bytes 24584 | tf_op jit(solution)/shard_map/ppermute | solution.py:16
  119.5 0.8 collective-permute-done.23
  120.2 1.3 collective-permute-done.29
  121.9 2.4 %collective-permute-done.30 = f32[8,256]{1,0:T(8,128)S(1)} collective-permute-done((f32[8,256]{1,0:T(8,128)S(1)}, f32[8,256]{1,0:T(8,128)S(1)}, u32[]{:S(2)}, u32[]{:S(2)}) %collective-permute-start.30) | collective-permute-done | bytes 8224 | tf_op jit(solution)/shard_map/ppermute | solution.py:16
  124.3 2.5 %collective-permute-start.31 = (f32[8,256]{1,0:T(8,128)S(1)}, f32[8,256]{1,0:T(8,128)S(1)}, u32[]{:S(2)}, u32[]{:S(2)}) collective-permute-start(f32[8,256]{1,0:T(8,128)S(1)} %add.77), channel_id=1, source_target_pairs={{0,8},{1,9},{2,10},{3,11},{4,12},{5,13},{6,14},{7,15},{8,0},{9,1},... | collective-permute-start | bytes 24584 | tf_op jit(solution)/shard_map/ppermute | solution.py:16
  126.8 4.1 %collective-permute-start.34 = (bf16[64,1280]{1,0:T(8,128)(2,1)S(1)}, bf16[64,1280]{1,0:T(8,128)(2,1)S(1)}, u32[]{:S(2)}, u32[]{:S(2)}) collective-permute-start(bf16[64,1280]{1,0:T(8,128)(2,1)S(1)} %get-tuple-element.112), channel_id=1, source_target_pairs={{0,2},{1,3},{2,0},{3,1},{4,6},{5,7},{6,4},{7,5},{8,10},{9,11},{10,... | collective-permute-start | bytes 491528 | tf_op jit(solution)/shard_map/ppermute | solution.py:16
  130.9 2.3 %dispatch_grad.1 = f32[64,256]{1,0:T(8,128)S(1)} custom-call(f32[64,1280]{1,0:T(8,128)S(1)} %get-tuple-element.113.refs_0_, bf16[8,256,1280]{2,1,0:T(8,128)(2,1)S(1)} %copy-done, f32[64,256]{1,0:T(8,128)S(1)} %get-tuple-element.88.refs_2_), custom_call_target="tpu_custom_call" | custom-call | tf_op jit(solution)/shard_map/dispatch_grad/pallas_call | solution.py:171
  133.2 1.5 collective-permute-start.32
  134.8 0.8 convolution_bitcast_fusion
  135.6 9.2 %collective-permute-start.33 = (f32[8,1280]{1,0:T(8,128)S(1)}, f32[8,1280]{1,0:T(8,128)S(1)}, u32[]{:S(2)}, u32[]{:S(2)}) collective-permute-start(f32[8,1280]{1,0:T(8,128)S(1)} %convolution_bitcast_fusion), channel_id=1, source_target_pairs={{0,64},{16,80},{32,96},{48,112},{64,0},{80,16},{96,32},{112,48},{1... | collective-permute-start | bytes 122888 | tf_op jit(solution)/shard_map/ppermute | solution.py:16
  144.8 2.0 %collective-permute-done.33 = f32[8,1280]{1,0:T(8,128)S(1)} collective-permute-done((f32[8,1280]{1,0:T(8,128)S(1)}, f32[8,1280]{1,0:T(8,128)S(1)}, u32[]{:S(2)}, u32[]{:S(2)}) %collective-permute-start.33) | collective-permute-done | bytes 40992 | tf_op jit(solution)/shard_map/ppermute | solution.py:16
  146.8 3.1 %collective-permute-start.39 = (f32[8,1280]{1,0:T(8,128)S(1)}, f32[8,1280]{1,0:T(8,128)S(1)}, u32[]{:S(2)}, u32[]{:S(2)}) collective-permute-start(f32[8,1280]{1,0:T(8,128)S(1)} %add.80), channel_id=1, source_target_pairs={{0,128},{16,144},{32,160},{48,176},{64,192},{80,208},{96,224},{112... | collective-permute-start | bytes 122888 | tf_op jit(solution)/shard_map/ppermute | solution.py:16
  149.9 0.8 collective-permute-start.37
  150.8 2.5 %collective-permute-start.36 = (bf16[2,64,1280]{2,1,0:T(8,128)(2,1)S(1)}, bf16[2,64,1280]{2,1,0:T(8,128)(2,1)S(1)}, u32[]{:S(2)}, u32[]{:S(2)}) collective-permute-start(bf16[2,64,1280]{2,1,0:T(8,128)(2,1)S(1)} %pad_maximum_fusion.7.pair), channel_id=1, source_target_pairs={{0,8},{1,9},{2,10},{3,11},{4,12},{5,13},{6,14},{7,15},{8,0},{9,1},... | collective-permute-start | bytes 983048 | tf_op jit(solution)/shard_map/ppermute | solution.py:16
  153.3 1.9 %collective-permute-start.40 = (bf16[256,256]{1,0:T(8,128)(2,1)S(1)}, bf16[256,256]{1,0:T(8,128)(2,1)S(1)}, u32[]{:S(2)}, u32[]{:S(2)}) collective-permute-start(bf16[256,256]{1,0:T(8,128)(2,1)S(1)} %pad_maximum_fusion.10), channel_id=1, source_target_pairs={{0,8},{1,9},{2,10},{3,11},{4,12},{5,13},{6,14},{7,15},{8,0},{9,1},... | collective-permute-start | bytes 393224 | tf_op jit(solution)/shard_map/ppermute | solution.py:16
  155.3 1.4 collective-permute-start.41
  156.6 1.8 collective-permute-done.41
  158.4 9.1 %collective-permute-done.40 = bf16[256,256]{1,0:T(8,128)(2,1)S(1)} collective-permute-done((bf16[256,256]{1,0:T(8,128)(2,1)S(1)}, bf16[256,256]{1,0:T(8,128)(2,1)S(1)}, u32[]{:S(2)}, u32[]{:S(2)}) %collective-permute-start.40) | collective-permute-done | bytes 131104 | tf_op jit(solution)/shard_map/ppermute | solution.py:16
  167.5 0.7 through_logits.1.base
  168.3 0.8 through_slots.1
  169.1 5.6 %collective-permute-start.42 = (f32[128,1280]{1,0:T(8,128)S(1)}, f32[128,1280]{1,0:T(8,128)S(1)}, u32[]{:S(2)}, u32[]{:S(2)}) collective-permute-start(f32[128,1280]{1,0:T(8,128)S(1)} %get-tuple-element.110), channel_id=1, source_target_pairs={{0,1},{1,0},{2,3},{3,2},{4,5},{5,4},{6,7},{7,6},{8,9},{9,8},{10,11... | collective-permute-start | bytes 1966088 | tf_op jit(solution)/shard_map/ppermute | solution.py:16
  174.7 1.3 collective-permute-start.43
  176.0 3.0 %collective-permute-done.43 = f32[8,1280]{1,0:T(8,128)S(1)} collective-permute-done((f32[8,1280]{1,0:T(8,128)S(1)}, f32[8,1280]{1,0:T(8,128)S(1)}, u32[]{:S(2)}, u32[]{:S(2)}) %collective-permute-start.43) | collective-permute-done | bytes 40992 | tf_op jit(solution)/shard_map/ppermute | solution.py:16
  179.1 0.6 add_bitcast_fusion
  179.7 0.8 add_convert_fusion
  (83 shorter events, 1.8 us)
Async XLA Ops:
  0.6 1.5 copy-start.2
  2.1 3.8 %copy-start.3 = (bf16[1280,8]{0,1:T(8,128)(2,1)S(1)}, bf16[1280,8]{0,1:T(8,128)(2,1)}, u32[]{:S(2)}) copy-start(bf16[1280,8]{0,1:T(8,128)(2,1)} %param.7) | copy-start | bytes 61444
  2.3 14.9 %collective-permute-start.3 = (bf16[2,80,1280]{2,1,0:T(8,128)(2,1)S(1)}, bf16[2,80,1280]{2,1,0:T(8,128)(2,1)S(1)}, u32[]{:S(2)}, u32[]{:S(2)}) collective-permute-start(bf16[2,80,1280]{2,1,0:T(8,128)(2,1)S(1)} %pad_maximum_fusion.5.refs_0_), channel_id=1, source_target_pairs={{0,48},{16,32},{32,16},{48,0},{64,112},{80,96},{96,80},{112,64},{1... | collective-permute-start | bytes 1228808 | tf_op jit(solution)/shard_map/ppermute | solution.py:16
  5.9 11.3 %collective-permute-start.2 = (bf16[2,80,1280]{2,1,0:T(8,128)(2,1)S(1)}, bf16[2,80,1280]{2,1,0:T(8,128)(2,1)S(1)}, u32[]{:S(2)}, u32[]{:S(2)}) collective-permute-start(bf16[2,80,1280]{2,1,0:T(8,128)(2,1)S(1)} %pad_maximum_fusion.5.refs_0_), channel_id=1, source_target_pairs={{0,16},{16,0},{32,48},{48,32},{64,80},{80,64},{96,112},{112,96},{1... | collective-permute-start | bytes 1228808 | tf_op jit(solution)/shard_map/ppermute | solution.py:16
  5.9 8.1 %collective-permute-start.4 = (bf16[8,1280]{1,0:T(8,128)(2,1)S(1)}, bf16[8,1280]{1,0:T(8,128)(2,1)S(1)}, u32[]{:S(2)}, u32[]{:S(2)}) collective-permute-start(bf16[8,1280]{1,0:T(8,128)(2,1)S(1)} %bitcast.69), channel_id=1, source_target_pairs={{0,2},{1,3},{2,0},{3,1},{4,6},{5,7},{6,4},{7,5},{8,10},{9,11},{10,... | collective-permute-start | bytes 61448 | tf_op jit(solution)/shard_map/ppermute | solution.py:16
  12.9 17.6 %collective-permute-start = (bf16[2,80,1280]{2,1,0:T(8,128)(2,1)S(1)}, bf16[2,80,1280]{2,1,0:T(8,128)(2,1)S(1)}, u32[]{:S(2)}, u32[]{:S(2)}) collective-permute-start(bf16[2,80,1280]{2,1,0:T(8,128)(2,1)S(1)} %pad_maximum_fusion.3), channel_id=1, source_target_pairs={{0,64},{16,80},{32,96},{48,112},{64,0},{80,16},{96,32},{112,48},{1... | collective-permute-start | bytes 1228808 | tf_op jit(solution)/shard_map/ppermute | solution.py:16
  14.0 3.1 %collective-permute-start.5 = (bf16[16,1280]{1,0:T(8,128)(2,1)S(1)}, bf16[16,1280]{1,0:T(8,128)(2,1)S(1)}, u32[]{:S(2)}, u32[]{:S(2)}) collective-permute-start(bf16[16,1280]{1,0:T(8,128)(2,1)S(1)} %pad_maximum_fusion.13), channel_id=1, source_target_pairs={{0,4},{1,5},{2,6},{3,7},{4,0},{5,1},{6,2},{7,3},{8,12},{9,13},{10,... | collective-permute-start | bytes 122888 | tf_op jit(solution)/shard_map/ppermute | solution.py:16
  15.2 26.9 %copy-start = (bf16[8,256,1280]{2,1,0:T(8,128)(2,1)S(1)}, bf16[8,256,1280]{2,1,0:T(8,128)(2,1)}, u32[]{:S(2)}) copy-start(bf16[8,256,1280]{2,1,0:T(8,128)(2,1)} %refs_1_.2) | copy-start | bytes 15728644
  15.3 15.2 %collective-permute-start.1 = (bf16[2,80,1280]{2,1,0:T(8,128)(2,1)S(1)}, bf16[2,80,1280]{2,1,0:T(8,128)(2,1)S(1)}, u32[]{:S(2)}, u32[]{:S(2)}) collective-permute-start(bf16[2,80,1280]{2,1,0:T(8,128)(2,1)S(1)} %pad_maximum_fusion.4), channel_id=1, source_target_pairs={{0,128},{16,144},{32,160},{48,176},{64,192},{80,208},{96,224},{112... | collective-permute-start | bytes 1228808 | tf_op jit(solution)/shard_map/ppermute | solution.py:16
  17.2 5.3 %collective-permute-start.8 = (bf16[32,1280]{1,0:T(8,128)(2,1)S(1)}, bf16[32,1280]{1,0:T(8,128)(2,1)S(1)}, u32[]{:S(2)}, u32[]{:S(2)}) collective-permute-start(bf16[32,1280]{1,0:T(8,128)(2,1)S(1)} %pad_maximum_fusion.11), channel_id=1, source_target_pairs={{0,8},{1,9},{2,10},{3,11},{4,12},{5,13},{6,14},{7,15},{8,0},{9,1},... | collective-permute-start | bytes 245768 | tf_op jit(solution)/shard_map/ppermute | solution.py:16
  20.0 10.4 %collective-permute-start.7 = (bf16[80,1280]{1,0:T(8,128)(2,1)S(1)}, bf16[80,1280]{1,0:T(8,128)(2,1)S(1)}, u32[]{:S(2)}, u32[]{:S(2)}) collective-permute-start(bf16[80,1280]{1,0:T(8,128)(2,1)S(1)} %slice_bitcast_fusion.4), channel_id=1, source_target_pairs={{0,48},{16,32},{32,16},{48,0},{64,112},{80,96},{96,80},{112,64},{1... | collective-permute-start | bytes 614408 | tf_op jit(solution)/shard_map/ppermute | solution.py:16
  20.8 9.7 %collective-permute-start.6 = (bf16[80,1280]{1,0:T(8,128)(2,1)S(1)}, bf16[80,1280]{1,0:T(8,128)(2,1)S(1)}, u32[]{:S(2)}, u32[]{:S(2)}) collective-permute-start(bf16[80,1280]{1,0:T(8,128)(2,1)S(1)} %slice_bitcast_fusion.5), channel_id=1, source_target_pairs={{0,16},{16,0},{32,48},{48,32},{64,80},{80,64},{96,112},{112,96},{1... | collective-permute-start | bytes 614408 | tf_op jit(solution)/shard_map/ppermute | solution.py:16
  30.5 23.2 %collective-permute-start.11 = (bf16[2,2,80,1280]{3,2,1,0:T(8,128)(2,1)S(1)}, bf16[2,2,80,1280]{3,2,1,0:T(8,128)(2,1)S(1)}, u32[]{:S(2)}, u32[]{:S(2)}) collective-permute-start(bf16[2,2,80,1280]{3,2,1,0:T(8,128)(2,1)S(1)} %pad_maximum_fusion.refs_5_), channel_id=1, source_target_pairs={{0,48},{16,32},{32,16},{48,0},{64,112},{80,96},{96,80},{112,64},{1... | collective-permute-start | bytes 2457608 | tf_op jit(solution)/shard_map/ppermute | solution.py:16
  31.3 22.5 %collective-permute-start.10 = (bf16[2,2,80,1280]{3,2,1,0:T(8,128)(2,1)S(1)}, bf16[2,2,80,1280]{3,2,1,0:T(8,128)(2,1)S(1)}, u32[]{:S(2)}, u32[]{:S(2)}) collective-permute-start(bf16[2,2,80,1280]{3,2,1,0:T(8,128)(2,1)S(1)} %pad_maximum_fusion.refs_5_), channel_id=1, source_target_pairs={{0,16},{16,0},{32,48},{48,32},{64,80},{80,64},{96,112},{112,96},{1... | collective-permute-start | bytes 2457608 | tf_op jit(solution)/shard_map/ppermute | solution.py:16
  32.3 9.8 %collective-permute-start.9 = (bf16[64,1280]{1,0:T(8,128)(2,1)S(1)}, bf16[64,1280]{1,0:T(8,128)(2,1)S(1)}, u32[]{:S(2)}, u32[]{:S(2)}) collective-permute-start(bf16[64,1280]{1,0:T(8,128)(2,1)S(1)} %pad_maximum_fusion.9), channel_id=1, source_target_pairs={{0,1},{1,0},{2,3},{3,2},{4,5},{5,4},{6,7},{7,6},{8,9},{9,8},{10,11... | collective-permute-start | bytes 491528 | tf_op jit(solution)/shard_map/ppermute | solution.py:16
  39.1 14.7 %collective-permute-start.12 = (bf16[2,80,1280]{2,1,0:T(8,128)(2,1)S(1)}, bf16[2,80,1280]{2,1,0:T(8,128)(2,1)S(1)}, u32[]{:S(2)}, u32[]{:S(2)}) collective-permute-start(bf16[2,80,1280]{2,1,0:T(8,128)(2,1)S(1)} %pad_maximum_fusion.6), channel_id=1, source_target_pairs={{0,192},{16,208},{32,224},{48,240},{64,128},{80,144},{96,160},{112... | collective-permute-start | bytes 1228808 | tf_op jit(solution)/shard_map/ppermute | solution.py:16
  42.1 2.5 %copy-start.1 = (bf16[8,256,1280]{2,1,0:T(8,128)(2,1)S(1)}, bf16[8,256,1280]{2,1,0:T(8,128)(2,1)}, u32[]{:S(2)}) copy-start(bf16[8,256,1280]{2,1,0:T(8,128)(2,1)} %refs_1_.3) | copy-start | bytes 15728644
  53.8 21.2 %collective-permute-start.16 = (bf16[2,80,1280]{2,1,0:T(8,128)(2,1)S(1)}, bf16[2,80,1280]{2,1,0:T(8,128)(2,1)S(1)}, u32[]{:S(2)}, u32[]{:S(2)}) collective-permute-start(bf16[2,80,1280]{2,1,0:T(8,128)(2,1)S(1)} %collective-permute-done.12.refs_10_), channel_id=1, source_target_pairs={{0,48},{16,32},{32,16},{48,0},{64,112},{80,96},{96,80},{112,64},{1... | collective-permute-start | bytes 1228808 | tf_op jit(solution)/shard_map/ppermute | solution.py:16
  56.1 18.9 %collective-permute-start.15 = (bf16[2,80,1280]{2,1,0:T(8,128)(2,1)S(1)}, bf16[2,80,1280]{2,1,0:T(8,128)(2,1)S(1)}, u32[]{:S(2)}, u32[]{:S(2)}) collective-permute-start(bf16[2,80,1280]{2,1,0:T(8,128)(2,1)S(1)} %collective-permute-done.12.refs_10_), channel_id=1, source_target_pairs={{0,16},{16,0},{32,48},{48,32},{64,80},{80,64},{96,112},{112,96},{1... | collective-permute-start | bytes 1228808 | tf_op jit(solution)/shard_map/ppermute | solution.py:16
  56.1 18.8 %collective-permute-start.20 = (bf16[128,1280]{1,0:T(8,128)(2,1)S(1)}, bf16[128,1280]{1,0:T(8,128)(2,1)S(1)}, u32[]{:S(2)}, u32[]{:S(2)}) collective-permute-start(bf16[128,1280]{1,0:T(8,128)(2,1)S(1)} %bitcast.61), channel_id=1, source_target_pairs={{0,128},{16,144},{32,160},{48,176},{64,192},{80,208},{96,224},{112... | collective-permute-start | bytes 983048 | tf_op jit(solution)/shard_map/ppermute | solution.py:16
  61.2 15.5 %collective-permute-start.14 = (bf16[2,80,1280]{2,1,0:T(8,128)(2,1)S(1)}, bf16[2,80,1280]{2,1,0:T(8,128)(2,1)S(1)}, u32[]{:S(2)}, u32[]{:S(2)}) collective-permute-start(bf16[2,80,1280]{2,1,0:T(8,128)(2,1)S(1)} %slice_bitcast_fusion), channel_id=1, source_target_pairs={{0,48},{16,32},{32,16},{48,0},{64,112},{80,96},{96,80},{112,64},{1... | collective-permute-start | bytes 1228808 | tf_op jit(solution)/shard_map/ppermute | solution.py:16
  62.0 17.1 %collective-permute-start.13 = (bf16[2,80,1280]{2,1,0:T(8,128)(2,1)S(1)}, bf16[2,80,1280]{2,1,0:T(8,128)(2,1)S(1)}, u32[]{:S(2)}, u32[]{:S(2)}) collective-permute-start(bf16[2,80,1280]{2,1,0:T(8,128)(2,1)S(1)} %slice_bitcast_fusion.1), channel_id=1, source_target_pairs={{0,16},{16,0},{32,48},{48,32},{64,80},{80,64},{96,112},{112,96},{1... | collective-permute-start | bytes 1228808 | tf_op jit(solution)/shard_map/ppermute | solution.py:16
  75.0 7.3 %collective-permute-start.21 = (bf16[128,1280]{1,0:T(8,128)(2,1)S(1)}, bf16[128,1280]{1,0:T(8,128)(2,1)S(1)}, u32[]{:S(2)}, u32[]{:S(2)}) collective-permute-start(bf16[128,1280]{1,0:T(8,128)(2,1)S(1)} %collective-permute-done.20), channel_id=1, source_target_pairs={{0,64},{16,80},{32,96},{48,112},{64,0},{80,16},{96,32},{112,48},{1... | collective-permute-start | bytes 983048 | tf_op jit(solution)/shard_map/ppermute | solution.py:16
  75.0 5.9 %collective-permute-start.18 = (bf16[80,1280]{1,0:T(8,128)(2,1)S(1)}, bf16[80,1280]{1,0:T(8,128)(2,1)S(1)}, u32[]{:S(2)}, u32[]{:S(2)}) collective-permute-start(bf16[80,1280]{1,0:T(8,128)(2,1)S(1)} %slice_bitcast_fusion.2), channel_id=1, source_target_pairs={{0,48},{16,32},{32,16},{48,0},{64,112},{80,96},{96,80},{112,64},{1... | collective-permute-start | bytes 614408 | tf_op jit(solution)/shard_map/ppermute | solution.py:16
  75.9 5.0 %collective-permute-start.17 = (bf16[80,1280]{1,0:T(8,128)(2,1)S(1)}, bf16[80,1280]{1,0:T(8,128)(2,1)S(1)}, u32[]{:S(2)}, u32[]{:S(2)}) collective-permute-start(bf16[80,1280]{1,0:T(8,128)(2,1)S(1)} %slice_bitcast_fusion.3), channel_id=1, source_target_pairs={{0,16},{16,0},{32,48},{48,32},{64,80},{80,64},{96,112},{112,96},{1... | collective-permute-start | bytes 614408 | tf_op jit(solution)/shard_map/ppermute | solution.py:16
  76.7 12.6 %collective-permute-start.19 = (bf16[128,1280]{1,0:T(8,128)(2,1)S(1)}, bf16[128,1280]{1,0:T(8,128)(2,1)S(1)}, u32[]{:S(2)}, u32[]{:S(2)}) collective-permute-start(bf16[128,1280]{1,0:T(8,128)(2,1)S(1)} %bitcast.63), channel_id=1, source_target_pairs={{0,64},{16,80},{32,96},{48,112},{64,0},{80,16},{96,32},{112,48},{1... | collective-permute-start | bytes 983048 | tf_op jit(solution)/shard_map/ppermute | solution.py:16
  89.4 16.0 %slice-start = ((s8[5242880]{0:T(1024)(128)(4,1)}), s8[4194304]{0:T(1024)(128)(4,1)S(1)}, s32[]{:S(2)}) async-start(s8[5242880]{0:T(1024)(128)(4,1)} %bitcast.59), calls=%async_computation | async-start | bytes 8388608
  89.5 15.9 %slice-start.1 = ((s8[5242880]{0:T(1024)(128)(4,1)}), s8[1048576]{0:T(1024)(128)(4,1)S(1)}, s32[]{:S(2)}) async-start(s8[5242880]{0:T(1024)(128)(4,1)} %bitcast.59), calls=%async_computation.1 | async-start | bytes 2097152
  93.5 6.6 %collective-permute-start.25 = (bf16[64,1280]{1,0:T(8,128)(2,1)S(1)}, bf16[64,1280]{1,0:T(8,128)(2,1)S(1)}, u32[]{:S(2)}, u32[]{:S(2)}) collective-permute-start(bf16[64,1280]{1,0:T(8,128)(2,1)S(1)} %get-tuple-element.90), channel_id=1, source_target_pairs={{0,64},{16,80},{32,96},{48,112},{64,0},{80,16},{96,32},{112,48},{1... | collective-permute-start | bytes 491528 | tf_op jit(solution)/shard_map/ppermute | solution.py:16
  93.9 7.7 %collective-permute-start.26 = (bf16[64,1280]{1,0:T(8,128)(2,1)S(1)}, bf16[64,1280]{1,0:T(8,128)(2,1)S(1)}, u32[]{:S(2)}, u32[]{:S(2)}) collective-permute-start(bf16[64,1280]{1,0:T(8,128)(2,1)S(1)} %get-tuple-element.91), channel_id=1, source_target_pairs={{0,128},{16,144},{32,160},{48,176},{64,192},{80,208},{96,224},{112... | collective-permute-start | bytes 491528 | tf_op jit(solution)/shard_map/ppermute | solution.py:16
  96.6 8.7 %collective-permute-start.27 = (bf16[64,1280]{1,0:T(8,128)(2,1)S(1)}, bf16[64,1280]{1,0:T(8,128)(2,1)S(1)}, u32[]{:S(2)}, u32[]{:S(2)}) collective-permute-start(bf16[64,1280]{1,0:T(8,128)(2,1)S(1)} %get-tuple-element.92), channel_id=1, source_target_pairs={{0,192},{16,208},{32,224},{48,240},{64,128},{80,144},{96,160},{112... | collective-permute-start | bytes 491528 | tf_op jit(solution)/shard_map/ppermute | solution.py:16
  97.2 22.3 %collective-permute-start.22 = (bf16[64,1280]{1,0:T(8,128)(2,1)S(1)}, bf16[64,1280]{1,0:T(8,128)(2,1)S(1)}, u32[]{:S(2)}, u32[]{:S(2)}) collective-permute-start(bf16[64,1280]{1,0:T(8,128)(2,1)S(1)} %get-tuple-element.82), channel_id=1, source_target_pairs={{0,64},{16,80},{32,96},{48,112},{64,0},{80,16},{96,32},{112,48},{1... | collective-permute-start | bytes 491528 | tf_op jit(solution)/shard_map/ppermute | solution.py:16
  97.2 23.0 %collective-permute-start.23 = (bf16[64,1280]{1,0:T(8,128)(2,1)S(1)}, bf16[64,1280]{1,0:T(8,128)(2,1)S(1)}, u32[]{:S(2)}, u32[]{:S(2)}) collective-permute-start(bf16[64,1280]{1,0:T(8,128)(2,1)S(1)} %get-tuple-element.83), channel_id=1, source_target_pairs={{0,128},{16,144},{32,160},{48,176},{64,192},{80,208},{96,224},{112... | collective-permute-start | bytes 491528 | tf_op jit(solution)/shard_map/ppermute | solution.py:16
  100.1 20.1 %collective-permute-start.24 = (bf16[64,1280]{1,0:T(8,128)(2,1)S(1)}, bf16[64,1280]{1,0:T(8,128)(2,1)S(1)}, u32[]{:S(2)}, u32[]{:S(2)}) collective-permute-start(bf16[64,1280]{1,0:T(8,128)(2,1)S(1)} %get-tuple-element.84), channel_id=1, source_target_pairs={{0,192},{16,208},{32,224},{48,240},{64,128},{80,144},{96,160},{112... | collective-permute-start | bytes 491528 | tf_op jit(solution)/shard_map/ppermute | solution.py:16
  107.5 7.5 %collective-permute-start.28 = (f32[8,256]{1,0:T(8,128)S(1)}, f32[8,256]{1,0:T(8,128)S(1)}, u32[]{:S(2)}, u32[]{:S(2)}) collective-permute-start(f32[8,256]{1,0:T(8,128)S(1)} %get-tuple-element.98), channel_id=1, source_target_pairs={{0,1},{1,0},{2,3},{3,2},{4,5},{5,4},{6,7},{7,6},{8,9},{9,8},{10,11... | collective-permute-start | bytes 24584 | tf_op jit(solution)/shard_map/ppermute | solution.py:16
  115.0 6.5 %collective-permute-start.29 = (f32[8,256]{1,0:T(8,128)S(1)}, f32[8,256]{1,0:T(8,128)S(1)}, u32[]{:S(2)}, u32[]{:S(2)}) collective-permute-start(f32[8,256]{1,0:T(8,128)S(1)} %add.75), channel_id=1, source_target_pairs={{0,2},{1,3},{2,0},{3,1},{4,6},{5,7},{6,4},{7,5},{8,10},{9,11},{10,... | collective-permute-start | bytes 24584 | tf_op jit(solution)/shard_map/ppermute | solution.py:16
  121.5 2.8 %collective-permute-start.30 = (f32[8,256]{1,0:T(8,128)S(1)}, f32[8,256]{1,0:T(8,128)S(1)}, u32[]{:S(2)}, u32[]{:S(2)}) collective-permute-start(f32[8,256]{1,0:T(8,128)S(1)} %add.76), channel_id=1, source_target_pairs={{0,4},{1,5},{2,6},{3,7},{4,0},{5,1},{6,2},{7,3},{8,12},{9,13},{10,... | collective-permute-start | bytes 24584 | tf_op jit(solution)/shard_map/ppermute | solution.py:16
  124.3 8.9 %collective-permute-start.31 = (f32[8,256]{1,0:T(8,128)S(1)}, f32[8,256]{1,0:T(8,128)S(1)}, u32[]{:S(2)}, u32[]{:S(2)}) collective-permute-start(f32[8,256]{1,0:T(8,128)S(1)} %add.77), channel_id=1, source_target_pairs={{0,8},{1,9},{2,10},{3,11},{4,12},{5,13},{6,14},{7,15},{8,0},{9,1},... | collective-permute-start | bytes 24584 | tf_op jit(solution)/shard_map/ppermute | solution.py:16
  126.8 20.0 %collective-permute-start.34 = (bf16[64,1280]{1,0:T(8,128)(2,1)S(1)}, bf16[64,1280]{1,0:T(8,128)(2,1)S(1)}, u32[]{:S(2)}, u32[]{:S(2)}) collective-permute-start(bf16[64,1280]{1,0:T(8,128)(2,1)S(1)} %get-tuple-element.112), channel_id=1, source_target_pairs={{0,2},{1,3},{2,0},{3,1},{4,6},{5,7},{6,4},{7,5},{8,10},{9,11},{10,... | collective-permute-start | bytes 491528 | tf_op jit(solution)/shard_map/ppermute | solution.py:16
  133.2 11.6 %collective-permute-start.32 = (bf16[64,256]{1,0:T(8,128)(2,1)S(1)}, bf16[64,256]{1,0:T(8,128)(2,1)S(1)}, u32[]{:S(2)}, u32[]{:S(2)}) collective-permute-start(bf16[64,256]{1,0:T(8,128)(2,1)S(1)} %fusion.2), channel_id=1, source_target_pairs={{0,2},{1,3},{2,0},{3,1},{4,6},{5,7},{6,4},{7,5},{8,10},{9,11},{10,... | collective-permute-start | bytes 98312 | tf_op jit(solution)/shard_map/ppermute | solution.py:16
  135.6 11.2 %collective-permute-start.33 = (f32[8,1280]{1,0:T(8,128)S(1)}, f32[8,1280]{1,0:T(8,128)S(1)}, u32[]{:S(2)}, u32[]{:S(2)}) collective-permute-start(f32[8,1280]{1,0:T(8,128)S(1)} %convolution_bitcast_fusion), channel_id=1, source_target_pairs={{0,64},{16,80},{32,96},{48,112},{64,0},{80,16},{96,32},{112,48},{1... | collective-permute-start | bytes 122888 | tf_op jit(solution)/shard_map/ppermute | solution.py:16
  146.8 6.5 %collective-permute-start.39 = (f32[8,1280]{1,0:T(8,128)S(1)}, f32[8,1280]{1,0:T(8,128)S(1)}, u32[]{:S(2)}, u32[]{:S(2)}) collective-permute-start(f32[8,1280]{1,0:T(8,128)S(1)} %add.80), channel_id=1, source_target_pairs={{0,128},{16,144},{32,160},{48,176},{64,192},{80,208},{96,224},{112... | collective-permute-start | bytes 122888 | tf_op jit(solution)/shard_map/ppermute | solution.py:16
  149.9 3.4 %collective-permute-start.38 = (bf16[128,256]{1,0:T(8,128)(2,1)S(1)}, bf16[128,256]{1,0:T(8,128)(2,1)S(1)}, u32[]{:S(2)}, u32[]{:S(2)}) collective-permute-start(bf16[128,256]{1,0:T(8,128)(2,1)S(1)} %pad_maximum_fusion.12), channel_id=1, source_target_pairs={{0,4},{1,5},{2,6},{3,7},{4,0},{5,1},{6,2},{7,3},{8,12},{9,13},{10,... | collective-permute-start | bytes 196616 | tf_op jit(solution)/shard_map/ppermute | solution.py:16
  149.9 18.3 %collective-permute-start.37 = (bf16[2,64,1280]{2,1,0:T(8,128)(2,1)S(1)}, bf16[2,64,1280]{2,1,0:T(8,128)(2,1)S(1)}, u32[]{:S(2)}, u32[]{:S(2)}) collective-permute-start(bf16[2,64,1280]{2,1,0:T(8,128)(2,1)S(1)} %pad_maximum_fusion.7.pair), channel_id=1, source_target_pairs={{0,12},{1,13},{2,14},{3,15},{4,8},{5,9},{6,10},{7,11},{8,4},{9,5},... | collective-permute-start | bytes 983048 | tf_op jit(solution)/shard_map/ppermute | solution.py:16
  150.8 17.5 %collective-permute-start.36 = (bf16[2,64,1280]{2,1,0:T(8,128)(2,1)S(1)}, bf16[2,64,1280]{2,1,0:T(8,128)(2,1)S(1)}, u32[]{:S(2)}, u32[]{:S(2)}) collective-permute-start(bf16[2,64,1280]{2,1,0:T(8,128)(2,1)S(1)} %pad_maximum_fusion.7.pair), channel_id=1, source_target_pairs={{0,8},{1,9},{2,10},{3,11},{4,12},{5,13},{6,14},{7,15},{8,0},{9,1},... | collective-permute-start | bytes 983048 | tf_op jit(solution)/shard_map/ppermute | solution.py:16
  153.2 15.0 %collective-permute-start.35 = (bf16[2,64,1280]{2,1,0:T(8,128)(2,1)S(1)}, bf16[2,64,1280]{2,1,0:T(8,128)(2,1)S(1)}, u32[]{:S(2)}, u32[]{:S(2)}) collective-permute-start(bf16[2,64,1280]{2,1,0:T(8,128)(2,1)S(1)} %pad_maximum_fusion.7.pair), channel_id=1, source_target_pairs={{0,4},{1,5},{2,6},{3,7},{4,0},{5,1},{6,2},{7,3},{8,12},{9,13},{10,... | collective-permute-start | bytes 983048 | tf_op jit(solution)/shard_map/ppermute | solution.py:16
  153.3 14.2 %collective-permute-start.40 = (bf16[256,256]{1,0:T(8,128)(2,1)S(1)}, bf16[256,256]{1,0:T(8,128)(2,1)S(1)}, u32[]{:S(2)}, u32[]{:S(2)}) collective-permute-start(bf16[256,256]{1,0:T(8,128)(2,1)S(1)} %pad_maximum_fusion.10), channel_id=1, source_target_pairs={{0,8},{1,9},{2,10},{3,11},{4,12},{5,13},{6,14},{7,15},{8,0},{9,1},... | collective-permute-start | bytes 393224 | tf_op jit(solution)/shard_map/ppermute | solution.py:16
  155.3 3.1 %collective-permute-start.41 = (f32[8,1280]{1,0:T(8,128)S(1)}, f32[8,1280]{1,0:T(8,128)S(1)}, u32[]{:S(2)}, u32[]{:S(2)}) collective-permute-start(f32[8,1280]{1,0:T(8,128)S(1)} %add.81), channel_id=1, source_target_pairs={{0,16},{16,0},{32,48},{48,32},{64,80},{80,64},{96,112},{112,96},{1... | collective-permute-start | bytes 122888 | tf_op jit(solution)/shard_map/ppermute | solution.py:16
  169.1 10.6 %collective-permute-start.42 = (f32[128,1280]{1,0:T(8,128)S(1)}, f32[128,1280]{1,0:T(8,128)S(1)}, u32[]{:S(2)}, u32[]{:S(2)}) collective-permute-start(f32[128,1280]{1,0:T(8,128)S(1)} %get-tuple-element.110), channel_id=1, source_target_pairs={{0,1},{1,0},{2,3},{3,2},{4,5},{5,4},{6,7},{7,6},{8,9},{9,8},{10,11... | collective-permute-start | bytes 1966088 | tf_op jit(solution)/shard_map/ppermute | solution.py:16
  174.7 4.4 %collective-permute-start.43 = (f32[8,1280]{1,0:T(8,128)S(1)}, f32[8,1280]{1,0:T(8,128)S(1)}, u32[]{:S(2)}, u32[]{:S(2)}) collective-permute-start(f32[8,1280]{1,0:T(8,128)S(1)} %add.82), channel_id=1, source_target_pairs={{0,32},{16,48},{32,0},{48,16},{64,96},{80,112},{96,64},{112,80},{1... | collective-permute-start | bytes 122888 | tf_op jit(solution)/shard_map/ppermute | solution.py:16

commit v4 on v2

--- a/solution.py
+++ b/solution.py
@@ -23,7 +23,7 @@
 def ffn_kernel(rows_in, rows_go, *refs):
     own, l0, r0, p0, q0, both, lb, rb, pb, qb, last, l3, r3, p3, q3 = refs[:15]
     f0, f3 = (p0, q0), (p3, q3)
-    outs, grads, (w1, w2) = refs[15:19], refs[19:23], refs[23:]
+    outs, grads, (w1, w2) = refs[15:19], refs[19:22], refs[22:]
     me = lax.axis_index("dp")
     depth = w1.shape[0] // 16
 
@@ -48,10 +48,15 @@
     slope = cdf + 0.5 * pre * (1.0 - th * th) * (ROOT * (1.0 + 3 * 0.044715 * sq))
     hidden_grad = jnp.dot(rows_go[...], w2[...], preferred_element_type=F32)
     pre_grad = (hidden_grad * slope).astype(BF16)
-    own_rows = outs[0].shape[0]
-    for whole, blocks in ((nt(hidden, w2[...]), outs), (nt(pre_grad, w1[...]), grads)):
-        for a, block in enumerate(blocks):
-            block[...] = whole[a * own_rows : (a + 1) * own_rows].astype(block.dtype)
+    rows = outs[0].shape[0]
+    out = nt(hidden, w2[...])
+    for a, block in enumerate(outs):
+        block[...] = out[a * rows : (a + 1) * rows].astype(block.dtype)
+    grad = nt(pre_grad, w1[...])
+    grads[0][...] = grad[:rows]
+    grads[1][...] = grad[2 * rows : 3 * rows]
+    grads[2][0] = grad[rows : 2 * rows].astype(BF16)
+    grads[2][1] = grad[3 * rows :].astype(BF16)
 
 
 def ffn(rows_in, rows_go, blocks, own_rows):
@@ -60,9 +65,10 @@
     vmem = pl.BlockSpec(memory_space=pltpu.VMEM)
     return pl.pallas_call(
         ffn_kernel,
-        out_shape=[jax.ShapeDtypeStruct((own_rows, width), t) for t in (F32, BF16, BF16, BF16)] * 2,
+        out_shape=[jax.ShapeDtypeStruct((own_rows, width), t) for t in (F32, BF16, BF16, BF16, F32, F32)]
+        + [jax.ShapeDtypeStruct((2, own_rows, width), BF16)],
         in_specs=[vmem] * (2 + len(blocks)),
-        out_specs=[vmem] * 8,
+        out_specs=[vmem] * 7,
         scratch_shapes=[pltpu.VMEM((width, quarter), BF16), pltpu.VMEM((width, quarter), BF16)],
         compiler_params=pltpu.CompilerParams(vmem_limit_bytes=40 * 2**20),
         name="ffn",
@@ -135,6 +141,9 @@
             pl.BlockSpec((2, 32, slots * 4), lambda i: (0, i, 0)),
         ],
         compiler_params=pltpu.CompilerParams(vmem_limit_bytes=24 * 2**20),
+        cost_estimate=pl.CostEstimate(
+            flops=2 * tokens.size * (slots + 32), bytes_accessed=4 * tokens.size, transcendentals=2 * images * slots * count
+        ),
         name="slots",
     )(table, tokens, out_grad)
 
@@ -179,6 +188,7 @@
         ],
         out_specs=out_specs,
         compiler_params=pltpu.CompilerParams(vmem_limit_bytes=16 * 2**20),
+        cost_estimate=pl.CostEstimate(flops=64 * big.size, bytes_accessed=2 * big.size, transcendentals=0),
         name="dispatch_grad" if over_tokens else "combine_grad",
     )(rows, big, weight)
 
@@ -267,6 +277,11 @@
     return (own + one.astype(F32)) + (two.astype(F32) + three.astype(F32))
 
 
+def pair_z(own, second, others):
+    got = swap(others, "dp", 4)
+    return own + got[0].astype(F32), (second + got[1].astype(F32)).astype(BF16)
+
+
 def all_x(v):
     return [v, *together(swap(v, "expert", 4), swap(v, "expert", 8), swap(v, "expert", 12))]
 
@@ -283,24 +298,28 @@
     return v
 
 
+def summed_three(v, axis, *steps):
+    one, two, three = together(*[swap(v, axis, k) for k in steps])
+    return (v + one) + (two + three)
+
+
 def per_device(tokens, out_grad, slot_params, w_in, w_out):
     images, count, width = tokens.shape
     own = slot_params.shape[1]
     half = images * own
 
     units = units_of(w_in, w_out.T)
-    l0, r0 = swap(units[0], "dp", 1), swap(units[0], "dp", 3)
+    table = doubled(slot_params.T, "expert", 2)
     u1 = swap(units[1], "dp", 4)
     u2 = swap(units[2], "dp", 8)
-    table = doubled(slot_params.T, "expert", 2, 4)
-    l0, r0, table = together(l0, r0, table)
+    l0, r0 = swap(units[0], "dp", 1), swap(units[0], "dp", 3)
     p0, q0 = swap(r0[0], "dp", 1), swap(l0[1], "dp", 3)
-    table = doubled(table, "expert", 8, 1)
 
     u1, u2, p0, q0, table = together(u1, u2, p0, q0, table)
     both = jnp.stack([u1, u2], axis=1)
     lb, rb = swap(both, "dp", 1), swap(both, "dp", 3)
     u3 = swap(after(units[3], u1), "dp", 12)
+    table = doubled(table, "expert", 4, 8, 1)
     rows, dispatch, combine, spread = slots_call(table, tokens, out_grad)
     rows = rows.reshape(2 * half, width)
 
@@ -308,7 +327,7 @@
     z1, z2 = swap(rows, "dp", 4), swap(rows, "dp", 8)
     l3, r3 = swap(u3, "dp", 1), swap(u3, "dp", 3)
     pb, qb = swap(rb[0], "dp", 1), swap(lb[1], "dp", 3)
-    l3, r3, z2 = together(l3, r3, z2)
+    l3, r3, z1, z2 = together(l3, r3, z1, z2)
     p3, q3 = swap(r3[0], "dp", 1), swap(l3[1], "dp", 3)
     z3 = swap(z2, "dp", 4)
     pb, qb, p3, q3, z3 = together(pb, qb, p3, q3, z3)
@@ -318,27 +337,31 @@
     blocks = [units[0], l0, r0, p0, q0, both, lb, rb, pb, qb, u3, l3, r3, p3, q3]
     halves = ffn(rows_in, rows_go, blocks, half)
     slot_out = reduce_z(*halves[:4])
-    slot_in_grad = reduce_z(*halves[4:])
+    first, second = pair_z(*halves[4:])
+    slot_in_grad = first + swap(second, "dp", 8).astype(F32)
     near = slot_in_grad.astype(BF16)
     far = swap(near, "expert", 2)
 
-    part, mix = against(slot_out, out_grad, combine, False)
-    mix = summed(mix, "expert", 1, 2, 4, 8)
+    part, mix = against(after(slot_out, second), out_grad, combine, False)
+    mix = summed_three(mix, "expert", 1, 2, 3)
+    mix = summed_three(after(mix, near), "expert", 4, 8, 12)
     (back,) = against(slot_in_grad, tokens, dispatch, True)
     logit_grad = back + (part - combine * jnp.repeat(mix, own, axis=0))
     logit_grad_b = logit_grad.astype(BF16)
-    slot_term = jnp.einsum(
+    term = jnp.einsum(
         "bsm,bmd->sd", logit_grad_b.reshape(images, own, count), tokens, preferred_element_type=F32
     )
+
     line = doubled(logit_grad_b, "expert", 2)
-    line = doubled(after(line, far), "expert", 4, 8)
-    base = lines_call(line, table)
-
+    line, far = together(line, far)
+    term = summed(term, "dp", 4)
+    *line, term, far = together(*all_x(line), term, far)
     pieces = all_x(jnp.stack([near, far]))
-    slot_sum = summed(slot_term, "dp", 4, 8, 1)
-    slot_grad = summed(after(slot_sum, *pieces), "dp", 2).T
-
-    mine, theirs = spread_call(spread, pieces, after(base, slot_sum))
+    base = lines_call(jnp.concatenate(line, axis=0), table)
+    term = summed(term, "dp", 8, 1)
+    slot_grad = summed(after(term, *pieces), "dp", 2).T
+
+    mine, theirs = spread_call(spread, pieces, after(base, term))
     token_grad = (mine + swap(theirs, "expert", 1)).astype(BF16)
     return (token_grad.reshape(images, -1, width), slot_grad)
 

time: 175 us -> 182 us (1.040)
  waiting for transfers between devices: 50 us -> 84.1 us
  starting transfers between devices: 98.1 us -> 70.7 us
    ppermute x44 -> x46, waiting for transfers between devices: 50 us -> 84.1 us  [swap(): return lax.ppermute(value, axis, [(i, i ^ k) for i in range(count)])]
    ppermute x44 -> x46, starting transfers between devices: 98.1 us -> 70.7 us  [swap(): return lax.ppermute(value, axis, [(i, i ^ k) for i in range(count)])]
  transfers between devices with their start and end apart: 44 -> 46, of which waited for: 21 -> 18; matrix products, arithmetic and copies ran while one was open for 1% -> 1% of each run, Pallas kernels for 8% -> 7%
where the time goes in v4:
time: 182 us
  waiting for transfers between devices  84.1 us (46%)
  starting transfers between devices  70.7 us (39%)
  Pallas kernels  19.1 us (10%)
  local copies, waits for them, and re-layouts  4.25 us (2%)
  other arithmetic  2.02 us (1%)
    ppermute x46, waiting for transfers between devices, swap(): return lax.ppermute(value, axis, [(i, i ^ k) for i in range(count)])  84.1 us
    ppermute x46, starting transfers between devices, swap(): return lax.ppermute(value, axis, [(i, i ^ k) for i in range(count)])  70.7 us
    pallas_call x1, Pallas kernels, slots_call(): pl.pallas_call(slots_kernel, grid=(images // 2,), out_shape=[jax.ShapeDty...  9.17 us
    pallas_call x2, Pallas kernels, against(): pl.pallas_call(lambda *refs: against_kernel(over_tokens, *refs), grid=(im...  4.36 us
    pallas_call x1, Pallas kernels, ffn(): pl.pallas_call(ffn_kernel, out_shape=[jax.ShapeDtypeStruct((own_rows, wid...  4.04 us
  transfers between devices with their start and end apart: 46, of which 18 were waited for; matrix products, arithmetic and copies ran while one was open for 1% of the time, Pallas kernels for 7%

profile of v4, /device:TPU:1, one launch (start us, length us, event | category | flops | bytes accessed | tf_op | source)
XLA Modules:
  0.0 182.0 jit_solution(7108723794751657144)
XLA Ops:
  0.7 1.4 dynamic-slice_bitcast_fusion.1
  2.3 2.2 %collective-permute-start.4 = (bf16[2,80,1280]{2,1,0:T(8,128)(2,1)S(1)}, bf16[2,80,1280]{2,1,0:T(8,128)(2,1)S(1)}, u32[]{:S(2)}, u32[]{:S(2)}) collective-permute-start(bf16[2,80,1280]{2,1,0:T(8,128)(2,1)S(1)} %pad_maximum_fusion.5.refs_0_), channel_id=1, source_target_pairs={{0,16},{16,0},{32,48},{48,32},{64,80},{80,64},{96,112},{112,96},{1... | collective-permute-start | bytes 1228808 | tf_op jit(solution)/shard_map/ppermute | solution.py:16
  4.5 1.9 %collective-permute-start.2 = (bf16[2,80,1280]{2,1,0:T(8,128)(2,1)S(1)}, bf16[2,80,1280]{2,1,0:T(8,128)(2,1)S(1)}, u32[]{:S(2)}, u32[]{:S(2)}) collective-permute-start(bf16[2,80,1280]{2,1,0:T(8,128)(2,1)S(1)} %pad_maximum_fusion.5.refs_0_), channel_id=1, source_target_pairs={{0,48},{16,32},{32,16},{48,0},{64,112},{80,96},{96,80},{112,64},{1... | collective-permute-start | bytes 1228808 | tf_op jit(solution)/shard_map/ppermute | solution.py:16
  6.4 6.9 %collective-permute-start.6 = (bf16[8,1280]{1,0:T(8,128)(2,1)S(1)}, bf16[8,1280]{1,0:T(8,128)(2,1)S(1)}, u32[]{:S(2)}, u32[]{:S(2)}) collective-permute-start(bf16[8,1280]{1,0:T(8,128)(2,1)S(1)} %bitcast.80), channel_id=1, source_target_pairs={{0,2},{1,3},{2,0},{3,1},{4,6},{5,7},{6,4},{7,5},{8,10},{9,11},{10,... | collective-permute-start | bytes 61448 | tf_op jit(solution)/shard_map/ppermute | solution.py:16
  13.3 0.8 collective-permute-start
  14.2 1.3 collective-permute-start.1
  15.5 0.9 collective-permute-start.5
  16.6 15.5 %collective-permute-done = bf16[2,80,1280]{2,1,0:T(8,128)(2,1)S(1)} collective-permute-done((bf16[2,80,1280]{2,1,0:T(8,128)(2,1)S(1)}, bf16[2,80,1280]{2,1,0:T(8,128)(2,1)S(1)}, u32[]{:S(2)}, u32[]{:S(2)}) %collective-permute-start) | collective-permute-done | bytes 409632 | tf_op jit(solution)/shard_map/ppermute | solution.py:16
  32.1 1.3 collective-permute-start.7
  33.5 0.9 collective-permute-start.11
  34.5 1.7 collective-permute-start.12
  36.2 2.5 %collective-permute-start.8 = (bf16[32,1280]{1,0:T(8,128)(2,1)S(1)}, bf16[32,1280]{1,0:T(8,128)(2,1)S(1)}, u32[]{:S(2)}, u32[]{:S(2)}) collective-permute-start(bf16[32,1280]{1,0:T(8,128)(2,1)S(1)} %pad_maximum_fusion.10), channel_id=1, source_target_pairs={{0,8},{1,9},{2,10},{3,11},{4,12},{5,13},{6,14},{7,15},{8,0},{9,1},... | collective-permute-start | bytes 245768 | tf_op jit(solution)/shard_map/ppermute | solution.py:16
  38.7 2.3 %collective-permute-done.8 = bf16[32,1280]{1,0:T(8,128)(2,1)S(1)} collective-permute-done((bf16[32,1280]{1,0:T(8,128)(2,1)S(1)}, bf16[32,1280]{1,0:T(8,128)(2,1)S(1)}, u32[]{:S(2)}, u32[]{:S(2)}) %collective-permute-start.8) | collective-permute-done | bytes 81952 | tf_op jit(solution)/shard_map/ppermute | solution.py:16
  41.1 5.8 %collective-permute-start.9 = (bf16[64,1280]{1,0:T(8,128)(2,1)S(1)}, bf16[64,1280]{1,0:T(8,128)(2,1)S(1)}, u32[]{:S(2)}, u32[]{:S(2)}) collective-permute-start(bf16[64,1280]{1,0:T(8,128)(2,1)S(1)} %pad_maximum_fusion.9), channel_id=1, source_target_pairs={{0,1},{1,0},{2,3},{3,2},{4,5},{5,4},{6,7},{7,6},{8,9},{9,8},{10,11... | collective-permute-start | bytes 491528 | tf_op jit(solution)/shard_map/ppermute | solution.py:16
  46.9 1.0 collective-permute-done.9
  47.9 2.5 %copy-done.1 = bf16[8,256,1280]{2,1,0:T(8,128)(2,1)S(1)} copy-done((bf16[8,256,1280]{2,1,0:T(8,128)(2,1)S(1)}, bf16[8,256,1280]{2,1,0:T(8,128)(2,1)}, u32[]{:S(2)}) %copy-start.1) | copy-done | bytes 5242904
  50.4 9.2 %slots.1 = (bf16[2,64,1280]{2,1,0:T(8,128)(2,1)S(1)}, f32[64,256]{1,0:T(8,128)S(1)}, f32[64,256]{1,0:T(8,128)S(1)}, bf16[2,128,512]{2,1,0:T(8,128)(2,1)S(1)}) custom-call(bf16[128,1280]{1,0:T(8,128)(2,1)S(1)} %constant_dynamic-update-slice_fusion.table, bf16[8,256,1280]{2,1,0:T(8,128)(2,1)S(1)} %copy-done, bf16[8,256,1280]{2,1,0:T(8,128)(2,1)S(1)} %copy-done.1), custom_call_target="tpu_custom_call" | custom-call | flops 838860800 | bytes 10485760 | tf_op jit(solution)/shard_map/slots/pallas_call | solution.py:123
  59.7 1.9 %collective-permute-start.15 = (bf16[128,1280]{1,0:T(8,128)(2,1)S(1)}, bf16[128,1280]{1,0:T(8,128)(2,1)S(1)}, u32[]{:S(2)}, u32[]{:S(2)}) collective-permute-start(bf16[128,1280]{1,0:T(8,128)(2,1)S(1)} %bitcast.73), channel_id=1, source_target_pairs={{0,64},{16,80},{32,96},{48,112},{64,0},{80,16},{96,32},{112,48},{1... | collective-permute-start | bytes 983048 | tf_op jit(solution)/shard_map/ppermute | solution.py:16
  61.6 2.0 %collective-permute-start.14 = (bf16[2,80,1280]{2,1,0:T(8,128)(2,1)S(1)}, bf16[2,80,1280]{2,1,0:T(8,128)(2,1)S(1)}, u32[]{:S(2)}, u32[]{:S(2)}) collective-permute-start(bf16[2,80,1280]{2,1,0:T(8,128)(2,1)S(1)} %collective-permute-done.12.refs_10_), channel_id=1, source_target_pairs={{0,48},{16,32},{32,16},{48,0},{64,112},{80,96},{96,80},{112,64},{1... | collective-permute-start | bytes 1228808 | tf_op jit(solution)/shard_map/ppermute | solution.py:16
  63.6 1.1 collective-permute-start.13
  64.8 0.9 collective-permute-start.18
  65.6 11.0 %collective-permute-done.16 = bf16[128,1280]{1,0:T(8,128)(2,1)S(1)} collective-permute-done((bf16[128,1280]{1,0:T(8,128)(2,1)S(1)}, bf16[128,1280]{1,0:T(8,128)(2,1)S(1)}, u32[]{:S(2)}, u32[]{:S(2)}) %collective-permute-start.16) | collective-permute-done | bytes 327712 | tf_op jit(solution)/shard_map/ppermute | solution.py:16
  76.6 1.7 collective-permute-start.17
  78.4 2.0 %collective-permute-start.20 = (bf16[80,1280]{1,0:T(8,128)(2,1)S(1)}, bf16[80,1280]{1,0:T(8,128)(2,1)S(1)}, u32[]{:S(2)}, u32[]{:S(2)}) collective-permute-start(bf16[80,1280]{1,0:T(8,128)(2,1)S(1)} %slice_bitcast_fusion.4), channel_id=1, source_target_pairs={{0,48},{16,32},{32,16},{48,0},{64,112},{80,96},{96,80},{112,64},{1... | collective-permute-start | bytes 614408 | tf_op jit(solution)/shard_map/ppermute | solution.py:16
  80.5 1.2 collective-permute-done.18.refs_9_
  81.7 6.0 %collective-permute-done.17.refs_8_ = bf16[2,80,1280]{2,1,0:T(8,128)(2,1)S(1)} collective-permute-done((bf16[2,80,1280]{2,1,0:T(8,128)(2,1)S(1)}, bf16[2,80,1280]{2,1,0:T(8,128)(2,1)S(1)}, u32[]{:S(2)}, u32[]{:S(2)}) %collective-permute-start.17) | collective-permute-done | bytes 409632 | tf_op jit(solution)/shard_map/ppermute | solution.py:16
  87.7 4.4 %collective-permute-done.19.refs_13_ = bf16[80,1280]{1,0:T(8,128)(2,1)S(1)} collective-permute-done((bf16[80,1280]{1,0:T(8,128)(2,1)S(1)}, bf16[80,1280]{1,0:T(8,128)(2,1)S(1)}, u32[]{:S(2)}, u32[]{:S(2)}) %collective-permute-start.19) | collective-permute-done | bytes 204832 | tf_op jit(solution)/shard_map/ppermute | solution.py:16
  92.3 4.0 %ffn.1 = (f32[64,1280]{1,0:T(8,128)S(1)}, bf16[64,1280]{1,0:T(8,128)(2,1)S(1)}, bf16[64,1280]{1,0:T(8,128)(2,1)S(1)}, bf16[64,1280]{1,0:T(8,128)(2,1)S(1)}, f32[...) custom-call(bf16[256,1280]{1,0:T(8,128)(2,1)S(1)} %pad_maximum_fusion.1.rows_in, ...), custom_call_target="tpu_custom_call" | custom-call | tf_op jit(solution)/shard_map/ffn/pallas_call | solution.py:66
  96.4 1.9 %collective-permute-start.25 = (bf16[64,1280]{1,0:T(8,128)(2,1)S(1)}, bf16[64,1280]{1,0:T(8,128)(2,1)S(1)}, u32[]{:S(2)}, u32[]{:S(2)}) collective-permute-start(bf16[64,1280]{1,0:T(8,128)(2,1)S(1)} %get-tuple-element.90), channel_id=1, source_target_pairs={{0,128},{16,144},{32,160},{48,176},{64,192},{80,208},{96,224},{112... | collective-permute-start | bytes 491528 | tf_op jit(solution)/shard_map/ppermute | solution.py:16
  98.3 1.6 collective-permute-start.26
  99.9 3.7 %collective-permute-done.24 = bf16[64,1280]{1,0:T(8,128)(2,1)S(1)} collective-permute-done((bf16[64,1280]{1,0:T(8,128)(2,1)S(1)}, bf16[64,1280]{1,0:T(8,128)(2,1)S(1)}, u32[]{:S(2)}, u32[]{:S(2)}) %collective-permute-start.24) | collective-permute-done | bytes 163872 | tf_op jit(solution)/shard_map/ppermute | solution.py:16
  103.7 4.9 %collective-permute-done.26 = bf16[64,1280]{1,0:T(8,128)(2,1)S(1)} collective-permute-done((bf16[64,1280]{1,0:T(8,128)(2,1)S(1)}, bf16[64,1280]{1,0:T(8,128)(2,1)S(1)}, u32[]{:S(2)}, u32[]{:S(2)}) %collective-permute-start.26) | collective-permute-done | bytes 163872 | tf_op jit(solution)/shard_map/ppermute | solution.py:16
  108.6 6.9 %collective-permute-done.22 = bf16[2,64,1280]{2,1,0:T(8,128)(2,1)S(1)} collective-permute-done((bf16[2,64,1280]{2,1,0:T(8,128)(2,1)S(1)}, bf16[2,64,1280]{2,1,0:T(8,128)(2,1)S(1)}, u32[]{:S(2)}, u32[]{:S(2)}) %collective-permute-start.22) | collective-permute-done | bytes 327712 | tf_op jit(solution)/shard_map/ppermute | solution.py:16
  115.6 2.1 %combine_grad.1 = (f32[64,256]{1,0:T(8,128)S(1)}, f32[8,256]{1,0:T(8,128)S(1)}) custom-call(f32[64,1280]{1,0:T(8,128)S(1)} %add_add_fusion.refs_0_, bf16[8,256,1280]{2,1,0:T(8,128)(2,1)S(1)} %bitcast.71, f32[64,256]{1,0:T(8,128)S(1)} %get-tuple-element.96.refs_2_), custom_call_target="tpu_custom_call" | custom-call | flops 167772160 | bytes 5242880 | tf_op jit(solution)/shard_map/combine_grad/pallas_call | solution.py:180
  117.6 1.9 %collective-permute-start.29 = (f32[8,256]{1,0:T(8,128)S(1)}, f32[8,256]{1,0:T(8,128)S(1)}, u32[]{:S(2)}, u32[]{:S(2)}) collective-permute-start(f32[8,256]{1,0:T(8,128)S(1)} %get-tuple-element.98), channel_id=1, source_target_pairs={{0,3},{1,2},{2,1},{3,0},{4,7},{5,6},{6,5},{7,4},{8,11},{9,10},{10,... | collective-permute-start | bytes 24584 | tf_op jit(solution)/shard_map/ppermute | solution.py:16
  119.6 5.0 %collective-permute-start.28 = (f32[8,256]{1,0:T(8,128)S(1)}, f32[8,256]{1,0:T(8,128)S(1)}, u32[]{:S(2)}, u32[]{:S(2)}) collective-permute-start(f32[8,256]{1,0:T(8,128)S(1)} %get-tuple-element.98), channel_id=1, source_target_pairs={{0,2},{1,3},{2,0},{3,1},{4,6},{5,7},{6,4},{7,5},{8,10},{9,11},{10,... | collective-permute-start | bytes 24584 | tf_op jit(solution)/shard_map/ppermute | solution.py:16
  125.0 1.0 collective-permute-done.28
  126.0 8.8 %collective-permute-done.23 = bf16[64,1280]{1,0:T(8,128)(2,1)S(1)} collective-permute-done((bf16[64,1280]{1,0:T(8,128)(2,1)S(1)}, bf16[64,1280]{1,0:T(8,128)(2,1)S(1)}, u32[]{:S(2)}, u32[]{:S(2)}) %collective-permute-start.23) | collective-permute-done | bytes 163872 | tf_op jit(solution)/shard_map/ppermute | solution.py:16
  134.9 1.7 collective-permute-start.32
  136.6 1.0 collective-permute-start.31
  137.6 0.7 collective-permute-start.30
  138.3 0.7 collective-permute-start.34
  138.9 2.3 %dispatch_grad.1 = f32[64,256]{1,0:T(8,128)S(1)} custom-call(f32[64,1280]{1,0:T(8,128)S(1)} %get-tuple-element.125.refs_0_, bf16[8,256,1280]{2,1,0:T(8,128)(2,1)S(1)} %copy-done, f32[64,256]{1,0:T(8,128)S(1)} %get-tuple-element.87.refs_2_), custom_call_target="tpu_custom_call" | custom-call | flops 167772160 | bytes 5242880 | tf_op jit(solution)/shard_map/dispatch_grad/pallas_call | solution.py:180
  141.3 4.8 %collective-permute-start.33 = (bf16[64,256]{1,0:T(8,128)(2,1)S(1)}, bf16[64,256]{1,0:T(8,128)(2,1)S(1)}, u32[]{:S(2)}, u32[]{:S(2)}) collective-permute-start(bf16[64,256]{1,0:T(8,128)(2,1)S(1)} %fusion.4), channel_id=1, source_target_pairs={{0,2},{1,3},{2,0},{3,1},{4,6},{5,7},{6,4},{7,5},{8,10},{9,11},{10,... | collective-permute-start | bytes 98312 | tf_op jit(solution)/shard_map/ppermute | solution.py:16
  146.1 2.8 %collective-permute-done.33 = bf16[64,256]{1,0:T(8,128)(2,1)S(1)} collective-permute-done((bf16[64,256]{1,0:T(8,128)(2,1)S(1)}, bf16[64,256]{1,0:T(8,128)(2,1)S(1)}, u32[]{:S(2)}, u32[]{:S(2)}) %collective-permute-start.33) | collective-permute-done | bytes 32800 | tf_op jit(solution)/shard_map/ppermute | solution.py:16
  148.8 2.4 %collective-permute-start.37 = (bf16[128,256]{1,0:T(8,128)(2,1)S(1)}, bf16[128,256]{1,0:T(8,128)(2,1)S(1)}, u32[]{:S(2)}, u32[]{:S(2)}) collective-permute-start(bf16[128,256]{1,0:T(8,128)(2,1)S(1)} %pad_maximum_fusion.11), channel_id=1, source_target_pairs={{0,12},{1,13},{2,14},{3,15},{4,8},{5,9},{6,10},{7,11},{8,4},{9,5},... | collective-permute-start | bytes 196616 | tf_op jit(solution)/shard_map/ppermute | solution.py:16
  151.2 0.6 collective-permute-start.36
  152.2 0.8 convolution_bitcast_fusion
  153.0 0.5 collective-permute-start.38
  153.5 2.7 %collective-permute-done.38 = f32[8,1280]{1,0:T(8,128)S(1)} collective-permute-done((f32[8,1280]{1,0:T(8,128)S(1)}, f32[8,1280]{1,0:T(8,128)S(1)}, u32[]{:S(2)}, u32[]{:S(2)}) %collective-permute-start.38) | collective-permute-done | bytes 40992 | tf_op jit(solution)/shard_map/ppermute | solution.py:16
  156.2 2.4 %collective-permute-start.41 = (bf16[2,64,1280]{2,1,0:T(8,128)(2,1)S(1)}, bf16[2,64,1280]{2,1,0:T(8,128)(2,1)S(1)}, u32[]{:S(2)}, u32[]{:S(2)}) collective-permute-start(bf16[2,64,1280]{2,1,0:T(8,128)(2,1)S(1)} %pad_maximum_fusion.7.pair), channel_id=1, source_target_pairs={{0,12},{1,13},{2,14},{3,15},{4,8},{5,9},{6,10},{7,11},{8,4},{9,5},... | collective-permute-start | bytes 983048 | tf_op jit(solution)/shard_map/ppermute | solution.py:16
  158.9 0.7 collective-permute-start.39
  159.5 0.6 collective-permute-start.42
  160.2 3.5 %collective-permute-done.42 = f32[8,1280]{1,0:T(8,128)S(1)} collective-permute-done((f32[8,1280]{1,0:T(8,128)S(1)}, f32[8,1280]{1,0:T(8,128)S(1)}, u32[]{:S(2)}, u32[]{:S(2)}) %collective-permute-start.42) | collective-permute-done | bytes 40992 | tf_op jit(solution)/shard_map/ppermute | solution.py:16
  163.7 1.1 collective-permute-start.43
  164.9 0.7 through_logits.1.base
  165.6 1.3 collective-permute-done.43
  166.9 5.4 %collective-permute-done.41.three = bf16[2,64,1280]{2,1,0:T(8,128)(2,1)S(1)} collective-permute-done((bf16[2,64,1280]{2,1,0:T(8,128)(2,1)S(1)}, bf16[2,64,1280]{2,1,0:T(8,128)(2,1)S(1)}, u32[]{:S(2)}, u32[]{:S(2)}) %collective-permute-start.41) | collective-permute-done | bytes 327712 | tf_op jit(solution)/shard_map/ppermute | solution.py:16
  172.3 0.8 through_slots.1
  173.2 3.1 %collective-permute-start.44 = (f32[128,1280]{1,0:T(8,128)S(1)}, f32[128,1280]{1,0:T(8,128)S(1)}, u32[]{:S(2)}, u32[]{:S(2)}) collective-permute-start(f32[128,1280]{1,0:T(8,128)S(1)} %get-tuple-element.122), channel_id=1, source_target_pairs={{0,1},{1,0},{2,3},{3,2},{4,5},{5,4},{6,7},{7,6},{8,9},{9,8},{10,11... | collective-permute-start | bytes 1966088 | tf_op jit(solution)/shard_map/ppermute | solution.py:16
  176.2 2.8 %collective-permute-start.45 = (f32[8,1280]{1,0:T(8,128)S(1)}, f32[8,1280]{1,0:T(8,128)S(1)}, u32[]{:S(2)}, u32[]{:S(2)}) collective-permute-start(f32[8,1280]{1,0:T(8,128)S(1)} %add.90), channel_id=1, source_target_pairs={{0,32},{16,48},{32,0},{48,16},{64,96},{80,112},{96,64},{112,80},{1... | collective-permute-start | bytes 122888 | tf_op jit(solution)/shard_map/ppermute | solution.py:16
  179.0 1.6 collective-permute-done.45
  180.6 0.6 add_bitcast_fusion
  181.2 0.8 add_convert_fusion
  (87 shorter events, 2.7 us)
Async XLA Ops:
  0.6 1.5 copy-start.2
  2.1 4.2 %copy-start.3 = (bf16[1280,8]{0,1:T(8,128)(2,1)S(1)}, bf16[1280,8]{0,1:T(8,128)(2,1)}, u32[]{:S(2)}) copy-start(bf16[1280,8]{0,1:T(8,128)(2,1)} %param.7) | copy-start | bytes 61444
  2.3 13.3 %collective-permute-start.4 = (bf16[2,80,1280]{2,1,0:T(8,128)(2,1)S(1)}, bf16[2,80,1280]{2,1,0:T(8,128)(2,1)S(1)}, u32[]{:S(2)}, u32[]{:S(2)}) collective-permute-start(bf16[2,80,1280]{2,1,0:T(8,128)(2,1)S(1)} %pad_maximum_fusion.5.refs_0_), channel_id=1, source_target_pairs={{0,16},{16,0},{32,48},{48,32},{64,80},{80,64},{96,112},{112,96},{1... | collective-permute-start | bytes 1228808 | tf_op jit(solution)/shard_map/ppermute | solution.py:16
  4.5 11.9 %collective-permute-start.2 = (bf16[2,80,1280]{2,1,0:T(8,128)(2,1)S(1)}, bf16[2,80,1280]{2,1,0:T(8,128)(2,1)S(1)}, u32[]{:S(2)}, u32[]{:S(2)}) collective-permute-start(bf16[2,80,1280]{2,1,0:T(8,128)(2,1)S(1)} %pad_maximum_fusion.5.refs_0_), channel_id=1, source_target_pairs={{0,48},{16,32},{32,16},{48,0},{64,112},{80,96},{96,80},{112,64},{1... | collective-permute-start | bytes 1228808 | tf_op jit(solution)/shard_map/ppermute | solution.py:16
  6.4 10.2 %collective-permute-start.6 = (bf16[8,1280]{1,0:T(8,128)(2,1)S(1)}, bf16[8,1280]{1,0:T(8,128)(2,1)S(1)}, u32[]{:S(2)}, u32[]{:S(2)}) collective-permute-start(bf16[8,1280]{1,0:T(8,128)(2,1)S(1)} %bitcast.80), channel_id=1, source_target_pairs={{0,2},{1,3},{2,0},{3,1},{4,6},{5,7},{6,4},{7,5},{8,10},{9,11},{10,... | collective-permute-start | bytes 61448 | tf_op jit(solution)/shard_map/ppermute | solution.py:16
  13.3 18.7 %collective-permute-start = (bf16[2,80,1280]{2,1,0:T(8,128)(2,1)S(1)}, bf16[2,80,1280]{2,1,0:T(8,128)(2,1)S(1)}, u32[]{:S(2)}, u32[]{:S(2)}) collective-permute-start(bf16[2,80,1280]{2,1,0:T(8,128)(2,1)S(1)} %pad_maximum_fusion.3), channel_id=1, source_target_pairs={{0,64},{16,80},{32,96},{48,112},{64,0},{80,16},{96,32},{112,48},{1... | collective-permute-start | bytes 1228808 | tf_op jit(solution)/shard_map/ppermute | solution.py:16
  14.1 33.8 %copy-start = (bf16[8,256,1280]{2,1,0:T(8,128)(2,1)S(1)}, bf16[8,256,1280]{2,1,0:T(8,128)(2,1)}, u32[]{:S(2)}) copy-start(bf16[8,256,1280]{2,1,0:T(8,128)(2,1)} %refs_1_.2) | copy-start | bytes 15728644
  14.2 17.9 %collective-permute-start.1 = (bf16[2,80,1280]{2,1,0:T(8,128)(2,1)S(1)}, bf16[2,80,1280]{2,1,0:T(8,128)(2,1)S(1)}, u32[]{:S(2)}, u32[]{:S(2)}) collective-permute-start(bf16[2,80,1280]{2,1,0:T(8,128)(2,1)S(1)} %pad_maximum_fusion.4), channel_id=1, source_target_pairs={{0,128},{16,144},{32,160},{48,176},{64,192},{80,208},{96,224},{112... | collective-permute-start | bytes 1228808 | tf_op jit(solution)/shard_map/ppermute | solution.py:16
  15.5 16.5 %collective-permute-start.5 = (bf16[80,1280]{1,0:T(8,128)(2,1)S(1)}, bf16[80,1280]{1,0:T(8,128)(2,1)S(1)}, u32[]{:S(2)}, u32[]{:S(2)}) collective-permute-start(bf16[80,1280]{1,0:T(8,128)(2,1)S(1)} %slice_bitcast_fusion.2), channel_id=1, source_target_pairs={{0,48},{16,32},{32,16},{48,0},{64,112},{80,96},{96,80},{112,64},{1... | collective-permute-start | bytes 614408 | tf_op jit(solution)/shard_map/ppermute | solution.py:16
  16.4 15.7 %collective-permute-start.3 = (bf16[80,1280]{1,0:T(8,128)(2,1)S(1)}, bf16[80,1280]{1,0:T(8,128)(2,1)S(1)}, u32[]{:S(2)}, u32[]{:S(2)}) collective-permute-start(bf16[80,1280]{1,0:T(8,128)(2,1)S(1)} %slice_bitcast_fusion.3), channel_id=1, source_target_pairs={{0,16},{16,0},{32,48},{48,32},{64,80},{80,64},{96,112},{112,96},{1... | collective-permute-start | bytes 614408 | tf_op jit(solution)/shard_map/ppermute | solution.py:16
  32.1 4.1 %collective-permute-start.7 = (bf16[16,1280]{1,0:T(8,128)(2,1)S(1)}, bf16[16,1280]{1,0:T(8,128)(2,1)S(1)}, u32[]{:S(2)}, u32[]{:S(2)}) collective-permute-start(bf16[16,1280]{1,0:T(8,128)(2,1)S(1)} %pad_maximum_fusion.12), channel_id=1, source_target_pairs={{0,4},{1,5},{2,6},{3,7},{4,0},{5,1},{6,2},{7,3},{8,12},{9,13},{10,... | collective-permute-start | bytes 122888 | tf_op jit(solution)/shard_map/ppermute | solution.py:16
  33.5 26.1 %collective-permute-start.11 = (bf16[2,2,80,1280]{3,2,1,0:T(8,128)(2,1)S(1)}, bf16[2,2,80,1280]{3,2,1,0:T(8,128)(2,1)S(1)}, u32[]{:S(2)}, u32[]{:S(2)}) collective-permute-start(bf16[2,2,80,1280]{3,2,1,0:T(8,128)(2,1)S(1)} %pad_maximum_fusion.refs_5_), channel_id=1, source_target_pairs={{0,48},{16,32},{32,16},{48,0},{64,112},{80,96},{96,80},{112,64},{1... | collective-permute-start | bytes 2457608 | tf_op jit(solution)/shard_map/ppermute | solution.py:16
  34.3 25.3 %collective-permute-start.10 = (bf16[2,2,80,1280]{3,2,1,0:T(8,128)(2,1)S(1)}, bf16[2,2,80,1280]{3,2,1,0:T(8,128)(2,1)S(1)}, u32[]{:S(2)}, u32[]{:S(2)}) collective-permute-start(bf16[2,2,80,1280]{3,2,1,0:T(8,128)(2,1)S(1)} %pad_maximum_fusion.refs_5_), channel_id=1, source_target_pairs={{0,16},{16,0},{32,48},{48,32},{64,80},{80,64},{96,112},{112,96},{1... | collective-permute-start | bytes 2457608 | tf_op jit(solution)/shard_map/ppermute | solution.py:16
  34.5 25.1 %collective-permute-start.12 = (bf16[2,80,1280]{2,1,0:T(8,128)(2,1)S(1)}, bf16[2,80,1280]{2,1,0:T(8,128)(2,1)S(1)}, u32[]{:S(2)}, u32[]{:S(2)}) collective-permute-start(bf16[2,80,1280]{2,1,0:T(8,128)(2,1)S(1)} %pad_maximum_fusion.6), channel_id=1, source_target_pairs={{0,192},{16,208},{32,224},{48,240},{64,128},{80,144},{96,160},{112... | collective-permute-start | bytes 1228808 | tf_op jit(solution)/shard_map/ppermute | solution.py:16
  36.2 4.9 %collective-permute-start.8 = (bf16[32,1280]{1,0:T(8,128)(2,1)S(1)}, bf16[32,1280]{1,0:T(8,128)(2,1)S(1)}, u32[]{:S(2)}, u32[]{:S(2)}) collective-permute-start(bf16[32,1280]{1,0:T(8,128)(2,1)S(1)} %pad_maximum_fusion.10), channel_id=1, source_target_pairs={{0,8},{1,9},{2,10},{3,11},{4,12},{5,13},{6,14},{7,15},{8,0},{9,1},... | collective-permute-start | bytes 245768 | tf_op jit(solution)/shard_map/ppermute | solution.py:16
  41.1 6.8 %collective-permute-start.9 = (bf16[64,1280]{1,0:T(8,128)(2,1)S(1)}, bf16[64,1280]{1,0:T(8,128)(2,1)S(1)}, u32[]{:S(2)}, u32[]{:S(2)}) collective-permute-start(bf16[64,1280]{1,0:T(8,128)(2,1)S(1)} %pad_maximum_fusion.9), channel_id=1, source_target_pairs={{0,1},{1,0},{2,3},{3,2},{4,5},{5,4},{6,7},{7,6},{8,9},{9,8},{10,11... | collective-permute-start | bytes 491528 | tf_op jit(solution)/shard_map/ppermute | solution.py:16
  47.9 2.5 %copy-start.1 = (bf16[8,256,1280]{2,1,0:T(8,128)(2,1)S(1)}, bf16[8,256,1280]{2,1,0:T(8,128)(2,1)}, u32[]{:S(2)}) copy-start(bf16[8,256,1280]{2,1,0:T(8,128)(2,1)} %refs_1_.3) | copy-start | bytes 15728644
  59.6 17.0 %collective-permute-start.16 = (bf16[128,1280]{1,0:T(8,128)(2,1)S(1)}, bf16[128,1280]{1,0:T(8,128)(2,1)S(1)}, u32[]{:S(2)}, u32[]{:S(2)}) collective-permute-start(bf16[128,1280]{1,0:T(8,128)(2,1)S(1)} %bitcast.72), channel_id=1, source_target_pairs={{0,128},{16,144},{32,160},{48,176},{64,192},{80,208},{96,224},{112... | collective-permute-start | bytes 983048 | tf_op jit(solution)/shard_map/ppermute | solution.py:16
  59.7 18.6 %collective-permute-start.15 = (bf16[128,1280]{1,0:T(8,128)(2,1)S(1)}, bf16[128,1280]{1,0:T(8,128)(2,1)S(1)}, u32[]{:S(2)}, u32[]{:S(2)}) collective-permute-start(bf16[128,1280]{1,0:T(8,128)(2,1)S(1)} %bitcast.73), channel_id=1, source_target_pairs={{0,64},{16,80},{32,96},{48,112},{64,0},{80,16},{96,32},{112,48},{1... | collective-permute-start | bytes 983048 | tf_op jit(solution)/shard_map/ppermute | solution.py:16
  61.6 16.7 %collective-permute-start.14 = (bf16[2,80,1280]{2,1,0:T(8,128)(2,1)S(1)}, bf16[2,80,1280]{2,1,0:T(8,128)(2,1)S(1)}, u32[]{:S(2)}, u32[]{:S(2)}) collective-permute-start(bf16[2,80,1280]{2,1,0:T(8,128)(2,1)S(1)} %collective-permute-done.12.refs_10_), channel_id=1, source_target_pairs={{0,48},{16,32},{32,16},{48,0},{64,112},{80,96},{96,80},{112,64},{1... | collective-permute-start | bytes 1228808 | tf_op jit(solution)/shard_map/ppermute | solution.py:16
  63.6 14.8 %collective-permute-start.13 = (bf16[2,80,1280]{2,1,0:T(8,128)(2,1)S(1)}, bf16[2,80,1280]{2,1,0:T(8,128)(2,1)S(1)}, u32[]{:S(2)}, u32[]{:S(2)}) collective-permute-start(bf16[2,80,1280]{2,1,0:T(8,128)(2,1)S(1)} %collective-permute-done.12.refs_10_), channel_id=1, source_target_pairs={{0,16},{16,0},{32,48},{48,32},{64,80},{80,64},{96,112},{112,96},{1... | collective-permute-start | bytes 1228808 | tf_op jit(solution)/shard_map/ppermute | solution.py:16
  64.8 16.9 %collective-permute-start.18 = (bf16[2,80,1280]{2,1,0:T(8,128)(2,1)S(1)}, bf16[2,80,1280]{2,1,0:T(8,128)(2,1)S(1)}, u32[]{:S(2)}, u32[]{:S(2)}) collective-permute-start(bf16[2,80,1280]{2,1,0:T(8,128)(2,1)S(1)} %slice_bitcast_fusion), channel_id=1, source_target_pairs={{0,48},{16,32},{32,16},{48,0},{64,112},{80,96},{96,80},{112,64},{1... | collective-permute-start | bytes 1228808 | tf_op jit(solution)/shard_map/ppermute | solution.py:16
  76.6 11.1 %collective-permute-start.17 = (bf16[2,80,1280]{2,1,0:T(8,128)(2,1)S(1)}, bf16[2,80,1280]{2,1,0:T(8,128)(2,1)S(1)}, u32[]{:S(2)}, u32[]{:S(2)}) collective-permute-start(bf16[2,80,1280]{2,1,0:T(8,128)(2,1)S(1)} %slice_bitcast_fusion.1), channel_id=1, source_target_pairs={{0,16},{16,0},{32,48},{48,32},{64,80},{80,64},{96,112},{112,96},{1... | collective-permute-start | bytes 1228808 | tf_op jit(solution)/shard_map/ppermute | solution.py:16
  78.4 9.3 %collective-permute-start.20 = (bf16[80,1280]{1,0:T(8,128)(2,1)S(1)}, bf16[80,1280]{1,0:T(8,128)(2,1)S(1)}, u32[]{:S(2)}, u32[]{:S(2)}) collective-permute-start(bf16[80,1280]{1,0:T(8,128)(2,1)S(1)} %slice_bitcast_fusion.4), channel_id=1, source_target_pairs={{0,48},{16,32},{32,16},{48,0},{64,112},{80,96},{96,80},{112,64},{1... | collective-permute-start | bytes 614408 | tf_op jit(solution)/shard_map/ppermute | solution.py:16
  80.4 11.7 %collective-permute-start.19 = (bf16[80,1280]{1,0:T(8,128)(2,1)S(1)}, bf16[80,1280]{1,0:T(8,128)(2,1)S(1)}, u32[]{:S(2)}, u32[]{:S(2)}) collective-permute-start(bf16[80,1280]{1,0:T(8,128)(2,1)S(1)} %slice_bitcast_fusion.5), channel_id=1, source_target_pairs={{0,16},{16,0},{32,48},{48,32},{64,80},{80,64},{96,112},{112,96},{1... | collective-permute-start | bytes 614408 | tf_op jit(solution)/shard_map/ppermute | solution.py:16
  80.4 11.7 %collective-permute-start.21 = (bf16[128,1280]{1,0:T(8,128)(2,1)S(1)}, bf16[128,1280]{1,0:T(8,128)(2,1)S(1)}, u32[]{:S(2)}, u32[]{:S(2)}) collective-permute-start(bf16[128,1280]{1,0:T(8,128)(2,1)S(1)} %collective-permute-done.16), channel_id=1, source_target_pairs={{0,64},{16,80},{32,96},{48,112},{64,0},{80,16},{96,32},{112,48},{1... | collective-permute-start | bytes 983048 | tf_op jit(solution)/shard_map/ppermute | solution.py:16
  92.2 23.3 %slice-start = ((s8[5242880]{0:T(1024)(128)(4,1)}), s8[4194304]{0:T(1024)(128)(4,1)S(1)}, s32[]{:S(2)}) async-start(s8[5242880]{0:T(1024)(128)(4,1)} %bitcast.70), calls=%async_computation | async-start | bytes 8388608
  92.2 23.3 %slice-start.1 = ((s8[5242880]{0:T(1024)(128)(4,1)}), s8[1048576]{0:T(1024)(128)(4,1)S(1)}, s32[]{:S(2)}) async-start(s8[5242880]{0:T(1024)(128)(4,1)} %bitcast.70), calls=%async_computation.1 | async-start | bytes 2097152
  96.3 7.4 %collective-permute-start.24 = (bf16[64,1280]{1,0:T(8,128)(2,1)S(1)}, bf16[64,1280]{1,0:T(8,128)(2,1)S(1)}, u32[]{:S(2)}, u32[]{:S(2)}) collective-permute-start(bf16[64,1280]{1,0:T(8,128)(2,1)S(1)} %get-tuple-element.89), channel_id=1, source_target_pairs={{0,64},{16,80},{32,96},{48,112},{64,0},{80,16},{96,32},{112,48},{1... | collective-permute-start | bytes 491528 | tf_op jit(solution)/shard_map/ppermute | solution.py:16
  96.4 7.3 %collective-permute-start.25 = (bf16[64,1280]{1,0:T(8,128)(2,1)S(1)}, bf16[64,1280]{1,0:T(8,128)(2,1)S(1)}, u32[]{:S(2)}, u32[]{:S(2)}) collective-permute-start(bf16[64,1280]{1,0:T(8,128)(2,1)S(1)} %get-tuple-element.90), channel_id=1, source_target_pairs={{0,128},{16,144},{32,160},{48,176},{64,192},{80,208},{96,224},{112... | collective-permute-start | bytes 491528 | tf_op jit(solution)/shard_map/ppermute | solution.py:16
  98.3 10.3 %collective-permute-start.26 = (bf16[64,1280]{1,0:T(8,128)(2,1)S(1)}, bf16[64,1280]{1,0:T(8,128)(2,1)S(1)}, u32[]{:S(2)}, u32[]{:S(2)}) collective-permute-start(bf16[64,1280]{1,0:T(8,128)(2,1)S(1)} %get-tuple-element.91), channel_id=1, source_target_pairs={{0,192},{16,208},{32,224},{48,240},{64,128},{80,144},{96,160},{112... | collective-permute-start | bytes 491528 | tf_op jit(solution)/shard_map/ppermute | solution.py:16
  99.9 15.5 %collective-permute-start.22 = (bf16[2,64,1280]{2,1,0:T(8,128)(2,1)S(1)}, bf16[2,64,1280]{2,1,0:T(8,128)(2,1)S(1)}, u32[]{:S(2)}, u32[]{:S(2)}) collective-permute-start(bf16[2,64,1280]{2,1,0:T(8,128)(2,1)S(1)} %get-tuple-element.85), channel_id=1, source_target_pairs={{0,64},{16,80},{32,96},{48,112},{64,0},{80,16},{96,32},{112,48},{1... | collective-permute-start | bytes 983048 | tf_op jit(solution)/shard_map/ppermute | solution.py:16
  117.6 7.4 %collective-permute-start.29 = (f32[8,256]{1,0:T(8,128)S(1)}, f32[8,256]{1,0:T(8,128)S(1)}, u32[]{:S(2)}, u32[]{:S(2)}) collective-permute-start(f32[8,256]{1,0:T(8,128)S(1)} %get-tuple-element.98), channel_id=1, source_target_pairs={{0,3},{1,2},{2,1},{3,0},{4,7},{5,6},{6,5},{7,4},{8,11},{9,10},{10,... | collective-permute-start | bytes 24584 | tf_op jit(solution)/shard_map/ppermute | solution.py:16
  119.6 6.4 %collective-permute-start.28 = (f32[8,256]{1,0:T(8,128)S(1)}, f32[8,256]{1,0:T(8,128)S(1)}, u32[]{:S(2)}, u32[]{:S(2)}) collective-permute-start(f32[8,256]{1,0:T(8,128)S(1)} %get-tuple-element.98), channel_id=1, source_target_pairs={{0,2},{1,3},{2,0},{3,1},{4,6},{5,7},{6,4},{7,5},{8,10},{9,11},{10,... | collective-permute-start | bytes 24584 | tf_op jit(solution)/shard_map/ppermute | solution.py:16
  124.6 1.5 collective-permute-start.27
  124.6 10.3 %collective-permute-start.23 = (bf16[64,1280]{1,0:T(8,128)(2,1)S(1)}, bf16[64,1280]{1,0:T(8,128)(2,1)S(1)}, u32[]{:S(2)}, u32[]{:S(2)}) collective-permute-start(bf16[64,1280]{1,0:T(8,128)(2,1)S(1)} %fusion), channel_id=1, source_target_pairs={{0,128},{16,144},{32,160},{48,176},{64,192},{80,208},{96,224},{112... | collective-permute-start | bytes 491528 | tf_op jit(solution)/shard_map/ppermute | solution.py:16
  134.9 6.3 %collective-permute-start.32 = (f32[8,256]{1,0:T(8,128)S(1)}, f32[8,256]{1,0:T(8,128)S(1)}, u32[]{:S(2)}, u32[]{:S(2)}) collective-permute-start(f32[8,256]{1,0:T(8,128)S(1)} %add_add_fusion.2), channel_id=1, source_target_pairs={{0,12},{1,13},{2,14},{3,15},{4,8},{5,9},{6,10},{7,11},{8,4},{9,5},... | collective-permute-start | bytes 24584 | tf_op jit(solution)/shard_map/ppermute | solution.py:16
  136.6 4.7 %collective-permute-start.31 = (f32[8,256]{1,0:T(8,128)S(1)}, f32[8,256]{1,0:T(8,128)S(1)}, u32[]{:S(2)}, u32[]{:S(2)}) collective-permute-start(f32[8,256]{1,0:T(8,128)S(1)} %add_add_fusion.2), channel_id=1, source_target_pairs={{0,8},{1,9},{2,10},{3,11},{4,12},{5,13},{6,14},{7,15},{8,0},{9,1},... | collective-permute-start | bytes 24584 | tf_op jit(solution)/shard_map/ppermute | solution.py:16
  137.6 3.7 %collective-permute-start.30 = (f32[8,256]{1,0:T(8,128)S(1)}, f32[8,256]{1,0:T(8,128)S(1)}, u32[]{:S(2)}, u32[]{:S(2)}) collective-permute-start(f32[8,256]{1,0:T(8,128)S(1)} %add_add_fusion.2), channel_id=1, source_target_pairs={{0,4},{1,5},{2,6},{3,7},{4,0},{5,1},{6,2},{7,3},{8,12},{9,13},{10,... | collective-permute-start | bytes 24584 | tf_op jit(solution)/shard_map/ppermute | solution.py:16
  138.3 10.6 %collective-permute-start.34 = (bf16[64,1280]{1,0:T(8,128)(2,1)S(1)}, bf16[64,1280]{1,0:T(8,128)(2,1)S(1)}, u32[]{:S(2)}, u32[]{:S(2)}) collective-permute-start(bf16[64,1280]{1,0:T(8,128)(2,1)S(1)} %get-tuple-element.124), channel_id=1, source_target_pairs={{0,2},{1,3},{2,0},{3,1},{4,6},{5,7},{6,4},{7,5},{8,10},{9,11},{10,... | collective-permute-start | bytes 491528 | tf_op jit(solution)/shard_map/ppermute | solution.py:16
  141.3 7.5 %collective-permute-start.33 = (bf16[64,256]{1,0:T(8,128)(2,1)S(1)}, bf16[64,256]{1,0:T(8,128)(2,1)S(1)}, u32[]{:S(2)}, u32[]{:S(2)}) collective-permute-start(bf16[64,256]{1,0:T(8,128)(2,1)S(1)} %fusion.4), channel_id=1, source_target_pairs={{0,2},{1,3},{2,0},{3,1},{4,6},{5,7},{6,4},{7,5},{8,10},{9,11},{10,... | collective-permute-start | bytes 98312 | tf_op jit(solution)/shard_map/ppermute | solution.py:16
  148.8 7.3 %collective-permute-start.37 = (bf16[128,256]{1,0:T(8,128)(2,1)S(1)}, bf16[128,256]{1,0:T(8,128)(2,1)S(1)}, u32[]{:S(2)}, u32[]{:S(2)}) collective-permute-start(bf16[128,256]{1,0:T(8,128)(2,1)S(1)} %pad_maximum_fusion.11), channel_id=1, source_target_pairs={{0,12},{1,13},{2,14},{3,15},{4,8},{5,9},{6,10},{7,11},{8,4},{9,5},... | collective-permute-start | bytes 196616 | tf_op jit(solution)/shard_map/ppermute | solution.py:16
  151.2 4.9 %collective-permute-start.36 = (bf16[128,256]{1,0:T(8,128)(2,1)S(1)}, bf16[128,256]{1,0:T(8,128)(2,1)S(1)}, u32[]{:S(2)}, u32[]{:S(2)}) collective-permute-start(bf16[128,256]{1,0:T(8,128)(2,1)S(1)} %pad_maximum_fusion.11), channel_id=1, source_target_pairs={{0,8},{1,9},{2,10},{3,11},{4,12},{5,13},{6,14},{7,15},{8,0},{9,1},... | collective-permute-start | bytes 196616 | tf_op jit(solution)/shard_map/ppermute | solution.py:16
  151.8 4.4 %collective-permute-start.35 = (bf16[128,256]{1,0:T(8,128)(2,1)S(1)}, bf16[128,256]{1,0:T(8,128)(2,1)S(1)}, u32[]{:S(2)}, u32[]{:S(2)}) collective-permute-start(bf16[128,256]{1,0:T(8,128)(2,1)S(1)} %pad_maximum_fusion.11), channel_id=1, source_target_pairs={{0,4},{1,5},{2,6},{3,7},{4,0},{5,1},{6,2},{7,3},{8,12},{9,13},{10,... | collective-permute-start | bytes 196616 | tf_op jit(solution)/shard_map/ppermute | solution.py:16
  153.0 3.2 %collective-permute-start.38 = (f32[8,1280]{1,0:T(8,128)S(1)}, f32[8,1280]{1,0:T(8,128)S(1)}, u32[]{:S(2)}, u32[]{:S(2)}) collective-permute-start(f32[8,1280]{1,0:T(8,128)S(1)} %convolution_bitcast_fusion), channel_id=1, source_target_pairs={{0,64},{16,80},{32,96},{48,112},{64,0},{80,16},{96,32},{112,48},{1... | collective-permute-start | bytes 122888 | tf_op jit(solution)/shard_map/ppermute | solution.py:16
  156.2 16.1 %collective-permute-start.41 = (bf16[2,64,1280]{2,1,0:T(8,128)(2,1)S(1)}, bf16[2,64,1280]{2,1,0:T(8,128)(2,1)S(1)}, u32[]{:S(2)}, u32[]{:S(2)}) collective-permute-start(bf16[2,64,1280]{2,1,0:T(8,128)(2,1)S(1)} %pad_maximum_fusion.7.pair), channel_id=1, source_target_pairs={{0,12},{1,13},{2,14},{3,15},{4,8},{5,9},{6,10},{7,11},{8,4},{9,5},... | collective-permute-start | bytes 983048 | tf_op jit(solution)/shard_map/ppermute | solution.py:16
  158.6 13.7 %collective-permute-start.40 = (bf16[2,64,1280]{2,1,0:T(8,128)(2,1)S(1)}, bf16[2,64,1280]{2,1,0:T(8,128)(2,1)S(1)}, u32[]{:S(2)}, u32[]{:S(2)}) collective-permute-start(bf16[2,64,1280]{2,1,0:T(8,128)(2,1)S(1)} %pad_maximum_fusion.7.pair), channel_id=1, source_target_pairs={{0,8},{1,9},{2,10},{3,11},{4,12},{5,13},{6,14},{7,15},{8,0},{9,1},... | collective-permute-start | bytes 983048 | tf_op jit(solution)/shard_map/ppermute | solution.py:16
  158.9 13.5 %collective-permute-start.39 = (bf16[2,64,1280]{2,1,0:T(8,128)(2,1)S(1)}, bf16[2,64,1280]{2,1,0:T(8,128)(2,1)S(1)}, u32[]{:S(2)}, u32[]{:S(2)}) collective-permute-start(bf16[2,64,1280]{2,1,0:T(8,128)(2,1)S(1)} %pad_maximum_fusion.7.pair), channel_id=1, source_target_pairs={{0,4},{1,5},{2,6},{3,7},{4,0},{5,1},{6,2},{7,3},{8,12},{9,13},{10,... | collective-permute-start | bytes 983048 | tf_op jit(solution)/shard_map/ppermute | solution.py:16
  159.5 4.2 %collective-permute-start.42 = (f32[8,1280]{1,0:T(8,128)S(1)}, f32[8,1280]{1,0:T(8,128)S(1)}, u32[]{:S(2)}, u32[]{:S(2)}) collective-permute-start(f32[8,1280]{1,0:T(8,128)S(1)} %add.88), channel_id=1, source_target_pairs={{0,128},{16,144},{32,160},{48,176},{64,192},{80,208},{96,224},{112... | collective-permute-start | bytes 122888 | tf_op jit(solution)/shard_map/ppermute | solution.py:16
  163.7 3.1 %collective-permute-start.43 = (f32[8,1280]{1,0:T(8,128)S(1)}, f32[8,1280]{1,0:T(8,128)S(1)}, u32[]{:S(2)}, u32[]{:S(2)}) collective-permute-start(f32[8,1280]{1,0:T(8,128)S(1)} %add.89), channel_id=1, source_target_pairs={{0,16},{16,0},{32,48},{48,32},{64,80},{80,64},{96,112},{112,96},{1... | collective-permute-start | bytes 122888 | tf_op jit(solution)/shard_map/ppermute | solution.py:16
  173.2 8.1 %collective-permute-start.44 = (f32[128,1280]{1,0:T(8,128)S(1)}, f32[128,1280]{1,0:T(8,128)S(1)}, u32[]{:S(2)}, u32[]{:S(2)}) collective-permute-start(f32[128,1280]{1,0:T(8,128)S(1)} %get-tuple-element.122), channel_id=1, source_target_pairs={{0,1},{1,0},{2,3},{3,2},{4,5},{5,4},{6,7},{7,6},{8,9},{9,8},{10,11... | collective-permute-start | bytes 1966088 | tf_op jit(solution)/shard_map/ppermute | solution.py:16
  176.2 4.4 %collective-permute-start.45 = (f32[8,1280]{1,0:T(8,128)S(1)}, f32[8,1280]{1,0:T(8,128)S(1)}, u32[]{:S(2)}, u32[]{:S(2)}) collective-permute-start(f32[8,1280]{1,0:T(8,128)S(1)} %add.90), channel_id=1, source_target_pairs={{0,32},{16,48},{32,0},{48,16},{64,96},{80,112},{96,64},{112,80},{1... | collective-permute-start | bytes 122888 | tf_op jit(solution)/shard_map/ppermute | solution.py:16

commit v5 on v2

--- a/solution.py
+++ b/solution.py
@@ -48,10 +48,10 @@
     slope = cdf + 0.5 * pre * (1.0 - th * th) * (ROOT * (1.0 + 3 * 0.044715 * sq))
     hidden_grad = jnp.dot(rows_go[...], w2[...], preferred_element_type=F32)
     pre_grad = (hidden_grad * slope).astype(BF16)
-    own_rows = outs[0].shape[0]
+    rows = outs[0].shape[0]
     for whole, blocks in ((nt(hidden, w2[...]), outs), (nt(pre_grad, w1[...]), grads)):
         for a, block in enumerate(blocks):
-            block[...] = whole[a * own_rows : (a + 1) * own_rows].astype(block.dtype)
+            block[...] = whole[a * rows : (a + 1) * rows].astype(block.dtype)
 
 
 def ffn(rows_in, rows_go, blocks, own_rows):
@@ -135,6 +135,9 @@
             pl.BlockSpec((2, 32, slots * 4), lambda i: (0, i, 0)),
         ],
         compiler_params=pltpu.CompilerParams(vmem_limit_bytes=24 * 2**20),
+        cost_estimate=pl.CostEstimate(
+            flops=2 * tokens.size * (slots + 32), bytes_accessed=4 * tokens.size, transcendentals=2 * images * slots * count
+        ),
         name="slots",
     )(table, tokens, out_grad)
 
@@ -179,17 +182,23 @@
         ],
         out_specs=out_specs,
         compiler_params=pltpu.CompilerParams(vmem_limit_bytes=16 * 2**20),
+        cost_estimate=pl.CostEstimate(flops=2048 * big.size, bytes_accessed=2 * big.size, transcendentals=0),
         name="dispatch_grad" if over_tokens else "combine_grad",
     )(rows, big, weight)
 
 
-def lines_kernel(grads, table, out):
-    total, count = grads.shape
+def tokens_kernel(spread, pair, one, two, three, table, mine, theirs):
+    half, width = mine.shape
+    pieces = [ref[...].reshape(2 * ref.shape[1], ref.shape[2]) for ref in (pair, one, two, three)]
+    depth = pieces[0].shape[0]
+    count = pieces[0].shape[1] - width
+    grads = jnp.concatenate([piece[:, width:] for piece in pieces], axis=0)
+    total = grads.shape[0]
     near = total // 8
     c = lax.broadcasted_iota(jnp.int32, (total, near), 0)
     q = lax.broadcasted_iota(jnp.int32, (total, near), 1)
     fold = ((c // 64 == q // 8) & (c % 8 == q % 8)).astype(BF16)
-    x = nt(pick_rows(count), grads[...])
+    x = nt(pick_rows(count), grads)
     parts = []
     for side in range(2):
         y = jnp.concatenate([x[16 * side : 16 * side + 16]] * 8, axis=0)
@@ -197,45 +206,25 @@
         col = lax.broadcasted_iota(jnp.int32, y.shape, 1)
         y = jnp.where((col // 8) % 8 == row // 16, y, 0.0).astype(BF16)
         parts.append(jnp.dot(y, fold, preferred_element_type=F32).astype(BF16))
-    lines = jnp.concatenate(parts, axis=0)
-    out[...] = jnp.dot(lines, table[:near], preferred_element_type=F32)
-
-
-def lines_call(line, table):
+    sums = jnp.dot(jnp.concatenate(parts, axis=0), table[:near], preferred_element_type=F32)
+    side = spread[...].reshape(2 * half, spread.shape[2])
+    for x, piece in enumerate(pieces):
+        sums = sums + jnp.dot(side[:, x * depth : (x + 1) * depth], piece[:, :width], preferred_element_type=F32)
+    mine[...] = sums[:half]
+    theirs[...] = sums[half:]
+
+
+def tokens_call(spread, pieces, table):
     vmem = pl.BlockSpec(memory_space=pltpu.VMEM)
+    half, width = spread.shape[1], table.shape[1]
     return pl.pallas_call(
-        lines_kernel,
-        out_shape=jax.ShapeDtypeStruct((256, table.shape[1]), F32),
-        in_specs=[vmem] * 2,
-        out_specs=vmem,
-        compiler_params=pltpu.CompilerParams(vmem_limit_bytes=24 * 2**20),
-        name="through_logits",
-    )(line, table)
-
-
-def spread_kernel(spread, pair, one, two, three, base, mine, theirs):
-    half = mine.shape[0]
-    side = spread[...].reshape(2 * half, spread.shape[2])
-    depth = side.shape[1] // 4
-    total = base[...]
-    for x, piece in enumerate((pair, one, two, three)):
-        block = piece[...].reshape(depth, piece.shape[2])
-        total = total + jnp.dot(side[:, x * depth : (x + 1) * depth], block, preferred_element_type=F32)
-    mine[...] = total[:half]
-    theirs[...] = total[half:]
-
-
-def spread_call(spread, pieces, base):
-    vmem = pl.BlockSpec(memory_space=pltpu.VMEM)
-    half, width = base.shape[0] // 2, base.shape[1]
-    return pl.pallas_call(
-        spread_kernel,
+        tokens_kernel,
         out_shape=[jax.ShapeDtypeStruct((half, width), F32)] * 2,
         in_specs=[vmem] * 6,
         out_specs=[vmem] * 2,
         compiler_params=pltpu.CompilerParams(vmem_limit_bytes=24 * 2**20),
-        name="through_slots",
-    )(spread, *pieces, base)
+        name="token_grad",
+    )(spread, *pieces, table)
 
 
 def after(value, *earlier):
@@ -283,6 +272,11 @@
     return v
 
 
+def summed_three(v, axis, *steps):
+    one, two, three = together(*[swap(v, axis, k) for k in steps])
+    return (v + one) + (two + three)
+
+
 def per_device(tokens, out_grad, slot_params, w_in, w_out):
     images, count, width = tokens.shape
     own = slot_params.shape[1]
@@ -292,15 +286,15 @@
     l0, r0 = swap(units[0], "dp", 1), swap(units[0], "dp", 3)
     u1 = swap(units[1], "dp", 4)
     u2 = swap(units[2], "dp", 8)
-    table = doubled(slot_params.T, "expert", 2, 4)
-    l0, r0, table = together(l0, r0, table)
+    l0, r0, u1 = together(l0, r0, u1)
     p0, q0 = swap(r0[0], "dp", 1), swap(l0[1], "dp", 3)
-    table = doubled(table, "expert", 8, 1)
+    table = doubled(after(slot_params.T, u1), "expert", 2)
 
     u1, u2, p0, q0, table = together(u1, u2, p0, q0, table)
     both = jnp.stack([u1, u2], axis=1)
     lb, rb = swap(both, "dp", 1), swap(both, "dp", 3)
     u3 = swap(after(units[3], u1), "dp", 12)
+    table = doubled(table, "expert", 4, 8, 1)
     rows, dispatch, combine, spread = slots_call(table, tokens, out_grad)
     rows = rows.reshape(2 * half, width)
 
@@ -308,7 +302,7 @@
     z1, z2 = swap(rows, "dp", 4), swap(rows, "dp", 8)
     l3, r3 = swap(u3, "dp", 1), swap(u3, "dp", 3)
     pb, qb = swap(rb[0], "dp", 1), swap(lb[1], "dp", 3)
-    l3, r3, z2 = together(l3, r3, z2)
+    l3, r3, z1, z2 = together(l3, r3, z1, z2)
     p3, q3 = swap(r3[0], "dp", 1), swap(l3[1], "dp", 3)
     z3 = swap(z2, "dp", 4)
     pb, qb, p3, q3, z3 = together(pb, qb, p3, q3, z3)
@@ -319,26 +313,26 @@
     halves = ffn(rows_in, rows_go, blocks, half)
     slot_out = reduce_z(*halves[:4])
     slot_in_grad = reduce_z(*halves[4:])
-    near = slot_in_grad.astype(BF16)
-    far = swap(near, "expert", 2)
-
     part, mix = against(slot_out, out_grad, combine, False)
-    mix = summed(mix, "expert", 1, 2, 4, 8)
+    mix = summed_three(mix, "expert", 1, 2, 3)
+    mix = summed_three(after(mix, slot_in_grad), "expert", 4, 8, 12)
     (back,) = against(slot_in_grad, tokens, dispatch, True)
     logit_grad = back + (part - combine * jnp.repeat(mix, own, axis=0))
     logit_grad_b = logit_grad.astype(BF16)
-    slot_term = jnp.einsum(
+
+    near = jnp.concatenate([slot_in_grad.astype(BF16), logit_grad_b], axis=1)
+    far = swap(near, "expert", 2)
+    term = jnp.einsum(
         "bsm,bmd->sd", logit_grad_b.reshape(images, own, count), tokens, preferred_element_type=F32
     )
-    line = doubled(logit_grad_b, "expert", 2)
-    line = doubled(after(line, far), "expert", 4, 8)
-    base = lines_call(line, table)
-
+    term = summed(term, "dp", 4)
+    term, far = together(term, far)
     pieces = all_x(jnp.stack([near, far]))
-    slot_sum = summed(slot_term, "dp", 4, 8, 1)
-    slot_grad = summed(after(slot_sum, *pieces), "dp", 2).T
-
-    mine, theirs = spread_call(spread, pieces, after(base, slot_sum))
+    term = summed(term, "dp", 8, 1)
+    slot_grad = summed(after(term, *pieces), "dp", 2).T
+
+    pieces[1] = after(pieces[1], term)
+    mine, theirs = tokens_call(spread, pieces, table)
     token_grad = (mine + swap(theirs, "expert", 1)).astype(BF16)
     return (token_grad.reshape(images, -1, width), slot_grad)
 

time: 175 us -> 183 us (1.046); the launches traced: 175 us -> 180 us
  waiting for transfers between devices: 50 us -> 71.3 us
  starting transfers between devices: 98.1 us -> 82.2 us
    ppermute x44 -> x43, waiting for transfers between devices: 50 us -> 71.3 us  [swap(): return lax.ppermute(value, axis, [(i, i ^ k) for i in range(count)])]
    ppermute x44 -> x43, starting transfers between devices: 98.1 us -> 82.2 us  [swap(): return lax.ppermute(value, axis, [(i, i ^ k) for i in range(count)])]
  transfers between devices with their start and end apart: 44 -> 43, of which waited for: 21 -> 18; matrix products, arithmetic and copies ran while one was open for 1% -> 1% of each run, Pallas kernels for 8% -> 7%
where the time goes in v5:
time: 183 us; the launch traced here: 180 us
  starting transfers between devices  82.2 us (45%)
  waiting for transfers between devices  71.3 us (39%)
  Pallas kernels  18.9 us (10%)
  local copies, waits for them, and re-layouts  4.25 us (2%)
  other arithmetic  2.02 us (1%)
    ppermute x43, starting transfers between devices, swap(): return lax.ppermute(value, axis, [(i, i ^ k) for i in range(count)])  82.2 us
    ppermute x43, waiting for transfers between devices, swap(): return lax.ppermute(value, axis, [(i, i ^ k) for i in range(count)])  71.3 us
    pallas_call x1, Pallas kernels, slots_call(): pl.pallas_call(slots_kernel, grid=(images // 2,), out_shape=[jax.ShapeDty...  9.17 us
    pallas_call x2, Pallas kernels, against(): pl.pallas_call(lambda *refs: against_kernel(over_tokens, *refs), grid=(im...  4.36 us
    pallas_call x1, Pallas kernels, ffn(): pl.pallas_call(ffn_kernel, out_shape=[jax.ShapeDtypeStruct((own_rows, wid...  4.04 us
  transfers between devices with their start and end apart: 43, of which 18 were waited for; matrix products, arithmetic and copies ran while one was open for 1% of the time, Pallas kernels for 7%

profile of v5, /device:TPU:1, one launch (start us, length us, event | category | flops | bytes accessed | tf_op | source)
XLA Modules:
  0.0 180.4 jit_solution(12775262583590557396)
XLA Ops:
  0.7 1.4 dynamic-slice_bitcast_fusion.1
  2.3 3.7 %collective-permute-start.1 = (bf16[2,80,1280]{2,1,0:T(8,128)(2,1)S(1)}, bf16[2,80,1280]{2,1,0:T(8,128)(2,1)S(1)}, u32[]{:S(2)}, u32[]{:S(2)}) collective-permute-start(bf16[2,80,1280]{2,1,0:T(8,128)(2,1)S(1)} %pad_maximum_fusion.3.refs_0_), channel_id=1, source_target_pairs={{0,48},{16,32},{32,16},{48,0},{64,112},{80,96},{96,80},{112,64},{1... | collective-permute-start | bytes 1228808 | tf_op jit(solution)/shard_map/ppermute | solution.py:16
  6.0 1.7 collective-permute-start.2
  7.7 3.1 %collective-permute-start.3 = (bf16[2,80,1280]{2,1,0:T(8,128)(2,1)S(1)}, bf16[2,80,1280]{2,1,0:T(8,128)(2,1)S(1)}, u32[]{:S(2)}, u32[]{:S(2)}) collective-permute-start(bf16[2,80,1280]{2,1,0:T(8,128)(2,1)S(1)} %pad_maximum_fusion.5), channel_id=1, source_target_pairs={{0,128},{16,144},{32,160},{48,176},{64,192},{80,208},{96,224},{112... | collective-permute-start | bytes 1228808 | tf_op jit(solution)/shard_map/ppermute | solution.py:16
  10.8 13.9 %collective-permute-done.2 = bf16[2,80,1280]{2,1,0:T(8,128)(2,1)S(1)} collective-permute-done((bf16[2,80,1280]{2,1,0:T(8,128)(2,1)S(1)}, bf16[2,80,1280]{2,1,0:T(8,128)(2,1)S(1)}, u32[]{:S(2)}, u32[]{:S(2)}) %collective-permute-start.2) | collective-permute-done | bytes 409632 | tf_op jit(solution)/shard_map/ppermute | solution.py:16
  24.7 6.2 %collective-permute-start.6 = (bf16[8,1280]{1,0:T(8,128)(2,1)S(1)}, bf16[8,1280]{1,0:T(8,128)(2,1)S(1)}, u32[]{:S(2)}, u32[]{:S(2)}) collective-permute-start(bf16[8,1280]{1,0:T(8,128)(2,1)S(1)} %bitcast.69), channel_id=1, source_target_pairs={{0,2},{1,3},{2,0},{3,1},{4,6},{5,7},{6,4},{7,5},{8,10},{9,11},{10,... | collective-permute-start | bytes 61448 | tf_op jit(solution)/shard_map/ppermute | solution.py:16
  30.9 0.6 collective-permute-start.5
  31.5 0.9 collective-permute-start.4
  32.5 4.4 %collective-permute-done.5.refs_4_ = bf16[80,1280]{1,0:T(8,128)(2,1)S(1)} collective-permute-done((bf16[80,1280]{1,0:T(8,128)(2,1)S(1)}, bf16[80,1280]{1,0:T(8,128)(2,1)S(1)}, u32[]{:S(2)}, u32[]{:S(2)}) %collective-permute-start.5) | collective-permute-done | bytes 204832 | tf_op jit(solution)/shard_map/ppermute | solution.py:16
  36.8 1.2 collective-permute-start.7
  38.2 1.8 %collective-permute-start.11 = (bf16[2,2,80,1280]{3,2,1,0:T(8,128)(2,1)S(1)}, bf16[2,2,80,1280]{3,2,1,0:T(8,128)(2,1)S(1)}, u32[]{:S(2)}, u32[]{:S(2)}) collective-permute-start(bf16[2,2,80,1280]{3,2,1,0:T(8,128)(2,1)S(1)} %pad_maximum_fusion.refs_5_), channel_id=1, source_target_pairs={{0,48},{16,32},{32,16},{48,0},{64,112},{80,96},{96,80},{112,64},{1... | collective-permute-start | bytes 2457608 | tf_op jit(solution)/shard_map/ppermute | solution.py:16
  40.0 0.1 collective-permute-start.10
  40.1 1.6 collective-permute-start.12
  41.8 2.5 %collective-permute-start.8 = (bf16[32,1280]{1,0:T(8,128)(2,1)S(1)}, bf16[32,1280]{1,0:T(8,128)(2,1)S(1)}, u32[]{:S(2)}, u32[]{:S(2)}) collective-permute-start(bf16[32,1280]{1,0:T(8,128)(2,1)S(1)} %pad_maximum_fusion.10), channel_id=1, source_target_pairs={{0,8},{1,9},{2,10},{3,11},{4,12},{5,13},{6,14},{7,15},{8,0},{9,1},... | collective-permute-start | bytes 245768 | tf_op jit(solution)/shard_map/ppermute | solution.py:16
  44.3 2.6 %collective-permute-done.8 = bf16[32,1280]{1,0:T(8,128)(2,1)S(1)} collective-permute-done((bf16[32,1280]{1,0:T(8,128)(2,1)S(1)}, bf16[32,1280]{1,0:T(8,128)(2,1)S(1)}, u32[]{:S(2)}, u32[]{:S(2)}) %collective-permute-start.8) | collective-permute-done | bytes 81952 | tf_op jit(solution)/shard_map/ppermute | solution.py:16
  46.9 5.9 %collective-permute-start.9 = (bf16[64,1280]{1,0:T(8,128)(2,1)S(1)}, bf16[64,1280]{1,0:T(8,128)(2,1)S(1)}, u32[]{:S(2)}, u32[]{:S(2)}) collective-permute-start(bf16[64,1280]{1,0:T(8,128)(2,1)S(1)} %pad_maximum_fusion.9), channel_id=1, source_target_pairs={{0,1},{1,0},{2,3},{3,2},{4,5},{5,4},{6,7},{7,6},{8,9},{9,8},{10,11... | collective-permute-start | bytes 491528 | tf_op jit(solution)/shard_map/ppermute | solution.py:16
  52.8 1.0 collective-permute-done.9
  53.9 2.5 %copy-done.1 = bf16[8,256,1280]{2,1,0:T(8,128)(2,1)S(1)} copy-done((bf16[8,256,1280]{2,1,0:T(8,128)(2,1)S(1)}, bf16[8,256,1280]{2,1,0:T(8,128)(2,1)}, u32[]{:S(2)}) %copy-start.1) | copy-done | bytes 5242904
  56.3 9.2 %slots.1 = (bf16[2,64,1280]{2,1,0:T(8,128)(2,1)S(1)}, f32[64,256]{1,0:T(8,128)S(1)}, f32[64,256]{1,0:T(8,128)S(1)}, bf16[2,128,512]{2,1,0:T(8,128)(2,1)S(1)}) custom-call(bf16[128,1280]{1,0:T(8,128)(2,1)S(1)} %constant_dynamic-update-slice_fusion.table, bf16[8,256,1280]{2,1,0:T(8,128)(2,1)S(1)} %copy-done, bf16[8,256,1280]{2,1,0:T(8,128)(2,1)S(1)} %copy-done.1), custom_call_target="tpu_custom_call" | custom-call | flops 838860800 | bytes 10485760 | tf_op jit(solution)/shard_map/slots/pallas_call | solution.py:117
  65.7 1.9 %collective-permute-start.15 = (bf16[128,1280]{1,0:T(8,128)(2,1)S(1)}, bf16[128,1280]{1,0:T(8,128)(2,1)S(1)}, u32[]{:S(2)}, u32[]{:S(2)}) collective-permute-start(bf16[128,1280]{1,0:T(8,128)(2,1)S(1)} %bitcast.63), channel_id=1, source_target_pairs={{0,64},{16,80},{32,96},{48,112},{64,0},{80,16},{96,32},{112,48},{1... | collective-permute-start | bytes 983048 | tf_op jit(solution)/shard_map/ppermute | solution.py:16
  67.6 0.4 collective-permute-start.14
  68.0 1.1 collective-permute-start.13
  69.2 1.8 %collective-permute-start.18 = (bf16[2,80,1280]{2,1,0:T(8,128)(2,1)S(1)}, bf16[2,80,1280]{2,1,0:T(8,128)(2,1)S(1)}, u32[]{:S(2)}, u32[]{:S(2)}) collective-permute-start(bf16[2,80,1280]{2,1,0:T(8,128)(2,1)S(1)} %slice_bitcast_fusion), channel_id=1, source_target_pairs={{0,48},{16,32},{32,16},{48,0},{64,112},{80,96},{96,80},{112,64},{1... | collective-permute-start | bytes 1228808 | tf_op jit(solution)/shard_map/ppermute | solution.py:16
  71.0 11.5 %collective-permute-done.16 = bf16[128,1280]{1,0:T(8,128)(2,1)S(1)} collective-permute-done((bf16[128,1280]{1,0:T(8,128)(2,1)S(1)}, bf16[128,1280]{1,0:T(8,128)(2,1)S(1)}, u32[]{:S(2)}, u32[]{:S(2)}) %collective-permute-start.16) | collective-permute-done | bytes 327712 | tf_op jit(solution)/shard_map/ppermute | solution.py:16
  82.5 1.2 collective-permute-start.17
  83.8 1.0 collective-permute-start.20
  84.9 2.7 %collective-permute-done.18.refs_9_ = bf16[2,80,1280]{2,1,0:T(8,128)(2,1)S(1)} collective-permute-done((bf16[2,80,1280]{2,1,0:T(8,128)(2,1)S(1)}, bf16[2,80,1280]{2,1,0:T(8,128)(2,1)S(1)}, u32[]{:S(2)}, u32[]{:S(2)}) %collective-permute-start.18) | collective-permute-done | bytes 409632 | tf_op jit(solution)/shard_map/ppermute | solution.py:16
  87.6 5.4 %collective-permute-done.17.refs_8_ = bf16[2,80,1280]{2,1,0:T(8,128)(2,1)S(1)} collective-permute-done((bf16[2,80,1280]{2,1,0:T(8,128)(2,1)S(1)}, bf16[2,80,1280]{2,1,0:T(8,128)(2,1)S(1)}, u32[]{:S(2)}, u32[]{:S(2)}) %collective-permute-start.17) | collective-permute-done | bytes 409632 | tf_op jit(solution)/shard_map/ppermute | solution.py:16
  93.0 4.4 %collective-permute-done.19.refs_13_ = bf16[80,1280]{1,0:T(8,128)(2,1)S(1)} collective-permute-done((bf16[80,1280]{1,0:T(8,128)(2,1)S(1)}, bf16[80,1280]{1,0:T(8,128)(2,1)S(1)}, u32[]{:S(2)}, u32[]{:S(2)}) %collective-permute-start.19) | collective-permute-done | bytes 204832 | tf_op jit(solution)/shard_map/ppermute | solution.py:16
  97.6 4.0 %ffn.1 = (f32[64,1280]{1,0:T(8,128)S(1)}, bf16[64,1280]{1,0:T(8,128)(2,1)S(1)}, bf16[64,1280]{1,0:T(8,128)(2,1)S(1)}, bf16[64,1280]{1,0:T(8,128)(2,1)S(1)}, f32[...) custom-call(bf16[256,1280]{1,0:T(8,128)(2,1)S(1)} %pad_maximum_fusio, ...), custom_call_target="tpu_custom_call" | custom-call | tf_op jit(solution)/shard_map/ffn/pallas_call | solution.py:61
  101.7 1.9 %collective-permute-start.26 = (bf16[64,1280]{1,0:T(8,128)(2,1)S(1)}, bf16[64,1280]{1,0:T(8,128)(2,1)S(1)}, u32[]{:S(2)}, u32[]{:S(2)}) collective-permute-start(bf16[64,1280]{1,0:T(8,128)(2,1)S(1)} %get-tuple-element.96), channel_id=1, source_target_pairs={{0,128},{16,144},{32,160},{48,176},{64,192},{80,208},{96,224},{112... | collective-permute-start | bytes 491528 | tf_op jit(solution)/shard_map/ppermute | solution.py:16
  103.6 1.6 collective-permute-start.27
  105.2 1.9 %collective-permute-start.23 = (bf16[64,1280]{1,0:T(8,128)(2,1)S(1)}, bf16[64,1280]{1,0:T(8,128)(2,1)S(1)}, u32[]{:S(2)}, u32[]{:S(2)}) collective-permute-start(bf16[64,1280]{1,0:T(8,128)(2,1)S(1)} %get-tuple-element.88), channel_id=1, source_target_pairs={{0,128},{16,144},{32,160},{48,176},{64,192},{80,208},{96,224},{112... | collective-permute-start | bytes 491528 | tf_op jit(solution)/shard_map/ppermute | solution.py:16
  107.2 1.7 collective-permute-done.25
  108.9 1.6 collective-permute-start.24
  110.5 3.0 %collective-permute-done.27 = bf16[64,1280]{1,0:T(8,128)(2,1)S(1)} collective-permute-done((bf16[64,1280]{1,0:T(8,128)(2,1)S(1)}, bf16[64,1280]{1,0:T(8,128)(2,1)S(1)}, u32[]{:S(2)}, u32[]{:S(2)}) %collective-permute-start.27) | collective-permute-done | bytes 163872 | tf_op jit(solution)/shard_map/ppermute | solution.py:16
  113.6 2.1 %combine_grad.1 = (f32[64,256]{1,0:T(8,128)S(1)}, f32[8,256]{1,0:T(8,128)S(1)}) custom-call(f32[64,1280]{1,0:T(8,128)S(1)} %add_add_fusion.refs_0_, bf16[8,256,1280]{2,1,0:T(8,128)(2,1)S(1)} %bitcast.61, f32[64,256]{1,0:T(8,128)S(1)} %get-tuple-element.101.refs_2_), custom_call_target="tpu_custom_call" | custom-call | flops 5368709120 | bytes 5242880 | tf_op jit(solution)/shard_map/combine_grad/pallas_call | solution.py:174
  115.7 4.4 %collective-permute-start.30 = (f32[8,256]{1,0:T(8,128)S(1)}, f32[8,256]{1,0:T(8,128)S(1)}, u32[]{:S(2)}, u32[]{:S(2)}) collective-permute-start(f32[8,256]{1,0:T(8,128)S(1)} %get-tuple-element.103), channel_id=1, source_target_pairs={{0,3},{1,2},{2,1},{3,0},{4,7},{5,6},{6,5},{7,4},{8,11},{9,10},{10,... | collective-permute-start | bytes 24584 | tf_op jit(solution)/shard_map/ppermute | solution.py:16
  120.2 5.6 %collective-permute-start.29 = (f32[8,256]{1,0:T(8,128)S(1)}, f32[8,256]{1,0:T(8,128)S(1)}, u32[]{:S(2)}, u32[]{:S(2)}) collective-permute-start(f32[8,256]{1,0:T(8,128)S(1)} %get-tuple-element.103), channel_id=1, source_target_pairs={{0,2},{1,3},{2,0},{3,1},{4,6},{5,7},{6,4},{7,5},{8,10},{9,11},{10,... | collective-permute-start | bytes 24584 | tf_op jit(solution)/shard_map/ppermute | solution.py:16
  125.8 3.1 %collective-permute-done.23 = bf16[64,1280]{1,0:T(8,128)(2,1)S(1)} collective-permute-done((bf16[64,1280]{1,0:T(8,128)(2,1)S(1)}, bf16[64,1280]{1,0:T(8,128)(2,1)S(1)}, u32[]{:S(2)}, u32[]{:S(2)}) %collective-permute-start.23) | collective-permute-done | bytes 163872 | tf_op jit(solution)/shard_map/ppermute | solution.py:16
  129.0 1.9 %collective-permute-start.33 = (f32[8,256]{1,0:T(8,128)S(1)}, f32[8,256]{1,0:T(8,128)S(1)}, u32[]{:S(2)}, u32[]{:S(2)}) collective-permute-start(f32[8,256]{1,0:T(8,128)S(1)} %add_add_fusion.3), channel_id=1, source_target_pairs={{0,12},{1,13},{2,14},{3,15},{4,8},{5,9},{6,10},{7,11},{8,4},{9,5},... | collective-permute-start | bytes 24584 | tf_op jit(solution)/shard_map/ppermute | solution.py:16
  130.9 0.8 collective-permute-start.32
  131.7 0.7 collective-permute-start.31
  132.4 2.3 %dispatch_grad.1 = f32[64,256]{1,0:T(8,128)S(1)} custom-call(f32[64,1280]{1,0:T(8,128)S(1)} %get-tuple-element.121.refs_0_, bf16[8,256,1280]{2,1,0:T(8,128)(2,1)S(1)} %copy-done, f32[64,256]{1,0:T(8,128)S(1)} %get-tuple-element.93.refs_2_), custom_call_target="tpu_custom_call" | custom-call | flops 5368709120 | bytes 5242880 | tf_op jit(solution)/shard_map/dispatch_grad/pallas_call | solution.py:174
  134.6 0.3 collective-permute-done.32
  135.0 3.4 %collective-permute-start.35 = (bf16[64,1536]{1,0:T(8,128)(2,1)S(1)}, bf16[64,1536]{1,0:T(8,128)(2,1)S(1)}, u32[]{:S(2)}, u32[]{:S(2)}) collective-permute-start(bf16[64,1536]{1,0:T(8,128)(2,1)S(1)} %get-tuple-element.139), channel_id=1, source_target_pairs={{0,2},{1,3},{2,0},{3,1},{4,6},{5,7},{6,4},{7,5},{8,10},{9,11},{10,... | collective-permute-start | bytes 589832 | tf_op jit(solution)/shard_map/ppermute | solution.py:16
  138.4 0.8 convolution_bitcast_fusion
  139.2 10.5 %collective-permute-start.34 = (f32[8,1280]{1,0:T(8,128)S(1)}, f32[8,1280]{1,0:T(8,128)S(1)}, u32[]{:S(2)}, u32[]{:S(2)}) collective-permute-start(f32[8,1280]{1,0:T(8,128)S(1)} %convolution_bitcast_fusion), channel_id=1, source_target_pairs={{0,64},{16,80},{32,96},{48,112},{64,0},{80,16},{96,32},{112,48},{1... | collective-permute-start | bytes 122888 | tf_op jit(solution)/shard_map/ppermute | solution.py:16
  149.8 2.9 %collective-permute-done.34 = f32[8,1280]{1,0:T(8,128)S(1)} collective-permute-done((f32[8,1280]{1,0:T(8,128)S(1)}, f32[8,1280]{1,0:T(8,128)S(1)}, u32[]{:S(2)}, u32[]{:S(2)}) %collective-permute-start.34) | collective-permute-done | bytes 40992 | tf_op jit(solution)/shard_map/ppermute | solution.py:16
  152.7 1.6 collective-permute-start.38
  154.2 1.0 collective-permute-start.37
  155.3 0.7 collective-permute-start.36
  156.0 3.2 %collective-permute-start.39 = (f32[8,1280]{1,0:T(8,128)S(1)}, f32[8,1280]{1,0:T(8,128)S(1)}, u32[]{:S(2)}, u32[]{:S(2)}) collective-permute-start(f32[8,1280]{1,0:T(8,128)S(1)} %add.88), channel_id=1, source_target_pairs={{0,128},{16,144},{32,160},{48,176},{64,192},{80,208},{96,224},{112... | collective-permute-start | bytes 122888 | tf_op jit(solution)/shard_map/ppermute | solution.py:16
  159.2 1.7 collective-permute-done.39
  160.9 1.2 collective-permute-start.40
  162.1 1.9 %collective-permute-done.40 = f32[8,1280]{1,0:T(8,128)S(1)} collective-permute-done((f32[8,1280]{1,0:T(8,128)S(1)}, f32[8,1280]{1,0:T(8,128)S(1)}, u32[]{:S(2)}, u32[]{:S(2)}) %collective-permute-start.40) | collective-permute-done | bytes 40992 | tf_op jit(solution)/shard_map/ppermute | solution.py:16
  164.0 8.2 %collective-permute-done.38.three = bf16[2,64,1536]{2,1,0:T(8,128)(2,1)S(1)} collective-permute-done((bf16[2,64,1536]{2,1,0:T(8,128)(2,1)S(1)}, bf16[2,64,1536]{2,1,0:T(8,128)(2,1)S(1)}, u32[]{:S(2)}, u32[]{:S(2)}) %collective-permute-start.38) | collective-permute-done | bytes 393248 | tf_op jit(solution)/shard_map/ppermute | solution.py:16
  172.3 0.9 collective-permute-done.36.one
  173.2 1.3 token_grad.1
  174.5 0.1 collective-permute-start.41
  174.6 2.8 %collective-permute-start.42 = (f32[8,1280]{1,0:T(8,128)S(1)}, f32[8,1280]{1,0:T(8,128)S(1)}, u32[]{:S(2)}, u32[]{:S(2)}) collective-permute-start(f32[8,1280]{1,0:T(8,128)S(1)} %add.90), channel_id=1, source_target_pairs={{0,32},{16,48},{32,0},{48,16},{64,96},{80,112},{96,64},{112,80},{1... | collective-permute-start | bytes 122888 | tf_op jit(solution)/shard_map/ppermute | solution.py:16
  177.4 1.6 collective-permute-done.42
  179.0 0.6 add_bitcast_fusion
  179.6 0.8 add_convert_fusion
  (78 shorter events, 1.3 us)
Async XLA Ops:
  0.6 1.5 copy-start.2
  2.3 22.5 %copy-start.3 = (bf16[1280,8]{0,1:T(8,128)(2,1)S(1)}, bf16[1280,8]{0,1:T(8,128)(2,1)}, u32[]{:S(2)}) copy-start(bf16[1280,8]{0,1:T(8,128)(2,1)} %param.7) | copy-start | bytes 61444
  2.3 22.4 %collective-permute-start.1 = (bf16[2,80,1280]{2,1,0:T(8,128)(2,1)S(1)}, bf16[2,80,1280]{2,1,0:T(8,128)(2,1)S(1)}, u32[]{:S(2)}, u32[]{:S(2)}) collective-permute-start(bf16[2,80,1280]{2,1,0:T(8,128)(2,1)S(1)} %pad_maximum_fusion.3.refs_0_), channel_id=1, source_target_pairs={{0,48},{16,32},{32,16},{48,0},{64,112},{80,96},{96,80},{112,64},{1... | collective-permute-start | bytes 1228808 | tf_op jit(solution)/shard_map/ppermute | solution.py:16
  5.9 18.8 %collective-permute-start = (bf16[2,80,1280]{2,1,0:T(8,128)(2,1)S(1)}, bf16[2,80,1280]{2,1,0:T(8,128)(2,1)S(1)}, u32[]{:S(2)}, u32[]{:S(2)}) collective-permute-start(bf16[2,80,1280]{2,1,0:T(8,128)(2,1)S(1)} %pad_maximum_fusion.3.refs_0_), channel_id=1, source_target_pairs={{0,16},{16,0},{32,48},{48,32},{64,80},{80,64},{96,112},{112,96},{1... | collective-permute-start | bytes 1228808 | tf_op jit(solution)/shard_map/ppermute | solution.py:16
  6.0 18.7 %collective-permute-start.2 = (bf16[2,80,1280]{2,1,0:T(8,128)(2,1)S(1)}, bf16[2,80,1280]{2,1,0:T(8,128)(2,1)S(1)}, u32[]{:S(2)}, u32[]{:S(2)}) collective-permute-start(bf16[2,80,1280]{2,1,0:T(8,128)(2,1)S(1)} %pad_maximum_fusion.4), channel_id=1, source_target_pairs={{0,64},{16,80},{32,96},{48,112},{64,0},{80,16},{96,32},{112,48},{1... | collective-permute-start | bytes 1228808 | tf_op jit(solution)/shard_map/ppermute | solution.py:16
  7.7 46.2 %copy-start = (bf16[8,256,1280]{2,1,0:T(8,128)(2,1)S(1)}, bf16[8,256,1280]{2,1,0:T(8,128)(2,1)}, u32[]{:S(2)}) copy-start(bf16[8,256,1280]{2,1,0:T(8,128)(2,1)} %refs_1_.2) | copy-start | bytes 15728644
  7.7 24.7 %collective-permute-start.3 = (bf16[2,80,1280]{2,1,0:T(8,128)(2,1)S(1)}, bf16[2,80,1280]{2,1,0:T(8,128)(2,1)S(1)}, u32[]{:S(2)}, u32[]{:S(2)}) collective-permute-start(bf16[2,80,1280]{2,1,0:T(8,128)(2,1)S(1)} %pad_maximum_fusion.5), channel_id=1, source_target_pairs={{0,128},{16,144},{32,160},{48,176},{64,192},{80,208},{96,224},{112... | collective-permute-start | bytes 1228808 | tf_op jit(solution)/shard_map/ppermute | solution.py:16
  24.7 7.7 %collective-permute-start.6 = (bf16[8,1280]{1,0:T(8,128)(2,1)S(1)}, bf16[8,1280]{1,0:T(8,128)(2,1)S(1)}, u32[]{:S(2)}, u32[]{:S(2)}) collective-permute-start(bf16[8,1280]{1,0:T(8,128)(2,1)S(1)} %bitcast.69), channel_id=1, source_target_pairs={{0,2},{1,3},{2,0},{3,1},{4,6},{5,7},{6,4},{7,5},{8,10},{9,11},{10,... | collective-permute-start | bytes 61448 | tf_op jit(solution)/shard_map/ppermute | solution.py:16
  30.9 5.9 %collective-permute-start.5 = (bf16[80,1280]{1,0:T(8,128)(2,1)S(1)}, bf16[80,1280]{1,0:T(8,128)(2,1)S(1)}, u32[]{:S(2)}, u32[]{:S(2)}) collective-permute-start(bf16[80,1280]{1,0:T(8,128)(2,1)S(1)} %slice_bitcast_fusion.4), channel_id=1, source_target_pairs={{0,48},{16,32},{32,16},{48,0},{64,112},{80,96},{96,80},{112,64},{1... | collective-permute-start | bytes 614408 | tf_op jit(solution)/shard_map/ppermute | solution.py:16
  31.5 5.3 %collective-permute-start.4 = (bf16[80,1280]{1,0:T(8,128)(2,1)S(1)}, bf16[80,1280]{1,0:T(8,128)(2,1)S(1)}, u32[]{:S(2)}, u32[]{:S(2)}) collective-permute-start(bf16[80,1280]{1,0:T(8,128)(2,1)S(1)} %slice_bitcast_fusion.5), channel_id=1, source_target_pairs={{0,16},{16,0},{32,48},{48,32},{64,80},{80,64},{96,112},{112,96},{1... | collective-permute-start | bytes 614408 | tf_op jit(solution)/shard_map/ppermute | solution.py:16
  36.8 4.9 %collective-permute-start.7 = (bf16[16,1280]{1,0:T(8,128)(2,1)S(1)}, bf16[16,1280]{1,0:T(8,128)(2,1)S(1)}, u32[]{:S(2)}, u32[]{:S(2)}) collective-permute-start(bf16[16,1280]{1,0:T(8,128)(2,1)S(1)} %pad_maximum_fusion.11), channel_id=1, source_target_pairs={{0,4},{1,5},{2,6},{3,7},{4,0},{5,1},{6,2},{7,3},{8,12},{9,13},{10,... | collective-permute-start | bytes 122888 | tf_op jit(solution)/shard_map/ppermute | solution.py:16
  38.2 27.4 %collective-permute-start.11 = (bf16[2,2,80,1280]{3,2,1,0:T(8,128)(2,1)S(1)}, bf16[2,2,80,1280]{3,2,1,0:T(8,128)(2,1)S(1)}, u32[]{:S(2)}, u32[]{:S(2)}) collective-permute-start(bf16[2,2,80,1280]{3,2,1,0:T(8,128)(2,1)S(1)} %pad_maximum_fusion.refs_5_), channel_id=1, source_target_pairs={{0,48},{16,32},{32,16},{48,0},{64,112},{80,96},{96,80},{112,64},{1... | collective-permute-start | bytes 2457608 | tf_op jit(solution)/shard_map/ppermute | solution.py:16
  40.0 25.6 %collective-permute-start.10 = (bf16[2,2,80,1280]{3,2,1,0:T(8,128)(2,1)S(1)}, bf16[2,2,80,1280]{3,2,1,0:T(8,128)(2,1)S(1)}, u32[]{:S(2)}, u32[]{:S(2)}) collective-permute-start(bf16[2,2,80,1280]{3,2,1,0:T(8,128)(2,1)S(1)} %pad_maximum_fusion.refs_5_), channel_id=1, source_target_pairs={{0,16},{16,0},{32,48},{48,32},{64,80},{80,64},{96,112},{112,96},{1... | collective-permute-start | bytes 2457608 | tf_op jit(solution)/shard_map/ppermute | solution.py:16
  40.1 25.4 %collective-permute-start.12 = (bf16[2,80,1280]{2,1,0:T(8,128)(2,1)S(1)}, bf16[2,80,1280]{2,1,0:T(8,128)(2,1)S(1)}, u32[]{:S(2)}, u32[]{:S(2)}) collective-permute-start(bf16[2,80,1280]{2,1,0:T(8,128)(2,1)S(1)} %pad_maximum_fusion.6), channel_id=1, source_target_pairs={{0,192},{16,208},{32,224},{48,240},{64,128},{80,144},{96,160},{112... | collective-permute-start | bytes 1228808 | tf_op jit(solution)/shard_map/ppermute | solution.py:16
  41.8 5.1 %collective-permute-start.8 = (bf16[32,1280]{1,0:T(8,128)(2,1)S(1)}, bf16[32,1280]{1,0:T(8,128)(2,1)S(1)}, u32[]{:S(2)}, u32[]{:S(2)}) collective-permute-start(bf16[32,1280]{1,0:T(8,128)(2,1)S(1)} %pad_maximum_fusion.10), channel_id=1, source_target_pairs={{0,8},{1,9},{2,10},{3,11},{4,12},{5,13},{6,14},{7,15},{8,0},{9,1},... | collective-permute-start | bytes 245768 | tf_op jit(solution)/shard_map/ppermute | solution.py:16
  46.9 6.9 %collective-permute-start.9 = (bf16[64,1280]{1,0:T(8,128)(2,1)S(1)}, bf16[64,1280]{1,0:T(8,128)(2,1)S(1)}, u32[]{:S(2)}, u32[]{:S(2)}) collective-permute-start(bf16[64,1280]{1,0:T(8,128)(2,1)S(1)} %pad_maximum_fusion.9), channel_id=1, source_target_pairs={{0,1},{1,0},{2,3},{3,2},{4,5},{5,4},{6,7},{7,6},{8,9},{9,8},{10,11... | collective-permute-start | bytes 491528 | tf_op jit(solution)/shard_map/ppermute | solution.py:16
  53.9 2.5 %copy-start.1 = (bf16[8,256,1280]{2,1,0:T(8,128)(2,1)S(1)}, bf16[8,256,1280]{2,1,0:T(8,128)(2,1)}, u32[]{:S(2)}) copy-start(bf16[8,256,1280]{2,1,0:T(8,128)(2,1)} %refs_1_.3) | copy-start | bytes 15728644
  65.6 17.0 %collective-permute-start.16 = (bf16[128,1280]{1,0:T(8,128)(2,1)S(1)}, bf16[128,1280]{1,0:T(8,128)(2,1)S(1)}, u32[]{:S(2)}, u32[]{:S(2)}) collective-permute-start(bf16[128,1280]{1,0:T(8,128)(2,1)S(1)} %bitcast.62), channel_id=1, source_target_pairs={{0,128},{16,144},{32,160},{48,176},{64,192},{80,208},{96,224},{112... | collective-permute-start | bytes 983048 | tf_op jit(solution)/shard_map/ppermute | solution.py:16
  65.7 18.1 %collective-permute-start.15 = (bf16[128,1280]{1,0:T(8,128)(2,1)S(1)}, bf16[128,1280]{1,0:T(8,128)(2,1)S(1)}, u32[]{:S(2)}, u32[]{:S(2)}) collective-permute-start(bf16[128,1280]{1,0:T(8,128)(2,1)S(1)} %bitcast.63), channel_id=1, source_target_pairs={{0,64},{16,80},{32,96},{48,112},{64,0},{80,16},{96,32},{112,48},{1... | collective-permute-start | bytes 983048 | tf_op jit(solution)/shard_map/ppermute | solution.py:16
  67.6 16.2 %collective-permute-start.14 = (bf16[2,80,1280]{2,1,0:T(8,128)(2,1)S(1)}, bf16[2,80,1280]{2,1,0:T(8,128)(2,1)S(1)}, u32[]{:S(2)}, u32[]{:S(2)}) collective-permute-start(bf16[2,80,1280]{2,1,0:T(8,128)(2,1)S(1)} %collective-permute-done.12.refs_10_), channel_id=1, source_target_pairs={{0,48},{16,32},{32,16},{48,0},{64,112},{80,96},{96,80},{112,64},{1... | collective-permute-start | bytes 1228808 | tf_op jit(solution)/shard_map/ppermute | solution.py:16
  68.0 15.8 %collective-permute-start.13 = (bf16[2,80,1280]{2,1,0:T(8,128)(2,1)S(1)}, bf16[2,80,1280]{2,1,0:T(8,128)(2,1)S(1)}, u32[]{:S(2)}, u32[]{:S(2)}) collective-permute-start(bf16[2,80,1280]{2,1,0:T(8,128)(2,1)S(1)} %collective-permute-done.12.refs_10_), channel_id=1, source_target_pairs={{0,16},{16,0},{32,48},{48,32},{64,80},{80,64},{96,112},{112,96},{1... | collective-permute-start | bytes 1228808 | tf_op jit(solution)/shard_map/ppermute | solution.py:16
  69.2 18.4 %collective-permute-start.18 = (bf16[2,80,1280]{2,1,0:T(8,128)(2,1)S(1)}, bf16[2,80,1280]{2,1,0:T(8,128)(2,1)S(1)}, u32[]{:S(2)}, u32[]{:S(2)}) collective-permute-start(bf16[2,80,1280]{2,1,0:T(8,128)(2,1)S(1)} %slice_bitcast_fusion), channel_id=1, source_target_pairs={{0,48},{16,32},{32,16},{48,0},{64,112},{80,96},{96,80},{112,64},{1... | collective-permute-start | bytes 1228808 | tf_op jit(solution)/shard_map/ppermute | solution.py:16
  82.5 10.5 %collective-permute-start.17 = (bf16[2,80,1280]{2,1,0:T(8,128)(2,1)S(1)}, bf16[2,80,1280]{2,1,0:T(8,128)(2,1)S(1)}, u32[]{:S(2)}, u32[]{:S(2)}) collective-permute-start(bf16[2,80,1280]{2,1,0:T(8,128)(2,1)S(1)} %slice_bitcast_fusion.1), channel_id=1, source_target_pairs={{0,16},{16,0},{32,48},{48,32},{64,80},{80,64},{96,112},{112,96},{1... | collective-permute-start | bytes 1228808 | tf_op jit(solution)/shard_map/ppermute | solution.py:16
  83.8 9.2 %collective-permute-start.20 = (bf16[80,1280]{1,0:T(8,128)(2,1)S(1)}, bf16[80,1280]{1,0:T(8,128)(2,1)S(1)}, u32[]{:S(2)}, u32[]{:S(2)}) collective-permute-start(bf16[80,1280]{1,0:T(8,128)(2,1)S(1)} %slice_bitcast_fusion.2), channel_id=1, source_target_pairs={{0,48},{16,32},{32,16},{48,0},{64,112},{80,96},{96,80},{112,64},{1... | collective-permute-start | bytes 614408 | tf_op jit(solution)/shard_map/ppermute | solution.py:16
  84.8 12.6 %collective-permute-start.19 = (bf16[80,1280]{1,0:T(8,128)(2,1)S(1)}, bf16[80,1280]{1,0:T(8,128)(2,1)S(1)}, u32[]{:S(2)}, u32[]{:S(2)}) collective-permute-start(bf16[80,1280]{1,0:T(8,128)(2,1)S(1)} %slice_bitcast_fusion.3), channel_id=1, source_target_pairs={{0,16},{16,0},{32,48},{48,32},{64,80},{80,64},{96,112},{112,96},{1... | collective-permute-start | bytes 614408 | tf_op jit(solution)/shard_map/ppermute | solution.py:16
  84.8 12.6 %collective-permute-start.21 = (bf16[128,1280]{1,0:T(8,128)(2,1)S(1)}, bf16[128,1280]{1,0:T(8,128)(2,1)S(1)}, u32[]{:S(2)}, u32[]{:S(2)}) collective-permute-start(bf16[128,1280]{1,0:T(8,128)(2,1)S(1)} %collective-permute-done.16), channel_id=1, source_target_pairs={{0,64},{16,80},{32,96},{48,112},{64,0},{80,16},{96,32},{112,48},{1... | collective-permute-start | bytes 983048 | tf_op jit(solution)/shard_map/ppermute | solution.py:16
  97.5 16.1 %slice-start = ((s8[5242880]{0:T(1024)(128)(4,1)}), s8[4194304]{0:T(1024)(128)(4,1)S(1)}, s32[]{:S(2)}) async-start(s8[5242880]{0:T(1024)(128)(4,1)} %bitcast.60), calls=%async_computation | async-start | bytes 8388608
  97.6 16.1 %slice-start.1 = ((s8[5242880]{0:T(1024)(128)(4,1)}), s8[1048576]{0:T(1024)(128)(4,1)S(1)}, s32[]{:S(2)}) async-start(s8[5242880]{0:T(1024)(128)(4,1)} %bitcast.60), calls=%async_computation.1 | async-start | bytes 2097152
  101.6 7.3 %collective-permute-start.25 = (bf16[64,1280]{1,0:T(8,128)(2,1)S(1)}, bf16[64,1280]{1,0:T(8,128)(2,1)S(1)}, u32[]{:S(2)}, u32[]{:S(2)}) collective-permute-start(bf16[64,1280]{1,0:T(8,128)(2,1)S(1)} %get-tuple-element.95), channel_id=1, source_target_pairs={{0,64},{16,80},{32,96},{48,112},{64,0},{80,16},{96,32},{112,48},{1... | collective-permute-start | bytes 491528 | tf_op jit(solution)/shard_map/ppermute | solution.py:16
  101.7 8.8 %collective-permute-start.26 = (bf16[64,1280]{1,0:T(8,128)(2,1)S(1)}, bf16[64,1280]{1,0:T(8,128)(2,1)S(1)}, u32[]{:S(2)}, u32[]{:S(2)}) collective-permute-start(bf16[64,1280]{1,0:T(8,128)(2,1)S(1)} %get-tuple-element.96), channel_id=1, source_target_pairs={{0,128},{16,144},{32,160},{48,176},{64,192},{80,208},{96,224},{112... | collective-permute-start | bytes 491528 | tf_op jit(solution)/shard_map/ppermute | solution.py:16
  103.6 9.9 %collective-permute-start.27 = (bf16[64,1280]{1,0:T(8,128)(2,1)S(1)}, bf16[64,1280]{1,0:T(8,128)(2,1)S(1)}, u32[]{:S(2)}, u32[]{:S(2)}) collective-permute-start(bf16[64,1280]{1,0:T(8,128)(2,1)S(1)} %get-tuple-element.97), channel_id=1, source_target_pairs={{0,192},{16,208},{32,224},{48,240},{64,128},{80,144},{96,160},{112... | collective-permute-start | bytes 491528 | tf_op jit(solution)/shard_map/ppermute | solution.py:16
  105.2 20.6 %collective-permute-start.22 = (bf16[64,1280]{1,0:T(8,128)(2,1)S(1)}, bf16[64,1280]{1,0:T(8,128)(2,1)S(1)}, u32[]{:S(2)}, u32[]{:S(2)}) collective-permute-start(bf16[64,1280]{1,0:T(8,128)(2,1)S(1)} %get-tuple-element.87), channel_id=1, source_target_pairs={{0,64},{16,80},{32,96},{48,112},{64,0},{80,16},{96,32},{112,48},{1... | collective-permute-start | bytes 491528 | tf_op jit(solution)/shard_map/ppermute | solution.py:16
  105.2 23.6 %collective-permute-start.23 = (bf16[64,1280]{1,0:T(8,128)(2,1)S(1)}, bf16[64,1280]{1,0:T(8,128)(2,1)S(1)}, u32[]{:S(2)}, u32[]{:S(2)}) collective-permute-start(bf16[64,1280]{1,0:T(8,128)(2,1)S(1)} %get-tuple-element.88), channel_id=1, source_target_pairs={{0,128},{16,144},{32,160},{48,176},{64,192},{80,208},{96,224},{112... | collective-permute-start | bytes 491528 | tf_op jit(solution)/shard_map/ppermute | solution.py:16
  108.9 20.0 %collective-permute-start.24 = (bf16[64,1280]{1,0:T(8,128)(2,1)S(1)}, bf16[64,1280]{1,0:T(8,128)(2,1)S(1)}, u32[]{:S(2)}, u32[]{:S(2)}) collective-permute-start(bf16[64,1280]{1,0:T(8,128)(2,1)S(1)} %get-tuple-element.89), channel_id=1, source_target_pairs={{0,192},{16,208},{32,224},{48,240},{64,128},{80,144},{96,160},{112... | collective-permute-start | bytes 491528 | tf_op jit(solution)/shard_map/ppermute | solution.py:16
  115.7 13.2 %collective-permute-start.30 = (f32[8,256]{1,0:T(8,128)S(1)}, f32[8,256]{1,0:T(8,128)S(1)}, u32[]{:S(2)}, u32[]{:S(2)}) collective-permute-start(f32[8,256]{1,0:T(8,128)S(1)} %get-tuple-element.103), channel_id=1, source_target_pairs={{0,3},{1,2},{2,1},{3,0},{4,7},{5,6},{6,5},{7,4},{8,11},{9,10},{10,... | collective-permute-start | bytes 24584 | tf_op jit(solution)/shard_map/ppermute | solution.py:16
  120.2 8.8 %collective-permute-start.29 = (f32[8,256]{1,0:T(8,128)S(1)}, f32[8,256]{1,0:T(8,128)S(1)}, u32[]{:S(2)}, u32[]{:S(2)}) collective-permute-start(f32[8,256]{1,0:T(8,128)S(1)} %get-tuple-element.103), channel_id=1, source_target_pairs={{0,2},{1,3},{2,0},{3,1},{4,6},{5,7},{6,4},{7,5},{8,10},{9,11},{10,... | collective-permute-start | bytes 24584 | tf_op jit(solution)/shard_map/ppermute | solution.py:16
  125.8 3.2 %collective-permute-start.28 = (f32[8,256]{1,0:T(8,128)S(1)}, f32[8,256]{1,0:T(8,128)S(1)}, u32[]{:S(2)}, u32[]{:S(2)}) collective-permute-start(f32[8,256]{1,0:T(8,128)S(1)} %get-tuple-element.103), channel_id=1, source_target_pairs={{0,1},{1,0},{2,3},{3,2},{4,5},{5,4},{6,7},{7,6},{8,9},{9,8},{10,11... | collective-permute-start | bytes 24584 | tf_op jit(solution)/shard_map/ppermute | solution.py:16
  129.0 5.6 %collective-permute-start.33 = (f32[8,256]{1,0:T(8,128)S(1)}, f32[8,256]{1,0:T(8,128)S(1)}, u32[]{:S(2)}, u32[]{:S(2)}) collective-permute-start(f32[8,256]{1,0:T(8,128)S(1)} %add_add_fusion.3), channel_id=1, source_target_pairs={{0,12},{1,13},{2,14},{3,15},{4,8},{5,9},{6,10},{7,11},{8,4},{9,5},... | collective-permute-start | bytes 24584 | tf_op jit(solution)/shard_map/ppermute | solution.py:16
  130.9 4.0 %collective-permute-start.32 = (f32[8,256]{1,0:T(8,128)S(1)}, f32[8,256]{1,0:T(8,128)S(1)}, u32[]{:S(2)}, u32[]{:S(2)}) collective-permute-start(f32[8,256]{1,0:T(8,128)S(1)} %add_add_fusion.3), channel_id=1, source_target_pairs={{0,8},{1,9},{2,10},{3,11},{4,12},{5,13},{6,14},{7,15},{8,0},{9,1},... | collective-permute-start | bytes 24584 | tf_op jit(solution)/shard_map/ppermute | solution.py:16
  131.7 3.2 %collective-permute-start.31 = (f32[8,256]{1,0:T(8,128)S(1)}, f32[8,256]{1,0:T(8,128)S(1)}, u32[]{:S(2)}, u32[]{:S(2)}) collective-permute-start(f32[8,256]{1,0:T(8,128)S(1)} %add_add_fusion.3), channel_id=1, source_target_pairs={{0,4},{1,5},{2,6},{3,7},{4,0},{5,1},{6,2},{7,3},{8,12},{9,13},{10,... | collective-permute-start | bytes 24584 | tf_op jit(solution)/shard_map/ppermute | solution.py:16
  135.0 17.6 %collective-permute-start.35 = (bf16[64,1536]{1,0:T(8,128)(2,1)S(1)}, bf16[64,1536]{1,0:T(8,128)(2,1)S(1)}, u32[]{:S(2)}, u32[]{:S(2)}) collective-permute-start(bf16[64,1536]{1,0:T(8,128)(2,1)S(1)} %get-tuple-element.139), channel_id=1, source_target_pairs={{0,2},{1,3},{2,0},{3,1},{4,6},{5,7},{6,4},{7,5},{8,10},{9,11},{10,... | collective-permute-start | bytes 589832 | tf_op jit(solution)/shard_map/ppermute | solution.py:16
  139.2 13.4 %collective-permute-start.34 = (f32[8,1280]{1,0:T(8,128)S(1)}, f32[8,1280]{1,0:T(8,128)S(1)}, u32[]{:S(2)}, u32[]{:S(2)}) collective-permute-start(f32[8,1280]{1,0:T(8,128)S(1)} %convolution_bitcast_fusion), channel_id=1, source_target_pairs={{0,64},{16,80},{32,96},{48,112},{64,0},{80,16},{96,32},{112,48},{1... | collective-permute-start | bytes 122888 | tf_op jit(solution)/shard_map/ppermute | solution.py:16
  152.7 19.6 %collective-permute-start.38 = (bf16[2,64,1536]{2,1,0:T(8,128)(2,1)S(1)}, bf16[2,64,1536]{2,1,0:T(8,128)(2,1)S(1)}, u32[]{:S(2)}, u32[]{:S(2)}) collective-permute-start(bf16[2,64,1536]{2,1,0:T(8,128)(2,1)S(1)} %pad_maximum_fusion.7.pair), channel_id=1, source_target_pairs={{0,12},{1,13},{2,14},{3,15},{4,8},{5,9},{6,10},{7,11},{8,4},{9,5},... | collective-permute-start | bytes 1179656 | tf_op jit(solution)/shard_map/ppermute | solution.py:16
  154.2 18.0 %collective-permute-start.37 = (bf16[2,64,1536]{2,1,0:T(8,128)(2,1)S(1)}, bf16[2,64,1536]{2,1,0:T(8,128)(2,1)S(1)}, u32[]{:S(2)}, u32[]{:S(2)}) collective-permute-start(bf16[2,64,1536]{2,1,0:T(8,128)(2,1)S(1)} %pad_maximum_fusion.7.pair), channel_id=1, source_target_pairs={{0,8},{1,9},{2,10},{3,11},{4,12},{5,13},{6,14},{7,15},{8,0},{9,1},... | collective-permute-start | bytes 1179656 | tf_op jit(solution)/shard_map/ppermute | solution.py:16
  155.3 17.9 %collective-permute-start.36 = (bf16[2,64,1536]{2,1,0:T(8,128)(2,1)S(1)}, bf16[2,64,1536]{2,1,0:T(8,128)(2,1)S(1)}, u32[]{:S(2)}, u32[]{:S(2)}) collective-permute-start(bf16[2,64,1536]{2,1,0:T(8,128)(2,1)S(1)} %pad_maximum_fusion.7.pair), channel_id=1, source_target_pairs={{0,4},{1,5},{2,6},{3,7},{4,0},{5,1},{6,2},{7,3},{8,12},{9,13},{10,... | collective-permute-start | bytes 1179656 | tf_op jit(solution)/shard_map/ppermute | solution.py:16
  156.0 4.9 %collective-permute-start.39 = (f32[8,1280]{1,0:T(8,128)S(1)}, f32[8,1280]{1,0:T(8,128)S(1)}, u32[]{:S(2)}, u32[]{:S(2)}) collective-permute-start(f32[8,1280]{1,0:T(8,128)S(1)} %add.88), channel_id=1, source_target_pairs={{0,128},{16,144},{32,160},{48,176},{64,192},{80,208},{96,224},{112... | collective-permute-start | bytes 122888 | tf_op jit(solution)/shard_map/ppermute | solution.py:16
  160.9 3.1 %collective-permute-start.40 = (f32[8,1280]{1,0:T(8,128)S(1)}, f32[8,1280]{1,0:T(8,128)S(1)}, u32[]{:S(2)}, u32[]{:S(2)}) collective-permute-start(f32[8,1280]{1,0:T(8,128)S(1)} %add.89), channel_id=1, source_target_pairs={{0,16},{16,0},{32,48},{48,32},{64,80},{80,64},{96,112},{112,96},{1... | collective-permute-start | bytes 122888 | tf_op jit(solution)/shard_map/ppermute | solution.py:16
  174.5 5.2 %collective-permute-start.41 = (f32[128,1280]{1,0:T(8,128)S(1)}, f32[128,1280]{1,0:T(8,128)S(1)}, u32[]{:S(2)}, u32[]{:S(2)}) collective-permute-start(f32[128,1280]{1,0:T(8,128)S(1)} %get-tuple-element.118), channel_id=1, source_target_pairs={{0,1},{1,0},{2,3},{3,2},{4,5},{5,4},{6,7},{7,6},{8,9},{9,8},{10,11... | collective-permute-start | bytes 1966088 | tf_op jit(solution)/shard_map/ppermute | solution.py:16
  174.6 4.4 %collective-permute-start.42 = (f32[8,1280]{1,0:T(8,128)S(1)}, f32[8,1280]{1,0:T(8,128)S(1)}, u32[]{:S(2)}, u32[]{:S(2)}) collective-permute-start(f32[8,1280]{1,0:T(8,128)S(1)} %add.90), channel_id=1, source_target_pairs={{0,32},{16,48},{32,0},{48,16},{64,96},{80,112},{96,64},{112,80},{1... | collective-permute-start | bytes 122888 | tf_op jit(solution)/shard_map/ppermute | solution.py:16

commit v6 on v5

--- a/solution.py
+++ b/solution.py
@@ -286,15 +286,15 @@
     l0, r0 = swap(units[0], "dp", 1), swap(units[0], "dp", 3)
     u1 = swap(units[1], "dp", 4)
     u2 = swap(units[2], "dp", 8)
-    l0, r0, u1 = together(l0, r0, u1)
+    table = doubled(slot_params.T, "expert", 2, 4)
+    l0, r0, table = together(l0, r0, table)
     p0, q0 = swap(r0[0], "dp", 1), swap(l0[1], "dp", 3)
-    table = doubled(after(slot_params.T, u1), "expert", 2)
+    table = doubled(table, "expert", 8, 1)
 
     u1, u2, p0, q0, table = together(u1, u2, p0, q0, table)
     both = jnp.stack([u1, u2], axis=1)
     lb, rb = swap(both, "dp", 1), swap(both, "dp", 3)
     u3 = swap(after(units[3], u1), "dp", 12)
-    table = doubled(table, "expert", 4, 8, 1)
     rows, dispatch, combine, spread = slots_call(table, tokens, out_grad)
     rows = rows.reshape(2 * half, width)
 
@@ -302,7 +302,7 @@
     z1, z2 = swap(rows, "dp", 4), swap(rows, "dp", 8)
     l3, r3 = swap(u3, "dp", 1), swap(u3, "dp", 3)
     pb, qb = swap(rb[0], "dp", 1), swap(lb[1], "dp", 3)
-    l3, r3, z1, z2 = together(l3, r3, z1, z2)
+    l3, r3, z2 = together(l3, r3, z2)
     p3, q3 = swap(r3[0], "dp", 1), swap(l3[1], "dp", 3)
     z3 = swap(z2, "dp", 4)
     pb, qb, p3, q3, z3 = together(pb, qb, p3, q3, z3)
@@ -315,7 +315,7 @@
     slot_in_grad = reduce_z(*halves[4:])
     part, mix = against(slot_out, out_grad, combine, False)
     mix = summed_three(mix, "expert", 1, 2, 3)
-    mix = summed_three(after(mix, slot_in_grad), "expert", 4, 8, 12)
+    mix = summed_three(mix, "expert", 4, 8, 12)
     (back,) = against(slot_in_grad, tokens, dispatch, True)
     logit_grad = back + (part - combine * jnp.repeat(mix, own, axis=0))
     logit_grad_b = logit_grad.astype(BF16)
@@ -328,8 +328,8 @@
     term = summed(term, "dp", 4)
     term, far = together(term, far)
     pieces = all_x(jnp.stack([near, far]))
-    term = summed(term, "dp", 8, 1)
-    slot_grad = summed(after(term, *pieces), "dp", 2).T
+    term = summed(term, "dp", 8, 1, 2)
+    slot_grad = term.T
 
     pieces[1] = after(pieces[1], term)
     mine, theirs = tokens_call(spread, pieces, table)

time: 183 us -> 168 us (0.918); the launches traced: 180 us -> 168 us
  waiting for transfers between devices: 71.3 us -> 47.2 us
  starting transfers between devices: 82.2 us -> 94.1 us
    ppermute x43, waiting for transfers between devices: 71.3 us -> 47.2 us  [swap(): return lax.ppermute(value, axis, [(i, i ^ k) for i in range(count)])]
    ppermute x43, starting transfers between devices: 82.2 us -> 94.1 us  [swap(): return lax.ppermute(value, axis, [(i, i ^ k) for i in range(count)])]
  transfers between devices with their start and end apart: 43 -> 43, of which waited for: 18 -> 22; matrix products, arithmetic and copies ran while one was open for 1% -> 1% of each run, Pallas kernels for 7% -> 8%
where the time goes in v6:
time: 168 us
  starting transfers between devices  94.1 us (56%)
  waiting for transfers between devices  47.2 us (28%)
  Pallas kernels  18.9 us (11%)
  local copies, waits for them, and re-layouts  4.23 us (3%)
  other arithmetic  2.04 us (1%)
    ppermute x43, starting transfers between devices, swap(): return lax.ppermute(value, axis, [(i, i ^ k) for i in range(count)])  94.1 us
    ppermute x43, waiting for transfers between devices, swap(): return lax.ppermute(value, axis, [(i, i ^ k) for i in range(count)])  47.2 us
    pallas_call x1, Pallas kernels, slots_call(): pl.pallas_call(slots_kernel, grid=(images // 2,), out_shape=[jax.ShapeDty...  9.18 us
    pallas_call x2, Pallas kernels, against(): pl.pallas_call(lambda *refs: against_kernel(over_tokens, *refs), grid=(im...  4.36 us
    pallas_call x1, Pallas kernels, ffn(): pl.pallas_call(ffn_kernel, out_shape=[jax.ShapeDtypeStruct((own_rows, wid...  4.03 us
  transfers between devices with their start and end apart: 43, of which 22 were waited for; matrix products, arithmetic and copies ran while one was open for 1% of the time, Pallas kernels for 8%

profile of v6, /device:TPU:1, one launch (start us, length us, event | category | flops | bytes accessed | tf_op | source)
XLA Modules:
  0.0 168.2 jit_solution(12452592450408232673)
XLA Ops:
  0.7 1.4 dynamic-slice_bitcast_fusion.1
  2.3 3.7 %collective-permute-start.3 = (bf16[2,80,1280]{2,1,0:T(8,128)(2,1)S(1)}, bf16[2,80,1280]{2,1,0:T(8,128)(2,1)S(1)}, u32[]{:S(2)}, u32[]{:S(2)}) collective-permute-start(bf16[2,80,1280]{2,1,0:T(8,128)(2,1)S(1)} %pad_maximum_fusion.5.refs_0_), channel_id=1, source_target_pairs={{0,48},{16,32},{32,16},{48,0},{64,112},{80,96},{96,80},{112,64},{1... | collective-permute-start | bytes 1228808 | tf_op jit(solution)/shard_map/ppermute | solution.py:16
  5.9 6.9 %collective-permute-start.4 = (bf16[8,1280]{1,0:T(8,128)(2,1)S(1)}, bf16[8,1280]{1,0:T(8,128)(2,1)S(1)}, u32[]{:S(2)}, u32[]{:S(2)}) collective-permute-start(bf16[8,1280]{1,0:T(8,128)(2,1)S(1)} %bitcast.68), channel_id=1, source_target_pairs={{0,2},{1,3},{2,0},{3,1},{4,6},{5,7},{6,4},{7,5},{8,10},{9,11},{10,... | collective-permute-start | bytes 61448 | tf_op jit(solution)/shard_map/ppermute | solution.py:16
  12.9 0.8 collective-permute-start
  14.0 1.2 collective-permute-start.5
  15.3 1.5 collective-permute-start.1
  17.2 2.8 %collective-permute-start.8 = (bf16[32,1280]{1,0:T(8,128)(2,1)S(1)}, bf16[32,1280]{1,0:T(8,128)(2,1)S(1)}, u32[]{:S(2)}, u32[]{:S(2)}) collective-permute-start(bf16[32,1280]{1,0:T(8,128)(2,1)S(1)} %pad_maximum_fusion.11), channel_id=1, source_target_pairs={{0,8},{1,9},{2,10},{3,11},{4,12},{5,13},{6,14},{7,15},{8,0},{9,1},... | collective-permute-start | bytes 245768 | tf_op jit(solution)/shard_map/ppermute | solution.py:16
  20.0 2.5 %collective-permute-done.8 = bf16[32,1280]{1,0:T(8,128)(2,1)S(1)} collective-permute-done((bf16[32,1280]{1,0:T(8,128)(2,1)S(1)}, bf16[32,1280]{1,0:T(8,128)(2,1)S(1)}, u32[]{:S(2)}, u32[]{:S(2)}) %collective-permute-start.8) | collective-permute-done | bytes 81952 | tf_op jit(solution)/shard_map/ppermute | solution.py:16
  22.5 3.8 %collective-permute-start.9 = (bf16[64,1280]{1,0:T(8,128)(2,1)S(1)}, bf16[64,1280]{1,0:T(8,128)(2,1)S(1)}, u32[]{:S(2)}, u32[]{:S(2)}) collective-permute-start(bf16[64,1280]{1,0:T(8,128)(2,1)S(1)} %pad_maximum_fusion.10), channel_id=1, source_target_pairs={{0,1},{1,0},{2,3},{3,2},{4,5},{5,4},{6,7},{7,6},{8,9},{9,8},{10,11... | collective-permute-start | bytes 491528 | tf_op jit(solution)/shard_map/ppermute | solution.py:16
  26.3 0.9 collective-permute-start.7
  27.2 0.9 collective-permute-start.6
  28.1 2.3 %collective-permute-done = bf16[2,80,1280]{2,1,0:T(8,128)(2,1)S(1)} collective-permute-done((bf16[2,80,1280]{2,1,0:T(8,128)(2,1)S(1)}, bf16[2,80,1280]{2,1,0:T(8,128)(2,1)S(1)}, u32[]{:S(2)}, u32[]{:S(2)}) %collective-permute-start) | collective-permute-done | bytes 409632 | tf_op jit(solution)/shard_map/ppermute | solution.py:16
  30.4 3.8 %collective-permute-done.7.refs_4_ = bf16[80,1280]{1,0:T(8,128)(2,1)S(1)} collective-permute-done((bf16[80,1280]{1,0:T(8,128)(2,1)S(1)}, bf16[80,1280]{1,0:T(8,128)(2,1)S(1)}, u32[]{:S(2)}, u32[]{:S(2)}) %collective-permute-start.7) | collective-permute-done | bytes 204832 | tf_op jit(solution)/shard_map/ppermute | solution.py:16
  34.3 1.2 collective-permute-start.11
  36.0 3.3 %collective-permute-start.12 = (bf16[2,80,1280]{2,1,0:T(8,128)(2,1)S(1)}, bf16[2,80,1280]{2,1,0:T(8,128)(2,1)S(1)}, u32[]{:S(2)}, u32[]{:S(2)}) collective-permute-start(bf16[2,80,1280]{2,1,0:T(8,128)(2,1)S(1)} %pad_maximum_fusion.6), channel_id=1, source_target_pairs={{0,192},{16,208},{32,224},{48,240},{64,128},{80,144},{96,160},{112... | collective-permute-start | bytes 1228808 | tf_op jit(solution)/shard_map/ppermute | solution.py:16
  39.3 2.5 %copy-done.1 = bf16[8,256,1280]{2,1,0:T(8,128)(2,1)S(1)} copy-done((bf16[8,256,1280]{2,1,0:T(8,128)(2,1)S(1)}, bf16[8,256,1280]{2,1,0:T(8,128)(2,1)}, u32[]{:S(2)}) %copy-start.1) | copy-done | bytes 5242904
  41.8 9.2 %slots.1 = (bf16[2,64,1280]{2,1,0:T(8,128)(2,1)S(1)}, f32[64,256]{1,0:T(8,128)S(1)}, f32[64,256]{1,0:T(8,128)S(1)}, bf16[2,128,512]{2,1,0:T(8,128)(2,1)S(1)}) custom-call(bf16[128,1280]{1,0:T(8,128)(2,1)S(1)} %pad_maximum_fusion.8.table, bf16[8,256,1280]{2,1,0:T(8,128)(2,1)S(1)} %copy-done, bf16[8,256,1280]{2,1,0:T(8,128)(2,1)S(1)} %copy-done.1), custom_call_target="tpu_custom_call" | custom-call | flops 838860800 | bytes 10485760 | tf_op jit(solution)/shard_map/slots/pallas_call | solution.py:117
  51.0 1.7 collective-permute-done.11.refs_7_
  52.9 3.4 %collective-permute-start.16 = (bf16[128,1280]{1,0:T(8,128)(2,1)S(1)}, bf16[128,1280]{1,0:T(8,128)(2,1)S(1)}, u32[]{:S(2)}, u32[]{:S(2)}) collective-permute-start(bf16[128,1280]{1,0:T(8,128)(2,1)S(1)} %bitcast.61), channel_id=1, source_target_pairs={{0,128},{16,144},{32,160},{48,176},{64,192},{80,208},{96,224},{112... | collective-permute-start | bytes 983048 | tf_op jit(solution)/shard_map/ppermute | solution.py:16
  56.2 0.8 collective-permute-start.13
  57.1 1.2 collective-permute-start.15
  58.2 0.9 collective-permute-start.14
  59.1 1.2 collective-permute-start.18
  60.4 7.6 %collective-permute-done.13 = bf16[128,1280]{1,0:T(8,128)(2,1)S(1)} collective-permute-done((bf16[128,1280]{1,0:T(8,128)(2,1)S(1)}, bf16[128,1280]{1,0:T(8,128)(2,1)S(1)}, u32[]{:S(2)}, u32[]{:S(2)}) %collective-permute-start.13) | collective-permute-done | bytes 327712 | tf_op jit(solution)/shard_map/ppermute | solution.py:16
  68.0 0.7 collective-permute-start.17
  68.8 1.9 %collective-permute-start.20 = (bf16[80,1280]{1,0:T(8,128)(2,1)S(1)}, bf16[80,1280]{1,0:T(8,128)(2,1)S(1)}, u32[]{:S(2)}, u32[]{:S(2)}) collective-permute-start(bf16[80,1280]{1,0:T(8,128)(2,1)S(1)} %slice_bitcast_fusion.2), channel_id=1, source_target_pairs={{0,48},{16,32},{32,16},{48,0},{64,112},{80,96},{96,80},{112,64},{1... | collective-permute-start | bytes 614408 | tf_op jit(solution)/shard_map/ppermute | solution.py:16
  70.7 0.6 collective-permute-start.19
  71.3 1.9 %collective-permute-start.21 = (bf16[128,1280]{1,0:T(8,128)(2,1)S(1)}, bf16[128,1280]{1,0:T(8,128)(2,1)S(1)}, u32[]{:S(2)}, u32[]{:S(2)}) collective-permute-start(bf16[128,1280]{1,0:T(8,128)(2,1)S(1)} %collective-permute-done.16), channel_id=1, source_target_pairs={{0,64},{16,80},{32,96},{48,112},{64,0},{80,16},{96,32},{112,48},{1... | collective-permute-start | bytes 983048 | tf_op jit(solution)/shard_map/ppermute | solution.py:16
  73.3 1.4 collective-permute-done.18.refs_9_
  74.7 1.1 collective-permute-done.17.refs_8_
  75.8 3.3 %collective-permute-done.20.refs_14_ = bf16[80,1280]{1,0:T(8,128)(2,1)S(1)} collective-permute-done((bf16[80,1280]{1,0:T(8,128)(2,1)S(1)}, bf16[80,1280]{1,0:T(8,128)(2,1)S(1)}, u32[]{:S(2)}, u32[]{:S(2)}) %collective-permute-start.20) | collective-permute-done | bytes 204832 | tf_op jit(solution)/shard_map/ppermute | solution.py:16
  79.1 1.1 collective-permute-done.19.refs_13_
  80.4 4.0 %ffn.1 = (f32[64,1280]{1,0:T(8,128)S(1)}, bf16[64,1280]{1,0:T(8,128)(2,1)S(1)}, bf16[64,1280]{1,0:T(8,128)(2,1)S(1)}, bf16[64,1280]{1,0:T(8,128)(2,1)S(1)}, f32[...) custom-call(bf16[256,1280]{1,0:T(8,128)(2,1)S(1)} %get-tuple-element, ...), custom_call_target="tpu_custom_call" | custom-call | tf_op jit(solution)/shard_map/ffn/pallas_call | solution.py:61
  84.4 2.3 %collective-permute-start.25 = (bf16[64,1280]{1,0:T(8,128)(2,1)S(1)}, bf16[64,1280]{1,0:T(8,128)(2,1)S(1)}, u32[]{:S(2)}, u32[]{:S(2)}) collective-permute-start(bf16[64,1280]{1,0:T(8,128)(2,1)S(1)} %get-tuple-element.89), channel_id=1, source_target_pairs={{0,64},{16,80},{32,96},{48,112},{64,0},{80,16},{96,32},{112,48},{1... | collective-permute-start | bytes 491528 | tf_op jit(solution)/shard_map/ppermute | solution.py:16
  86.7 3.9 %collective-permute-start.26 = (bf16[64,1280]{1,0:T(8,128)(2,1)S(1)}, bf16[64,1280]{1,0:T(8,128)(2,1)S(1)}, u32[]{:S(2)}, u32[]{:S(2)}) collective-permute-start(bf16[64,1280]{1,0:T(8,128)(2,1)S(1)} %get-tuple-element.90), channel_id=1, source_target_pairs={{0,128},{16,144},{32,160},{48,176},{64,192},{80,208},{96,224},{112... | collective-permute-start | bytes 491528 | tf_op jit(solution)/shard_map/ppermute | solution.py:16
  90.6 1.1 collective-permute-start.27
  91.9 2.2 %collective-permute-start.23 = (bf16[64,1280]{1,0:T(8,128)(2,1)S(1)}, bf16[64,1280]{1,0:T(8,128)(2,1)S(1)}, u32[]{:S(2)}, u32[]{:S(2)}) collective-permute-start(bf16[64,1280]{1,0:T(8,128)(2,1)S(1)} %get-tuple-element.82), channel_id=1, source_target_pairs={{0,128},{16,144},{32,160},{48,176},{64,192},{80,208},{96,224},{112... | collective-permute-start | bytes 491528 | tf_op jit(solution)/shard_map/ppermute | solution.py:16
  94.1 1.1 collective-permute-start.24
  95.2 4.4 %collective-permute-done.27 = bf16[64,1280]{1,0:T(8,128)(2,1)S(1)} collective-permute-done((bf16[64,1280]{1,0:T(8,128)(2,1)S(1)}, bf16[64,1280]{1,0:T(8,128)(2,1)S(1)}, u32[]{:S(2)}, u32[]{:S(2)}) %collective-permute-start.27) | collective-permute-done | bytes 163872 | tf_op jit(solution)/shard_map/ppermute | solution.py:16
  99.7 2.1 %combine_grad.1 = (f32[64,256]{1,0:T(8,128)S(1)}, f32[8,256]{1,0:T(8,128)S(1)}) custom-call(f32[64,1280]{1,0:T(8,128)S(1)} %add_add_fusion.refs_0_, bf16[8,256,1280]{2,1,0:T(8,128)(2,1)S(1)} %bitcast.60, f32[64,256]{1,0:T(8,128)S(1)} %get-tuple-element.95.refs_2_), custom_call_target="tpu_custom_call" | custom-call | flops 5368709120 | bytes 5242880 | tf_op jit(solution)/shard_map/combine_grad/pallas_call | solution.py:174
  101.8 12.0 %collective-permute-start.30 = (f32[8,256]{1,0:T(8,128)S(1)}, f32[8,256]{1,0:T(8,128)S(1)}, u32[]{:S(2)}, u32[]{:S(2)}) collective-permute-start(f32[8,256]{1,0:T(8,128)S(1)} %get-tuple-element.97), channel_id=1, source_target_pairs={{0,3},{1,2},{2,1},{3,0},{4,7},{5,6},{6,5},{7,4},{8,11},{9,10},{10,... | collective-permute-start | bytes 24584 | tf_op jit(solution)/shard_map/ppermute | solution.py:16
  113.8 1.1 collective-permute-start.29
  115.2 5.1 %collective-permute-done.29 = f32[8,256]{1,0:T(8,128)S(1)} collective-permute-done((f32[8,256]{1,0:T(8,128)S(1)}, f32[8,256]{1,0:T(8,128)S(1)}, u32[]{:S(2)}, u32[]{:S(2)}) %collective-permute-start.29) | collective-permute-done | bytes 8224 | tf_op jit(solution)/shard_map/ppermute | solution.py:16
  120.4 3.3 %collective-permute-start.33 = (f32[8,256]{1,0:T(8,128)S(1)}, f32[8,256]{1,0:T(8,128)S(1)}, u32[]{:S(2)}, u32[]{:S(2)}) collective-permute-start(f32[8,256]{1,0:T(8,128)S(1)} %add_add_fusion.3), channel_id=1, source_target_pairs={{0,12},{1,13},{2,14},{3,15},{4,8},{5,9},{6,10},{7,11},{8,4},{9,5},... | collective-permute-start | bytes 24584 | tf_op jit(solution)/shard_map/ppermute | solution.py:16
  123.8 0.5 collective-permute-start.31
  124.4 2.3 %dispatch_grad.1 = f32[64,256]{1,0:T(8,128)S(1)} custom-call(f32[64,1280]{1,0:T(8,128)S(1)} %get-tuple-element.113.refs_0_, bf16[8,256,1280]{2,1,0:T(8,128)(2,1)S(1)} %copy-done, f32[64,256]{1,0:T(8,128)S(1)} %get-tuple-element.87.refs_2_), custom_call_target="tpu_custom_call" | custom-call | flops 5368709120 | bytes 5242880 | tf_op jit(solution)/shard_map/dispatch_grad/pallas_call | solution.py:174
  126.6 1.0 collective-permute-done.32
  128.0 0.8 convolution_bitcast_fusion
  128.8 8.3 %collective-permute-start.34 = (f32[8,1280]{1,0:T(8,128)S(1)}, f32[8,1280]{1,0:T(8,128)S(1)}, u32[]{:S(2)}, u32[]{:S(2)}) collective-permute-start(f32[8,1280]{1,0:T(8,128)S(1)} %convolution_bitcast_fusion), channel_id=1, source_target_pairs={{0,64},{16,80},{32,96},{48,112},{64,0},{80,16},{96,32},{112,48},{1... | collective-permute-start | bytes 122888 | tf_op jit(solution)/shard_map/ppermute | solution.py:16
  137.1 2.8 %collective-permute-done.34 = f32[8,1280]{1,0:T(8,128)S(1)} collective-permute-done((f32[8,1280]{1,0:T(8,128)S(1)}, f32[8,1280]{1,0:T(8,128)S(1)}, u32[]{:S(2)}, u32[]{:S(2)}) %collective-permute-start.34) | collective-permute-done | bytes 40992 | tf_op jit(solution)/shard_map/ppermute | solution.py:16
  140.0 1.5 collective-permute-start.38
  141.5 0.7 collective-permute-start.37
  142.2 1.2 collective-permute-start.36
  143.4 5.6 %collective-permute-start.39 = (f32[8,1280]{1,0:T(8,128)S(1)}, f32[8,1280]{1,0:T(8,128)S(1)}, u32[]{:S(2)}, u32[]{:S(2)}) collective-permute-start(f32[8,1280]{1,0:T(8,128)S(1)} %add.88), channel_id=1, source_target_pairs={{0,128},{16,144},{32,160},{48,176},{64,192},{80,208},{96,224},{112... | collective-permute-start | bytes 122888 | tf_op jit(solution)/shard_map/ppermute | solution.py:16
  148.9 1.7 %collective-permute-done.39 = f32[8,1280]{1,0:T(8,128)S(1)} collective-permute-done((f32[8,1280]{1,0:T(8,128)S(1)}, f32[8,1280]{1,0:T(8,128)S(1)}, u32[]{:S(2)}, u32[]{:S(2)}) %collective-permute-start.39) | collective-permute-done | bytes 40992 | tf_op jit(solution)/shard_map/ppermute | solution.py:16
  150.6 1.1 collective-permute-start.40
  151.8 2.0 %collective-permute-done.40 = f32[8,1280]{1,0:T(8,128)S(1)} collective-permute-done((f32[8,1280]{1,0:T(8,128)S(1)}, f32[8,1280]{1,0:T(8,128)S(1)}, u32[]{:S(2)}, u32[]{:S(2)}) %collective-permute-start.40) | collective-permute-done | bytes 40992 | tf_op jit(solution)/shard_map/ppermute | solution.py:16
  153.8 2.2 %collective-permute-start.41 = (f32[8,1280]{1,0:T(8,128)S(1)}, f32[8,1280]{1,0:T(8,128)S(1)}, u32[]{:S(2)}, u32[]{:S(2)}) collective-permute-start(f32[8,1280]{1,0:T(8,128)S(1)} %add.90), channel_id=1, source_target_pairs={{0,32},{16,48},{32,0},{48,16},{64,96},{80,112},{96,64},{112,80},{1... | collective-permute-start | bytes 122888 | tf_op jit(solution)/shard_map/ppermute | solution.py:16
  156.0 2.2 %collective-permute-done.41 = f32[8,1280]{1,0:T(8,128)S(1)} collective-permute-done((f32[8,1280]{1,0:T(8,128)S(1)}, f32[8,1280]{1,0:T(8,128)S(1)}, u32[]{:S(2)}, u32[]{:S(2)}) %collective-permute-start.41) | collective-permute-done | bytes 40992 | tf_op jit(solution)/shard_map/ppermute | solution.py:16
  158.1 0.6 add.91
  159.0 1.3 token_grad.1
  160.3 5.3 %collective-permute-start.42 = (f32[128,1280]{1,0:T(8,128)S(1)}, f32[128,1280]{1,0:T(8,128)S(1)}, u32[]{:S(2)}, u32[]{:S(2)}) collective-permute-start(f32[128,1280]{1,0:T(8,128)S(1)} %get-tuple-element.111), channel_id=1, source_target_pairs={{0,1},{1,0},{2,3},{3,2},{4,5},{5,4},{6,7},{7,6},{8,9},{9,8},{10,11... | collective-permute-start | bytes 1966088 | tf_op jit(solution)/shard_map/ppermute | solution.py:16
  165.7 1.7 %collective-permute-done.42 = f32[128,1280]{1,0:T(8,128)S(1)} collective-permute-done((f32[128,1280]{1,0:T(8,128)S(1)}, f32[128,1280]{1,0:T(8,128)S(1)}, u32[]{:S(2)}, u32[]{:S(2)}) %collective-permute-start.42) | collective-permute-done | bytes 655392 | tf_op jit(solution)/shard_map/ppermute | solution.py:16
  167.4 0.8 add_convert_fusion
  (75 shorter events, 3.5 us)
Async XLA Ops:
  0.6 1.5 copy-start.2
  2.1 3.8 %copy-start.3 = (bf16[1280,8]{0,1:T(8,128)(2,1)S(1)}, bf16[1280,8]{0,1:T(8,128)(2,1)}, u32[]{:S(2)}) copy-start(bf16[1280,8]{0,1:T(8,128)(2,1)} %param.7) | copy-start | bytes 61444
  2.3 14.9 %collective-permute-start.3 = (bf16[2,80,1280]{2,1,0:T(8,128)(2,1)S(1)}, bf16[2,80,1280]{2,1,0:T(8,128)(2,1)S(1)}, u32[]{:S(2)}, u32[]{:S(2)}) collective-permute-start(bf16[2,80,1280]{2,1,0:T(8,128)(2,1)S(1)} %pad_maximum_fusion.5.refs_0_), channel_id=1, source_target_pairs={{0,48},{16,32},{32,16},{48,0},{64,112},{80,96},{96,80},{112,64},{1... | collective-permute-start | bytes 1228808 | tf_op jit(solution)/shard_map/ppermute | solution.py:16
  5.9 11.3 %collective-permute-start.2 = (bf16[2,80,1280]{2,1,0:T(8,128)(2,1)S(1)}, bf16[2,80,1280]{2,1,0:T(8,128)(2,1)S(1)}, u32[]{:S(2)}, u32[]{:S(2)}) collective-permute-start(bf16[2,80,1280]{2,1,0:T(8,128)(2,1)S(1)} %pad_maximum_fusion.5.refs_0_), channel_id=1, source_target_pairs={{0,16},{16,0},{32,48},{48,32},{64,80},{80,64},{96,112},{112,96},{1... | collective-permute-start | bytes 1228808 | tf_op jit(solution)/shard_map/ppermute | solution.py:16
  5.9 8.1 %collective-permute-start.4 = (bf16[8,1280]{1,0:T(8,128)(2,1)S(1)}, bf16[8,1280]{1,0:T(8,128)(2,1)S(1)}, u32[]{:S(2)}, u32[]{:S(2)}) collective-permute-start(bf16[8,1280]{1,0:T(8,128)(2,1)S(1)} %bitcast.68), channel_id=1, source_target_pairs={{0,2},{1,3},{2,0},{3,1},{4,6},{5,7},{6,4},{7,5},{8,10},{9,11},{10,... | collective-permute-start | bytes 61448 | tf_op jit(solution)/shard_map/ppermute | solution.py:16
  12.9 17.6 %collective-permute-start = (bf16[2,80,1280]{2,1,0:T(8,128)(2,1)S(1)}, bf16[2,80,1280]{2,1,0:T(8,128)(2,1)S(1)}, u32[]{:S(2)}, u32[]{:S(2)}) collective-permute-start(bf16[2,80,1280]{2,1,0:T(8,128)(2,1)S(1)} %pad_maximum_fusion.3), channel_id=1, source_target_pairs={{0,64},{16,80},{32,96},{48,112},{64,0},{80,16},{96,32},{112,48},{1... | collective-permute-start | bytes 1228808 | tf_op jit(solution)/shard_map/ppermute | solution.py:16
  14.0 3.1 %collective-permute-start.5 = (bf16[16,1280]{1,0:T(8,128)(2,1)S(1)}, bf16[16,1280]{1,0:T(8,128)(2,1)S(1)}, u32[]{:S(2)}, u32[]{:S(2)}) collective-permute-start(bf16[16,1280]{1,0:T(8,128)(2,1)S(1)} %pad_maximum_fusion.12), channel_id=1, source_target_pairs={{0,4},{1,5},{2,6},{3,7},{4,0},{5,1},{6,2},{7,3},{8,12},{9,13},{10,... | collective-permute-start | bytes 122888 | tf_op jit(solution)/shard_map/ppermute | solution.py:16
  15.2 24.1 %copy-start = (bf16[8,256,1280]{2,1,0:T(8,128)(2,1)S(1)}, bf16[8,256,1280]{2,1,0:T(8,128)(2,1)}, u32[]{:S(2)}) copy-start(bf16[8,256,1280]{2,1,0:T(8,128)(2,1)} %refs_1_.2) | copy-start | bytes 15728644
  15.3 15.2 %collective-permute-start.1 = (bf16[2,80,1280]{2,1,0:T(8,128)(2,1)S(1)}, bf16[2,80,1280]{2,1,0:T(8,128)(2,1)S(1)}, u32[]{:S(2)}, u32[]{:S(2)}) collective-permute-start(bf16[2,80,1280]{2,1,0:T(8,128)(2,1)S(1)} %pad_maximum_fusion.4), channel_id=1, source_target_pairs={{0,128},{16,144},{32,160},{48,176},{64,192},{80,208},{96,224},{112... | collective-permute-start | bytes 1228808 | tf_op jit(solution)/shard_map/ppermute | solution.py:16
  17.2 5.3 %collective-permute-start.8 = (bf16[32,1280]{1,0:T(8,128)(2,1)S(1)}, bf16[32,1280]{1,0:T(8,128)(2,1)S(1)}, u32[]{:S(2)}, u32[]{:S(2)}) collective-permute-start(bf16[32,1280]{1,0:T(8,128)(2,1)S(1)} %pad_maximum_fusion.11), channel_id=1, source_target_pairs={{0,8},{1,9},{2,10},{3,11},{4,12},{5,13},{6,14},{7,15},{8,0},{9,1},... | collective-permute-start | bytes 245768 | tf_op jit(solution)/shard_map/ppermute | solution.py:16
  22.5 5.6 %collective-permute-start.9 = (bf16[64,1280]{1,0:T(8,128)(2,1)S(1)}, bf16[64,1280]{1,0:T(8,128)(2,1)S(1)}, u32[]{:S(2)}, u32[]{:S(2)}) collective-permute-start(bf16[64,1280]{1,0:T(8,128)(2,1)S(1)} %pad_maximum_fusion.10), channel_id=1, source_target_pairs={{0,1},{1,0},{2,3},{3,2},{4,5},{5,4},{6,7},{7,6},{8,9},{9,8},{10,11... | collective-permute-start | bytes 491528 | tf_op jit(solution)/shard_map/ppermute | solution.py:16
  26.3 8.0 %collective-permute-start.7 = (bf16[80,1280]{1,0:T(8,128)(2,1)S(1)}, bf16[80,1280]{1,0:T(8,128)(2,1)S(1)}, u32[]{:S(2)}, u32[]{:S(2)}) collective-permute-start(bf16[80,1280]{1,0:T(8,128)(2,1)S(1)} %slice_bitcast_fusion.4), channel_id=1, source_target_pairs={{0,48},{16,32},{32,16},{48,0},{64,112},{80,96},{96,80},{112,64},{1... | collective-permute-start | bytes 614408 | tf_op jit(solution)/shard_map/ppermute | solution.py:16
  27.2 7.1 %collective-permute-start.6 = (bf16[80,1280]{1,0:T(8,128)(2,1)S(1)}, bf16[80,1280]{1,0:T(8,128)(2,1)S(1)}, u32[]{:S(2)}, u32[]{:S(2)}) collective-permute-start(bf16[80,1280]{1,0:T(8,128)(2,1)S(1)} %slice_bitcast_fusion.5), channel_id=1, source_target_pairs={{0,16},{16,0},{32,48},{48,32},{64,80},{80,64},{96,112},{112,96},{1... | collective-permute-start | bytes 614408 | tf_op jit(solution)/shard_map/ppermute | solution.py:16
  34.3 18.3 %collective-permute-start.11 = (bf16[2,2,80,1280]{3,2,1,0:T(8,128)(2,1)S(1)}, bf16[2,2,80,1280]{3,2,1,0:T(8,128)(2,1)S(1)}, u32[]{:S(2)}, u32[]{:S(2)}) collective-permute-start(bf16[2,2,80,1280]{3,2,1,0:T(8,128)(2,1)S(1)} %pad_maximum_fusion.refs_5_), channel_id=1, source_target_pairs={{0,48},{16,32},{32,16},{48,0},{64,112},{80,96},{96,80},{112,64},{1... | collective-permute-start | bytes 2457608 | tf_op jit(solution)/shard_map/ppermute | solution.py:16
  35.6 17.3 %collective-permute-start.10 = (bf16[2,2,80,1280]{3,2,1,0:T(8,128)(2,1)S(1)}, bf16[2,2,80,1280]{3,2,1,0:T(8,128)(2,1)S(1)}, u32[]{:S(2)}, u32[]{:S(2)}) collective-permute-start(bf16[2,2,80,1280]{3,2,1,0:T(8,128)(2,1)S(1)} %pad_maximum_fusion.refs_5_), channel_id=1, source_target_pairs={{0,16},{16,0},{32,48},{48,32},{64,80},{80,64},{96,112},{112,96},{1... | collective-permute-start | bytes 2457608 | tf_op jit(solution)/shard_map/ppermute | solution.py:16
  36.0 15.0 %collective-permute-start.12 = (bf16[2,80,1280]{2,1,0:T(8,128)(2,1)S(1)}, bf16[2,80,1280]{2,1,0:T(8,128)(2,1)S(1)}, u32[]{:S(2)}, u32[]{:S(2)}) collective-permute-start(bf16[2,80,1280]{2,1,0:T(8,128)(2,1)S(1)} %pad_maximum_fusion.6), channel_id=1, source_target_pairs={{0,192},{16,208},{32,224},{48,240},{64,128},{80,144},{96,160},{112... | collective-permute-start | bytes 1228808 | tf_op jit(solution)/shard_map/ppermute | solution.py:16
  39.3 2.5 %copy-start.1 = (bf16[8,256,1280]{2,1,0:T(8,128)(2,1)S(1)}, bf16[8,256,1280]{2,1,0:T(8,128)(2,1)}, u32[]{:S(2)}) copy-start(bf16[8,256,1280]{2,1,0:T(8,128)(2,1)} %refs_1_.3) | copy-start | bytes 15728644
  52.9 15.9 %collective-permute-start.16 = (bf16[128,1280]{1,0:T(8,128)(2,1)S(1)}, bf16[128,1280]{1,0:T(8,128)(2,1)S(1)}, u32[]{:S(2)}, u32[]{:S(2)}) collective-permute-start(bf16[128,1280]{1,0:T(8,128)(2,1)S(1)} %bitcast.61), channel_id=1, source_target_pairs={{0,128},{16,144},{32,160},{48,176},{64,192},{80,208},{96,224},{112... | collective-permute-start | bytes 983048 | tf_op jit(solution)/shard_map/ppermute | solution.py:16
  56.2 11.8 %collective-permute-start.13 = (bf16[128,1280]{1,0:T(8,128)(2,1)S(1)}, bf16[128,1280]{1,0:T(8,128)(2,1)S(1)}, u32[]{:S(2)}, u32[]{:S(2)}) collective-permute-start(bf16[128,1280]{1,0:T(8,128)(2,1)S(1)} %bitcast.62), channel_id=1, source_target_pairs={{0,64},{16,80},{32,96},{48,112},{64,0},{80,16},{96,32},{112,48},{1... | collective-permute-start | bytes 983048 | tf_op jit(solution)/shard_map/ppermute | solution.py:16
  57.1 11.7 %collective-permute-start.15 = (bf16[2,80,1280]{2,1,0:T(8,128)(2,1)S(1)}, bf16[2,80,1280]{2,1,0:T(8,128)(2,1)S(1)}, u32[]{:S(2)}, u32[]{:S(2)}) collective-permute-start(bf16[2,80,1280]{2,1,0:T(8,128)(2,1)S(1)} %collective-permute-done.12.refs_10_), channel_id=1, source_target_pairs={{0,48},{16,32},{32,16},{48,0},{64,112},{80,96},{96,80},{112,64},{1... | collective-permute-start | bytes 1228808 | tf_op jit(solution)/shard_map/ppermute | solution.py:16
  58.2 10.6 %collective-permute-start.14 = (bf16[2,80,1280]{2,1,0:T(8,128)(2,1)S(1)}, bf16[2,80,1280]{2,1,0:T(8,128)(2,1)S(1)}, u32[]{:S(2)}, u32[]{:S(2)}) collective-permute-start(bf16[2,80,1280]{2,1,0:T(8,128)(2,1)S(1)} %collective-permute-done.12.refs_10_), channel_id=1, source_target_pairs={{0,16},{16,0},{32,48},{48,32},{64,80},{80,64},{96,112},{112,96},{1... | collective-permute-start | bytes 1228808 | tf_op jit(solution)/shard_map/ppermute | solution.py:16
  59.1 15.5 %collective-permute-start.18 = (bf16[2,80,1280]{2,1,0:T(8,128)(2,1)S(1)}, bf16[2,80,1280]{2,1,0:T(8,128)(2,1)S(1)}, u32[]{:S(2)}, u32[]{:S(2)}) collective-permute-start(bf16[2,80,1280]{2,1,0:T(8,128)(2,1)S(1)} %slice_bitcast_fusion), channel_id=1, source_target_pairs={{0,48},{16,32},{32,16},{48,0},{64,112},{80,96},{96,80},{112,64},{1... | collective-permute-start | bytes 1228808 | tf_op jit(solution)/shard_map/ppermute | solution.py:16
  68.0 7.8 %collective-permute-start.17 = (bf16[2,80,1280]{2,1,0:T(8,128)(2,1)S(1)}, bf16[2,80,1280]{2,1,0:T(8,128)(2,1)S(1)}, u32[]{:S(2)}, u32[]{:S(2)}) collective-permute-start(bf16[2,80,1280]{2,1,0:T(8,128)(2,1)S(1)} %slice_bitcast_fusion.1), channel_id=1, source_target_pairs={{0,16},{16,0},{32,48},{48,32},{64,80},{80,64},{96,112},{112,96},{1... | collective-permute-start | bytes 1228808 | tf_op jit(solution)/shard_map/ppermute | solution.py:16
  68.8 10.2 %collective-permute-start.20 = (bf16[80,1280]{1,0:T(8,128)(2,1)S(1)}, bf16[80,1280]{1,0:T(8,128)(2,1)S(1)}, u32[]{:S(2)}, u32[]{:S(2)}) collective-permute-start(bf16[80,1280]{1,0:T(8,128)(2,1)S(1)} %slice_bitcast_fusion.2), channel_id=1, source_target_pairs={{0,48},{16,32},{32,16},{48,0},{64,112},{80,96},{96,80},{112,64},{1... | collective-permute-start | bytes 614408 | tf_op jit(solution)/shard_map/ppermute | solution.py:16
  70.7 9.5 %collective-permute-start.19 = (bf16[80,1280]{1,0:T(8,128)(2,1)S(1)}, bf16[80,1280]{1,0:T(8,128)(2,1)S(1)}, u32[]{:S(2)}, u32[]{:S(2)}) collective-permute-start(bf16[80,1280]{1,0:T(8,128)(2,1)S(1)} %slice_bitcast_fusion.3), channel_id=1, source_target_pairs={{0,16},{16,0},{32,48},{48,32},{64,80},{80,64},{96,112},{112,96},{1... | collective-permute-start | bytes 614408 | tf_op jit(solution)/shard_map/ppermute | solution.py:16
  71.3 8.9 %collective-permute-start.21 = (bf16[128,1280]{1,0:T(8,128)(2,1)S(1)}, bf16[128,1280]{1,0:T(8,128)(2,1)S(1)}, u32[]{:S(2)}, u32[]{:S(2)}) collective-permute-start(bf16[128,1280]{1,0:T(8,128)(2,1)S(1)} %collective-permute-done.16), channel_id=1, source_target_pairs={{0,64},{16,80},{32,96},{48,112},{64,0},{80,16},{96,32},{112,48},{1... | collective-permute-start | bytes 983048 | tf_op jit(solution)/shard_map/ppermute | solution.py:16
  80.2 19.5 %slice-start = ((s8[5242880]{0:T(1024)(128)(4,1)}), s8[4194304]{0:T(1024)(128)(4,1)S(1)}, s32[]{:S(2)}) async-start(s8[5242880]{0:T(1024)(128)(4,1)} %bitcast.59), calls=%async_computation | async-start | bytes 8388608
  80.3 19.4 %slice-start.1 = ((s8[5242880]{0:T(1024)(128)(4,1)}), s8[1048576]{0:T(1024)(128)(4,1)S(1)}, s32[]{:S(2)}) async-start(s8[5242880]{0:T(1024)(128)(4,1)} %bitcast.59), calls=%async_computation.1 | async-start | bytes 2097152
  84.4 9.7 %collective-permute-start.25 = (bf16[64,1280]{1,0:T(8,128)(2,1)S(1)}, bf16[64,1280]{1,0:T(8,128)(2,1)S(1)}, u32[]{:S(2)}, u32[]{:S(2)}) collective-permute-start(bf16[64,1280]{1,0:T(8,128)(2,1)S(1)} %get-tuple-element.89), channel_id=1, source_target_pairs={{0,64},{16,80},{32,96},{48,112},{64,0},{80,16},{96,32},{112,48},{1... | collective-permute-start | bytes 491528 | tf_op jit(solution)/shard_map/ppermute | solution.py:16
  86.7 8.5 %collective-permute-start.26 = (bf16[64,1280]{1,0:T(8,128)(2,1)S(1)}, bf16[64,1280]{1,0:T(8,128)(2,1)S(1)}, u32[]{:S(2)}, u32[]{:S(2)}) collective-permute-start(bf16[64,1280]{1,0:T(8,128)(2,1)S(1)} %get-tuple-element.90), channel_id=1, source_target_pairs={{0,128},{16,144},{32,160},{48,176},{64,192},{80,208},{96,224},{112... | collective-permute-start | bytes 491528 | tf_op jit(solution)/shard_map/ppermute | solution.py:16
  90.6 9.1 %collective-permute-start.27 = (bf16[64,1280]{1,0:T(8,128)(2,1)S(1)}, bf16[64,1280]{1,0:T(8,128)(2,1)S(1)}, u32[]{:S(2)}, u32[]{:S(2)}) collective-permute-start(bf16[64,1280]{1,0:T(8,128)(2,1)S(1)} %get-tuple-element.91), channel_id=1, source_target_pairs={{0,192},{16,208},{32,224},{48,240},{64,128},{80,144},{96,160},{112... | collective-permute-start | bytes 491528 | tf_op jit(solution)/shard_map/ppermute | solution.py:16
  91.7 23.3 %collective-permute-start.22 = (bf16[64,1280]{1,0:T(8,128)(2,1)S(1)}, bf16[64,1280]{1,0:T(8,128)(2,1)S(1)}, u32[]{:S(2)}, u32[]{:S(2)}) collective-permute-start(bf16[64,1280]{1,0:T(8,128)(2,1)S(1)} %get-tuple-element.81), channel_id=1, source_target_pairs={{0,64},{16,80},{32,96},{48,112},{64,0},{80,16},{96,32},{112,48},{1... | collective-permute-start | bytes 491528 | tf_op jit(solution)/shard_map/ppermute | solution.py:16
  91.9 23.2 %collective-permute-start.23 = (bf16[64,1280]{1,0:T(8,128)(2,1)S(1)}, bf16[64,1280]{1,0:T(8,128)(2,1)S(1)}, u32[]{:S(2)}, u32[]{:S(2)}) collective-permute-start(bf16[64,1280]{1,0:T(8,128)(2,1)S(1)} %get-tuple-element.82), channel_id=1, source_target_pairs={{0,128},{16,144},{32,160},{48,176},{64,192},{80,208},{96,224},{112... | collective-permute-start | bytes 491528 | tf_op jit(solution)/shard_map/ppermute | solution.py:16
  94.1 21.0 %collective-permute-start.24 = (bf16[64,1280]{1,0:T(8,128)(2,1)S(1)}, bf16[64,1280]{1,0:T(8,128)(2,1)S(1)}, u32[]{:S(2)}, u32[]{:S(2)}) collective-permute-start(bf16[64,1280]{1,0:T(8,128)(2,1)S(1)} %get-tuple-element.83), channel_id=1, source_target_pairs={{0,192},{16,208},{32,224},{48,240},{64,128},{80,144},{96,160},{112... | collective-permute-start | bytes 491528 | tf_op jit(solution)/shard_map/ppermute | solution.py:16
  101.8 13.4 %collective-permute-start.30 = (f32[8,256]{1,0:T(8,128)S(1)}, f32[8,256]{1,0:T(8,128)S(1)}, u32[]{:S(2)}, u32[]{:S(2)}) collective-permute-start(f32[8,256]{1,0:T(8,128)S(1)} %get-tuple-element.97), channel_id=1, source_target_pairs={{0,3},{1,2},{2,1},{3,0},{4,7},{5,6},{6,5},{7,4},{8,11},{9,10},{10,... | collective-permute-start | bytes 24584 | tf_op jit(solution)/shard_map/ppermute | solution.py:16
  113.8 6.5 %collective-permute-start.29 = (f32[8,256]{1,0:T(8,128)S(1)}, f32[8,256]{1,0:T(8,128)S(1)}, u32[]{:S(2)}, u32[]{:S(2)}) collective-permute-start(f32[8,256]{1,0:T(8,128)S(1)} %get-tuple-element.97), channel_id=1, source_target_pairs={{0,2},{1,3},{2,0},{3,1},{4,6},{5,7},{6,4},{7,5},{8,10},{9,11},{10,... | collective-permute-start | bytes 24584 | tf_op jit(solution)/shard_map/ppermute | solution.py:16
  115.0 5.4 %collective-permute-start.28 = (f32[8,256]{1,0:T(8,128)S(1)}, f32[8,256]{1,0:T(8,128)S(1)}, u32[]{:S(2)}, u32[]{:S(2)}) collective-permute-start(f32[8,256]{1,0:T(8,128)S(1)} %get-tuple-element.97), channel_id=1, source_target_pairs={{0,1},{1,0},{2,3},{3,2},{4,5},{5,4},{6,7},{7,6},{8,9},{9,8},{10,11... | collective-permute-start | bytes 24584 | tf_op jit(solution)/shard_map/ppermute | solution.py:16
  120.4 6.3 %collective-permute-start.33 = (f32[8,256]{1,0:T(8,128)S(1)}, f32[8,256]{1,0:T(8,128)S(1)}, u32[]{:S(2)}, u32[]{:S(2)}) collective-permute-start(f32[8,256]{1,0:T(8,128)S(1)} %add_add_fusion.3), channel_id=1, source_target_pairs={{0,12},{1,13},{2,14},{3,15},{4,8},{5,9},{6,10},{7,11},{8,4},{9,5},... | collective-permute-start | bytes 24584 | tf_op jit(solution)/shard_map/ppermute | solution.py:16
  123.7 4.0 %collective-permute-start.32 = (f32[8,256]{1,0:T(8,128)S(1)}, f32[8,256]{1,0:T(8,128)S(1)}, u32[]{:S(2)}, u32[]{:S(2)}) collective-permute-start(f32[8,256]{1,0:T(8,128)S(1)} %add_add_fusion.3), channel_id=1, source_target_pairs={{0,8},{1,9},{2,10},{3,11},{4,12},{5,13},{6,14},{7,15},{8,0},{9,1},... | collective-permute-start | bytes 24584 | tf_op jit(solution)/shard_map/ppermute | solution.py:16
  123.8 3.8 %collective-permute-start.31 = (f32[8,256]{1,0:T(8,128)S(1)}, f32[8,256]{1,0:T(8,128)S(1)}, u32[]{:S(2)}, u32[]{:S(2)}) collective-permute-start(f32[8,256]{1,0:T(8,128)S(1)} %add_add_fusion.3), channel_id=1, source_target_pairs={{0,4},{1,5},{2,6},{3,7},{4,0},{5,1},{6,2},{7,3},{8,12},{9,13},{10,... | collective-permute-start | bytes 24584 | tf_op jit(solution)/shard_map/ppermute | solution.py:16
  127.8 12.2 %collective-permute-start.35 = (bf16[64,1536]{1,0:T(8,128)(2,1)S(1)}, bf16[64,1536]{1,0:T(8,128)(2,1)S(1)}, u32[]{:S(2)}, u32[]{:S(2)}) collective-permute-start(bf16[64,1536]{1,0:T(8,128)(2,1)S(1)} %get-tuple-element.131), channel_id=1, source_target_pairs={{0,2},{1,3},{2,0},{3,1},{4,6},{5,7},{6,4},{7,5},{8,10},{9,11},{10,... | collective-permute-start | bytes 589832 | tf_op jit(solution)/shard_map/ppermute | solution.py:16
  128.8 11.1 %collective-permute-start.34 = (f32[8,1280]{1,0:T(8,128)S(1)}, f32[8,1280]{1,0:T(8,128)S(1)}, u32[]{:S(2)}, u32[]{:S(2)}) collective-permute-start(f32[8,1280]{1,0:T(8,128)S(1)} %convolution_bitcast_fusion), channel_id=1, source_target_pairs={{0,64},{16,80},{32,96},{48,112},{64,0},{80,16},{96,32},{112,48},{1... | collective-permute-start | bytes 122888 | tf_op jit(solution)/shard_map/ppermute | solution.py:16
  140.0 19.0 %collective-permute-start.38 = (bf16[2,64,1536]{2,1,0:T(8,128)(2,1)S(1)}, bf16[2,64,1536]{2,1,0:T(8,128)(2,1)S(1)}, u32[]{:S(2)}, u32[]{:S(2)}) collective-permute-start(bf16[2,64,1536]{2,1,0:T(8,128)(2,1)S(1)} %pad_maximum_fusion.7.pair), channel_id=1, source_target_pairs={{0,12},{1,13},{2,14},{3,15},{4,8},{5,9},{6,10},{7,11},{8,4},{9,5},... | collective-permute-start | bytes 1179656 | tf_op jit(solution)/shard_map/ppermute | solution.py:16
  141.5 17.5 %collective-permute-start.37 = (bf16[2,64,1536]{2,1,0:T(8,128)(2,1)S(1)}, bf16[2,64,1536]{2,1,0:T(8,128)(2,1)S(1)}, u32[]{:S(2)}, u32[]{:S(2)}) collective-permute-start(bf16[2,64,1536]{2,1,0:T(8,128)(2,1)S(1)} %pad_maximum_fusion.7.pair), channel_id=1, source_target_pairs={{0,8},{1,9},{2,10},{3,11},{4,12},{5,13},{6,14},{7,15},{8,0},{9,1},... | collective-permute-start | bytes 1179656 | tf_op jit(solution)/shard_map/ppermute | solution.py:16
  142.2 16.9 %collective-permute-start.36 = (bf16[2,64,1536]{2,1,0:T(8,128)(2,1)S(1)}, bf16[2,64,1536]{2,1,0:T(8,128)(2,1)S(1)}, u32[]{:S(2)}, u32[]{:S(2)}) collective-permute-start(bf16[2,64,1536]{2,1,0:T(8,128)(2,1)S(1)} %pad_maximum_fusion.7.pair), channel_id=1, source_target_pairs={{0,4},{1,5},{2,6},{3,7},{4,0},{5,1},{6,2},{7,3},{8,12},{9,13},{10,... | collective-permute-start | bytes 1179656 | tf_op jit(solution)/shard_map/ppermute | solution.py:16
  143.4 7.3 %collective-permute-start.39 = (f32[8,1280]{1,0:T(8,128)S(1)}, f32[8,1280]{1,0:T(8,128)S(1)}, u32[]{:S(2)}, u32[]{:S(2)}) collective-permute-start(f32[8,1280]{1,0:T(8,128)S(1)} %add.88), channel_id=1, source_target_pairs={{0,128},{16,144},{32,160},{48,176},{64,192},{80,208},{96,224},{112... | collective-permute-start | bytes 122888 | tf_op jit(solution)/shard_map/ppermute | solution.py:16
  150.6 3.1 %collective-permute-start.40 = (f32[8,1280]{1,0:T(8,128)S(1)}, f32[8,1280]{1,0:T(8,128)S(1)}, u32[]{:S(2)}, u32[]{:S(2)}) collective-permute-start(f32[8,1280]{1,0:T(8,128)S(1)} %add.89), channel_id=1, source_target_pairs={{0,16},{16,0},{32,48},{48,32},{64,80},{80,64},{96,112},{112,96},{1... | collective-permute-start | bytes 122888 | tf_op jit(solution)/shard_map/ppermute | solution.py:16
  153.8 4.4 %collective-permute-start.41 = (f32[8,1280]{1,0:T(8,128)S(1)}, f32[8,1280]{1,0:T(8,128)S(1)}, u32[]{:S(2)}, u32[]{:S(2)}) collective-permute-start(f32[8,1280]{1,0:T(8,128)S(1)} %add.90), channel_id=1, source_target_pairs={{0,32},{16,48},{32,0},{48,16},{64,96},{80,112},{96,64},{112,80},{1... | collective-permute-start | bytes 122888 | tf_op jit(solution)/shard_map/ppermute | solution.py:16
  160.3 7.1 %collective-permute-start.42 = (f32[128,1280]{1,0:T(8,128)S(1)}, f32[128,1280]{1,0:T(8,128)S(1)}, u32[]{:S(2)}, u32[]{:S(2)}) collective-permute-start(f32[128,1280]{1,0:T(8,128)S(1)} %get-tuple-element.111), channel_id=1, source_target_pairs={{0,1},{1,0},{2,3},{3,2},{4,5},{5,4},{6,7},{7,6},{8,9},{9,8},{10,11... | collective-permute-start | bytes 1966088 | tf_op jit(solution)/shard_map/ppermute | solution.py:16

commit v7 on v6

--- a/solution.py
+++ b/solution.py
@@ -182,7 +182,6 @@
         ],
         out_specs=out_specs,
         compiler_params=pltpu.CompilerParams(vmem_limit_bytes=16 * 2**20),
-        cost_estimate=pl.CostEstimate(flops=2048 * big.size, bytes_accessed=2 * big.size, transcendentals=0),
         name="dispatch_grad" if over_tokens else "combine_grad",
     )(rows, big, weight)
 
@@ -284,14 +283,14 @@
 
     units = units_of(w_in, w_out.T)
     l0, r0 = swap(units[0], "dp", 1), swap(units[0], "dp", 3)
+    u2 = swap(units[2], "dp", 8)
     u1 = swap(units[1], "dp", 4)
-    u2 = swap(units[2], "dp", 8)
     table = doubled(slot_params.T, "expert", 2, 4)
-    l0, r0, table = together(l0, r0, table)
     p0, q0 = swap(r0[0], "dp", 1), swap(l0[1], "dp", 3)
-    table = doubled(table, "expert", 8, 1)
-
-    u1, u2, p0, q0, table = together(u1, u2, p0, q0, table)
+    table = doubled(table, "expert", 8)
+    table = doubled(after(table, p0, q0), "expert", 1)
+
+    table, p0, q0, u1, u2 = together(table, p0, q0, u1, u2)
     both = jnp.stack([u1, u2], axis=1)
     lb, rb = swap(both, "dp", 1), swap(both, "dp", 3)
     u3 = swap(after(units[3], u1), "dp", 12)

time: 168 us -> 168 us (level); the launches traced: 168 us -> 166 us
  starting transfers between devices: 94.1 us -> 86.9 us
  waiting for transfers between devices: 47.2 us -> 52.1 us
    ppermute x43, starting transfers between devices: 94.1 us -> 86.9 us  [swap(): return lax.ppermute(value, axis, [(i, i ^ k) for i in range(count)])]
    ppermute x43, waiting for transfers between devices: 47.2 us -> 52.1 us  [swap(): return lax.ppermute(value, axis, [(i, i ^ k) for i in range(count)])]
where the time goes in v7:
time: 168 us; the launch traced here: 166 us
  starting transfers between devices  86.9 us (52%)
  waiting for transfers between devices  52.1 us (31%)
  Pallas kernels  18.9 us (11%)
  local copies, waits for them, and re-layouts  4.23 us (3%)
  other arithmetic  2.05 us (1%)
    ppermute x43, starting transfers between devices, swap(): return lax.ppermute(value, axis, [(i, i ^ k) for i in range(count)])  86.9 us
    ppermute x43, waiting for transfers between devices, swap(): return lax.ppermute(value, axis, [(i, i ^ k) for i in range(count)])  52.1 us
    pallas_call x1, Pallas kernels, slots_call(): pl.pallas_call(slots_kernel, grid=(images // 2,), out_shape=[jax.ShapeDty...  9.18 us
    pallas_call x2, Pallas kernels, against(): pl.pallas_call(lambda *refs: against_kernel(over_tokens, *refs), grid=(im...  4.38 us
    pallas_call x1, Pallas kernels, ffn(): pl.pallas_call(ffn_kernel, out_shape=[jax.ShapeDtypeStruct((own_rows, wid...  4.04 us
  transfers between devices with their start and end apart: 43, of which 22 were waited for; matrix products, arithmetic and copies ran while one was open for 1% of the time, Pallas kernels for 8%

profile of v7, /device:TPU:1, one launch (start us, length us, event | category | flops | bytes accessed | tf_op | source)
XLA Modules:
  0.0 165.9 jit_solution(1772862275395521035)
XLA Ops:
  0.7 1.4 dynamic-slice_bitcast_fusion.1
  2.3 2.2 %collective-permute-start.5 = (bf16[2,80,1280]{2,1,0:T(8,128)(2,1)S(1)}, bf16[2,80,1280]{2,1,0:T(8,128)(2,1)S(1)}, u32[]{:S(2)}, u32[]{:S(2)}) collective-permute-start(bf16[2,80,1280]{2,1,0:T(8,128)(2,1)S(1)} %pad_maximum_fusion.3.refs_0_), channel_id=1, source_target_pairs={{0,16},{16,0},{32,48},{48,32},{64,80},{80,64},{96,112},{112,96},{1... | collective-permute-start | bytes 1228808 | tf_op jit(solution)/shard_map/ppermute | solution.py:16
  4.5 1.9 %collective-permute-start.3 = (bf16[2,80,1280]{2,1,0:T(8,128)(2,1)S(1)}, bf16[2,80,1280]{2,1,0:T(8,128)(2,1)S(1)}, u32[]{:S(2)}, u32[]{:S(2)}) collective-permute-start(bf16[2,80,1280]{2,1,0:T(8,128)(2,1)S(1)} %pad_maximum_fusion.3.refs_0_), channel_id=1, source_target_pairs={{0,48},{16,32},{32,16},{48,0},{64,112},{80,96},{96,80},{112,64},{1... | collective-permute-start | bytes 1228808 | tf_op jit(solution)/shard_map/ppermute | solution.py:16
  6.4 6.9 %collective-permute-start = (bf16[8,1280]{1,0:T(8,128)(2,1)S(1)}, bf16[8,1280]{1,0:T(8,128)(2,1)S(1)}, u32[]{:S(2)}, u32[]{:S(2)}) collective-permute-start(bf16[8,1280]{1,0:T(8,128)(2,1)S(1)} %bitcast.68), channel_id=1, source_target_pairs={{0,2},{1,3},{2,0},{3,1},{4,6},{5,7},{6,4},{7,5},{8,10},{9,11},{10,... | collective-permute-start | bytes 61448 | tf_op jit(solution)/shard_map/ppermute | solution.py:16
  13.3 1.3 collective-permute-start.9
  14.6 1.2 collective-permute-start.1
  15.9 0.8 collective-permute-start.8
  16.7 0.8 collective-permute-done.1
  17.5 2.7 %collective-permute-start.2 = (bf16[32,1280]{1,0:T(8,128)(2,1)S(1)}, bf16[32,1280]{1,0:T(8,128)(2,1)S(1)}, u32[]{:S(2)}, u32[]{:S(2)}) collective-permute-start(bf16[32,1280]{1,0:T(8,128)(2,1)S(1)} %pad_maximum_fusion.11), channel_id=1, source_target_pairs={{0,8},{1,9},{2,10},{3,11},{4,12},{5,13},{6,14},{7,15},{8,0},{9,1},... | collective-permute-start | bytes 245768 | tf_op jit(solution)/shard_map/ppermute | solution.py:16
  20.2 1.2 collective-permute-start.6
  21.5 1.2 collective-permute-done.2
  22.7 3.6 %collective-permute-done.6.refs_4_ = bf16[80,1280]{1,0:T(8,128)(2,1)S(1)} collective-permute-done((bf16[80,1280]{1,0:T(8,128)(2,1)S(1)}, bf16[80,1280]{1,0:T(8,128)(2,1)S(1)}, u32[]{:S(2)}, u32[]{:S(2)}) %collective-permute-start.6) | collective-permute-done | bytes 204832 | tf_op jit(solution)/shard_map/ppermute | solution.py:16
  26.4 4.3 %collective-permute-start.7 = (bf16[64,1280]{1,0:T(8,128)(2,1)S(1)}, bf16[64,1280]{1,0:T(8,128)(2,1)S(1)}, u32[]{:S(2)}, u32[]{:S(2)}) collective-permute-start(bf16[64,1280]{1,0:T(8,128)(2,1)S(1)} %pad_maximum_fusion.10), channel_id=1, source_target_pairs={{0,1},{1,0},{2,3},{3,2},{4,5},{5,4},{6,7},{7,6},{8,9},{9,8},{10,11... | collective-permute-start | bytes 491528 | tf_op jit(solution)/shard_map/ppermute | solution.py:16
  30.7 1.0 collective-permute-done.7
  31.8 2.4 %collective-permute-done.9 = bf16[2,80,1280]{2,1,0:T(8,128)(2,1)S(1)} collective-permute-done((bf16[2,80,1280]{2,1,0:T(8,128)(2,1)S(1)}, bf16[2,80,1280]{2,1,0:T(8,128)(2,1)S(1)}, u32[]{:S(2)}, u32[]{:S(2)}) %collective-permute-start.9) | collective-permute-done | bytes 409632 | tf_op jit(solution)/shard_map/ppermute | solution.py:16
  34.3 0.9 collective-permute-start.11
  35.2 2.2 %collective-permute-start.12 = (bf16[2,80,1280]{2,1,0:T(8,128)(2,1)S(1)}, bf16[2,80,1280]{2,1,0:T(8,128)(2,1)S(1)}, u32[]{:S(2)}, u32[]{:S(2)}) collective-permute-start(bf16[2,80,1280]{2,1,0:T(8,128)(2,1)S(1)} %pad_maximum_fusion.6), channel_id=1, source_target_pairs={{0,192},{16,208},{32,224},{48,240},{64,128},{80,144},{96,160},{112... | collective-permute-start | bytes 1228808 | tf_op jit(solution)/shard_map/ppermute | solution.py:16
  37.4 2.5 %copy-done.1 = bf16[8,256,1280]{2,1,0:T(8,128)(2,1)S(1)} copy-done((bf16[8,256,1280]{2,1,0:T(8,128)(2,1)S(1)}, bf16[8,256,1280]{2,1,0:T(8,128)(2,1)}, u32[]{:S(2)}) %copy-start.1) | copy-done | bytes 5242904
  39.9 9.2 %slots.1 = (bf16[2,64,1280]{2,1,0:T(8,128)(2,1)S(1)}, f32[64,256]{1,0:T(8,128)S(1)}, f32[64,256]{1,0:T(8,128)S(1)}, bf16[2,128,512]{2,1,0:T(8,128)(2,1)S(1)}) custom-call(bf16[128,1280]{1,0:T(8,128)(2,1)S(1)} %pad_maximum_fusion.8.table, bf16[8,256,1280]{2,1,0:T(8,128)(2,1)S(1)} %copy-done, bf16[8,256,1280]{2,1,0:T(8,128)(2,1)S(1)} %copy-done.1), custom_call_target="tpu_custom_call" | custom-call | flops 838860800 | bytes 10485760 | tf_op jit(solution)/shard_map/slots/pallas_call | solution.py:117
  49.1 4.4 %collective-permute-done.11.refs_7_ = bf16[2,2,80,1280]{3,2,1,0:T(8,128)(2,1)S(1)} collective-permute-done((bf16[2,2,80,1280]{3,2,1,0:T(8,128)(2,1)S(1)}, bf16[2,2,80,1280]{3,2,1,0:T(8,128)(2,1)S(1)}, u32[]{:S(2)}, u32[]{:S(2)}) %collective-permute-start.11) | collective-permute-done | bytes 819232 | tf_op jit(solution)/shard_map/ppermute | solution.py:16
  53.5 1.4 collective-permute-start.13
  54.9 1.2 collective-permute-start.15
  56.2 1.6 collective-permute-start.18
  57.8 7.0 %collective-permute-done.13 = bf16[128,1280]{1,0:T(8,128)(2,1)S(1)} collective-permute-done((bf16[128,1280]{1,0:T(8,128)(2,1)S(1)}, bf16[128,1280]{1,0:T(8,128)(2,1)S(1)}, u32[]{:S(2)}, u32[]{:S(2)}) %collective-permute-start.13) | collective-permute-done | bytes 327712 | tf_op jit(solution)/shard_map/ppermute | solution.py:16
  64.8 0.4 collective-permute-start.17
  65.2 4.0 %collective-permute-done.16 = bf16[128,1280]{1,0:T(8,128)(2,1)S(1)} collective-permute-done((bf16[128,1280]{1,0:T(8,128)(2,1)S(1)}, bf16[128,1280]{1,0:T(8,128)(2,1)S(1)}, u32[]{:S(2)}, u32[]{:S(2)}) %collective-permute-start.16) | collective-permute-done | bytes 327712 | tf_op jit(solution)/shard_map/ppermute | solution.py:16
  69.3 1.0 collective-permute-start.20
  70.3 1.6 collective-permute-start.19
  72.0 0.8 collective-permute-done.17.refs_8_
  72.9 4.9 %collective-permute-done.20.refs_14_ = bf16[80,1280]{1,0:T(8,128)(2,1)S(1)} collective-permute-done((bf16[80,1280]{1,0:T(8,128)(2,1)S(1)}, bf16[80,1280]{1,0:T(8,128)(2,1)S(1)}, u32[]{:S(2)}, u32[]{:S(2)}) %collective-permute-start.20) | collective-permute-done | bytes 204832 | tf_op jit(solution)/shard_map/ppermute | solution.py:16
  77.8 1.4 collective-permute-done.21
  79.3 4.0 %ffn.1 = (f32[64,1280]{1,0:T(8,128)S(1)}, bf16[64,1280]{1,0:T(8,128)(2,1)S(1)}, bf16[64,1280]{1,0:T(8,128)(2,1)S(1)}, bf16[64,1280]{1,0:T(8,128)(2,1)S(1)}, f32[...) custom-call(bf16[256,1280]{1,0:T(8,128)(2,1)S(1)} %get-tuple-element, ...), custom_call_target="tpu_custom_call" | custom-call | tf_op jit(solution)/shard_map/ffn/pallas_call | solution.py:61
  83.4 1.3 collective-permute-start.26
  84.8 2.2 %collective-permute-start.27 = (bf16[64,1280]{1,0:T(8,128)(2,1)S(1)}, bf16[64,1280]{1,0:T(8,128)(2,1)S(1)}, u32[]{:S(2)}, u32[]{:S(2)}) collective-permute-start(bf16[64,1280]{1,0:T(8,128)(2,1)S(1)} %get-tuple-element.87), channel_id=1, source_target_pairs={{0,192},{16,208},{32,224},{48,240},{64,128},{80,144},{96,160},{112... | collective-permute-start | bytes 491528 | tf_op jit(solution)/shard_map/ppermute | solution.py:16
  87.0 1.3 collective-permute-start.23
  88.3 0.4 collective-permute-done.25
  88.7 1.8 %collective-permute-start.24 = (bf16[64,1280]{1,0:T(8,128)(2,1)S(1)}, bf16[64,1280]{1,0:T(8,128)(2,1)S(1)}, u32[]{:S(2)}, u32[]{:S(2)}) collective-permute-start(bf16[64,1280]{1,0:T(8,128)(2,1)S(1)} %get-tuple-element.79), channel_id=1, source_target_pairs={{0,192},{16,208},{32,224},{48,240},{64,128},{80,144},{96,160},{112... | collective-permute-start | bytes 491528 | tf_op jit(solution)/shard_map/ppermute | solution.py:16
  90.5 1.2 collective-permute-done.26
  91.8 0.9 collective-permute-done.27
  92.8 2.1 %combine_grad.1 = (f32[64,256]{1,0:T(8,128)S(1)}, f32[8,256]{1,0:T(8,128)S(1)}) custom-call(f32[64,1280]{1,0:T(8,128)S(1)} %add_add_fusion.refs_0_, bf16[8,256,1280]{2,1,0:T(8,128)(2,1)S(1)} %bitcast.60, f32[64,256]{1,0:T(8,128)S(1)} %get-tuple-element.91.refs_2_), custom_call_target="tpu_custom_call" | custom-call | tf_op jit(solution)/shard_map/combine_grad/pallas_call | solution.py:174
  94.9 18.2 %collective-permute-start.30 = (f32[8,256]{1,0:T(8,128)S(1)}, f32[8,256]{1,0:T(8,128)S(1)}, u32[]{:S(2)}, u32[]{:S(2)}) collective-permute-start(f32[8,256]{1,0:T(8,128)S(1)} %get-tuple-element.93), channel_id=1, source_target_pairs={{0,3},{1,2},{2,1},{3,0},{4,7},{5,6},{6,5},{7,4},{8,11},{9,10},{10,... | collective-permute-start | bytes 24584 | tf_op jit(solution)/shard_map/ppermute | solution.py:16
  113.1 0.5 collective-permute-start.28
  113.6 0.8 collective-permute-done.30
  114.4 5.2 %collective-permute-done.29 = f32[8,256]{1,0:T(8,128)S(1)} collective-permute-done((f32[8,256]{1,0:T(8,128)S(1)}, f32[8,256]{1,0:T(8,128)S(1)}, u32[]{:S(2)}, u32[]{:S(2)}) %collective-permute-start.29) | collective-permute-done | bytes 8224 | tf_op jit(solution)/shard_map/ppermute | solution.py:16
  119.7 1.5 collective-permute-start.32
  121.2 1.7 %collective-permute-start.31 = (f32[8,256]{1,0:T(8,128)S(1)}, f32[8,256]{1,0:T(8,128)S(1)}, u32[]{:S(2)}, u32[]{:S(2)}) collective-permute-start(f32[8,256]{1,0:T(8,128)S(1)} %add_add_fusion.3), channel_id=1, source_target_pairs={{0,4},{1,5},{2,6},{3,7},{4,0},{5,1},{6,2},{7,3},{8,12},{9,13},{10,... | collective-permute-start | bytes 24584 | tf_op jit(solution)/shard_map/ppermute | solution.py:16
  123.0 2.3 %dispatch_grad.1 = f32[64,256]{1,0:T(8,128)S(1)} custom-call(f32[64,1280]{1,0:T(8,128)S(1)} %get-tuple-element.109.refs_0_, bf16[8,256,1280]{2,1,0:T(8,128)(2,1)S(1)} %copy-done, f32[64,256]{1,0:T(8,128)S(1)} %get-tuple-element.83.refs_2_), custom_call_target="tpu_custom_call" | custom-call | tf_op jit(solution)/shard_map/dispatch_grad/pallas_call | solution.py:174
  125.7 0.8 convolution_bitcast_fusion
  126.5 9.0 %collective-permute-start.34 = (f32[8,1280]{1,0:T(8,128)S(1)}, f32[8,1280]{1,0:T(8,128)S(1)}, u32[]{:S(2)}, u32[]{:S(2)}) collective-permute-start(f32[8,1280]{1,0:T(8,128)S(1)} %convolution_bitcast_fusion), channel_id=1, source_target_pairs={{0,64},{16,80},{32,96},{48,112},{64,0},{80,16},{96,32},{112,48},{1... | collective-permute-start | bytes 122888 | tf_op jit(solution)/shard_map/ppermute | solution.py:16
  135.6 2.8 %collective-permute-done.34 = f32[8,1280]{1,0:T(8,128)S(1)} collective-permute-done((f32[8,1280]{1,0:T(8,128)S(1)}, f32[8,1280]{1,0:T(8,128)S(1)}, u32[]{:S(2)}, u32[]{:S(2)}) %collective-permute-start.34) | collective-permute-done | bytes 40992 | tf_op jit(solution)/shard_map/ppermute | solution.py:16
  138.4 1.4 collective-permute-start.38
  139.8 1.1 collective-permute-start.37
  140.9 0.9 collective-permute-start.36
  141.8 7.1 %collective-permute-start.39 = (f32[8,1280]{1,0:T(8,128)S(1)}, f32[8,1280]{1,0:T(8,128)S(1)}, u32[]{:S(2)}, u32[]{:S(2)}) collective-permute-start(f32[8,1280]{1,0:T(8,128)S(1)} %add.88), channel_id=1, source_target_pairs={{0,128},{16,144},{32,160},{48,176},{64,192},{80,208},{96,224},{112... | collective-permute-start | bytes 122888 | tf_op jit(solution)/shard_map/ppermute | solution.py:16
  148.9 1.7 %collective-permute-done.39 = f32[8,1280]{1,0:T(8,128)S(1)} collective-permute-done((f32[8,1280]{1,0:T(8,128)S(1)}, f32[8,1280]{1,0:T(8,128)S(1)}, u32[]{:S(2)}, u32[]{:S(2)}) %collective-permute-start.39) | collective-permute-done | bytes 40992 | tf_op jit(solution)/shard_map/ppermute | solution.py:16
  150.6 1.5 collective-permute-start.40
  152.1 1.7 %collective-permute-done.40 = f32[8,1280]{1,0:T(8,128)S(1)} collective-permute-done((f32[8,1280]{1,0:T(8,128)S(1)}, f32[8,1280]{1,0:T(8,128)S(1)}, u32[]{:S(2)}, u32[]{:S(2)}) %collective-permute-start.40) | collective-permute-done | bytes 40992 | tf_op jit(solution)/shard_map/ppermute | solution.py:16
  153.8 0.6 collective-permute-start.41
  154.4 3.8 %collective-permute-done.41 = f32[8,1280]{1,0:T(8,128)S(1)} collective-permute-done((f32[8,1280]{1,0:T(8,128)S(1)}, f32[8,1280]{1,0:T(8,128)S(1)}, u32[]{:S(2)}, u32[]{:S(2)}) %collective-permute-start.41) | collective-permute-done | bytes 40992 | tf_op jit(solution)/shard_map/ppermute | solution.py:16
  158.1 0.6 add.91
  158.8 1.3 token_grad.1
  160.1 3.3 %collective-permute-start.42 = (f32[128,1280]{1,0:T(8,128)S(1)}, f32[128,1280]{1,0:T(8,128)S(1)}, u32[]{:S(2)}, u32[]{:S(2)}) collective-permute-start(f32[128,1280]{1,0:T(8,128)S(1)} %get-tuple-element.107), channel_id=1, source_target_pairs={{0,1},{1,0},{2,3},{3,2},{4,5},{5,4},{6,7},{7,6},{8,9},{9,8},{10,11... | collective-permute-start | bytes 1966088 | tf_op jit(solution)/shard_map/ppermute | solution.py:16
  163.3 1.7 %collective-permute-done.42 = f32[128,1280]{1,0:T(8,128)S(1)} collective-permute-done((f32[128,1280]{1,0:T(8,128)S(1)}, f32[128,1280]{1,0:T(8,128)S(1)}, u32[]{:S(2)}, u32[]{:S(2)}) %collective-permute-start.42) | collective-permute-done | bytes 655392 | tf_op jit(solution)/shard_map/ppermute | solution.py:16
  165.1 0.8 add_convert_fusion
  (75 shorter events, 1.8 us)
Async XLA Ops:
  0.6 1.5 copy-start.2
  2.1 4.2 %copy-start.3 = (bf16[1280,8]{0,1:T(8,128)(2,1)S(1)}, bf16[1280,8]{0,1:T(8,128)(2,1)}, u32[]{:S(2)}) copy-start(bf16[1280,8]{0,1:T(8,128)(2,1)} %param.7) | copy-start | bytes 61444
  2.3 18.0 %collective-permute-start.5 = (bf16[2,80,1280]{2,1,0:T(8,128)(2,1)S(1)}, bf16[2,80,1280]{2,1,0:T(8,128)(2,1)S(1)}, u32[]{:S(2)}, u32[]{:S(2)}) collective-permute-start(bf16[2,80,1280]{2,1,0:T(8,128)(2,1)S(1)} %pad_maximum_fusion.3.refs_0_), channel_id=1, source_target_pairs={{0,16},{16,0},{32,48},{48,32},{64,80},{80,64},{96,112},{112,96},{1... | collective-permute-start | bytes 1228808 | tf_op jit(solution)/shard_map/ppermute | solution.py:16
  4.5 16.9 %collective-permute-start.3 = (bf16[2,80,1280]{2,1,0:T(8,128)(2,1)S(1)}, bf16[2,80,1280]{2,1,0:T(8,128)(2,1)S(1)}, u32[]{:S(2)}, u32[]{:S(2)}) collective-permute-start(bf16[2,80,1280]{2,1,0:T(8,128)(2,1)S(1)} %pad_maximum_fusion.3.refs_0_), channel_id=1, source_target_pairs={{0,48},{16,32},{32,16},{48,0},{64,112},{80,96},{96,80},{112,64},{1... | collective-permute-start | bytes 1228808 | tf_op jit(solution)/shard_map/ppermute | solution.py:16
  6.4 8.2 %collective-permute-start = (bf16[8,1280]{1,0:T(8,128)(2,1)S(1)}, bf16[8,1280]{1,0:T(8,128)(2,1)S(1)}, u32[]{:S(2)}, u32[]{:S(2)}) collective-permute-start(bf16[8,1280]{1,0:T(8,128)(2,1)S(1)} %bitcast.68), channel_id=1, source_target_pairs={{0,2},{1,3},{2,0},{3,1},{4,6},{5,7},{6,4},{7,5},{8,10},{9,11},{10,... | collective-permute-start | bytes 61448 | tf_op jit(solution)/shard_map/ppermute | solution.py:16
  13.3 20.9 %collective-permute-start.9 = (bf16[2,80,1280]{2,1,0:T(8,128)(2,1)S(1)}, bf16[2,80,1280]{2,1,0:T(8,128)(2,1)S(1)}, u32[]{:S(2)}, u32[]{:S(2)}) collective-permute-start(bf16[2,80,1280]{2,1,0:T(8,128)(2,1)S(1)} %pad_maximum_fusion.5), channel_id=1, source_target_pairs={{0,128},{16,144},{32,160},{48,176},{64,192},{80,208},{96,224},{112... | collective-permute-start | bytes 1228808 | tf_op jit(solution)/shard_map/ppermute | solution.py:16
  14.6 2.9 %collective-permute-start.1 = (bf16[16,1280]{1,0:T(8,128)(2,1)S(1)}, bf16[16,1280]{1,0:T(8,128)(2,1)S(1)}, u32[]{:S(2)}, u32[]{:S(2)}) collective-permute-start(bf16[16,1280]{1,0:T(8,128)(2,1)S(1)} %pad_maximum_fusion.12), channel_id=1, source_target_pairs={{0,4},{1,5},{2,6},{3,7},{4,0},{5,1},{6,2},{7,3},{8,12},{9,13},{10,... | collective-permute-start | bytes 122888 | tf_op jit(solution)/shard_map/ppermute | solution.py:16
  15.8 21.6 %copy-start = (bf16[8,256,1280]{2,1,0:T(8,128)(2,1)S(1)}, bf16[8,256,1280]{2,1,0:T(8,128)(2,1)}, u32[]{:S(2)}) copy-start(bf16[8,256,1280]{2,1,0:T(8,128)(2,1)} %refs_1_.2) | copy-start | bytes 15728644
  15.9 18.4 %collective-permute-start.8 = (bf16[2,80,1280]{2,1,0:T(8,128)(2,1)S(1)}, bf16[2,80,1280]{2,1,0:T(8,128)(2,1)S(1)}, u32[]{:S(2)}, u32[]{:S(2)}) collective-permute-start(bf16[2,80,1280]{2,1,0:T(8,128)(2,1)S(1)} %pad_maximum_fusion.4), channel_id=1, source_target_pairs={{0,64},{16,80},{32,96},{48,112},{64,0},{80,16},{96,32},{112,48},{1... | collective-permute-start | bytes 1228808 | tf_op jit(solution)/shard_map/ppermute | solution.py:16
  17.5 5.2 %collective-permute-start.2 = (bf16[32,1280]{1,0:T(8,128)(2,1)S(1)}, bf16[32,1280]{1,0:T(8,128)(2,1)S(1)}, u32[]{:S(2)}, u32[]{:S(2)}) collective-permute-start(bf16[32,1280]{1,0:T(8,128)(2,1)S(1)} %pad_maximum_fusion.11), channel_id=1, source_target_pairs={{0,8},{1,9},{2,10},{3,11},{4,12},{5,13},{6,14},{7,15},{8,0},{9,1},... | collective-permute-start | bytes 245768 | tf_op jit(solution)/shard_map/ppermute | solution.py:16
  20.2 6.0 %collective-permute-start.6 = (bf16[80,1280]{1,0:T(8,128)(2,1)S(1)}, bf16[80,1280]{1,0:T(8,128)(2,1)S(1)}, u32[]{:S(2)}, u32[]{:S(2)}) collective-permute-start(bf16[80,1280]{1,0:T(8,128)(2,1)S(1)} %slice_bitcast_fusion.2), channel_id=1, source_target_pairs={{0,48},{16,32},{32,16},{48,0},{64,112},{80,96},{96,80},{112,64},{1... | collective-permute-start | bytes 614408 | tf_op jit(solution)/shard_map/ppermute | solution.py:16
  21.4 5.0 %collective-permute-start.4 = (bf16[80,1280]{1,0:T(8,128)(2,1)S(1)}, bf16[80,1280]{1,0:T(8,128)(2,1)S(1)}, u32[]{:S(2)}, u32[]{:S(2)}) collective-permute-start(bf16[80,1280]{1,0:T(8,128)(2,1)S(1)} %slice_bitcast_fusion.3), channel_id=1, source_target_pairs={{0,16},{16,0},{32,48},{48,32},{64,80},{80,64},{96,112},{112,96},{1... | collective-permute-start | bytes 614408 | tf_op jit(solution)/shard_map/ppermute | solution.py:16
  26.4 5.3 %collective-permute-start.7 = (bf16[64,1280]{1,0:T(8,128)(2,1)S(1)}, bf16[64,1280]{1,0:T(8,128)(2,1)S(1)}, u32[]{:S(2)}, u32[]{:S(2)}) collective-permute-start(bf16[64,1280]{1,0:T(8,128)(2,1)S(1)} %pad_maximum_fusion.10), channel_id=1, source_target_pairs={{0,1},{1,0},{2,3},{3,2},{4,5},{5,4},{6,7},{7,6},{8,9},{9,8},{10,11... | collective-permute-start | bytes 491528 | tf_op jit(solution)/shard_map/ppermute | solution.py:16
  34.3 19.2 %collective-permute-start.11 = (bf16[2,2,80,1280]{3,2,1,0:T(8,128)(2,1)S(1)}, bf16[2,2,80,1280]{3,2,1,0:T(8,128)(2,1)S(1)}, u32[]{:S(2)}, u32[]{:S(2)}) collective-permute-start(bf16[2,2,80,1280]{3,2,1,0:T(8,128)(2,1)S(1)} %pad_maximum_fusion.refs_5_), channel_id=1, source_target_pairs={{0,48},{16,32},{32,16},{48,0},{64,112},{80,96},{96,80},{112,64},{1... | collective-permute-start | bytes 2457608 | tf_op jit(solution)/shard_map/ppermute | solution.py:16
  35.2 18.3 %collective-permute-start.10 = (bf16[2,2,80,1280]{3,2,1,0:T(8,128)(2,1)S(1)}, bf16[2,2,80,1280]{3,2,1,0:T(8,128)(2,1)S(1)}, u32[]{:S(2)}, u32[]{:S(2)}) collective-permute-start(bf16[2,2,80,1280]{3,2,1,0:T(8,128)(2,1)S(1)} %pad_maximum_fusion.refs_5_), channel_id=1, source_target_pairs={{0,16},{16,0},{32,48},{48,32},{64,80},{80,64},{96,112},{112,96},{1... | collective-permute-start | bytes 2457608 | tf_op jit(solution)/shard_map/ppermute | solution.py:16
  35.2 13.8 %collective-permute-start.12 = (bf16[2,80,1280]{2,1,0:T(8,128)(2,1)S(1)}, bf16[2,80,1280]{2,1,0:T(8,128)(2,1)S(1)}, u32[]{:S(2)}, u32[]{:S(2)}) collective-permute-start(bf16[2,80,1280]{2,1,0:T(8,128)(2,1)S(1)} %pad_maximum_fusion.6), channel_id=1, source_target_pairs={{0,192},{16,208},{32,224},{48,240},{64,128},{80,144},{96,160},{112... | collective-permute-start | bytes 1228808 | tf_op jit(solution)/shard_map/ppermute | solution.py:16
  37.4 2.5 %copy-start.1 = (bf16[8,256,1280]{2,1,0:T(8,128)(2,1)S(1)}, bf16[8,256,1280]{2,1,0:T(8,128)(2,1)}, u32[]{:S(2)}) copy-start(bf16[8,256,1280]{2,1,0:T(8,128)(2,1)} %refs_1_.3) | copy-start | bytes 15728644
  53.5 15.7 %collective-permute-start.16 = (bf16[128,1280]{1,0:T(8,128)(2,1)S(1)}, bf16[128,1280]{1,0:T(8,128)(2,1)S(1)}, u32[]{:S(2)}, u32[]{:S(2)}) collective-permute-start(bf16[128,1280]{1,0:T(8,128)(2,1)S(1)} %bitcast.61), channel_id=1, source_target_pairs={{0,128},{16,144},{32,160},{48,176},{64,192},{80,208},{96,224},{112... | collective-permute-start | bytes 983048 | tf_op jit(solution)/shard_map/ppermute | solution.py:16
  53.5 11.3 %collective-permute-start.13 = (bf16[128,1280]{1,0:T(8,128)(2,1)S(1)}, bf16[128,1280]{1,0:T(8,128)(2,1)S(1)}, u32[]{:S(2)}, u32[]{:S(2)}) collective-permute-start(bf16[128,1280]{1,0:T(8,128)(2,1)S(1)} %bitcast.62), channel_id=1, source_target_pairs={{0,64},{16,80},{32,96},{48,112},{64,0},{80,16},{96,32},{112,48},{1... | collective-permute-start | bytes 983048 | tf_op jit(solution)/shard_map/ppermute | solution.py:16
  54.9 14.3 %collective-permute-start.15 = (bf16[2,80,1280]{2,1,0:T(8,128)(2,1)S(1)}, bf16[2,80,1280]{2,1,0:T(8,128)(2,1)S(1)}, u32[]{:S(2)}, u32[]{:S(2)}) collective-permute-start(bf16[2,80,1280]{2,1,0:T(8,128)(2,1)S(1)} %collective-permute-done.12.refs_10_), channel_id=1, source_target_pairs={{0,48},{16,32},{32,16},{48,0},{64,112},{80,96},{96,80},{112,64},{1... | collective-permute-start | bytes 1228808 | tf_op jit(solution)/shard_map/ppermute | solution.py:16
  56.1 13.1 %collective-permute-start.14 = (bf16[2,80,1280]{2,1,0:T(8,128)(2,1)S(1)}, bf16[2,80,1280]{2,1,0:T(8,128)(2,1)S(1)}, u32[]{:S(2)}, u32[]{:S(2)}) collective-permute-start(bf16[2,80,1280]{2,1,0:T(8,128)(2,1)S(1)} %collective-permute-done.12.refs_10_), channel_id=1, source_target_pairs={{0,16},{16,0},{32,48},{48,32},{64,80},{80,64},{96,112},{112,96},{1... | collective-permute-start | bytes 1228808 | tf_op jit(solution)/shard_map/ppermute | solution.py:16
  56.2 15.8 %collective-permute-start.18 = (bf16[2,80,1280]{2,1,0:T(8,128)(2,1)S(1)}, bf16[2,80,1280]{2,1,0:T(8,128)(2,1)S(1)}, u32[]{:S(2)}, u32[]{:S(2)}) collective-permute-start(bf16[2,80,1280]{2,1,0:T(8,128)(2,1)S(1)} %slice_bitcast_fusion), channel_id=1, source_target_pairs={{0,48},{16,32},{32,16},{48,0},{64,112},{80,96},{96,80},{112,64},{1... | collective-permute-start | bytes 1228808 | tf_op jit(solution)/shard_map/ppermute | solution.py:16
  64.8 8.1 %collective-permute-start.17 = (bf16[2,80,1280]{2,1,0:T(8,128)(2,1)S(1)}, bf16[2,80,1280]{2,1,0:T(8,128)(2,1)S(1)}, u32[]{:S(2)}, u32[]{:S(2)}) collective-permute-start(bf16[2,80,1280]{2,1,0:T(8,128)(2,1)S(1)} %slice_bitcast_fusion.1), channel_id=1, source_target_pairs={{0,16},{16,0},{32,48},{48,32},{64,80},{80,64},{96,112},{112,96},{1... | collective-permute-start | bytes 1228808 | tf_op jit(solution)/shard_map/ppermute | solution.py:16
  69.3 8.5 %collective-permute-start.20 = (bf16[80,1280]{1,0:T(8,128)(2,1)S(1)}, bf16[80,1280]{1,0:T(8,128)(2,1)S(1)}, u32[]{:S(2)}, u32[]{:S(2)}) collective-permute-start(bf16[80,1280]{1,0:T(8,128)(2,1)S(1)} %slice_bitcast_fusion.4), channel_id=1, source_target_pairs={{0,48},{16,32},{32,16},{48,0},{64,112},{80,96},{96,80},{112,64},{1... | collective-permute-start | bytes 614408 | tf_op jit(solution)/shard_map/ppermute | solution.py:16
  70.3 7.4 %collective-permute-start.19 = (bf16[80,1280]{1,0:T(8,128)(2,1)S(1)}, bf16[80,1280]{1,0:T(8,128)(2,1)S(1)}, u32[]{:S(2)}, u32[]{:S(2)}) collective-permute-start(bf16[80,1280]{1,0:T(8,128)(2,1)S(1)} %slice_bitcast_fusion.5), channel_id=1, source_target_pairs={{0,16},{16,0},{32,48},{48,32},{64,80},{80,64},{96,112},{112,96},{1... | collective-permute-start | bytes 614408 | tf_op jit(solution)/shard_map/ppermute | solution.py:16
  72.0 7.2 %collective-permute-start.21 = (bf16[128,1280]{1,0:T(8,128)(2,1)S(1)}, bf16[128,1280]{1,0:T(8,128)(2,1)S(1)}, u32[]{:S(2)}, u32[]{:S(2)}) collective-permute-start(bf16[128,1280]{1,0:T(8,128)(2,1)S(1)} %collective-permute-done.16), channel_id=1, source_target_pairs={{0,64},{16,80},{32,96},{48,112},{64,0},{80,16},{96,32},{112,48},{1... | collective-permute-start | bytes 983048 | tf_op jit(solution)/shard_map/ppermute | solution.py:16
  79.2 13.6 %slice-start = ((s8[5242880]{0:T(1024)(128)(4,1)}), s8[4194304]{0:T(1024)(128)(4,1)S(1)}, s32[]{:S(2)}) async-start(s8[5242880]{0:T(1024)(128)(4,1)} %bitcast.59), calls=%async_computation | async-start | bytes 8388608
  79.3 13.5 %slice-start.1 = ((s8[5242880]{0:T(1024)(128)(4,1)}), s8[1048576]{0:T(1024)(128)(4,1)S(1)}, s32[]{:S(2)}) async-start(s8[5242880]{0:T(1024)(128)(4,1)} %bitcast.59), calls=%async_computation.1 | async-start | bytes 2097152
  83.3 5.4 %collective-permute-start.25 = (bf16[64,1280]{1,0:T(8,128)(2,1)S(1)}, bf16[64,1280]{1,0:T(8,128)(2,1)S(1)}, u32[]{:S(2)}, u32[]{:S(2)}) collective-permute-start(bf16[64,1280]{1,0:T(8,128)(2,1)S(1)} %get-tuple-element.85), channel_id=1, source_target_pairs={{0,64},{16,80},{32,96},{48,112},{64,0},{80,16},{96,32},{112,48},{1... | collective-permute-start | bytes 491528 | tf_op jit(solution)/shard_map/ppermute | solution.py:16
  83.4 8.3 %collective-permute-start.26 = (bf16[64,1280]{1,0:T(8,128)(2,1)S(1)}, bf16[64,1280]{1,0:T(8,128)(2,1)S(1)}, u32[]{:S(2)}, u32[]{:S(2)}) collective-permute-start(bf16[64,1280]{1,0:T(8,128)(2,1)S(1)} %get-tuple-element.86), channel_id=1, source_target_pairs={{0,128},{16,144},{32,160},{48,176},{64,192},{80,208},{96,224},{112... | collective-permute-start | bytes 491528 | tf_op jit(solution)/shard_map/ppermute | solution.py:16
  84.8 7.9 %collective-permute-start.27 = (bf16[64,1280]{1,0:T(8,128)(2,1)S(1)}, bf16[64,1280]{1,0:T(8,128)(2,1)S(1)}, u32[]{:S(2)}, u32[]{:S(2)}) collective-permute-start(bf16[64,1280]{1,0:T(8,128)(2,1)S(1)} %get-tuple-element.87), channel_id=1, source_target_pairs={{0,192},{16,208},{32,224},{48,240},{64,128},{80,144},{96,160},{112... | collective-permute-start | bytes 491528 | tf_op jit(solution)/shard_map/ppermute | solution.py:16
  87.0 26.1 %collective-permute-start.22 = (bf16[64,1280]{1,0:T(8,128)(2,1)S(1)}, bf16[64,1280]{1,0:T(8,128)(2,1)S(1)}, u32[]{:S(2)}, u32[]{:S(2)}) collective-permute-start(bf16[64,1280]{1,0:T(8,128)(2,1)S(1)} %get-tuple-element.77), channel_id=1, source_target_pairs={{0,64},{16,80},{32,96},{48,112},{64,0},{80,16},{96,32},{112,48},{1... | collective-permute-start | bytes 491528 | tf_op jit(solution)/shard_map/ppermute | solution.py:16
  87.0 26.6 %collective-permute-start.23 = (bf16[64,1280]{1,0:T(8,128)(2,1)S(1)}, bf16[64,1280]{1,0:T(8,128)(2,1)S(1)}, u32[]{:S(2)}, u32[]{:S(2)}) collective-permute-start(bf16[64,1280]{1,0:T(8,128)(2,1)S(1)} %get-tuple-element.78), channel_id=1, source_target_pairs={{0,128},{16,144},{32,160},{48,176},{64,192},{80,208},{96,224},{112... | collective-permute-start | bytes 491528 | tf_op jit(solution)/shard_map/ppermute | solution.py:16
  88.7 24.9 %collective-permute-start.24 = (bf16[64,1280]{1,0:T(8,128)(2,1)S(1)}, bf16[64,1280]{1,0:T(8,128)(2,1)S(1)}, u32[]{:S(2)}, u32[]{:S(2)}) collective-permute-start(bf16[64,1280]{1,0:T(8,128)(2,1)S(1)} %get-tuple-element.79), channel_id=1, source_target_pairs={{0,192},{16,208},{32,224},{48,240},{64,128},{80,144},{96,160},{112... | collective-permute-start | bytes 491528 | tf_op jit(solution)/shard_map/ppermute | solution.py:16
  94.9 19.6 %collective-permute-start.30 = (f32[8,256]{1,0:T(8,128)S(1)}, f32[8,256]{1,0:T(8,128)S(1)}, u32[]{:S(2)}, u32[]{:S(2)}) collective-permute-start(f32[8,256]{1,0:T(8,128)S(1)} %get-tuple-element.93), channel_id=1, source_target_pairs={{0,3},{1,2},{2,1},{3,0},{4,7},{5,6},{6,5},{7,4},{8,11},{9,10},{10,... | collective-permute-start | bytes 24584 | tf_op jit(solution)/shard_map/ppermute | solution.py:16
  113.1 6.5 %collective-permute-start.29 = (f32[8,256]{1,0:T(8,128)S(1)}, f32[8,256]{1,0:T(8,128)S(1)}, u32[]{:S(2)}, u32[]{:S(2)}) collective-permute-start(f32[8,256]{1,0:T(8,128)S(1)} %get-tuple-element.93), channel_id=1, source_target_pairs={{0,2},{1,3},{2,0},{3,1},{4,6},{5,7},{6,4},{7,5},{8,10},{9,11},{10,... | collective-permute-start | bytes 24584 | tf_op jit(solution)/shard_map/ppermute | solution.py:16
  113.1 6.5 %collective-permute-start.28 = (f32[8,256]{1,0:T(8,128)S(1)}, f32[8,256]{1,0:T(8,128)S(1)}, u32[]{:S(2)}, u32[]{:S(2)}) collective-permute-start(f32[8,256]{1,0:T(8,128)S(1)} %get-tuple-element.93), channel_id=1, source_target_pairs={{0,1},{1,0},{2,3},{3,2},{4,5},{5,4},{6,7},{7,6},{8,9},{9,8},{10,11... | collective-permute-start | bytes 24584 | tf_op jit(solution)/shard_map/ppermute | solution.py:16
  119.6 5.7 %collective-permute-start.33 = (f32[8,256]{1,0:T(8,128)S(1)}, f32[8,256]{1,0:T(8,128)S(1)}, u32[]{:S(2)}, u32[]{:S(2)}) collective-permute-start(f32[8,256]{1,0:T(8,128)S(1)} %add_add_fusion.3), channel_id=1, source_target_pairs={{0,12},{1,13},{2,14},{3,15},{4,8},{5,9},{6,10},{7,11},{8,4},{9,5},... | collective-permute-start | bytes 24584 | tf_op jit(solution)/shard_map/ppermute | solution.py:16
  119.7 5.6 %collective-permute-start.32 = (f32[8,256]{1,0:T(8,128)S(1)}, f32[8,256]{1,0:T(8,128)S(1)}, u32[]{:S(2)}, u32[]{:S(2)}) collective-permute-start(f32[8,256]{1,0:T(8,128)S(1)} %add_add_fusion.3), channel_id=1, source_target_pairs={{0,8},{1,9},{2,10},{3,11},{4,12},{5,13},{6,14},{7,15},{8,0},{9,1},... | collective-permute-start | bytes 24584 | tf_op jit(solution)/shard_map/ppermute | solution.py:16
  121.2 4.1 %collective-permute-start.31 = (f32[8,256]{1,0:T(8,128)S(1)}, f32[8,256]{1,0:T(8,128)S(1)}, u32[]{:S(2)}, u32[]{:S(2)}) collective-permute-start(f32[8,256]{1,0:T(8,128)S(1)} %add_add_fusion.3), channel_id=1, source_target_pairs={{0,4},{1,5},{2,6},{3,7},{4,0},{5,1},{6,2},{7,3},{8,12},{9,13},{10,... | collective-permute-start | bytes 24584 | tf_op jit(solution)/shard_map/ppermute | solution.py:16
  125.5 12.9 %collective-permute-start.35 = (bf16[64,1536]{1,0:T(8,128)(2,1)S(1)}, bf16[64,1536]{1,0:T(8,128)(2,1)S(1)}, u32[]{:S(2)}, u32[]{:S(2)}) collective-permute-start(bf16[64,1536]{1,0:T(8,128)(2,1)S(1)} %get-tuple-element.127), channel_id=1, source_target_pairs={{0,2},{1,3},{2,0},{3,1},{4,6},{5,7},{6,4},{7,5},{8,10},{9,11},{10,... | collective-permute-start | bytes 589832 | tf_op jit(solution)/shard_map/ppermute | solution.py:16
  126.5 11.9 %collective-permute-start.34 = (f32[8,1280]{1,0:T(8,128)S(1)}, f32[8,1280]{1,0:T(8,128)S(1)}, u32[]{:S(2)}, u32[]{:S(2)}) collective-permute-start(f32[8,1280]{1,0:T(8,128)S(1)} %convolution_bitcast_fusion), channel_id=1, source_target_pairs={{0,64},{16,80},{32,96},{48,112},{64,0},{80,16},{96,32},{112,48},{1... | collective-permute-start | bytes 122888 | tf_op jit(solution)/shard_map/ppermute | solution.py:16
  138.4 20.3 %collective-permute-start.38 = (bf16[2,64,1536]{2,1,0:T(8,128)(2,1)S(1)}, bf16[2,64,1536]{2,1,0:T(8,128)(2,1)S(1)}, u32[]{:S(2)}, u32[]{:S(2)}) collective-permute-start(bf16[2,64,1536]{2,1,0:T(8,128)(2,1)S(1)} %pad_maximum_fusion.7.pair), channel_id=1, source_target_pairs={{0,12},{1,13},{2,14},{3,15},{4,8},{5,9},{6,10},{7,11},{8,4},{9,5},... | collective-permute-start | bytes 1179656 | tf_op jit(solution)/shard_map/ppermute | solution.py:16
  139.8 19.0 %collective-permute-start.37 = (bf16[2,64,1536]{2,1,0:T(8,128)(2,1)S(1)}, bf16[2,64,1536]{2,1,0:T(8,128)(2,1)S(1)}, u32[]{:S(2)}, u32[]{:S(2)}) collective-permute-start(bf16[2,64,1536]{2,1,0:T(8,128)(2,1)S(1)} %pad_maximum_fusion.7.pair), channel_id=1, source_target_pairs={{0,8},{1,9},{2,10},{3,11},{4,12},{5,13},{6,14},{7,15},{8,0},{9,1},... | collective-permute-start | bytes 1179656 | tf_op jit(solution)/shard_map/ppermute | solution.py:16
  140.9 17.9 %collective-permute-start.36 = (bf16[2,64,1536]{2,1,0:T(8,128)(2,1)S(1)}, bf16[2,64,1536]{2,1,0:T(8,128)(2,1)S(1)}, u32[]{:S(2)}, u32[]{:S(2)}) collective-permute-start(bf16[2,64,1536]{2,1,0:T(8,128)(2,1)S(1)} %pad_maximum_fusion.7.pair), channel_id=1, source_target_pairs={{0,4},{1,5},{2,6},{3,7},{4,0},{5,1},{6,2},{7,3},{8,12},{9,13},{10,... | collective-permute-start | bytes 1179656 | tf_op jit(solution)/shard_map/ppermute | solution.py:16
  141.8 8.8 %collective-permute-start.39 = (f32[8,1280]{1,0:T(8,128)S(1)}, f32[8,1280]{1,0:T(8,128)S(1)}, u32[]{:S(2)}, u32[]{:S(2)}) collective-permute-start(f32[8,1280]{1,0:T(8,128)S(1)} %add.88), channel_id=1, source_target_pairs={{0,128},{16,144},{32,160},{48,176},{64,192},{80,208},{96,224},{112... | collective-permute-start | bytes 122888 | tf_op jit(solution)/shard_map/ppermute | solution.py:16
  150.6 3.2 %collective-permute-start.40 = (f32[8,1280]{1,0:T(8,128)S(1)}, f32[8,1280]{1,0:T(8,128)S(1)}, u32[]{:S(2)}, u32[]{:S(2)}) collective-permute-start(f32[8,1280]{1,0:T(8,128)S(1)} %add.89), channel_id=1, source_target_pairs={{0,16},{16,0},{32,48},{48,32},{64,80},{80,64},{96,112},{112,96},{1... | collective-permute-start | bytes 122888 | tf_op jit(solution)/shard_map/ppermute | solution.py:16
  153.8 4.4 %collective-permute-start.41 = (f32[8,1280]{1,0:T(8,128)S(1)}, f32[8,1280]{1,0:T(8,128)S(1)}, u32[]{:S(2)}, u32[]{:S(2)}) collective-permute-start(f32[8,1280]{1,0:T(8,128)S(1)} %add.90), channel_id=1, source_target_pairs={{0,32},{16,48},{32,0},{48,16},{64,96},{80,112},{96,64},{112,80},{1... | collective-permute-start | bytes 122888 | tf_op jit(solution)/shard_map/ppermute | solution.py:16
  160.1 5.0 %collective-permute-start.42 = (f32[128,1280]{1,0:T(8,128)S(1)}, f32[128,1280]{1,0:T(8,128)S(1)}, u32[]{:S(2)}, u32[]{:S(2)}) collective-permute-start(f32[128,1280]{1,0:T(8,128)S(1)} %get-tuple-element.107), channel_id=1, source_target_pairs={{0,1},{1,0},{2,3},{3,2},{4,5},{5,4},{6,7},{7,6},{8,9},{9,8},{10,11... | collective-permute-start | bytes 1966088 | tf_op jit(solution)/shard_map/ppermute | solution.py:16

commit v8 on v7

--- a/solution.py
+++ b/solution.py
@@ -23,7 +23,7 @@
 def ffn_kernel(rows_in, rows_go, *refs):
     own, l0, r0, p0, q0, both, lb, rb, pb, qb, last, l3, r3, p3, q3 = refs[:15]
     f0, f3 = (p0, q0), (p3, q3)
-    outs, grads, (w1, w2) = refs[15:19], refs[19:23], refs[23:]
+    outs, grads, (w1, w2) = refs[15:21], refs[21:25], refs[25:]
     me = lax.axis_index("dp")
     depth = w1.shape[0] // 16
 
@@ -48,10 +48,12 @@
     slope = cdf + 0.5 * pre * (1.0 - th * th) * (ROOT * (1.0 + 3 * 0.044715 * sq))
     hidden_grad = jnp.dot(rows_go[...], w2[...], preferred_element_type=F32)
     pre_grad = (hidden_grad * slope).astype(BF16)
-    rows = outs[0].shape[0]
     for whole, blocks in ((nt(hidden, w2[...]), outs), (nt(pre_grad, w1[...]), grads)):
-        for a, block in enumerate(blocks):
-            block[...] = whole[a * rows : (a + 1) * rows].astype(block.dtype)
+        start = 0
+        for block in blocks:
+            stop = start + block.shape[0]
+            block[...] = whole[start:stop].astype(block.dtype)
+            start = stop
 
 
 def ffn(rows_in, rows_go, blocks, own_rows):
@@ -60,9 +62,11 @@
     vmem = pl.BlockSpec(memory_space=pltpu.VMEM)
     return pl.pallas_call(
         ffn_kernel,
-        out_shape=[jax.ShapeDtypeStruct((own_rows, width), t) for t in (F32, BF16, BF16, BF16)] * 2,
+        out_shape=[jax.ShapeDtypeStruct((own_rows, width), F32), jax.ShapeDtypeStruct((own_rows, width), BF16)]
+        + [jax.ShapeDtypeStruct((own_rows // 2, width), BF16)] * 4
+        + [jax.ShapeDtypeStruct((own_rows, width), t) for t in (F32, BF16, BF16, BF16)],
         in_specs=[vmem] * (2 + len(blocks)),
-        out_specs=[vmem] * 8,
+        out_specs=[vmem] * 10,
         scratch_shapes=[pltpu.VMEM((width, quarter), BF16), pltpu.VMEM((width, quarter), BF16)],
         compiler_params=pltpu.CompilerParams(vmem_limit_bytes=40 * 2**20),
         name="ffn",
@@ -250,8 +254,17 @@
     return lax.optimization_barrier(values)
 
 
-def reduce_z(own, *far):
-    one, two, three = together(*[swap(v, "dp", 4 * a) for a, v in enumerate(far, 1)])
+def sent_z(blocks):
+    places = (1, 2, 3) if len(blocks) == 3 else (1, 2, 2, 3, 3)
+    return [swap(v, "dp", 4 * a) for a, v in zip(places, blocks)]
+
+
+def added(own, *parts):
+    parts = together(*parts)
+    if len(parts) > 3:
+        one, two, two_b, three, three_b = parts
+        parts = one, jnp.concatenate([two, two_b], axis=0), jnp.concatenate([three, three_b], axis=0)
+    one, two, three = parts
     return (own + one.astype(F32)) + (two.astype(F32) + three.astype(F32))
 
 
@@ -285,15 +298,16 @@
     l0, r0 = swap(units[0], "dp", 1), swap(units[0], "dp", 3)
     u2 = swap(units[2], "dp", 8)
     u1 = swap(units[1], "dp", 4)
-    table = doubled(slot_params.T, "expert", 2, 4)
+    table = doubled(slot_params.T, "expert", 4, 1)
     p0, q0 = swap(r0[0], "dp", 1), swap(l0[1], "dp", 3)
     table = doubled(table, "expert", 8)
-    table = doubled(after(table, p0, q0), "expert", 1)
+    table = doubled(after(table, p0, q0), "expert", 2)
 
     table, p0, q0, u1, u2 = together(table, p0, q0, u1, u2)
     both = jnp.stack([u1, u2], axis=1)
     lb, rb = swap(both, "dp", 1), swap(both, "dp", 3)
     u3 = swap(after(units[3], u1), "dp", 12)
+    table = table.reshape(2, 2, 2, 2, own, width).transpose(2, 1, 3, 0, 4, 5).reshape(-1, width)
     rows, dispatch, combine, spread = slots_call(table, tokens, out_grad)
     rows = rows.reshape(2 * half, width)
 
@@ -310,8 +324,8 @@
 
     blocks = [units[0], l0, r0, p0, q0, both, lb, rb, pb, qb, u3, l3, r3, p3, q3]
     halves = ffn(rows_in, rows_go, blocks, half)
-    slot_out = reduce_z(*halves[:4])
-    slot_in_grad = reduce_z(*halves[4:])
+    slot_out = added(halves[0], *sent_z(halves[1:6]))
+    slot_in_grad = added(halves[6], *sent_z(halves[7:]))
     part, mix = against(slot_out, out_grad, combine, False)
     mix = summed_three(mix, "expert", 1, 2, 3)
     mix = summed_three(mix, "expert", 4, 8, 12)

time: 168 us -> 178 us (1.060); the launches traced: 166 us -> 178 us
  waiting for transfers between devices: 52.1 us -> 61.5 us
  starting transfers between devices: 86.9 us -> 90.8 us
    ppermute x43 -> x45, waiting for transfers between devices: 52.1 us -> 61.5 us  [swap(): return lax.ppermute(value, axis, [(i, i ^ k) for i in range(count)])]
    ppermute x43 -> x45, starting transfers between devices: 86.9 us -> 90.8 us  [swap(): return lax.ppermute(value, axis, [(i, i ^ k) for i in range(count)])]
    unnamed x12 -> x6, local copies, waits for them, and re-layouts: 2.61 us -> 0.01 us
  transfers between devices with their start and end apart: 43 -> 45, of which waited for: 22 -> 23; matrix products, arithmetic and copies ran while one was open for 1% -> 1% of each run, Pallas kernels for 8% -> 8%
where the time goes in v8:
time: 178 us
  starting transfers between devices  90.8 us (51%)
  waiting for transfers between devices  61.5 us (35%)
  Pallas kernels  18.9 us (11%)
  local copies, waits for them, and re-layouts  3.28 us (2%)
  other arithmetic  2.04 us (1%)
    ppermute x45, starting transfers between devices, swap(): return lax.ppermute(value, axis, [(i, i ^ k) for i in range(count)])  90.8 us
    ppermute x45, waiting for transfers between devices, swap(): return lax.ppermute(value, axis, [(i, i ^ k) for i in range(count)])  61.5 us
    pallas_call x1, Pallas kernels, slots_call(): pl.pallas_call(slots_kernel, grid=(images // 2,), out_shape=[jax.ShapeDty...  9.2 us
    pallas_call x2, Pallas kernels, against(): pl.pallas_call(lambda *refs: against_kernel(over_tokens, *refs), grid=(im...  4.38 us
    pallas_call x1, Pallas kernels, ffn(): pl.pallas_call(ffn_kernel, out_shape=[jax.ShapeDtypeStruct((own_rows, wid...  4.04 us
  transfers between devices with their start and end apart: 45, of which 23 were waited for; matrix products, arithmetic and copies ran while one was open for 1% of the time, Pallas kernels for 8%

profile of v8, /device:TPU:1, one launch (start us, length us, event | category | flops | bytes accessed | tf_op | source)
XLA Modules:
  0.0 178.2 jit_solution(3191798805795329206)
XLA Ops:
  0.7 1.4 dynamic-slice_bitcast_fusion.1
  2.1 1.6 dynamic-slice_bitcast_fusion
  3.8 2.2 %collective-permute-start.5 = (bf16[2,80,1280]{2,1,0:T(8,128)(2,1)S(1)}, bf16[2,80,1280]{2,1,0:T(8,128)(2,1)S(1)}, u32[]{:S(2)}, u32[]{:S(2)}) collective-permute-start(bf16[2,80,1280]{2,1,0:T(8,128)(2,1)S(1)} %pad_maximum_fusion.3.refs_0_), channel_id=1, source_target_pairs={{0,16},{16,0},{32,48},{48,32},{64,80},{80,64},{96,112},{112,96},{1... | collective-permute-start | bytes 1228808 | tf_op jit(solution)/shard_map/ppermute | solution.py:16
  6.0 1.9 %collective-permute-start.3 = (bf16[2,80,1280]{2,1,0:T(8,128)(2,1)S(1)}, bf16[2,80,1280]{2,1,0:T(8,128)(2,1)S(1)}, u32[]{:S(2)}, u32[]{:S(2)}) collective-permute-start(bf16[2,80,1280]{2,1,0:T(8,128)(2,1)S(1)} %pad_maximum_fusion.3.refs_0_), channel_id=1, source_target_pairs={{0,48},{16,32},{32,16},{48,0},{64,112},{80,96},{96,80},{112,64},{1... | collective-permute-start | bytes 1228808 | tf_op jit(solution)/shard_map/ppermute | solution.py:16
  7.9 1.2 collective-permute-start
  9.2 3.1 %collective-permute-start.9 = (bf16[2,80,1280]{2,1,0:T(8,128)(2,1)S(1)}, bf16[2,80,1280]{2,1,0:T(8,128)(2,1)S(1)}, u32[]{:S(2)}, u32[]{:S(2)}) collective-permute-start(bf16[2,80,1280]{2,1,0:T(8,128)(2,1)S(1)} %pad_maximum_fusion.5), channel_id=1, source_target_pairs={{0,128},{16,144},{32,160},{48,176},{64,192},{80,208},{96,224},{112... | collective-permute-start | bytes 1228808 | tf_op jit(solution)/shard_map/ppermute | solution.py:16
  12.2 1.8 %collective-permute-start.1 = (bf16[16,1280]{1,0:T(8,128)(2,1)S(1)}, bf16[16,1280]{1,0:T(8,128)(2,1)S(1)}, u32[]{:S(2)}, u32[]{:S(2)}) collective-permute-start(bf16[16,1280]{1,0:T(8,128)(2,1)S(1)} %pad_maximum_fusion.12), channel_id=1, source_target_pairs={{0,1},{1,0},{2,3},{3,2},{4,5},{5,4},{6,7},{7,6},{8,9},{9,8},{10,11... | collective-permute-start | bytes 122888 | tf_op jit(solution)/shard_map/ppermute | solution.py:16
  14.1 1.7 collective-permute-start.8
  15.8 2.5 %collective-permute-start.2 = (bf16[32,1280]{1,0:T(8,128)(2,1)S(1)}, bf16[32,1280]{1,0:T(8,128)(2,1)S(1)}, u32[]{:S(2)}, u32[]{:S(2)}) collective-permute-start(bf16[32,1280]{1,0:T(8,128)(2,1)S(1)} %pad_maximum_fusion.11), channel_id=1, source_target_pairs={{0,8},{1,9},{2,10},{3,11},{4,12},{5,13},{6,14},{7,15},{8,0},{9,1},... | collective-permute-start | bytes 245768 | tf_op jit(solution)/shard_map/ppermute | solution.py:16
  18.4 0.9 collective-permute-start.6
  19.4 1.8 collective-permute-done.2
  21.2 4.6 %collective-permute-done.6.refs_4_ = bf16[80,1280]{1,0:T(8,128)(2,1)S(1)} collective-permute-done((bf16[80,1280]{1,0:T(8,128)(2,1)S(1)}, bf16[80,1280]{1,0:T(8,128)(2,1)S(1)}, u32[]{:S(2)}, u32[]{:S(2)}) %collective-permute-start.6) | collective-permute-done | bytes 204832 | tf_op jit(solution)/shard_map/ppermute | solution.py:16
  25.7 5.2 %collective-permute-start.7 = (bf16[64,1280]{1,0:T(8,128)(2,1)S(1)}, bf16[64,1280]{1,0:T(8,128)(2,1)S(1)}, u32[]{:S(2)}, u32[]{:S(2)}) collective-permute-start(bf16[64,1280]{1,0:T(8,128)(2,1)S(1)} %pad_maximum_fusion.10), channel_id=1, source_target_pairs={{0,2},{1,3},{2,0},{3,1},{4,6},{5,7},{6,4},{7,5},{8,10},{9,11},{10,... | collective-permute-start | bytes 491528 | tf_op jit(solution)/shard_map/ppermute | solution.py:16
  30.9 6.5 %collective-permute-done.7 = bf16[64,1280]{1,0:T(8,128)(2,1)S(1)} collective-permute-done((bf16[64,1280]{1,0:T(8,128)(2,1)S(1)}, bf16[64,1280]{1,0:T(8,128)(2,1)S(1)}, u32[]{:S(2)}, u32[]{:S(2)}) %collective-permute-start.7) | collective-permute-done | bytes 163872 | tf_op jit(solution)/shard_map/ppermute | solution.py:16
  37.5 0.9 collective-permute-start.11
  38.6 3.1 %collective-permute-start.12 = (bf16[2,80,1280]{2,1,0:T(8,128)(2,1)S(1)}, bf16[2,80,1280]{2,1,0:T(8,128)(2,1)S(1)}, u32[]{:S(2)}, u32[]{:S(2)}) collective-permute-start(bf16[2,80,1280]{2,1,0:T(8,128)(2,1)S(1)} %pad_maximum_fusion.6), channel_id=1, source_target_pairs={{0,192},{16,208},{32,224},{48,240},{64,128},{80,144},{96,160},{112... | collective-permute-start | bytes 1228808 | tf_op jit(solution)/shard_map/ppermute | solution.py:16
  41.8 9.2 %slots.1 = (bf16[2,64,1280]{2,1,0:T(8,128)(2,1)S(1)}, f32[64,256]{1,0:T(8,128)S(1)}, f32[64,256]{1,0:T(8,128)S(1)}, bf16[2,128,512]{2,1,0:T(8,128)(2,1)S(1)}) custom-call(bf16[128,1280]{1,0:T(8,128)(2,1)S(1)} %bitcast.63, bf16[8,256,1280]{2,1,0:T(8,128)(2,1)S(1)} %copy-done, bf16[8,256,1280]{2,1,0:T(8,128)(2,1)S(1)} %copy-done.1), custom_call_target="tpu_custom_call" | custom-call | flops 838860800 | bytes 10485760 | tf_op jit(solution)/shard_map/slots/pallas_call | solution.py:121
  51.0 4.1 %collective-permute-done.12.refs_10_ = bf16[2,80,1280]{2,1,0:T(8,128)(2,1)S(1)} collective-permute-done((bf16[2,80,1280]{2,1,0:T(8,128)(2,1)S(1)}, bf16[2,80,1280]{2,1,0:T(8,128)(2,1)S(1)}, u32[]{:S(2)}, u32[]{:S(2)}) %collective-permute-start.12) | collective-permute-done | bytes 409632 | tf_op jit(solution)/shard_map/ppermute | solution.py:16
  55.1 0.8 collective-permute-done.11.refs_7_
  55.8 11.2 %collective-permute-start.16 = (bf16[128,1280]{1,0:T(8,128)(2,1)S(1)}, bf16[128,1280]{1,0:T(8,128)(2,1)S(1)}, u32[]{:S(2)}, u32[]{:S(2)}) collective-permute-start(bf16[128,1280]{1,0:T(8,128)(2,1)S(1)} %bitcast.65), channel_id=1, source_target_pairs={{0,128},{16,144},{32,160},{48,176},{64,192},{80,208},{96,224},{112... | collective-permute-start | bytes 983048 | tf_op jit(solution)/shard_map/ppermute | solution.py:16
  67.1 1.2 collective-permute-start.15
  68.3 1.6 collective-permute-start.18
  69.9 9.5 %collective-permute-done.13 = bf16[128,1280]{1,0:T(8,128)(2,1)S(1)} collective-permute-done((bf16[128,1280]{1,0:T(8,128)(2,1)S(1)}, bf16[128,1280]{1,0:T(8,128)(2,1)S(1)}, u32[]{:S(2)}, u32[]{:S(2)}) %collective-permute-start.13) | collective-permute-done | bytes 327712 | tf_op jit(solution)/shard_map/ppermute | solution.py:16
  79.4 1.2 collective-permute-done.16
  80.6 1.3 collective-permute-start.20
  81.9 1.6 collective-permute-start.21
  83.5 2.4 %collective-permute-done.18.refs_9_ = bf16[2,80,1280]{2,1,0:T(8,128)(2,1)S(1)} collective-permute-done((bf16[2,80,1280]{2,1,0:T(8,128)(2,1)S(1)}, bf16[2,80,1280]{2,1,0:T(8,128)(2,1)S(1)}, u32[]{:S(2)}, u32[]{:S(2)}) %collective-permute-start.18) | collective-permute-done | bytes 409632 | tf_op jit(solution)/shard_map/ppermute | solution.py:16
  85.9 1.7 collective-permute-done.17.refs_8_
  87.7 2.7 %collective-permute-done.20.refs_14_ = bf16[80,1280]{1,0:T(8,128)(2,1)S(1)} collective-permute-done((bf16[80,1280]{1,0:T(8,128)(2,1)S(1)}, bf16[80,1280]{1,0:T(8,128)(2,1)S(1)}, u32[]{:S(2)}, u32[]{:S(2)}) %collective-permute-start.20) | collective-permute-done | bytes 204832 | tf_op jit(solution)/shard_map/ppermute | solution.py:16
  90.3 1.7 collective-permute-done.19.refs_13_
  92.2 4.0 %ffn.1 = (f32[64,1280]{1,0:T(8,128)S(1)}, bf16[64,1280]{1,0:T(8,128)(2,1)S(1)}, bf16[32,1280]{1,0:T(8,128)(2,1)S(1)}, bf16[32,1280]{1,0:T(8,128)(2,1)S(1)}, bf16...) custom-call(bf16[256,1280]{1,0:T(8,128)(2,1)S(1)} %get-tuple-element, ...), custom_call_target="tpu_custom_call" | custom-call | tf_op jit(solution)/shard_map/ffn/pallas_call | solution.py:63
  96.2 2.3 %collective-permute-start.25 = (bf16[64,1280]{1,0:T(8,128)(2,1)S(1)}, bf16[64,1280]{1,0:T(8,128)(2,1)S(1)}, u32[]{:S(2)}, u32[]{:S(2)}) collective-permute-start(bf16[64,1280]{1,0:T(8,128)(2,1)S(1)} %get-tuple-element.89), channel_id=1, source_target_pairs={{0,64},{16,80},{32,96},{48,112},{64,0},{80,16},{96,32},{112,48},{1... | collective-permute-start | bytes 491528 | tf_op jit(solution)/shard_map/ppermute | solution.py:16
  99.0 1.9 %collective-permute-start.27 = (bf16[32,1280]{1,0:T(8,128)(2,1)S(1)}, bf16[32,1280]{1,0:T(8,128)(2,1)S(1)}, u32[]{:S(2)}, u32[]{:S(2)}) collective-permute-start(bf16[32,1280]{1,0:T(8,128)(2,1)S(1)} %get-tuple-element.91), channel_id=1, source_target_pairs={{0,128},{16,144},{32,160},{48,176},{64,192},{80,208},{96,224},{112... | collective-permute-start | bytes 245768 | tf_op jit(solution)/shard_map/ppermute | solution.py:16
  100.9 1.6 collective-permute-start.28
  102.5 1.7 collective-permute-start.29
  104.2 1.6 collective-permute-done.27
  106.0 0.8 collective-permute-done.28
  106.8 1.5 collective-permute-start.24
  108.7 2.1 %combine_grad.1 = (f32[64,256]{1,0:T(8,128)S(1)}, f32[8,256]{1,0:T(8,128)S(1)}) custom-call(f32[64,1280]{1,0:T(8,128)S(1)} %add_add_fusion.refs_0_, bf16[8,256,1280]{2,1,0:T(8,128)(2,1)S(1)} %copy-done.1, f32[64,256]{1,0:T(8,128)S(1)} %get-tuple-element.99.refs_2_), custom_call_target="tpu_custom_call" | custom-call | tf_op jit(solution)/shard_map/combine_grad/pallas_call | solution.py:178
  110.7 13.1 %collective-permute-start.32 = (f32[8,256]{1,0:T(8,128)S(1)}, f32[8,256]{1,0:T(8,128)S(1)}, u32[]{:S(2)}, u32[]{:S(2)}) collective-permute-start(f32[8,256]{1,0:T(8,128)S(1)} %get-tuple-element.101), channel_id=1, source_target_pairs={{0,3},{1,2},{2,1},{3,0},{4,7},{5,6},{6,5},{7,4},{8,11},{9,10},{10,... | collective-permute-start | bytes 24584 | tf_op jit(solution)/shard_map/ppermute | solution.py:16
  123.8 3.1 %collective-permute-start.31 = (f32[8,256]{1,0:T(8,128)S(1)}, f32[8,256]{1,0:T(8,128)S(1)}, u32[]{:S(2)}, u32[]{:S(2)}) collective-permute-start(f32[8,256]{1,0:T(8,128)S(1)} %get-tuple-element.101), channel_id=1, source_target_pairs={{0,2},{1,3},{2,0},{3,1},{4,6},{5,7},{6,4},{7,5},{8,10},{9,11},{10,... | collective-permute-start | bytes 24584 | tf_op jit(solution)/shard_map/ppermute | solution.py:16
  126.9 3.4 %collective-permute-done.31 = f32[8,256]{1,0:T(8,128)S(1)} collective-permute-done((f32[8,256]{1,0:T(8,128)S(1)}, f32[8,256]{1,0:T(8,128)S(1)}, u32[]{:S(2)}, u32[]{:S(2)}) %collective-permute-start.31) | collective-permute-done | bytes 8224 | tf_op jit(solution)/shard_map/ppermute | solution.py:16
  130.3 2.8 %collective-permute-start.35 = (f32[8,256]{1,0:T(8,128)S(1)}, f32[8,256]{1,0:T(8,128)S(1)}, u32[]{:S(2)}, u32[]{:S(2)}) collective-permute-start(f32[8,256]{1,0:T(8,128)S(1)} %add_add_fusion.3), channel_id=1, source_target_pairs={{0,12},{1,13},{2,14},{3,15},{4,8},{5,9},{6,10},{7,11},{8,4},{9,5},... | collective-permute-start | bytes 24584 | tf_op jit(solution)/shard_map/ppermute | solution.py:16
  133.1 0.5 collective-permute-start.34
  134.0 2.3 %dispatch_grad.1 = f32[64,256]{1,0:T(8,128)S(1)} custom-call(f32[64,1280]{1,0:T(8,128)S(1)} %get-tuple-element.117.refs_0_, bf16[8,256,1280]{2,1,0:T(8,128)(2,1)S(1)} %copy-done, f32[64,256]{1,0:T(8,128)S(1)} %get-tuple-element.87.refs_2_), custom_call_target="tpu_custom_call" | custom-call | tf_op jit(solution)/shard_map/dispatch_grad/pallas_call | solution.py:178
  136.2 1.0 collective-permute-done.34
  137.3 3.1 %collective-permute-start.37 = (bf16[64,1536]{1,0:T(8,128)(2,1)S(1)}, bf16[64,1536]{1,0:T(8,128)(2,1)S(1)}, u32[]{:S(2)}, u32[]{:S(2)}) collective-permute-start(bf16[64,1536]{1,0:T(8,128)(2,1)S(1)} %get-tuple-element.135), channel_id=1, source_target_pairs={{0,2},{1,3},{2,0},{3,1},{4,6},{5,7},{6,4},{7,5},{8,10},{9,11},{10,... | collective-permute-start | bytes 589832 | tf_op jit(solution)/shard_map/ppermute | solution.py:16
  140.4 0.8 convolution_bitcast_fusion
  141.1 6.6 %collective-permute-start.36 = (f32[8,1280]{1,0:T(8,128)S(1)}, f32[8,1280]{1,0:T(8,128)S(1)}, u32[]{:S(2)}, u32[]{:S(2)}) collective-permute-start(f32[8,1280]{1,0:T(8,128)S(1)} %convolution_bitcast_fusion), channel_id=1, source_target_pairs={{0,64},{16,80},{32,96},{48,112},{64,0},{80,16},{96,32},{112,48},{1... | collective-permute-start | bytes 122888 | tf_op jit(solution)/shard_map/ppermute | solution.py:16
  147.7 4.6 %collective-permute-done.36 = f32[8,1280]{1,0:T(8,128)S(1)} collective-permute-done((f32[8,1280]{1,0:T(8,128)S(1)}, f32[8,1280]{1,0:T(8,128)S(1)}, u32[]{:S(2)}, u32[]{:S(2)}) %collective-permute-start.36) | collective-permute-done | bytes 40992 | tf_op jit(solution)/shard_map/ppermute | solution.py:16
  152.4 1.6 collective-permute-start.40
  154.6 1.2 collective-permute-start.38
  155.8 2.2 %collective-permute-start.41 = (f32[8,1280]{1,0:T(8,128)S(1)}, f32[8,1280]{1,0:T(8,128)S(1)}, u32[]{:S(2)}, u32[]{:S(2)}) collective-permute-start(f32[8,1280]{1,0:T(8,128)S(1)} %add.88), channel_id=1, source_target_pairs={{0,128},{16,144},{32,160},{48,176},{64,192},{80,208},{96,224},{112... | collective-permute-start | bytes 122888 | tf_op jit(solution)/shard_map/ppermute | solution.py:16
  158.0 1.9 %collective-permute-done.41 = f32[8,1280]{1,0:T(8,128)S(1)} collective-permute-done((f32[8,1280]{1,0:T(8,128)S(1)}, f32[8,1280]{1,0:T(8,128)S(1)}, u32[]{:S(2)}, u32[]{:S(2)}) %collective-permute-start.41) | collective-permute-done | bytes 40992 | tf_op jit(solution)/shard_map/ppermute | solution.py:16
  159.8 1.1 collective-permute-start.42
  160.9 2.1 %collective-permute-done.42 = f32[8,1280]{1,0:T(8,128)S(1)} collective-permute-done((f32[8,1280]{1,0:T(8,128)S(1)}, f32[8,1280]{1,0:T(8,128)S(1)}, u32[]{:S(2)}, u32[]{:S(2)}) %collective-permute-start.42) | collective-permute-done | bytes 40992 | tf_op jit(solution)/shard_map/ppermute | solution.py:16
  163.0 2.2 %collective-permute-start.43 = (f32[8,1280]{1,0:T(8,128)S(1)}, f32[8,1280]{1,0:T(8,128)S(1)}, u32[]{:S(2)}, u32[]{:S(2)}) collective-permute-start(f32[8,1280]{1,0:T(8,128)S(1)} %add.90), channel_id=1, source_target_pairs={{0,32},{16,48},{32,0},{48,16},{64,96},{80,112},{96,64},{112,80},{1... | collective-permute-start | bytes 122888 | tf_op jit(solution)/shard_map/ppermute | solution.py:16
  165.2 2.2 %collective-permute-done.43 = f32[8,1280]{1,0:T(8,128)S(1)} collective-permute-done((f32[8,1280]{1,0:T(8,128)S(1)}, f32[8,1280]{1,0:T(8,128)S(1)}, u32[]{:S(2)}, u32[]{:S(2)}) %collective-permute-start.43) | collective-permute-done | bytes 40992 | tf_op jit(solution)/shard_map/ppermute | solution.py:16
  167.4 0.6 add.91
  168.0 4.9 %collective-permute-done.40.three = bf16[2,64,1536]{2,1,0:T(8,128)(2,1)S(1)} collective-permute-done((bf16[2,64,1536]{2,1,0:T(8,128)(2,1)S(1)}, bf16[2,64,1536]{2,1,0:T(8,128)(2,1)S(1)}, u32[]{:S(2)}, u32[]{:S(2)}) %collective-permute-start.40) | collective-permute-done | bytes 393248 | tf_op jit(solution)/shard_map/ppermute | solution.py:16
  173.2 1.3 token_grad.1
  174.5 1.2 collective-permute-start.44
  175.7 1.7 collective-permute-done.44
  177.4 0.8 add_convert_fusion
  (73 shorter events, 3.3 us)
Async XLA Ops:
  0.6 7.3 %copy-start.2 = (bf16[1280,8]{0,1:T(8,128)(2,1)S(1)}, bf16[1280,8]{0,1:T(8,128)(2,1)}, u32[]{:S(2)}) copy-start(bf16[1280,8]{0,1:T(8,128)(2,1)} %param.7) | copy-start | bytes 61444
  0.7 41.1 %copy-start.1 = (bf16[8,256,1280]{2,1,0:T(8,128)(2,1)S(1)}, bf16[8,256,1280]{2,1,0:T(8,128)(2,1)}, u32[]{:S(2)}) copy-start(bf16[8,256,1280]{2,1,0:T(8,128)(2,1)} %refs_1_.3) | copy-start | bytes 15728644
  3.8 14.6 %collective-permute-start.5 = (bf16[2,80,1280]{2,1,0:T(8,128)(2,1)S(1)}, bf16[2,80,1280]{2,1,0:T(8,128)(2,1)S(1)}, u32[]{:S(2)}, u32[]{:S(2)}) collective-permute-start(bf16[2,80,1280]{2,1,0:T(8,128)(2,1)S(1)} %pad_maximum_fusion.3.refs_0_), channel_id=1, source_target_pairs={{0,16},{16,0},{32,48},{48,32},{64,80},{80,64},{96,112},{112,96},{1... | collective-permute-start | bytes 1228808 | tf_op jit(solution)/shard_map/ppermute | solution.py:16
  6.0 13.2 %collective-permute-start.3 = (bf16[2,80,1280]{2,1,0:T(8,128)(2,1)S(1)}, bf16[2,80,1280]{2,1,0:T(8,128)(2,1)S(1)}, u32[]{:S(2)}, u32[]{:S(2)}) collective-permute-start(bf16[2,80,1280]{2,1,0:T(8,128)(2,1)S(1)} %pad_maximum_fusion.3.refs_0_), channel_id=1, source_target_pairs={{0,48},{16,32},{32,16},{48,0},{64,112},{80,96},{96,80},{112,64},{1... | collective-permute-start | bytes 1228808 | tf_op jit(solution)/shard_map/ppermute | solution.py:16
  7.9 4.3 %collective-permute-start = (bf16[8,1280]{1,0:T(8,128)(2,1)S(1)}, bf16[8,1280]{1,0:T(8,128)(2,1)S(1)}, u32[]{:S(2)}, u32[]{:S(2)}) collective-permute-start(bf16[8,1280]{1,0:T(8,128)(2,1)S(1)} %bitcast.73), channel_id=1, source_target_pairs={{0,4},{1,5},{2,6},{3,7},{4,0},{5,1},{6,2},{7,3},{8,12},{9,13},{10,... | collective-permute-start | bytes 61448 | tf_op jit(solution)/shard_map/ppermute | solution.py:16
  9.2 28.3 %collective-permute-start.9 = (bf16[2,80,1280]{2,1,0:T(8,128)(2,1)S(1)}, bf16[2,80,1280]{2,1,0:T(8,128)(2,1)S(1)}, u32[]{:S(2)}, u32[]{:S(2)}) collective-permute-start(bf16[2,80,1280]{2,1,0:T(8,128)(2,1)S(1)} %pad_maximum_fusion.5), channel_id=1, source_target_pairs={{0,128},{16,144},{32,160},{48,176},{64,192},{80,208},{96,224},{112... | collective-permute-start | bytes 1228808 | tf_op jit(solution)/shard_map/ppermute | solution.py:16
  12.2 3.6 %collective-permute-start.1 = (bf16[16,1280]{1,0:T(8,128)(2,1)S(1)}, bf16[16,1280]{1,0:T(8,128)(2,1)S(1)}, u32[]{:S(2)}, u32[]{:S(2)}) collective-permute-start(bf16[16,1280]{1,0:T(8,128)(2,1)S(1)} %pad_maximum_fusion.12), channel_id=1, source_target_pairs={{0,1},{1,0},{2,3},{3,2},{4,5},{5,4},{6,7},{7,6},{8,9},{9,8},{10,11... | collective-permute-start | bytes 122888 | tf_op jit(solution)/shard_map/ppermute | solution.py:16
  14.0 27.8 %copy-start = (bf16[8,256,1280]{2,1,0:T(8,128)(2,1)S(1)}, bf16[8,256,1280]{2,1,0:T(8,128)(2,1)}, u32[]{:S(2)}) copy-start(bf16[8,256,1280]{2,1,0:T(8,128)(2,1)} %refs_1_.2) | copy-start | bytes 15728644
  14.1 23.4 %collective-permute-start.8 = (bf16[2,80,1280]{2,1,0:T(8,128)(2,1)S(1)}, bf16[2,80,1280]{2,1,0:T(8,128)(2,1)S(1)}, u32[]{:S(2)}, u32[]{:S(2)}) collective-permute-start(bf16[2,80,1280]{2,1,0:T(8,128)(2,1)S(1)} %pad_maximum_fusion.4), channel_id=1, source_target_pairs={{0,64},{16,80},{32,96},{48,112},{64,0},{80,16},{96,32},{112,48},{1... | collective-permute-start | bytes 1228808 | tf_op jit(solution)/shard_map/ppermute | solution.py:16
  15.8 5.3 %collective-permute-start.2 = (bf16[32,1280]{1,0:T(8,128)(2,1)S(1)}, bf16[32,1280]{1,0:T(8,128)(2,1)S(1)}, u32[]{:S(2)}, u32[]{:S(2)}) collective-permute-start(bf16[32,1280]{1,0:T(8,128)(2,1)S(1)} %pad_maximum_fusion.11), channel_id=1, source_target_pairs={{0,8},{1,9},{2,10},{3,11},{4,12},{5,13},{6,14},{7,15},{8,0},{9,1},... | collective-permute-start | bytes 245768 | tf_op jit(solution)/shard_map/ppermute | solution.py:16
  18.4 7.3 %collective-permute-start.6 = (bf16[80,1280]{1,0:T(8,128)(2,1)S(1)}, bf16[80,1280]{1,0:T(8,128)(2,1)S(1)}, u32[]{:S(2)}, u32[]{:S(2)}) collective-permute-start(bf16[80,1280]{1,0:T(8,128)(2,1)S(1)} %slice_bitcast_fusion.2), channel_id=1, source_target_pairs={{0,48},{16,32},{32,16},{48,0},{64,112},{80,96},{96,80},{112,64},{1... | collective-permute-start | bytes 614408 | tf_op jit(solution)/shard_map/ppermute | solution.py:16
  19.3 6.5 %collective-permute-start.4 = (bf16[80,1280]{1,0:T(8,128)(2,1)S(1)}, bf16[80,1280]{1,0:T(8,128)(2,1)S(1)}, u32[]{:S(2)}, u32[]{:S(2)}) collective-permute-start(bf16[80,1280]{1,0:T(8,128)(2,1)S(1)} %slice_bitcast_fusion.3), channel_id=1, source_target_pairs={{0,16},{16,0},{32,48},{48,32},{64,80},{80,64},{96,112},{112,96},{1... | collective-permute-start | bytes 614408 | tf_op jit(solution)/shard_map/ppermute | solution.py:16
  25.7 11.7 %collective-permute-start.7 = (bf16[64,1280]{1,0:T(8,128)(2,1)S(1)}, bf16[64,1280]{1,0:T(8,128)(2,1)S(1)}, u32[]{:S(2)}, u32[]{:S(2)}) collective-permute-start(bf16[64,1280]{1,0:T(8,128)(2,1)S(1)} %pad_maximum_fusion.10), channel_id=1, source_target_pairs={{0,2},{1,3},{2,0},{3,1},{4,6},{5,7},{6,4},{7,5},{8,10},{9,11},{10,... | collective-permute-start | bytes 491528 | tf_op jit(solution)/shard_map/ppermute | solution.py:16
  37.5 18.3 %collective-permute-start.11 = (bf16[2,2,80,1280]{3,2,1,0:T(8,128)(2,1)S(1)}, bf16[2,2,80,1280]{3,2,1,0:T(8,128)(2,1)S(1)}, u32[]{:S(2)}, u32[]{:S(2)}) collective-permute-start(bf16[2,2,80,1280]{3,2,1,0:T(8,128)(2,1)S(1)} %pad_maximum_fusion.refs_5_), channel_id=1, source_target_pairs={{0,48},{16,32},{32,16},{48,0},{64,112},{80,96},{96,80},{112,64},{1... | collective-permute-start | bytes 2457608 | tf_op jit(solution)/shard_map/ppermute | solution.py:16
  38.4 17.4 %collective-permute-start.10 = (bf16[2,2,80,1280]{3,2,1,0:T(8,128)(2,1)S(1)}, bf16[2,2,80,1280]{3,2,1,0:T(8,128)(2,1)S(1)}, u32[]{:S(2)}, u32[]{:S(2)}) collective-permute-start(bf16[2,2,80,1280]{3,2,1,0:T(8,128)(2,1)S(1)} %pad_maximum_fusion.refs_5_), channel_id=1, source_target_pairs={{0,16},{16,0},{32,48},{48,32},{64,80},{80,64},{96,112},{112,96},{1... | collective-permute-start | bytes 2457608 | tf_op jit(solution)/shard_map/ppermute | solution.py:16
  38.6 16.4 %collective-permute-start.12 = (bf16[2,80,1280]{2,1,0:T(8,128)(2,1)S(1)}, bf16[2,80,1280]{2,1,0:T(8,128)(2,1)S(1)}, u32[]{:S(2)}, u32[]{:S(2)}) collective-permute-start(bf16[2,80,1280]{2,1,0:T(8,128)(2,1)S(1)} %pad_maximum_fusion.6), channel_id=1, source_target_pairs={{0,192},{16,208},{32,224},{48,240},{64,128},{80,144},{96,160},{112... | collective-permute-start | bytes 1228808 | tf_op jit(solution)/shard_map/ppermute | solution.py:16
  55.8 24.7 %collective-permute-start.16 = (bf16[128,1280]{1,0:T(8,128)(2,1)S(1)}, bf16[128,1280]{1,0:T(8,128)(2,1)S(1)}, u32[]{:S(2)}, u32[]{:S(2)}) collective-permute-start(bf16[128,1280]{1,0:T(8,128)(2,1)S(1)} %bitcast.65), channel_id=1, source_target_pairs={{0,128},{16,144},{32,160},{48,176},{64,192},{80,208},{96,224},{112... | collective-permute-start | bytes 983048 | tf_op jit(solution)/shard_map/ppermute | solution.py:16
  67.1 12.3 %collective-permute-start.13 = (bf16[128,1280]{1,0:T(8,128)(2,1)S(1)}, bf16[128,1280]{1,0:T(8,128)(2,1)S(1)}, u32[]{:S(2)}, u32[]{:S(2)}) collective-permute-start(bf16[128,1280]{1,0:T(8,128)(2,1)S(1)} %bitcast.66), channel_id=1, source_target_pairs={{0,64},{16,80},{32,96},{48,112},{64,0},{80,16},{96,32},{112,48},{1... | collective-permute-start | bytes 983048 | tf_op jit(solution)/shard_map/ppermute | solution.py:16
  67.1 13.5 %collective-permute-start.15 = (bf16[2,80,1280]{2,1,0:T(8,128)(2,1)S(1)}, bf16[2,80,1280]{2,1,0:T(8,128)(2,1)S(1)}, u32[]{:S(2)}, u32[]{:S(2)}) collective-permute-start(bf16[2,80,1280]{2,1,0:T(8,128)(2,1)S(1)} %collective-permute-done.12.refs_10_), channel_id=1, source_target_pairs={{0,48},{16,32},{32,16},{48,0},{64,112},{80,96},{96,80},{112,64},{1... | collective-permute-start | bytes 1228808 | tf_op jit(solution)/shard_map/ppermute | solution.py:16
  68.2 12.4 %collective-permute-start.14 = (bf16[2,80,1280]{2,1,0:T(8,128)(2,1)S(1)}, bf16[2,80,1280]{2,1,0:T(8,128)(2,1)S(1)}, u32[]{:S(2)}, u32[]{:S(2)}) collective-permute-start(bf16[2,80,1280]{2,1,0:T(8,128)(2,1)S(1)} %collective-permute-done.12.refs_10_), channel_id=1, source_target_pairs={{0,16},{16,0},{32,48},{48,32},{64,80},{80,64},{96,112},{112,96},{1... | collective-permute-start | bytes 1228808 | tf_op jit(solution)/shard_map/ppermute | solution.py:16
  68.3 17.6 %collective-permute-start.18 = (bf16[2,80,1280]{2,1,0:T(8,128)(2,1)S(1)}, bf16[2,80,1280]{2,1,0:T(8,128)(2,1)S(1)}, u32[]{:S(2)}, u32[]{:S(2)}) collective-permute-start(bf16[2,80,1280]{2,1,0:T(8,128)(2,1)S(1)} %slice_bitcast_fusion), channel_id=1, source_target_pairs={{0,48},{16,32},{32,16},{48,0},{64,112},{80,96},{96,80},{112,64},{1... | collective-permute-start | bytes 1228808 | tf_op jit(solution)/shard_map/ppermute | solution.py:16
  79.4 8.3 %collective-permute-start.17 = (bf16[2,80,1280]{2,1,0:T(8,128)(2,1)S(1)}, bf16[2,80,1280]{2,1,0:T(8,128)(2,1)S(1)}, u32[]{:S(2)}, u32[]{:S(2)}) collective-permute-start(bf16[2,80,1280]{2,1,0:T(8,128)(2,1)S(1)} %slice_bitcast_fusion.1), channel_id=1, source_target_pairs={{0,16},{16,0},{32,48},{48,32},{64,80},{80,64},{96,112},{112,96},{1... | collective-permute-start | bytes 1228808 | tf_op jit(solution)/shard_map/ppermute | solution.py:16
  80.6 9.7 %collective-permute-start.20 = (bf16[80,1280]{1,0:T(8,128)(2,1)S(1)}, bf16[80,1280]{1,0:T(8,128)(2,1)S(1)}, u32[]{:S(2)}, u32[]{:S(2)}) collective-permute-start(bf16[80,1280]{1,0:T(8,128)(2,1)S(1)} %slice_bitcast_fusion.4), channel_id=1, source_target_pairs={{0,48},{16,32},{32,16},{48,0},{64,112},{80,96},{96,80},{112,64},{1... | collective-permute-start | bytes 614408 | tf_op jit(solution)/shard_map/ppermute | solution.py:16
  81.9 10.2 %collective-permute-start.19 = (bf16[80,1280]{1,0:T(8,128)(2,1)S(1)}, bf16[80,1280]{1,0:T(8,128)(2,1)S(1)}, u32[]{:S(2)}, u32[]{:S(2)}) collective-permute-start(bf16[80,1280]{1,0:T(8,128)(2,1)S(1)} %slice_bitcast_fusion.5), channel_id=1, source_target_pairs={{0,16},{16,0},{32,48},{48,32},{64,80},{80,64},{96,112},{112,96},{1... | collective-permute-start | bytes 614408 | tf_op jit(solution)/shard_map/ppermute | solution.py:16
  81.9 10.2 %collective-permute-start.21 = (bf16[128,1280]{1,0:T(8,128)(2,1)S(1)}, bf16[128,1280]{1,0:T(8,128)(2,1)S(1)}, u32[]{:S(2)}, u32[]{:S(2)}) collective-permute-start(bf16[128,1280]{1,0:T(8,128)(2,1)S(1)} %collective-permute-done.16), channel_id=1, source_target_pairs={{0,64},{16,80},{32,96},{48,112},{64,0},{80,16},{96,32},{112,48},{1... | collective-permute-start | bytes 983048 | tf_op jit(solution)/shard_map/ppermute | solution.py:16
  96.2 12.4 %collective-permute-start.25 = (bf16[64,1280]{1,0:T(8,128)(2,1)S(1)}, bf16[64,1280]{1,0:T(8,128)(2,1)S(1)}, u32[]{:S(2)}, u32[]{:S(2)}) collective-permute-start(bf16[64,1280]{1,0:T(8,128)(2,1)S(1)} %get-tuple-element.89), channel_id=1, source_target_pairs={{0,64},{16,80},{32,96},{48,112},{64,0},{80,16},{96,32},{112,48},{1... | collective-permute-start | bytes 491528 | tf_op jit(solution)/shard_map/ppermute | solution.py:16
  98.5 5.6 %collective-permute-start.26 = (bf16[32,1280]{1,0:T(8,128)(2,1)S(1)}, bf16[32,1280]{1,0:T(8,128)(2,1)S(1)}, u32[]{:S(2)}, u32[]{:S(2)}) collective-permute-start(bf16[32,1280]{1,0:T(8,128)(2,1)S(1)} %get-tuple-element.90), channel_id=1, source_target_pairs={{0,128},{16,144},{32,160},{48,176},{64,192},{80,208},{96,224},{112... | collective-permute-start | bytes 245768 | tf_op jit(solution)/shard_map/ppermute | solution.py:16
  99.0 6.7 %collective-permute-start.27 = (bf16[32,1280]{1,0:T(8,128)(2,1)S(1)}, bf16[32,1280]{1,0:T(8,128)(2,1)S(1)}, u32[]{:S(2)}, u32[]{:S(2)}) collective-permute-start(bf16[32,1280]{1,0:T(8,128)(2,1)S(1)} %get-tuple-element.91), channel_id=1, source_target_pairs={{0,128},{16,144},{32,160},{48,176},{64,192},{80,208},{96,224},{112... | collective-permute-start | bytes 245768 | tf_op jit(solution)/shard_map/ppermute | solution.py:16
  100.9 5.9 %collective-permute-start.28 = (bf16[32,1280]{1,0:T(8,128)(2,1)S(1)}, bf16[32,1280]{1,0:T(8,128)(2,1)S(1)}, u32[]{:S(2)}, u32[]{:S(2)}) collective-permute-start(bf16[32,1280]{1,0:T(8,128)(2,1)S(1)} %get-tuple-element.92), channel_id=1, source_target_pairs={{0,192},{16,208},{32,224},{48,240},{64,128},{80,144},{96,160},{112... | collective-permute-start | bytes 245768 | tf_op jit(solution)/shard_map/ppermute | solution.py:16
  102.5 6.1 %collective-permute-start.29 = (bf16[32,1280]{1,0:T(8,128)(2,1)S(1)}, bf16[32,1280]{1,0:T(8,128)(2,1)S(1)}, u32[]{:S(2)}, u32[]{:S(2)}) collective-permute-start(bf16[32,1280]{1,0:T(8,128)(2,1)S(1)} %get-tuple-element.93), channel_id=1, source_target_pairs={{0,192},{16,208},{32,224},{48,240},{64,128},{80,144},{96,160},{112... | collective-permute-start | bytes 245768 | tf_op jit(solution)/shard_map/ppermute | solution.py:16
  104.2 22.7 %collective-permute-start.22 = (bf16[64,1280]{1,0:T(8,128)(2,1)S(1)}, bf16[64,1280]{1,0:T(8,128)(2,1)S(1)}, u32[]{:S(2)}, u32[]{:S(2)}) collective-permute-start(bf16[64,1280]{1,0:T(8,128)(2,1)S(1)} %get-tuple-element.81), channel_id=1, source_target_pairs={{0,64},{16,80},{32,96},{48,112},{64,0},{80,16},{96,32},{112,48},{1... | collective-permute-start | bytes 491528 | tf_op jit(solution)/shard_map/ppermute | solution.py:16
  105.7 21.2 %collective-permute-start.23 = (bf16[64,1280]{1,0:T(8,128)(2,1)S(1)}, bf16[64,1280]{1,0:T(8,128)(2,1)S(1)}, u32[]{:S(2)}, u32[]{:S(2)}) collective-permute-start(bf16[64,1280]{1,0:T(8,128)(2,1)S(1)} %get-tuple-element.82), channel_id=1, source_target_pairs={{0,128},{16,144},{32,160},{48,176},{64,192},{80,208},{96,224},{112... | collective-permute-start | bytes 491528 | tf_op jit(solution)/shard_map/ppermute | solution.py:16
  106.8 20.1 %collective-permute-start.24 = (bf16[64,1280]{1,0:T(8,128)(2,1)S(1)}, bf16[64,1280]{1,0:T(8,128)(2,1)S(1)}, u32[]{:S(2)}, u32[]{:S(2)}) collective-permute-start(bf16[64,1280]{1,0:T(8,128)(2,1)S(1)} %get-tuple-element.83), channel_id=1, source_target_pairs={{0,192},{16,208},{32,224},{48,240},{64,128},{80,144},{96,160},{112... | collective-permute-start | bytes 491528 | tf_op jit(solution)/shard_map/ppermute | solution.py:16
  110.7 16.2 %collective-permute-start.32 = (f32[8,256]{1,0:T(8,128)S(1)}, f32[8,256]{1,0:T(8,128)S(1)}, u32[]{:S(2)}, u32[]{:S(2)}) collective-permute-start(f32[8,256]{1,0:T(8,128)S(1)} %get-tuple-element.101), channel_id=1, source_target_pairs={{0,3},{1,2},{2,1},{3,0},{4,7},{5,6},{6,5},{7,4},{8,11},{9,10},{10,... | collective-permute-start | bytes 24584 | tf_op jit(solution)/shard_map/ppermute | solution.py:16
  123.8 6.5 %collective-permute-start.31 = (f32[8,256]{1,0:T(8,128)S(1)}, f32[8,256]{1,0:T(8,128)S(1)}, u32[]{:S(2)}, u32[]{:S(2)}) collective-permute-start(f32[8,256]{1,0:T(8,128)S(1)} %get-tuple-element.101), channel_id=1, source_target_pairs={{0,2},{1,3},{2,0},{3,1},{4,6},{5,7},{6,4},{7,5},{8,10},{9,11},{10,... | collective-permute-start | bytes 24584 | tf_op jit(solution)/shard_map/ppermute | solution.py:16
  126.9 3.4 %collective-permute-start.30 = (f32[8,256]{1,0:T(8,128)S(1)}, f32[8,256]{1,0:T(8,128)S(1)}, u32[]{:S(2)}, u32[]{:S(2)}) collective-permute-start(f32[8,256]{1,0:T(8,128)S(1)} %get-tuple-element.101), channel_id=1, source_target_pairs={{0,1},{1,0},{2,3},{3,2},{4,5},{5,4},{6,7},{7,6},{8,9},{9,8},{10,11... | collective-permute-start | bytes 24584 | tf_op jit(solution)/shard_map/ppermute | solution.py:16
  130.3 5.9 %collective-permute-start.35 = (f32[8,256]{1,0:T(8,128)S(1)}, f32[8,256]{1,0:T(8,128)S(1)}, u32[]{:S(2)}, u32[]{:S(2)}) collective-permute-start(f32[8,256]{1,0:T(8,128)S(1)} %add_add_fusion.3), channel_id=1, source_target_pairs={{0,12},{1,13},{2,14},{3,15},{4,8},{5,9},{6,10},{7,11},{8,4},{9,5},... | collective-permute-start | bytes 24584 | tf_op jit(solution)/shard_map/ppermute | solution.py:16
  133.1 4.1 %collective-permute-start.34 = (f32[8,256]{1,0:T(8,128)S(1)}, f32[8,256]{1,0:T(8,128)S(1)}, u32[]{:S(2)}, u32[]{:S(2)}) collective-permute-start(f32[8,256]{1,0:T(8,128)S(1)} %add_add_fusion.3), channel_id=1, source_target_pairs={{0,8},{1,9},{2,10},{3,11},{4,12},{5,13},{6,14},{7,15},{8,0},{9,1},... | collective-permute-start | bytes 24584 | tf_op jit(solution)/shard_map/ppermute | solution.py:16
  133.6 3.6 %collective-permute-start.33 = (f32[8,256]{1,0:T(8,128)S(1)}, f32[8,256]{1,0:T(8,128)S(1)}, u32[]{:S(2)}, u32[]{:S(2)}) collective-permute-start(f32[8,256]{1,0:T(8,128)S(1)} %add_add_fusion.3), channel_id=1, source_target_pairs={{0,4},{1,5},{2,6},{3,7},{4,0},{5,1},{6,2},{7,3},{8,12},{9,13},{10,... | collective-permute-start | bytes 24584 | tf_op jit(solution)/shard_map/ppermute | solution.py:16
  137.3 15.1 %collective-permute-start.37 = (bf16[64,1536]{1,0:T(8,128)(2,1)S(1)}, bf16[64,1536]{1,0:T(8,128)(2,1)S(1)}, u32[]{:S(2)}, u32[]{:S(2)}) collective-permute-start(bf16[64,1536]{1,0:T(8,128)(2,1)S(1)} %get-tuple-element.135), channel_id=1, source_target_pairs={{0,2},{1,3},{2,0},{3,1},{4,6},{5,7},{6,4},{7,5},{8,10},{9,11},{10,... | collective-permute-start | bytes 589832 | tf_op jit(solution)/shard_map/ppermute | solution.py:16
  141.1 11.2 %collective-permute-start.36 = (f32[8,1280]{1,0:T(8,128)S(1)}, f32[8,1280]{1,0:T(8,128)S(1)}, u32[]{:S(2)}, u32[]{:S(2)}) collective-permute-start(f32[8,1280]{1,0:T(8,128)S(1)} %convolution_bitcast_fusion), channel_id=1, source_target_pairs={{0,64},{16,80},{32,96},{48,112},{64,0},{80,16},{96,32},{112,48},{1... | collective-permute-start | bytes 122888 | tf_op jit(solution)/shard_map/ppermute | solution.py:16
  152.4 20.5 %collective-permute-start.40 = (bf16[2,64,1536]{2,1,0:T(8,128)(2,1)S(1)}, bf16[2,64,1536]{2,1,0:T(8,128)(2,1)S(1)}, u32[]{:S(2)}, u32[]{:S(2)}) collective-permute-start(bf16[2,64,1536]{2,1,0:T(8,128)(2,1)S(1)} %pad_maximum_fusion.7.pair), channel_id=1, source_target_pairs={{0,12},{1,13},{2,14},{3,15},{4,8},{5,9},{6,10},{7,11},{8,4},{9,5},... | collective-permute-start | bytes 1179656 | tf_op jit(solution)/shard_map/ppermute | solution.py:16
  154.1 18.8 %collective-permute-start.39 = (bf16[2,64,1536]{2,1,0:T(8,128)(2,1)S(1)}, bf16[2,64,1536]{2,1,0:T(8,128)(2,1)S(1)}, u32[]{:S(2)}, u32[]{:S(2)}) collective-permute-start(bf16[2,64,1536]{2,1,0:T(8,128)(2,1)S(1)} %pad_maximum_fusion.7.pair), channel_id=1, source_target_pairs={{0,8},{1,9},{2,10},{3,11},{4,12},{5,13},{6,14},{7,15},{8,0},{9,1},... | collective-permute-start | bytes 1179656 | tf_op jit(solution)/shard_map/ppermute | solution.py:16
  154.6 18.6 %collective-permute-start.38 = (bf16[2,64,1536]{2,1,0:T(8,128)(2,1)S(1)}, bf16[2,64,1536]{2,1,0:T(8,128)(2,1)S(1)}, u32[]{:S(2)}, u32[]{:S(2)}) collective-permute-start(bf16[2,64,1536]{2,1,0:T(8,128)(2,1)S(1)} %pad_maximum_fusion.7.pair), channel_id=1, source_target_pairs={{0,4},{1,5},{2,6},{3,7},{4,0},{5,1},{6,2},{7,3},{8,12},{9,13},{10,... | collective-permute-start | bytes 1179656 | tf_op jit(solution)/shard_map/ppermute | solution.py:16
  155.8 4.0 %collective-permute-start.41 = (f32[8,1280]{1,0:T(8,128)S(1)}, f32[8,1280]{1,0:T(8,128)S(1)}, u32[]{:S(2)}, u32[]{:S(2)}) collective-permute-start(f32[8,1280]{1,0:T(8,128)S(1)} %add.88), channel_id=1, source_target_pairs={{0,128},{16,144},{32,160},{48,176},{64,192},{80,208},{96,224},{112... | collective-permute-start | bytes 122888 | tf_op jit(solution)/shard_map/ppermute | solution.py:16
  159.8 3.1 %collective-permute-start.42 = (f32[8,1280]{1,0:T(8,128)S(1)}, f32[8,1280]{1,0:T(8,128)S(1)}, u32[]{:S(2)}, u32[]{:S(2)}) collective-permute-start(f32[8,1280]{1,0:T(8,128)S(1)} %add.89), channel_id=1, source_target_pairs={{0,16},{16,0},{32,48},{48,32},{64,80},{80,64},{96,112},{112,96},{1... | collective-permute-start | bytes 122888 | tf_op jit(solution)/shard_map/ppermute | solution.py:16
  163.0 4.4 %collective-permute-start.43 = (f32[8,1280]{1,0:T(8,128)S(1)}, f32[8,1280]{1,0:T(8,128)S(1)}, u32[]{:S(2)}, u32[]{:S(2)}) collective-permute-start(f32[8,1280]{1,0:T(8,128)S(1)} %add.90), channel_id=1, source_target_pairs={{0,32},{16,48},{32,0},{48,16},{64,96},{80,112},{96,64},{112,80},{1... | collective-permute-start | bytes 122888 | tf_op jit(solution)/shard_map/ppermute | solution.py:16
  174.5 2.9 %collective-permute-start.44 = (f32[128,1280]{1,0:T(8,128)S(1)}, f32[128,1280]{1,0:T(8,128)S(1)}, u32[]{:S(2)}, u32[]{:S(2)}) collective-permute-start(f32[128,1280]{1,0:T(8,128)S(1)} %get-tuple-element.115), channel_id=1, source_target_pairs={{0,1},{1,0},{2,3},{3,2},{4,5},{5,4},{6,7},{7,6},{8,9},{9,8},{10,11... | collective-permute-start | bytes 1966088 | tf_op jit(solution)/shard_map/ppermute | solution.py:16

commit v9 on v7

--- a/solution.py
+++ b/solution.py
@@ -76,13 +76,10 @@
     return (col == owner * 16 + row % 16).astype(BF16)
 
 
-def slots_kernel(table, tokens, out_grad, rows, dispatch_own, combine_own, spread):
-    step = pl.program_id(0)
+def slots_kernel(table, tokens, rows, dispatch_own, combine_own, near_out):
     own = 8
     near = table.shape[0] // 2
-    count = tokens.shape[1]
-    pick = pick_rows(count)
-    ins, gos, disp, comb, mine, theirs = [], [], [], [], [], []
+    ins, disp, comb = [], [], []
     for i in range(2):
         logits = nt(table[...], tokens[i])
         up = jnp.exp(logits[:near] - jnp.max(logits[:near], axis=1, keepdims=True))
@@ -91,55 +88,69 @@
         combine = down[:own] / jnp.sum(down, axis=0, keepdims=True)
         dispatch_b = dispatch.astype(BF16)
         ins.append(jnp.dot(dispatch_b[:16], tokens[i], preferred_element_type=F32)[:own])
-        both = jnp.concatenate([combine, combine], axis=0).astype(BF16)
-        gos.append(jnp.dot(both, out_grad[i], preferred_element_type=F32)[:own])
         disp.append(dispatch[:own])
         comb.append(combine)
-        lines = nt(pick, dispatch_b).astype(BF16)
-        image = 2 * step + i
-        q = lax.broadcasted_iota(jnp.int32, (near, 8 * near), 0)
-        col = lax.broadcasted_iota(jnp.int32, (near, 8 * near), 1)
-        wide = (col == (q // 8) * 64 + q % 8 + image * 8).astype(BF16)
-        lines = jnp.dot(lines, wide, preferred_element_type=F32)
-        mine.append(lines[:16])
-        theirs.append(lines[16:])
-    rows[0] = jnp.concatenate(ins, axis=0).astype(BF16)
-    rows[1] = jnp.concatenate(gos, axis=0).astype(BF16)
+        near_out[i] = dispatch_b
+    rows[...] = jnp.concatenate(ins, axis=0).astype(BF16)
     dispatch_own[...] = jnp.concatenate(disp, axis=0)
     combine_own[...] = jnp.concatenate(comb, axis=0)
-    spread[0] = jnp.concatenate(mine, axis=0).astype(BF16)
-    spread[1] = jnp.concatenate(theirs, axis=0).astype(BF16)
-
-
-def slots_call(table, tokens, out_grad):
+
+
+def slots_call(table, tokens):
     images, count, width = tokens.shape
     slots = table.shape[0]
     return pl.pallas_call(
         slots_kernel,
         grid=(images // 2,),
         out_shape=[
-            jax.ShapeDtypeStruct((2, images * 8, width), BF16),
+            jax.ShapeDtypeStruct((images * 8, width), BF16),
             jax.ShapeDtypeStruct((images * 8, count), F32),
             jax.ShapeDtypeStruct((images * 8, count), F32),
-            jax.ShapeDtypeStruct((2, images * 16, slots * 4), BF16),
+            jax.ShapeDtypeStruct((images, slots // 2, count), BF16),
         ],
         in_specs=[
             pl.BlockSpec((slots, width), lambda i: (0, 0)),
             pl.BlockSpec((2, count, width), lambda i: (i, 0, 0)),
-            pl.BlockSpec((2, count, width), lambda i: (i, 0, 0)),
         ],
         out_specs=[
-            pl.BlockSpec((2, 16, width), lambda i: (0, i, 0)),
+            pl.BlockSpec((16, width), lambda i: (i, 0)),
             pl.BlockSpec((16, count), lambda i: (i, 0)),
             pl.BlockSpec((16, count), lambda i: (i, 0)),
-            pl.BlockSpec((2, 32, slots * 4), lambda i: (0, i, 0)),
+            pl.BlockSpec((2, slots // 2, count), lambda i: (i, 0, 0)),
         ],
         compiler_params=pltpu.CompilerParams(vmem_limit_bytes=24 * 2**20),
         cost_estimate=pl.CostEstimate(
-            flops=2 * tokens.size * (slots + 32), bytes_accessed=4 * tokens.size, transcendentals=2 * images * slots * count
+            flops=2 * tokens.size * (slots + 16), bytes_accessed=2 * tokens.size, transcendentals=2 * images * slots * count
         ),
         name="slots",
-    )(table, tokens, out_grad)
+    )(table, tokens)
+
+
+def spread_kernel(near, out):
+    images, slots, count = near.shape
+    pick = pick_rows(count)
+    q = lax.broadcasted_iota(jnp.int32, (slots, 8 * slots), 0)
+    col = lax.broadcasted_iota(jnp.int32, (slots, 8 * slots), 1)
+    first = (q // 8) * 64 + q % 8
+    for image in range(images):
+        lines = nt(pick, near[image]).astype(BF16)
+        wide = (col == first + image * 8).astype(BF16)
+        lines = jnp.dot(lines, wide, preferred_element_type=F32).astype(BF16)
+        out[0, 16 * image : 16 * image + 16] = lines[:16]
+        out[1, 16 * image : 16 * image + 16] = lines[16:]
+
+
+def spread_call(near):
+    images, slots, _ = near.shape
+    vmem = pl.BlockSpec(memory_space=pltpu.VMEM)
+    return pl.pallas_call(
+        spread_kernel,
+        out_shape=jax.ShapeDtypeStruct((2, images * 16, slots * 8), BF16),
+        in_specs=[vmem],
+        out_specs=vmem,
+        compiler_params=pltpu.CompilerParams(vmem_limit_bytes=16 * 2**20),
+        name="spread",
+    )(near)
 
 
 def against_kernel(over_tokens, rows, big, weight, *outs):
@@ -285,23 +296,26 @@
     l0, r0 = swap(units[0], "dp", 1), swap(units[0], "dp", 3)
     u2 = swap(units[2], "dp", 8)
     u1 = swap(units[1], "dp", 4)
+    p0, q0 = swap(r0[0], "dp", 1), swap(l0[1], "dp", 3)
     table = doubled(slot_params.T, "expert", 2, 4)
-    p0, q0 = swap(r0[0], "dp", 1), swap(l0[1], "dp", 3)
-    table = doubled(table, "expert", 8)
-    table = doubled(after(table, p0, q0), "expert", 1)
 
     table, p0, q0, u1, u2 = together(table, p0, q0, u1, u2)
     both = jnp.stack([u1, u2], axis=1)
     lb, rb = swap(both, "dp", 1), swap(both, "dp", 3)
     u3 = swap(after(units[3], u1), "dp", 12)
-    rows, dispatch, combine, spread = slots_call(table, tokens, out_grad)
-    rows = rows.reshape(2 * half, width)
+    table = doubled(table, "expert", 8, 1)
+    slot_in, dispatch, combine, near = slots_call(table, tokens)
+    slot_go = jnp.einsum(
+        "bsm,bmd->bsd", combine.astype(BF16).reshape(images, own, count), out_grad, preferred_element_type=F32
+    )
+    rows = jnp.concatenate([slot_in, slot_go.astype(BF16).reshape(half, width)], axis=0)
 
     lb, rb, u3, rows = together(lb, rb, u3, rows)
-    z1, z2 = swap(rows, "dp", 4), swap(rows, "dp", 8)
+    z2, z1 = swap(rows, "dp", 8), swap(rows, "dp", 4)
     l3, r3 = swap(u3, "dp", 1), swap(u3, "dp", 3)
     pb, qb = swap(rb[0], "dp", 1), swap(lb[1], "dp", 3)
-    l3, r3, z2 = together(l3, r3, z2)
+    spread = spread_call(near)
+    l3, r3, z2, spread = together(l3, r3, z2, spread)
     p3, q3 = swap(r3[0], "dp", 1), swap(l3[1], "dp", 3)
     z3 = swap(z2, "dp", 4)
     pb, qb, p3, q3, z3 = together(pb, qb, p3, q3, z3)

time: 168 us -> 167 us (level)
  waiting for transfers between devices: 52.1 us -> 67.3 us
  starting transfers between devices: 86.9 us -> 75.6 us
  local copies, waits for them, and re-layouts: 4.23 us -> 1.76 us
  Pallas kernels: 18.9 us -> 16.7 us
    ppermute x43, waiting for transfers between devices: 52.1 us -> 67.3 us  [swap(): return lax.ppermute(value, axis, [(i, i ^ k) for i in range(count)])]
    ppermute x43, starting transfers between devices: 86.9 us -> 75.6 us  [swap(): return lax.ppermute(value, axis, [(i, i ^ k) for i in range(count)])]
    pallas_call x1, Pallas kernels: 9.18 us -> 6.63 us  [slots_call(): pl.pallas_call(slots_kernel, grid=(images // 2,), out_shape=[jax.ShapeDty...]
    unnamed x12 -> x10, local copies, waits for them, and re-layouts: 2.61 us -> 0.12 us
  transfers between devices with their start and end apart: 43 -> 43, of which waited for: 22 -> 20; matrix products, arithmetic and copies ran while one was open for 1% -> 2% of each run, Pallas kernels for 8% -> 7%
where the time goes in v9:
time: 167 us; the launch traced here: 166 us
  starting transfers between devices  75.6 us (45%)
  waiting for transfers between devices  67.3 us (40%)
  Pallas kernels  16.7 us (10%)
  other arithmetic  2.04 us (1%)
  local copies, waits for them, and re-layouts  1.76 us (1%)
    ppermute x43, starting transfers between devices, swap(): return lax.ppermute(value, axis, [(i, i ^ k) for i in range(count)])  75.6 us
    ppermute x43, waiting for transfers between devices, swap(): return lax.ppermute(value, axis, [(i, i ^ k) for i in range(count)])  67.3 us
    pallas_call x1, Pallas kernels, slots_call(): pl.pallas_call(slots_kernel, grid=(images // 2,), out_shape=[jax.ShapeDty...  6.63 us
    pallas_call x2, Pallas kernels, against(): pl.pallas_call(lambda *refs: against_kernel(over_tokens, *refs), grid=(im...  4.38 us
    pallas_call x1, Pallas kernels, ffn(): pl.pallas_call(ffn_kernel, out_shape=[jax.ShapeDtypeStruct((own_rows, wid...  4.04 us
  transfers between devices with their start and end apart: 43, of which 20 were waited for; matrix products, arithmetic and copies ran while one was open for 2% of the time, Pallas kernels for 7%

profile of v9, /device:TPU:1, one launch (start us, length us, event | category | flops | bytes accessed | tf_op | source)
XLA Modules:
  0.0 166.0 jit_solution(12855675867887662193)
XLA Ops:
  0.7 1.4 dynamic-slice_bitcast_fusion.1
  2.3 2.2 %collective-permute-start.4 = (bf16[2,80,1280]{2,1,0:T(8,128)(2,1)S(1)}, bf16[2,80,1280]{2,1,0:T(8,128)(2,1)S(1)}, u32[]{:S(2)}, u32[]{:S(2)}) collective-permute-start(bf16[2,80,1280]{2,1,0:T(8,128)(2,1)S(1)} %pad_maximum_fusion.3.refs_0_), channel_id=1, source_target_pairs={{0,16},{16,0},{32,48},{48,32},{64,80},{80,64},{96,112},{112,96},{1... | collective-permute-start | bytes 1228808 | tf_op jit(solution)/shard_map/ppermute | solution.py:16
  4.5 1.9 %collective-permute-start.2 = (bf16[2,80,1280]{2,1,0:T(8,128)(2,1)S(1)}, bf16[2,80,1280]{2,1,0:T(8,128)(2,1)S(1)}, u32[]{:S(2)}, u32[]{:S(2)}) collective-permute-start(bf16[2,80,1280]{2,1,0:T(8,128)(2,1)S(1)} %pad_maximum_fusion.3.refs_0_), channel_id=1, source_target_pairs={{0,48},{16,32},{32,16},{48,0},{64,112},{80,96},{96,80},{112,64},{1... | collective-permute-start | bytes 1228808 | tf_op jit(solution)/shard_map/ppermute | solution.py:16
  6.4 6.9 %collective-permute-start = (bf16[8,1280]{1,0:T(8,128)(2,1)S(1)}, bf16[8,1280]{1,0:T(8,128)(2,1)S(1)}, u32[]{:S(2)}, u32[]{:S(2)}) collective-permute-start(bf16[8,1280]{1,0:T(8,128)(2,1)S(1)} %bitcast.68), channel_id=1, source_target_pairs={{0,2},{1,3},{2,0},{3,1},{4,6},{5,7},{6,4},{7,5},{8,10},{9,11},{10,... | collective-permute-start | bytes 61448 | tf_op jit(solution)/shard_map/ppermute | solution.py:16
  13.3 1.3 collective-permute-start.7
  14.6 0.8 collective-permute-start.6
  15.5 1.3 collective-permute-start.1
  16.9 0.9 collective-permute-start.5
  17.8 0.6 collective-permute-done.1
  18.5 15.7 %collective-permute-done.7 = bf16[2,80,1280]{2,1,0:T(8,128)(2,1)S(1)} collective-permute-done((bf16[2,80,1280]{2,1,0:T(8,128)(2,1)S(1)}, bf16[2,80,1280]{2,1,0:T(8,128)(2,1)S(1)}, u32[]{:S(2)}, u32[]{:S(2)}) %collective-permute-start.7) | collective-permute-done | bytes 409632 | tf_op jit(solution)/shard_map/ppermute | solution.py:16
  34.2 2.8 %collective-permute-start.11 = (bf16[32,1280]{1,0:T(8,128)(2,1)S(1)}, bf16[32,1280]{1,0:T(8,128)(2,1)S(1)}, u32[]{:S(2)}, u32[]{:S(2)}) collective-permute-start(bf16[32,1280]{1,0:T(8,128)(2,1)S(1)} %pad_maximum_fusion.11), channel_id=1, source_target_pairs={{0,8},{1,9},{2,10},{3,11},{4,12},{5,13},{6,14},{7,15},{8,0},{9,1},... | collective-permute-start | bytes 245768 | tf_op jit(solution)/shard_map/ppermute | solution.py:16
  37.2 0.9 collective-permute-start.9
  38.0 2.0 %collective-permute-start.10 = (bf16[2,80,1280]{2,1,0:T(8,128)(2,1)S(1)}, bf16[2,80,1280]{2,1,0:T(8,128)(2,1)S(1)}, u32[]{:S(2)}, u32[]{:S(2)}) collective-permute-start(bf16[2,80,1280]{2,1,0:T(8,128)(2,1)S(1)} %pad_maximum_fusion.6), channel_id=1, source_target_pairs={{0,192},{16,208},{32,224},{48,240},{64,128},{80,144},{96,160},{112... | collective-permute-start | bytes 1228808 | tf_op jit(solution)/shard_map/ppermute | solution.py:16
  40.1 1.7 %collective-permute-start.12 = (bf16[64,1280]{1,0:T(8,128)(2,1)S(1)}, bf16[64,1280]{1,0:T(8,128)(2,1)S(1)}, u32[]{:S(2)}, u32[]{:S(2)}) collective-permute-start(bf16[64,1280]{1,0:T(8,128)(2,1)S(1)} %pad_maximum_fusion.10), channel_id=1, source_target_pairs={{0,1},{1,0},{2,3},{3,2},{4,5},{5,4},{6,7},{7,6},{8,9},{9,8},{10,11... | collective-permute-start | bytes 491528 | tf_op jit(solution)/shard_map/ppermute | solution.py:16
  41.7 1.0 collective-permute-done.12
  42.8 6.6 %slots.1 = (bf16[64,1280]{1,0:T(8,128)(2,1)S(1)}, f32[64,256]{1,0:T(8,128)S(1)}, f32[64,256]{1,0:T(8,128)S(1)}, bf16[8,64,256]{2,1,0:T(8,128)(2,1)S(1)}) custom-call(bf16[128,1280]{1,0:T(8,128)(2,1)S(1)} %constant_dynamic-update-slice_fusion.table, bf16[8,256,1280]{2,1,0:T(8,128)(2,1)S(1)} %copy-done), custom_call_target="tpu_custom_call" | custom-call | flops 754974720 | bytes 5242880 | tf_op jit(solution)/shard_map/slots/pallas_call | solution.py:102
  49.4 0.8 fusion
  50.2 0.4 spread.1
  50.7 6.1 %collective-permute-done.9.refs_7_ = bf16[2,2,80,1280]{3,2,1,0:T(8,128)(2,1)S(1)} collective-permute-done((bf16[2,2,80,1280]{3,2,1,0:T(8,128)(2,1)S(1)}, bf16[2,2,80,1280]{3,2,1,0:T(8,128)(2,1)S(1)}, u32[]{:S(2)}, u32[]{:S(2)}) %collective-permute-start.9) | collective-permute-done | bytes 819232 | tf_op jit(solution)/shard_map/ppermute | solution.py:16
  56.8 2.7 %collective-permute-start.15 = (bf16[128,1280]{1,0:T(8,128)(2,1)S(1)}, bf16[128,1280]{1,0:T(8,128)(2,1)S(1)}, u32[]{:S(2)}, u32[]{:S(2)}) collective-permute-start(bf16[128,1280]{1,0:T(8,128)(2,1)S(1)} %pad_maximum_fusion.8), channel_id=1, source_target_pairs={{0,128},{16,144},{32,160},{48,176},{64,192},{80,208},{96,224},{112... | collective-permute-start | bytes 983048 | tf_op jit(solution)/shard_map/ppermute | solution.py:16
  59.5 1.2 collective-permute-start.14
  60.7 1.8 %collective-permute-start.18 = (bf16[2,80,1280]{2,1,0:T(8,128)(2,1)S(1)}, bf16[2,80,1280]{2,1,0:T(8,128)(2,1)S(1)}, u32[]{:S(2)}, u32[]{:S(2)}) collective-permute-start(bf16[2,80,1280]{2,1,0:T(8,128)(2,1)S(1)} %slice_bitcast_fusion), channel_id=1, source_target_pairs={{0,48},{16,32},{32,16},{48,0},{64,112},{80,96},{96,80},{112,64},{1... | collective-permute-start | bytes 1228808 | tf_op jit(solution)/shard_map/ppermute | solution.py:16
  62.5 9.4 %collective-permute-done.16 = bf16[128,1280]{1,0:T(8,128)(2,1)S(1)} collective-permute-done((bf16[128,1280]{1,0:T(8,128)(2,1)S(1)}, bf16[128,1280]{1,0:T(8,128)(2,1)S(1)}, u32[]{:S(2)}, u32[]{:S(2)}) %collective-permute-start.16) | collective-permute-done | bytes 327712 | tf_op jit(solution)/shard_map/ppermute | solution.py:16
  72.1 1.5 collective-permute-start.20
  73.6 0.6 collective-permute-start.19
  74.2 3.7 %collective-permute-done.18.refs_9_ = bf16[2,80,1280]{2,1,0:T(8,128)(2,1)S(1)} collective-permute-done((bf16[2,80,1280]{2,1,0:T(8,128)(2,1)S(1)}, bf16[2,80,1280]{2,1,0:T(8,128)(2,1)S(1)}, u32[]{:S(2)}, u32[]{:S(2)}) %collective-permute-start.18) | collective-permute-done | bytes 409632 | tf_op jit(solution)/shard_map/ppermute | solution.py:16
  77.9 3.2 %collective-permute-done.17.refs_8_ = bf16[2,80,1280]{2,1,0:T(8,128)(2,1)S(1)} collective-permute-done((bf16[2,80,1280]{2,1,0:T(8,128)(2,1)S(1)}, bf16[2,80,1280]{2,1,0:T(8,128)(2,1)S(1)}, u32[]{:S(2)}, u32[]{:S(2)}) %collective-permute-start.17) | collective-permute-done | bytes 409632 | tf_op jit(solution)/shard_map/ppermute | solution.py:16
  81.2 1.2 collective-permute-done.20.refs_14_
  82.3 3.2 %collective-permute-done.19.refs_13_ = bf16[80,1280]{1,0:T(8,128)(2,1)S(1)} collective-permute-done((bf16[80,1280]{1,0:T(8,128)(2,1)S(1)}, bf16[80,1280]{1,0:T(8,128)(2,1)S(1)}, u32[]{:S(2)}, u32[]{:S(2)}) %collective-permute-start.19) | collective-permute-done | bytes 204832 | tf_op jit(solution)/shard_map/ppermute | solution.py:16
  85.7 4.0 %ffn.1 = (f32[64,1280]{1,0:T(8,128)S(1)}, bf16[64,1280]{1,0:T(8,128)(2,1)S(1)}, bf16[64,1280]{1,0:T(8,128)(2,1)S(1)}, bf16[64,1280]{1,0:T(8,128)(2,1)S(1)}, f32[...) custom-call(bf16[256,1280]{1,0:T(8,128)(2,1)S(1)} %get-tuple-element, ...), custom_call_target="tpu_custom_call" | custom-call | tf_op jit(solution)/shard_map/ffn/pallas_call | solution.py:61
  89.8 2.1 %collective-permute-start.26 = (bf16[64,1280]{1,0:T(8,128)(2,1)S(1)}, bf16[64,1280]{1,0:T(8,128)(2,1)S(1)}, u32[]{:S(2)}, u32[]{:S(2)}) collective-permute-start(bf16[64,1280]{1,0:T(8,128)(2,1)S(1)} %get-tuple-element.87), channel_id=1, source_target_pairs={{0,128},{16,144},{32,160},{48,176},{64,192},{80,208},{96,224},{112... | collective-permute-start | bytes 491528 | tf_op jit(solution)/shard_map/ppermute | solution.py:16
  91.9 1.5 collective-permute-start.27
  93.4 2.1 %collective-permute-start.23 = (bf16[64,1280]{1,0:T(8,128)(2,1)S(1)}, bf16[64,1280]{1,0:T(8,128)(2,1)S(1)}, u32[]{:S(2)}, u32[]{:S(2)}) collective-permute-start(bf16[64,1280]{1,0:T(8,128)(2,1)S(1)} %get-tuple-element.79), channel_id=1, source_target_pairs={{0,128},{16,144},{32,160},{48,176},{64,192},{80,208},{96,224},{112... | collective-permute-start | bytes 491528 | tf_op jit(solution)/shard_map/ppermute | solution.py:16
  95.4 1.5 collective-permute-start.24
  97.0 3.5 %collective-permute-done.27 = bf16[64,1280]{1,0:T(8,128)(2,1)S(1)} collective-permute-done((bf16[64,1280]{1,0:T(8,128)(2,1)S(1)}, bf16[64,1280]{1,0:T(8,128)(2,1)S(1)}, u32[]{:S(2)}, u32[]{:S(2)}) %collective-permute-start.27) | collective-permute-done | bytes 163872 | tf_op jit(solution)/shard_map/ppermute | solution.py:16
  100.5 2.1 %combine_grad.1 = (f32[64,256]{1,0:T(8,128)S(1)}, f32[8,256]{1,0:T(8,128)S(1)}) custom-call(f32[64,1280]{1,0:T(8,128)S(1)} %add_add_fusion.refs_0_, bf16[8,256,1280]{2,1,0:T(8,128)(2,1)S(1)} %copy-done.1, f32[64,256]{1,0:T(8,128)S(1)} %get-tuple-element.60.refs_2_), custom_call_target="tpu_custom_call" | custom-call | tf_op jit(solution)/shard_map/combine_grad/pallas_call | solution.py:185
  102.6 7.9 %collective-permute-start.30 = (f32[8,256]{1,0:T(8,128)S(1)}, f32[8,256]{1,0:T(8,128)S(1)}, u32[]{:S(2)}, u32[]{:S(2)}) collective-permute-start(f32[8,256]{1,0:T(8,128)S(1)} %get-tuple-element.93), channel_id=1, source_target_pairs={{0,3},{1,2},{2,1},{3,0},{4,7},{5,6},{6,5},{7,4},{8,11},{9,10},{10,... | collective-permute-start | bytes 24584 | tf_op jit(solution)/shard_map/ppermute | solution.py:16
  110.5 4.8 %collective-permute-start.29 = (f32[8,256]{1,0:T(8,128)S(1)}, f32[8,256]{1,0:T(8,128)S(1)}, u32[]{:S(2)}, u32[]{:S(2)}) collective-permute-start(f32[8,256]{1,0:T(8,128)S(1)} %get-tuple-element.93), channel_id=1, source_target_pairs={{0,2},{1,3},{2,0},{3,1},{4,6},{5,7},{6,4},{7,5},{8,10},{9,11},{10,... | collective-permute-start | bytes 24584 | tf_op jit(solution)/shard_map/ppermute | solution.py:16
  115.2 1.5 collective-permute-done.23
  116.7 0.5 collective-permute-done.29
  117.2 0.9 collective-permute-start.33
  118.2 1.3 collective-permute-start.32
  119.4 1.1 collective-permute-start.31
  120.6 2.3 %dispatch_grad.1 = f32[64,256]{1,0:T(8,128)S(1)} custom-call(f32[64,1280]{1,0:T(8,128)S(1)} %get-tuple-element.109.refs_0_, bf16[8,256,1280]{2,1,0:T(8,128)(2,1)S(1)} %copy-done, f32[64,256]{1,0:T(8,128)S(1)} %get-tuple-element.84.refs_2_), custom_call_target="tpu_custom_call" | custom-call | tf_op jit(solution)/shard_map/dispatch_grad/pallas_call | solution.py:185
  123.1 4.6 %collective-permute-start.35 = (bf16[64,1536]{1,0:T(8,128)(2,1)S(1)}, bf16[64,1536]{1,0:T(8,128)(2,1)S(1)}, u32[]{:S(2)}, u32[]{:S(2)}) collective-permute-start(bf16[64,1536]{1,0:T(8,128)(2,1)S(1)} %get-tuple-element.127), channel_id=1, source_target_pairs={{0,2},{1,3},{2,0},{3,1},{4,6},{5,7},{6,4},{7,5},{8,10},{9,11},{10,... | collective-permute-start | bytes 589832 | tf_op jit(solution)/shard_map/ppermute | solution.py:16
  127.7 0.8 convolution_bitcast_fusion
  128.5 9.4 %collective-permute-start.34 = (f32[8,1280]{1,0:T(8,128)S(1)}, f32[8,1280]{1,0:T(8,128)S(1)}, u32[]{:S(2)}, u32[]{:S(2)}) collective-permute-start(f32[8,1280]{1,0:T(8,128)S(1)} %convolution_bitcast_fusion), channel_id=1, source_target_pairs={{0,64},{16,80},{32,96},{48,112},{64,0},{80,16},{96,32},{112,48},{1... | collective-permute-start | bytes 122888 | tf_op jit(solution)/shard_map/ppermute | solution.py:16
  137.9 3.8 %collective-permute-done.34 = f32[8,1280]{1,0:T(8,128)S(1)} collective-permute-done((f32[8,1280]{1,0:T(8,128)S(1)}, f32[8,1280]{1,0:T(8,128)S(1)}, u32[]{:S(2)}, u32[]{:S(2)}) %collective-permute-start.34) | collective-permute-done | bytes 40992 | tf_op jit(solution)/shard_map/ppermute | solution.py:16
  141.8 1.3 collective-permute-start.38
  143.1 1.1 collective-permute-start.37
  144.1 1.0 collective-permute-start.36
  145.1 2.7 %collective-permute-start.39 = (f32[8,1280]{1,0:T(8,128)S(1)}, f32[8,1280]{1,0:T(8,128)S(1)}, u32[]{:S(2)}, u32[]{:S(2)}) collective-permute-start(f32[8,1280]{1,0:T(8,128)S(1)} %add.88), channel_id=1, source_target_pairs={{0,128},{16,144},{32,160},{48,176},{64,192},{80,208},{96,224},{112... | collective-permute-start | bytes 122888 | tf_op jit(solution)/shard_map/ppermute | solution.py:16
  147.8 1.7 %collective-permute-done.39 = f32[8,1280]{1,0:T(8,128)S(1)} collective-permute-done((f32[8,1280]{1,0:T(8,128)S(1)}, f32[8,1280]{1,0:T(8,128)S(1)}, u32[]{:S(2)}, u32[]{:S(2)}) %collective-permute-start.39) | collective-permute-done | bytes 40992 | tf_op jit(solution)/shard_map/ppermute | solution.py:16
  149.5 0.3 collective-permute-start.40
  149.8 2.8 %collective-permute-done.40 = f32[8,1280]{1,0:T(8,128)S(1)} collective-permute-done((f32[8,1280]{1,0:T(8,128)S(1)}, f32[8,1280]{1,0:T(8,128)S(1)}, u32[]{:S(2)}, u32[]{:S(2)}) %collective-permute-start.40) | collective-permute-done | bytes 40992 | tf_op jit(solution)/shard_map/ppermute | solution.py:16
  152.6 0.9 collective-permute-start.41
  153.6 3.4 %collective-permute-done.41 = f32[8,1280]{1,0:T(8,128)S(1)} collective-permute-done((f32[8,1280]{1,0:T(8,128)S(1)}, f32[8,1280]{1,0:T(8,128)S(1)}, u32[]{:S(2)}, u32[]{:S(2)}) %collective-permute-start.41) | collective-permute-done | bytes 40992 | tf_op jit(solution)/shard_map/ppermute | solution.py:16
  157.0 0.6 add.91
  157.6 3.4 %collective-permute-done.38.three = bf16[2,64,1536]{2,1,0:T(8,128)(2,1)S(1)} collective-permute-done((bf16[2,64,1536]{2,1,0:T(8,128)(2,1)S(1)}, bf16[2,64,1536]{2,1,0:T(8,128)(2,1)S(1)}, u32[]{:S(2)}, u32[]{:S(2)}) %collective-permute-start.38) | collective-permute-done | bytes 393248 | tf_op jit(solution)/shard_map/ppermute | solution.py:16
  161.0 0.6 collective-permute-done.36.one
  161.6 1.3 token_grad.1
  162.9 0.6 collective-permute-start.42
  163.5 1.7 %collective-permute-done.42 = f32[128,1280]{1,0:T(8,128)S(1)} collective-permute-done((f32[128,1280]{1,0:T(8,128)S(1)}, f32[128,1280]{1,0:T(8,128)S(1)}, u32[]{:S(2)}, u32[]{:S(2)}) %collective-permute-start.42) | collective-permute-done | bytes 655392 | tf_op jit(solution)/shard_map/ppermute | solution.py:16
  165.2 0.8 add_convert_fusion
  (75 shorter events, 1.4 us)
Async XLA Ops:
  0.6 1.5 copy-start.2
  2.1 4.2 %copy-start.3 = (bf16[1280,8]{0,1:T(8,128)(2,1)S(1)}, bf16[1280,8]{0,1:T(8,128)(2,1)}, u32[]{:S(2)}) copy-start(bf16[1280,8]{0,1:T(8,128)(2,1)} %param.7) | copy-start | bytes 61444
  2.3 14.6 %collective-permute-start.4 = (bf16[2,80,1280]{2,1,0:T(8,128)(2,1)S(1)}, bf16[2,80,1280]{2,1,0:T(8,128)(2,1)S(1)}, u32[]{:S(2)}, u32[]{:S(2)}) collective-permute-start(bf16[2,80,1280]{2,1,0:T(8,128)(2,1)S(1)} %pad_maximum_fusion.3.refs_0_), channel_id=1, source_target_pairs={{0,16},{16,0},{32,48},{48,32},{64,80},{80,64},{96,112},{112,96},{1... | collective-permute-start | bytes 1228808 | tf_op jit(solution)/shard_map/ppermute | solution.py:16
  4.5 13.3 %collective-permute-start.2 = (bf16[2,80,1280]{2,1,0:T(8,128)(2,1)S(1)}, bf16[2,80,1280]{2,1,0:T(8,128)(2,1)S(1)}, u32[]{:S(2)}, u32[]{:S(2)}) collective-permute-start(bf16[2,80,1280]{2,1,0:T(8,128)(2,1)S(1)} %pad_maximum_fusion.3.refs_0_), channel_id=1, source_target_pairs={{0,48},{16,32},{32,16},{48,0},{64,112},{80,96},{96,80},{112,64},{1... | collective-permute-start | bytes 1228808 | tf_op jit(solution)/shard_map/ppermute | solution.py:16
  6.4 9.1 %collective-permute-start = (bf16[8,1280]{1,0:T(8,128)(2,1)S(1)}, bf16[8,1280]{1,0:T(8,128)(2,1)S(1)}, u32[]{:S(2)}, u32[]{:S(2)}) collective-permute-start(bf16[8,1280]{1,0:T(8,128)(2,1)S(1)} %bitcast.68), channel_id=1, source_target_pairs={{0,2},{1,3},{2,0},{3,1},{4,6},{5,7},{6,4},{7,5},{8,10},{9,11},{10,... | collective-permute-start | bytes 61448 | tf_op jit(solution)/shard_map/ppermute | solution.py:16
  13.3 20.9 %collective-permute-start.7 = (bf16[2,80,1280]{2,1,0:T(8,128)(2,1)S(1)}, bf16[2,80,1280]{2,1,0:T(8,128)(2,1)S(1)}, u32[]{:S(2)}, u32[]{:S(2)}) collective-permute-start(bf16[2,80,1280]{2,1,0:T(8,128)(2,1)S(1)} %pad_maximum_fusion.5), channel_id=1, source_target_pairs={{0,128},{16,144},{32,160},{48,176},{64,192},{80,208},{96,224},{112... | collective-permute-start | bytes 1228808 | tf_op jit(solution)/shard_map/ppermute | solution.py:16
  14.6 28.2 %copy-start = (bf16[8,256,1280]{2,1,0:T(8,128)(2,1)S(1)}, bf16[8,256,1280]{2,1,0:T(8,128)(2,1)}, u32[]{:S(2)}) copy-start(bf16[8,256,1280]{2,1,0:T(8,128)(2,1)} %refs_1_.2) | copy-start | bytes 15728644
  14.6 19.6 %collective-permute-start.6 = (bf16[2,80,1280]{2,1,0:T(8,128)(2,1)S(1)}, bf16[2,80,1280]{2,1,0:T(8,128)(2,1)S(1)}, u32[]{:S(2)}, u32[]{:S(2)}) collective-permute-start(bf16[2,80,1280]{2,1,0:T(8,128)(2,1)S(1)} %pad_maximum_fusion.4), channel_id=1, source_target_pairs={{0,64},{16,80},{32,96},{48,112},{64,0},{80,16},{96,32},{112,48},{1... | collective-permute-start | bytes 1228808 | tf_op jit(solution)/shard_map/ppermute | solution.py:16
  15.5 2.9 %collective-permute-start.1 = (bf16[16,1280]{1,0:T(8,128)(2,1)S(1)}, bf16[16,1280]{1,0:T(8,128)(2,1)S(1)}, u32[]{:S(2)}, u32[]{:S(2)}) collective-permute-start(bf16[16,1280]{1,0:T(8,128)(2,1)S(1)} %pad_maximum_fusion.12), channel_id=1, source_target_pairs={{0,4},{1,5},{2,6},{3,7},{4,0},{5,1},{6,2},{7,3},{8,12},{9,13},{10,... | collective-permute-start | bytes 122888 | tf_op jit(solution)/shard_map/ppermute | solution.py:16
  16.9 17.4 %collective-permute-start.5 = (bf16[80,1280]{1,0:T(8,128)(2,1)S(1)}, bf16[80,1280]{1,0:T(8,128)(2,1)S(1)}, u32[]{:S(2)}, u32[]{:S(2)}) collective-permute-start(bf16[80,1280]{1,0:T(8,128)(2,1)S(1)} %slice_bitcast_fusion.2), channel_id=1, source_target_pairs={{0,48},{16,32},{32,16},{48,0},{64,112},{80,96},{96,80},{112,64},{1... | collective-permute-start | bytes 614408 | tf_op jit(solution)/shard_map/ppermute | solution.py:16
  17.7 16.5 %collective-permute-start.3 = (bf16[80,1280]{1,0:T(8,128)(2,1)S(1)}, bf16[80,1280]{1,0:T(8,128)(2,1)S(1)}, u32[]{:S(2)}, u32[]{:S(2)}) collective-permute-start(bf16[80,1280]{1,0:T(8,128)(2,1)S(1)} %slice_bitcast_fusion.3), channel_id=1, source_target_pairs={{0,16},{16,0},{32,48},{48,32},{64,80},{80,64},{96,112},{112,96},{1... | collective-permute-start | bytes 614408 | tf_op jit(solution)/shard_map/ppermute | solution.py:16
  34.2 5.8 %collective-permute-start.11 = (bf16[32,1280]{1,0:T(8,128)(2,1)S(1)}, bf16[32,1280]{1,0:T(8,128)(2,1)S(1)}, u32[]{:S(2)}, u32[]{:S(2)}) collective-permute-start(bf16[32,1280]{1,0:T(8,128)(2,1)S(1)} %pad_maximum_fusion.11), channel_id=1, source_target_pairs={{0,8},{1,9},{2,10},{3,11},{4,12},{5,13},{6,14},{7,15},{8,0},{9,1},... | collective-permute-start | bytes 245768 | tf_op jit(solution)/shard_map/ppermute | solution.py:16
  37.2 19.7 %collective-permute-start.9 = (bf16[2,2,80,1280]{3,2,1,0:T(8,128)(2,1)S(1)}, bf16[2,2,80,1280]{3,2,1,0:T(8,128)(2,1)S(1)}, u32[]{:S(2)}, u32[]{:S(2)}) collective-permute-start(bf16[2,2,80,1280]{3,2,1,0:T(8,128)(2,1)S(1)} %pad_maximum_fusion.refs_5_), channel_id=1, source_target_pairs={{0,48},{16,32},{32,16},{48,0},{64,112},{80,96},{96,80},{112,64},{1... | collective-permute-start | bytes 2457608 | tf_op jit(solution)/shard_map/ppermute | solution.py:16
  38.0 18.8 %collective-permute-start.8 = (bf16[2,2,80,1280]{3,2,1,0:T(8,128)(2,1)S(1)}, bf16[2,2,80,1280]{3,2,1,0:T(8,128)(2,1)S(1)}, u32[]{:S(2)}, u32[]{:S(2)}) collective-permute-start(bf16[2,2,80,1280]{3,2,1,0:T(8,128)(2,1)S(1)} %pad_maximum_fusion.refs_5_), channel_id=1, source_target_pairs={{0,16},{16,0},{32,48},{48,32},{64,80},{80,64},{96,112},{112,96},{1... | collective-permute-start | bytes 2457608 | tf_op jit(solution)/shard_map/ppermute | solution.py:16
  38.0 12.6 %collective-permute-start.10 = (bf16[2,80,1280]{2,1,0:T(8,128)(2,1)S(1)}, bf16[2,80,1280]{2,1,0:T(8,128)(2,1)S(1)}, u32[]{:S(2)}, u32[]{:S(2)}) collective-permute-start(bf16[2,80,1280]{2,1,0:T(8,128)(2,1)S(1)} %pad_maximum_fusion.6), channel_id=1, source_target_pairs={{0,192},{16,208},{32,224},{48,240},{64,128},{80,144},{96,160},{112... | collective-permute-start | bytes 1228808 | tf_op jit(solution)/shard_map/ppermute | solution.py:16
  40.1 2.7 %collective-permute-start.12 = (bf16[64,1280]{1,0:T(8,128)(2,1)S(1)}, bf16[64,1280]{1,0:T(8,128)(2,1)S(1)}, u32[]{:S(2)}, u32[]{:S(2)}) collective-permute-start(bf16[64,1280]{1,0:T(8,128)(2,1)S(1)} %pad_maximum_fusion.10), channel_id=1, source_target_pairs={{0,1},{1,0},{2,3},{3,2},{4,5},{5,4},{6,7},{7,6},{8,9},{9,8},{10,11... | collective-permute-start | bytes 491528 | tf_op jit(solution)/shard_map/ppermute | solution.py:16
  42.8 6.6 %copy-start.1 = (bf16[8,256,1280]{2,1,0:T(8,128)(2,1)S(1)}, bf16[8,256,1280]{2,1,0:T(8,128)(2,1)}, u32[]{:S(2)}) copy-start(bf16[8,256,1280]{2,1,0:T(8,128)(2,1)} %refs_1_.3) | copy-start | bytes 15728644
  56.8 15.1 %collective-permute-start.16 = (bf16[128,1280]{1,0:T(8,128)(2,1)S(1)}, bf16[128,1280]{1,0:T(8,128)(2,1)S(1)}, u32[]{:S(2)}, u32[]{:S(2)}) collective-permute-start(bf16[128,1280]{1,0:T(8,128)(2,1)S(1)} %pad_maximum_fusion.8), channel_id=1, source_target_pairs={{0,64},{16,80},{32,96},{48,112},{64,0},{80,16},{96,32},{112,48},{1... | collective-permute-start | bytes 983048 | tf_op jit(solution)/shard_map/ppermute | solution.py:16
  56.8 15.2 %collective-permute-start.15 = (bf16[128,1280]{1,0:T(8,128)(2,1)S(1)}, bf16[128,1280]{1,0:T(8,128)(2,1)S(1)}, u32[]{:S(2)}, u32[]{:S(2)}) collective-permute-start(bf16[128,1280]{1,0:T(8,128)(2,1)S(1)} %pad_maximum_fusion.8), channel_id=1, source_target_pairs={{0,128},{16,144},{32,160},{48,176},{64,192},{80,208},{96,224},{112... | collective-permute-start | bytes 983048 | tf_op jit(solution)/shard_map/ppermute | solution.py:16
  59.5 12.5 %collective-permute-start.14 = (bf16[2,80,1280]{2,1,0:T(8,128)(2,1)S(1)}, bf16[2,80,1280]{2,1,0:T(8,128)(2,1)S(1)}, u32[]{:S(2)}, u32[]{:S(2)}) collective-permute-start(bf16[2,80,1280]{2,1,0:T(8,128)(2,1)S(1)} %collective-permute-done.10.refs_10_), channel_id=1, source_target_pairs={{0,48},{16,32},{32,16},{48,0},{64,112},{80,96},{96,80},{112,64},{1... | collective-permute-start | bytes 1228808 | tf_op jit(solution)/shard_map/ppermute | solution.py:16
  60.7 11.3 %collective-permute-start.13 = (bf16[2,80,1280]{2,1,0:T(8,128)(2,1)S(1)}, bf16[2,80,1280]{2,1,0:T(8,128)(2,1)S(1)}, u32[]{:S(2)}, u32[]{:S(2)}) collective-permute-start(bf16[2,80,1280]{2,1,0:T(8,128)(2,1)S(1)} %collective-permute-done.10.refs_10_), channel_id=1, source_target_pairs={{0,16},{16,0},{32,48},{48,32},{64,80},{80,64},{96,112},{112,96},{1... | collective-permute-start | bytes 1228808 | tf_op jit(solution)/shard_map/ppermute | solution.py:16
  60.7 17.2 %collective-permute-start.18 = (bf16[2,80,1280]{2,1,0:T(8,128)(2,1)S(1)}, bf16[2,80,1280]{2,1,0:T(8,128)(2,1)S(1)}, u32[]{:S(2)}, u32[]{:S(2)}) collective-permute-start(bf16[2,80,1280]{2,1,0:T(8,128)(2,1)S(1)} %slice_bitcast_fusion), channel_id=1, source_target_pairs={{0,48},{16,32},{32,16},{48,0},{64,112},{80,96},{96,80},{112,64},{1... | collective-permute-start | bytes 1228808 | tf_op jit(solution)/shard_map/ppermute | solution.py:16
  72.0 9.2 %collective-permute-start.17 = (bf16[2,80,1280]{2,1,0:T(8,128)(2,1)S(1)}, bf16[2,80,1280]{2,1,0:T(8,128)(2,1)S(1)}, u32[]{:S(2)}, u32[]{:S(2)}) collective-permute-start(bf16[2,80,1280]{2,1,0:T(8,128)(2,1)S(1)} %slice_bitcast_fusion.1), channel_id=1, source_target_pairs={{0,16},{16,0},{32,48},{48,32},{64,80},{80,64},{96,112},{112,96},{1... | collective-permute-start | bytes 1228808 | tf_op jit(solution)/shard_map/ppermute | solution.py:16
  72.1 10.3 %collective-permute-start.20 = (bf16[80,1280]{1,0:T(8,128)(2,1)S(1)}, bf16[80,1280]{1,0:T(8,128)(2,1)S(1)}, u32[]{:S(2)}, u32[]{:S(2)}) collective-permute-start(bf16[80,1280]{1,0:T(8,128)(2,1)S(1)} %slice_bitcast_fusion.4), channel_id=1, source_target_pairs={{0,48},{16,32},{32,16},{48,0},{64,112},{80,96},{96,80},{112,64},{1... | collective-permute-start | bytes 614408 | tf_op jit(solution)/shard_map/ppermute | solution.py:16
  73.6 12.0 %collective-permute-start.19 = (bf16[80,1280]{1,0:T(8,128)(2,1)S(1)}, bf16[80,1280]{1,0:T(8,128)(2,1)S(1)}, u32[]{:S(2)}, u32[]{:S(2)}) collective-permute-start(bf16[80,1280]{1,0:T(8,128)(2,1)S(1)} %slice_bitcast_fusion.5), channel_id=1, source_target_pairs={{0,16},{16,0},{32,48},{48,32},{64,80},{80,64},{96,112},{112,96},{1... | collective-permute-start | bytes 614408 | tf_op jit(solution)/shard_map/ppermute | solution.py:16
  74.2 11.3 %collective-permute-start.21 = (bf16[128,1280]{1,0:T(8,128)(2,1)S(1)}, bf16[128,1280]{1,0:T(8,128)(2,1)S(1)}, u32[]{:S(2)}, u32[]{:S(2)}) collective-permute-start(bf16[128,1280]{1,0:T(8,128)(2,1)S(1)} %collective-permute-done.15), channel_id=1, source_target_pairs={{0,64},{16,80},{32,96},{48,112},{64,0},{80,16},{96,32},{112,48},{1... | collective-permute-start | bytes 983048 | tf_op jit(solution)/shard_map/ppermute | solution.py:16
  89.7 5.7 %collective-permute-start.25 = (bf16[64,1280]{1,0:T(8,128)(2,1)S(1)}, bf16[64,1280]{1,0:T(8,128)(2,1)S(1)}, u32[]{:S(2)}, u32[]{:S(2)}) collective-permute-start(bf16[64,1280]{1,0:T(8,128)(2,1)S(1)} %get-tuple-element.86), channel_id=1, source_target_pairs={{0,64},{16,80},{32,96},{48,112},{64,0},{80,16},{96,32},{112,48},{1... | collective-permute-start | bytes 491528 | tf_op jit(solution)/shard_map/ppermute | solution.py:16
  89.8 7.2 %collective-permute-start.26 = (bf16[64,1280]{1,0:T(8,128)(2,1)S(1)}, bf16[64,1280]{1,0:T(8,128)(2,1)S(1)}, u32[]{:S(2)}, u32[]{:S(2)}) collective-permute-start(bf16[64,1280]{1,0:T(8,128)(2,1)S(1)} %get-tuple-element.87), channel_id=1, source_target_pairs={{0,128},{16,144},{32,160},{48,176},{64,192},{80,208},{96,224},{112... | collective-permute-start | bytes 491528 | tf_op jit(solution)/shard_map/ppermute | solution.py:16
  91.9 8.6 %collective-permute-start.27 = (bf16[64,1280]{1,0:T(8,128)(2,1)S(1)}, bf16[64,1280]{1,0:T(8,128)(2,1)S(1)}, u32[]{:S(2)}, u32[]{:S(2)}) collective-permute-start(bf16[64,1280]{1,0:T(8,128)(2,1)S(1)} %get-tuple-element.88), channel_id=1, source_target_pairs={{0,192},{16,208},{32,224},{48,240},{64,128},{80,144},{96,160},{112... | collective-permute-start | bytes 491528 | tf_op jit(solution)/shard_map/ppermute | solution.py:16
  93.4 21.9 %collective-permute-start.22 = (bf16[64,1280]{1,0:T(8,128)(2,1)S(1)}, bf16[64,1280]{1,0:T(8,128)(2,1)S(1)}, u32[]{:S(2)}, u32[]{:S(2)}) collective-permute-start(bf16[64,1280]{1,0:T(8,128)(2,1)S(1)} %get-tuple-element.78), channel_id=1, source_target_pairs={{0,64},{16,80},{32,96},{48,112},{64,0},{80,16},{96,32},{112,48},{1... | collective-permute-start | bytes 491528 | tf_op jit(solution)/shard_map/ppermute | solution.py:16
  93.4 23.3 %collective-permute-start.23 = (bf16[64,1280]{1,0:T(8,128)(2,1)S(1)}, bf16[64,1280]{1,0:T(8,128)(2,1)S(1)}, u32[]{:S(2)}, u32[]{:S(2)}) collective-permute-start(bf16[64,1280]{1,0:T(8,128)(2,1)S(1)} %get-tuple-element.79), channel_id=1, source_target_pairs={{0,128},{16,144},{32,160},{48,176},{64,192},{80,208},{96,224},{112... | collective-permute-start | bytes 491528 | tf_op jit(solution)/shard_map/ppermute | solution.py:16
  95.4 21.3 %collective-permute-start.24 = (bf16[64,1280]{1,0:T(8,128)(2,1)S(1)}, bf16[64,1280]{1,0:T(8,128)(2,1)S(1)}, u32[]{:S(2)}, u32[]{:S(2)}) collective-permute-start(bf16[64,1280]{1,0:T(8,128)(2,1)S(1)} %get-tuple-element.80), channel_id=1, source_target_pairs={{0,192},{16,208},{32,224},{48,240},{64,128},{80,144},{96,160},{112... | collective-permute-start | bytes 491528 | tf_op jit(solution)/shard_map/ppermute | solution.py:16
  102.6 14.1 %collective-permute-start.30 = (f32[8,256]{1,0:T(8,128)S(1)}, f32[8,256]{1,0:T(8,128)S(1)}, u32[]{:S(2)}, u32[]{:S(2)}) collective-permute-start(f32[8,256]{1,0:T(8,128)S(1)} %get-tuple-element.93), channel_id=1, source_target_pairs={{0,3},{1,2},{2,1},{3,0},{4,7},{5,6},{6,5},{7,4},{8,11},{9,10},{10,... | collective-permute-start | bytes 24584 | tf_op jit(solution)/shard_map/ppermute | solution.py:16
  110.5 6.7 %collective-permute-start.29 = (f32[8,256]{1,0:T(8,128)S(1)}, f32[8,256]{1,0:T(8,128)S(1)}, u32[]{:S(2)}, u32[]{:S(2)}) collective-permute-start(f32[8,256]{1,0:T(8,128)S(1)} %get-tuple-element.93), channel_id=1, source_target_pairs={{0,2},{1,3},{2,0},{3,1},{4,6},{5,7},{6,4},{7,5},{8,10},{9,11},{10,... | collective-permute-start | bytes 24584 | tf_op jit(solution)/shard_map/ppermute | solution.py:16
  115.2 2.0 %collective-permute-start.28 = (f32[8,256]{1,0:T(8,128)S(1)}, f32[8,256]{1,0:T(8,128)S(1)}, u32[]{:S(2)}, u32[]{:S(2)}) collective-permute-start(f32[8,256]{1,0:T(8,128)S(1)} %get-tuple-element.93), channel_id=1, source_target_pairs={{0,1},{1,0},{2,3},{3,2},{4,5},{5,4},{6,7},{7,6},{8,9},{9,8},{10,11... | collective-permute-start | bytes 24584 | tf_op jit(solution)/shard_map/ppermute | solution.py:16
  117.2 5.7 %collective-permute-start.33 = (f32[8,256]{1,0:T(8,128)S(1)}, f32[8,256]{1,0:T(8,128)S(1)}, u32[]{:S(2)}, u32[]{:S(2)}) collective-permute-start(f32[8,256]{1,0:T(8,128)S(1)} %add_add_fusion.3), channel_id=1, source_target_pairs={{0,12},{1,13},{2,14},{3,15},{4,8},{5,9},{6,10},{7,11},{8,4},{9,5},... | collective-permute-start | bytes 24584 | tf_op jit(solution)/shard_map/ppermute | solution.py:16
  118.2 4.8 %collective-permute-start.32 = (f32[8,256]{1,0:T(8,128)S(1)}, f32[8,256]{1,0:T(8,128)S(1)}, u32[]{:S(2)}, u32[]{:S(2)}) collective-permute-start(f32[8,256]{1,0:T(8,128)S(1)} %add_add_fusion.3), channel_id=1, source_target_pairs={{0,8},{1,9},{2,10},{3,11},{4,12},{5,13},{6,14},{7,15},{8,0},{9,1},... | collective-permute-start | bytes 24584 | tf_op jit(solution)/shard_map/ppermute | solution.py:16
  119.4 3.5 %collective-permute-start.31 = (f32[8,256]{1,0:T(8,128)S(1)}, f32[8,256]{1,0:T(8,128)S(1)}, u32[]{:S(2)}, u32[]{:S(2)}) collective-permute-start(f32[8,256]{1,0:T(8,128)S(1)} %add_add_fusion.3), channel_id=1, source_target_pairs={{0,4},{1,5},{2,6},{3,7},{4,0},{5,1},{6,2},{7,3},{8,12},{9,13},{10,... | collective-permute-start | bytes 24584 | tf_op jit(solution)/shard_map/ppermute | solution.py:16
  123.1 18.6 %collective-permute-start.35 = (bf16[64,1536]{1,0:T(8,128)(2,1)S(1)}, bf16[64,1536]{1,0:T(8,128)(2,1)S(1)}, u32[]{:S(2)}, u32[]{:S(2)}) collective-permute-start(bf16[64,1536]{1,0:T(8,128)(2,1)S(1)} %get-tuple-element.127), channel_id=1, source_target_pairs={{0,2},{1,3},{2,0},{3,1},{4,6},{5,7},{6,4},{7,5},{8,10},{9,11},{10,... | collective-permute-start | bytes 589832 | tf_op jit(solution)/shard_map/ppermute | solution.py:16
  128.5 13.2 %collective-permute-start.34 = (f32[8,1280]{1,0:T(8,128)S(1)}, f32[8,1280]{1,0:T(8,128)S(1)}, u32[]{:S(2)}, u32[]{:S(2)}) collective-permute-start(f32[8,1280]{1,0:T(8,128)S(1)} %convolution_bitcast_fusion), channel_id=1, source_target_pairs={{0,64},{16,80},{32,96},{48,112},{64,0},{80,16},{96,32},{112,48},{1... | collective-permute-start | bytes 122888 | tf_op jit(solution)/shard_map/ppermute | solution.py:16
  141.8 19.2 %collective-permute-start.38 = (bf16[2,64,1536]{2,1,0:T(8,128)(2,1)S(1)}, bf16[2,64,1536]{2,1,0:T(8,128)(2,1)S(1)}, u32[]{:S(2)}, u32[]{:S(2)}) collective-permute-start(bf16[2,64,1536]{2,1,0:T(8,128)(2,1)S(1)} %pad_maximum_fusion.7.pair), channel_id=1, source_target_pairs={{0,12},{1,13},{2,14},{3,15},{4,8},{5,9},{6,10},{7,11},{8,4},{9,5},... | collective-permute-start | bytes 1179656 | tf_op jit(solution)/shard_map/ppermute | solution.py:16
  143.1 17.9 %collective-permute-start.37 = (bf16[2,64,1536]{2,1,0:T(8,128)(2,1)S(1)}, bf16[2,64,1536]{2,1,0:T(8,128)(2,1)S(1)}, u32[]{:S(2)}, u32[]{:S(2)}) collective-permute-start(bf16[2,64,1536]{2,1,0:T(8,128)(2,1)S(1)} %pad_maximum_fusion.7.pair), channel_id=1, source_target_pairs={{0,8},{1,9},{2,10},{3,11},{4,12},{5,13},{6,14},{7,15},{8,0},{9,1},... | collective-permute-start | bytes 1179656 | tf_op jit(solution)/shard_map/ppermute | solution.py:16
  144.1 17.4 %collective-permute-start.36 = (bf16[2,64,1536]{2,1,0:T(8,128)(2,1)S(1)}, bf16[2,64,1536]{2,1,0:T(8,128)(2,1)S(1)}, u32[]{:S(2)}, u32[]{:S(2)}) collective-permute-start(bf16[2,64,1536]{2,1,0:T(8,128)(2,1)S(1)} %pad_maximum_fusion.7.pair), channel_id=1, source_target_pairs={{0,4},{1,5},{2,6},{3,7},{4,0},{5,1},{6,2},{7,3},{8,12},{9,13},{10,... | collective-permute-start | bytes 1179656 | tf_op jit(solution)/shard_map/ppermute | solution.py:16
  145.1 4.4 %collective-permute-start.39 = (f32[8,1280]{1,0:T(8,128)S(1)}, f32[8,1280]{1,0:T(8,128)S(1)}, u32[]{:S(2)}, u32[]{:S(2)}) collective-permute-start(f32[8,1280]{1,0:T(8,128)S(1)} %add.88), channel_id=1, source_target_pairs={{0,128},{16,144},{32,160},{48,176},{64,192},{80,208},{96,224},{112... | collective-permute-start | bytes 122888 | tf_op jit(solution)/shard_map/ppermute | solution.py:16
  149.5 3.1 %collective-permute-start.40 = (f32[8,1280]{1,0:T(8,128)S(1)}, f32[8,1280]{1,0:T(8,128)S(1)}, u32[]{:S(2)}, u32[]{:S(2)}) collective-permute-start(f32[8,1280]{1,0:T(8,128)S(1)} %add.89), channel_id=1, source_target_pairs={{0,16},{16,0},{32,48},{48,32},{64,80},{80,64},{96,112},{112,96},{1... | collective-permute-start | bytes 122888 | tf_op jit(solution)/shard_map/ppermute | solution.py:16
  152.6 4.4 %collective-permute-start.41 = (f32[8,1280]{1,0:T(8,128)S(1)}, f32[8,1280]{1,0:T(8,128)S(1)}, u32[]{:S(2)}, u32[]{:S(2)}) collective-permute-start(f32[8,1280]{1,0:T(8,128)S(1)} %add.90), channel_id=1, source_target_pairs={{0,32},{16,48},{32,0},{48,16},{64,96},{80,112},{96,64},{112,80},{1... | collective-permute-start | bytes 122888 | tf_op jit(solution)/shard_map/ppermute | solution.py:16
  162.9 2.3 %collective-permute-start.42 = (f32[128,1280]{1,0:T(8,128)S(1)}, f32[128,1280]{1,0:T(8,128)S(1)}, u32[]{:S(2)}, u32[]{:S(2)}) collective-permute-start(f32[128,1280]{1,0:T(8,128)S(1)} %get-tuple-element.107), channel_id=1, source_target_pairs={{0,1},{1,0},{2,3},{3,2},{4,5},{5,4},{6,7},{7,6},{8,9},{9,8},{10,11... | collective-permute-start | bytes 1966088 | tf_op jit(solution)/shard_map/ppermute | solution.py:16

commit v10 on v9

--- a/solution.py
+++ b/solution.py
@@ -299,10 +299,10 @@
     p0, q0 = swap(r0[0], "dp", 1), swap(l0[1], "dp", 3)
     table = doubled(slot_params.T, "expert", 2, 4)
 
+    u3 = swap(after(units[3], u1), "dp", 12)
     table, p0, q0, u1, u2 = together(table, p0, q0, u1, u2)
     both = jnp.stack([u1, u2], axis=1)
     lb, rb = swap(both, "dp", 1), swap(both, "dp", 3)
-    u3 = swap(after(units[3], u1), "dp", 12)
     table = doubled(table, "expert", 8, 1)
     slot_in, dispatch, combine, near = slots_call(table, tokens)
     slot_go = jnp.einsum(
@@ -310,8 +310,8 @@
     )
     rows = jnp.concatenate([slot_in, slot_go.astype(BF16).reshape(half, width)], axis=0)
 
-    lb, rb, u3, rows = together(lb, rb, u3, rows)
     z2, z1 = swap(rows, "dp", 8), swap(rows, "dp", 4)
+    lb, rb, u3, z1 = together(lb, rb, u3, z1)
     l3, r3 = swap(u3, "dp", 1), swap(u3, "dp", 3)
     pb, qb = swap(rb[0], "dp", 1), swap(lb[1], "dp", 3)
     spread = spread_call(near)

time: 167 us -> 172 us (1.030)
  starting transfers between devices: 75.6 us -> 79.1 us
    ppermute x43, starting transfers between devices: 75.6 us -> 79.1 us  [swap(): return lax.ppermute(value, axis, [(i, i ^ k) for i in range(count)])]
    ppermute x43, waiting for transfers between devices: 67.3 us -> 69 us  [swap(): return lax.ppermute(value, axis, [(i, i ^ k) for i in range(count)])]
where the time goes in v10:
time: 172 us; the launch traced here: 171 us
  starting transfers between devices  79.1 us (46%)
  waiting for transfers between devices  69 us (40%)
  Pallas kernels  16.7 us (10%)
  other arithmetic  2.05 us (1%)
  local copies, waits for them, and re-layouts  1.74 us (1%)
    ppermute x43, starting transfers between devices, swap(): return lax.ppermute(value, axis, [(i, i ^ k) for i in range(count)])  79.1 us
    ppermute x43, waiting for transfers between devices, swap(): return lax.ppermute(value, axis, [(i, i ^ k) for i in range(count)])  69 us
    pallas_call x1, Pallas kernels, slots_call(): pl.pallas_call(slots_kernel, grid=(images // 2,), out_shape=[jax.ShapeDty...  6.63 us
    pallas_call x2, Pallas kernels, against(): pl.pallas_call(lambda *refs: against_kernel(over_tokens, *refs), grid=(im...  4.38 us
    pallas_call x1, Pallas kernels, ffn(): pl.pallas_call(ffn_kernel, out_shape=[jax.ShapeDtypeStruct((own_rows, wid...  4.04 us
  transfers between devices with their start and end apart: 43, of which 20 were waited for; matrix products, arithmetic and copies ran while one was open for 2% of the time, Pallas kernels for 7%

profile of v10, /device:TPU:1, one launch (start us, length us, event | category | flops | bytes accessed | tf_op | source)
XLA Modules:
  0.0 171.2 jit_solution(7853431714091819707)
XLA Ops:
  0.7 1.4 dynamic-slice_bitcast_fusion.1
  2.3 2.2 %collective-permute-start.4 = (bf16[2,80,1280]{2,1,0:T(8,128)(2,1)S(1)}, bf16[2,80,1280]{2,1,0:T(8,128)(2,1)S(1)}, u32[]{:S(2)}, u32[]{:S(2)}) collective-permute-start(bf16[2,80,1280]{2,1,0:T(8,128)(2,1)S(1)} %pad_maximum_fusion.3.refs_0_), channel_id=1, source_target_pairs={{0,16},{16,0},{32,48},{48,32},{64,80},{80,64},{96,112},{112,96},{1... | collective-permute-start | bytes 1228808 | tf_op jit(solution)/shard_map/ppermute | solution.py:16
  4.5 1.9 %collective-permute-start.2 = (bf16[2,80,1280]{2,1,0:T(8,128)(2,1)S(1)}, bf16[2,80,1280]{2,1,0:T(8,128)(2,1)S(1)}, u32[]{:S(2)}, u32[]{:S(2)}) collective-permute-start(bf16[2,80,1280]{2,1,0:T(8,128)(2,1)S(1)} %pad_maximum_fusion.3.refs_0_), channel_id=1, source_target_pairs={{0,48},{16,32},{32,16},{48,0},{64,112},{80,96},{96,80},{112,64},{1... | collective-permute-start | bytes 1228808 | tf_op jit(solution)/shard_map/ppermute | solution.py:16
  6.4 6.9 %collective-permute-start = (bf16[8,1280]{1,0:T(8,128)(2,1)S(1)}, bf16[8,1280]{1,0:T(8,128)(2,1)S(1)}, u32[]{:S(2)}, u32[]{:S(2)}) collective-permute-start(bf16[8,1280]{1,0:T(8,128)(2,1)S(1)} %bitcast.68), channel_id=1, source_target_pairs={{0,2},{1,3},{2,0},{3,1},{4,6},{5,7},{6,4},{7,5},{8,10},{9,11},{10,... | collective-permute-start | bytes 61448 | tf_op jit(solution)/shard_map/ppermute | solution.py:16
  13.3 1.3 collective-permute-start.7
  14.6 0.8 collective-permute-start.6
  15.5 1.3 collective-permute-start.1
  16.9 0.9 collective-permute-start.5
  17.8 0.6 collective-permute-done.1
  18.5 12.6 %collective-permute-done.6 = bf16[2,80,1280]{2,1,0:T(8,128)(2,1)S(1)} collective-permute-done((bf16[2,80,1280]{2,1,0:T(8,128)(2,1)S(1)}, bf16[2,80,1280]{2,1,0:T(8,128)(2,1)S(1)}, u32[]{:S(2)}, u32[]{:S(2)}) %collective-permute-start.6) | collective-permute-done | bytes 409632 | tf_op jit(solution)/shard_map/ppermute | solution.py:16
  31.1 1.7 %collective-permute-start.10 = (bf16[2,80,1280]{2,1,0:T(8,128)(2,1)S(1)}, bf16[2,80,1280]{2,1,0:T(8,128)(2,1)S(1)}, u32[]{:S(2)}, u32[]{:S(2)}) collective-permute-start(bf16[2,80,1280]{2,1,0:T(8,128)(2,1)S(1)} %pad_maximum_fusion.6), channel_id=1, source_target_pairs={{0,192},{16,208},{32,224},{48,240},{64,128},{80,144},{96,160},{112... | collective-permute-start | bytes 1228808 | tf_op jit(solution)/shard_map/ppermute | solution.py:16
  32.8 1.4 collective-permute-done.7
  34.2 2.7 %collective-permute-start.11 = (bf16[32,1280]{1,0:T(8,128)(2,1)S(1)}, bf16[32,1280]{1,0:T(8,128)(2,1)S(1)}, u32[]{:S(2)}, u32[]{:S(2)}) collective-permute-start(bf16[32,1280]{1,0:T(8,128)(2,1)S(1)} %pad_maximum_fusion.11), channel_id=1, source_target_pairs={{0,8},{1,9},{2,10},{3,11},{4,12},{5,13},{6,14},{7,15},{8,0},{9,1},... | collective-permute-start | bytes 245768 | tf_op jit(solution)/shard_map/ppermute | solution.py:16
  37.1 0.9 collective-permute-start.9
  37.9 1.1 collective-permute-done.11
  39.0 2.5 %collective-permute-start.12 = (bf16[64,1280]{1,0:T(8,128)(2,1)S(1)}, bf16[64,1280]{1,0:T(8,128)(2,1)S(1)}, u32[]{:S(2)}, u32[]{:S(2)}) collective-permute-start(bf16[64,1280]{1,0:T(8,128)(2,1)S(1)} %pad_maximum_fusion.10), channel_id=1, source_target_pairs={{0,1},{1,0},{2,3},{3,2},{4,5},{5,4},{6,7},{7,6},{8,9},{9,8},{10,11... | collective-permute-start | bytes 491528 | tf_op jit(solution)/shard_map/ppermute | solution.py:16
  41.5 1.0 collective-permute-done.12
  42.6 6.6 %slots.1 = (bf16[64,1280]{1,0:T(8,128)(2,1)S(1)}, f32[64,256]{1,0:T(8,128)S(1)}, f32[64,256]{1,0:T(8,128)S(1)}, bf16[8,64,256]{2,1,0:T(8,128)(2,1)S(1)}) custom-call(bf16[128,1280]{1,0:T(8,128)(2,1)S(1)} %constant_dynamic-update-slice_fusion.table, bf16[8,256,1280]{2,1,0:T(8,128)(2,1)S(1)} %copy-done), custom_call_target="tpu_custom_call" | custom-call | flops 754974720 | bytes 5242880 | tf_op jit(solution)/shard_map/slots/pallas_call | solution.py:102
  49.2 0.8 fusion
  50.0 1.3 collective-permute-start.13
  51.3 2.6 %collective-permute-start.16 = (bf16[128,1280]{1,0:T(8,128)(2,1)S(1)}, bf16[128,1280]{1,0:T(8,128)(2,1)S(1)}, u32[]{:S(2)}, u32[]{:S(2)}) collective-permute-start(bf16[128,1280]{1,0:T(8,128)(2,1)S(1)} %pad_maximum_fusion.8), channel_id=1, source_target_pairs={{0,128},{16,144},{32,160},{48,176},{64,192},{80,208},{96,224},{112... | collective-permute-start | bytes 983048 | tf_op jit(solution)/shard_map/ppermute | solution.py:16
  54.3 11.5 %collective-permute-done.13 = bf16[128,1280]{1,0:T(8,128)(2,1)S(1)} collective-permute-done((bf16[128,1280]{1,0:T(8,128)(2,1)S(1)}, bf16[128,1280]{1,0:T(8,128)(2,1)S(1)}, u32[]{:S(2)}, u32[]{:S(2)}) %collective-permute-start.13) | collective-permute-done | bytes 327712 | tf_op jit(solution)/shard_map/ppermute | solution.py:16
  65.9 0.8 collective-permute-start.15
  66.6 0.6 collective-permute-start.14
  67.3 1.6 collective-permute-start.18
  68.9 0.9 collective-permute-start.17
  69.8 7.1 %collective-permute-done.15.refs_12_ = bf16[2,80,1280]{2,1,0:T(8,128)(2,1)S(1)} collective-permute-done((bf16[2,80,1280]{2,1,0:T(8,128)(2,1)S(1)}, bf16[2,80,1280]{2,1,0:T(8,128)(2,1)S(1)}, u32[]{:S(2)}, u32[]{:S(2)}) %collective-permute-start.15) | collective-permute-done | bytes 409632 | tf_op jit(solution)/shard_map/ppermute | solution.py:16
  76.9 1.3 collective-permute-start.20
  78.2 7.4 %collective-permute-done.18.refs_9_ = bf16[2,80,1280]{2,1,0:T(8,128)(2,1)S(1)} collective-permute-done((bf16[2,80,1280]{2,1,0:T(8,128)(2,1)S(1)}, bf16[2,80,1280]{2,1,0:T(8,128)(2,1)S(1)}, u32[]{:S(2)}, u32[]{:S(2)}) %collective-permute-start.18) | collective-permute-done | bytes 409632 | tf_op jit(solution)/shard_map/ppermute | solution.py:16
  85.6 4.4 %collective-permute-done.20.refs_14_ = bf16[80,1280]{1,0:T(8,128)(2,1)S(1)} collective-permute-done((bf16[80,1280]{1,0:T(8,128)(2,1)S(1)}, bf16[80,1280]{1,0:T(8,128)(2,1)S(1)}, u32[]{:S(2)}, u32[]{:S(2)}) %collective-permute-start.20) | collective-permute-done | bytes 204832 | tf_op jit(solution)/shard_map/ppermute | solution.py:16
  90.1 4.0 %ffn.1 = (f32[64,1280]{1,0:T(8,128)S(1)}, bf16[64,1280]{1,0:T(8,128)(2,1)S(1)}, bf16[64,1280]{1,0:T(8,128)(2,1)S(1)}, bf16[64,1280]{1,0:T(8,128)(2,1)S(1)}, f32[...) custom-call(bf16[256,1280]{1,0:T(8,128)(2,1)S(1)} %get-tuple-element, ...), custom_call_target="tpu_custom_call" | custom-call | tf_op jit(solution)/shard_map/ffn/pallas_call | solution.py:61
  94.3 2.5 %collective-permute-start.26 = (bf16[64,1280]{1,0:T(8,128)(2,1)S(1)}, bf16[64,1280]{1,0:T(8,128)(2,1)S(1)}, u32[]{:S(2)}, u32[]{:S(2)}) collective-permute-start(bf16[64,1280]{1,0:T(8,128)(2,1)S(1)} %get-tuple-element.87), channel_id=1, source_target_pairs={{0,128},{16,144},{32,160},{48,176},{64,192},{80,208},{96,224},{112... | collective-permute-start | bytes 491528 | tf_op jit(solution)/shard_map/ppermute | solution.py:16
  96.8 1.0 collective-permute-start.27
  97.8 2.6 %collective-permute-start.23 = (bf16[64,1280]{1,0:T(8,128)(2,1)S(1)}, bf16[64,1280]{1,0:T(8,128)(2,1)S(1)}, u32[]{:S(2)}, u32[]{:S(2)}) collective-permute-start(bf16[64,1280]{1,0:T(8,128)(2,1)S(1)} %get-tuple-element.79), channel_id=1, source_target_pairs={{0,128},{16,144},{32,160},{48,176},{64,192},{80,208},{96,224},{112... | collective-permute-start | bytes 491528 | tf_op jit(solution)/shard_map/ppermute | solution.py:16
  100.4 0.7 collective-permute-done.25
  101.0 2.2 %collective-permute-start.24 = (bf16[64,1280]{1,0:T(8,128)(2,1)S(1)}, bf16[64,1280]{1,0:T(8,128)(2,1)S(1)}, u32[]{:S(2)}, u32[]{:S(2)}) collective-permute-start(bf16[64,1280]{1,0:T(8,128)(2,1)S(1)} %get-tuple-element.80), channel_id=1, source_target_pairs={{0,192},{16,208},{32,224},{48,240},{64,128},{80,144},{96,160},{112... | collective-permute-start | bytes 491528 | tf_op jit(solution)/shard_map/ppermute | solution.py:16
  103.2 2.4 %collective-permute-done.27 = bf16[64,1280]{1,0:T(8,128)(2,1)S(1)} collective-permute-done((bf16[64,1280]{1,0:T(8,128)(2,1)S(1)}, bf16[64,1280]{1,0:T(8,128)(2,1)S(1)}, u32[]{:S(2)}, u32[]{:S(2)}) %collective-permute-start.27) | collective-permute-done | bytes 163872 | tf_op jit(solution)/shard_map/ppermute | solution.py:16
  105.7 2.1 %combine_grad.1 = (f32[64,256]{1,0:T(8,128)S(1)}, f32[8,256]{1,0:T(8,128)S(1)}) custom-call(f32[64,1280]{1,0:T(8,128)S(1)} %add_add_fusion.refs_0_, bf16[8,256,1280]{2,1,0:T(8,128)(2,1)S(1)} %copy-done.1, f32[64,256]{1,0:T(8,128)S(1)} %get-tuple-element.60.refs_2_), custom_call_target="tpu_custom_call" | custom-call | tf_op jit(solution)/shard_map/combine_grad/pallas_call | solution.py:185
  107.8 5.9 %collective-permute-start.30 = (f32[8,256]{1,0:T(8,128)S(1)}, f32[8,256]{1,0:T(8,128)S(1)}, u32[]{:S(2)}, u32[]{:S(2)}) collective-permute-start(f32[8,256]{1,0:T(8,128)S(1)} %get-tuple-element.93), channel_id=1, source_target_pairs={{0,3},{1,2},{2,1},{3,0},{4,7},{5,6},{6,5},{7,4},{8,11},{9,10},{10,... | collective-permute-start | bytes 24584 | tf_op jit(solution)/shard_map/ppermute | solution.py:16
  113.7 5.4 %collective-permute-start.29 = (f32[8,256]{1,0:T(8,128)S(1)}, f32[8,256]{1,0:T(8,128)S(1)}, u32[]{:S(2)}, u32[]{:S(2)}) collective-permute-start(f32[8,256]{1,0:T(8,128)S(1)} %get-tuple-element.93), channel_id=1, source_target_pairs={{0,2},{1,3},{2,0},{3,1},{4,6},{5,7},{6,4},{7,5},{8,10},{9,11},{10,... | collective-permute-start | bytes 24584 | tf_op jit(solution)/shard_map/ppermute | solution.py:16
  119.2 2.0 %collective-permute-done.23 = bf16[64,1280]{1,0:T(8,128)(2,1)S(1)} collective-permute-done((bf16[64,1280]{1,0:T(8,128)(2,1)S(1)}, bf16[64,1280]{1,0:T(8,128)(2,1)S(1)}, u32[]{:S(2)}, u32[]{:S(2)}) %collective-permute-start.23) | collective-permute-done | bytes 163872 | tf_op jit(solution)/shard_map/ppermute | solution.py:16
  121.2 2.6 %collective-permute-start.33 = (f32[8,256]{1,0:T(8,128)S(1)}, f32[8,256]{1,0:T(8,128)S(1)}, u32[]{:S(2)}, u32[]{:S(2)}) collective-permute-start(f32[8,256]{1,0:T(8,128)S(1)} %add_add_fusion.3), channel_id=1, source_target_pairs={{0,12},{1,13},{2,14},{3,15},{4,8},{5,9},{6,10},{7,11},{8,4},{9,5},... | collective-permute-start | bytes 24584 | tf_op jit(solution)/shard_map/ppermute | solution.py:16
  123.8 0.6 collective-permute-start.32
  124.8 2.3 %dispatch_grad.1 = f32[64,256]{1,0:T(8,128)S(1)} custom-call(f32[64,1280]{1,0:T(8,128)S(1)} %get-tuple-element.109.refs_0_, bf16[8,256,1280]{2,1,0:T(8,128)(2,1)S(1)} %copy-done, f32[64,256]{1,0:T(8,128)S(1)} %get-tuple-element.84.refs_2_), custom_call_target="tpu_custom_call" | custom-call | tf_op jit(solution)/shard_map/dispatch_grad/pallas_call | solution.py:185
  127.1 0.7 collective-permute-done.32
  127.9 4.9 %collective-permute-start.35 = (bf16[64,1536]{1,0:T(8,128)(2,1)S(1)}, bf16[64,1536]{1,0:T(8,128)(2,1)S(1)}, u32[]{:S(2)}, u32[]{:S(2)}) collective-permute-start(bf16[64,1536]{1,0:T(8,128)(2,1)S(1)} %get-tuple-element.125), channel_id=1, source_target_pairs={{0,2},{1,3},{2,0},{3,1},{4,6},{5,7},{6,4},{7,5},{8,10},{9,11},{10,... | collective-permute-start | bytes 589832 | tf_op jit(solution)/shard_map/ppermute | solution.py:16
  132.8 0.8 convolution_bitcast_fusion
  133.6 9.7 %collective-permute-start.34 = (f32[8,1280]{1,0:T(8,128)S(1)}, f32[8,1280]{1,0:T(8,128)S(1)}, u32[]{:S(2)}, u32[]{:S(2)}) collective-permute-start(f32[8,1280]{1,0:T(8,128)S(1)} %convolution_bitcast_fusion), channel_id=1, source_target_pairs={{0,64},{16,80},{32,96},{48,112},{64,0},{80,16},{96,32},{112,48},{1... | collective-permute-start | bytes 122888 | tf_op jit(solution)/shard_map/ppermute | solution.py:16
  143.3 2.9 %collective-permute-done.34 = f32[8,1280]{1,0:T(8,128)S(1)} collective-permute-done((f32[8,1280]{1,0:T(8,128)S(1)}, f32[8,1280]{1,0:T(8,128)S(1)}, u32[]{:S(2)}, u32[]{:S(2)}) %collective-permute-start.34) | collective-permute-done | bytes 40992 | tf_op jit(solution)/shard_map/ppermute | solution.py:16
  146.2 1.6 collective-permute-start.38
  147.8 0.6 collective-permute-start.37
  148.4 1.2 collective-permute-start.36
  149.6 3.7 %collective-permute-start.39 = (f32[8,1280]{1,0:T(8,128)S(1)}, f32[8,1280]{1,0:T(8,128)S(1)}, u32[]{:S(2)}, u32[]{:S(2)}) collective-permute-start(f32[8,1280]{1,0:T(8,128)S(1)} %add.88), channel_id=1, source_target_pairs={{0,128},{16,144},{32,160},{48,176},{64,192},{80,208},{96,224},{112... | collective-permute-start | bytes 122888 | tf_op jit(solution)/shard_map/ppermute | solution.py:16
  153.3 1.7 collective-permute-done.39
  155.0 3.1 %collective-permute-done.40 = f32[8,1280]{1,0:T(8,128)S(1)} collective-permute-done((f32[8,1280]{1,0:T(8,128)S(1)}, f32[8,1280]{1,0:T(8,128)S(1)}, u32[]{:S(2)}, u32[]{:S(2)}) %collective-permute-start.40) | collective-permute-done | bytes 40992 | tf_op jit(solution)/shard_map/ppermute | solution.py:16
  158.1 1.1 collective-permute-start.41
  159.2 3.3 %collective-permute-done.41 = f32[8,1280]{1,0:T(8,128)S(1)} collective-permute-done((f32[8,1280]{1,0:T(8,128)S(1)}, f32[8,1280]{1,0:T(8,128)S(1)}, u32[]{:S(2)}, u32[]{:S(2)}) %collective-permute-start.41) | collective-permute-done | bytes 40992 | tf_op jit(solution)/shard_map/ppermute | solution.py:16
  162.5 0.6 add.91
  163.1 2.4 %collective-permute-done.38.three = bf16[2,64,1536]{2,1,0:T(8,128)(2,1)S(1)} collective-permute-done((bf16[2,64,1536]{2,1,0:T(8,128)(2,1)S(1)}, bf16[2,64,1536]{2,1,0:T(8,128)(2,1)S(1)}, u32[]{:S(2)}, u32[]{:S(2)}) %collective-permute-start.38) | collective-permute-done | bytes 393248 | tf_op jit(solution)/shard_map/ppermute | solution.py:16
  165.5 0.9 collective-permute-done.36.one
  166.4 1.3 token_grad.1
  167.7 1.0 collective-permute-start.42
  168.7 1.7 %collective-permute-done.42 = f32[128,1280]{1,0:T(8,128)S(1)} collective-permute-done((f32[128,1280]{1,0:T(8,128)S(1)}, f32[128,1280]{1,0:T(8,128)S(1)}, u32[]{:S(2)}, u32[]{:S(2)}) %collective-permute-start.42) | collective-permute-done | bytes 655392 | tf_op jit(solution)/shard_map/ppermute | solution.py:16
  170.4 0.8 add_convert_fusion
  (74 shorter events, 2.0 us)
Async XLA Ops:
  0.6 1.5 copy-start.2
  2.1 4.2 %copy-start.3 = (bf16[1280,8]{0,1:T(8,128)(2,1)S(1)}, bf16[1280,8]{0,1:T(8,128)(2,1)}, u32[]{:S(2)}) copy-start(bf16[1280,8]{0,1:T(8,128)(2,1)} %param.7) | copy-start | bytes 61444
  2.3 14.6 %collective-permute-start.4 = (bf16[2,80,1280]{2,1,0:T(8,128)(2,1)S(1)}, bf16[2,80,1280]{2,1,0:T(8,128)(2,1)S(1)}, u32[]{:S(2)}, u32[]{:S(2)}) collective-permute-start(bf16[2,80,1280]{2,1,0:T(8,128)(2,1)S(1)} %pad_maximum_fusion.3.refs_0_), channel_id=1, source_target_pairs={{0,16},{16,0},{32,48},{48,32},{64,80},{80,64},{96,112},{112,96},{1... | collective-permute-start | bytes 1228808 | tf_op jit(solution)/shard_map/ppermute | solution.py:16
  4.5 13.3 %collective-permute-start.2 = (bf16[2,80,1280]{2,1,0:T(8,128)(2,1)S(1)}, bf16[2,80,1280]{2,1,0:T(8,128)(2,1)S(1)}, u32[]{:S(2)}, u32[]{:S(2)}) collective-permute-start(bf16[2,80,1280]{2,1,0:T(8,128)(2,1)S(1)} %pad_maximum_fusion.3.refs_0_), channel_id=1, source_target_pairs={{0,48},{16,32},{32,16},{48,0},{64,112},{80,96},{96,80},{112,64},{1... | collective-permute-start | bytes 1228808 | tf_op jit(solution)/shard_map/ppermute | solution.py:16
  6.4 9.1 %collective-permute-start = (bf16[8,1280]{1,0:T(8,128)(2,1)S(1)}, bf16[8,1280]{1,0:T(8,128)(2,1)S(1)}, u32[]{:S(2)}, u32[]{:S(2)}) collective-permute-start(bf16[8,1280]{1,0:T(8,128)(2,1)S(1)} %bitcast.68), channel_id=1, source_target_pairs={{0,2},{1,3},{2,0},{3,1},{4,6},{5,7},{6,4},{7,5},{8,10},{9,11},{10,... | collective-permute-start | bytes 61448 | tf_op jit(solution)/shard_map/ppermute | solution.py:16
  13.3 20.9 %collective-permute-start.7 = (bf16[2,80,1280]{2,1,0:T(8,128)(2,1)S(1)}, bf16[2,80,1280]{2,1,0:T(8,128)(2,1)S(1)}, u32[]{:S(2)}, u32[]{:S(2)}) collective-permute-start(bf16[2,80,1280]{2,1,0:T(8,128)(2,1)S(1)} %pad_maximum_fusion.5), channel_id=1, source_target_pairs={{0,128},{16,144},{32,160},{48,176},{64,192},{80,208},{96,224},{112... | collective-permute-start | bytes 1228808 | tf_op jit(solution)/shard_map/ppermute | solution.py:16
  14.6 27.9 %copy-start = (bf16[8,256,1280]{2,1,0:T(8,128)(2,1)S(1)}, bf16[8,256,1280]{2,1,0:T(8,128)(2,1)}, u32[]{:S(2)}) copy-start(bf16[8,256,1280]{2,1,0:T(8,128)(2,1)} %refs_1_.2) | copy-start | bytes 15728644
  14.6 16.4 %collective-permute-start.6 = (bf16[2,80,1280]{2,1,0:T(8,128)(2,1)S(1)}, bf16[2,80,1280]{2,1,0:T(8,128)(2,1)S(1)}, u32[]{:S(2)}, u32[]{:S(2)}) collective-permute-start(bf16[2,80,1280]{2,1,0:T(8,128)(2,1)S(1)} %pad_maximum_fusion.4), channel_id=1, source_target_pairs={{0,64},{16,80},{32,96},{48,112},{64,0},{80,16},{96,32},{112,48},{1... | collective-permute-start | bytes 1228808 | tf_op jit(solution)/shard_map/ppermute | solution.py:16
  15.5 2.9 %collective-permute-start.1 = (bf16[16,1280]{1,0:T(8,128)(2,1)S(1)}, bf16[16,1280]{1,0:T(8,128)(2,1)S(1)}, u32[]{:S(2)}, u32[]{:S(2)}) collective-permute-start(bf16[16,1280]{1,0:T(8,128)(2,1)S(1)} %pad_maximum_fusion.12), channel_id=1, source_target_pairs={{0,4},{1,5},{2,6},{3,7},{4,0},{5,1},{6,2},{7,3},{8,12},{9,13},{10,... | collective-permute-start | bytes 122888 | tf_op jit(solution)/shard_map/ppermute | solution.py:16
  16.9 17.4 %collective-permute-start.5 = (bf16[80,1280]{1,0:T(8,128)(2,1)S(1)}, bf16[80,1280]{1,0:T(8,128)(2,1)S(1)}, u32[]{:S(2)}, u32[]{:S(2)}) collective-permute-start(bf16[80,1280]{1,0:T(8,128)(2,1)S(1)} %slice_bitcast_fusion.2), channel_id=1, source_target_pairs={{0,48},{16,32},{32,16},{48,0},{64,112},{80,96},{96,80},{112,64},{1... | collective-permute-start | bytes 614408 | tf_op jit(solution)/shard_map/ppermute | solution.py:16
  17.7 16.5 %collective-permute-start.3 = (bf16[80,1280]{1,0:T(8,128)(2,1)S(1)}, bf16[80,1280]{1,0:T(8,128)(2,1)S(1)}, u32[]{:S(2)}, u32[]{:S(2)}) collective-permute-start(bf16[80,1280]{1,0:T(8,128)(2,1)S(1)} %slice_bitcast_fusion.3), channel_id=1, source_target_pairs={{0,16},{16,0},{32,48},{48,32},{64,80},{80,64},{96,112},{112,96},{1... | collective-permute-start | bytes 614408 | tf_op jit(solution)/shard_map/ppermute | solution.py:16
  31.1 23.3 %collective-permute-start.10 = (bf16[2,80,1280]{2,1,0:T(8,128)(2,1)S(1)}, bf16[2,80,1280]{2,1,0:T(8,128)(2,1)S(1)}, u32[]{:S(2)}, u32[]{:S(2)}) collective-permute-start(bf16[2,80,1280]{2,1,0:T(8,128)(2,1)S(1)} %pad_maximum_fusion.6), channel_id=1, source_target_pairs={{0,192},{16,208},{32,224},{48,240},{64,128},{80,144},{96,160},{112... | collective-permute-start | bytes 1228808 | tf_op jit(solution)/shard_map/ppermute | solution.py:16
  34.2 4.8 %collective-permute-start.11 = (bf16[32,1280]{1,0:T(8,128)(2,1)S(1)}, bf16[32,1280]{1,0:T(8,128)(2,1)S(1)}, u32[]{:S(2)}, u32[]{:S(2)}) collective-permute-start(bf16[32,1280]{1,0:T(8,128)(2,1)S(1)} %pad_maximum_fusion.11), channel_id=1, source_target_pairs={{0,8},{1,9},{2,10},{3,11},{4,12},{5,13},{6,14},{7,15},{8,0},{9,1},... | collective-permute-start | bytes 245768 | tf_op jit(solution)/shard_map/ppermute | solution.py:16
  37.1 28.8 %collective-permute-start.9 = (bf16[2,2,80,1280]{3,2,1,0:T(8,128)(2,1)S(1)}, bf16[2,2,80,1280]{3,2,1,0:T(8,128)(2,1)S(1)}, u32[]{:S(2)}, u32[]{:S(2)}) collective-permute-start(bf16[2,2,80,1280]{3,2,1,0:T(8,128)(2,1)S(1)} %pad_maximum_fusion.refs_5_), channel_id=1, source_target_pairs={{0,48},{16,32},{32,16},{48,0},{64,112},{80,96},{96,80},{112,64},{1... | collective-permute-start | bytes 2457608 | tf_op jit(solution)/shard_map/ppermute | solution.py:16
  37.9 27.9 %collective-permute-start.8 = (bf16[2,2,80,1280]{3,2,1,0:T(8,128)(2,1)S(1)}, bf16[2,2,80,1280]{3,2,1,0:T(8,128)(2,1)S(1)}, u32[]{:S(2)}, u32[]{:S(2)}) collective-permute-start(bf16[2,2,80,1280]{3,2,1,0:T(8,128)(2,1)S(1)} %pad_maximum_fusion.refs_5_), channel_id=1, source_target_pairs={{0,16},{16,0},{32,48},{48,32},{64,80},{80,64},{96,112},{112,96},{1... | collective-permute-start | bytes 2457608 | tf_op jit(solution)/shard_map/ppermute | solution.py:16
  39.0 3.5 %collective-permute-start.12 = (bf16[64,1280]{1,0:T(8,128)(2,1)S(1)}, bf16[64,1280]{1,0:T(8,128)(2,1)S(1)}, u32[]{:S(2)}, u32[]{:S(2)}) collective-permute-start(bf16[64,1280]{1,0:T(8,128)(2,1)S(1)} %pad_maximum_fusion.10), channel_id=1, source_target_pairs={{0,1},{1,0},{2,3},{3,2},{4,5},{5,4},{6,7},{7,6},{8,9},{9,8},{10,11... | collective-permute-start | bytes 491528 | tf_op jit(solution)/shard_map/ppermute | solution.py:16
  42.6 6.6 %copy-start.1 = (bf16[8,256,1280]{2,1,0:T(8,128)(2,1)S(1)}, bf16[8,256,1280]{2,1,0:T(8,128)(2,1)}, u32[]{:S(2)}) copy-start(bf16[8,256,1280]{2,1,0:T(8,128)(2,1)} %refs_1_.3) | copy-start | bytes 15728644
  50.0 15.8 %collective-permute-start.13 = (bf16[128,1280]{1,0:T(8,128)(2,1)S(1)}, bf16[128,1280]{1,0:T(8,128)(2,1)S(1)}, u32[]{:S(2)}, u32[]{:S(2)}) collective-permute-start(bf16[128,1280]{1,0:T(8,128)(2,1)S(1)} %pad_maximum_fusion.8), channel_id=1, source_target_pairs={{0,64},{16,80},{32,96},{48,112},{64,0},{80,16},{96,32},{112,48},{1... | collective-permute-start | bytes 983048 | tf_op jit(solution)/shard_map/ppermute | solution.py:16
  51.3 18.5 %collective-permute-start.16 = (bf16[128,1280]{1,0:T(8,128)(2,1)S(1)}, bf16[128,1280]{1,0:T(8,128)(2,1)S(1)}, u32[]{:S(2)}, u32[]{:S(2)}) collective-permute-start(bf16[128,1280]{1,0:T(8,128)(2,1)S(1)} %pad_maximum_fusion.8), channel_id=1, source_target_pairs={{0,128},{16,144},{32,160},{48,176},{64,192},{80,208},{96,224},{112... | collective-permute-start | bytes 983048 | tf_op jit(solution)/shard_map/ppermute | solution.py:16
  65.9 11.0 %collective-permute-start.15 = (bf16[2,80,1280]{2,1,0:T(8,128)(2,1)S(1)}, bf16[2,80,1280]{2,1,0:T(8,128)(2,1)S(1)}, u32[]{:S(2)}, u32[]{:S(2)}) collective-permute-start(bf16[2,80,1280]{2,1,0:T(8,128)(2,1)S(1)} %collective-permute-done.10.refs_10_), channel_id=1, source_target_pairs={{0,48},{16,32},{32,16},{48,0},{64,112},{80,96},{96,80},{112,64},{1... | collective-permute-start | bytes 1228808 | tf_op jit(solution)/shard_map/ppermute | solution.py:16
  66.6 10.2 %collective-permute-start.14 = (bf16[2,80,1280]{2,1,0:T(8,128)(2,1)S(1)}, bf16[2,80,1280]{2,1,0:T(8,128)(2,1)S(1)}, u32[]{:S(2)}, u32[]{:S(2)}) collective-permute-start(bf16[2,80,1280]{2,1,0:T(8,128)(2,1)S(1)} %collective-permute-done.10.refs_10_), channel_id=1, source_target_pairs={{0,16},{16,0},{32,48},{48,32},{64,80},{80,64},{96,112},{112,96},{1... | collective-permute-start | bytes 1228808 | tf_op jit(solution)/shard_map/ppermute | solution.py:16
  67.3 18.3 %collective-permute-start.18 = (bf16[2,80,1280]{2,1,0:T(8,128)(2,1)S(1)}, bf16[2,80,1280]{2,1,0:T(8,128)(2,1)S(1)}, u32[]{:S(2)}, u32[]{:S(2)}) collective-permute-start(bf16[2,80,1280]{2,1,0:T(8,128)(2,1)S(1)} %slice_bitcast_fusion), channel_id=1, source_target_pairs={{0,48},{16,32},{32,16},{48,0},{64,112},{80,96},{96,80},{112,64},{1... | collective-permute-start | bytes 1228808 | tf_op jit(solution)/shard_map/ppermute | solution.py:16
  68.9 16.7 %collective-permute-start.17 = (bf16[2,80,1280]{2,1,0:T(8,128)(2,1)S(1)}, bf16[2,80,1280]{2,1,0:T(8,128)(2,1)S(1)}, u32[]{:S(2)}, u32[]{:S(2)}) collective-permute-start(bf16[2,80,1280]{2,1,0:T(8,128)(2,1)S(1)} %slice_bitcast_fusion.1), channel_id=1, source_target_pairs={{0,16},{16,0},{32,48},{48,32},{64,80},{80,64},{96,112},{112,96},{1... | collective-permute-start | bytes 1228808 | tf_op jit(solution)/shard_map/ppermute | solution.py:16
  76.9 13.1 %collective-permute-start.20 = (bf16[80,1280]{1,0:T(8,128)(2,1)S(1)}, bf16[80,1280]{1,0:T(8,128)(2,1)S(1)}, u32[]{:S(2)}, u32[]{:S(2)}) collective-permute-start(bf16[80,1280]{1,0:T(8,128)(2,1)S(1)} %slice_bitcast_fusion.4), channel_id=1, source_target_pairs={{0,48},{16,32},{32,16},{48,0},{64,112},{80,96},{96,80},{112,64},{1... | collective-permute-start | bytes 614408 | tf_op jit(solution)/shard_map/ppermute | solution.py:16
  78.1 11.9 %collective-permute-start.19 = (bf16[80,1280]{1,0:T(8,128)(2,1)S(1)}, bf16[80,1280]{1,0:T(8,128)(2,1)S(1)}, u32[]{:S(2)}, u32[]{:S(2)}) collective-permute-start(bf16[80,1280]{1,0:T(8,128)(2,1)S(1)} %slice_bitcast_fusion.5), channel_id=1, source_target_pairs={{0,16},{16,0},{32,48},{48,32},{64,80},{80,64},{96,112},{112,96},{1... | collective-permute-start | bytes 614408 | tf_op jit(solution)/shard_map/ppermute | solution.py:16
  78.2 11.9 %collective-permute-start.21 = (bf16[128,1280]{1,0:T(8,128)(2,1)S(1)}, bf16[128,1280]{1,0:T(8,128)(2,1)S(1)}, u32[]{:S(2)}, u32[]{:S(2)}) collective-permute-start(bf16[128,1280]{1,0:T(8,128)(2,1)S(1)} %collective-permute-done.16), channel_id=1, source_target_pairs={{0,64},{16,80},{32,96},{48,112},{64,0},{80,16},{96,32},{112,48},{1... | collective-permute-start | bytes 983048 | tf_op jit(solution)/shard_map/ppermute | solution.py:16
  94.2 6.9 %collective-permute-start.25 = (bf16[64,1280]{1,0:T(8,128)(2,1)S(1)}, bf16[64,1280]{1,0:T(8,128)(2,1)S(1)}, u32[]{:S(2)}, u32[]{:S(2)}) collective-permute-start(bf16[64,1280]{1,0:T(8,128)(2,1)S(1)} %get-tuple-element.86), channel_id=1, source_target_pairs={{0,64},{16,80},{32,96},{48,112},{64,0},{80,16},{96,32},{112,48},{1... | collective-permute-start | bytes 491528 | tf_op jit(solution)/shard_map/ppermute | solution.py:16
  94.3 9.0 %collective-permute-start.26 = (bf16[64,1280]{1,0:T(8,128)(2,1)S(1)}, bf16[64,1280]{1,0:T(8,128)(2,1)S(1)}, u32[]{:S(2)}, u32[]{:S(2)}) collective-permute-start(bf16[64,1280]{1,0:T(8,128)(2,1)S(1)} %get-tuple-element.87), channel_id=1, source_target_pairs={{0,128},{16,144},{32,160},{48,176},{64,192},{80,208},{96,224},{112... | collective-permute-start | bytes 491528 | tf_op jit(solution)/shard_map/ppermute | solution.py:16
  96.8 8.8 %collective-permute-start.27 = (bf16[64,1280]{1,0:T(8,128)(2,1)S(1)}, bf16[64,1280]{1,0:T(8,128)(2,1)S(1)}, u32[]{:S(2)}, u32[]{:S(2)}) collective-permute-start(bf16[64,1280]{1,0:T(8,128)(2,1)S(1)} %get-tuple-element.88), channel_id=1, source_target_pairs={{0,192},{16,208},{32,224},{48,240},{64,128},{80,144},{96,160},{112... | collective-permute-start | bytes 491528 | tf_op jit(solution)/shard_map/ppermute | solution.py:16
  97.8 21.4 %collective-permute-start.22 = (bf16[64,1280]{1,0:T(8,128)(2,1)S(1)}, bf16[64,1280]{1,0:T(8,128)(2,1)S(1)}, u32[]{:S(2)}, u32[]{:S(2)}) collective-permute-start(bf16[64,1280]{1,0:T(8,128)(2,1)S(1)} %get-tuple-element.78), channel_id=1, source_target_pairs={{0,64},{16,80},{32,96},{48,112},{64,0},{80,16},{96,32},{112,48},{1... | collective-permute-start | bytes 491528 | tf_op jit(solution)/shard_map/ppermute | solution.py:16
  97.8 23.4 %collective-permute-start.23 = (bf16[64,1280]{1,0:T(8,128)(2,1)S(1)}, bf16[64,1280]{1,0:T(8,128)(2,1)S(1)}, u32[]{:S(2)}, u32[]{:S(2)}) collective-permute-start(bf16[64,1280]{1,0:T(8,128)(2,1)S(1)} %get-tuple-element.79), channel_id=1, source_target_pairs={{0,128},{16,144},{32,160},{48,176},{64,192},{80,208},{96,224},{112... | collective-permute-start | bytes 491528 | tf_op jit(solution)/shard_map/ppermute | solution.py:16
  101.0 20.2 %collective-permute-start.24 = (bf16[64,1280]{1,0:T(8,128)(2,1)S(1)}, bf16[64,1280]{1,0:T(8,128)(2,1)S(1)}, u32[]{:S(2)}, u32[]{:S(2)}) collective-permute-start(bf16[64,1280]{1,0:T(8,128)(2,1)S(1)} %get-tuple-element.80), channel_id=1, source_target_pairs={{0,192},{16,208},{32,224},{48,240},{64,128},{80,144},{96,160},{112... | collective-permute-start | bytes 491528 | tf_op jit(solution)/shard_map/ppermute | solution.py:16
  107.8 13.4 %collective-permute-start.30 = (f32[8,256]{1,0:T(8,128)S(1)}, f32[8,256]{1,0:T(8,128)S(1)}, u32[]{:S(2)}, u32[]{:S(2)}) collective-permute-start(f32[8,256]{1,0:T(8,128)S(1)} %get-tuple-element.93), channel_id=1, source_target_pairs={{0,3},{1,2},{2,1},{3,0},{4,7},{5,6},{6,5},{7,4},{8,11},{9,10},{10,... | collective-permute-start | bytes 24584 | tf_op jit(solution)/shard_map/ppermute | solution.py:16
  113.7 7.5 %collective-permute-start.29 = (f32[8,256]{1,0:T(8,128)S(1)}, f32[8,256]{1,0:T(8,128)S(1)}, u32[]{:S(2)}, u32[]{:S(2)}) collective-permute-start(f32[8,256]{1,0:T(8,128)S(1)} %get-tuple-element.93), channel_id=1, source_target_pairs={{0,2},{1,3},{2,0},{3,1},{4,6},{5,7},{6,4},{7,5},{8,10},{9,11},{10,... | collective-permute-start | bytes 24584 | tf_op jit(solution)/shard_map/ppermute | solution.py:16
  119.2 2.0 %collective-permute-start.28 = (f32[8,256]{1,0:T(8,128)S(1)}, f32[8,256]{1,0:T(8,128)S(1)}, u32[]{:S(2)}, u32[]{:S(2)}) collective-permute-start(f32[8,256]{1,0:T(8,128)S(1)} %get-tuple-element.93), channel_id=1, source_target_pairs={{0,1},{1,0},{2,3},{3,2},{4,5},{5,4},{6,7},{7,6},{8,9},{9,8},{10,11... | collective-permute-start | bytes 24584 | tf_op jit(solution)/shard_map/ppermute | solution.py:16
  121.2 5.8 %collective-permute-start.33 = (f32[8,256]{1,0:T(8,128)S(1)}, f32[8,256]{1,0:T(8,128)S(1)}, u32[]{:S(2)}, u32[]{:S(2)}) collective-permute-start(f32[8,256]{1,0:T(8,128)S(1)} %add_add_fusion.3), channel_id=1, source_target_pairs={{0,12},{1,13},{2,14},{3,15},{4,8},{5,9},{6,10},{7,11},{8,4},{9,5},... | collective-permute-start | bytes 24584 | tf_op jit(solution)/shard_map/ppermute | solution.py:16
  123.8 4.0 %collective-permute-start.32 = (f32[8,256]{1,0:T(8,128)S(1)}, f32[8,256]{1,0:T(8,128)S(1)}, u32[]{:S(2)}, u32[]{:S(2)}) collective-permute-start(f32[8,256]{1,0:T(8,128)S(1)} %add_add_fusion.3), channel_id=1, source_target_pairs={{0,8},{1,9},{2,10},{3,11},{4,12},{5,13},{6,14},{7,15},{8,0},{9,1},... | collective-permute-start | bytes 24584 | tf_op jit(solution)/shard_map/ppermute | solution.py:16
  124.4 3.5 %collective-permute-start.31 = (f32[8,256]{1,0:T(8,128)S(1)}, f32[8,256]{1,0:T(8,128)S(1)}, u32[]{:S(2)}, u32[]{:S(2)}) collective-permute-start(f32[8,256]{1,0:T(8,128)S(1)} %add_add_fusion.3), channel_id=1, source_target_pairs={{0,4},{1,5},{2,6},{3,7},{4,0},{5,1},{6,2},{7,3},{8,12},{9,13},{10,... | collective-permute-start | bytes 24584 | tf_op jit(solution)/shard_map/ppermute | solution.py:16
  127.9 18.3 %collective-permute-start.35 = (bf16[64,1536]{1,0:T(8,128)(2,1)S(1)}, bf16[64,1536]{1,0:T(8,128)(2,1)S(1)}, u32[]{:S(2)}, u32[]{:S(2)}) collective-permute-start(bf16[64,1536]{1,0:T(8,128)(2,1)S(1)} %get-tuple-element.125), channel_id=1, source_target_pairs={{0,2},{1,3},{2,0},{3,1},{4,6},{5,7},{6,4},{7,5},{8,10},{9,11},{10,... | collective-permute-start | bytes 589832 | tf_op jit(solution)/shard_map/ppermute | solution.py:16
  133.6 12.6 %collective-permute-start.34 = (f32[8,1280]{1,0:T(8,128)S(1)}, f32[8,1280]{1,0:T(8,128)S(1)}, u32[]{:S(2)}, u32[]{:S(2)}) collective-permute-start(f32[8,1280]{1,0:T(8,128)S(1)} %convolution_bitcast_fusion), channel_id=1, source_target_pairs={{0,64},{16,80},{32,96},{48,112},{64,0},{80,16},{96,32},{112,48},{1... | collective-permute-start | bytes 122888 | tf_op jit(solution)/shard_map/ppermute | solution.py:16
  146.2 19.3 %collective-permute-start.38 = (bf16[2,64,1536]{2,1,0:T(8,128)(2,1)S(1)}, bf16[2,64,1536]{2,1,0:T(8,128)(2,1)S(1)}, u32[]{:S(2)}, u32[]{:S(2)}) collective-permute-start(bf16[2,64,1536]{2,1,0:T(8,128)(2,1)S(1)} %pad_maximum_fusion.7.pair), channel_id=1, source_target_pairs={{0,12},{1,13},{2,14},{3,15},{4,8},{5,9},{6,10},{7,11},{8,4},{9,5},... | collective-permute-start | bytes 1179656 | tf_op jit(solution)/shard_map/ppermute | solution.py:16
  147.8 17.7 %collective-permute-start.37 = (bf16[2,64,1536]{2,1,0:T(8,128)(2,1)S(1)}, bf16[2,64,1536]{2,1,0:T(8,128)(2,1)S(1)}, u32[]{:S(2)}, u32[]{:S(2)}) collective-permute-start(bf16[2,64,1536]{2,1,0:T(8,128)(2,1)S(1)} %pad_maximum_fusion.7.pair), channel_id=1, source_target_pairs={{0,8},{1,9},{2,10},{3,11},{4,12},{5,13},{6,14},{7,15},{8,0},{9,1},... | collective-permute-start | bytes 1179656 | tf_op jit(solution)/shard_map/ppermute | solution.py:16
  148.4 18.0 %collective-permute-start.36 = (bf16[2,64,1536]{2,1,0:T(8,128)(2,1)S(1)}, bf16[2,64,1536]{2,1,0:T(8,128)(2,1)S(1)}, u32[]{:S(2)}, u32[]{:S(2)}) collective-permute-start(bf16[2,64,1536]{2,1,0:T(8,128)(2,1)S(1)} %pad_maximum_fusion.7.pair), channel_id=1, source_target_pairs={{0,4},{1,5},{2,6},{3,7},{4,0},{5,1},{6,2},{7,3},{8,12},{9,13},{10,... | collective-permute-start | bytes 1179656 | tf_op jit(solution)/shard_map/ppermute | solution.py:16
  149.6 5.4 %collective-permute-start.39 = (f32[8,1280]{1,0:T(8,128)S(1)}, f32[8,1280]{1,0:T(8,128)S(1)}, u32[]{:S(2)}, u32[]{:S(2)}) collective-permute-start(f32[8,1280]{1,0:T(8,128)S(1)} %add.88), channel_id=1, source_target_pairs={{0,128},{16,144},{32,160},{48,176},{64,192},{80,208},{96,224},{112... | collective-permute-start | bytes 122888 | tf_op jit(solution)/shard_map/ppermute | solution.py:16
  155.0 3.1 %collective-permute-start.40 = (f32[8,1280]{1,0:T(8,128)S(1)}, f32[8,1280]{1,0:T(8,128)S(1)}, u32[]{:S(2)}, u32[]{:S(2)}) collective-permute-start(f32[8,1280]{1,0:T(8,128)S(1)} %add.89), channel_id=1, source_target_pairs={{0,16},{16,0},{32,48},{48,32},{64,80},{80,64},{96,112},{112,96},{1... | collective-permute-start | bytes 122888 | tf_op jit(solution)/shard_map/ppermute | solution.py:16
  158.1 4.4 %collective-permute-start.41 = (f32[8,1280]{1,0:T(8,128)S(1)}, f32[8,1280]{1,0:T(8,128)S(1)}, u32[]{:S(2)}, u32[]{:S(2)}) collective-permute-start(f32[8,1280]{1,0:T(8,128)S(1)} %add.90), channel_id=1, source_target_pairs={{0,32},{16,48},{32,0},{48,16},{64,96},{80,112},{96,64},{112,80},{1... | collective-permute-start | bytes 122888 | tf_op jit(solution)/shard_map/ppermute | solution.py:16
  167.7 2.7 %collective-permute-start.42 = (f32[128,1280]{1,0:T(8,128)S(1)}, f32[128,1280]{1,0:T(8,128)S(1)}, u32[]{:S(2)}, u32[]{:S(2)}) collective-permute-start(f32[128,1280]{1,0:T(8,128)S(1)} %get-tuple-element.107), channel_id=1, source_target_pairs={{0,1},{1,0},{2,3},{3,2},{4,5},{5,4},{6,7},{7,6},{8,9},{9,8},{10,11... | collective-permute-start | bytes 1966088 | tf_op jit(solution)/shard_map/ppermute | solution.py:16

commit v11 on v9

--- a/solution.py
+++ b/solution.py
@@ -153,8 +153,11 @@
     )(near)
 
 
-def against_kernel(over_tokens, rows, big, weight, *outs):
-    value = rows[...]
+def against_kernel(over_tokens, parts, *refs):
+    value = refs[0][...]
+    for ref in refs[1:parts]:
+        value = value + ref[...].astype(F32)
+    big, weight, *outs = refs[parts:]
     high = value.astype(BF16)
     low = (value - high.astype(F32)).astype(BF16)
     both = jnp.concatenate([high, low], axis=0)
@@ -174,7 +177,7 @@
             outs[1][pl.ds(2 * step + i, 1), :] = jnp.sum(part[8 * i : 8 * i + 8], axis=0, keepdims=True)
 
 
-def against(rows, big, weight, over_tokens):
+def against(parts, big, weight, over_tokens):
     images, count, width = big.shape
     total = images * 8
     out_shape = [jax.ShapeDtypeStruct((total, count), F32)]
@@ -183,18 +186,18 @@
         out_shape.append(jax.ShapeDtypeStruct((images, count), F32))
         out_specs.append(pl.BlockSpec((images, count), lambda i: (0, 0)))
     return pl.pallas_call(
-        lambda *refs: against_kernel(over_tokens, *refs),
+        lambda *refs: against_kernel(over_tokens, len(parts), *refs),
         grid=(images // 2,),
         out_shape=out_shape,
-        in_specs=[
-            pl.BlockSpec((16, width), lambda i: (i, 0)),
+        in_specs=[pl.BlockSpec((16, width), lambda i: (i, 0))] * len(parts)
+        + [
             pl.BlockSpec((2, count, width), lambda i: (i, 0, 0)),
             pl.BlockSpec((16, count), lambda i: (i, 0)),
         ],
         out_specs=out_specs,
         compiler_params=pltpu.CompilerParams(vmem_limit_bytes=16 * 2**20),
         name="dispatch_grad" if over_tokens else "combine_grad",
-    )(rows, big, weight)
+    )(*parts, big, weight)
 
 
 def tokens_kernel(spread, pair, one, two, three, table, mine, theirs):
@@ -261,9 +264,8 @@
     return lax.optimization_barrier(values)
 
 
-def reduce_z(own, *far):
-    one, two, three = together(*[swap(v, "dp", 4 * a) for a, v in enumerate(far, 1)])
-    return (own + one.astype(F32)) + (two.astype(F32) + three.astype(F32))
+def parts_z(own, *far):
+    return [own, *together(*[swap(v, "dp", 4 * a) for a, v in enumerate(far, 1)])]
 
 
 def all_x(v):
@@ -310,12 +312,14 @@
     )
     rows = jnp.concatenate([slot_in, slot_go.astype(BF16).reshape(half, width)], axis=0)
 
-    lb, rb, u3, rows = together(lb, rb, u3, rows)
-    z2, z1 = swap(rows, "dp", 8), swap(rows, "dp", 4)
+    u3, rows = together(u3, rows)
+    z2 = swap(rows, "dp", 8)
+    lb, rb, u3 = together(lb, rb, u3)
+    z1 = swap(after(rows, lb), "dp", 4)
     l3, r3 = swap(u3, "dp", 1), swap(u3, "dp", 3)
     pb, qb = swap(rb[0], "dp", 1), swap(lb[1], "dp", 3)
     spread = spread_call(near)
-    l3, r3, z2, spread = together(l3, r3, z2, spread)
+    l3, r3, z1, z2, spread = together(l3, r3, z1, z2, spread)
     p3, q3 = swap(r3[0], "dp", 1), swap(l3[1], "dp", 3)
     z3 = swap(z2, "dp", 4)
     pb, qb, p3, q3, z3 = together(pb, qb, p3, q3, z3)
@@ -324,12 +328,13 @@
 
     blocks = [units[0], l0, r0, p0, q0, both, lb, rb, pb, qb, u3, l3, r3, p3, q3]
     halves = ffn(rows_in, rows_go, blocks, half)
-    slot_out = reduce_z(*halves[:4])
-    slot_in_grad = reduce_z(*halves[4:])
-    part, mix = against(slot_out, out_grad, combine, False)
+    outs = parts_z(*halves[:4])
+    own_grad, one, two, three = parts_z(*halves[4:])
+    slot_in_grad = (own_grad + one.astype(F32)) + (two.astype(F32) + three.astype(F32))
+    part, mix = against(outs, out_grad, combine, False)
     mix = summed_three(mix, "expert", 1, 2, 3)
     mix = summed_three(mix, "expert", 4, 8, 12)
-    (back,) = against(slot_in_grad, tokens, dispatch, True)
+    (back,) = against([slot_in_grad], tokens, dispatch, True)
     logit_grad = back + (part - combine * jnp.repeat(mix, own, axis=0))
     logit_grad_b = logit_grad.astype(BF16)
 
@@ -341,10 +346,11 @@
     term = summed(term, "dp", 4)
     term, far = together(term, far)
     pieces = all_x(jnp.stack([near, far]))
-    term = summed(term, "dp", 8, 1, 2)
-    slot_grad = term.T
-
-    pieces[1] = after(pieces[1], term)
+    term = summed(term, "dp", 8, 1)
+    last = swap(term, "dp", 2)
+    slot_grad = (term + last).T
+
+    pieces[1] = after(pieces[1], last)
     mine, theirs = tokens_call(spread, pieces, table)
     token_grad = (mine + swap(theirs, "expert", 1)).astype(BF16)
     return (token_grad.reshape(images, -1, width), slot_grad)

time: 167 us -> 166 us (level)
  waiting for transfers between devices: 67.3 us -> 57.3 us
  starting transfers between devices: 75.6 us -> 85.3 us
    ppermute x43, waiting for transfers between devices: 67.3 us -> 57.3 us  [swap(): return lax.ppermute(value, axis, [(i, i ^ k) for i in range(count)])]
    ppermute x43, starting transfers between devices: 75.6 us -> 85.3 us  [swap(): return lax.ppermute(value, axis, [(i, i ^ k) for i in range(count)])]
where the time goes in v11:
time: 166 us
  starting transfers between devices  85.3 us (51%)
  waiting for transfers between devices  57.3 us (35%)
  Pallas kernels  16.7 us (10%)
  other arithmetic  1.98 us (1%)
  local copies, waits for them, and re-layouts  1.76 us (1%)
    ppermute x43, starting transfers between devices, swap(): return lax.ppermute(value, axis, [(i, i ^ k) for i in range(count)])  85.3 us
    ppermute x43, waiting for transfers between devices, swap(): return lax.ppermute(value, axis, [(i, i ^ k) for i in range(count)])  57.3 us
    pallas_call x1, Pallas kernels, slots_call(): pl.pallas_call(slots_kernel, grid=(images // 2,), out_shape=[jax.ShapeDty...  6.63 us
    pallas_call x2, Pallas kernels, against(): pl.pallas_call(lambda *refs: against_kernel(over_tokens, len(parts), *ref...  4.32 us
    pallas_call x1, Pallas kernels, ffn(): pl.pallas_call(ffn_kernel, out_shape=[jax.ShapeDtypeStruct((own_rows, wid...  4.04 us
  transfers between devices with their start and end apart: 43, of which 20 were waited for; matrix products, arithmetic and copies ran while one was open for 2% of the time, Pallas kernels for 7%

profile of v11, /device:TPU:1, one launch (start us, length us, event | category | flops | bytes accessed | tf_op | source)
XLA Modules:
  0.0 165.6 jit_solution(7265539049500855005)
XLA Ops:
  0.7 1.4 dynamic-slice_bitcast_fusion.1
  2.3 2.2 %collective-permute-start.4 = (bf16[2,80,1280]{2,1,0:T(8,128)(2,1)S(1)}, bf16[2,80,1280]{2,1,0:T(8,128)(2,1)S(1)}, u32[]{:S(2)}, u32[]{:S(2)}) collective-permute-start(bf16[2,80,1280]{2,1,0:T(8,128)(2,1)S(1)} %pad_maximum_fusion.3.refs_0_), channel_id=1, source_target_pairs={{0,16},{16,0},{32,48},{48,32},{64,80},{80,64},{96,112},{112,96},{1... | collective-permute-start | bytes 1228808 | tf_op jit(solution)/shard_map/ppermute | solution.py:16
  4.5 1.9 %collective-permute-start.2 = (bf16[2,80,1280]{2,1,0:T(8,128)(2,1)S(1)}, bf16[2,80,1280]{2,1,0:T(8,128)(2,1)S(1)}, u32[]{:S(2)}, u32[]{:S(2)}) collective-permute-start(bf16[2,80,1280]{2,1,0:T(8,128)(2,1)S(1)} %pad_maximum_fusion.3.refs_0_), channel_id=1, source_target_pairs={{0,48},{16,32},{32,16},{48,0},{64,112},{80,96},{96,80},{112,64},{1... | collective-permute-start | bytes 1228808 | tf_op jit(solution)/shard_map/ppermute | solution.py:16
  6.4 6.9 %collective-permute-start = (bf16[8,1280]{1,0:T(8,128)(2,1)S(1)}, bf16[8,1280]{1,0:T(8,128)(2,1)S(1)}, u32[]{:S(2)}, u32[]{:S(2)}) collective-permute-start(bf16[8,1280]{1,0:T(8,128)(2,1)S(1)} %bitcast.69), channel_id=1, source_target_pairs={{0,2},{1,3},{2,0},{3,1},{4,6},{5,7},{6,4},{7,5},{8,10},{9,11},{10,... | collective-permute-start | bytes 61448 | tf_op jit(solution)/shard_map/ppermute | solution.py:16
  13.3 1.3 collective-permute-start.7
  14.6 0.8 collective-permute-start.6
  15.5 1.3 collective-permute-start.1
  16.9 0.9 collective-permute-start.5
  17.8 0.6 collective-permute-done.1
  18.5 15.7 %collective-permute-done.7 = bf16[2,80,1280]{2,1,0:T(8,128)(2,1)S(1)} collective-permute-done((bf16[2,80,1280]{2,1,0:T(8,128)(2,1)S(1)}, bf16[2,80,1280]{2,1,0:T(8,128)(2,1)S(1)}, u32[]{:S(2)}, u32[]{:S(2)}) %collective-permute-start.7) | collective-permute-done | bytes 409632 | tf_op jit(solution)/shard_map/ppermute | solution.py:16
  34.2 2.8 %collective-permute-start.11 = (bf16[32,1280]{1,0:T(8,128)(2,1)S(1)}, bf16[32,1280]{1,0:T(8,128)(2,1)S(1)}, u32[]{:S(2)}, u32[]{:S(2)}) collective-permute-start(bf16[32,1280]{1,0:T(8,128)(2,1)S(1)} %pad_maximum_fusion.11), channel_id=1, source_target_pairs={{0,8},{1,9},{2,10},{3,11},{4,12},{5,13},{6,14},{7,15},{8,0},{9,1},... | collective-permute-start | bytes 245768 | tf_op jit(solution)/shard_map/ppermute | solution.py:16
  37.2 0.9 collective-permute-start.9
  38.0 2.0 %collective-permute-start.10 = (bf16[2,80,1280]{2,1,0:T(8,128)(2,1)S(1)}, bf16[2,80,1280]{2,1,0:T(8,128)(2,1)S(1)}, u32[]{:S(2)}, u32[]{:S(2)}) collective-permute-start(bf16[2,80,1280]{2,1,0:T(8,128)(2,1)S(1)} %pad_maximum_fusion.6), channel_id=1, source_target_pairs={{0,192},{16,208},{32,224},{48,240},{64,128},{80,144},{96,160},{112... | collective-permute-start | bytes 1228808 | tf_op jit(solution)/shard_map/ppermute | solution.py:16
  40.1 1.7 %collective-permute-start.12 = (bf16[64,1280]{1,0:T(8,128)(2,1)S(1)}, bf16[64,1280]{1,0:T(8,128)(2,1)S(1)}, u32[]{:S(2)}, u32[]{:S(2)}) collective-permute-start(bf16[64,1280]{1,0:T(8,128)(2,1)S(1)} %pad_maximum_fusion.10), channel_id=1, source_target_pairs={{0,1},{1,0},{2,3},{3,2},{4,5},{5,4},{6,7},{7,6},{8,9},{9,8},{10,11... | collective-permute-start | bytes 491528 | tf_op jit(solution)/shard_map/ppermute | solution.py:16
  41.7 1.0 collective-permute-done.12
  42.8 6.6 %slots.1 = (bf16[64,1280]{1,0:T(8,128)(2,1)S(1)}, f32[64,256]{1,0:T(8,128)S(1)}, f32[64,256]{1,0:T(8,128)S(1)}, bf16[8,64,256]{2,1,0:T(8,128)(2,1)S(1)}) custom-call(bf16[128,1280]{1,0:T(8,128)(2,1)S(1)} %constant_dynamic-update-slice_fusion.table, bf16[8,256,1280]{2,1,0:T(8,128)(2,1)S(1)} %copy-done), custom_call_target="tpu_custom_call" | custom-call | flops 754974720 | bytes 5242880 | tf_op jit(solution)/shard_map/slots/pallas_call | solution.py:102
  49.4 0.8 fusion
  50.2 0.4 spread.1
  50.7 3.8 %collective-permute-start.16 = (bf16[128,1280]{1,0:T(8,128)(2,1)S(1)}, bf16[128,1280]{1,0:T(8,128)(2,1)S(1)}, u32[]{:S(2)}, u32[]{:S(2)}) collective-permute-start(bf16[128,1280]{1,0:T(8,128)(2,1)S(1)} %pad_maximum_fusion.8), channel_id=1, source_target_pairs={{0,128},{16,144},{32,160},{48,176},{64,192},{80,208},{96,224},{112... | collective-permute-start | bytes 983048 | tf_op jit(solution)/shard_map/ppermute | solution.py:16
  54.5 2.3 %collective-permute-done.9.refs_7_ = bf16[2,2,80,1280]{3,2,1,0:T(8,128)(2,1)S(1)} collective-permute-done((bf16[2,2,80,1280]{3,2,1,0:T(8,128)(2,1)S(1)}, bf16[2,2,80,1280]{3,2,1,0:T(8,128)(2,1)S(1)}, u32[]{:S(2)}, u32[]{:S(2)}) %collective-permute-start.9) | collective-permute-done | bytes 819232 | tf_op jit(solution)/shard_map/ppermute | solution.py:16
  56.9 1.3 collective-permute-start.14
  58.1 1.5 collective-permute-start.18
  59.7 4.9 %collective-permute-done.16 = bf16[128,1280]{1,0:T(8,128)(2,1)S(1)} collective-permute-done((bf16[128,1280]{1,0:T(8,128)(2,1)S(1)}, bf16[128,1280]{1,0:T(8,128)(2,1)S(1)}, u32[]{:S(2)}, u32[]{:S(2)}) %collective-permute-start.16) | collective-permute-done | bytes 327712 | tf_op jit(solution)/shard_map/ppermute | solution.py:16
  64.6 1.5 collective-permute-start.17
  66.0 3.2 %collective-permute-done.15 = bf16[128,1280]{1,0:T(8,128)(2,1)S(1)} collective-permute-done((bf16[128,1280]{1,0:T(8,128)(2,1)S(1)}, bf16[128,1280]{1,0:T(8,128)(2,1)S(1)}, u32[]{:S(2)}, u32[]{:S(2)}) %collective-permute-start.15) | collective-permute-done | bytes 327712 | tf_op jit(solution)/shard_map/ppermute | solution.py:16
  69.3 2.1 %collective-permute-start.20 = (bf16[80,1280]{1,0:T(8,128)(2,1)S(1)}, bf16[80,1280]{1,0:T(8,128)(2,1)S(1)}, u32[]{:S(2)}, u32[]{:S(2)}) collective-permute-start(bf16[80,1280]{1,0:T(8,128)(2,1)S(1)} %slice_bitcast_fusion.4), channel_id=1, source_target_pairs={{0,48},{16,32},{32,16},{48,0},{64,112},{80,96},{96,80},{112,64},{1... | collective-permute-start | bytes 614408 | tf_op jit(solution)/shard_map/ppermute | solution.py:16
  71.4 1.9 %collective-permute-start.19 = (bf16[80,1280]{1,0:T(8,128)(2,1)S(1)}, bf16[80,1280]{1,0:T(8,128)(2,1)S(1)}, u32[]{:S(2)}, u32[]{:S(2)}) collective-permute-start(bf16[80,1280]{1,0:T(8,128)(2,1)S(1)} %slice_bitcast_fusion.5), channel_id=1, source_target_pairs={{0,16},{16,0},{32,48},{48,32},{64,80},{80,64},{96,112},{112,96},{1... | collective-permute-start | bytes 614408 | tf_op jit(solution)/shard_map/ppermute | solution.py:16
  73.3 1.7 %collective-permute-done.17.refs_8_ = bf16[2,80,1280]{2,1,0:T(8,128)(2,1)S(1)} collective-permute-done((bf16[2,80,1280]{2,1,0:T(8,128)(2,1)S(1)}, bf16[2,80,1280]{2,1,0:T(8,128)(2,1)S(1)}, u32[]{:S(2)}, u32[]{:S(2)}) %collective-permute-start.17) | collective-permute-done | bytes 409632 | tf_op jit(solution)/shard_map/ppermute | solution.py:16
  75.1 2.7 %collective-permute-done.20.refs_14_ = bf16[80,1280]{1,0:T(8,128)(2,1)S(1)} collective-permute-done((bf16[80,1280]{1,0:T(8,128)(2,1)S(1)}, bf16[80,1280]{1,0:T(8,128)(2,1)S(1)}, u32[]{:S(2)}, u32[]{:S(2)}) %collective-permute-start.20) | collective-permute-done | bytes 204832 | tf_op jit(solution)/shard_map/ppermute | solution.py:16
  77.7 1.7 %collective-permute-done.19.refs_13_ = bf16[80,1280]{1,0:T(8,128)(2,1)S(1)} collective-permute-done((bf16[80,1280]{1,0:T(8,128)(2,1)S(1)}, bf16[80,1280]{1,0:T(8,128)(2,1)S(1)}, u32[]{:S(2)}, u32[]{:S(2)}) %collective-permute-start.19) | collective-permute-done | bytes 204832 | tf_op jit(solution)/shard_map/ppermute | solution.py:16
  79.6 4.0 %ffn.1 = (f32[64,1280]{1,0:T(8,128)S(1)}, bf16[64,1280]{1,0:T(8,128)(2,1)S(1)}, bf16[64,1280]{1,0:T(8,128)(2,1)S(1)}, bf16[64,1280]{1,0:T(8,128)(2,1)S(1)}, f32[...) custom-call(bf16[256,1280]{1,0:T(8,128)(2,1)S(1)} %pad_maximum_fusio, ...), custom_call_target="tpu_custom_call" | custom-call | tf_op jit(solution)/shard_map/ffn/pallas_call | solution.py:61
  83.8 1.2 collective-permute-start.26
  84.9 2.4 %collective-permute-start.27 = (bf16[64,1280]{1,0:T(8,128)(2,1)S(1)}, bf16[64,1280]{1,0:T(8,128)(2,1)S(1)}, u32[]{:S(2)}, u32[]{:S(2)}) collective-permute-start(bf16[64,1280]{1,0:T(8,128)(2,1)S(1)} %get-tuple-element.94), channel_id=1, source_target_pairs={{0,192},{16,208},{32,224},{48,240},{64,128},{80,144},{96,160},{112... | collective-permute-start | bytes 491528 | tf_op jit(solution)/shard_map/ppermute | solution.py:16
  87.3 1.2 collective-permute-start.23
  88.5 0.7 collective-permute-done.25.refs_1_
  89.2 2.5 %collective-permute-start.24 = (bf16[64,1280]{1,0:T(8,128)(2,1)S(1)}, bf16[64,1280]{1,0:T(8,128)(2,1)S(1)}, u32[]{:S(2)}, u32[]{:S(2)}) collective-permute-start(bf16[64,1280]{1,0:T(8,128)(2,1)S(1)} %get-tuple-element.86), channel_id=1, source_target_pairs={{0,192},{16,208},{32,224},{48,240},{64,128},{80,144},{96,160},{112... | collective-permute-start | bytes 491528 | tf_op jit(solution)/shard_map/ppermute | solution.py:16
  91.7 0.9 collective-permute-done.26.refs_2_
  92.6 2.0 %combine_grad.1 = (f32[64,256]{1,0:T(8,128)S(1)}, f32[8,256]{1,0:T(8,128)S(1)}) custom-call(f32[64,1280]{1,0:T(8,128)S(1)} %get-tuple-element.91.refs_0_, bf16[64,1280]{1,0:T(8,128)(2,1)S(1)} %collective-permute-done.25.refs_1_, bf16[64,1280]{1,0:T(8,128)(2,1)S(1)} %collective-permute-done.26.refs_2_, bf16[64,1280]{1,0:T(8,128)(2,1)S(1)} %collective-permute-done.27.refs_3_, ...), custom_call_target="tpu_custom_call" | custom-call | tf_op jit(solution)/shard_map/combine_grad/pallas_call | solution.py:188
  94.6 17.2 %collective-permute-start.30 = (f32[8,256]{1,0:T(8,128)S(1)}, f32[8,256]{1,0:T(8,128)S(1)}, u32[]{:S(2)}, u32[]{:S(2)}) collective-permute-start(f32[8,256]{1,0:T(8,128)S(1)} %get-tuple-element.99), channel_id=1, source_target_pairs={{0,3},{1,2},{2,1},{3,0},{4,7},{5,6},{6,5},{7,4},{8,11},{9,10},{10,... | collective-permute-start | bytes 24584 | tf_op jit(solution)/shard_map/ppermute | solution.py:16
  111.9 1.2 collective-permute-start.29
  113.3 5.0 %collective-permute-done.29 = f32[8,256]{1,0:T(8,128)S(1)} collective-permute-done((f32[8,256]{1,0:T(8,128)S(1)}, f32[8,256]{1,0:T(8,128)S(1)}, u32[]{:S(2)}, u32[]{:S(2)}) %collective-permute-start.29) | collective-permute-done | bytes 8224 | tf_op jit(solution)/shard_map/ppermute | solution.py:16
  118.3 0.9 collective-permute-start.33
  119.2 1.2 collective-permute-start.32
  120.5 1.1 collective-permute-start.31
  121.7 2.3 %dispatch_grad.1 = f32[64,256]{1,0:T(8,128)S(1)} custom-call(f32[64,1280]{1,0:T(8,128)S(1)} %get-tuple-element.115.refs_0_, bf16[8,256,1280]{2,1,0:T(8,128)(2,1)S(1)} %copy-done, f32[64,256]{1,0:T(8,128)S(1)} %get-tuple-element.90.refs_2_), custom_call_target="tpu_custom_call" | custom-call | tf_op jit(solution)/shard_map/dispatch_grad/pallas_call | solution.py:188
  124.1 1.3 collective-permute-start.35
  125.4 0.8 convolution_bitcast_fusion
  126.2 7.6 %collective-permute-start.34 = (f32[8,1280]{1,0:T(8,128)S(1)}, f32[8,1280]{1,0:T(8,128)S(1)}, u32[]{:S(2)}, u32[]{:S(2)}) collective-permute-start(f32[8,1280]{1,0:T(8,128)S(1)} %convolution_bitcast_fusion), channel_id=1, source_target_pairs={{0,64},{16,80},{32,96},{48,112},{64,0},{80,16},{96,32},{112,48},{1... | collective-permute-start | bytes 122888 | tf_op jit(solution)/shard_map/ppermute | solution.py:16
  133.8 5.9 %collective-permute-done.34 = f32[8,1280]{1,0:T(8,128)S(1)} collective-permute-done((f32[8,1280]{1,0:T(8,128)S(1)}, f32[8,1280]{1,0:T(8,128)S(1)}, u32[]{:S(2)}, u32[]{:S(2)}) %collective-permute-start.34) | collective-permute-done | bytes 40992 | tf_op jit(solution)/shard_map/ppermute | solution.py:16
  139.8 1.1 collective-permute-start.38
  140.8 1.0 collective-permute-start.37
  141.9 1.2 collective-permute-start.36
  143.1 2.2 %collective-permute-start.39 = (f32[8,1280]{1,0:T(8,128)S(1)}, f32[8,1280]{1,0:T(8,128)S(1)}, u32[]{:S(2)}, u32[]{:S(2)}) collective-permute-start(f32[8,1280]{1,0:T(8,128)S(1)} %add.76), channel_id=1, source_target_pairs={{0,128},{16,144},{32,160},{48,176},{64,192},{80,208},{96,224},{112... | collective-permute-start | bytes 122888 | tf_op jit(solution)/shard_map/ppermute | solution.py:16
  145.3 1.9 %collective-permute-done.39 = f32[8,1280]{1,0:T(8,128)S(1)} collective-permute-done((f32[8,1280]{1,0:T(8,128)S(1)}, f32[8,1280]{1,0:T(8,128)S(1)}, u32[]{:S(2)}, u32[]{:S(2)}) %collective-permute-start.39) | collective-permute-done | bytes 40992 | tf_op jit(solution)/shard_map/ppermute | solution.py:16
  147.2 1.3 collective-permute-start.40
  148.5 1.8 %collective-permute-done.40 = f32[8,1280]{1,0:T(8,128)S(1)} collective-permute-done((f32[8,1280]{1,0:T(8,128)S(1)}, f32[8,1280]{1,0:T(8,128)S(1)}, u32[]{:S(2)}, u32[]{:S(2)}) %collective-permute-start.40) | collective-permute-done | bytes 40992 | tf_op jit(solution)/shard_map/ppermute | solution.py:16
  150.3 4.1 %collective-permute-start.41 = (f32[8,1280]{1,0:T(8,128)S(1)}, f32[8,1280]{1,0:T(8,128)S(1)}, u32[]{:S(2)}, u32[]{:S(2)}) collective-permute-start(f32[8,1280]{1,0:T(8,128)S(1)} %add.78), channel_id=1, source_target_pairs={{0,32},{16,48},{32,0},{48,16},{64,96},{80,112},{96,64},{112,80},{1... | collective-permute-start | bytes 122888 | tf_op jit(solution)/shard_map/ppermute | solution.py:16
  154.4 5.4 %collective-permute-done.38.three = bf16[2,64,1536]{2,1,0:T(8,128)(2,1)S(1)} collective-permute-done((bf16[2,64,1536]{2,1,0:T(8,128)(2,1)S(1)}, bf16[2,64,1536]{2,1,0:T(8,128)(2,1)S(1)}, u32[]{:S(2)}, u32[]{:S(2)}) %collective-permute-start.38) | collective-permute-done | bytes 393248 | tf_op jit(solution)/shard_map/ppermute | solution.py:16
  159.8 0.3 collective-permute-done.36.one
  160.2 1.3 token_grad.1
  161.5 1.6 collective-permute-start.42
  163.1 0.6 add_bitcast_fusion
  163.7 1.1 collective-permute-done.42
  164.8 0.8 add_convert_fusion
  (74 shorter events, 1.5 us)
Async XLA Ops:
  0.6 1.5 copy-start.2
  2.1 4.2 %copy-start.3 = (bf16[1280,8]{0,1:T(8,128)(2,1)S(1)}, bf16[1280,8]{0,1:T(8,128)(2,1)}, u32[]{:S(2)}) copy-start(bf16[1280,8]{0,1:T(8,128)(2,1)} %param.7) | copy-start | bytes 61444
  2.3 14.6 %collective-permute-start.4 = (bf16[2,80,1280]{2,1,0:T(8,128)(2,1)S(1)}, bf16[2,80,1280]{2,1,0:T(8,128)(2,1)S(1)}, u32[]{:S(2)}, u32[]{:S(2)}) collective-permute-start(bf16[2,80,1280]{2,1,0:T(8,128)(2,1)S(1)} %pad_maximum_fusion.3.refs_0_), channel_id=1, source_target_pairs={{0,16},{16,0},{32,48},{48,32},{64,80},{80,64},{96,112},{112,96},{1... | collective-permute-start | bytes 1228808 | tf_op jit(solution)/shard_map/ppermute | solution.py:16
  4.5 13.3 %collective-permute-start.2 = (bf16[2,80,1280]{2,1,0:T(8,128)(2,1)S(1)}, bf16[2,80,1280]{2,1,0:T(8,128)(2,1)S(1)}, u32[]{:S(2)}, u32[]{:S(2)}) collective-permute-start(bf16[2,80,1280]{2,1,0:T(8,128)(2,1)S(1)} %pad_maximum_fusion.3.refs_0_), channel_id=1, source_target_pairs={{0,48},{16,32},{32,16},{48,0},{64,112},{80,96},{96,80},{112,64},{1... | collective-permute-start | bytes 1228808 | tf_op jit(solution)/shard_map/ppermute | solution.py:16
  6.4 9.1 %collective-permute-start = (bf16[8,1280]{1,0:T(8,128)(2,1)S(1)}, bf16[8,1280]{1,0:T(8,128)(2,1)S(1)}, u32[]{:S(2)}, u32[]{:S(2)}) collective-permute-start(bf16[8,1280]{1,0:T(8,128)(2,1)S(1)} %bitcast.69), channel_id=1, source_target_pairs={{0,2},{1,3},{2,0},{3,1},{4,6},{5,7},{6,4},{7,5},{8,10},{9,11},{10,... | collective-permute-start | bytes 61448 | tf_op jit(solution)/shard_map/ppermute | solution.py:16
  13.3 20.9 %collective-permute-start.7 = (bf16[2,80,1280]{2,1,0:T(8,128)(2,1)S(1)}, bf16[2,80,1280]{2,1,0:T(8,128)(2,1)S(1)}, u32[]{:S(2)}, u32[]{:S(2)}) collective-permute-start(bf16[2,80,1280]{2,1,0:T(8,128)(2,1)S(1)} %pad_maximum_fusion.5), channel_id=1, source_target_pairs={{0,128},{16,144},{32,160},{48,176},{64,192},{80,208},{96,224},{112... | collective-permute-start | bytes 1228808 | tf_op jit(solution)/shard_map/ppermute | solution.py:16
  14.6 28.2 %copy-start = (bf16[8,256,1280]{2,1,0:T(8,128)(2,1)S(1)}, bf16[8,256,1280]{2,1,0:T(8,128)(2,1)}, u32[]{:S(2)}) copy-start(bf16[8,256,1280]{2,1,0:T(8,128)(2,1)} %refs_1_.1) | copy-start | bytes 15728644
  14.6 19.6 %collective-permute-start.6 = (bf16[2,80,1280]{2,1,0:T(8,128)(2,1)S(1)}, bf16[2,80,1280]{2,1,0:T(8,128)(2,1)S(1)}, u32[]{:S(2)}, u32[]{:S(2)}) collective-permute-start(bf16[2,80,1280]{2,1,0:T(8,128)(2,1)S(1)} %pad_maximum_fusion.4), channel_id=1, source_target_pairs={{0,64},{16,80},{32,96},{48,112},{64,0},{80,16},{96,32},{112,48},{1... | collective-permute-start | bytes 1228808 | tf_op jit(solution)/shard_map/ppermute | solution.py:16
  15.5 2.9 %collective-permute-start.1 = (bf16[16,1280]{1,0:T(8,128)(2,1)S(1)}, bf16[16,1280]{1,0:T(8,128)(2,1)S(1)}, u32[]{:S(2)}, u32[]{:S(2)}) collective-permute-start(bf16[16,1280]{1,0:T(8,128)(2,1)S(1)} %pad_maximum_fusion.12), channel_id=1, source_target_pairs={{0,4},{1,5},{2,6},{3,7},{4,0},{5,1},{6,2},{7,3},{8,12},{9,13},{10,... | collective-permute-start | bytes 122888 | tf_op jit(solution)/shard_map/ppermute | solution.py:16
  16.9 17.4 %collective-permute-start.5 = (bf16[80,1280]{1,0:T(8,128)(2,1)S(1)}, bf16[80,1280]{1,0:T(8,128)(2,1)S(1)}, u32[]{:S(2)}, u32[]{:S(2)}) collective-permute-start(bf16[80,1280]{1,0:T(8,128)(2,1)S(1)} %slice_bitcast_fusion.2), channel_id=1, source_target_pairs={{0,48},{16,32},{32,16},{48,0},{64,112},{80,96},{96,80},{112,64},{1... | collective-permute-start | bytes 614408 | tf_op jit(solution)/shard_map/ppermute | solution.py:16
  17.7 16.5 %collective-permute-start.3 = (bf16[80,1280]{1,0:T(8,128)(2,1)S(1)}, bf16[80,1280]{1,0:T(8,128)(2,1)S(1)}, u32[]{:S(2)}, u32[]{:S(2)}) collective-permute-start(bf16[80,1280]{1,0:T(8,128)(2,1)S(1)} %slice_bitcast_fusion.3), channel_id=1, source_target_pairs={{0,16},{16,0},{32,48},{48,32},{64,80},{80,64},{96,112},{112,96},{1... | collective-permute-start | bytes 614408 | tf_op jit(solution)/shard_map/ppermute | solution.py:16
  34.2 5.8 %collective-permute-start.11 = (bf16[32,1280]{1,0:T(8,128)(2,1)S(1)}, bf16[32,1280]{1,0:T(8,128)(2,1)S(1)}, u32[]{:S(2)}, u32[]{:S(2)}) collective-permute-start(bf16[32,1280]{1,0:T(8,128)(2,1)S(1)} %pad_maximum_fusion.11), channel_id=1, source_target_pairs={{0,8},{1,9},{2,10},{3,11},{4,12},{5,13},{6,14},{7,15},{8,0},{9,1},... | collective-permute-start | bytes 245768 | tf_op jit(solution)/shard_map/ppermute | solution.py:16
  37.2 19.7 %collective-permute-start.9 = (bf16[2,2,80,1280]{3,2,1,0:T(8,128)(2,1)S(1)}, bf16[2,2,80,1280]{3,2,1,0:T(8,128)(2,1)S(1)}, u32[]{:S(2)}, u32[]{:S(2)}) collective-permute-start(bf16[2,2,80,1280]{3,2,1,0:T(8,128)(2,1)S(1)} %pad_maximum_fusion.refs_5_), channel_id=1, source_target_pairs={{0,48},{16,32},{32,16},{48,0},{64,112},{80,96},{96,80},{112,64},{1... | collective-permute-start | bytes 2457608 | tf_op jit(solution)/shard_map/ppermute | solution.py:16
  38.0 18.8 %collective-permute-start.8 = (bf16[2,2,80,1280]{3,2,1,0:T(8,128)(2,1)S(1)}, bf16[2,2,80,1280]{3,2,1,0:T(8,128)(2,1)S(1)}, u32[]{:S(2)}, u32[]{:S(2)}) collective-permute-start(bf16[2,2,80,1280]{3,2,1,0:T(8,128)(2,1)S(1)} %pad_maximum_fusion.refs_5_), channel_id=1, source_target_pairs={{0,16},{16,0},{32,48},{48,32},{64,80},{80,64},{96,112},{112,96},{1... | collective-permute-start | bytes 2457608 | tf_op jit(solution)/shard_map/ppermute | solution.py:16
  38.0 12.6 %collective-permute-start.10 = (bf16[2,80,1280]{2,1,0:T(8,128)(2,1)S(1)}, bf16[2,80,1280]{2,1,0:T(8,128)(2,1)S(1)}, u32[]{:S(2)}, u32[]{:S(2)}) collective-permute-start(bf16[2,80,1280]{2,1,0:T(8,128)(2,1)S(1)} %pad_maximum_fusion.6), channel_id=1, source_target_pairs={{0,192},{16,208},{32,224},{48,240},{64,128},{80,144},{96,160},{112... | collective-permute-start | bytes 1228808 | tf_op jit(solution)/shard_map/ppermute | solution.py:16
  40.1 2.7 %collective-permute-start.12 = (bf16[64,1280]{1,0:T(8,128)(2,1)S(1)}, bf16[64,1280]{1,0:T(8,128)(2,1)S(1)}, u32[]{:S(2)}, u32[]{:S(2)}) collective-permute-start(bf16[64,1280]{1,0:T(8,128)(2,1)S(1)} %pad_maximum_fusion.10), channel_id=1, source_target_pairs={{0,1},{1,0},{2,3},{3,2},{4,5},{5,4},{6,7},{7,6},{8,9},{9,8},{10,11... | collective-permute-start | bytes 491528 | tf_op jit(solution)/shard_map/ppermute | solution.py:16
  42.8 6.6 %copy-start.1 = (bf16[8,256,1280]{2,1,0:T(8,128)(2,1)S(1)}, bf16[8,256,1280]{2,1,0:T(8,128)(2,1)}, u32[]{:S(2)}) copy-start(bf16[8,256,1280]{2,1,0:T(8,128)(2,1)} %refs_4_.1) | copy-start | bytes 15728644
  50.7 13.9 %collective-permute-start.16 = (bf16[128,1280]{1,0:T(8,128)(2,1)S(1)}, bf16[128,1280]{1,0:T(8,128)(2,1)S(1)}, u32[]{:S(2)}, u32[]{:S(2)}) collective-permute-start(bf16[128,1280]{1,0:T(8,128)(2,1)S(1)} %pad_maximum_fusion.8), channel_id=1, source_target_pairs={{0,128},{16,144},{32,160},{48,176},{64,192},{80,208},{96,224},{112... | collective-permute-start | bytes 983048 | tf_op jit(solution)/shard_map/ppermute | solution.py:16
  56.9 12.4 %collective-permute-start.14 = (bf16[2,80,1280]{2,1,0:T(8,128)(2,1)S(1)}, bf16[2,80,1280]{2,1,0:T(8,128)(2,1)S(1)}, u32[]{:S(2)}, u32[]{:S(2)}) collective-permute-start(bf16[2,80,1280]{2,1,0:T(8,128)(2,1)S(1)} %collective-permute-done.10.refs_10_), channel_id=1, source_target_pairs={{0,48},{16,32},{32,16},{48,0},{64,112},{80,96},{96,80},{112,64},{1... | collective-permute-start | bytes 1228808 | tf_op jit(solution)/shard_map/ppermute | solution.py:16
  58.1 11.1 %collective-permute-start.13 = (bf16[2,80,1280]{2,1,0:T(8,128)(2,1)S(1)}, bf16[2,80,1280]{2,1,0:T(8,128)(2,1)S(1)}, u32[]{:S(2)}, u32[]{:S(2)}) collective-permute-start(bf16[2,80,1280]{2,1,0:T(8,128)(2,1)S(1)} %collective-permute-done.10.refs_10_), channel_id=1, source_target_pairs={{0,16},{16,0},{32,48},{48,32},{64,80},{80,64},{96,112},{112,96},{1... | collective-permute-start | bytes 1228808 | tf_op jit(solution)/shard_map/ppermute | solution.py:16
  58.1 11.1 %collective-permute-start.15 = (bf16[128,1280]{1,0:T(8,128)(2,1)S(1)}, bf16[128,1280]{1,0:T(8,128)(2,1)S(1)}, u32[]{:S(2)}, u32[]{:S(2)}) collective-permute-start(bf16[128,1280]{1,0:T(8,128)(2,1)S(1)} %pad_maximum_fusion.8), channel_id=1, source_target_pairs={{0,64},{16,80},{32,96},{48,112},{64,0},{80,16},{96,32},{112,48},{1... | collective-permute-start | bytes 983048 | tf_op jit(solution)/shard_map/ppermute | solution.py:16
  58.1 15.2 %collective-permute-start.18 = (bf16[2,80,1280]{2,1,0:T(8,128)(2,1)S(1)}, bf16[2,80,1280]{2,1,0:T(8,128)(2,1)S(1)}, u32[]{:S(2)}, u32[]{:S(2)}) collective-permute-start(bf16[2,80,1280]{2,1,0:T(8,128)(2,1)S(1)} %slice_bitcast_fusion), channel_id=1, source_target_pairs={{0,48},{16,32},{32,16},{48,0},{64,112},{80,96},{96,80},{112,64},{1... | collective-permute-start | bytes 1228808 | tf_op jit(solution)/shard_map/ppermute | solution.py:16
  64.6 10.5 %collective-permute-start.17 = (bf16[2,80,1280]{2,1,0:T(8,128)(2,1)S(1)}, bf16[2,80,1280]{2,1,0:T(8,128)(2,1)S(1)}, u32[]{:S(2)}, u32[]{:S(2)}) collective-permute-start(bf16[2,80,1280]{2,1,0:T(8,128)(2,1)S(1)} %slice_bitcast_fusion.1), channel_id=1, source_target_pairs={{0,16},{16,0},{32,48},{48,32},{64,80},{80,64},{96,112},{112,96},{1... | collective-permute-start | bytes 1228808 | tf_op jit(solution)/shard_map/ppermute | solution.py:16
  69.3 8.5 %collective-permute-start.20 = (bf16[80,1280]{1,0:T(8,128)(2,1)S(1)}, bf16[80,1280]{1,0:T(8,128)(2,1)S(1)}, u32[]{:S(2)}, u32[]{:S(2)}) collective-permute-start(bf16[80,1280]{1,0:T(8,128)(2,1)S(1)} %slice_bitcast_fusion.4), channel_id=1, source_target_pairs={{0,48},{16,32},{32,16},{48,0},{64,112},{80,96},{96,80},{112,64},{1... | collective-permute-start | bytes 614408 | tf_op jit(solution)/shard_map/ppermute | solution.py:16
  71.4 8.1 %collective-permute-start.19 = (bf16[80,1280]{1,0:T(8,128)(2,1)S(1)}, bf16[80,1280]{1,0:T(8,128)(2,1)S(1)}, u32[]{:S(2)}, u32[]{:S(2)}) collective-permute-start(bf16[80,1280]{1,0:T(8,128)(2,1)S(1)} %slice_bitcast_fusion.5), channel_id=1, source_target_pairs={{0,16},{16,0},{32,48},{48,32},{64,80},{80,64},{96,112},{112,96},{1... | collective-permute-start | bytes 614408 | tf_op jit(solution)/shard_map/ppermute | solution.py:16
  73.3 6.2 %collective-permute-start.21 = (bf16[128,1280]{1,0:T(8,128)(2,1)S(1)}, bf16[128,1280]{1,0:T(8,128)(2,1)S(1)}, u32[]{:S(2)}, u32[]{:S(2)}) collective-permute-start(bf16[128,1280]{1,0:T(8,128)(2,1)S(1)} %collective-permute-done.16), channel_id=1, source_target_pairs={{0,64},{16,80},{32,96},{48,112},{64,0},{80,16},{96,32},{112,48},{1... | collective-permute-start | bytes 983048 | tf_op jit(solution)/shard_map/ppermute | solution.py:16
  83.7 5.5 %collective-permute-start.25 = (bf16[64,1280]{1,0:T(8,128)(2,1)S(1)}, bf16[64,1280]{1,0:T(8,128)(2,1)S(1)}, u32[]{:S(2)}, u32[]{:S(2)}) collective-permute-start(bf16[64,1280]{1,0:T(8,128)(2,1)S(1)} %get-tuple-element.92), channel_id=1, source_target_pairs={{0,64},{16,80},{32,96},{48,112},{64,0},{80,16},{96,32},{112,48},{1... | collective-permute-start | bytes 491528 | tf_op jit(solution)/shard_map/ppermute | solution.py:16
  83.8 8.8 %collective-permute-start.26 = (bf16[64,1280]{1,0:T(8,128)(2,1)S(1)}, bf16[64,1280]{1,0:T(8,128)(2,1)S(1)}, u32[]{:S(2)}, u32[]{:S(2)}) collective-permute-start(bf16[64,1280]{1,0:T(8,128)(2,1)S(1)} %get-tuple-element.93), channel_id=1, source_target_pairs={{0,128},{16,144},{32,160},{48,176},{64,192},{80,208},{96,224},{112... | collective-permute-start | bytes 491528 | tf_op jit(solution)/shard_map/ppermute | solution.py:16
  84.9 7.7 %collective-permute-start.27 = (bf16[64,1280]{1,0:T(8,128)(2,1)S(1)}, bf16[64,1280]{1,0:T(8,128)(2,1)S(1)}, u32[]{:S(2)}, u32[]{:S(2)}) collective-permute-start(bf16[64,1280]{1,0:T(8,128)(2,1)S(1)} %get-tuple-element.94), channel_id=1, source_target_pairs={{0,192},{16,208},{32,224},{48,240},{64,128},{80,144},{96,160},{112... | collective-permute-start | bytes 491528 | tf_op jit(solution)/shard_map/ppermute | solution.py:16
  87.3 25.7 %collective-permute-start.22 = (bf16[64,1280]{1,0:T(8,128)(2,1)S(1)}, bf16[64,1280]{1,0:T(8,128)(2,1)S(1)}, u32[]{:S(2)}, u32[]{:S(2)}) collective-permute-start(bf16[64,1280]{1,0:T(8,128)(2,1)S(1)} %get-tuple-element.84), channel_id=1, source_target_pairs={{0,64},{16,80},{32,96},{48,112},{64,0},{80,16},{96,32},{112,48},{1... | collective-permute-start | bytes 491528 | tf_op jit(solution)/shard_map/ppermute | solution.py:16
  87.3 25.7 %collective-permute-start.23 = (bf16[64,1280]{1,0:T(8,128)(2,1)S(1)}, bf16[64,1280]{1,0:T(8,128)(2,1)S(1)}, u32[]{:S(2)}, u32[]{:S(2)}) collective-permute-start(bf16[64,1280]{1,0:T(8,128)(2,1)S(1)} %get-tuple-element.85), channel_id=1, source_target_pairs={{0,128},{16,144},{32,160},{48,176},{64,192},{80,208},{96,224},{112... | collective-permute-start | bytes 491528 | tf_op jit(solution)/shard_map/ppermute | solution.py:16
  89.2 23.9 %collective-permute-start.24 = (bf16[64,1280]{1,0:T(8,128)(2,1)S(1)}, bf16[64,1280]{1,0:T(8,128)(2,1)S(1)}, u32[]{:S(2)}, u32[]{:S(2)}) collective-permute-start(bf16[64,1280]{1,0:T(8,128)(2,1)S(1)} %get-tuple-element.86), channel_id=1, source_target_pairs={{0,192},{16,208},{32,224},{48,240},{64,128},{80,144},{96,160},{112... | collective-permute-start | bytes 491528 | tf_op jit(solution)/shard_map/ppermute | solution.py:16
  94.6 18.7 %collective-permute-start.30 = (f32[8,256]{1,0:T(8,128)S(1)}, f32[8,256]{1,0:T(8,128)S(1)}, u32[]{:S(2)}, u32[]{:S(2)}) collective-permute-start(f32[8,256]{1,0:T(8,128)S(1)} %get-tuple-element.99), channel_id=1, source_target_pairs={{0,3},{1,2},{2,1},{3,0},{4,7},{5,6},{6,5},{7,4},{8,11},{9,10},{10,... | collective-permute-start | bytes 24584 | tf_op jit(solution)/shard_map/ppermute | solution.py:16
  111.9 6.4 %collective-permute-start.29 = (f32[8,256]{1,0:T(8,128)S(1)}, f32[8,256]{1,0:T(8,128)S(1)}, u32[]{:S(2)}, u32[]{:S(2)}) collective-permute-start(f32[8,256]{1,0:T(8,128)S(1)} %get-tuple-element.99), channel_id=1, source_target_pairs={{0,2},{1,3},{2,0},{3,1},{4,6},{5,7},{6,4},{7,5},{8,10},{9,11},{10,... | collective-permute-start | bytes 24584 | tf_op jit(solution)/shard_map/ppermute | solution.py:16
  113.1 5.2 %collective-permute-start.28 = (f32[8,256]{1,0:T(8,128)S(1)}, f32[8,256]{1,0:T(8,128)S(1)}, u32[]{:S(2)}, u32[]{:S(2)}) collective-permute-start(f32[8,256]{1,0:T(8,128)S(1)} %get-tuple-element.99), channel_id=1, source_target_pairs={{0,1},{1,0},{2,3},{3,2},{4,5},{5,4},{6,7},{7,6},{8,9},{9,8},{10,11... | collective-permute-start | bytes 24584 | tf_op jit(solution)/shard_map/ppermute | solution.py:16
  118.3 5.7 %collective-permute-start.33 = (f32[8,256]{1,0:T(8,128)S(1)}, f32[8,256]{1,0:T(8,128)S(1)}, u32[]{:S(2)}, u32[]{:S(2)}) collective-permute-start(f32[8,256]{1,0:T(8,128)S(1)} %add_add_fusion.2), channel_id=1, source_target_pairs={{0,12},{1,13},{2,14},{3,15},{4,8},{5,9},{6,10},{7,11},{8,4},{9,5},... | collective-permute-start | bytes 24584 | tf_op jit(solution)/shard_map/ppermute | solution.py:16
  119.2 4.8 %collective-permute-start.32 = (f32[8,256]{1,0:T(8,128)S(1)}, f32[8,256]{1,0:T(8,128)S(1)}, u32[]{:S(2)}, u32[]{:S(2)}) collective-permute-start(f32[8,256]{1,0:T(8,128)S(1)} %add_add_fusion.2), channel_id=1, source_target_pairs={{0,8},{1,9},{2,10},{3,11},{4,12},{5,13},{6,14},{7,15},{8,0},{9,1},... | collective-permute-start | bytes 24584 | tf_op jit(solution)/shard_map/ppermute | solution.py:16
  120.5 3.6 %collective-permute-start.31 = (f32[8,256]{1,0:T(8,128)S(1)}, f32[8,256]{1,0:T(8,128)S(1)}, u32[]{:S(2)}, u32[]{:S(2)}) collective-permute-start(f32[8,256]{1,0:T(8,128)S(1)} %add_add_fusion.2), channel_id=1, source_target_pairs={{0,4},{1,5},{2,6},{3,7},{4,0},{5,1},{6,2},{7,3},{8,12},{9,13},{10,... | collective-permute-start | bytes 24584 | tf_op jit(solution)/shard_map/ppermute | solution.py:16
  124.1 15.6 %collective-permute-start.35 = (bf16[64,1536]{1,0:T(8,128)(2,1)S(1)}, bf16[64,1536]{1,0:T(8,128)(2,1)S(1)}, u32[]{:S(2)}, u32[]{:S(2)}) collective-permute-start(bf16[64,1536]{1,0:T(8,128)(2,1)S(1)} %get-tuple-element.133), channel_id=1, source_target_pairs={{0,2},{1,3},{2,0},{3,1},{4,6},{5,7},{6,4},{7,5},{8,10},{9,11},{10,... | collective-permute-start | bytes 589832 | tf_op jit(solution)/shard_map/ppermute | solution.py:16
  126.2 13.5 %collective-permute-start.34 = (f32[8,1280]{1,0:T(8,128)S(1)}, f32[8,1280]{1,0:T(8,128)S(1)}, u32[]{:S(2)}, u32[]{:S(2)}) collective-permute-start(f32[8,1280]{1,0:T(8,128)S(1)} %convolution_bitcast_fusion), channel_id=1, source_target_pairs={{0,64},{16,80},{32,96},{48,112},{64,0},{80,16},{96,32},{112,48},{1... | collective-permute-start | bytes 122888 | tf_op jit(solution)/shard_map/ppermute | solution.py:16
  139.8 20.0 %collective-permute-start.38 = (bf16[2,64,1536]{2,1,0:T(8,128)(2,1)S(1)}, bf16[2,64,1536]{2,1,0:T(8,128)(2,1)S(1)}, u32[]{:S(2)}, u32[]{:S(2)}) collective-permute-start(bf16[2,64,1536]{2,1,0:T(8,128)(2,1)S(1)} %pad_maximum_fusion.7.pair), channel_id=1, source_target_pairs={{0,12},{1,13},{2,14},{3,15},{4,8},{5,9},{6,10},{7,11},{8,4},{9,5},... | collective-permute-start | bytes 1179656 | tf_op jit(solution)/shard_map/ppermute | solution.py:16
  140.8 19.0 %collective-permute-start.37 = (bf16[2,64,1536]{2,1,0:T(8,128)(2,1)S(1)}, bf16[2,64,1536]{2,1,0:T(8,128)(2,1)S(1)}, u32[]{:S(2)}, u32[]{:S(2)}) collective-permute-start(bf16[2,64,1536]{2,1,0:T(8,128)(2,1)S(1)} %pad_maximum_fusion.7.pair), channel_id=1, source_target_pairs={{0,8},{1,9},{2,10},{3,11},{4,12},{5,13},{6,14},{7,15},{8,0},{9,1},... | collective-permute-start | bytes 1179656 | tf_op jit(solution)/shard_map/ppermute | solution.py:16
  141.9 18.3 %collective-permute-start.36 = (bf16[2,64,1536]{2,1,0:T(8,128)(2,1)S(1)}, bf16[2,64,1536]{2,1,0:T(8,128)(2,1)S(1)}, u32[]{:S(2)}, u32[]{:S(2)}) collective-permute-start(bf16[2,64,1536]{2,1,0:T(8,128)(2,1)S(1)} %pad_maximum_fusion.7.pair), channel_id=1, source_target_pairs={{0,4},{1,5},{2,6},{3,7},{4,0},{5,1},{6,2},{7,3},{8,12},{9,13},{10,... | collective-permute-start | bytes 1179656 | tf_op jit(solution)/shard_map/ppermute | solution.py:16
  143.1 4.0 %collective-permute-start.39 = (f32[8,1280]{1,0:T(8,128)S(1)}, f32[8,1280]{1,0:T(8,128)S(1)}, u32[]{:S(2)}, u32[]{:S(2)}) collective-permute-start(f32[8,1280]{1,0:T(8,128)S(1)} %add.76), channel_id=1, source_target_pairs={{0,128},{16,144},{32,160},{48,176},{64,192},{80,208},{96,224},{112... | collective-permute-start | bytes 122888 | tf_op jit(solution)/shard_map/ppermute | solution.py:16
  147.2 3.1 %collective-permute-start.40 = (f32[8,1280]{1,0:T(8,128)S(1)}, f32[8,1280]{1,0:T(8,128)S(1)}, u32[]{:S(2)}, u32[]{:S(2)}) collective-permute-start(f32[8,1280]{1,0:T(8,128)S(1)} %add.77), channel_id=1, source_target_pairs={{0,16},{16,0},{32,48},{48,32},{64,80},{80,64},{96,112},{112,96},{1... | collective-permute-start | bytes 122888 | tf_op jit(solution)/shard_map/ppermute | solution.py:16
  150.3 9.8 %collective-permute-start.41 = (f32[8,1280]{1,0:T(8,128)S(1)}, f32[8,1280]{1,0:T(8,128)S(1)}, u32[]{:S(2)}, u32[]{:S(2)}) collective-permute-start(f32[8,1280]{1,0:T(8,128)S(1)} %add.78), channel_id=1, source_target_pairs={{0,32},{16,48},{32,0},{48,16},{64,96},{80,112},{96,64},{112,80},{1... | collective-permute-start | bytes 122888 | tf_op jit(solution)/shard_map/ppermute | solution.py:16
  161.5 3.3 %collective-permute-start.42 = (f32[128,1280]{1,0:T(8,128)S(1)}, f32[128,1280]{1,0:T(8,128)S(1)}, u32[]{:S(2)}, u32[]{:S(2)}) collective-permute-start(f32[128,1280]{1,0:T(8,128)S(1)} %get-tuple-element.113), channel_id=1, source_target_pairs={{0,1},{1,0},{2,3},{3,2},{4,5},{5,4},{6,7},{7,6},{8,9},{9,8},{10,11... | collective-permute-start | bytes 1966088 | tf_op jit(solution)/shard_map/ppermute | solution.py:16

commit v12 on v11

--- a/solution.py
+++ b/solution.py
@@ -200,6 +200,36 @@
     )(*parts, big, weight)
 
 
+def pack_kernel(back, part, combine, mix, grad, near, send, lines):
+    images, count = mix.shape
+    width = grad.shape[1]
+    own = back.shape[0] // images
+    spread = jnp.concatenate([jnp.broadcast_to(mix[i : i + 1], (own, count)) for i in range(images)], axis=0)
+    value = (back[...] + (part[...] - combine[...] * spread)).astype(BF16)
+    lines[...] = value
+    place = (lax.axis_index("expert") // 2) % 2
+    col = lax.broadcasted_iota(jnp.int32, (count, count // 2), 1)
+    row = lax.broadcasted_iota(jnp.int32, (count, count // 2), 0)
+    for out, wanted in ((near, place), (send, 1 - place)):
+        pick = (row == (col // 32) * 64 + wanted * 32 + col % 32).astype(BF16)
+        out[:, :width] = grad[...].astype(BF16)
+        out[:, width:] = jnp.dot(value, pick, preferred_element_type=F32).astype(BF16)
+
+
+def pack_call(back, part, combine, mix, grad):
+    vmem = pl.BlockSpec(memory_space=pltpu.VMEM)
+    rows, count = back.shape
+    message = jax.ShapeDtypeStruct((rows, grad.shape[1] + count // 2), BF16)
+    return pl.pallas_call(
+        pack_kernel,
+        out_shape=[message, message, jax.ShapeDtypeStruct((rows, count), BF16)],
+        in_specs=[vmem] * 5,
+        out_specs=[vmem] * 3,
+        compiler_params=pltpu.CompilerParams(vmem_limit_bytes=16 * 2**20),
+        name="logit_grad",
+    )(back, part, combine, mix, grad)
+
+
 def tokens_kernel(spread, pair, one, two, three, table, mine, theirs):
     half, width = mine.shape
     pieces = [ref[...].reshape(2 * ref.shape[1], ref.shape[2]) for ref in (pair, one, two, three)]
@@ -211,7 +241,10 @@
     c = lax.broadcasted_iota(jnp.int32, (total, near), 0)
     q = lax.broadcasted_iota(jnp.int32, (total, near), 1)
     fold = ((c // 64 == q // 8) & (c % 8 == q % 8)).astype(BF16)
-    x = nt(pick_rows(count), grads)
+    col = lax.broadcasted_iota(jnp.int32, (32, count), 1)
+    row = lax.broadcasted_iota(jnp.int32, (32, count), 0)
+    owner = lax.axis_index("expert") ^ (row // 16)
+    x = nt((col == (owner // 4) * 32 + (owner % 2) * 16 + row % 16).astype(BF16), grads)
     parts = []
     for side in range(2):
         y = jnp.concatenate([x[16 * side : 16 * side + 16]] * 8, axis=0)
@@ -312,17 +345,15 @@
     )
     rows = jnp.concatenate([slot_in, slot_go.astype(BF16).reshape(half, width)], axis=0)
 
-    u3, rows = together(u3, rows)
-    z2 = swap(rows, "dp", 8)
-    lb, rb, u3 = together(lb, rb, u3)
-    z1 = swap(after(rows, lb), "dp", 4)
+    lb, rb, u3, rows = together(lb, rb, u3, rows)
+    z1, z2 = swap(rows, "dp", 4), swap(rows, "dp", 8)
     l3, r3 = swap(u3, "dp", 1), swap(u3, "dp", 3)
     pb, qb = swap(rb[0], "dp", 1), swap(lb[1], "dp", 3)
-    spread = spread_call(near)
-    l3, r3, z1, z2, spread = together(l3, r3, z1, z2, spread)
+    l3, r3, z2 = together(l3, r3, z2)
     p3, q3 = swap(r3[0], "dp", 1), swap(l3[1], "dp", 3)
     z3 = swap(z2, "dp", 4)
-    pb, qb, p3, q3, z3 = together(pb, qb, p3, q3, z3)
+    spread = spread_call(near)
+    pb, qb, p3, q3, z3, spread = together(pb, qb, p3, q3, z3, spread)
     rows_in = jnp.concatenate([v[:half] for v in (rows, z1, z2, z3)], axis=0)
     rows_go = jnp.concatenate([v[half:] for v in (rows, z1, z2, z3)], axis=0)
 
@@ -335,11 +366,8 @@
     mix = summed_three(mix, "expert", 1, 2, 3)
     mix = summed_three(mix, "expert", 4, 8, 12)
     (back,) = against([slot_in_grad], tokens, dispatch, True)
-    logit_grad = back + (part - combine * jnp.repeat(mix, own, axis=0))
-    logit_grad_b = logit_grad.astype(BF16)
-
-    near = jnp.concatenate([slot_in_grad.astype(BF16), logit_grad_b], axis=1)
-    far = swap(near, "expert", 2)
+    near, send, logit_grad_b = pack_call(back, part, combine, mix, slot_in_grad)
+    far = swap(send, "expert", 2)
     term = jnp.einsum(
         "bsm,bmd->sd", logit_grad_b.reshape(images, own, count), tokens, preferred_element_type=F32
     )

time: 166 us -> 166 us (level)
  starting transfers between devices: 85.3 us -> 76 us
  waiting for transfers between devices: 57.3 us -> 65.8 us
    ppermute x43, starting transfers between devices: 85.3 us -> 76 us  [swap(): return lax.ppermute(value, axis, [(i, i ^ k) for i in range(count)])]
    ppermute x43, waiting for transfers between devices: 57.3 us -> 65.8 us  [swap(): return lax.ppermute(value, axis, [(i, i ^ k) for i in range(count)])]
  transfers between devices with their start and end apart: 43 -> 43, of which waited for: 20 -> 19; matrix products, arithmetic and copies ran while one was open for 2% -> 2% of each run, Pallas kernels for 7% -> 7%
where the time goes in v12:
time: 166 us; the launch traced here: 165 us
  starting transfers between devices  76 us (46%)
  waiting for transfers between devices  65.8 us (40%)
  Pallas kernels  16.8 us (10%)
  other arithmetic  1.93 us (1%)
  local copies, waits for them, and re-layouts  1.76 us (1%)
    ppermute x43, starting transfers between devices, swap(): return lax.ppermute(value, axis, [(i, i ^ k) for i in range(count)])  76 us
    ppermute x43, waiting for transfers between devices, swap(): return lax.ppermute(value, axis, [(i, i ^ k) for i in range(count)])  65.8 us
    pallas_call x1, Pallas kernels, slots_call(): pl.pallas_call(slots_kernel, grid=(images // 2,), out_shape=[jax.ShapeDty...  6.63 us
    pallas_call x2, Pallas kernels, against(): pl.pallas_call(lambda *refs: against_kernel(over_tokens, len(parts), *ref...  4.32 us
    pallas_call x1, Pallas kernels, ffn(): pl.pallas_call(ffn_kernel, out_shape=[jax.ShapeDtypeStruct((own_rows, wid...  4.04 us
  transfers between devices with their start and end apart: 43, of which 19 were waited for; matrix products, arithmetic and copies ran while one was open for 2% of the time, Pallas kernels for 7%

profile of v12, /device:TPU:1, one launch (start us, length us, event | category | flops | bytes accessed | tf_op | source)
XLA Modules:
  0.0 164.9 jit_solution(13873119007504339348)
XLA Ops:
  0.7 1.4 dynamic-slice_bitcast_fusion.1
  2.3 2.2 %collective-permute-start.4 = (bf16[2,80,1280]{2,1,0:T(8,128)(2,1)S(1)}, bf16[2,80,1280]{2,1,0:T(8,128)(2,1)S(1)}, u32[]{:S(2)}, u32[]{:S(2)}) collective-permute-start(bf16[2,80,1280]{2,1,0:T(8,128)(2,1)S(1)} %pad_maximum_fusion.3.refs_0_), channel_id=1, source_target_pairs={{0,16},{16,0},{32,48},{48,32},{64,80},{80,64},{96,112},{112,96},{1... | collective-permute-start | bytes 1228808 | tf_op jit(solution)/shard_map/ppermute | solution.py:16
  4.5 1.9 %collective-permute-start.2 = (bf16[2,80,1280]{2,1,0:T(8,128)(2,1)S(1)}, bf16[2,80,1280]{2,1,0:T(8,128)(2,1)S(1)}, u32[]{:S(2)}, u32[]{:S(2)}) collective-permute-start(bf16[2,80,1280]{2,1,0:T(8,128)(2,1)S(1)} %pad_maximum_fusion.3.refs_0_), channel_id=1, source_target_pairs={{0,48},{16,32},{32,16},{48,0},{64,112},{80,96},{96,80},{112,64},{1... | collective-permute-start | bytes 1228808 | tf_op jit(solution)/shard_map/ppermute | solution.py:16
  6.4 6.9 %collective-permute-start = (bf16[8,1280]{1,0:T(8,128)(2,1)S(1)}, bf16[8,1280]{1,0:T(8,128)(2,1)S(1)}, u32[]{:S(2)}, u32[]{:S(2)}) collective-permute-start(bf16[8,1280]{1,0:T(8,128)(2,1)S(1)} %bitcast.61), channel_id=1, source_target_pairs={{0,2},{1,3},{2,0},{3,1},{4,6},{5,7},{6,4},{7,5},{8,10},{9,11},{10,... | collective-permute-start | bytes 61448 | tf_op jit(solution)/shard_map/ppermute | solution.py:16
  13.3 1.3 collective-permute-start.7
  14.6 0.8 collective-permute-start.6
  15.5 1.3 collective-permute-start.1
  16.9 0.9 collective-permute-start.5
  17.8 0.6 collective-permute-done.1
  18.5 15.7 %collective-permute-done.7 = bf16[2,80,1280]{2,1,0:T(8,128)(2,1)S(1)} collective-permute-done((bf16[2,80,1280]{2,1,0:T(8,128)(2,1)S(1)}, bf16[2,80,1280]{2,1,0:T(8,128)(2,1)S(1)}, u32[]{:S(2)}, u32[]{:S(2)}) %collective-permute-start.7) | collective-permute-done | bytes 409632 | tf_op jit(solution)/shard_map/ppermute | solution.py:16
  34.2 2.8 %collective-permute-start.11 = (bf16[32,1280]{1,0:T(8,128)(2,1)S(1)}, bf16[32,1280]{1,0:T(8,128)(2,1)S(1)}, u32[]{:S(2)}, u32[]{:S(2)}) collective-permute-start(bf16[32,1280]{1,0:T(8,128)(2,1)S(1)} %pad_maximum_fusion.10), channel_id=1, source_target_pairs={{0,8},{1,9},{2,10},{3,11},{4,12},{5,13},{6,14},{7,15},{8,0},{9,1},... | collective-permute-start | bytes 245768 | tf_op jit(solution)/shard_map/ppermute | solution.py:16
  37.2 0.9 collective-permute-start.9
  38.0 2.0 %collective-permute-start.10 = (bf16[2,80,1280]{2,1,0:T(8,128)(2,1)S(1)}, bf16[2,80,1280]{2,1,0:T(8,128)(2,1)S(1)}, u32[]{:S(2)}, u32[]{:S(2)}) collective-permute-start(bf16[2,80,1280]{2,1,0:T(8,128)(2,1)S(1)} %pad_maximum_fusion.6), channel_id=1, source_target_pairs={{0,192},{16,208},{32,224},{48,240},{64,128},{80,144},{96,160},{112... | collective-permute-start | bytes 1228808 | tf_op jit(solution)/shard_map/ppermute | solution.py:16
  40.1 1.7 %collective-permute-start.12 = (bf16[64,1280]{1,0:T(8,128)(2,1)S(1)}, bf16[64,1280]{1,0:T(8,128)(2,1)S(1)}, u32[]{:S(2)}, u32[]{:S(2)}) collective-permute-start(bf16[64,1280]{1,0:T(8,128)(2,1)S(1)} %pad_maximum_fusion.9), channel_id=1, source_target_pairs={{0,1},{1,0},{2,3},{3,2},{4,5},{5,4},{6,7},{7,6},{8,9},{9,8},{10,11... | collective-permute-start | bytes 491528 | tf_op jit(solution)/shard_map/ppermute | solution.py:16
  41.7 1.0 collective-permute-done.12
  42.8 6.6 %slots.1 = (bf16[64,1280]{1,0:T(8,128)(2,1)S(1)}, f32[64,256]{1,0:T(8,128)S(1)}, f32[64,256]{1,0:T(8,128)S(1)}, bf16[8,64,256]{2,1,0:T(8,128)(2,1)S(1)}) custom-call(bf16[128,1280]{1,0:T(8,128)(2,1)S(1)} %constant_dynamic-update-slice_fusion.table, bf16[8,256,1280]{2,1,0:T(8,128)(2,1)S(1)} %copy-done), custom_call_target="tpu_custom_call" | custom-call | flops 754974720 | bytes 5242880 | tf_op jit(solution)/shard_map/slots/pallas_call | solution.py:102
  49.4 0.8 fusion
  50.2 0.4 spread.1
  50.7 6.1 %collective-permute-done.9.refs_7_ = bf16[2,2,80,1280]{3,2,1,0:T(8,128)(2,1)S(1)} collective-permute-done((bf16[2,2,80,1280]{3,2,1,0:T(8,128)(2,1)S(1)}, bf16[2,2,80,1280]{3,2,1,0:T(8,128)(2,1)S(1)}, u32[]{:S(2)}, u32[]{:S(2)}) %collective-permute-start.9) | collective-permute-done | bytes 819232 | tf_op jit(solution)/shard_map/ppermute | solution.py:16
  56.8 2.7 %collective-permute-start.17 = (bf16[128,1280]{1,0:T(8,128)(2,1)S(1)}, bf16[128,1280]{1,0:T(8,128)(2,1)S(1)}, u32[]{:S(2)}, u32[]{:S(2)}) collective-permute-start(bf16[128,1280]{1,0:T(8,128)(2,1)S(1)} %pad_maximum_fusion.8), channel_id=1, source_target_pairs={{0,128},{16,144},{32,160},{48,176},{64,192},{80,208},{96,224},{112... | collective-permute-start | bytes 983048 | tf_op jit(solution)/shard_map/ppermute | solution.py:16
  59.5 1.2 collective-permute-start.16
  60.7 1.8 %collective-permute-start.14 = (bf16[2,80,1280]{2,1,0:T(8,128)(2,1)S(1)}, bf16[2,80,1280]{2,1,0:T(8,128)(2,1)S(1)}, u32[]{:S(2)}, u32[]{:S(2)}) collective-permute-start(bf16[2,80,1280]{2,1,0:T(8,128)(2,1)S(1)} %slice_bitcast_fusion), channel_id=1, source_target_pairs={{0,48},{16,32},{32,16},{48,0},{64,112},{80,96},{96,80},{112,64},{1... | collective-permute-start | bytes 1228808 | tf_op jit(solution)/shard_map/ppermute | solution.py:16
  62.5 9.4 %collective-permute-done.21 = bf16[128,1280]{1,0:T(8,128)(2,1)S(1)} collective-permute-done((bf16[128,1280]{1,0:T(8,128)(2,1)S(1)}, bf16[128,1280]{1,0:T(8,128)(2,1)S(1)}, u32[]{:S(2)}, u32[]{:S(2)}) %collective-permute-start.21) | collective-permute-done | bytes 327712 | tf_op jit(solution)/shard_map/ppermute | solution.py:16
  72.1 1.5 collective-permute-start.19
  73.6 0.6 collective-permute-start.18
  74.2 3.7 %collective-permute-done.14.refs_9_ = bf16[2,80,1280]{2,1,0:T(8,128)(2,1)S(1)} collective-permute-done((bf16[2,80,1280]{2,1,0:T(8,128)(2,1)S(1)}, bf16[2,80,1280]{2,1,0:T(8,128)(2,1)S(1)}, u32[]{:S(2)}, u32[]{:S(2)}) %collective-permute-start.14) | collective-permute-done | bytes 409632 | tf_op jit(solution)/shard_map/ppermute | solution.py:16
  77.9 3.2 %collective-permute-done.13.refs_8_ = bf16[2,80,1280]{2,1,0:T(8,128)(2,1)S(1)} collective-permute-done((bf16[2,80,1280]{2,1,0:T(8,128)(2,1)S(1)}, bf16[2,80,1280]{2,1,0:T(8,128)(2,1)S(1)}, u32[]{:S(2)}, u32[]{:S(2)}) %collective-permute-start.13) | collective-permute-done | bytes 409632 | tf_op jit(solution)/shard_map/ppermute | solution.py:16
  81.2 1.2 collective-permute-done.19.refs_14_
  82.3 3.2 %collective-permute-done.18.refs_13_ = bf16[80,1280]{1,0:T(8,128)(2,1)S(1)} collective-permute-done((bf16[80,1280]{1,0:T(8,128)(2,1)S(1)}, bf16[80,1280]{1,0:T(8,128)(2,1)S(1)}, u32[]{:S(2)}, u32[]{:S(2)}) %collective-permute-start.18) | collective-permute-done | bytes 204832 | tf_op jit(solution)/shard_map/ppermute | solution.py:16
  85.7 4.0 %ffn.1 = (f32[64,1280]{1,0:T(8,128)S(1)}, bf16[64,1280]{1,0:T(8,128)(2,1)S(1)}, bf16[64,1280]{1,0:T(8,128)(2,1)S(1)}, bf16[64,1280]{1,0:T(8,128)(2,1)S(1)}, f32[...) custom-call(bf16[256,1280]{1,0:T(8,128)(2,1)S(1)} %get-tuple-element, ...), custom_call_target="tpu_custom_call" | custom-call | tf_op jit(solution)/shard_map/ffn/pallas_call | solution.py:61
  89.8 2.1 %collective-permute-start.26 = (bf16[64,1280]{1,0:T(8,128)(2,1)S(1)}, bf16[64,1280]{1,0:T(8,128)(2,1)S(1)}, u32[]{:S(2)}, u32[]{:S(2)}) collective-permute-start(bf16[64,1280]{1,0:T(8,128)(2,1)S(1)} %get-tuple-element.90), channel_id=1, source_target_pairs={{0,128},{16,144},{32,160},{48,176},{64,192},{80,208},{96,224},{112... | collective-permute-start | bytes 491528 | tf_op jit(solution)/shard_map/ppermute | solution.py:16
  91.9 1.5 collective-permute-start.27
  93.4 2.1 %collective-permute-start.23 = (bf16[64,1280]{1,0:T(8,128)(2,1)S(1)}, bf16[64,1280]{1,0:T(8,128)(2,1)S(1)}, u32[]{:S(2)}, u32[]{:S(2)}) collective-permute-start(bf16[64,1280]{1,0:T(8,128)(2,1)S(1)} %get-tuple-element.82), channel_id=1, source_target_pairs={{0,128},{16,144},{32,160},{48,176},{64,192},{80,208},{96,224},{112... | collective-permute-start | bytes 491528 | tf_op jit(solution)/shard_map/ppermute | solution.py:16
  95.4 1.5 collective-permute-start.24
  97.0 3.5 %collective-permute-done.27.refs_3_ = bf16[64,1280]{1,0:T(8,128)(2,1)S(1)} collective-permute-done((bf16[64,1280]{1,0:T(8,128)(2,1)S(1)}, bf16[64,1280]{1,0:T(8,128)(2,1)S(1)}, u32[]{:S(2)}, u32[]{:S(2)}) %collective-permute-start.27) | collective-permute-done | bytes 163872 | tf_op jit(solution)/shard_map/ppermute | solution.py:16
  100.5 2.0 %combine_grad.1 = (f32[64,256]{1,0:T(8,128)S(1)}, f32[8,256]{1,0:T(8,128)S(1)}) custom-call(f32[64,1280]{1,0:T(8,128)S(1)} %get-tuple-element.88.refs_0_, bf16[64,1280]{1,0:T(8,128)(2,1)S(1)} %collective-permute-done.25.refs_1_, bf16[64,1280]{1,0:T(8,128)(2,1)S(1)} %collective-permute-done.26.refs_2_, bf16[64,1280]{1,0:T(8,128)(2,1)S(1)} %collective-permute-done.27.refs_3_, ...), custom_call_target="tpu_custom_call" | custom-call | tf_op jit(solution)/shard_map/combine_grad/pallas_call | solution.py:188
  102.5 7.9 %collective-permute-start.30 = (f32[8,256]{1,0:T(8,128)S(1)}, f32[8,256]{1,0:T(8,128)S(1)}, u32[]{:S(2)}, u32[]{:S(2)}) collective-permute-start(f32[8,256]{1,0:T(8,128)S(1)} %get-tuple-element.96), channel_id=1, source_target_pairs={{0,3},{1,2},{2,1},{3,0},{4,7},{5,6},{6,5},{7,4},{8,11},{9,10},{10,... | collective-permute-start | bytes 24584 | tf_op jit(solution)/shard_map/ppermute | solution.py:16
  110.4 4.8 %collective-permute-start.29 = (f32[8,256]{1,0:T(8,128)S(1)}, f32[8,256]{1,0:T(8,128)S(1)}, u32[]{:S(2)}, u32[]{:S(2)}) collective-permute-start(f32[8,256]{1,0:T(8,128)S(1)} %get-tuple-element.96), channel_id=1, source_target_pairs={{0,2},{1,3},{2,0},{3,1},{4,6},{5,7},{6,4},{7,5},{8,10},{9,11},{10,... | collective-permute-start | bytes 24584 | tf_op jit(solution)/shard_map/ppermute | solution.py:16
  115.1 1.6 collective-permute-done.23
  116.7 0.4 collective-permute-done.29
  117.1 0.9 collective-permute-start.33
  118.1 1.3 collective-permute-start.32
  119.3 1.1 collective-permute-start.31
  120.5 2.3 %dispatch_grad.1.back = f32[64,256]{1,0:T(8,128)S(1)} custom-call(f32[64,1280]{1,0:T(8,128)S(1)} %add_add_fusion.refs_0_.grad, bf16[8,256,1280]{2,1,0:T(8,128)(2,1)S(1)} %copy-done, f32[64,256]{1,0:T(8,128)S(1)} %get-tuple-element.87.refs_2_), custom_call_target="tpu_custom_call" | custom-call | tf_op jit(solution)/shard_map/dispatch_grad/pallas_call | solution.py:188
  122.9 0.2 logit_grad.1
  123.0 4.6 %collective-permute-start.35 = (bf16[64,1408]{1,0:T(8,128)(2,1)S(1)}, bf16[64,1408]{1,0:T(8,128)(2,1)S(1)}, u32[]{:S(2)}, u32[]{:S(2)}) collective-permute-start(bf16[64,1408]{1,0:T(8,128)(2,1)S(1)} %get-tuple-element.105), channel_id=1, source_target_pairs={{0,2},{1,3},{2,0},{3,1},{4,6},{5,7},{6,4},{7,5},{8,10},{9,11},{10,... | collective-permute-start | bytes 540680 | tf_op jit(solution)/shard_map/ppermute | solution.py:16
  127.7 0.8 convolution_bitcast_fusion
  128.4 9.5 %collective-permute-start.34 = (f32[8,1280]{1,0:T(8,128)S(1)}, f32[8,1280]{1,0:T(8,128)S(1)}, u32[]{:S(2)}, u32[]{:S(2)}) collective-permute-start(f32[8,1280]{1,0:T(8,128)S(1)} %convolution_bitcast_fusion), channel_id=1, source_target_pairs={{0,64},{16,80},{32,96},{48,112},{64,0},{80,16},{96,32},{112,48},{1... | collective-permute-start | bytes 122888 | tf_op jit(solution)/shard_map/ppermute | solution.py:16
  137.9 3.4 %collective-permute-done.34 = f32[8,1280]{1,0:T(8,128)S(1)} collective-permute-done((f32[8,1280]{1,0:T(8,128)S(1)}, f32[8,1280]{1,0:T(8,128)S(1)}, u32[]{:S(2)}, u32[]{:S(2)}) %collective-permute-start.34) | collective-permute-done | bytes 40992 | tf_op jit(solution)/shard_map/ppermute | solution.py:16
  141.4 1.3 collective-permute-start.38
  142.7 1.1 collective-permute-start.37
  143.8 1.0 collective-permute-start.36
  144.7 2.7 %collective-permute-start.39 = (f32[8,1280]{1,0:T(8,128)S(1)}, f32[8,1280]{1,0:T(8,128)S(1)}, u32[]{:S(2)}, u32[]{:S(2)}) collective-permute-start(f32[8,1280]{1,0:T(8,128)S(1)} %add.72), channel_id=1, source_target_pairs={{0,128},{16,144},{32,160},{48,176},{64,192},{80,208},{96,224},{112... | collective-permute-start | bytes 122888 | tf_op jit(solution)/shard_map/ppermute | solution.py:16
  147.4 1.7 %collective-permute-done.39 = f32[8,1280]{1,0:T(8,128)S(1)} collective-permute-done((f32[8,1280]{1,0:T(8,128)S(1)}, f32[8,1280]{1,0:T(8,128)S(1)}, u32[]{:S(2)}, u32[]{:S(2)}) %collective-permute-start.39) | collective-permute-done | bytes 40992 | tf_op jit(solution)/shard_map/ppermute | solution.py:16
  149.1 0.3 collective-permute-start.40
  149.4 2.8 %collective-permute-done.40 = f32[8,1280]{1,0:T(8,128)S(1)} collective-permute-done((f32[8,1280]{1,0:T(8,128)S(1)}, f32[8,1280]{1,0:T(8,128)S(1)}, u32[]{:S(2)}, u32[]{:S(2)}) %collective-permute-start.40) | collective-permute-done | bytes 40992 | tf_op jit(solution)/shard_map/ppermute | solution.py:16
  152.3 0.9 collective-permute-start.41
  153.2 5.7 %collective-permute-done.38.three = bf16[2,64,1408]{2,1,0:T(8,128)(2,1)S(1)} collective-permute-done((bf16[2,64,1408]{2,1,0:T(8,128)(2,1)S(1)}, bf16[2,64,1408]{2,1,0:T(8,128)(2,1)S(1)}, u32[]{:S(2)}, u32[]{:S(2)}) %collective-permute-start.38) | collective-permute-done | bytes 360480 | tf_op jit(solution)/shard_map/ppermute | solution.py:16
  158.9 1.2 collective-permute-done.36.one
  160.1 1.2 token_grad.1
  161.3 1.0 collective-permute-start.42
  162.4 0.6 add_bitcast_fusion
  163.0 1.1 collective-permute-done.42
  164.1 0.8 add_convert_fusion
  (73 shorter events, 1.3 us)
Async XLA Ops:
  0.6 1.5 copy-start.2
  2.1 4.2 %copy-start.3 = (bf16[1280,8]{0,1:T(8,128)(2,1)S(1)}, bf16[1280,8]{0,1:T(8,128)(2,1)}, u32[]{:S(2)}) copy-start(bf16[1280,8]{0,1:T(8,128)(2,1)} %param.7) | copy-start | bytes 61444
  2.3 14.6 %collective-permute-start.4 = (bf16[2,80,1280]{2,1,0:T(8,128)(2,1)S(1)}, bf16[2,80,1280]{2,1,0:T(8,128)(2,1)S(1)}, u32[]{:S(2)}, u32[]{:S(2)}) collective-permute-start(bf16[2,80,1280]{2,1,0:T(8,128)(2,1)S(1)} %pad_maximum_fusion.3.refs_0_), channel_id=1, source_target_pairs={{0,16},{16,0},{32,48},{48,32},{64,80},{80,64},{96,112},{112,96},{1... | collective-permute-start | bytes 1228808 | tf_op jit(solution)/shard_map/ppermute | solution.py:16
  4.5 13.3 %collective-permute-start.2 = (bf16[2,80,1280]{2,1,0:T(8,128)(2,1)S(1)}, bf16[2,80,1280]{2,1,0:T(8,128)(2,1)S(1)}, u32[]{:S(2)}, u32[]{:S(2)}) collective-permute-start(bf16[2,80,1280]{2,1,0:T(8,128)(2,1)S(1)} %pad_maximum_fusion.3.refs_0_), channel_id=1, source_target_pairs={{0,48},{16,32},{32,16},{48,0},{64,112},{80,96},{96,80},{112,64},{1... | collective-permute-start | bytes 1228808 | tf_op jit(solution)/shard_map/ppermute | solution.py:16
  6.4 9.1 %collective-permute-start = (bf16[8,1280]{1,0:T(8,128)(2,1)S(1)}, bf16[8,1280]{1,0:T(8,128)(2,1)S(1)}, u32[]{:S(2)}, u32[]{:S(2)}) collective-permute-start(bf16[8,1280]{1,0:T(8,128)(2,1)S(1)} %bitcast.61), channel_id=1, source_target_pairs={{0,2},{1,3},{2,0},{3,1},{4,6},{5,7},{6,4},{7,5},{8,10},{9,11},{10,... | collective-permute-start | bytes 61448 | tf_op jit(solution)/shard_map/ppermute | solution.py:16
  13.3 20.9 %collective-permute-start.7 = (bf16[2,80,1280]{2,1,0:T(8,128)(2,1)S(1)}, bf16[2,80,1280]{2,1,0:T(8,128)(2,1)S(1)}, u32[]{:S(2)}, u32[]{:S(2)}) collective-permute-start(bf16[2,80,1280]{2,1,0:T(8,128)(2,1)S(1)} %pad_maximum_fusion.5), channel_id=1, source_target_pairs={{0,128},{16,144},{32,160},{48,176},{64,192},{80,208},{96,224},{112... | collective-permute-start | bytes 1228808 | tf_op jit(solution)/shard_map/ppermute | solution.py:16
  14.6 28.2 %copy-start = (bf16[8,256,1280]{2,1,0:T(8,128)(2,1)S(1)}, bf16[8,256,1280]{2,1,0:T(8,128)(2,1)}, u32[]{:S(2)}) copy-start(bf16[8,256,1280]{2,1,0:T(8,128)(2,1)} %refs_1_.1) | copy-start | bytes 15728644
  14.6 19.6 %collective-permute-start.6 = (bf16[2,80,1280]{2,1,0:T(8,128)(2,1)S(1)}, bf16[2,80,1280]{2,1,0:T(8,128)(2,1)S(1)}, u32[]{:S(2)}, u32[]{:S(2)}) collective-permute-start(bf16[2,80,1280]{2,1,0:T(8,128)(2,1)S(1)} %pad_maximum_fusion.4), channel_id=1, source_target_pairs={{0,64},{16,80},{32,96},{48,112},{64,0},{80,16},{96,32},{112,48},{1... | collective-permute-start | bytes 1228808 | tf_op jit(solution)/shard_map/ppermute | solution.py:16
  15.5 2.9 %collective-permute-start.1 = (bf16[16,1280]{1,0:T(8,128)(2,1)S(1)}, bf16[16,1280]{1,0:T(8,128)(2,1)S(1)}, u32[]{:S(2)}, u32[]{:S(2)}) collective-permute-start(bf16[16,1280]{1,0:T(8,128)(2,1)S(1)} %pad_maximum_fusion.11), channel_id=1, source_target_pairs={{0,4},{1,5},{2,6},{3,7},{4,0},{5,1},{6,2},{7,3},{8,12},{9,13},{10,... | collective-permute-start | bytes 122888 | tf_op jit(solution)/shard_map/ppermute | solution.py:16
  16.9 17.4 %collective-permute-start.5 = (bf16[80,1280]{1,0:T(8,128)(2,1)S(1)}, bf16[80,1280]{1,0:T(8,128)(2,1)S(1)}, u32[]{:S(2)}, u32[]{:S(2)}) collective-permute-start(bf16[80,1280]{1,0:T(8,128)(2,1)S(1)} %slice_bitcast_fusion.2), channel_id=1, source_target_pairs={{0,48},{16,32},{32,16},{48,0},{64,112},{80,96},{96,80},{112,64},{1... | collective-permute-start | bytes 614408 | tf_op jit(solution)/shard_map/ppermute | solution.py:16
  17.7 16.5 %collective-permute-start.3 = (bf16[80,1280]{1,0:T(8,128)(2,1)S(1)}, bf16[80,1280]{1,0:T(8,128)(2,1)S(1)}, u32[]{:S(2)}, u32[]{:S(2)}) collective-permute-start(bf16[80,1280]{1,0:T(8,128)(2,1)S(1)} %slice_bitcast_fusion.3), channel_id=1, source_target_pairs={{0,16},{16,0},{32,48},{48,32},{64,80},{80,64},{96,112},{112,96},{1... | collective-permute-start | bytes 614408 | tf_op jit(solution)/shard_map/ppermute | solution.py:16
  34.2 5.8 %collective-permute-start.11 = (bf16[32,1280]{1,0:T(8,128)(2,1)S(1)}, bf16[32,1280]{1,0:T(8,128)(2,1)S(1)}, u32[]{:S(2)}, u32[]{:S(2)}) collective-permute-start(bf16[32,1280]{1,0:T(8,128)(2,1)S(1)} %pad_maximum_fusion.10), channel_id=1, source_target_pairs={{0,8},{1,9},{2,10},{3,11},{4,12},{5,13},{6,14},{7,15},{8,0},{9,1},... | collective-permute-start | bytes 245768 | tf_op jit(solution)/shard_map/ppermute | solution.py:16
  37.2 19.7 %collective-permute-start.9 = (bf16[2,2,80,1280]{3,2,1,0:T(8,128)(2,1)S(1)}, bf16[2,2,80,1280]{3,2,1,0:T(8,128)(2,1)S(1)}, u32[]{:S(2)}, u32[]{:S(2)}) collective-permute-start(bf16[2,2,80,1280]{3,2,1,0:T(8,128)(2,1)S(1)} %pad_maximum_fusion.refs_5_), channel_id=1, source_target_pairs={{0,48},{16,32},{32,16},{48,0},{64,112},{80,96},{96,80},{112,64},{1... | collective-permute-start | bytes 2457608 | tf_op jit(solution)/shard_map/ppermute | solution.py:16
  38.0 18.8 %collective-permute-start.8 = (bf16[2,2,80,1280]{3,2,1,0:T(8,128)(2,1)S(1)}, bf16[2,2,80,1280]{3,2,1,0:T(8,128)(2,1)S(1)}, u32[]{:S(2)}, u32[]{:S(2)}) collective-permute-start(bf16[2,2,80,1280]{3,2,1,0:T(8,128)(2,1)S(1)} %pad_maximum_fusion.refs_5_), channel_id=1, source_target_pairs={{0,16},{16,0},{32,48},{48,32},{64,80},{80,64},{96,112},{112,96},{1... | collective-permute-start | bytes 2457608 | tf_op jit(solution)/shard_map/ppermute | solution.py:16
  38.0 12.6 %collective-permute-start.10 = (bf16[2,80,1280]{2,1,0:T(8,128)(2,1)S(1)}, bf16[2,80,1280]{2,1,0:T(8,128)(2,1)S(1)}, u32[]{:S(2)}, u32[]{:S(2)}) collective-permute-start(bf16[2,80,1280]{2,1,0:T(8,128)(2,1)S(1)} %pad_maximum_fusion.6), channel_id=1, source_target_pairs={{0,192},{16,208},{32,224},{48,240},{64,128},{80,144},{96,160},{112... | collective-permute-start | bytes 1228808 | tf_op jit(solution)/shard_map/ppermute | solution.py:16
  40.1 2.7 %collective-permute-start.12 = (bf16[64,1280]{1,0:T(8,128)(2,1)S(1)}, bf16[64,1280]{1,0:T(8,128)(2,1)S(1)}, u32[]{:S(2)}, u32[]{:S(2)}) collective-permute-start(bf16[64,1280]{1,0:T(8,128)(2,1)S(1)} %pad_maximum_fusion.9), channel_id=1, source_target_pairs={{0,1},{1,0},{2,3},{3,2},{4,5},{5,4},{6,7},{7,6},{8,9},{9,8},{10,11... | collective-permute-start | bytes 491528 | tf_op jit(solution)/shard_map/ppermute | solution.py:16
  42.8 6.6 %copy-start.1 = (bf16[8,256,1280]{2,1,0:T(8,128)(2,1)S(1)}, bf16[8,256,1280]{2,1,0:T(8,128)(2,1)}, u32[]{:S(2)}) copy-start(bf16[8,256,1280]{2,1,0:T(8,128)(2,1)} %refs_4_.1) | copy-start | bytes 15728644
  56.8 15.1 %collective-permute-start.21 = (bf16[128,1280]{1,0:T(8,128)(2,1)S(1)}, bf16[128,1280]{1,0:T(8,128)(2,1)S(1)}, u32[]{:S(2)}, u32[]{:S(2)}) collective-permute-start(bf16[128,1280]{1,0:T(8,128)(2,1)S(1)} %pad_maximum_fusion.8), channel_id=1, source_target_pairs={{0,64},{16,80},{32,96},{48,112},{64,0},{80,16},{96,32},{112,48},{1... | collective-permute-start | bytes 983048 | tf_op jit(solution)/shard_map/ppermute | solution.py:16
  56.8 15.2 %collective-permute-start.17 = (bf16[128,1280]{1,0:T(8,128)(2,1)S(1)}, bf16[128,1280]{1,0:T(8,128)(2,1)S(1)}, u32[]{:S(2)}, u32[]{:S(2)}) collective-permute-start(bf16[128,1280]{1,0:T(8,128)(2,1)S(1)} %pad_maximum_fusion.8), channel_id=1, source_target_pairs={{0,128},{16,144},{32,160},{48,176},{64,192},{80,208},{96,224},{112... | collective-permute-start | bytes 983048 | tf_op jit(solution)/shard_map/ppermute | solution.py:16
  59.5 12.5 %collective-permute-start.16 = (bf16[2,80,1280]{2,1,0:T(8,128)(2,1)S(1)}, bf16[2,80,1280]{2,1,0:T(8,128)(2,1)S(1)}, u32[]{:S(2)}, u32[]{:S(2)}) collective-permute-start(bf16[2,80,1280]{2,1,0:T(8,128)(2,1)S(1)} %collective-permute-done.10.refs_10_), channel_id=1, source_target_pairs={{0,48},{16,32},{32,16},{48,0},{64,112},{80,96},{96,80},{112,64},{1... | collective-permute-start | bytes 1228808 | tf_op jit(solution)/shard_map/ppermute | solution.py:16
  60.7 11.3 %collective-permute-start.15 = (bf16[2,80,1280]{2,1,0:T(8,128)(2,1)S(1)}, bf16[2,80,1280]{2,1,0:T(8,128)(2,1)S(1)}, u32[]{:S(2)}, u32[]{:S(2)}) collective-permute-start(bf16[2,80,1280]{2,1,0:T(8,128)(2,1)S(1)} %collective-permute-done.10.refs_10_), channel_id=1, source_target_pairs={{0,16},{16,0},{32,48},{48,32},{64,80},{80,64},{96,112},{112,96},{1... | collective-permute-start | bytes 1228808 | tf_op jit(solution)/shard_map/ppermute | solution.py:16
  60.7 17.2 %collective-permute-start.14 = (bf16[2,80,1280]{2,1,0:T(8,128)(2,1)S(1)}, bf16[2,80,1280]{2,1,0:T(8,128)(2,1)S(1)}, u32[]{:S(2)}, u32[]{:S(2)}) collective-permute-start(bf16[2,80,1280]{2,1,0:T(8,128)(2,1)S(1)} %slice_bitcast_fusion), channel_id=1, source_target_pairs={{0,48},{16,32},{32,16},{48,0},{64,112},{80,96},{96,80},{112,64},{1... | collective-permute-start | bytes 1228808 | tf_op jit(solution)/shard_map/ppermute | solution.py:16
  72.0 9.2 %collective-permute-start.13 = (bf16[2,80,1280]{2,1,0:T(8,128)(2,1)S(1)}, bf16[2,80,1280]{2,1,0:T(8,128)(2,1)S(1)}, u32[]{:S(2)}, u32[]{:S(2)}) collective-permute-start(bf16[2,80,1280]{2,1,0:T(8,128)(2,1)S(1)} %slice_bitcast_fusion.1), channel_id=1, source_target_pairs={{0,16},{16,0},{32,48},{48,32},{64,80},{80,64},{96,112},{112,96},{1... | collective-permute-start | bytes 1228808 | tf_op jit(solution)/shard_map/ppermute | solution.py:16
  72.1 10.3 %collective-permute-start.19 = (bf16[80,1280]{1,0:T(8,128)(2,1)S(1)}, bf16[80,1280]{1,0:T(8,128)(2,1)S(1)}, u32[]{:S(2)}, u32[]{:S(2)}) collective-permute-start(bf16[80,1280]{1,0:T(8,128)(2,1)S(1)} %slice_bitcast_fusion.4), channel_id=1, source_target_pairs={{0,48},{16,32},{32,16},{48,0},{64,112},{80,96},{96,80},{112,64},{1... | collective-permute-start | bytes 614408 | tf_op jit(solution)/shard_map/ppermute | solution.py:16
  73.6 12.0 %collective-permute-start.18 = (bf16[80,1280]{1,0:T(8,128)(2,1)S(1)}, bf16[80,1280]{1,0:T(8,128)(2,1)S(1)}, u32[]{:S(2)}, u32[]{:S(2)}) collective-permute-start(bf16[80,1280]{1,0:T(8,128)(2,1)S(1)} %slice_bitcast_fusion.5), channel_id=1, source_target_pairs={{0,16},{16,0},{32,48},{48,32},{64,80},{80,64},{96,112},{112,96},{1... | collective-permute-start | bytes 614408 | tf_op jit(solution)/shard_map/ppermute | solution.py:16
  74.2 11.3 %collective-permute-start.20 = (bf16[128,1280]{1,0:T(8,128)(2,1)S(1)}, bf16[128,1280]{1,0:T(8,128)(2,1)S(1)}, u32[]{:S(2)}, u32[]{:S(2)}) collective-permute-start(bf16[128,1280]{1,0:T(8,128)(2,1)S(1)} %collective-permute-done.17), channel_id=1, source_target_pairs={{0,64},{16,80},{32,96},{48,112},{64,0},{80,16},{96,32},{112,48},{1... | collective-permute-start | bytes 983048 | tf_op jit(solution)/shard_map/ppermute | solution.py:16
  89.7 5.7 %collective-permute-start.25 = (bf16[64,1280]{1,0:T(8,128)(2,1)S(1)}, bf16[64,1280]{1,0:T(8,128)(2,1)S(1)}, u32[]{:S(2)}, u32[]{:S(2)}) collective-permute-start(bf16[64,1280]{1,0:T(8,128)(2,1)S(1)} %get-tuple-element.89), channel_id=1, source_target_pairs={{0,64},{16,80},{32,96},{48,112},{64,0},{80,16},{96,32},{112,48},{1... | collective-permute-start | bytes 491528 | tf_op jit(solution)/shard_map/ppermute | solution.py:16
  89.8 7.2 %collective-permute-start.26 = (bf16[64,1280]{1,0:T(8,128)(2,1)S(1)}, bf16[64,1280]{1,0:T(8,128)(2,1)S(1)}, u32[]{:S(2)}, u32[]{:S(2)}) collective-permute-start(bf16[64,1280]{1,0:T(8,128)(2,1)S(1)} %get-tuple-element.90), channel_id=1, source_target_pairs={{0,128},{16,144},{32,160},{48,176},{64,192},{80,208},{96,224},{112... | collective-permute-start | bytes 491528 | tf_op jit(solution)/shard_map/ppermute | solution.py:16
  91.9 8.6 %collective-permute-start.27 = (bf16[64,1280]{1,0:T(8,128)(2,1)S(1)}, bf16[64,1280]{1,0:T(8,128)(2,1)S(1)}, u32[]{:S(2)}, u32[]{:S(2)}) collective-permute-start(bf16[64,1280]{1,0:T(8,128)(2,1)S(1)} %get-tuple-element.91), channel_id=1, source_target_pairs={{0,192},{16,208},{32,224},{48,240},{64,128},{80,144},{96,160},{112... | collective-permute-start | bytes 491528 | tf_op jit(solution)/shard_map/ppermute | solution.py:16
  93.4 21.8 %collective-permute-start.22 = (bf16[64,1280]{1,0:T(8,128)(2,1)S(1)}, bf16[64,1280]{1,0:T(8,128)(2,1)S(1)}, u32[]{:S(2)}, u32[]{:S(2)}) collective-permute-start(bf16[64,1280]{1,0:T(8,128)(2,1)S(1)} %get-tuple-element.81), channel_id=1, source_target_pairs={{0,64},{16,80},{32,96},{48,112},{64,0},{80,16},{96,32},{112,48},{1... | collective-permute-start | bytes 491528 | tf_op jit(solution)/shard_map/ppermute | solution.py:16
  93.4 23.3 %collective-permute-start.23 = (bf16[64,1280]{1,0:T(8,128)(2,1)S(1)}, bf16[64,1280]{1,0:T(8,128)(2,1)S(1)}, u32[]{:S(2)}, u32[]{:S(2)}) collective-permute-start(bf16[64,1280]{1,0:T(8,128)(2,1)S(1)} %get-tuple-element.82), channel_id=1, source_target_pairs={{0,128},{16,144},{32,160},{48,176},{64,192},{80,208},{96,224},{112... | collective-permute-start | bytes 491528 | tf_op jit(solution)/shard_map/ppermute | solution.py:16
  95.4 21.3 %collective-permute-start.24 = (bf16[64,1280]{1,0:T(8,128)(2,1)S(1)}, bf16[64,1280]{1,0:T(8,128)(2,1)S(1)}, u32[]{:S(2)}, u32[]{:S(2)}) collective-permute-start(bf16[64,1280]{1,0:T(8,128)(2,1)S(1)} %get-tuple-element.83), channel_id=1, source_target_pairs={{0,192},{16,208},{32,224},{48,240},{64,128},{80,144},{96,160},{112... | collective-permute-start | bytes 491528 | tf_op jit(solution)/shard_map/ppermute | solution.py:16
  102.5 14.2 %collective-permute-start.30 = (f32[8,256]{1,0:T(8,128)S(1)}, f32[8,256]{1,0:T(8,128)S(1)}, u32[]{:S(2)}, u32[]{:S(2)}) collective-permute-start(f32[8,256]{1,0:T(8,128)S(1)} %get-tuple-element.96), channel_id=1, source_target_pairs={{0,3},{1,2},{2,1},{3,0},{4,7},{5,6},{6,5},{7,4},{8,11},{9,10},{10,... | collective-permute-start | bytes 24584 | tf_op jit(solution)/shard_map/ppermute | solution.py:16
  110.4 6.7 %collective-permute-start.29 = (f32[8,256]{1,0:T(8,128)S(1)}, f32[8,256]{1,0:T(8,128)S(1)}, u32[]{:S(2)}, u32[]{:S(2)}) collective-permute-start(f32[8,256]{1,0:T(8,128)S(1)} %get-tuple-element.96), channel_id=1, source_target_pairs={{0,2},{1,3},{2,0},{3,1},{4,6},{5,7},{6,4},{7,5},{8,10},{9,11},{10,... | collective-permute-start | bytes 24584 | tf_op jit(solution)/shard_map/ppermute | solution.py:16
  115.1 2.0 %collective-permute-start.28 = (f32[8,256]{1,0:T(8,128)S(1)}, f32[8,256]{1,0:T(8,128)S(1)}, u32[]{:S(2)}, u32[]{:S(2)}) collective-permute-start(f32[8,256]{1,0:T(8,128)S(1)} %get-tuple-element.96), channel_id=1, source_target_pairs={{0,1},{1,0},{2,3},{3,2},{4,5},{5,4},{6,7},{7,6},{8,9},{9,8},{10,11... | collective-permute-start | bytes 24584 | tf_op jit(solution)/shard_map/ppermute | solution.py:16
  117.1 5.7 %collective-permute-start.33 = (f32[8,256]{1,0:T(8,128)S(1)}, f32[8,256]{1,0:T(8,128)S(1)}, u32[]{:S(2)}, u32[]{:S(2)}) collective-permute-start(f32[8,256]{1,0:T(8,128)S(1)} %add_add_fusion.2), channel_id=1, source_target_pairs={{0,12},{1,13},{2,14},{3,15},{4,8},{5,9},{6,10},{7,11},{8,4},{9,5},... | collective-permute-start | bytes 24584 | tf_op jit(solution)/shard_map/ppermute | solution.py:16
  118.1 4.8 %collective-permute-start.32 = (f32[8,256]{1,0:T(8,128)S(1)}, f32[8,256]{1,0:T(8,128)S(1)}, u32[]{:S(2)}, u32[]{:S(2)}) collective-permute-start(f32[8,256]{1,0:T(8,128)S(1)} %add_add_fusion.2), channel_id=1, source_target_pairs={{0,8},{1,9},{2,10},{3,11},{4,12},{5,13},{6,14},{7,15},{8,0},{9,1},... | collective-permute-start | bytes 24584 | tf_op jit(solution)/shard_map/ppermute | solution.py:16
  119.3 3.5 %collective-permute-start.31 = (f32[8,256]{1,0:T(8,128)S(1)}, f32[8,256]{1,0:T(8,128)S(1)}, u32[]{:S(2)}, u32[]{:S(2)}) collective-permute-start(f32[8,256]{1,0:T(8,128)S(1)} %add_add_fusion.2), channel_id=1, source_target_pairs={{0,4},{1,5},{2,6},{3,7},{4,0},{5,1},{6,2},{7,3},{8,12},{9,13},{10,... | collective-permute-start | bytes 24584 | tf_op jit(solution)/shard_map/ppermute | solution.py:16
  123.0 18.3 %collective-permute-start.35 = (bf16[64,1408]{1,0:T(8,128)(2,1)S(1)}, bf16[64,1408]{1,0:T(8,128)(2,1)S(1)}, u32[]{:S(2)}, u32[]{:S(2)}) collective-permute-start(bf16[64,1408]{1,0:T(8,128)(2,1)S(1)} %get-tuple-element.105), channel_id=1, source_target_pairs={{0,2},{1,3},{2,0},{3,1},{4,6},{5,7},{6,4},{7,5},{8,10},{9,11},{10,... | collective-permute-start | bytes 540680 | tf_op jit(solution)/shard_map/ppermute | solution.py:16
  128.4 12.9 %collective-permute-start.34 = (f32[8,1280]{1,0:T(8,128)S(1)}, f32[8,1280]{1,0:T(8,128)S(1)}, u32[]{:S(2)}, u32[]{:S(2)}) collective-permute-start(f32[8,1280]{1,0:T(8,128)S(1)} %convolution_bitcast_fusion), channel_id=1, source_target_pairs={{0,64},{16,80},{32,96},{48,112},{64,0},{80,16},{96,32},{112,48},{1... | collective-permute-start | bytes 122888 | tf_op jit(solution)/shard_map/ppermute | solution.py:16
  141.4 17.5 %collective-permute-start.38 = (bf16[2,64,1408]{2,1,0:T(8,128)(2,1)S(1)}, bf16[2,64,1408]{2,1,0:T(8,128)(2,1)S(1)}, u32[]{:S(2)}, u32[]{:S(2)}) collective-permute-start(bf16[2,64,1408]{2,1,0:T(8,128)(2,1)S(1)} %pad_maximum_fusion.7.pair), channel_id=1, source_target_pairs={{0,12},{1,13},{2,14},{3,15},{4,8},{5,9},{6,10},{7,11},{8,4},{9,5},... | collective-permute-start | bytes 1081352 | tf_op jit(solution)/shard_map/ppermute | solution.py:16
  142.7 16.2 %collective-permute-start.37 = (bf16[2,64,1408]{2,1,0:T(8,128)(2,1)S(1)}, bf16[2,64,1408]{2,1,0:T(8,128)(2,1)S(1)}, u32[]{:S(2)}, u32[]{:S(2)}) collective-permute-start(bf16[2,64,1408]{2,1,0:T(8,128)(2,1)S(1)} %pad_maximum_fusion.7.pair), channel_id=1, source_target_pairs={{0,8},{1,9},{2,10},{3,11},{4,12},{5,13},{6,14},{7,15},{8,0},{9,1},... | collective-permute-start | bytes 1081352 | tf_op jit(solution)/shard_map/ppermute | solution.py:16
  143.8 16.3 %collective-permute-start.36 = (bf16[2,64,1408]{2,1,0:T(8,128)(2,1)S(1)}, bf16[2,64,1408]{2,1,0:T(8,128)(2,1)S(1)}, u32[]{:S(2)}, u32[]{:S(2)}) collective-permute-start(bf16[2,64,1408]{2,1,0:T(8,128)(2,1)S(1)} %pad_maximum_fusion.7.pair), channel_id=1, source_target_pairs={{0,4},{1,5},{2,6},{3,7},{4,0},{5,1},{6,2},{7,3},{8,12},{9,13},{10,... | collective-permute-start | bytes 1081352 | tf_op jit(solution)/shard_map/ppermute | solution.py:16
  144.7 4.4 %collective-permute-start.39 = (f32[8,1280]{1,0:T(8,128)S(1)}, f32[8,1280]{1,0:T(8,128)S(1)}, u32[]{:S(2)}, u32[]{:S(2)}) collective-permute-start(f32[8,1280]{1,0:T(8,128)S(1)} %add.72), channel_id=1, source_target_pairs={{0,128},{16,144},{32,160},{48,176},{64,192},{80,208},{96,224},{112... | collective-permute-start | bytes 122888 | tf_op jit(solution)/shard_map/ppermute | solution.py:16
  149.1 3.1 %collective-permute-start.40 = (f32[8,1280]{1,0:T(8,128)S(1)}, f32[8,1280]{1,0:T(8,128)S(1)}, u32[]{:S(2)}, u32[]{:S(2)}) collective-permute-start(f32[8,1280]{1,0:T(8,128)S(1)} %add.73), channel_id=1, source_target_pairs={{0,16},{16,0},{32,48},{48,32},{64,80},{80,64},{96,112},{112,96},{1... | collective-permute-start | bytes 122888 | tf_op jit(solution)/shard_map/ppermute | solution.py:16
  152.3 7.8 %collective-permute-start.41 = (f32[8,1280]{1,0:T(8,128)S(1)}, f32[8,1280]{1,0:T(8,128)S(1)}, u32[]{:S(2)}, u32[]{:S(2)}) collective-permute-start(f32[8,1280]{1,0:T(8,128)S(1)} %add.74), channel_id=1, source_target_pairs={{0,32},{16,48},{32,0},{48,16},{64,96},{80,112},{96,64},{112,80},{1... | collective-permute-start | bytes 122888 | tf_op jit(solution)/shard_map/ppermute | solution.py:16
  161.3 2.8 %collective-permute-start.42 = (f32[128,1280]{1,0:T(8,128)S(1)}, f32[128,1280]{1,0:T(8,128)S(1)}, u32[]{:S(2)}, u32[]{:S(2)}) collective-permute-start(f32[128,1280]{1,0:T(8,128)S(1)} %get-tuple-element.113), channel_id=1, source_target_pairs={{0,1},{1,0},{2,3},{3,2},{4,5},{5,4},{6,7},{7,6},{8,9},{9,8},{10,11... | collective-permute-start | bytes 1966088 | tf_op jit(solution)/shard_map/ppermute | solution.py:16

commit v13 on v12

--- a/solution.py
+++ b/solution.py
@@ -371,14 +371,12 @@
     term = jnp.einsum(
         "bsm,bmd->sd", logit_grad_b.reshape(images, own, count), tokens, preferred_element_type=F32
     )
-    term = summed(term, "dp", 4)
     term, far = together(term, far)
     pieces = all_x(jnp.stack([near, far]))
-    term = summed(term, "dp", 8, 1)
-    last = swap(term, "dp", 2)
-    slot_grad = (term + last).T
-
-    pieces[1] = after(pieces[1], last)
+    term = summed(term, "dp", 4, 8, 1)
+    pieces[1] = after(pieces[1], term)
+    slot_grad = summed(after(term, *pieces), "dp", 2).T
+
     mine, theirs = tokens_call(spread, pieces, table)
     token_grad = (mine + swap(theirs, "expert", 1)).astype(BF16)
     return (token_grad.reshape(images, -1, width), slot_grad)

time: 166 us -> 167 us (level)
  starting transfers between devices: 76 us -> 80.9 us
  waiting for transfers between devices: 65.8 us -> 62.2 us
    ppermute x43, starting transfers between devices: 76 us -> 80.9 us  [swap(): return lax.ppermute(value, axis, [(i, i ^ k) for i in range(count)])]
    ppermute x43, waiting for transfers between devices: 65.8 us -> 62.2 us  [swap(): return lax.ppermute(value, axis, [(i, i ^ k) for i in range(count)])]
  transfers between devices with their start and end apart: 43 -> 43, of which waited for: 19 -> 18; matrix products, arithmetic and copies ran while one was open for 2% -> 2% of each run, Pallas kernels for 7% -> 7%
where the time goes in v13:
time: 167 us; the launch traced here: 166 us
  starting transfers between devices  80.9 us (48%)
  waiting for transfers between devices  62.2 us (37%)
  Pallas kernels  16.8 us (10%)
  other arithmetic  1.93 us (1%)
  local copies, waits for them, and re-layouts  1.76 us (1%)
    ppermute x43, starting transfers between devices, swap(): return lax.ppermute(value, axis, [(i, i ^ k) for i in range(count)])  80.9 us
    ppermute x43, waiting for transfers between devices, swap(): return lax.ppermute(value, axis, [(i, i ^ k) for i in range(count)])  62.2 us
    pallas_call x1, Pallas kernels, slots_call(): pl.pallas_call(slots_kernel, grid=(images // 2,), out_shape=[jax.ShapeDty...  6.63 us
    pallas_call x2, Pallas kernels, against(): pl.pallas_call(lambda *refs: against_kernel(over_tokens, len(parts), *ref...  4.32 us
    pallas_call x1, Pallas kernels, ffn(): pl.pallas_call(ffn_kernel, out_shape=[jax.ShapeDtypeStruct((own_rows, wid...  4.04 us
  transfers between devices with their start and end apart: 43, of which 18 were waited for; matrix products, arithmetic and copies ran while one was open for 2% of the time, Pallas kernels for 7%

profile of v13, /device:TPU:1, one launch (start us, length us, event | category | flops | bytes accessed | tf_op | source)
XLA Modules:
  0.0 166.1 jit_solution(3381990000829493846)
XLA Ops:
  0.7 1.4 dynamic-slice_bitcast_fusion.1
  2.3 2.2 %collective-permute-start.4 = (bf16[2,80,1280]{2,1,0:T(8,128)(2,1)S(1)}, bf16[2,80,1280]{2,1,0:T(8,128)(2,1)S(1)}, u32[]{:S(2)}, u32[]{:S(2)}) collective-permute-start(bf16[2,80,1280]{2,1,0:T(8,128)(2,1)S(1)} %pad_maximum_fusion.3.refs_0_), channel_id=1, source_target_pairs={{0,16},{16,0},{32,48},{48,32},{64,80},{80,64},{96,112},{112,96},{1... | collective-permute-start | bytes 1228808 | tf_op jit(solution)/shard_map/ppermute | solution.py:16
  4.5 1.9 %collective-permute-start.2 = (bf16[2,80,1280]{2,1,0:T(8,128)(2,1)S(1)}, bf16[2,80,1280]{2,1,0:T(8,128)(2,1)S(1)}, u32[]{:S(2)}, u32[]{:S(2)}) collective-permute-start(bf16[2,80,1280]{2,1,0:T(8,128)(2,1)S(1)} %pad_maximum_fusion.3.refs_0_), channel_id=1, source_target_pairs={{0,48},{16,32},{32,16},{48,0},{64,112},{80,96},{96,80},{112,64},{1... | collective-permute-start | bytes 1228808 | tf_op jit(solution)/shard_map/ppermute | solution.py:16
  6.4 6.9 %collective-permute-start = (bf16[8,1280]{1,0:T(8,128)(2,1)S(1)}, bf16[8,1280]{1,0:T(8,128)(2,1)S(1)}, u32[]{:S(2)}, u32[]{:S(2)}) collective-permute-start(bf16[8,1280]{1,0:T(8,128)(2,1)S(1)} %bitcast.61), channel_id=1, source_target_pairs={{0,2},{1,3},{2,0},{3,1},{4,6},{5,7},{6,4},{7,5},{8,10},{9,11},{10,... | collective-permute-start | bytes 61448 | tf_op jit(solution)/shard_map/ppermute | solution.py:16
  13.3 1.3 collective-permute-start.7
  14.6 0.8 collective-permute-start.6
  15.5 1.3 collective-permute-start.1
  16.9 0.9 collective-permute-start.5
  17.8 0.6 collective-permute-done.1
  18.5 15.7 %collective-permute-done.7 = bf16[2,80,1280]{2,1,0:T(8,128)(2,1)S(1)} collective-permute-done((bf16[2,80,1280]{2,1,0:T(8,128)(2,1)S(1)}, bf16[2,80,1280]{2,1,0:T(8,128)(2,1)S(1)}, u32[]{:S(2)}, u32[]{:S(2)}) %collective-permute-start.7) | collective-permute-done | bytes 409632 | tf_op jit(solution)/shard_map/ppermute | solution.py:16
  34.2 2.8 %collective-permute-start.11 = (bf16[32,1280]{1,0:T(8,128)(2,1)S(1)}, bf16[32,1280]{1,0:T(8,128)(2,1)S(1)}, u32[]{:S(2)}, u32[]{:S(2)}) collective-permute-start(bf16[32,1280]{1,0:T(8,128)(2,1)S(1)} %pad_maximum_fusion.10), channel_id=1, source_target_pairs={{0,8},{1,9},{2,10},{3,11},{4,12},{5,13},{6,14},{7,15},{8,0},{9,1},... | collective-permute-start | bytes 245768 | tf_op jit(solution)/shard_map/ppermute | solution.py:16
  37.2 0.9 collective-permute-start.9
  38.0 2.0 %collective-permute-start.10 = (bf16[2,80,1280]{2,1,0:T(8,128)(2,1)S(1)}, bf16[2,80,1280]{2,1,0:T(8,128)(2,1)S(1)}, u32[]{:S(2)}, u32[]{:S(2)}) collective-permute-start(bf16[2,80,1280]{2,1,0:T(8,128)(2,1)S(1)} %pad_maximum_fusion.6), channel_id=1, source_target_pairs={{0,192},{16,208},{32,224},{48,240},{64,128},{80,144},{96,160},{112... | collective-permute-start | bytes 1228808 | tf_op jit(solution)/shard_map/ppermute | solution.py:16
  40.1 1.7 %collective-permute-start.12 = (bf16[64,1280]{1,0:T(8,128)(2,1)S(1)}, bf16[64,1280]{1,0:T(8,128)(2,1)S(1)}, u32[]{:S(2)}, u32[]{:S(2)}) collective-permute-start(bf16[64,1280]{1,0:T(8,128)(2,1)S(1)} %pad_maximum_fusion.9), channel_id=1, source_target_pairs={{0,1},{1,0},{2,3},{3,2},{4,5},{5,4},{6,7},{7,6},{8,9},{9,8},{10,11... | collective-permute-start | bytes 491528 | tf_op jit(solution)/shard_map/ppermute | solution.py:16
  41.7 1.0 collective-permute-done.12
  42.8 6.6 %slots.1 = (bf16[64,1280]{1,0:T(8,128)(2,1)S(1)}, f32[64,256]{1,0:T(8,128)S(1)}, f32[64,256]{1,0:T(8,128)S(1)}, bf16[8,64,256]{2,1,0:T(8,128)(2,1)S(1)}) custom-call(bf16[128,1280]{1,0:T(8,128)(2,1)S(1)} %constant_dynamic-update-slice_fusion.table, bf16[8,256,1280]{2,1,0:T(8,128)(2,1)S(1)} %copy-done), custom_call_target="tpu_custom_call" | custom-call | flops 754974720 | bytes 5242880 | tf_op jit(solution)/shard_map/slots/pallas_call | solution.py:102
  49.4 0.8 fusion
  50.2 0.4 spread.1
  50.7 6.1 %collective-permute-done.9.refs_7_ = bf16[2,2,80,1280]{3,2,1,0:T(8,128)(2,1)S(1)} collective-permute-done((bf16[2,2,80,1280]{3,2,1,0:T(8,128)(2,1)S(1)}, bf16[2,2,80,1280]{3,2,1,0:T(8,128)(2,1)S(1)}, u32[]{:S(2)}, u32[]{:S(2)}) %collective-permute-start.9) | collective-permute-done | bytes 819232 | tf_op jit(solution)/shard_map/ppermute | solution.py:16
  56.8 2.7 %collective-permute-start.17 = (bf16[128,1280]{1,0:T(8,128)(2,1)S(1)}, bf16[128,1280]{1,0:T(8,128)(2,1)S(1)}, u32[]{:S(2)}, u32[]{:S(2)}) collective-permute-start(bf16[128,1280]{1,0:T(8,128)(2,1)S(1)} %pad_maximum_fusion.8), channel_id=1, source_target_pairs={{0,128},{16,144},{32,160},{48,176},{64,192},{80,208},{96,224},{112... | collective-permute-start | bytes 983048 | tf_op jit(solution)/shard_map/ppermute | solution.py:16
  59.5 1.2 collective-permute-start.16
  60.7 1.8 %collective-permute-start.14 = (bf16[2,80,1280]{2,1,0:T(8,128)(2,1)S(1)}, bf16[2,80,1280]{2,1,0:T(8,128)(2,1)S(1)}, u32[]{:S(2)}, u32[]{:S(2)}) collective-permute-start(bf16[2,80,1280]{2,1,0:T(8,128)(2,1)S(1)} %slice_bitcast_fusion), channel_id=1, source_target_pairs={{0,48},{16,32},{32,16},{48,0},{64,112},{80,96},{96,80},{112,64},{1... | collective-permute-start | bytes 1228808 | tf_op jit(solution)/shard_map/ppermute | solution.py:16
  62.5 9.4 %collective-permute-done.21 = bf16[128,1280]{1,0:T(8,128)(2,1)S(1)} collective-permute-done((bf16[128,1280]{1,0:T(8,128)(2,1)S(1)}, bf16[128,1280]{1,0:T(8,128)(2,1)S(1)}, u32[]{:S(2)}, u32[]{:S(2)}) %collective-permute-start.21) | collective-permute-done | bytes 327712 | tf_op jit(solution)/shard_map/ppermute | solution.py:16
  72.1 1.5 collective-permute-start.19
  73.6 0.6 collective-permute-start.18
  74.2 3.7 %collective-permute-done.14.refs_9_ = bf16[2,80,1280]{2,1,0:T(8,128)(2,1)S(1)} collective-permute-done((bf16[2,80,1280]{2,1,0:T(8,128)(2,1)S(1)}, bf16[2,80,1280]{2,1,0:T(8,128)(2,1)S(1)}, u32[]{:S(2)}, u32[]{:S(2)}) %collective-permute-start.14) | collective-permute-done | bytes 409632 | tf_op jit(solution)/shard_map/ppermute | solution.py:16
  77.9 3.2 %collective-permute-done.13.refs_8_ = bf16[2,80,1280]{2,1,0:T(8,128)(2,1)S(1)} collective-permute-done((bf16[2,80,1280]{2,1,0:T(8,128)(2,1)S(1)}, bf16[2,80,1280]{2,1,0:T(8,128)(2,1)S(1)}, u32[]{:S(2)}, u32[]{:S(2)}) %collective-permute-start.13) | collective-permute-done | bytes 409632 | tf_op jit(solution)/shard_map/ppermute | solution.py:16
  81.2 1.2 collective-permute-done.19.refs_14_
  82.3 3.2 %collective-permute-done.18.refs_13_ = bf16[80,1280]{1,0:T(8,128)(2,1)S(1)} collective-permute-done((bf16[80,1280]{1,0:T(8,128)(2,1)S(1)}, bf16[80,1280]{1,0:T(8,128)(2,1)S(1)}, u32[]{:S(2)}, u32[]{:S(2)}) %collective-permute-start.18) | collective-permute-done | bytes 204832 | tf_op jit(solution)/shard_map/ppermute | solution.py:16
  85.7 4.0 %ffn.1 = (f32[64,1280]{1,0:T(8,128)S(1)}, bf16[64,1280]{1,0:T(8,128)(2,1)S(1)}, bf16[64,1280]{1,0:T(8,128)(2,1)S(1)}, bf16[64,1280]{1,0:T(8,128)(2,1)S(1)}, f32[...) custom-call(bf16[256,1280]{1,0:T(8,128)(2,1)S(1)} %get-tuple-element, ...), custom_call_target="tpu_custom_call" | custom-call | tf_op jit(solution)/shard_map/ffn/pallas_call | solution.py:61
  89.7 0.1 collective-permute-start.25
  89.8 2.1 %collective-permute-start.26 = (bf16[64,1280]{1,0:T(8,128)(2,1)S(1)}, bf16[64,1280]{1,0:T(8,128)(2,1)S(1)}, u32[]{:S(2)}, u32[]{:S(2)}) collective-permute-start(bf16[64,1280]{1,0:T(8,128)(2,1)S(1)} %get-tuple-element.91), channel_id=1, source_target_pairs={{0,128},{16,144},{32,160},{48,176},{64,192},{80,208},{96,224},{112... | collective-permute-start | bytes 491528 | tf_op jit(solution)/shard_map/ppermute | solution.py:16
  91.9 1.5 collective-permute-start.27
  93.4 2.1 %collective-permute-start.23 = (bf16[64,1280]{1,0:T(8,128)(2,1)S(1)}, bf16[64,1280]{1,0:T(8,128)(2,1)S(1)}, u32[]{:S(2)}, u32[]{:S(2)}) collective-permute-start(bf16[64,1280]{1,0:T(8,128)(2,1)S(1)} %get-tuple-element.83), channel_id=1, source_target_pairs={{0,128},{16,144},{32,160},{48,176},{64,192},{80,208},{96,224},{112... | collective-permute-start | bytes 491528 | tf_op jit(solution)/shard_map/ppermute | solution.py:16
  95.4 1.5 collective-permute-start.24
  97.0 3.5 %collective-permute-done.27.refs_3_ = bf16[64,1280]{1,0:T(8,128)(2,1)S(1)} collective-permute-done((bf16[64,1280]{1,0:T(8,128)(2,1)S(1)}, bf16[64,1280]{1,0:T(8,128)(2,1)S(1)}, u32[]{:S(2)}, u32[]{:S(2)}) %collective-permute-start.27) | collective-permute-done | bytes 163872 | tf_op jit(solution)/shard_map/ppermute | solution.py:16
  100.5 2.0 %combine_grad.1 = (f32[64,256]{1,0:T(8,128)S(1)}, f32[8,256]{1,0:T(8,128)S(1)}) custom-call(f32[64,1280]{1,0:T(8,128)S(1)} %get-tuple-element.89.refs_0_, bf16[64,1280]{1,0:T(8,128)(2,1)S(1)} %collective-permute-done.25.refs_1_, bf16[64,1280]{1,0:T(8,128)(2,1)S(1)} %collective-permute-done.26.refs_2_, bf16[64,1280]{1,0:T(8,128)(2,1)S(1)} %collective-permute-done.27.refs_3_, ...), custom_call_target="tpu_custom_call" | custom-call | tf_op jit(solution)/shard_map/combine_grad/pallas_call | solution.py:188
  102.5 7.9 %collective-permute-start.30 = (f32[8,256]{1,0:T(8,128)S(1)}, f32[8,256]{1,0:T(8,128)S(1)}, u32[]{:S(2)}, u32[]{:S(2)}) collective-permute-start(f32[8,256]{1,0:T(8,128)S(1)} %get-tuple-element.97), channel_id=1, source_target_pairs={{0,3},{1,2},{2,1},{3,0},{4,7},{5,6},{6,5},{7,4},{8,11},{9,10},{10,... | collective-permute-start | bytes 24584 | tf_op jit(solution)/shard_map/ppermute | solution.py:16
  110.4 4.8 %collective-permute-start.29 = (f32[8,256]{1,0:T(8,128)S(1)}, f32[8,256]{1,0:T(8,128)S(1)}, u32[]{:S(2)}, u32[]{:S(2)}) collective-permute-start(f32[8,256]{1,0:T(8,128)S(1)} %get-tuple-element.97), channel_id=1, source_target_pairs={{0,2},{1,3},{2,0},{3,1},{4,6},{5,7},{6,4},{7,5},{8,10},{9,11},{10,... | collective-permute-start | bytes 24584 | tf_op jit(solution)/shard_map/ppermute | solution.py:16
  115.1 1.6 collective-permute-done.23
  116.7 0.4 collective-permute-done.29
  117.1 0.9 collective-permute-start.33
  118.1 1.3 collective-permute-start.32
  119.3 1.1 collective-permute-start.31
  120.5 2.3 %dispatch_grad.1.back = f32[64,256]{1,0:T(8,128)S(1)} custom-call(f32[64,1280]{1,0:T(8,128)S(1)} %add_add_fusion.refs_0_.grad, bf16[8,256,1280]{2,1,0:T(8,128)(2,1)S(1)} %copy-done, f32[64,256]{1,0:T(8,128)S(1)} %get-tuple-element.88.refs_2_), custom_call_target="tpu_custom_call" | custom-call | tf_op jit(solution)/shard_map/dispatch_grad/pallas_call | solution.py:188
  122.9 0.2 logit_grad.1
  123.0 4.6 %collective-permute-start.34 = (bf16[64,1408]{1,0:T(8,128)(2,1)S(1)}, bf16[64,1408]{1,0:T(8,128)(2,1)S(1)}, u32[]{:S(2)}, u32[]{:S(2)}) collective-permute-start(bf16[64,1408]{1,0:T(8,128)(2,1)S(1)} %get-tuple-element.106), channel_id=1, source_target_pairs={{0,2},{1,3},{2,0},{3,1},{4,6},{5,7},{6,4},{7,5},{8,10},{9,11},{10,... | collective-permute-start | bytes 540680 | tf_op jit(solution)/shard_map/ppermute | solution.py:16
  127.7 0.8 convolution_bitcast_fusion
  128.4 2.9 %collective-permute-done.34 = bf16[64,1408]{1,0:T(8,128)(2,1)S(1)} collective-permute-done((bf16[64,1408]{1,0:T(8,128)(2,1)S(1)}, bf16[64,1408]{1,0:T(8,128)(2,1)S(1)}, u32[]{:S(2)}, u32[]{:S(2)}) %collective-permute-start.34) | collective-permute-done | bytes 180256 | tf_op jit(solution)/shard_map/ppermute | solution.py:16
  131.4 1.1 collective-permute-start.37
  132.5 1.1 collective-permute-start.36
  133.6 1.1 collective-permute-start.35
  134.8 10.0 %collective-permute-start.38 = (f32[8,1280]{1,0:T(8,128)S(1)}, f32[8,1280]{1,0:T(8,128)S(1)}, u32[]{:S(2)}, u32[]{:S(2)}) collective-permute-start(f32[8,1280]{1,0:T(8,128)S(1)} %convolution_bitcast_fusion), channel_id=1, source_target_pairs={{0,64},{16,80},{32,96},{48,112},{64,0},{80,16},{96,32},{112,48},{1... | collective-permute-start | bytes 122888 | tf_op jit(solution)/shard_map/ppermute | solution.py:16
  144.7 1.7 %collective-permute-done.38 = f32[8,1280]{1,0:T(8,128)S(1)} collective-permute-done((f32[8,1280]{1,0:T(8,128)S(1)}, f32[8,1280]{1,0:T(8,128)S(1)}, u32[]{:S(2)}, u32[]{:S(2)}) %collective-permute-start.38) | collective-permute-done | bytes 40992 | tf_op jit(solution)/shard_map/ppermute | solution.py:16
  146.4 1.8 %collective-permute-start.39 = (f32[8,1280]{1,0:T(8,128)S(1)}, f32[8,1280]{1,0:T(8,128)S(1)}, u32[]{:S(2)}, u32[]{:S(2)}) collective-permute-start(f32[8,1280]{1,0:T(8,128)S(1)} %add.72), channel_id=1, source_target_pairs={{0,128},{16,144},{32,160},{48,176},{64,192},{80,208},{96,224},{112... | collective-permute-start | bytes 122888 | tf_op jit(solution)/shard_map/ppermute | solution.py:16
  148.2 2.2 %collective-permute-done.39 = f32[8,1280]{1,0:T(8,128)S(1)} collective-permute-done((f32[8,1280]{1,0:T(8,128)S(1)}, f32[8,1280]{1,0:T(8,128)S(1)}, u32[]{:S(2)}, u32[]{:S(2)}) %collective-permute-start.39) | collective-permute-done | bytes 40992 | tf_op jit(solution)/shard_map/ppermute | solution.py:16
  150.5 0.3 collective-permute-start.40
  150.8 2.5 %collective-permute-done.40 = f32[8,1280]{1,0:T(8,128)S(1)} collective-permute-done((f32[8,1280]{1,0:T(8,128)S(1)}, f32[8,1280]{1,0:T(8,128)S(1)}, u32[]{:S(2)}, u32[]{:S(2)}) %collective-permute-start.40) | collective-permute-done | bytes 40992 | tf_op jit(solution)/shard_map/ppermute | solution.py:16
  153.4 1.2 token_grad.1
  154.6 5.7 %collective-permute-start.41 = (f32[128,1280]{1,0:T(8,128)S(1)}, f32[128,1280]{1,0:T(8,128)S(1)}, u32[]{:S(2)}, u32[]{:S(2)}) collective-permute-start(f32[128,1280]{1,0:T(8,128)S(1)} %get-tuple-element.114), channel_id=1, source_target_pairs={{0,1},{1,0},{2,3},{3,2},{4,5},{5,4},{6,7},{7,6},{8,9},{9,8},{10,11... | collective-permute-start | bytes 1966088 | tf_op jit(solution)/shard_map/ppermute | solution.py:16
  160.3 1.5 collective-permute-start.42
  161.8 2.9 %collective-permute-done.42 = f32[8,1280]{1,0:T(8,128)S(1)} collective-permute-done((f32[8,1280]{1,0:T(8,128)S(1)}, f32[8,1280]{1,0:T(8,128)S(1)}, u32[]{:S(2)}, u32[]{:S(2)}) %collective-permute-start.42) | collective-permute-done | bytes 40992 | tf_op jit(solution)/shard_map/ppermute | solution.py:16
  164.7 0.6 add_bitcast_fusion
  165.3 0.8 add_convert_fusion
  (73 shorter events, 1.2 us)
Async XLA Ops:
  0.6 1.5 copy-start.2
  2.1 4.2 %copy-start.3 = (bf16[1280,8]{0,1:T(8,128)(2,1)S(1)}, bf16[1280,8]{0,1:T(8,128)(2,1)}, u32[]{:S(2)}) copy-start(bf16[1280,8]{0,1:T(8,128)(2,1)} %param.7) | copy-start | bytes 61444
  2.3 14.6 %collective-permute-start.4 = (bf16[2,80,1280]{2,1,0:T(8,128)(2,1)S(1)}, bf16[2,80,1280]{2,1,0:T(8,128)(2,1)S(1)}, u32[]{:S(2)}, u32[]{:S(2)}) collective-permute-start(bf16[2,80,1280]{2,1,0:T(8,128)(2,1)S(1)} %pad_maximum_fusion.3.refs_0_), channel_id=1, source_target_pairs={{0,16},{16,0},{32,48},{48,32},{64,80},{80,64},{96,112},{112,96},{1... | collective-permute-start | bytes 1228808 | tf_op jit(solution)/shard_map/ppermute | solution.py:16
  4.5 13.3 %collective-permute-start.2 = (bf16[2,80,1280]{2,1,0:T(8,128)(2,1)S(1)}, bf16[2,80,1280]{2,1,0:T(8,128)(2,1)S(1)}, u32[]{:S(2)}, u32[]{:S(2)}) collective-permute-start(bf16[2,80,1280]{2,1,0:T(8,128)(2,1)S(1)} %pad_maximum_fusion.3.refs_0_), channel_id=1, source_target_pairs={{0,48},{16,32},{32,16},{48,0},{64,112},{80,96},{96,80},{112,64},{1... | collective-permute-start | bytes 1228808 | tf_op jit(solution)/shard_map/ppermute | solution.py:16
  6.4 9.1 %collective-permute-start = (bf16[8,1280]{1,0:T(8,128)(2,1)S(1)}, bf16[8,1280]{1,0:T(8,128)(2,1)S(1)}, u32[]{:S(2)}, u32[]{:S(2)}) collective-permute-start(bf16[8,1280]{1,0:T(8,128)(2,1)S(1)} %bitcast.61), channel_id=1, source_target_pairs={{0,2},{1,3},{2,0},{3,1},{4,6},{5,7},{6,4},{7,5},{8,10},{9,11},{10,... | collective-permute-start | bytes 61448 | tf_op jit(solution)/shard_map/ppermute | solution.py:16
  13.3 20.9 %collective-permute-start.7 = (bf16[2,80,1280]{2,1,0:T(8,128)(2,1)S(1)}, bf16[2,80,1280]{2,1,0:T(8,128)(2,1)S(1)}, u32[]{:S(2)}, u32[]{:S(2)}) collective-permute-start(bf16[2,80,1280]{2,1,0:T(8,128)(2,1)S(1)} %pad_maximum_fusion.5), channel_id=1, source_target_pairs={{0,128},{16,144},{32,160},{48,176},{64,192},{80,208},{96,224},{112... | collective-permute-start | bytes 1228808 | tf_op jit(solution)/shard_map/ppermute | solution.py:16
  14.6 28.2 %copy-start = (bf16[8,256,1280]{2,1,0:T(8,128)(2,1)S(1)}, bf16[8,256,1280]{2,1,0:T(8,128)(2,1)}, u32[]{:S(2)}) copy-start(bf16[8,256,1280]{2,1,0:T(8,128)(2,1)} %refs_1_.1) | copy-start | bytes 15728644
  14.6 19.6 %collective-permute-start.6 = (bf16[2,80,1280]{2,1,0:T(8,128)(2,1)S(1)}, bf16[2,80,1280]{2,1,0:T(8,128)(2,1)S(1)}, u32[]{:S(2)}, u32[]{:S(2)}) collective-permute-start(bf16[2,80,1280]{2,1,0:T(8,128)(2,1)S(1)} %pad_maximum_fusion.4), channel_id=1, source_target_pairs={{0,64},{16,80},{32,96},{48,112},{64,0},{80,16},{96,32},{112,48},{1... | collective-permute-start | bytes 1228808 | tf_op jit(solution)/shard_map/ppermute | solution.py:16
  15.5 2.9 %collective-permute-start.1 = (bf16[16,1280]{1,0:T(8,128)(2,1)S(1)}, bf16[16,1280]{1,0:T(8,128)(2,1)S(1)}, u32[]{:S(2)}, u32[]{:S(2)}) collective-permute-start(bf16[16,1280]{1,0:T(8,128)(2,1)S(1)} %pad_maximum_fusion.11), channel_id=1, source_target_pairs={{0,4},{1,5},{2,6},{3,7},{4,0},{5,1},{6,2},{7,3},{8,12},{9,13},{10,... | collective-permute-start | bytes 122888 | tf_op jit(solution)/shard_map/ppermute | solution.py:16
  16.9 17.4 %collective-permute-start.5 = (bf16[80,1280]{1,0:T(8,128)(2,1)S(1)}, bf16[80,1280]{1,0:T(8,128)(2,1)S(1)}, u32[]{:S(2)}, u32[]{:S(2)}) collective-permute-start(bf16[80,1280]{1,0:T(8,128)(2,1)S(1)} %slice_bitcast_fusion.2), channel_id=1, source_target_pairs={{0,48},{16,32},{32,16},{48,0},{64,112},{80,96},{96,80},{112,64},{1... | collective-permute-start | bytes 614408 | tf_op jit(solution)/shard_map/ppermute | solution.py:16
  17.7 16.5 %collective-permute-start.3 = (bf16[80,1280]{1,0:T(8,128)(2,1)S(1)}, bf16[80,1280]{1,0:T(8,128)(2,1)S(1)}, u32[]{:S(2)}, u32[]{:S(2)}) collective-permute-start(bf16[80,1280]{1,0:T(8,128)(2,1)S(1)} %slice_bitcast_fusion.3), channel_id=1, source_target_pairs={{0,16},{16,0},{32,48},{48,32},{64,80},{80,64},{96,112},{112,96},{1... | collective-permute-start | bytes 614408 | tf_op jit(solution)/shard_map/ppermute | solution.py:16
  34.2 5.8 %collective-permute-start.11 = (bf16[32,1280]{1,0:T(8,128)(2,1)S(1)}, bf16[32,1280]{1,0:T(8,128)(2,1)S(1)}, u32[]{:S(2)}, u32[]{:S(2)}) collective-permute-start(bf16[32,1280]{1,0:T(8,128)(2,1)S(1)} %pad_maximum_fusion.10), channel_id=1, source_target_pairs={{0,8},{1,9},{2,10},{3,11},{4,12},{5,13},{6,14},{7,15},{8,0},{9,1},... | collective-permute-start | bytes 245768 | tf_op jit(solution)/shard_map/ppermute | solution.py:16
  37.2 19.7 %collective-permute-start.9 = (bf16[2,2,80,1280]{3,2,1,0:T(8,128)(2,1)S(1)}, bf16[2,2,80,1280]{3,2,1,0:T(8,128)(2,1)S(1)}, u32[]{:S(2)}, u32[]{:S(2)}) collective-permute-start(bf16[2,2,80,1280]{3,2,1,0:T(8,128)(2,1)S(1)} %pad_maximum_fusion.refs_5_), channel_id=1, source_target_pairs={{0,48},{16,32},{32,16},{48,0},{64,112},{80,96},{96,80},{112,64},{1... | collective-permute-start | bytes 2457608 | tf_op jit(solution)/shard_map/ppermute | solution.py:16
  38.0 18.8 %collective-permute-start.8 = (bf16[2,2,80,1280]{3,2,1,0:T(8,128)(2,1)S(1)}, bf16[2,2,80,1280]{3,2,1,0:T(8,128)(2,1)S(1)}, u32[]{:S(2)}, u32[]{:S(2)}) collective-permute-start(bf16[2,2,80,1280]{3,2,1,0:T(8,128)(2,1)S(1)} %pad_maximum_fusion.refs_5_), channel_id=1, source_target_pairs={{0,16},{16,0},{32,48},{48,32},{64,80},{80,64},{96,112},{112,96},{1... | collective-permute-start | bytes 2457608 | tf_op jit(solution)/shard_map/ppermute | solution.py:16
  38.0 12.6 %collective-permute-start.10 = (bf16[2,80,1280]{2,1,0:T(8,128)(2,1)S(1)}, bf16[2,80,1280]{2,1,0:T(8,128)(2,1)S(1)}, u32[]{:S(2)}, u32[]{:S(2)}) collective-permute-start(bf16[2,80,1280]{2,1,0:T(8,128)(2,1)S(1)} %pad_maximum_fusion.6), channel_id=1, source_target_pairs={{0,192},{16,208},{32,224},{48,240},{64,128},{80,144},{96,160},{112... | collective-permute-start | bytes 1228808 | tf_op jit(solution)/shard_map/ppermute | solution.py:16
  40.1 2.7 %collective-permute-start.12 = (bf16[64,1280]{1,0:T(8,128)(2,1)S(1)}, bf16[64,1280]{1,0:T(8,128)(2,1)S(1)}, u32[]{:S(2)}, u32[]{:S(2)}) collective-permute-start(bf16[64,1280]{1,0:T(8,128)(2,1)S(1)} %pad_maximum_fusion.9), channel_id=1, source_target_pairs={{0,1},{1,0},{2,3},{3,2},{4,5},{5,4},{6,7},{7,6},{8,9},{9,8},{10,11... | collective-permute-start | bytes 491528 | tf_op jit(solution)/shard_map/ppermute | solution.py:16
  42.8 6.6 %copy-start.1 = (bf16[8,256,1280]{2,1,0:T(8,128)(2,1)S(1)}, bf16[8,256,1280]{2,1,0:T(8,128)(2,1)}, u32[]{:S(2)}) copy-start(bf16[8,256,1280]{2,1,0:T(8,128)(2,1)} %refs_4_.1) | copy-start | bytes 15728644
  56.8 15.1 %collective-permute-start.21 = (bf16[128,1280]{1,0:T(8,128)(2,1)S(1)}, bf16[128,1280]{1,0:T(8,128)(2,1)S(1)}, u32[]{:S(2)}, u32[]{:S(2)}) collective-permute-start(bf16[128,1280]{1,0:T(8,128)(2,1)S(1)} %pad_maximum_fusion.8), channel_id=1, source_target_pairs={{0,64},{16,80},{32,96},{48,112},{64,0},{80,16},{96,32},{112,48},{1... | collective-permute-start | bytes 983048 | tf_op jit(solution)/shard_map/ppermute | solution.py:16
  56.8 15.2 %collective-permute-start.17 = (bf16[128,1280]{1,0:T(8,128)(2,1)S(1)}, bf16[128,1280]{1,0:T(8,128)(2,1)S(1)}, u32[]{:S(2)}, u32[]{:S(2)}) collective-permute-start(bf16[128,1280]{1,0:T(8,128)(2,1)S(1)} %pad_maximum_fusion.8), channel_id=1, source_target_pairs={{0,128},{16,144},{32,160},{48,176},{64,192},{80,208},{96,224},{112... | collective-permute-start | bytes 983048 | tf_op jit(solution)/shard_map/ppermute | solution.py:16
  59.5 12.5 %collective-permute-start.16 = (bf16[2,80,1280]{2,1,0:T(8,128)(2,1)S(1)}, bf16[2,80,1280]{2,1,0:T(8,128)(2,1)S(1)}, u32[]{:S(2)}, u32[]{:S(2)}) collective-permute-start(bf16[2,80,1280]{2,1,0:T(8,128)(2,1)S(1)} %collective-permute-done.10.refs_10_), channel_id=1, source_target_pairs={{0,48},{16,32},{32,16},{48,0},{64,112},{80,96},{96,80},{112,64},{1... | collective-permute-start | bytes 1228808 | tf_op jit(solution)/shard_map/ppermute | solution.py:16
  60.7 11.3 %collective-permute-start.15 = (bf16[2,80,1280]{2,1,0:T(8,128)(2,1)S(1)}, bf16[2,80,1280]{2,1,0:T(8,128)(2,1)S(1)}, u32[]{:S(2)}, u32[]{:S(2)}) collective-permute-start(bf16[2,80,1280]{2,1,0:T(8,128)(2,1)S(1)} %collective-permute-done.10.refs_10_), channel_id=1, source_target_pairs={{0,16},{16,0},{32,48},{48,32},{64,80},{80,64},{96,112},{112,96},{1... | collective-permute-start | bytes 1228808 | tf_op jit(solution)/shard_map/ppermute | solution.py:16
  60.7 17.2 %collective-permute-start.14 = (bf16[2,80,1280]{2,1,0:T(8,128)(2,1)S(1)}, bf16[2,80,1280]{2,1,0:T(8,128)(2,1)S(1)}, u32[]{:S(2)}, u32[]{:S(2)}) collective-permute-start(bf16[2,80,1280]{2,1,0:T(8,128)(2,1)S(1)} %slice_bitcast_fusion), channel_id=1, source_target_pairs={{0,48},{16,32},{32,16},{48,0},{64,112},{80,96},{96,80},{112,64},{1... | collective-permute-start | bytes 1228808 | tf_op jit(solution)/shard_map/ppermute | solution.py:16
  72.0 9.2 %collective-permute-start.13 = (bf16[2,80,1280]{2,1,0:T(8,128)(2,1)S(1)}, bf16[2,80,1280]{2,1,0:T(8,128)(2,1)S(1)}, u32[]{:S(2)}, u32[]{:S(2)}) collective-permute-start(bf16[2,80,1280]{2,1,0:T(8,128)(2,1)S(1)} %slice_bitcast_fusion.1), channel_id=1, source_target_pairs={{0,16},{16,0},{32,48},{48,32},{64,80},{80,64},{96,112},{112,96},{1... | collective-permute-start | bytes 1228808 | tf_op jit(solution)/shard_map/ppermute | solution.py:16
  72.1 10.3 %collective-permute-start.19 = (bf16[80,1280]{1,0:T(8,128)(2,1)S(1)}, bf16[80,1280]{1,0:T(8,128)(2,1)S(1)}, u32[]{:S(2)}, u32[]{:S(2)}) collective-permute-start(bf16[80,1280]{1,0:T(8,128)(2,1)S(1)} %slice_bitcast_fusion.4), channel_id=1, source_target_pairs={{0,48},{16,32},{32,16},{48,0},{64,112},{80,96},{96,80},{112,64},{1... | collective-permute-start | bytes 614408 | tf_op jit(solution)/shard_map/ppermute | solution.py:16
  73.6 12.0 %collective-permute-start.18 = (bf16[80,1280]{1,0:T(8,128)(2,1)S(1)}, bf16[80,1280]{1,0:T(8,128)(2,1)S(1)}, u32[]{:S(2)}, u32[]{:S(2)}) collective-permute-start(bf16[80,1280]{1,0:T(8,128)(2,1)S(1)} %slice_bitcast_fusion.5), channel_id=1, source_target_pairs={{0,16},{16,0},{32,48},{48,32},{64,80},{80,64},{96,112},{112,96},{1... | collective-permute-start | bytes 614408 | tf_op jit(solution)/shard_map/ppermute | solution.py:16
  74.2 11.3 %collective-permute-start.20 = (bf16[128,1280]{1,0:T(8,128)(2,1)S(1)}, bf16[128,1280]{1,0:T(8,128)(2,1)S(1)}, u32[]{:S(2)}, u32[]{:S(2)}) collective-permute-start(bf16[128,1280]{1,0:T(8,128)(2,1)S(1)} %collective-permute-done.17), channel_id=1, source_target_pairs={{0,64},{16,80},{32,96},{48,112},{64,0},{80,16},{96,32},{112,48},{1... | collective-permute-start | bytes 983048 | tf_op jit(solution)/shard_map/ppermute | solution.py:16
  89.7 5.7 %collective-permute-start.25 = (bf16[64,1280]{1,0:T(8,128)(2,1)S(1)}, bf16[64,1280]{1,0:T(8,128)(2,1)S(1)}, u32[]{:S(2)}, u32[]{:S(2)}) collective-permute-start(bf16[64,1280]{1,0:T(8,128)(2,1)S(1)} %get-tuple-element.90), channel_id=1, source_target_pairs={{0,64},{16,80},{32,96},{48,112},{64,0},{80,16},{96,32},{112,48},{1... | collective-permute-start | bytes 491528 | tf_op jit(solution)/shard_map/ppermute | solution.py:16
  89.8 7.2 %collective-permute-start.26 = (bf16[64,1280]{1,0:T(8,128)(2,1)S(1)}, bf16[64,1280]{1,0:T(8,128)(2,1)S(1)}, u32[]{:S(2)}, u32[]{:S(2)}) collective-permute-start(bf16[64,1280]{1,0:T(8,128)(2,1)S(1)} %get-tuple-element.91), channel_id=1, source_target_pairs={{0,128},{16,144},{32,160},{48,176},{64,192},{80,208},{96,224},{112... | collective-permute-start | bytes 491528 | tf_op jit(solution)/shard_map/ppermute | solution.py:16
  91.9 8.6 %collective-permute-start.27 = (bf16[64,1280]{1,0:T(8,128)(2,1)S(1)}, bf16[64,1280]{1,0:T(8,128)(2,1)S(1)}, u32[]{:S(2)}, u32[]{:S(2)}) collective-permute-start(bf16[64,1280]{1,0:T(8,128)(2,1)S(1)} %get-tuple-element.92), channel_id=1, source_target_pairs={{0,192},{16,208},{32,224},{48,240},{64,128},{80,144},{96,160},{112... | collective-permute-start | bytes 491528 | tf_op jit(solution)/shard_map/ppermute | solution.py:16
  93.4 21.8 %collective-permute-start.22 = (bf16[64,1280]{1,0:T(8,128)(2,1)S(1)}, bf16[64,1280]{1,0:T(8,128)(2,1)S(1)}, u32[]{:S(2)}, u32[]{:S(2)}) collective-permute-start(bf16[64,1280]{1,0:T(8,128)(2,1)S(1)} %get-tuple-element.82), channel_id=1, source_target_pairs={{0,64},{16,80},{32,96},{48,112},{64,0},{80,16},{96,32},{112,48},{1... | collective-permute-start | bytes 491528 | tf_op jit(solution)/shard_map/ppermute | solution.py:16
  93.4 23.3 %collective-permute-start.23 = (bf16[64,1280]{1,0:T(8,128)(2,1)S(1)}, bf16[64,1280]{1,0:T(8,128)(2,1)S(1)}, u32[]{:S(2)}, u32[]{:S(2)}) collective-permute-start(bf16[64,1280]{1,0:T(8,128)(2,1)S(1)} %get-tuple-element.83), channel_id=1, source_target_pairs={{0,128},{16,144},{32,160},{48,176},{64,192},{80,208},{96,224},{112... | collective-permute-start | bytes 491528 | tf_op jit(solution)/shard_map/ppermute | solution.py:16
  95.4 21.3 %collective-permute-start.24 = (bf16[64,1280]{1,0:T(8,128)(2,1)S(1)}, bf16[64,1280]{1,0:T(8,128)(2,1)S(1)}, u32[]{:S(2)}, u32[]{:S(2)}) collective-permute-start(bf16[64,1280]{1,0:T(8,128)(2,1)S(1)} %get-tuple-element.84), channel_id=1, source_target_pairs={{0,192},{16,208},{32,224},{48,240},{64,128},{80,144},{96,160},{112... | collective-permute-start | bytes 491528 | tf_op jit(solution)/shard_map/ppermute | solution.py:16
  102.5 14.2 %collective-permute-start.30 = (f32[8,256]{1,0:T(8,128)S(1)}, f32[8,256]{1,0:T(8,128)S(1)}, u32[]{:S(2)}, u32[]{:S(2)}) collective-permute-start(f32[8,256]{1,0:T(8,128)S(1)} %get-tuple-element.97), channel_id=1, source_target_pairs={{0,3},{1,2},{2,1},{3,0},{4,7},{5,6},{6,5},{7,4},{8,11},{9,10},{10,... | collective-permute-start | bytes 24584 | tf_op jit(solution)/shard_map/ppermute | solution.py:16
  110.4 6.7 %collective-permute-start.29 = (f32[8,256]{1,0:T(8,128)S(1)}, f32[8,256]{1,0:T(8,128)S(1)}, u32[]{:S(2)}, u32[]{:S(2)}) collective-permute-start(f32[8,256]{1,0:T(8,128)S(1)} %get-tuple-element.97), channel_id=1, source_target_pairs={{0,2},{1,3},{2,0},{3,1},{4,6},{5,7},{6,4},{7,5},{8,10},{9,11},{10,... | collective-permute-start | bytes 24584 | tf_op jit(solution)/shard_map/ppermute | solution.py:16
  115.1 2.0 %collective-permute-start.28 = (f32[8,256]{1,0:T(8,128)S(1)}, f32[8,256]{1,0:T(8,128)S(1)}, u32[]{:S(2)}, u32[]{:S(2)}) collective-permute-start(f32[8,256]{1,0:T(8,128)S(1)} %get-tuple-element.97), channel_id=1, source_target_pairs={{0,1},{1,0},{2,3},{3,2},{4,5},{5,4},{6,7},{7,6},{8,9},{9,8},{10,11... | collective-permute-start | bytes 24584 | tf_op jit(solution)/shard_map/ppermute | solution.py:16
  117.1 5.7 %collective-permute-start.33 = (f32[8,256]{1,0:T(8,128)S(1)}, f32[8,256]{1,0:T(8,128)S(1)}, u32[]{:S(2)}, u32[]{:S(2)}) collective-permute-start(f32[8,256]{1,0:T(8,128)S(1)} %add_add_fusion.2), channel_id=1, source_target_pairs={{0,12},{1,13},{2,14},{3,15},{4,8},{5,9},{6,10},{7,11},{8,4},{9,5},... | collective-permute-start | bytes 24584 | tf_op jit(solution)/shard_map/ppermute | solution.py:16
  118.1 4.8 %collective-permute-start.32 = (f32[8,256]{1,0:T(8,128)S(1)}, f32[8,256]{1,0:T(8,128)S(1)}, u32[]{:S(2)}, u32[]{:S(2)}) collective-permute-start(f32[8,256]{1,0:T(8,128)S(1)} %add_add_fusion.2), channel_id=1, source_target_pairs={{0,8},{1,9},{2,10},{3,11},{4,12},{5,13},{6,14},{7,15},{8,0},{9,1},... | collective-permute-start | bytes 24584 | tf_op jit(solution)/shard_map/ppermute | solution.py:16
  119.3 3.5 %collective-permute-start.31 = (f32[8,256]{1,0:T(8,128)S(1)}, f32[8,256]{1,0:T(8,128)S(1)}, u32[]{:S(2)}, u32[]{:S(2)}) collective-permute-start(f32[8,256]{1,0:T(8,128)S(1)} %add_add_fusion.2), channel_id=1, source_target_pairs={{0,4},{1,5},{2,6},{3,7},{4,0},{5,1},{6,2},{7,3},{8,12},{9,13},{10,... | collective-permute-start | bytes 24584 | tf_op jit(solution)/shard_map/ppermute | solution.py:16
  123.0 8.3 %collective-permute-start.34 = (bf16[64,1408]{1,0:T(8,128)(2,1)S(1)}, bf16[64,1408]{1,0:T(8,128)(2,1)S(1)}, u32[]{:S(2)}, u32[]{:S(2)}) collective-permute-start(bf16[64,1408]{1,0:T(8,128)(2,1)S(1)} %get-tuple-element.106), channel_id=1, source_target_pairs={{0,2},{1,3},{2,0},{3,1},{4,6},{5,7},{6,4},{7,5},{8,10},{9,11},{10,... | collective-permute-start | bytes 540680 | tf_op jit(solution)/shard_map/ppermute | solution.py:16
  131.4 21.9 %collective-permute-start.37 = (bf16[2,64,1408]{2,1,0:T(8,128)(2,1)S(1)}, bf16[2,64,1408]{2,1,0:T(8,128)(2,1)S(1)}, u32[]{:S(2)}, u32[]{:S(2)}) collective-permute-start(bf16[2,64,1408]{2,1,0:T(8,128)(2,1)S(1)} %pad_maximum_fusion.7.pair), channel_id=1, source_target_pairs={{0,12},{1,13},{2,14},{3,15},{4,8},{5,9},{6,10},{7,11},{8,4},{9,5},... | collective-permute-start | bytes 1081352 | tf_op jit(solution)/shard_map/ppermute | solution.py:16
  132.5 20.8 %collective-permute-start.36 = (bf16[2,64,1408]{2,1,0:T(8,128)(2,1)S(1)}, bf16[2,64,1408]{2,1,0:T(8,128)(2,1)S(1)}, u32[]{:S(2)}, u32[]{:S(2)}) collective-permute-start(bf16[2,64,1408]{2,1,0:T(8,128)(2,1)S(1)} %pad_maximum_fusion.7.pair), channel_id=1, source_target_pairs={{0,8},{1,9},{2,10},{3,11},{4,12},{5,13},{6,14},{7,15},{8,0},{9,1},... | collective-permute-start | bytes 1081352 | tf_op jit(solution)/shard_map/ppermute | solution.py:16
  133.6 19.7 %collective-permute-start.35 = (bf16[2,64,1408]{2,1,0:T(8,128)(2,1)S(1)}, bf16[2,64,1408]{2,1,0:T(8,128)(2,1)S(1)}, u32[]{:S(2)}, u32[]{:S(2)}) collective-permute-start(bf16[2,64,1408]{2,1,0:T(8,128)(2,1)S(1)} %pad_maximum_fusion.7.pair), channel_id=1, source_target_pairs={{0,4},{1,5},{2,6},{3,7},{4,0},{5,1},{6,2},{7,3},{8,12},{9,13},{10,... | collective-permute-start | bytes 1081352 | tf_op jit(solution)/shard_map/ppermute | solution.py:16
  134.8 11.6 %collective-permute-start.38 = (f32[8,1280]{1,0:T(8,128)S(1)}, f32[8,1280]{1,0:T(8,128)S(1)}, u32[]{:S(2)}, u32[]{:S(2)}) collective-permute-start(f32[8,1280]{1,0:T(8,128)S(1)} %convolution_bitcast_fusion), channel_id=1, source_target_pairs={{0,64},{16,80},{32,96},{48,112},{64,0},{80,16},{96,32},{112,48},{1... | collective-permute-start | bytes 122888 | tf_op jit(solution)/shard_map/ppermute | solution.py:16
  146.4 4.0 %collective-permute-start.39 = (f32[8,1280]{1,0:T(8,128)S(1)}, f32[8,1280]{1,0:T(8,128)S(1)}, u32[]{:S(2)}, u32[]{:S(2)}) collective-permute-start(f32[8,1280]{1,0:T(8,128)S(1)} %add.72), channel_id=1, source_target_pairs={{0,128},{16,144},{32,160},{48,176},{64,192},{80,208},{96,224},{112... | collective-permute-start | bytes 122888 | tf_op jit(solution)/shard_map/ppermute | solution.py:16
  150.5 2.9 %collective-permute-start.40 = (f32[8,1280]{1,0:T(8,128)S(1)}, f32[8,1280]{1,0:T(8,128)S(1)}, u32[]{:S(2)}, u32[]{:S(2)}) collective-permute-start(f32[8,1280]{1,0:T(8,128)S(1)} %add.73), channel_id=1, source_target_pairs={{0,16},{16,0},{32,48},{48,32},{64,80},{80,64},{96,112},{112,96},{1... | collective-permute-start | bytes 122888 | tf_op jit(solution)/shard_map/ppermute | solution.py:16
  154.6 10.7 %collective-permute-start.41 = (f32[128,1280]{1,0:T(8,128)S(1)}, f32[128,1280]{1,0:T(8,128)S(1)}, u32[]{:S(2)}, u32[]{:S(2)}) collective-permute-start(f32[128,1280]{1,0:T(8,128)S(1)} %get-tuple-element.114), channel_id=1, source_target_pairs={{0,1},{1,0},{2,3},{3,2},{4,5},{5,4},{6,7},{7,6},{8,9},{9,8},{10,11... | collective-permute-start | bytes 1966088 | tf_op jit(solution)/shard_map/ppermute | solution.py:16
  160.3 4.4 %collective-permute-start.42 = (f32[8,1280]{1,0:T(8,128)S(1)}, f32[8,1280]{1,0:T(8,128)S(1)}, u32[]{:S(2)}, u32[]{:S(2)}) collective-permute-start(f32[8,1280]{1,0:T(8,128)S(1)} %add.74), channel_id=1, source_target_pairs={{0,32},{16,48},{32,0},{48,16},{64,96},{80,112},{96,64},{112,80},{1... | collective-permute-start | bytes 122888 | tf_op jit(solution)/shard_map/ppermute | solution.py:16

commit v14 on v12

--- a/solution.py
+++ b/solution.py
@@ -230,9 +230,10 @@
     )(back, part, combine, mix, grad)
 
 
-def tokens_kernel(spread, pair, one, two, three, table, mine, theirs):
+def tokens_kernel(spread, table, *refs):
+    mine, theirs = refs[8:]
     half, width = mine.shape
-    pieces = [ref[...].reshape(2 * ref.shape[1], ref.shape[2]) for ref in (pair, one, two, three)]
+    pieces = [jnp.concatenate([near[...], far[...]], axis=0) for near, far in zip(refs[:4], refs[4:8])]
     depth = pieces[0].shape[0]
     count = pieces[0].shape[1] - width
     grads = jnp.concatenate([piece[:, width:] for piece in pieces], axis=0)
@@ -260,17 +261,17 @@
     theirs[...] = sums[half:]
 
 
-def tokens_call(spread, pieces, table):
+def tokens_call(spread, table, pieces):
     vmem = pl.BlockSpec(memory_space=pltpu.VMEM)
     half, width = spread.shape[1], table.shape[1]
     return pl.pallas_call(
         tokens_kernel,
         out_shape=[jax.ShapeDtypeStruct((half, width), F32)] * 2,
-        in_specs=[vmem] * 6,
+        in_specs=[vmem] * 10,
         out_specs=[vmem] * 2,
         compiler_params=pltpu.CompilerParams(vmem_limit_bytes=24 * 2**20),
         name="token_grad",
-    )(spread, *pieces, table)
+    )(spread, table, *pieces)
 
 
 def after(value, *earlier):
@@ -368,18 +369,19 @@
     (back,) = against([slot_in_grad], tokens, dispatch, True)
     near, send, logit_grad_b = pack_call(back, part, combine, mix, slot_in_grad)
     far = swap(send, "expert", 2)
+    nears = all_x(near)
     term = jnp.einsum(
         "bsm,bmd->sd", logit_grad_b.reshape(images, own, count), tokens, preferred_element_type=F32
     )
     term = summed(term, "dp", 4)
     term, far = together(term, far)
-    pieces = all_x(jnp.stack([near, far]))
+    fars = all_x(far)
+    *nears, term = together(*nears, term)
     term = summed(term, "dp", 8, 1)
-    last = swap(term, "dp", 2)
-    slot_grad = (term + last).T
-
-    pieces[1] = after(pieces[1], last)
-    mine, theirs = tokens_call(spread, pieces, table)
+    fars[0] = after(fars[0], term)
+    slot_grad = summed(after(term, *fars[1:]), "dp", 2).T
+
+    mine, theirs = tokens_call(spread, table, nears + fars)
     token_grad = (mine + swap(theirs, "expert", 1)).astype(BF16)
     return (token_grad.reshape(images, -1, width), slot_grad)
 

time: 166 us -> 166 us (level)
  starting transfers between devices: 76 us -> 80 us
  waiting for transfers between devices: 65.8 us -> 63 us
    ppermute x43 -> x46, starting transfers between devices: 76 us -> 80 us  [swap(): return lax.ppermute(value, axis, [(i, i ^ k) for i in range(count)])]
    ppermute x43 -> x46, waiting for transfers between devices: 65.8 us -> 63 us  [swap(): return lax.ppermute(value, axis, [(i, i ^ k) for i in range(count)])]
  transfers between devices with their start and end apart: 43 -> 46, of which waited for: 19 -> 19; matrix products, arithmetic and copies ran while one was open for 2% -> 2% of each run, Pallas kernels for 7% -> 7%
where the time goes in v14:
time: 166 us
  starting transfers between devices  80 us (48%)
  waiting for transfers between devices  63 us (38%)
  Pallas kernels  16.8 us (10%)
  other arithmetic  1.89 us (1%)
  local copies, waits for them, and re-layouts  1.76 us (1%)
    ppermute x46, starting transfers between devices, swap(): return lax.ppermute(value, axis, [(i, i ^ k) for i in range(count)])  80 us
    ppermute x46, waiting for transfers between devices, swap(): return lax.ppermute(value, axis, [(i, i ^ k) for i in range(count)])  63 us
    pallas_call x1, Pallas kernels, slots_call(): pl.pallas_call(slots_kernel, grid=(images // 2,), out_shape=[jax.ShapeDty...  6.63 us
    pallas_call x2, Pallas kernels, against(): pl.pallas_call(lambda *refs: against_kernel(over_tokens, len(parts), *ref...  4.32 us
    pallas_call x1, Pallas kernels, ffn(): pl.pallas_call(ffn_kernel, out_shape=[jax.ShapeDtypeStruct((own_rows, wid...  4.04 us
  transfers between devices with their start and end apart: 46, of which 19 were waited for; matrix products, arithmetic and copies ran while one was open for 2% of the time, Pallas kernels for 7%

profile of v14, /device:TPU:1, one launch (start us, length us, event | category | flops | bytes accessed | tf_op | source)
XLA Modules:
  0.0 166.0 jit_solution(4447587279113415954)
XLA Ops:
  0.7 1.4 dynamic-slice_bitcast_fusion.1
  2.3 2.2 %collective-permute-start.4 = (bf16[2,80,1280]{2,1,0:T(8,128)(2,1)S(1)}, bf16[2,80,1280]{2,1,0:T(8,128)(2,1)S(1)}, u32[]{:S(2)}, u32[]{:S(2)}) collective-permute-start(bf16[2,80,1280]{2,1,0:T(8,128)(2,1)S(1)} %pad_maximum_fusion.3.refs_0_), channel_id=1, source_target_pairs={{0,16},{16,0},{32,48},{48,32},{64,80},{80,64},{96,112},{112,96},{1... | collective-permute-start | bytes 1228808 | tf_op jit(solution)/shard_map/ppermute | solution.py:16
  4.5 1.9 %collective-permute-start.2 = (bf16[2,80,1280]{2,1,0:T(8,128)(2,1)S(1)}, bf16[2,80,1280]{2,1,0:T(8,128)(2,1)S(1)}, u32[]{:S(2)}, u32[]{:S(2)}) collective-permute-start(bf16[2,80,1280]{2,1,0:T(8,128)(2,1)S(1)} %pad_maximum_fusion.3.refs_0_), channel_id=1, source_target_pairs={{0,48},{16,32},{32,16},{48,0},{64,112},{80,96},{96,80},{112,64},{1... | collective-permute-start | bytes 1228808 | tf_op jit(solution)/shard_map/ppermute | solution.py:16
  6.4 6.9 %collective-permute-start = (bf16[8,1280]{1,0:T(8,128)(2,1)S(1)}, bf16[8,1280]{1,0:T(8,128)(2,1)S(1)}, u32[]{:S(2)}, u32[]{:S(2)}) collective-permute-start(bf16[8,1280]{1,0:T(8,128)(2,1)S(1)} %bitcast.57), channel_id=1, source_target_pairs={{0,2},{1,3},{2,0},{3,1},{4,6},{5,7},{6,4},{7,5},{8,10},{9,11},{10,... | collective-permute-start | bytes 61448 | tf_op jit(solution)/shard_map/ppermute | solution.py:16
  13.3 1.3 collective-permute-start.7
  14.6 0.8 collective-permute-start.6
  15.5 1.3 collective-permute-start.1
  16.9 0.9 collective-permute-start.5
  17.8 0.6 collective-permute-done.1
  18.5 15.7 %collective-permute-done.7 = bf16[2,80,1280]{2,1,0:T(8,128)(2,1)S(1)} collective-permute-done((bf16[2,80,1280]{2,1,0:T(8,128)(2,1)S(1)}, bf16[2,80,1280]{2,1,0:T(8,128)(2,1)S(1)}, u32[]{:S(2)}, u32[]{:S(2)}) %collective-permute-start.7) | collective-permute-done | bytes 409632 | tf_op jit(solution)/shard_map/ppermute | solution.py:16
  34.2 2.8 %collective-permute-start.11 = (bf16[32,1280]{1,0:T(8,128)(2,1)S(1)}, bf16[32,1280]{1,0:T(8,128)(2,1)S(1)}, u32[]{:S(2)}, u32[]{:S(2)}) collective-permute-start(bf16[32,1280]{1,0:T(8,128)(2,1)S(1)} %pad_maximum_fusion.9), channel_id=1, source_target_pairs={{0,8},{1,9},{2,10},{3,11},{4,12},{5,13},{6,14},{7,15},{8,0},{9,1},... | collective-permute-start | bytes 245768 | tf_op jit(solution)/shard_map/ppermute | solution.py:16
  37.2 0.9 collective-permute-start.9
  38.0 2.0 %collective-permute-start.10 = (bf16[2,80,1280]{2,1,0:T(8,128)(2,1)S(1)}, bf16[2,80,1280]{2,1,0:T(8,128)(2,1)S(1)}, u32[]{:S(2)}, u32[]{:S(2)}) collective-permute-start(bf16[2,80,1280]{2,1,0:T(8,128)(2,1)S(1)} %pad_maximum_fusion.6), channel_id=1, source_target_pairs={{0,192},{16,208},{32,224},{48,240},{64,128},{80,144},{96,160},{112... | collective-permute-start | bytes 1228808 | tf_op jit(solution)/shard_map/ppermute | solution.py:16
  40.1 1.7 %collective-permute-start.12 = (bf16[64,1280]{1,0:T(8,128)(2,1)S(1)}, bf16[64,1280]{1,0:T(8,128)(2,1)S(1)}, u32[]{:S(2)}, u32[]{:S(2)}) collective-permute-start(bf16[64,1280]{1,0:T(8,128)(2,1)S(1)} %pad_maximum_fusion.8), channel_id=1, source_target_pairs={{0,1},{1,0},{2,3},{3,2},{4,5},{5,4},{6,7},{7,6},{8,9},{9,8},{10,11... | collective-permute-start | bytes 491528 | tf_op jit(solution)/shard_map/ppermute | solution.py:16
  41.7 1.0 collective-permute-done.12
  42.8 6.6 %slots.1 = (bf16[64,1280]{1,0:T(8,128)(2,1)S(1)}, f32[64,256]{1,0:T(8,128)S(1)}, f32[64,256]{1,0:T(8,128)S(1)}, bf16[8,64,256]{2,1,0:T(8,128)(2,1)S(1)}) custom-call(bf16[128,1280]{1,0:T(8,128)(2,1)S(1)} %constant_dynamic-update-slice_fusion.table, bf16[8,256,1280]{2,1,0:T(8,128)(2,1)S(1)} %copy-done), custom_call_target="tpu_custom_call" | custom-call | flops 754974720 | bytes 5242880 | tf_op jit(solution)/shard_map/slots/pallas_call | solution.py:102
  49.4 0.8 fusion
  50.2 0.4 spread.1
  50.7 6.1 %collective-permute-done.9.refs_7_ = bf16[2,2,80,1280]{3,2,1,0:T(8,128)(2,1)S(1)} collective-permute-done((bf16[2,2,80,1280]{3,2,1,0:T(8,128)(2,1)S(1)}, bf16[2,2,80,1280]{3,2,1,0:T(8,128)(2,1)S(1)}, u32[]{:S(2)}, u32[]{:S(2)}) %collective-permute-start.9) | collective-permute-done | bytes 819232 | tf_op jit(solution)/shard_map/ppermute | solution.py:16
  56.8 2.7 %collective-permute-start.17 = (bf16[128,1280]{1,0:T(8,128)(2,1)S(1)}, bf16[128,1280]{1,0:T(8,128)(2,1)S(1)}, u32[]{:S(2)}, u32[]{:S(2)}) collective-permute-start(bf16[128,1280]{1,0:T(8,128)(2,1)S(1)} %pad_maximum_fusion.7), channel_id=1, source_target_pairs={{0,128},{16,144},{32,160},{48,176},{64,192},{80,208},{96,224},{112... | collective-permute-start | bytes 983048 | tf_op jit(solution)/shard_map/ppermute | solution.py:16
  59.5 1.2 collective-permute-start.16
  60.7 1.8 %collective-permute-start.14 = (bf16[2,80,1280]{2,1,0:T(8,128)(2,1)S(1)}, bf16[2,80,1280]{2,1,0:T(8,128)(2,1)S(1)}, u32[]{:S(2)}, u32[]{:S(2)}) collective-permute-start(bf16[2,80,1280]{2,1,0:T(8,128)(2,1)S(1)} %slice_bitcast_fusion), channel_id=1, source_target_pairs={{0,48},{16,32},{32,16},{48,0},{64,112},{80,96},{96,80},{112,64},{1... | collective-permute-start | bytes 1228808 | tf_op jit(solution)/shard_map/ppermute | solution.py:16
  62.5 9.4 %collective-permute-done.21 = bf16[128,1280]{1,0:T(8,128)(2,1)S(1)} collective-permute-done((bf16[128,1280]{1,0:T(8,128)(2,1)S(1)}, bf16[128,1280]{1,0:T(8,128)(2,1)S(1)}, u32[]{:S(2)}, u32[]{:S(2)}) %collective-permute-start.21) | collective-permute-done | bytes 327712 | tf_op jit(solution)/shard_map/ppermute | solution.py:16
  72.1 1.5 collective-permute-start.19
  73.6 0.6 collective-permute-start.18
  74.2 3.7 %collective-permute-done.14.refs_9_ = bf16[2,80,1280]{2,1,0:T(8,128)(2,1)S(1)} collective-permute-done((bf16[2,80,1280]{2,1,0:T(8,128)(2,1)S(1)}, bf16[2,80,1280]{2,1,0:T(8,128)(2,1)S(1)}, u32[]{:S(2)}, u32[]{:S(2)}) %collective-permute-start.14) | collective-permute-done | bytes 409632 | tf_op jit(solution)/shard_map/ppermute | solution.py:16
  77.9 3.2 %collective-permute-done.13.refs_8_ = bf16[2,80,1280]{2,1,0:T(8,128)(2,1)S(1)} collective-permute-done((bf16[2,80,1280]{2,1,0:T(8,128)(2,1)S(1)}, bf16[2,80,1280]{2,1,0:T(8,128)(2,1)S(1)}, u32[]{:S(2)}, u32[]{:S(2)}) %collective-permute-start.13) | collective-permute-done | bytes 409632 | tf_op jit(solution)/shard_map/ppermute | solution.py:16
  81.2 1.2 collective-permute-done.19.refs_14_
  82.3 3.2 %collective-permute-done.18.refs_13_ = bf16[80,1280]{1,0:T(8,128)(2,1)S(1)} collective-permute-done((bf16[80,1280]{1,0:T(8,128)(2,1)S(1)}, bf16[80,1280]{1,0:T(8,128)(2,1)S(1)}, u32[]{:S(2)}, u32[]{:S(2)}) %collective-permute-start.18) | collective-permute-done | bytes 204832 | tf_op jit(solution)/shard_map/ppermute | solution.py:16
  85.7 4.0 %ffn.1 = (f32[64,1280]{1,0:T(8,128)S(1)}, bf16[64,1280]{1,0:T(8,128)(2,1)S(1)}, bf16[64,1280]{1,0:T(8,128)(2,1)S(1)}, bf16[64,1280]{1,0:T(8,128)(2,1)S(1)}, f32[...) custom-call(bf16[256,1280]{1,0:T(8,128)(2,1)S(1)} %get-tuple-element, ...), custom_call_target="tpu_custom_call" | custom-call | tf_op jit(solution)/shard_map/ffn/pallas_call | solution.py:61
  89.8 2.1 %collective-permute-start.26 = (bf16[64,1280]{1,0:T(8,128)(2,1)S(1)}, bf16[64,1280]{1,0:T(8,128)(2,1)S(1)}, u32[]{:S(2)}, u32[]{:S(2)}) collective-permute-start(bf16[64,1280]{1,0:T(8,128)(2,1)S(1)} %get-tuple-element.99), channel_id=1, source_target_pairs={{0,128},{16,144},{32,160},{48,176},{64,192},{80,208},{96,224},{112... | collective-permute-start | bytes 491528 | tf_op jit(solution)/shard_map/ppermute | solution.py:16
  91.9 1.5 collective-permute-start.27
  93.4 2.1 %collective-permute-start.23 = (bf16[64,1280]{1,0:T(8,128)(2,1)S(1)}, bf16[64,1280]{1,0:T(8,128)(2,1)S(1)}, u32[]{:S(2)}, u32[]{:S(2)}) collective-permute-start(bf16[64,1280]{1,0:T(8,128)(2,1)S(1)} %get-tuple-element.91), channel_id=1, source_target_pairs={{0,128},{16,144},{32,160},{48,176},{64,192},{80,208},{96,224},{112... | collective-permute-start | bytes 491528 | tf_op jit(solution)/shard_map/ppermute | solution.py:16
  95.4 1.5 collective-permute-start.24
  97.0 3.5 %collective-permute-done.27.refs_3_ = bf16[64,1280]{1,0:T(8,128)(2,1)S(1)} collective-permute-done((bf16[64,1280]{1,0:T(8,128)(2,1)S(1)}, bf16[64,1280]{1,0:T(8,128)(2,1)S(1)}, u32[]{:S(2)}, u32[]{:S(2)}) %collective-permute-start.27) | collective-permute-done | bytes 163872 | tf_op jit(solution)/shard_map/ppermute | solution.py:16
  100.5 2.0 %combine_grad.1 = (f32[64,256]{1,0:T(8,128)S(1)}, f32[8,256]{1,0:T(8,128)S(1)}) custom-call(f32[64,1280]{1,0:T(8,128)S(1)} %get-tuple-element.97.refs_0_, bf16[64,1280]{1,0:T(8,128)(2,1)S(1)} %collective-permute-done.25.refs_1_, bf16[64,1280]{1,0:T(8,128)(2,1)S(1)} %collective-permute-done.26.refs_2_, bf16[64,1280]{1,0:T(8,128)(2,1)S(1)} %collective-permute-done.27.refs_3_, ...), custom_call_target="tpu_custom_call" | custom-call | tf_op jit(solution)/shard_map/combine_grad/pallas_call | solution.py:188
  102.5 7.9 %collective-permute-start.30 = (f32[8,256]{1,0:T(8,128)S(1)}, f32[8,256]{1,0:T(8,128)S(1)}, u32[]{:S(2)}, u32[]{:S(2)}) collective-permute-start(f32[8,256]{1,0:T(8,128)S(1)} %get-tuple-element.105), channel_id=1, source_target_pairs={{0,3},{1,2},{2,1},{3,0},{4,7},{5,6},{6,5},{7,4},{8,11},{9,10},{10,... | collective-permute-start | bytes 24584 | tf_op jit(solution)/shard_map/ppermute | solution.py:16
  110.4 4.8 %collective-permute-start.29 = (f32[8,256]{1,0:T(8,128)S(1)}, f32[8,256]{1,0:T(8,128)S(1)}, u32[]{:S(2)}, u32[]{:S(2)}) collective-permute-start(f32[8,256]{1,0:T(8,128)S(1)} %get-tuple-element.105), channel_id=1, source_target_pairs={{0,2},{1,3},{2,0},{3,1},{4,6},{5,7},{6,4},{7,5},{8,10},{9,11},{10,... | collective-permute-start | bytes 24584 | tf_op jit(solution)/shard_map/ppermute | solution.py:16
  115.1 1.6 collective-permute-done.23
  117.1 0.9 collective-permute-start.33
  118.1 1.3 collective-permute-start.32
  119.3 1.1 collective-permute-start.31
  120.5 2.3 %dispatch_grad.1.back = f32[64,256]{1,0:T(8,128)S(1)} custom-call(f32[64,1280]{1,0:T(8,128)S(1)} %add_add_fusion.refs_0_.grad, bf16[8,256,1280]{2,1,0:T(8,128)(2,1)S(1)} %copy-done, f32[64,256]{1,0:T(8,128)S(1)} %get-tuple-element.96.refs_2_), custom_call_target="tpu_custom_call" | custom-call | tf_op jit(solution)/shard_map/dispatch_grad/pallas_call | solution.py:188
  123.0 1.1 collective-permute-start.36
  124.1 1.1 collective-permute-start.35
  125.2 1.1 collective-permute-start.34
  126.4 4.5 %collective-permute-start.38 = (bf16[64,1408]{1,0:T(8,128)(2,1)S(1)}, bf16[64,1408]{1,0:T(8,128)(2,1)S(1)}, u32[]{:S(2)}, u32[]{:S(2)}) collective-permute-start(bf16[64,1408]{1,0:T(8,128)(2,1)S(1)} %get-tuple-element.117), channel_id=1, source_target_pairs={{0,2},{1,3},{2,0},{3,1},{4,6},{5,7},{6,4},{7,5},{8,10},{9,11},{10,... | collective-permute-start | bytes 540680 | tf_op jit(solution)/shard_map/ppermute | solution.py:16
  130.9 0.8 convolution_bitcast_fusion
  131.7 9.5 %collective-permute-start.37 = (f32[8,1280]{1,0:T(8,128)S(1)}, f32[8,1280]{1,0:T(8,128)S(1)}, u32[]{:S(2)}, u32[]{:S(2)}) collective-permute-start(f32[8,1280]{1,0:T(8,128)S(1)} %convolution_bitcast_fusion), channel_id=1, source_target_pairs={{0,64},{16,80},{32,96},{48,112},{64,0},{80,16},{96,32},{112,48},{1... | collective-permute-start | bytes 122888 | tf_op jit(solution)/shard_map/ppermute | solution.py:16
  141.1 3.6 %collective-permute-done.37 = f32[8,1280]{1,0:T(8,128)S(1)} collective-permute-done((f32[8,1280]{1,0:T(8,128)S(1)}, f32[8,1280]{1,0:T(8,128)S(1)}, u32[]{:S(2)}, u32[]{:S(2)}) %collective-permute-start.37) | collective-permute-done | bytes 40992 | tf_op jit(solution)/shard_map/ppermute | solution.py:16
  144.8 1.7 %collective-permute-start.43 = (bf16[64,1408]{1,0:T(8,128)(2,1)S(1)}, bf16[64,1408]{1,0:T(8,128)(2,1)S(1)}, u32[]{:S(2)}, u32[]{:S(2)}) collective-permute-start(bf16[64,1408]{1,0:T(8,128)(2,1)S(1)} %collective-permute-done.38.refs_4_), channel_id=1, source_target_pairs={{0,12},{1,13},{2,14},{3,15},{4,8},{5,9},{6,10},{7,11},{8,4},{9,5},... | collective-permute-start | bytes 540680 | tf_op jit(solution)/shard_map/ppermute | solution.py:16
  146.5 1.1 collective-permute-start.42
  147.6 0.5 collective-permute-start.41
  148.2 2.5 %collective-permute-start.39 = (f32[8,1280]{1,0:T(8,128)S(1)}, f32[8,1280]{1,0:T(8,128)S(1)}, u32[]{:S(2)}, u32[]{:S(2)}) collective-permute-start(f32[8,1280]{1,0:T(8,128)S(1)} %add.72), channel_id=1, source_target_pairs={{0,128},{16,144},{32,160},{48,176},{64,192},{80,208},{96,224},{112... | collective-permute-start | bytes 122888 | tf_op jit(solution)/shard_map/ppermute | solution.py:16
  150.7 1.7 %collective-permute-done.39 = f32[8,1280]{1,0:T(8,128)S(1)} collective-permute-done((f32[8,1280]{1,0:T(8,128)S(1)}, f32[8,1280]{1,0:T(8,128)S(1)}, u32[]{:S(2)}, u32[]{:S(2)}) %collective-permute-start.39) | collective-permute-done | bytes 40992 | tf_op jit(solution)/shard_map/ppermute | solution.py:16
  152.6 2.8 %collective-permute-done.40 = f32[8,1280]{1,0:T(8,128)S(1)} collective-permute-done((f32[8,1280]{1,0:T(8,128)S(1)}, f32[8,1280]{1,0:T(8,128)S(1)}, u32[]{:S(2)}, u32[]{:S(2)}) %collective-permute-start.40) | collective-permute-done | bytes 40992 | tf_op jit(solution)/shard_map/ppermute | solution.py:16
  155.5 0.8 collective-permute-done.43.refs_7_
  156.3 0.7 collective-permute-done.41.refs_5_
  157.0 1.2 token_grad.1
  158.2 2.0 %collective-permute-start.44 = (f32[128,1280]{1,0:T(8,128)S(1)}, f32[128,1280]{1,0:T(8,128)S(1)}, u32[]{:S(2)}, u32[]{:S(2)}) collective-permute-start(f32[128,1280]{1,0:T(8,128)S(1)} %get-tuple-element.130), channel_id=1, source_target_pairs={{0,1},{1,0},{2,3},{3,2},{4,5},{5,4},{6,7},{7,6},{8,9},{9,8},{10,11... | collective-permute-start | bytes 1966088 | tf_op jit(solution)/shard_map/ppermute | solution.py:16
  160.2 0.9 collective-permute-start.45
  161.1 3.5 %collective-permute-done.45 = f32[8,1280]{1,0:T(8,128)S(1)} collective-permute-done((f32[8,1280]{1,0:T(8,128)S(1)}, f32[8,1280]{1,0:T(8,128)S(1)}, u32[]{:S(2)}, u32[]{:S(2)}) %collective-permute-start.45) | collective-permute-done | bytes 40992 | tf_op jit(solution)/shard_map/ppermute | solution.py:16
  164.6 0.6 add_bitcast_fusion
  165.2 0.8 add_convert_fusion
  (78 shorter events, 2.1 us)
Async XLA Ops:
  0.6 1.5 copy-start.2
  2.1 4.2 %copy-start.3 = (bf16[1280,8]{0,1:T(8,128)(2,1)S(1)}, bf16[1280,8]{0,1:T(8,128)(2,1)}, u32[]{:S(2)}) copy-start(bf16[1280,8]{0,1:T(8,128)(2,1)} %param.7) | copy-start | bytes 61444
  2.3 14.6 %collective-permute-start.4 = (bf16[2,80,1280]{2,1,0:T(8,128)(2,1)S(1)}, bf16[2,80,1280]{2,1,0:T(8,128)(2,1)S(1)}, u32[]{:S(2)}, u32[]{:S(2)}) collective-permute-start(bf16[2,80,1280]{2,1,0:T(8,128)(2,1)S(1)} %pad_maximum_fusion.3.refs_0_), channel_id=1, source_target_pairs={{0,16},{16,0},{32,48},{48,32},{64,80},{80,64},{96,112},{112,96},{1... | collective-permute-start | bytes 1228808 | tf_op jit(solution)/shard_map/ppermute | solution.py:16
  4.5 13.3 %collective-permute-start.2 = (bf16[2,80,1280]{2,1,0:T(8,128)(2,1)S(1)}, bf16[2,80,1280]{2,1,0:T(8,128)(2,1)S(1)}, u32[]{:S(2)}, u32[]{:S(2)}) collective-permute-start(bf16[2,80,1280]{2,1,0:T(8,128)(2,1)S(1)} %pad_maximum_fusion.3.refs_0_), channel_id=1, source_target_pairs={{0,48},{16,32},{32,16},{48,0},{64,112},{80,96},{96,80},{112,64},{1... | collective-permute-start | bytes 1228808 | tf_op jit(solution)/shard_map/ppermute | solution.py:16
  6.4 9.1 %collective-permute-start = (bf16[8,1280]{1,0:T(8,128)(2,1)S(1)}, bf16[8,1280]{1,0:T(8,128)(2,1)S(1)}, u32[]{:S(2)}, u32[]{:S(2)}) collective-permute-start(bf16[8,1280]{1,0:T(8,128)(2,1)S(1)} %bitcast.57), channel_id=1, source_target_pairs={{0,2},{1,3},{2,0},{3,1},{4,6},{5,7},{6,4},{7,5},{8,10},{9,11},{10,... | collective-permute-start | bytes 61448 | tf_op jit(solution)/shard_map/ppermute | solution.py:16
  13.3 20.9 %collective-permute-start.7 = (bf16[2,80,1280]{2,1,0:T(8,128)(2,1)S(1)}, bf16[2,80,1280]{2,1,0:T(8,128)(2,1)S(1)}, u32[]{:S(2)}, u32[]{:S(2)}) collective-permute-start(bf16[2,80,1280]{2,1,0:T(8,128)(2,1)S(1)} %pad_maximum_fusion.5), channel_id=1, source_target_pairs={{0,128},{16,144},{32,160},{48,176},{64,192},{80,208},{96,224},{112... | collective-permute-start | bytes 1228808 | tf_op jit(solution)/shard_map/ppermute | solution.py:16
  14.6 28.2 %copy-start = (bf16[8,256,1280]{2,1,0:T(8,128)(2,1)S(1)}, bf16[8,256,1280]{2,1,0:T(8,128)(2,1)}, u32[]{:S(2)}) copy-start(bf16[8,256,1280]{2,1,0:T(8,128)(2,1)} %refs_1_.1) | copy-start | bytes 15728644
  14.6 19.6 %collective-permute-start.6 = (bf16[2,80,1280]{2,1,0:T(8,128)(2,1)S(1)}, bf16[2,80,1280]{2,1,0:T(8,128)(2,1)S(1)}, u32[]{:S(2)}, u32[]{:S(2)}) collective-permute-start(bf16[2,80,1280]{2,1,0:T(8,128)(2,1)S(1)} %pad_maximum_fusion.4), channel_id=1, source_target_pairs={{0,64},{16,80},{32,96},{48,112},{64,0},{80,16},{96,32},{112,48},{1... | collective-permute-start | bytes 1228808 | tf_op jit(solution)/shard_map/ppermute | solution.py:16
  15.5 2.9 %collective-permute-start.1 = (bf16[16,1280]{1,0:T(8,128)(2,1)S(1)}, bf16[16,1280]{1,0:T(8,128)(2,1)S(1)}, u32[]{:S(2)}, u32[]{:S(2)}) collective-permute-start(bf16[16,1280]{1,0:T(8,128)(2,1)S(1)} %pad_maximum_fusion.10), channel_id=1, source_target_pairs={{0,4},{1,5},{2,6},{3,7},{4,0},{5,1},{6,2},{7,3},{8,12},{9,13},{10,... | collective-permute-start | bytes 122888 | tf_op jit(solution)/shard_map/ppermute | solution.py:16
  16.9 17.4 %collective-permute-start.5 = (bf16[80,1280]{1,0:T(8,128)(2,1)S(1)}, bf16[80,1280]{1,0:T(8,128)(2,1)S(1)}, u32[]{:S(2)}, u32[]{:S(2)}) collective-permute-start(bf16[80,1280]{1,0:T(8,128)(2,1)S(1)} %slice_bitcast_fusion.2), channel_id=1, source_target_pairs={{0,48},{16,32},{32,16},{48,0},{64,112},{80,96},{96,80},{112,64},{1... | collective-permute-start | bytes 614408 | tf_op jit(solution)/shard_map/ppermute | solution.py:16
  17.7 16.5 %collective-permute-start.3 = (bf16[80,1280]{1,0:T(8,128)(2,1)S(1)}, bf16[80,1280]{1,0:T(8,128)(2,1)S(1)}, u32[]{:S(2)}, u32[]{:S(2)}) collective-permute-start(bf16[80,1280]{1,0:T(8,128)(2,1)S(1)} %slice_bitcast_fusion.3), channel_id=1, source_target_pairs={{0,16},{16,0},{32,48},{48,32},{64,80},{80,64},{96,112},{112,96},{1... | collective-permute-start | bytes 614408 | tf_op jit(solution)/shard_map/ppermute | solution.py:16
  34.2 5.8 %collective-permute-start.11 = (bf16[32,1280]{1,0:T(8,128)(2,1)S(1)}, bf16[32,1280]{1,0:T(8,128)(2,1)S(1)}, u32[]{:S(2)}, u32[]{:S(2)}) collective-permute-start(bf16[32,1280]{1,0:T(8,128)(2,1)S(1)} %pad_maximum_fusion.9), channel_id=1, source_target_pairs={{0,8},{1,9},{2,10},{3,11},{4,12},{5,13},{6,14},{7,15},{8,0},{9,1},... | collective-permute-start | bytes 245768 | tf_op jit(solution)/shard_map/ppermute | solution.py:16
  37.2 19.7 %collective-permute-start.9 = (bf16[2,2,80,1280]{3,2,1,0:T(8,128)(2,1)S(1)}, bf16[2,2,80,1280]{3,2,1,0:T(8,128)(2,1)S(1)}, u32[]{:S(2)}, u32[]{:S(2)}) collective-permute-start(bf16[2,2,80,1280]{3,2,1,0:T(8,128)(2,1)S(1)} %pad_maximum_fusion.refs_5_), channel_id=1, source_target_pairs={{0,48},{16,32},{32,16},{48,0},{64,112},{80,96},{96,80},{112,64},{1... | collective-permute-start | bytes 2457608 | tf_op jit(solution)/shard_map/ppermute | solution.py:16
  38.0 18.8 %collective-permute-start.8 = (bf16[2,2,80,1280]{3,2,1,0:T(8,128)(2,1)S(1)}, bf16[2,2,80,1280]{3,2,1,0:T(8,128)(2,1)S(1)}, u32[]{:S(2)}, u32[]{:S(2)}) collective-permute-start(bf16[2,2,80,1280]{3,2,1,0:T(8,128)(2,1)S(1)} %pad_maximum_fusion.refs_5_), channel_id=1, source_target_pairs={{0,16},{16,0},{32,48},{48,32},{64,80},{80,64},{96,112},{112,96},{1... | collective-permute-start | bytes 2457608 | tf_op jit(solution)/shard_map/ppermute | solution.py:16
  38.0 12.6 %collective-permute-start.10 = (bf16[2,80,1280]{2,1,0:T(8,128)(2,1)S(1)}, bf16[2,80,1280]{2,1,0:T(8,128)(2,1)S(1)}, u32[]{:S(2)}, u32[]{:S(2)}) collective-permute-start(bf16[2,80,1280]{2,1,0:T(8,128)(2,1)S(1)} %pad_maximum_fusion.6), channel_id=1, source_target_pairs={{0,192},{16,208},{32,224},{48,240},{64,128},{80,144},{96,160},{112... | collective-permute-start | bytes 1228808 | tf_op jit(solution)/shard_map/ppermute | solution.py:16
  40.1 2.7 %collective-permute-start.12 = (bf16[64,1280]{1,0:T(8,128)(2,1)S(1)}, bf16[64,1280]{1,0:T(8,128)(2,1)S(1)}, u32[]{:S(2)}, u32[]{:S(2)}) collective-permute-start(bf16[64,1280]{1,0:T(8,128)(2,1)S(1)} %pad_maximum_fusion.8), channel_id=1, source_target_pairs={{0,1},{1,0},{2,3},{3,2},{4,5},{5,4},{6,7},{7,6},{8,9},{9,8},{10,11... | collective-permute-start | bytes 491528 | tf_op jit(solution)/shard_map/ppermute | solution.py:16
  42.8 6.6 %copy-start.1 = (bf16[8,256,1280]{2,1,0:T(8,128)(2,1)S(1)}, bf16[8,256,1280]{2,1,0:T(8,128)(2,1)}, u32[]{:S(2)}) copy-start(bf16[8,256,1280]{2,1,0:T(8,128)(2,1)} %refs_4_.1) | copy-start | bytes 15728644
  56.8 15.1 %collective-permute-start.21 = (bf16[128,1280]{1,0:T(8,128)(2,1)S(1)}, bf16[128,1280]{1,0:T(8,128)(2,1)S(1)}, u32[]{:S(2)}, u32[]{:S(2)}) collective-permute-start(bf16[128,1280]{1,0:T(8,128)(2,1)S(1)} %pad_maximum_fusion.7), channel_id=1, source_target_pairs={{0,64},{16,80},{32,96},{48,112},{64,0},{80,16},{96,32},{112,48},{1... | collective-permute-start | bytes 983048 | tf_op jit(solution)/shard_map/ppermute | solution.py:16
  56.8 15.2 %collective-permute-start.17 = (bf16[128,1280]{1,0:T(8,128)(2,1)S(1)}, bf16[128,1280]{1,0:T(8,128)(2,1)S(1)}, u32[]{:S(2)}, u32[]{:S(2)}) collective-permute-start(bf16[128,1280]{1,0:T(8,128)(2,1)S(1)} %pad_maximum_fusion.7), channel_id=1, source_target_pairs={{0,128},{16,144},{32,160},{48,176},{64,192},{80,208},{96,224},{112... | collective-permute-start | bytes 983048 | tf_op jit(solution)/shard_map/ppermute | solution.py:16
  59.5 12.5 %collective-permute-start.16 = (bf16[2,80,1280]{2,1,0:T(8,128)(2,1)S(1)}, bf16[2,80,1280]{2,1,0:T(8,128)(2,1)S(1)}, u32[]{:S(2)}, u32[]{:S(2)}) collective-permute-start(bf16[2,80,1280]{2,1,0:T(8,128)(2,1)S(1)} %collective-permute-done.10.refs_10_), channel_id=1, source_target_pairs={{0,48},{16,32},{32,16},{48,0},{64,112},{80,96},{96,80},{112,64},{1... | collective-permute-start | bytes 1228808 | tf_op jit(solution)/shard_map/ppermute | solution.py:16
  60.7 11.3 %collective-permute-start.15 = (bf16[2,80,1280]{2,1,0:T(8,128)(2,1)S(1)}, bf16[2,80,1280]{2,1,0:T(8,128)(2,1)S(1)}, u32[]{:S(2)}, u32[]{:S(2)}) collective-permute-start(bf16[2,80,1280]{2,1,0:T(8,128)(2,1)S(1)} %collective-permute-done.10.refs_10_), channel_id=1, source_target_pairs={{0,16},{16,0},{32,48},{48,32},{64,80},{80,64},{96,112},{112,96},{1... | collective-permute-start | bytes 1228808 | tf_op jit(solution)/shard_map/ppermute | solution.py:16
  60.7 17.2 %collective-permute-start.14 = (bf16[2,80,1280]{2,1,0:T(8,128)(2,1)S(1)}, bf16[2,80,1280]{2,1,0:T(8,128)(2,1)S(1)}, u32[]{:S(2)}, u32[]{:S(2)}) collective-permute-start(bf16[2,80,1280]{2,1,0:T(8,128)(2,1)S(1)} %slice_bitcast_fusion), channel_id=1, source_target_pairs={{0,48},{16,32},{32,16},{48,0},{64,112},{80,96},{96,80},{112,64},{1... | collective-permute-start | bytes 1228808 | tf_op jit(solution)/shard_map/ppermute | solution.py:16
  72.0 9.2 %collective-permute-start.13 = (bf16[2,80,1280]{2,1,0:T(8,128)(2,1)S(1)}, bf16[2,80,1280]{2,1,0:T(8,128)(2,1)S(1)}, u32[]{:S(2)}, u32[]{:S(2)}) collective-permute-start(bf16[2,80,1280]{2,1,0:T(8,128)(2,1)S(1)} %slice_bitcast_fusion.1), channel_id=1, source_target_pairs={{0,16},{16,0},{32,48},{48,32},{64,80},{80,64},{96,112},{112,96},{1... | collective-permute-start | bytes 1228808 | tf_op jit(solution)/shard_map/ppermute | solution.py:16
  72.1 10.3 %collective-permute-start.19 = (bf16[80,1280]{1,0:T(8,128)(2,1)S(1)}, bf16[80,1280]{1,0:T(8,128)(2,1)S(1)}, u32[]{:S(2)}, u32[]{:S(2)}) collective-permute-start(bf16[80,1280]{1,0:T(8,128)(2,1)S(1)} %slice_bitcast_fusion.4), channel_id=1, source_target_pairs={{0,48},{16,32},{32,16},{48,0},{64,112},{80,96},{96,80},{112,64},{1... | collective-permute-start | bytes 614408 | tf_op jit(solution)/shard_map/ppermute | solution.py:16
  73.6 12.0 %collective-permute-start.18 = (bf16[80,1280]{1,0:T(8,128)(2,1)S(1)}, bf16[80,1280]{1,0:T(8,128)(2,1)S(1)}, u32[]{:S(2)}, u32[]{:S(2)}) collective-permute-start(bf16[80,1280]{1,0:T(8,128)(2,1)S(1)} %slice_bitcast_fusion.5), channel_id=1, source_target_pairs={{0,16},{16,0},{32,48},{48,32},{64,80},{80,64},{96,112},{112,96},{1... | collective-permute-start | bytes 614408 | tf_op jit(solution)/shard_map/ppermute | solution.py:16
  74.2 11.3 %collective-permute-start.20 = (bf16[128,1280]{1,0:T(8,128)(2,1)S(1)}, bf16[128,1280]{1,0:T(8,128)(2,1)S(1)}, u32[]{:S(2)}, u32[]{:S(2)}) collective-permute-start(bf16[128,1280]{1,0:T(8,128)(2,1)S(1)} %collective-permute-done.17), channel_id=1, source_target_pairs={{0,64},{16,80},{32,96},{48,112},{64,0},{80,16},{96,32},{112,48},{1... | collective-permute-start | bytes 983048 | tf_op jit(solution)/shard_map/ppermute | solution.py:16
  89.7 5.7 %collective-permute-start.25 = (bf16[64,1280]{1,0:T(8,128)(2,1)S(1)}, bf16[64,1280]{1,0:T(8,128)(2,1)S(1)}, u32[]{:S(2)}, u32[]{:S(2)}) collective-permute-start(bf16[64,1280]{1,0:T(8,128)(2,1)S(1)} %get-tuple-element.98), channel_id=1, source_target_pairs={{0,64},{16,80},{32,96},{48,112},{64,0},{80,16},{96,32},{112,48},{1... | collective-permute-start | bytes 491528 | tf_op jit(solution)/shard_map/ppermute | solution.py:16
  89.8 7.2 %collective-permute-start.26 = (bf16[64,1280]{1,0:T(8,128)(2,1)S(1)}, bf16[64,1280]{1,0:T(8,128)(2,1)S(1)}, u32[]{:S(2)}, u32[]{:S(2)}) collective-permute-start(bf16[64,1280]{1,0:T(8,128)(2,1)S(1)} %get-tuple-element.99), channel_id=1, source_target_pairs={{0,128},{16,144},{32,160},{48,176},{64,192},{80,208},{96,224},{112... | collective-permute-start | bytes 491528 | tf_op jit(solution)/shard_map/ppermute | solution.py:16
  91.9 8.6 %collective-permute-start.27 = (bf16[64,1280]{1,0:T(8,128)(2,1)S(1)}, bf16[64,1280]{1,0:T(8,128)(2,1)S(1)}, u32[]{:S(2)}, u32[]{:S(2)}) collective-permute-start(bf16[64,1280]{1,0:T(8,128)(2,1)S(1)} %get-tuple-element.100), channel_id=1, source_target_pairs={{0,192},{16,208},{32,224},{48,240},{64,128},{80,144},{96,160},{112... | collective-permute-start | bytes 491528 | tf_op jit(solution)/shard_map/ppermute | solution.py:16
  93.4 21.8 %collective-permute-start.22 = (bf16[64,1280]{1,0:T(8,128)(2,1)S(1)}, bf16[64,1280]{1,0:T(8,128)(2,1)S(1)}, u32[]{:S(2)}, u32[]{:S(2)}) collective-permute-start(bf16[64,1280]{1,0:T(8,128)(2,1)S(1)} %get-tuple-element.90), channel_id=1, source_target_pairs={{0,64},{16,80},{32,96},{48,112},{64,0},{80,16},{96,32},{112,48},{1... | collective-permute-start | bytes 491528 | tf_op jit(solution)/shard_map/ppermute | solution.py:16
  93.4 23.3 %collective-permute-start.23 = (bf16[64,1280]{1,0:T(8,128)(2,1)S(1)}, bf16[64,1280]{1,0:T(8,128)(2,1)S(1)}, u32[]{:S(2)}, u32[]{:S(2)}) collective-permute-start(bf16[64,1280]{1,0:T(8,128)(2,1)S(1)} %get-tuple-element.91), channel_id=1, source_target_pairs={{0,128},{16,144},{32,160},{48,176},{64,192},{80,208},{96,224},{112... | collective-permute-start | bytes 491528 | tf_op jit(solution)/shard_map/ppermute | solution.py:16
  95.4 21.3 %collective-permute-start.24 = (bf16[64,1280]{1,0:T(8,128)(2,1)S(1)}, bf16[64,1280]{1,0:T(8,128)(2,1)S(1)}, u32[]{:S(2)}, u32[]{:S(2)}) collective-permute-start(bf16[64,1280]{1,0:T(8,128)(2,1)S(1)} %get-tuple-element.92), channel_id=1, source_target_pairs={{0,192},{16,208},{32,224},{48,240},{64,128},{80,144},{96,160},{112... | collective-permute-start | bytes 491528 | tf_op jit(solution)/shard_map/ppermute | solution.py:16
  102.5 14.2 %collective-permute-start.30 = (f32[8,256]{1,0:T(8,128)S(1)}, f32[8,256]{1,0:T(8,128)S(1)}, u32[]{:S(2)}, u32[]{:S(2)}) collective-permute-start(f32[8,256]{1,0:T(8,128)S(1)} %get-tuple-element.105), channel_id=1, source_target_pairs={{0,3},{1,2},{2,1},{3,0},{4,7},{5,6},{6,5},{7,4},{8,11},{9,10},{10,... | collective-permute-start | bytes 24584 | tf_op jit(solution)/shard_map/ppermute | solution.py:16
  110.4 6.7 %collective-permute-start.29 = (f32[8,256]{1,0:T(8,128)S(1)}, f32[8,256]{1,0:T(8,128)S(1)}, u32[]{:S(2)}, u32[]{:S(2)}) collective-permute-start(f32[8,256]{1,0:T(8,128)S(1)} %get-tuple-element.105), channel_id=1, source_target_pairs={{0,2},{1,3},{2,0},{3,1},{4,6},{5,7},{6,4},{7,5},{8,10},{9,11},{10,... | collective-permute-start | bytes 24584 | tf_op jit(solution)/shard_map/ppermute | solution.py:16
  115.1 2.0 %collective-permute-start.28 = (f32[8,256]{1,0:T(8,128)S(1)}, f32[8,256]{1,0:T(8,128)S(1)}, u32[]{:S(2)}, u32[]{:S(2)}) collective-permute-start(f32[8,256]{1,0:T(8,128)S(1)} %get-tuple-element.105), channel_id=1, source_target_pairs={{0,1},{1,0},{2,3},{3,2},{4,5},{5,4},{6,7},{7,6},{8,9},{9,8},{10,11... | collective-permute-start | bytes 24584 | tf_op jit(solution)/shard_map/ppermute | solution.py:16
  117.1 5.7 %collective-permute-start.33 = (f32[8,256]{1,0:T(8,128)S(1)}, f32[8,256]{1,0:T(8,128)S(1)}, u32[]{:S(2)}, u32[]{:S(2)}) collective-permute-start(f32[8,256]{1,0:T(8,128)S(1)} %add_add_fusion.2), channel_id=1, source_target_pairs={{0,12},{1,13},{2,14},{3,15},{4,8},{5,9},{6,10},{7,11},{8,4},{9,5},... | collective-permute-start | bytes 24584 | tf_op jit(solution)/shard_map/ppermute | solution.py:16
  118.1 4.8 %collective-permute-start.32 = (f32[8,256]{1,0:T(8,128)S(1)}, f32[8,256]{1,0:T(8,128)S(1)}, u32[]{:S(2)}, u32[]{:S(2)}) collective-permute-start(f32[8,256]{1,0:T(8,128)S(1)} %add_add_fusion.2), channel_id=1, source_target_pairs={{0,8},{1,9},{2,10},{3,11},{4,12},{5,13},{6,14},{7,15},{8,0},{9,1},... | collective-permute-start | bytes 24584 | tf_op jit(solution)/shard_map/ppermute | solution.py:16
  119.3 3.5 %collective-permute-start.31 = (f32[8,256]{1,0:T(8,128)S(1)}, f32[8,256]{1,0:T(8,128)S(1)}, u32[]{:S(2)}, u32[]{:S(2)}) collective-permute-start(f32[8,256]{1,0:T(8,128)S(1)} %add_add_fusion.2), channel_id=1, source_target_pairs={{0,4},{1,5},{2,6},{3,7},{4,0},{5,1},{6,2},{7,3},{8,12},{9,13},{10,... | collective-permute-start | bytes 24584 | tf_op jit(solution)/shard_map/ppermute | solution.py:16
  123.0 24.6 %collective-permute-start.36 = (bf16[64,1408]{1,0:T(8,128)(2,1)S(1)}, bf16[64,1408]{1,0:T(8,128)(2,1)S(1)}, u32[]{:S(2)}, u32[]{:S(2)}) collective-permute-start(bf16[64,1408]{1,0:T(8,128)(2,1)S(1)} %get-tuple-element.119.refs_0_), channel_id=1, source_target_pairs={{0,12},{1,13},{2,14},{3,15},{4,8},{5,9},{6,10},{7,11},{8,4},{9,5},... | collective-permute-start | bytes 540680 | tf_op jit(solution)/shard_map/ppermute | solution.py:16
  124.1 24.0 %collective-permute-start.35 = (bf16[64,1408]{1,0:T(8,128)(2,1)S(1)}, bf16[64,1408]{1,0:T(8,128)(2,1)S(1)}, u32[]{:S(2)}, u32[]{:S(2)}) collective-permute-start(bf16[64,1408]{1,0:T(8,128)(2,1)S(1)} %get-tuple-element.119.refs_0_), channel_id=1, source_target_pairs={{0,8},{1,9},{2,10},{3,11},{4,12},{5,13},{6,14},{7,15},{8,0},{9,1},... | collective-permute-start | bytes 540680 | tf_op jit(solution)/shard_map/ppermute | solution.py:16
  125.2 22.9 %collective-permute-start.34 = (bf16[64,1408]{1,0:T(8,128)(2,1)S(1)}, bf16[64,1408]{1,0:T(8,128)(2,1)S(1)}, u32[]{:S(2)}, u32[]{:S(2)}) collective-permute-start(bf16[64,1408]{1,0:T(8,128)(2,1)S(1)} %get-tuple-element.119.refs_0_), channel_id=1, source_target_pairs={{0,4},{1,5},{2,6},{3,7},{4,0},{5,1},{6,2},{7,3},{8,12},{9,13},{10,... | collective-permute-start | bytes 540680 | tf_op jit(solution)/shard_map/ppermute | solution.py:16
  126.4 18.4 %collective-permute-start.38 = (bf16[64,1408]{1,0:T(8,128)(2,1)S(1)}, bf16[64,1408]{1,0:T(8,128)(2,1)S(1)}, u32[]{:S(2)}, u32[]{:S(2)}) collective-permute-start(bf16[64,1408]{1,0:T(8,128)(2,1)S(1)} %get-tuple-element.117), channel_id=1, source_target_pairs={{0,2},{1,3},{2,0},{3,1},{4,6},{5,7},{6,4},{7,5},{8,10},{9,11},{10,... | collective-permute-start | bytes 540680 | tf_op jit(solution)/shard_map/ppermute | solution.py:16
  131.7 13.1 %collective-permute-start.37 = (f32[8,1280]{1,0:T(8,128)S(1)}, f32[8,1280]{1,0:T(8,128)S(1)}, u32[]{:S(2)}, u32[]{:S(2)}) collective-permute-start(f32[8,1280]{1,0:T(8,128)S(1)} %convolution_bitcast_fusion), channel_id=1, source_target_pairs={{0,64},{16,80},{32,96},{48,112},{64,0},{80,16},{96,32},{112,48},{1... | collective-permute-start | bytes 122888 | tf_op jit(solution)/shard_map/ppermute | solution.py:16
  144.8 11.5 %collective-permute-start.43 = (bf16[64,1408]{1,0:T(8,128)(2,1)S(1)}, bf16[64,1408]{1,0:T(8,128)(2,1)S(1)}, u32[]{:S(2)}, u32[]{:S(2)}) collective-permute-start(bf16[64,1408]{1,0:T(8,128)(2,1)S(1)} %collective-permute-done.38.refs_4_), channel_id=1, source_target_pairs={{0,12},{1,13},{2,14},{3,15},{4,8},{5,9},{6,10},{7,11},{8,4},{9,5},... | collective-permute-start | bytes 540680 | tf_op jit(solution)/shard_map/ppermute | solution.py:16
  146.5 9.8 %collective-permute-start.42 = (bf16[64,1408]{1,0:T(8,128)(2,1)S(1)}, bf16[64,1408]{1,0:T(8,128)(2,1)S(1)}, u32[]{:S(2)}, u32[]{:S(2)}) collective-permute-start(bf16[64,1408]{1,0:T(8,128)(2,1)S(1)} %collective-permute-done.38.refs_4_), channel_id=1, source_target_pairs={{0,8},{1,9},{2,10},{3,11},{4,12},{5,13},{6,14},{7,15},{8,0},{9,1},... | collective-permute-start | bytes 540680 | tf_op jit(solution)/shard_map/ppermute | solution.py:16
  147.6 9.4 %collective-permute-start.41 = (bf16[64,1408]{1,0:T(8,128)(2,1)S(1)}, bf16[64,1408]{1,0:T(8,128)(2,1)S(1)}, u32[]{:S(2)}, u32[]{:S(2)}) collective-permute-start(bf16[64,1408]{1,0:T(8,128)(2,1)S(1)} %collective-permute-done.38.refs_4_), channel_id=1, source_target_pairs={{0,4},{1,5},{2,6},{3,7},{4,0},{5,1},{6,2},{7,3},{8,12},{9,13},{10,... | collective-permute-start | bytes 540680 | tf_op jit(solution)/shard_map/ppermute | solution.py:16
  148.2 4.2 %collective-permute-start.39 = (f32[8,1280]{1,0:T(8,128)S(1)}, f32[8,1280]{1,0:T(8,128)S(1)}, u32[]{:S(2)}, u32[]{:S(2)}) collective-permute-start(f32[8,1280]{1,0:T(8,128)S(1)} %add.72), channel_id=1, source_target_pairs={{0,128},{16,144},{32,160},{48,176},{64,192},{80,208},{96,224},{112... | collective-permute-start | bytes 122888 | tf_op jit(solution)/shard_map/ppermute | solution.py:16
  152.3 3.1 %collective-permute-start.40 = (f32[8,1280]{1,0:T(8,128)S(1)}, f32[8,1280]{1,0:T(8,128)S(1)}, u32[]{:S(2)}, u32[]{:S(2)}) collective-permute-start(f32[8,1280]{1,0:T(8,128)S(1)} %add.73), channel_id=1, source_target_pairs={{0,16},{16,0},{32,48},{48,32},{64,80},{80,64},{96,112},{112,96},{1... | collective-permute-start | bytes 122888 | tf_op jit(solution)/shard_map/ppermute | solution.py:16
  158.2 7.0 %collective-permute-start.44 = (f32[128,1280]{1,0:T(8,128)S(1)}, f32[128,1280]{1,0:T(8,128)S(1)}, u32[]{:S(2)}, u32[]{:S(2)}) collective-permute-start(f32[128,1280]{1,0:T(8,128)S(1)} %get-tuple-element.130), channel_id=1, source_target_pairs={{0,1},{1,0},{2,3},{3,2},{4,5},{5,4},{6,7},{7,6},{8,9},{9,8},{10,11... | collective-permute-start | bytes 1966088 | tf_op jit(solution)/shard_map/ppermute | solution.py:16
  160.2 4.4 %collective-permute-start.45 = (f32[8,1280]{1,0:T(8,128)S(1)}, f32[8,1280]{1,0:T(8,128)S(1)}, u32[]{:S(2)}, u32[]{:S(2)}) collective-permute-start(f32[8,1280]{1,0:T(8,128)S(1)} %add.74), channel_id=1, source_target_pairs={{0,32},{16,48},{32,0},{48,16},{64,96},{80,112},{96,64},{112,80},{1... | collective-permute-start | bytes 122888 | tf_op jit(solution)/shard_map/ppermute | solution.py:16

commit v15 on v12

--- a/solution.py
+++ b/solution.py
@@ -345,15 +345,17 @@
     )
     rows = jnp.concatenate([slot_in, slot_go.astype(BF16).reshape(half, width)], axis=0)
 
-    lb, rb, u3, rows = together(lb, rb, u3, rows)
-    z1, z2 = swap(rows, "dp", 4), swap(rows, "dp", 8)
+    u3, rows = together(u3, rows)
+    z2 = swap(rows, "dp", 8)
+    lb, rb, u3 = together(lb, rb, u3)
+    z1 = swap(after(rows, lb), "dp", 4)
     l3, r3 = swap(u3, "dp", 1), swap(u3, "dp", 3)
     pb, qb = swap(rb[0], "dp", 1), swap(lb[1], "dp", 3)
-    l3, r3, z2 = together(l3, r3, z2)
+    spread = spread_call(near)
+    l3, r3, z1, z2, spread = together(l3, r3, z1, z2, spread)
     p3, q3 = swap(r3[0], "dp", 1), swap(l3[1], "dp", 3)
     z3 = swap(z2, "dp", 4)
-    spread = spread_call(near)
-    pb, qb, p3, q3, z3, spread = together(pb, qb, p3, q3, z3, spread)
+    pb, qb, p3, q3, z3 = together(pb, qb, p3, q3, z3)
     rows_in = jnp.concatenate([v[:half] for v in (rows, z1, z2, z3)], axis=0)
     rows_go = jnp.concatenate([v[half:] for v in (rows, z1, z2, z3)], axis=0)
 

time: 166 us -> 164 us (0.988)
  waiting for transfers between devices: 65.8 us -> 55.3 us
  starting transfers between devices: 76 us -> 85.4 us
    ppermute x43, waiting for transfers between devices: 65.8 us -> 55.3 us  [swap(): return lax.ppermute(value, axis, [(i, i ^ k) for i in range(count)])]
    ppermute x43, starting transfers between devices: 76 us -> 85.4 us  [swap(): return lax.ppermute(value, axis, [(i, i ^ k) for i in range(count)])]
  transfers between devices with their start and end apart: 43 -> 43, of which waited for: 19 -> 20; matrix products, arithmetic and copies ran while one was open for 2% -> 2% of each run, Pallas kernels for 7% -> 7%
where the time goes in v15:
time: 164 us
  starting transfers between devices  85.4 us (52%)
  waiting for transfers between devices  55.3 us (34%)
  Pallas kernels  16.8 us (10%)
  other arithmetic  1.93 us (1%)
  local copies, waits for them, and re-layouts  1.76 us (1%)
    ppermute x43, starting transfers between devices, swap(): return lax.ppermute(value, axis, [(i, i ^ k) for i in range(count)])  85.4 us
    ppermute x43, waiting for transfers between devices, swap(): return lax.ppermute(value, axis, [(i, i ^ k) for i in range(count)])  55.3 us
    pallas_call x1, Pallas kernels, slots_call(): pl.pallas_call(slots_kernel, grid=(images // 2,), out_shape=[jax.ShapeDty...  6.63 us
    pallas_call x2, Pallas kernels, against(): pl.pallas_call(lambda *refs: against_kernel(over_tokens, len(parts), *ref...  4.32 us
    pallas_call x1, Pallas kernels, ffn(): pl.pallas_call(ffn_kernel, out_shape=[jax.ShapeDtypeStruct((own_rows, wid...  4.04 us
  transfers between devices with their start and end apart: 43, of which 20 were waited for; matrix products, arithmetic and copies ran while one was open for 2% of the time, Pallas kernels for 7%

profile of v15, /device:TPU:1, one launch (start us, length us, event | category | flops | bytes accessed | tf_op | source)
XLA Modules:
  0.0 163.7 jit_solution(5571861666605121465)
XLA Ops:
  0.7 1.4 dynamic-slice_bitcast_fusion.1
  2.3 2.2 %collective-permute-start.4 = (bf16[2,80,1280]{2,1,0:T(8,128)(2,1)S(1)}, bf16[2,80,1280]{2,1,0:T(8,128)(2,1)S(1)}, u32[]{:S(2)}, u32[]{:S(2)}) collective-permute-start(bf16[2,80,1280]{2,1,0:T(8,128)(2,1)S(1)} %pad_maximum_fusion.3.refs_0_), channel_id=1, source_target_pairs={{0,16},{16,0},{32,48},{48,32},{64,80},{80,64},{96,112},{112,96},{1... | collective-permute-start | bytes 1228808 | tf_op jit(solution)/shard_map/ppermute | solution.py:16
  4.5 1.9 %collective-permute-start.2 = (bf16[2,80,1280]{2,1,0:T(8,128)(2,1)S(1)}, bf16[2,80,1280]{2,1,0:T(8,128)(2,1)S(1)}, u32[]{:S(2)}, u32[]{:S(2)}) collective-permute-start(bf16[2,80,1280]{2,1,0:T(8,128)(2,1)S(1)} %pad_maximum_fusion.3.refs_0_), channel_id=1, source_target_pairs={{0,48},{16,32},{32,16},{48,0},{64,112},{80,96},{96,80},{112,64},{1... | collective-permute-start | bytes 1228808 | tf_op jit(solution)/shard_map/ppermute | solution.py:16
  6.4 6.9 %collective-permute-start = (bf16[8,1280]{1,0:T(8,128)(2,1)S(1)}, bf16[8,1280]{1,0:T(8,128)(2,1)S(1)}, u32[]{:S(2)}, u32[]{:S(2)}) collective-permute-start(bf16[8,1280]{1,0:T(8,128)(2,1)S(1)} %bitcast.61), channel_id=1, source_target_pairs={{0,2},{1,3},{2,0},{3,1},{4,6},{5,7},{6,4},{7,5},{8,10},{9,11},{10,... | collective-permute-start | bytes 61448 | tf_op jit(solution)/shard_map/ppermute | solution.py:16
  13.3 1.3 collective-permute-start.7
  14.6 0.8 collective-permute-start.6
  15.5 1.3 collective-permute-start.1
  16.9 0.9 collective-permute-start.5
  17.8 0.6 collective-permute-done.1
  18.5 15.7 %collective-permute-done.7 = bf16[2,80,1280]{2,1,0:T(8,128)(2,1)S(1)} collective-permute-done((bf16[2,80,1280]{2,1,0:T(8,128)(2,1)S(1)}, bf16[2,80,1280]{2,1,0:T(8,128)(2,1)S(1)}, u32[]{:S(2)}, u32[]{:S(2)}) %collective-permute-start.7) | collective-permute-done | bytes 409632 | tf_op jit(solution)/shard_map/ppermute | solution.py:16
  34.2 2.8 %collective-permute-start.11 = (bf16[32,1280]{1,0:T(8,128)(2,1)S(1)}, bf16[32,1280]{1,0:T(8,128)(2,1)S(1)}, u32[]{:S(2)}, u32[]{:S(2)}) collective-permute-start(bf16[32,1280]{1,0:T(8,128)(2,1)S(1)} %pad_maximum_fusion.10), channel_id=1, source_target_pairs={{0,8},{1,9},{2,10},{3,11},{4,12},{5,13},{6,14},{7,15},{8,0},{9,1},... | collective-permute-start | bytes 245768 | tf_op jit(solution)/shard_map/ppermute | solution.py:16
  37.2 0.9 collective-permute-start.9
  38.0 2.0 %collective-permute-start.10 = (bf16[2,80,1280]{2,1,0:T(8,128)(2,1)S(1)}, bf16[2,80,1280]{2,1,0:T(8,128)(2,1)S(1)}, u32[]{:S(2)}, u32[]{:S(2)}) collective-permute-start(bf16[2,80,1280]{2,1,0:T(8,128)(2,1)S(1)} %pad_maximum_fusion.6), channel_id=1, source_target_pairs={{0,192},{16,208},{32,224},{48,240},{64,128},{80,144},{96,160},{112... | collective-permute-start | bytes 1228808 | tf_op jit(solution)/shard_map/ppermute | solution.py:16
  40.1 1.7 %collective-permute-start.12 = (bf16[64,1280]{1,0:T(8,128)(2,1)S(1)}, bf16[64,1280]{1,0:T(8,128)(2,1)S(1)}, u32[]{:S(2)}, u32[]{:S(2)}) collective-permute-start(bf16[64,1280]{1,0:T(8,128)(2,1)S(1)} %pad_maximum_fusion.9), channel_id=1, source_target_pairs={{0,1},{1,0},{2,3},{3,2},{4,5},{5,4},{6,7},{7,6},{8,9},{9,8},{10,11... | collective-permute-start | bytes 491528 | tf_op jit(solution)/shard_map/ppermute | solution.py:16
  41.7 1.0 collective-permute-done.12
  42.8 6.6 %slots.1 = (bf16[64,1280]{1,0:T(8,128)(2,1)S(1)}, f32[64,256]{1,0:T(8,128)S(1)}, f32[64,256]{1,0:T(8,128)S(1)}, bf16[8,64,256]{2,1,0:T(8,128)(2,1)S(1)}) custom-call(bf16[128,1280]{1,0:T(8,128)(2,1)S(1)} %constant_dynamic-update-slice_fusion.table, bf16[8,256,1280]{2,1,0:T(8,128)(2,1)S(1)} %copy-done), custom_call_target="tpu_custom_call" | custom-call | flops 754974720 | bytes 5242880 | tf_op jit(solution)/shard_map/slots/pallas_call | solution.py:102
  49.4 0.8 fusion
  50.2 0.4 spread.1
  50.7 3.8 %collective-permute-start.16 = (bf16[128,1280]{1,0:T(8,128)(2,1)S(1)}, bf16[128,1280]{1,0:T(8,128)(2,1)S(1)}, u32[]{:S(2)}, u32[]{:S(2)}) collective-permute-start(bf16[128,1280]{1,0:T(8,128)(2,1)S(1)} %pad_maximum_fusion.8), channel_id=1, source_target_pairs={{0,128},{16,144},{32,160},{48,176},{64,192},{80,208},{96,224},{112... | collective-permute-start | bytes 983048 | tf_op jit(solution)/shard_map/ppermute | solution.py:16
  54.5 2.3 %collective-permute-done.9.refs_7_ = bf16[2,2,80,1280]{3,2,1,0:T(8,128)(2,1)S(1)} collective-permute-done((bf16[2,2,80,1280]{3,2,1,0:T(8,128)(2,1)S(1)}, bf16[2,2,80,1280]{3,2,1,0:T(8,128)(2,1)S(1)}, u32[]{:S(2)}, u32[]{:S(2)}) %collective-permute-start.9) | collective-permute-done | bytes 819232 | tf_op jit(solution)/shard_map/ppermute | solution.py:16
  56.9 1.3 collective-permute-start.14
  58.1 1.5 collective-permute-start.18
  59.7 4.9 %collective-permute-done.16 = bf16[128,1280]{1,0:T(8,128)(2,1)S(1)} collective-permute-done((bf16[128,1280]{1,0:T(8,128)(2,1)S(1)}, bf16[128,1280]{1,0:T(8,128)(2,1)S(1)}, u32[]{:S(2)}, u32[]{:S(2)}) %collective-permute-start.16) | collective-permute-done | bytes 327712 | tf_op jit(solution)/shard_map/ppermute | solution.py:16
  64.6 1.5 collective-permute-start.17
  66.0 3.2 %collective-permute-done.15 = bf16[128,1280]{1,0:T(8,128)(2,1)S(1)} collective-permute-done((bf16[128,1280]{1,0:T(8,128)(2,1)S(1)}, bf16[128,1280]{1,0:T(8,128)(2,1)S(1)}, u32[]{:S(2)}, u32[]{:S(2)}) %collective-permute-start.15) | collective-permute-done | bytes 327712 | tf_op jit(solution)/shard_map/ppermute | solution.py:16
  69.3 2.1 %collective-permute-start.20 = (bf16[80,1280]{1,0:T(8,128)(2,1)S(1)}, bf16[80,1280]{1,0:T(8,128)(2,1)S(1)}, u32[]{:S(2)}, u32[]{:S(2)}) collective-permute-start(bf16[80,1280]{1,0:T(8,128)(2,1)S(1)} %slice_bitcast_fusion.4), channel_id=1, source_target_pairs={{0,48},{16,32},{32,16},{48,0},{64,112},{80,96},{96,80},{112,64},{1... | collective-permute-start | bytes 614408 | tf_op jit(solution)/shard_map/ppermute | solution.py:16
  71.4 1.9 %collective-permute-start.19 = (bf16[80,1280]{1,0:T(8,128)(2,1)S(1)}, bf16[80,1280]{1,0:T(8,128)(2,1)S(1)}, u32[]{:S(2)}, u32[]{:S(2)}) collective-permute-start(bf16[80,1280]{1,0:T(8,128)(2,1)S(1)} %slice_bitcast_fusion.5), channel_id=1, source_target_pairs={{0,16},{16,0},{32,48},{48,32},{64,80},{80,64},{96,112},{112,96},{1... | collective-permute-start | bytes 614408 | tf_op jit(solution)/shard_map/ppermute | solution.py:16
  73.3 1.7 %collective-permute-done.17.refs_8_ = bf16[2,80,1280]{2,1,0:T(8,128)(2,1)S(1)} collective-permute-done((bf16[2,80,1280]{2,1,0:T(8,128)(2,1)S(1)}, bf16[2,80,1280]{2,1,0:T(8,128)(2,1)S(1)}, u32[]{:S(2)}, u32[]{:S(2)}) %collective-permute-start.17) | collective-permute-done | bytes 409632 | tf_op jit(solution)/shard_map/ppermute | solution.py:16
  75.1 2.7 %collective-permute-done.20.refs_14_ = bf16[80,1280]{1,0:T(8,128)(2,1)S(1)} collective-permute-done((bf16[80,1280]{1,0:T(8,128)(2,1)S(1)}, bf16[80,1280]{1,0:T(8,128)(2,1)S(1)}, u32[]{:S(2)}, u32[]{:S(2)}) %collective-permute-start.20) | collective-permute-done | bytes 204832 | tf_op jit(solution)/shard_map/ppermute | solution.py:16
  77.7 1.7 %collective-permute-done.19.refs_13_ = bf16[80,1280]{1,0:T(8,128)(2,1)S(1)} collective-permute-done((bf16[80,1280]{1,0:T(8,128)(2,1)S(1)}, bf16[80,1280]{1,0:T(8,128)(2,1)S(1)}, u32[]{:S(2)}, u32[]{:S(2)}) %collective-permute-start.19) | collective-permute-done | bytes 204832 | tf_op jit(solution)/shard_map/ppermute | solution.py:16
  79.6 4.0 %ffn.1 = (f32[64,1280]{1,0:T(8,128)S(1)}, bf16[64,1280]{1,0:T(8,128)(2,1)S(1)}, bf16[64,1280]{1,0:T(8,128)(2,1)S(1)}, bf16[64,1280]{1,0:T(8,128)(2,1)S(1)}, f32[...) custom-call(bf16[256,1280]{1,0:T(8,128)(2,1)S(1)} %pad_maximum_fusio, ...), custom_call_target="tpu_custom_call" | custom-call | tf_op jit(solution)/shard_map/ffn/pallas_call | solution.py:61
  83.8 1.2 collective-permute-start.26
  84.9 2.4 %collective-permute-start.27 = (bf16[64,1280]{1,0:T(8,128)(2,1)S(1)}, bf16[64,1280]{1,0:T(8,128)(2,1)S(1)}, u32[]{:S(2)}, u32[]{:S(2)}) collective-permute-start(bf16[64,1280]{1,0:T(8,128)(2,1)S(1)} %get-tuple-element.97), channel_id=1, source_target_pairs={{0,192},{16,208},{32,224},{48,240},{64,128},{80,144},{96,160},{112... | collective-permute-start | bytes 491528 | tf_op jit(solution)/shard_map/ppermute | solution.py:16
  87.3 1.2 collective-permute-start.23
  88.5 0.7 collective-permute-done.25.refs_1_
  89.2 2.5 %collective-permute-start.24 = (bf16[64,1280]{1,0:T(8,128)(2,1)S(1)}, bf16[64,1280]{1,0:T(8,128)(2,1)S(1)}, u32[]{:S(2)}, u32[]{:S(2)}) collective-permute-start(bf16[64,1280]{1,0:T(8,128)(2,1)S(1)} %get-tuple-element.89), channel_id=1, source_target_pairs={{0,192},{16,208},{32,224},{48,240},{64,128},{80,144},{96,160},{112... | collective-permute-start | bytes 491528 | tf_op jit(solution)/shard_map/ppermute | solution.py:16
  91.7 0.9 collective-permute-done.26.refs_2_
  92.6 2.0 %combine_grad.1 = (f32[64,256]{1,0:T(8,128)S(1)}, f32[8,256]{1,0:T(8,128)S(1)}) custom-call(f32[64,1280]{1,0:T(8,128)S(1)} %get-tuple-element.94.refs_0_, bf16[64,1280]{1,0:T(8,128)(2,1)S(1)} %collective-permute-done.25.refs_1_, bf16[64,1280]{1,0:T(8,128)(2,1)S(1)} %collective-permute-done.26.refs_2_, bf16[64,1280]{1,0:T(8,128)(2,1)S(1)} %collective-permute-done.27.refs_3_, ...), custom_call_target="tpu_custom_call" | custom-call | tf_op jit(solution)/shard_map/combine_grad/pallas_call | solution.py:188
  94.6 17.2 %collective-permute-start.30 = (f32[8,256]{1,0:T(8,128)S(1)}, f32[8,256]{1,0:T(8,128)S(1)}, u32[]{:S(2)}, u32[]{:S(2)}) collective-permute-start(f32[8,256]{1,0:T(8,128)S(1)} %get-tuple-element.102), channel_id=1, source_target_pairs={{0,3},{1,2},{2,1},{3,0},{4,7},{5,6},{6,5},{7,4},{8,11},{9,10},{10,... | collective-permute-start | bytes 24584 | tf_op jit(solution)/shard_map/ppermute | solution.py:16
  111.9 1.2 collective-permute-start.29
  113.3 5.0 %collective-permute-done.29 = f32[8,256]{1,0:T(8,128)S(1)} collective-permute-done((f32[8,256]{1,0:T(8,128)S(1)}, f32[8,256]{1,0:T(8,128)S(1)}, u32[]{:S(2)}, u32[]{:S(2)}) %collective-permute-start.29) | collective-permute-done | bytes 8224 | tf_op jit(solution)/shard_map/ppermute | solution.py:16
  118.3 0.9 collective-permute-start.33
  119.2 1.2 collective-permute-start.32
  120.5 1.1 collective-permute-start.31
  121.7 2.3 %dispatch_grad.1.back = f32[64,256]{1,0:T(8,128)S(1)} custom-call(f32[64,1280]{1,0:T(8,128)S(1)} %add_add_fusion.refs_0_.grad, bf16[8,256,1280]{2,1,0:T(8,128)(2,1)S(1)} %copy-done, f32[64,256]{1,0:T(8,128)S(1)} %get-tuple-element.93.refs_2_), custom_call_target="tpu_custom_call" | custom-call | tf_op jit(solution)/shard_map/dispatch_grad/pallas_call | solution.py:188
  124.2 1.3 collective-permute-start.35
  125.5 0.8 convolution_bitcast_fusion
  126.3 7.7 %collective-permute-start.34 = (f32[8,1280]{1,0:T(8,128)S(1)}, f32[8,1280]{1,0:T(8,128)S(1)}, u32[]{:S(2)}, u32[]{:S(2)}) collective-permute-start(f32[8,1280]{1,0:T(8,128)S(1)} %convolution_bitcast_fusion), channel_id=1, source_target_pairs={{0,64},{16,80},{32,96},{48,112},{64,0},{80,16},{96,32},{112,48},{1... | collective-permute-start | bytes 122888 | tf_op jit(solution)/shard_map/ppermute | solution.py:16
  133.9 5.3 %collective-permute-done.34 = f32[8,1280]{1,0:T(8,128)S(1)} collective-permute-done((f32[8,1280]{1,0:T(8,128)S(1)}, f32[8,1280]{1,0:T(8,128)S(1)}, u32[]{:S(2)}, u32[]{:S(2)}) %collective-permute-start.34) | collective-permute-done | bytes 40992 | tf_op jit(solution)/shard_map/ppermute | solution.py:16
  139.4 1.2 collective-permute-start.38
  140.6 0.7 collective-permute-start.37
  141.3 1.4 collective-permute-start.36
  142.7 2.3 %collective-permute-start.39 = (f32[8,1280]{1,0:T(8,128)S(1)}, f32[8,1280]{1,0:T(8,128)S(1)}, u32[]{:S(2)}, u32[]{:S(2)}) collective-permute-start(f32[8,1280]{1,0:T(8,128)S(1)} %add.72), channel_id=1, source_target_pairs={{0,128},{16,144},{32,160},{48,176},{64,192},{80,208},{96,224},{112... | collective-permute-start | bytes 122888 | tf_op jit(solution)/shard_map/ppermute | solution.py:16
  145.0 1.7 %collective-permute-done.39 = f32[8,1280]{1,0:T(8,128)S(1)} collective-permute-done((f32[8,1280]{1,0:T(8,128)S(1)}, f32[8,1280]{1,0:T(8,128)S(1)}, u32[]{:S(2)}, u32[]{:S(2)}) %collective-permute-start.39) | collective-permute-done | bytes 40992 | tf_op jit(solution)/shard_map/ppermute | solution.py:16
  146.8 1.3 collective-permute-start.40
  148.1 1.8 %collective-permute-done.40 = f32[8,1280]{1,0:T(8,128)S(1)} collective-permute-done((f32[8,1280]{1,0:T(8,128)S(1)}, f32[8,1280]{1,0:T(8,128)S(1)}, u32[]{:S(2)}, u32[]{:S(2)}) %collective-permute-start.40) | collective-permute-done | bytes 40992 | tf_op jit(solution)/shard_map/ppermute | solution.py:16
  149.9 3.9 %collective-permute-start.41 = (f32[8,1280]{1,0:T(8,128)S(1)}, f32[8,1280]{1,0:T(8,128)S(1)}, u32[]{:S(2)}, u32[]{:S(2)}) collective-permute-start(f32[8,1280]{1,0:T(8,128)S(1)} %add.74), channel_id=1, source_target_pairs={{0,32},{16,48},{32,0},{48,16},{64,96},{80,112},{96,64},{112,80},{1... | collective-permute-start | bytes 122888 | tf_op jit(solution)/shard_map/ppermute | solution.py:16
  153.8 4.1 %collective-permute-done.38.three = bf16[2,64,1408]{2,1,0:T(8,128)(2,1)S(1)} collective-permute-done((bf16[2,64,1408]{2,1,0:T(8,128)(2,1)S(1)}, bf16[2,64,1408]{2,1,0:T(8,128)(2,1)S(1)}, u32[]{:S(2)}, u32[]{:S(2)}) %collective-permute-start.38) | collective-permute-done | bytes 360480 | tf_op jit(solution)/shard_map/ppermute | solution.py:16
  158.0 0.3 collective-permute-done.36.one
  158.3 1.2 token_grad.1
  159.6 1.6 collective-permute-start.42
  161.2 0.6 add_bitcast_fusion
  161.8 1.1 collective-permute-done.42
  162.9 0.8 add_convert_fusion
  (73 shorter events, 1.7 us)
Async XLA Ops:
  0.6 1.5 copy-start.2
  2.1 4.2 %copy-start.3 = (bf16[1280,8]{0,1:T(8,128)(2,1)S(1)}, bf16[1280,8]{0,1:T(8,128)(2,1)}, u32[]{:S(2)}) copy-start(bf16[1280,8]{0,1:T(8,128)(2,1)} %param.7) | copy-start | bytes 61444
  2.3 14.6 %collective-permute-start.4 = (bf16[2,80,1280]{2,1,0:T(8,128)(2,1)S(1)}, bf16[2,80,1280]{2,1,0:T(8,128)(2,1)S(1)}, u32[]{:S(2)}, u32[]{:S(2)}) collective-permute-start(bf16[2,80,1280]{2,1,0:T(8,128)(2,1)S(1)} %pad_maximum_fusion.3.refs_0_), channel_id=1, source_target_pairs={{0,16},{16,0},{32,48},{48,32},{64,80},{80,64},{96,112},{112,96},{1... | collective-permute-start | bytes 1228808 | tf_op jit(solution)/shard_map/ppermute | solution.py:16
  4.5 13.3 %collective-permute-start.2 = (bf16[2,80,1280]{2,1,0:T(8,128)(2,1)S(1)}, bf16[2,80,1280]{2,1,0:T(8,128)(2,1)S(1)}, u32[]{:S(2)}, u32[]{:S(2)}) collective-permute-start(bf16[2,80,1280]{2,1,0:T(8,128)(2,1)S(1)} %pad_maximum_fusion.3.refs_0_), channel_id=1, source_target_pairs={{0,48},{16,32},{32,16},{48,0},{64,112},{80,96},{96,80},{112,64},{1... | collective-permute-start | bytes 1228808 | tf_op jit(solution)/shard_map/ppermute | solution.py:16
  6.4 9.1 %collective-permute-start = (bf16[8,1280]{1,0:T(8,128)(2,1)S(1)}, bf16[8,1280]{1,0:T(8,128)(2,1)S(1)}, u32[]{:S(2)}, u32[]{:S(2)}) collective-permute-start(bf16[8,1280]{1,0:T(8,128)(2,1)S(1)} %bitcast.61), channel_id=1, source_target_pairs={{0,2},{1,3},{2,0},{3,1},{4,6},{5,7},{6,4},{7,5},{8,10},{9,11},{10,... | collective-permute-start | bytes 61448 | tf_op jit(solution)/shard_map/ppermute | solution.py:16
  13.3 20.9 %collective-permute-start.7 = (bf16[2,80,1280]{2,1,0:T(8,128)(2,1)S(1)}, bf16[2,80,1280]{2,1,0:T(8,128)(2,1)S(1)}, u32[]{:S(2)}, u32[]{:S(2)}) collective-permute-start(bf16[2,80,1280]{2,1,0:T(8,128)(2,1)S(1)} %pad_maximum_fusion.5), channel_id=1, source_target_pairs={{0,128},{16,144},{32,160},{48,176},{64,192},{80,208},{96,224},{112... | collective-permute-start | bytes 1228808 | tf_op jit(solution)/shard_map/ppermute | solution.py:16
  14.6 28.2 %copy-start = (bf16[8,256,1280]{2,1,0:T(8,128)(2,1)S(1)}, bf16[8,256,1280]{2,1,0:T(8,128)(2,1)}, u32[]{:S(2)}) copy-start(bf16[8,256,1280]{2,1,0:T(8,128)(2,1)} %refs_1_.1) | copy-start | bytes 15728644
  14.6 19.6 %collective-permute-start.6 = (bf16[2,80,1280]{2,1,0:T(8,128)(2,1)S(1)}, bf16[2,80,1280]{2,1,0:T(8,128)(2,1)S(1)}, u32[]{:S(2)}, u32[]{:S(2)}) collective-permute-start(bf16[2,80,1280]{2,1,0:T(8,128)(2,1)S(1)} %pad_maximum_fusion.4), channel_id=1, source_target_pairs={{0,64},{16,80},{32,96},{48,112},{64,0},{80,16},{96,32},{112,48},{1... | collective-permute-start | bytes 1228808 | tf_op jit(solution)/shard_map/ppermute | solution.py:16
  15.5 2.9 %collective-permute-start.1 = (bf16[16,1280]{1,0:T(8,128)(2,1)S(1)}, bf16[16,1280]{1,0:T(8,128)(2,1)S(1)}, u32[]{:S(2)}, u32[]{:S(2)}) collective-permute-start(bf16[16,1280]{1,0:T(8,128)(2,1)S(1)} %pad_maximum_fusion.11), channel_id=1, source_target_pairs={{0,4},{1,5},{2,6},{3,7},{4,0},{5,1},{6,2},{7,3},{8,12},{9,13},{10,... | collective-permute-start | bytes 122888 | tf_op jit(solution)/shard_map/ppermute | solution.py:16
  16.9 17.4 %collective-permute-start.5 = (bf16[80,1280]{1,0:T(8,128)(2,1)S(1)}, bf16[80,1280]{1,0:T(8,128)(2,1)S(1)}, u32[]{:S(2)}, u32[]{:S(2)}) collective-permute-start(bf16[80,1280]{1,0:T(8,128)(2,1)S(1)} %slice_bitcast_fusion.2), channel_id=1, source_target_pairs={{0,48},{16,32},{32,16},{48,0},{64,112},{80,96},{96,80},{112,64},{1... | collective-permute-start | bytes 614408 | tf_op jit(solution)/shard_map/ppermute | solution.py:16
  17.7 16.5 %collective-permute-start.3 = (bf16[80,1280]{1,0:T(8,128)(2,1)S(1)}, bf16[80,1280]{1,0:T(8,128)(2,1)S(1)}, u32[]{:S(2)}, u32[]{:S(2)}) collective-permute-start(bf16[80,1280]{1,0:T(8,128)(2,1)S(1)} %slice_bitcast_fusion.3), channel_id=1, source_target_pairs={{0,16},{16,0},{32,48},{48,32},{64,80},{80,64},{96,112},{112,96},{1... | collective-permute-start | bytes 614408 | tf_op jit(solution)/shard_map/ppermute | solution.py:16
  34.2 5.8 %collective-permute-start.11 = (bf16[32,1280]{1,0:T(8,128)(2,1)S(1)}, bf16[32,1280]{1,0:T(8,128)(2,1)S(1)}, u32[]{:S(2)}, u32[]{:S(2)}) collective-permute-start(bf16[32,1280]{1,0:T(8,128)(2,1)S(1)} %pad_maximum_fusion.10), channel_id=1, source_target_pairs={{0,8},{1,9},{2,10},{3,11},{4,12},{5,13},{6,14},{7,15},{8,0},{9,1},... | collective-permute-start | bytes 245768 | tf_op jit(solution)/shard_map/ppermute | solution.py:16
  37.2 19.7 %collective-permute-start.9 = (bf16[2,2,80,1280]{3,2,1,0:T(8,128)(2,1)S(1)}, bf16[2,2,80,1280]{3,2,1,0:T(8,128)(2,1)S(1)}, u32[]{:S(2)}, u32[]{:S(2)}) collective-permute-start(bf16[2,2,80,1280]{3,2,1,0:T(8,128)(2,1)S(1)} %pad_maximum_fusion.refs_5_), channel_id=1, source_target_pairs={{0,48},{16,32},{32,16},{48,0},{64,112},{80,96},{96,80},{112,64},{1... | collective-permute-start | bytes 2457608 | tf_op jit(solution)/shard_map/ppermute | solution.py:16
  38.0 18.8 %collective-permute-start.8 = (bf16[2,2,80,1280]{3,2,1,0:T(8,128)(2,1)S(1)}, bf16[2,2,80,1280]{3,2,1,0:T(8,128)(2,1)S(1)}, u32[]{:S(2)}, u32[]{:S(2)}) collective-permute-start(bf16[2,2,80,1280]{3,2,1,0:T(8,128)(2,1)S(1)} %pad_maximum_fusion.refs_5_), channel_id=1, source_target_pairs={{0,16},{16,0},{32,48},{48,32},{64,80},{80,64},{96,112},{112,96},{1... | collective-permute-start | bytes 2457608 | tf_op jit(solution)/shard_map/ppermute | solution.py:16
  38.0 12.6 %collective-permute-start.10 = (bf16[2,80,1280]{2,1,0:T(8,128)(2,1)S(1)}, bf16[2,80,1280]{2,1,0:T(8,128)(2,1)S(1)}, u32[]{:S(2)}, u32[]{:S(2)}) collective-permute-start(bf16[2,80,1280]{2,1,0:T(8,128)(2,1)S(1)} %pad_maximum_fusion.6), channel_id=1, source_target_pairs={{0,192},{16,208},{32,224},{48,240},{64,128},{80,144},{96,160},{112... | collective-permute-start | bytes 1228808 | tf_op jit(solution)/shard_map/ppermute | solution.py:16
  40.1 2.7 %collective-permute-start.12 = (bf16[64,1280]{1,0:T(8,128)(2,1)S(1)}, bf16[64,1280]{1,0:T(8,128)(2,1)S(1)}, u32[]{:S(2)}, u32[]{:S(2)}) collective-permute-start(bf16[64,1280]{1,0:T(8,128)(2,1)S(1)} %pad_maximum_fusion.9), channel_id=1, source_target_pairs={{0,1},{1,0},{2,3},{3,2},{4,5},{5,4},{6,7},{7,6},{8,9},{9,8},{10,11... | collective-permute-start | bytes 491528 | tf_op jit(solution)/shard_map/ppermute | solution.py:16
  42.8 6.6 %copy-start.1 = (bf16[8,256,1280]{2,1,0:T(8,128)(2,1)S(1)}, bf16[8,256,1280]{2,1,0:T(8,128)(2,1)}, u32[]{:S(2)}) copy-start(bf16[8,256,1280]{2,1,0:T(8,128)(2,1)} %refs_4_.1) | copy-start | bytes 15728644
  50.7 13.9 %collective-permute-start.16 = (bf16[128,1280]{1,0:T(8,128)(2,1)S(1)}, bf16[128,1280]{1,0:T(8,128)(2,1)S(1)}, u32[]{:S(2)}, u32[]{:S(2)}) collective-permute-start(bf16[128,1280]{1,0:T(8,128)(2,1)S(1)} %pad_maximum_fusion.8), channel_id=1, source_target_pairs={{0,128},{16,144},{32,160},{48,176},{64,192},{80,208},{96,224},{112... | collective-permute-start | bytes 983048 | tf_op jit(solution)/shard_map/ppermute | solution.py:16
  56.9 12.4 %collective-permute-start.14 = (bf16[2,80,1280]{2,1,0:T(8,128)(2,1)S(1)}, bf16[2,80,1280]{2,1,0:T(8,128)(2,1)S(1)}, u32[]{:S(2)}, u32[]{:S(2)}) collective-permute-start(bf16[2,80,1280]{2,1,0:T(8,128)(2,1)S(1)} %collective-permute-done.10.refs_10_), channel_id=1, source_target_pairs={{0,48},{16,32},{32,16},{48,0},{64,112},{80,96},{96,80},{112,64},{1... | collective-permute-start | bytes 1228808 | tf_op jit(solution)/shard_map/ppermute | solution.py:16
  58.1 11.1 %collective-permute-start.13 = (bf16[2,80,1280]{2,1,0:T(8,128)(2,1)S(1)}, bf16[2,80,1280]{2,1,0:T(8,128)(2,1)S(1)}, u32[]{:S(2)}, u32[]{:S(2)}) collective-permute-start(bf16[2,80,1280]{2,1,0:T(8,128)(2,1)S(1)} %collective-permute-done.10.refs_10_), channel_id=1, source_target_pairs={{0,16},{16,0},{32,48},{48,32},{64,80},{80,64},{96,112},{112,96},{1... | collective-permute-start | bytes 1228808 | tf_op jit(solution)/shard_map/ppermute | solution.py:16
  58.1 11.1 %collective-permute-start.15 = (bf16[128,1280]{1,0:T(8,128)(2,1)S(1)}, bf16[128,1280]{1,0:T(8,128)(2,1)S(1)}, u32[]{:S(2)}, u32[]{:S(2)}) collective-permute-start(bf16[128,1280]{1,0:T(8,128)(2,1)S(1)} %pad_maximum_fusion.8), channel_id=1, source_target_pairs={{0,64},{16,80},{32,96},{48,112},{64,0},{80,16},{96,32},{112,48},{1... | collective-permute-start | bytes 983048 | tf_op jit(solution)/shard_map/ppermute | solution.py:16
  58.1 15.2 %collective-permute-start.18 = (bf16[2,80,1280]{2,1,0:T(8,128)(2,1)S(1)}, bf16[2,80,1280]{2,1,0:T(8,128)(2,1)S(1)}, u32[]{:S(2)}, u32[]{:S(2)}) collective-permute-start(bf16[2,80,1280]{2,1,0:T(8,128)(2,1)S(1)} %slice_bitcast_fusion), channel_id=1, source_target_pairs={{0,48},{16,32},{32,16},{48,0},{64,112},{80,96},{96,80},{112,64},{1... | collective-permute-start | bytes 1228808 | tf_op jit(solution)/shard_map/ppermute | solution.py:16
  64.6 10.5 %collective-permute-start.17 = (bf16[2,80,1280]{2,1,0:T(8,128)(2,1)S(1)}, bf16[2,80,1280]{2,1,0:T(8,128)(2,1)S(1)}, u32[]{:S(2)}, u32[]{:S(2)}) collective-permute-start(bf16[2,80,1280]{2,1,0:T(8,128)(2,1)S(1)} %slice_bitcast_fusion.1), channel_id=1, source_target_pairs={{0,16},{16,0},{32,48},{48,32},{64,80},{80,64},{96,112},{112,96},{1... | collective-permute-start | bytes 1228808 | tf_op jit(solution)/shard_map/ppermute | solution.py:16
  69.3 8.5 %collective-permute-start.20 = (bf16[80,1280]{1,0:T(8,128)(2,1)S(1)}, bf16[80,1280]{1,0:T(8,128)(2,1)S(1)}, u32[]{:S(2)}, u32[]{:S(2)}) collective-permute-start(bf16[80,1280]{1,0:T(8,128)(2,1)S(1)} %slice_bitcast_fusion.4), channel_id=1, source_target_pairs={{0,48},{16,32},{32,16},{48,0},{64,112},{80,96},{96,80},{112,64},{1... | collective-permute-start | bytes 614408 | tf_op jit(solution)/shard_map/ppermute | solution.py:16
  71.4 8.1 %collective-permute-start.19 = (bf16[80,1280]{1,0:T(8,128)(2,1)S(1)}, bf16[80,1280]{1,0:T(8,128)(2,1)S(1)}, u32[]{:S(2)}, u32[]{:S(2)}) collective-permute-start(bf16[80,1280]{1,0:T(8,128)(2,1)S(1)} %slice_bitcast_fusion.5), channel_id=1, source_target_pairs={{0,16},{16,0},{32,48},{48,32},{64,80},{80,64},{96,112},{112,96},{1... | collective-permute-start | bytes 614408 | tf_op jit(solution)/shard_map/ppermute | solution.py:16
  73.3 6.2 %collective-permute-start.21 = (bf16[128,1280]{1,0:T(8,128)(2,1)S(1)}, bf16[128,1280]{1,0:T(8,128)(2,1)S(1)}, u32[]{:S(2)}, u32[]{:S(2)}) collective-permute-start(bf16[128,1280]{1,0:T(8,128)(2,1)S(1)} %collective-permute-done.16), channel_id=1, source_target_pairs={{0,64},{16,80},{32,96},{48,112},{64,0},{80,16},{96,32},{112,48},{1... | collective-permute-start | bytes 983048 | tf_op jit(solution)/shard_map/ppermute | solution.py:16
  83.7 5.5 %collective-permute-start.25 = (bf16[64,1280]{1,0:T(8,128)(2,1)S(1)}, bf16[64,1280]{1,0:T(8,128)(2,1)S(1)}, u32[]{:S(2)}, u32[]{:S(2)}) collective-permute-start(bf16[64,1280]{1,0:T(8,128)(2,1)S(1)} %get-tuple-element.95), channel_id=1, source_target_pairs={{0,64},{16,80},{32,96},{48,112},{64,0},{80,16},{96,32},{112,48},{1... | collective-permute-start | bytes 491528 | tf_op jit(solution)/shard_map/ppermute | solution.py:16
  83.8 8.8 %collective-permute-start.26 = (bf16[64,1280]{1,0:T(8,128)(2,1)S(1)}, bf16[64,1280]{1,0:T(8,128)(2,1)S(1)}, u32[]{:S(2)}, u32[]{:S(2)}) collective-permute-start(bf16[64,1280]{1,0:T(8,128)(2,1)S(1)} %get-tuple-element.96), channel_id=1, source_target_pairs={{0,128},{16,144},{32,160},{48,176},{64,192},{80,208},{96,224},{112... | collective-permute-start | bytes 491528 | tf_op jit(solution)/shard_map/ppermute | solution.py:16
  84.9 7.7 %collective-permute-start.27 = (bf16[64,1280]{1,0:T(8,128)(2,1)S(1)}, bf16[64,1280]{1,0:T(8,128)(2,1)S(1)}, u32[]{:S(2)}, u32[]{:S(2)}) collective-permute-start(bf16[64,1280]{1,0:T(8,128)(2,1)S(1)} %get-tuple-element.97), channel_id=1, source_target_pairs={{0,192},{16,208},{32,224},{48,240},{64,128},{80,144},{96,160},{112... | collective-permute-start | bytes 491528 | tf_op jit(solution)/shard_map/ppermute | solution.py:16
  87.3 25.7 %collective-permute-start.22 = (bf16[64,1280]{1,0:T(8,128)(2,1)S(1)}, bf16[64,1280]{1,0:T(8,128)(2,1)S(1)}, u32[]{:S(2)}, u32[]{:S(2)}) collective-permute-start(bf16[64,1280]{1,0:T(8,128)(2,1)S(1)} %get-tuple-element.87), channel_id=1, source_target_pairs={{0,64},{16,80},{32,96},{48,112},{64,0},{80,16},{96,32},{112,48},{1... | collective-permute-start | bytes 491528 | tf_op jit(solution)/shard_map/ppermute | solution.py:16
  87.3 25.7 %collective-permute-start.23 = (bf16[64,1280]{1,0:T(8,128)(2,1)S(1)}, bf16[64,1280]{1,0:T(8,128)(2,1)S(1)}, u32[]{:S(2)}, u32[]{:S(2)}) collective-permute-start(bf16[64,1280]{1,0:T(8,128)(2,1)S(1)} %get-tuple-element.88), channel_id=1, source_target_pairs={{0,128},{16,144},{32,160},{48,176},{64,192},{80,208},{96,224},{112... | collective-permute-start | bytes 491528 | tf_op jit(solution)/shard_map/ppermute | solution.py:16
  89.2 23.9 %collective-permute-start.24 = (bf16[64,1280]{1,0:T(8,128)(2,1)S(1)}, bf16[64,1280]{1,0:T(8,128)(2,1)S(1)}, u32[]{:S(2)}, u32[]{:S(2)}) collective-permute-start(bf16[64,1280]{1,0:T(8,128)(2,1)S(1)} %get-tuple-element.89), channel_id=1, source_target_pairs={{0,192},{16,208},{32,224},{48,240},{64,128},{80,144},{96,160},{112... | collective-permute-start | bytes 491528 | tf_op jit(solution)/shard_map/ppermute | solution.py:16
  94.6 18.7 %collective-permute-start.30 = (f32[8,256]{1,0:T(8,128)S(1)}, f32[8,256]{1,0:T(8,128)S(1)}, u32[]{:S(2)}, u32[]{:S(2)}) collective-permute-start(f32[8,256]{1,0:T(8,128)S(1)} %get-tuple-element.102), channel_id=1, source_target_pairs={{0,3},{1,2},{2,1},{3,0},{4,7},{5,6},{6,5},{7,4},{8,11},{9,10},{10,... | collective-permute-start | bytes 24584 | tf_op jit(solution)/shard_map/ppermute | solution.py:16
  111.9 6.4 %collective-permute-start.29 = (f32[8,256]{1,0:T(8,128)S(1)}, f32[8,256]{1,0:T(8,128)S(1)}, u32[]{:S(2)}, u32[]{:S(2)}) collective-permute-start(f32[8,256]{1,0:T(8,128)S(1)} %get-tuple-element.102), channel_id=1, source_target_pairs={{0,2},{1,3},{2,0},{3,1},{4,6},{5,7},{6,4},{7,5},{8,10},{9,11},{10,... | collective-permute-start | bytes 24584 | tf_op jit(solution)/shard_map/ppermute | solution.py:16
  113.1 5.2 %collective-permute-start.28 = (f32[8,256]{1,0:T(8,128)S(1)}, f32[8,256]{1,0:T(8,128)S(1)}, u32[]{:S(2)}, u32[]{:S(2)}) collective-permute-start(f32[8,256]{1,0:T(8,128)S(1)} %get-tuple-element.102), channel_id=1, source_target_pairs={{0,1},{1,0},{2,3},{3,2},{4,5},{5,4},{6,7},{7,6},{8,9},{9,8},{10,11... | collective-permute-start | bytes 24584 | tf_op jit(solution)/shard_map/ppermute | solution.py:16
  118.3 5.7 %collective-permute-start.33 = (f32[8,256]{1,0:T(8,128)S(1)}, f32[8,256]{1,0:T(8,128)S(1)}, u32[]{:S(2)}, u32[]{:S(2)}) collective-permute-start(f32[8,256]{1,0:T(8,128)S(1)} %add_add_fusion.2), channel_id=1, source_target_pairs={{0,12},{1,13},{2,14},{3,15},{4,8},{5,9},{6,10},{7,11},{8,4},{9,5},... | collective-permute-start | bytes 24584 | tf_op jit(solution)/shard_map/ppermute | solution.py:16
  119.2 4.8 %collective-permute-start.32 = (f32[8,256]{1,0:T(8,128)S(1)}, f32[8,256]{1,0:T(8,128)S(1)}, u32[]{:S(2)}, u32[]{:S(2)}) collective-permute-start(f32[8,256]{1,0:T(8,128)S(1)} %add_add_fusion.2), channel_id=1, source_target_pairs={{0,8},{1,9},{2,10},{3,11},{4,12},{5,13},{6,14},{7,15},{8,0},{9,1},... | collective-permute-start | bytes 24584 | tf_op jit(solution)/shard_map/ppermute | solution.py:16
  120.5 3.5 %collective-permute-start.31 = (f32[8,256]{1,0:T(8,128)S(1)}, f32[8,256]{1,0:T(8,128)S(1)}, u32[]{:S(2)}, u32[]{:S(2)}) collective-permute-start(f32[8,256]{1,0:T(8,128)S(1)} %add_add_fusion.2), channel_id=1, source_target_pairs={{0,4},{1,5},{2,6},{3,7},{4,0},{5,1},{6,2},{7,3},{8,12},{9,13},{10,... | collective-permute-start | bytes 24584 | tf_op jit(solution)/shard_map/ppermute | solution.py:16
  124.2 15.1 %collective-permute-start.35 = (bf16[64,1408]{1,0:T(8,128)(2,1)S(1)}, bf16[64,1408]{1,0:T(8,128)(2,1)S(1)}, u32[]{:S(2)}, u32[]{:S(2)}) collective-permute-start(bf16[64,1408]{1,0:T(8,128)(2,1)S(1)} %get-tuple-element.111), channel_id=1, source_target_pairs={{0,2},{1,3},{2,0},{3,1},{4,6},{5,7},{6,4},{7,5},{8,10},{9,11},{10,... | collective-permute-start | bytes 540680 | tf_op jit(solution)/shard_map/ppermute | solution.py:16
  126.3 13.0 %collective-permute-start.34 = (f32[8,1280]{1,0:T(8,128)S(1)}, f32[8,1280]{1,0:T(8,128)S(1)}, u32[]{:S(2)}, u32[]{:S(2)}) collective-permute-start(f32[8,1280]{1,0:T(8,128)S(1)} %convolution_bitcast_fusion), channel_id=1, source_target_pairs={{0,64},{16,80},{32,96},{48,112},{64,0},{80,16},{96,32},{112,48},{1... | collective-permute-start | bytes 122888 | tf_op jit(solution)/shard_map/ppermute | solution.py:16
  139.4 18.6 %collective-permute-start.38 = (bf16[2,64,1408]{2,1,0:T(8,128)(2,1)S(1)}, bf16[2,64,1408]{2,1,0:T(8,128)(2,1)S(1)}, u32[]{:S(2)}, u32[]{:S(2)}) collective-permute-start(bf16[2,64,1408]{2,1,0:T(8,128)(2,1)S(1)} %pad_maximum_fusion.7.pair), channel_id=1, source_target_pairs={{0,12},{1,13},{2,14},{3,15},{4,8},{5,9},{6,10},{7,11},{8,4},{9,5},... | collective-permute-start | bytes 1081352 | tf_op jit(solution)/shard_map/ppermute | solution.py:16
  140.6 17.4 %collective-permute-start.37 = (bf16[2,64,1408]{2,1,0:T(8,128)(2,1)S(1)}, bf16[2,64,1408]{2,1,0:T(8,128)(2,1)S(1)}, u32[]{:S(2)}, u32[]{:S(2)}) collective-permute-start(bf16[2,64,1408]{2,1,0:T(8,128)(2,1)S(1)} %pad_maximum_fusion.7.pair), channel_id=1, source_target_pairs={{0,8},{1,9},{2,10},{3,11},{4,12},{5,13},{6,14},{7,15},{8,0},{9,1},... | collective-permute-start | bytes 1081352 | tf_op jit(solution)/shard_map/ppermute | solution.py:16
  141.3 17.0 %collective-permute-start.36 = (bf16[2,64,1408]{2,1,0:T(8,128)(2,1)S(1)}, bf16[2,64,1408]{2,1,0:T(8,128)(2,1)S(1)}, u32[]{:S(2)}, u32[]{:S(2)}) collective-permute-start(bf16[2,64,1408]{2,1,0:T(8,128)(2,1)S(1)} %pad_maximum_fusion.7.pair), channel_id=1, source_target_pairs={{0,4},{1,5},{2,6},{3,7},{4,0},{5,1},{6,2},{7,3},{8,12},{9,13},{10,... | collective-permute-start | bytes 1081352 | tf_op jit(solution)/shard_map/ppermute | solution.py:16
  142.7 4.0 %collective-permute-start.39 = (f32[8,1280]{1,0:T(8,128)S(1)}, f32[8,1280]{1,0:T(8,128)S(1)}, u32[]{:S(2)}, u32[]{:S(2)}) collective-permute-start(f32[8,1280]{1,0:T(8,128)S(1)} %add.72), channel_id=1, source_target_pairs={{0,128},{16,144},{32,160},{48,176},{64,192},{80,208},{96,224},{112... | collective-permute-start | bytes 122888 | tf_op jit(solution)/shard_map/ppermute | solution.py:16
  146.8 3.1 %collective-permute-start.40 = (f32[8,1280]{1,0:T(8,128)S(1)}, f32[8,1280]{1,0:T(8,128)S(1)}, u32[]{:S(2)}, u32[]{:S(2)}) collective-permute-start(f32[8,1280]{1,0:T(8,128)S(1)} %add.73), channel_id=1, source_target_pairs={{0,16},{16,0},{32,48},{48,32},{64,80},{80,64},{96,112},{112,96},{1... | collective-permute-start | bytes 122888 | tf_op jit(solution)/shard_map/ppermute | solution.py:16
  149.9 8.4 %collective-permute-start.41 = (f32[8,1280]{1,0:T(8,128)S(1)}, f32[8,1280]{1,0:T(8,128)S(1)}, u32[]{:S(2)}, u32[]{:S(2)}) collective-permute-start(f32[8,1280]{1,0:T(8,128)S(1)} %add.74), channel_id=1, source_target_pairs={{0,32},{16,48},{32,0},{48,16},{64,96},{80,112},{96,64},{112,80},{1... | collective-permute-start | bytes 122888 | tf_op jit(solution)/shard_map/ppermute | solution.py:16
  159.6 3.3 %collective-permute-start.42 = (f32[128,1280]{1,0:T(8,128)S(1)}, f32[128,1280]{1,0:T(8,128)S(1)}, u32[]{:S(2)}, u32[]{:S(2)}) collective-permute-start(f32[128,1280]{1,0:T(8,128)S(1)} %get-tuple-element.119), channel_id=1, source_target_pairs={{0,1},{1,0},{2,3},{3,2},{4,5},{5,4},{6,7},{7,6},{8,9},{9,8},{10,11... | collective-permute-start | bytes 1966088 | tf_op jit(solution)/shard_map/ppermute | solution.py:16
